TPU v7x, 32 devices: a whole 2x2x4 slice. The times are simulated.
32 devices in a mesh: sub: 32 (over z, y, x, core).
Axes of the slice: x: 2, y: 2, z: 4, core: 2. Of those that a mesh axis runs over, the one named last changes fastest.
Arguments:
- right_side: bfloat16 [32, 1024, 128], P('sub'), may hold values from -6 to 6
- schur: bfloat16 [32, 1024, 1024], P('sub'), may hold values from -1 to 2
- neumann: bfloat16 [32, 1024, 1024], P('sub'), may hold values from -1 to 1
- weights: float32 [32, 1024], P('sub'), may hold values from 0.25 to 1
- neighbours: int32 [32, 4], P('sub'), may hold values from -1 to 31, as said below
- counts: int32 [32], P('sub'), may hold values from 512 to 1024, as said below
- shared_rows: int32 [32, 4, 128], P('sub'), may hold values from 0 to 1023, as said below
Outputs:
- solution: float32 [32, 1024, 128], P('sub')
Inputs may be any that keep to these rules, and one draw needn't show every extreme that they name: `neighbours`: slot 0 holds s + 1, slot 1 s - 1, slot 2 s + 16, slot 3 s - 16 where that link exists, else -1; links are symmetric: s names t in a slot exactly when t names s in the opposite slot. Subdomains 32 - 2 and 31 are always linked. `counts`: every subdomain has at least 512 nodes in use; some subdomain uses all 1024. `shared_rows`: every entry of subdomain s is below counts[s]; entries of one list may repeat.
All inputs are finite; a program needn't handle non-finite values.
Results may differ from a plain program's by a relative error of at most 0.0075.
Values may be sent and summed in bfloat16 or wider, within the bound.
No kernel may reach another device: no remote copies, remote signals or barrier semaphores. Data moves between devices by JAX's collectives and lax.ppermute only.
A program may use at most 64 MiB of HBM per device.

v0:
```python
import jax
import jax.numpy as jnp
from jax import lax
from jax.sharding import PartitionSpec as P

ITERS = 4


link_offsets = (1, -1, 16, -16)
opposite_slot = (1, 0, 3, 2)
damping_factor = 0.7


def from_behind(block, axis, distance):
    devices = range(lax.axis_size(axis))
    route = [(i - distance, i) for i in devices if i - distance in devices]
    return lax.ppermute(block, axis, route)


def schur_product(s_mat, current):
    return lax.dot_general(
        s_mat, current, (((0,), (0,)), ((), ())), preferred_element_type=jnp.float32
    )


def neumann_product(n_mat, scaled):
    return jnp.dot(n_mat, scaled, preferred_element_type=jnp.float32)


def select_rows(picker, block):
    return lax.dot_general(
        picker, block, (((0,), (0,)), ((), ())), preferred_element_type=jnp.float32
    ).astype(jnp.bfloat16)


def body(right_side, schur, neumann, weights, neighbours, counts, shared_rows):
    rhs = right_side[0].astype(jnp.float32)
    s_mat = schur[0]
    n_mat = neumann[0]
    weight = weights[0][:, None]
    live = (neighbours[0] >= 0).astype(jnp.bfloat16)
    count = counts[0]
    links = shared_rows[0]
    width = s_mat.shape[0]
    share = links.shape[1]
    mask = (jnp.arange(width) < count).astype(jnp.float32)[:, None]
    positions = jnp.arange(width)[:, None]

    def one_hot(rows):
        return (positions == rows[None, :]).astype(jnp.bfloat16)

    placer = jnp.concatenate([one_hot(links[slot]) * live[slot] for slot in range(4)], 1)
    own_picker = jnp.concatenate([one_hot(links[opposite_slot[slot]]) for slot in range(4)], 1)

    def assemble(own, sent):
        received = []
        packed_all = select_rows(own_picker, sent)
        for slot in (0, 1):
            packed = packed_all[slot * share : (slot + 1) * share]
            received.append(from_behind(packed, "sub", -link_offsets[slot]))
        for slot in (2, 3):
            packed = packed_all[slot * share : (slot + 1) * share]
            received.append(from_behind(packed, "sub", -link_offsets[slot]))
        stacked = jnp.concatenate(received, 0)
        return own + jnp.dot(placer, stacked, preferred_element_type=jnp.float32)

    solution = jnp.zeros(rhs.shape, jnp.float32)
    for step in range(ITERS):
        current = solution.astype(jnp.bfloat16)
        local = mask * (rhs - schur_product(s_mat, current))
        residual = assemble(local, local.astype(jnp.bfloat16))
        scaled = (weight * residual).astype(jnp.bfloat16)
        correction = neumann_product(n_mat, scaled)
        weighted = mask * weight * correction
        update = assemble(weighted, weighted.astype(jnp.bfloat16))
        solution = solution + damping_factor * update
    return solution[None]


def solution(mesh):
    in_specs = (
        P("sub", None, None),
        P("sub", None, None),
        P("sub", None, None),
        P("sub", None),
        P("sub", None),
        P("sub"),
        P("sub", None, None),
    )
    out_specs = P("sub", None, None)
    return jax.shard_map(body, mesh=mesh, in_specs=in_specs, out_specs=out_specs, check_vma=False)
```

profile of v0, /device:TPU:8, one launch (start us, length us, event | category | flops | bytes accessed | tf_op | source)
XLA Modules:
  0.0 166.6 jit_solution(12054514536277329424)
XLA Ops:
  4.2 3.7 %collective-permute-start = (bf16[128,128]{1,0:T(8,128)(2,1)S(1)}, bf16[128,128]{1,0:T(8,128)(2,1)S(1)}, u32[]{:S(2)}, u32[]{:S(2)}) collective-permute-start(bf16[128,128]{1,0:T(8,128)(2,1)S(1)} %get-tuple-element.33), channel_id=1, source_target_pairs={{1,0},{2,1},{3,2},{4,3},{5,4},{6,5},{7,6},{8,7},{9,8},{10,9},{11,1... | collective-permute-start | bytes 98312 | tf_op jit(solution)/shard_map/ppermute | solution.py:17
  7.9 4.5 %collective-permute-start.3 = (bf16[128,128]{1,0:T(8,128)(2,1)S(1)}, bf16[128,128]{1,0:T(8,128)(2,1)S(1)}, u32[]{:S(2)}, u32[]{:S(2)}) collective-permute-start(bf16[128,128]{1,0:T(8,128)(2,1)S(1)} %get-tuple-element.34), channel_id=1, source_target_pairs={{0,16},{1,17},{2,18},{3,19},{4,20},{5,21},{6,22},{7,23},{8,24},{9,... | collective-permute-start | bytes 98312 | tf_op jit(solution)/shard_map/ppermute | solution.py:17
  13.7 1.9 %collective-permute-start.1 = (bf16[128,128]{1,0:T(8,128)(2,1)S(1)}, bf16[128,128]{1,0:T(8,128)(2,1)S(1)}, u32[]{:S(2)}, u32[]{:S(2)}) collective-permute-start(bf16[128,128]{1,0:T(8,128)(2,1)S(1)} %get-tuple-element.36), channel_id=1, source_target_pairs={{0,1},{1,2},{2,3},{3,4},{4,5},{5,6},{6,7},{7,8},{8,9},{9,10},{10,1... | collective-permute-start | bytes 98312 | tf_op jit(solution)/shard_map/ppermute | solution.py:17
  16.3 2.2 %broadcast_select_fusion = (bf16[1024,128]{1,0:T(8,128)(2,1)}, bf16[1024,128]{1,0:T(8,128)(2,1)}) fusion(bf16[]{:T(256)} %bitcast.12, s32[128]{0:T(128)S(1)} %get-tuple-element.39, bf16[]{:T(256)} %bitcast.10, s32[128]{0:T(128)S(1)} %get-tuple-element.40), kind=kLoop, calls=%fused_computation.161 | loop fusion | flops 524288 | bytes 525316 | tf_op jit(solution)/shard_map/mul | solution.py:52
  18.5 2.2 %broadcast_select_fusion.2 = (bf16[1024,128]{1,0:T(8,128)(2,1)}, bf16[1024,128]{1,0:T(8,128)(2,1)}) fusion(bf16[]{:T(256)} %bitcast.8, s32[128]{0:T(128)S(1)} %get-tuple-element.37, bf16[]{:T(256)} %bitcast.6, s32[128]{0:T(128)S(1)} %get-tuple-element.38), kind=kLoop, calls=%fused_computation.163 | loop fusion | flops 524288 | bytes 525316 | tf_op jit(solution)/shard_map/mul | solution.py:52
  21.3 3.9 %fusion.83 = f32[1024,128]{0,1:T(8,128)} fusion(bf16[1,1024,1024]{2,1,0:T(8,128)(2,1)} %param.9, f32[1024,128]{0,1:T(8,128)S(1)} %fusion.77, f32[1024]{0:T(1024)S(1)} %bitcast.115, f32[1024]{0:T(1024)S(1)} %fusion.233, bf16[128,128]{1,0:T(8,128)(2,1)S(1)} %collective-permute-done.3, bf16[128,128]{1,0:T(8,128)(2,1)S(1)} %collective-permute-done.2, ...), kind=kOutput, calls=%fused_computation.66 | convolution fusion | flops 407896064 | bytes 4333568 | tf_op jit(solution)/shard_map/dot_general | solution.py:27
  25.3 1.8 %fusion.111 = bf16[512,128]{1,0:T(8,128)(2,1)S(1)} fusion(pred[1024,512]{1,0:T(32,128)(4,1)S(1)} %pad_add_fusion, f32[1024,128]{0,1:T(8,128)} %fusion.83), kind=kOutput, calls=%fused_computation.78 | convolution fusion | flops 134938624 | bytes 1179648 | tf_op jit(solution)/shard_map/dot_general | solution.py:31
  27.1 5.4 %collective-permute-start.4 = (bf16[128,128]{1,0:T(8,128)(2,1)S(1)}, bf16[128,128]{1,0:T(8,128)(2,1)S(1)}, u32[]{:S(2)}, u32[]{:S(2)}) collective-permute-start(bf16[128,128]{1,0:T(8,128)(2,1)S(1)} %get-tuple-element.29), channel_id=1, source_target_pairs={{1,0},{2,1},{3,2},{4,3},{5,4},{6,5},{7,6},{8,7},{9,8},{10,9},{11,1... | collective-permute-start | bytes 98312 | tf_op jit(solution)/shard_map/ppermute | solution.py:17
  32.5 5.4 %collective-permute-start.7 = (bf16[128,128]{1,0:T(8,128)(2,1)S(1)}, bf16[128,128]{1,0:T(8,128)(2,1)S(1)}, u32[]{:S(2)}, u32[]{:S(2)}) collective-permute-start(bf16[128,128]{1,0:T(8,128)(2,1)S(1)} %get-tuple-element.30), channel_id=1, source_target_pairs={{0,16},{1,17},{2,18},{3,19},{4,20},{5,21},{6,22},{7,23},{8,24},{9,... | collective-permute-start | bytes 98312 | tf_op jit(solution)/shard_map/ppermute | solution.py:17
  39.3 1.9 %collective-permute-start.5 = (bf16[128,128]{1,0:T(8,128)(2,1)S(1)}, bf16[128,128]{1,0:T(8,128)(2,1)S(1)}, u32[]{:S(2)}, u32[]{:S(2)}) collective-permute-start(bf16[128,128]{1,0:T(8,128)(2,1)S(1)} %get-tuple-element.32), channel_id=1, source_target_pairs={{0,1},{1,2},{2,3},{3,4},{4,5},{5,6},{6,7},{7,8},{8,9},{9,10},{10,1... | collective-permute-start | bytes 98312 | tf_op jit(solution)/shard_map/ppermute | solution.py:17
  41.2 3.5 %collective-permute-done.6 = bf16[128,128]{1,0:T(8,128)(2,1)S(1)} collective-permute-done((bf16[128,128]{1,0:T(8,128)(2,1)S(1)}, bf16[128,128]{1,0:T(8,128)(2,1)S(1)}, u32[]{:S(2)}, u32[]{:S(2)}) %collective-permute-start.6) | collective-permute-done | bytes 32800 | tf_op jit(solution)/shard_map/ppermute | solution.py:17
  44.7 1.6 collective-permute-done.5
  48.7 1.9 %collective-permute-start.8 = (bf16[128,128]{1,0:T(8,128)(2,1)S(1)}, bf16[128,128]{1,0:T(8,128)(2,1)S(1)}, u32[]{:S(2)}, u32[]{:S(2)}) collective-permute-start(bf16[128,128]{1,0:T(8,128)(2,1)S(1)} %get-tuple-element.25), channel_id=1, source_target_pairs={{1,0},{2,1},{3,2},{4,3},{5,4},{6,5},{7,6},{8,7},{9,8},{10,9},{11,1... | collective-permute-start | bytes 98312 | tf_op jit(solution)/shard_map/ppermute | solution.py:17
  50.6 5.4 %collective-permute-start.11 = (bf16[128,128]{1,0:T(8,128)(2,1)S(1)}, bf16[128,128]{1,0:T(8,128)(2,1)S(1)}, u32[]{:S(2)}, u32[]{:S(2)}) collective-permute-start(bf16[128,128]{1,0:T(8,128)(2,1)S(1)} %get-tuple-element.26), channel_id=1, source_target_pairs={{0,16},{1,17},{2,18},{3,19},{4,20},{5,21},{6,22},{7,23},{8,24},{9,... | collective-permute-start | bytes 98312 | tf_op jit(solution)/shard_map/ppermute | solution.py:17
  57.4 2.1 %collective-permute-start.9 = (bf16[128,128]{1,0:T(8,128)(2,1)S(1)}, bf16[128,128]{1,0:T(8,128)(2,1)}, u32[]{:S(2)}, u32[]{:S(2)}) collective-permute-start(bf16[128,128]{1,0:T(8,128)(2,1)S(1)} %get-tuple-element.28), channel_id=1, source_target_pairs={{0,1},{1,2},{2,3},{3,4},{4,5},{5,6},{6,7},{7,8},{8,9},{9,10},{10,1... | collective-permute-start | bytes 98312 | tf_op jit(solution)/shard_map/ppermute | solution.py:17
  59.5 3.3 %collective-permute-done.10 = bf16[128,128]{1,0:T(8,128)(2,1)S(1)} collective-permute-done((bf16[128,128]{1,0:T(8,128)(2,1)S(1)}, bf16[128,128]{1,0:T(8,128)(2,1)S(1)}, u32[]{:S(2)}, u32[]{:S(2)}) %collective-permute-start.10) | collective-permute-done | bytes 32800 | tf_op jit(solution)/shard_map/ppermute | solution.py:17
  62.8 1.7 %collective-permute-done.9 = bf16[128,128]{1,0:T(8,128)(2,1)} collective-permute-done((bf16[128,128]{1,0:T(8,128)(2,1)S(1)}, bf16[128,128]{1,0:T(8,128)(2,1)}, u32[]{:S(2)}, u32[]{:S(2)}) %collective-permute-start.9) | collective-permute-done | bytes 32800 | tf_op jit(solution)/shard_map/ppermute | solution.py:17
  64.5 4.1 %fusion.89 = f32[1024,128]{0,1:T(8,128)} fusion(bf16[1,1024,1024]{2,1,0:T(8,128)(2,1)} %param.9, f32[1024,128]{0,1:T(8,128)} %copy-done.4, f32[1024]{0:T(1024)S(1)} %bitcast.116, f32[1024]{0:T(1024)S(1)} %fusion.233, bf16[128,128]{1,0:T(8,128)(2,1)S(1)} %collective-permute-done.11, bf16[128,128]{1,0:T(8,128)(2,1)S(1)} %collective-permute-done.10, ...), kind=kOutput, calls=%fused_computation.68 | convolution fusion | flops 407896064 | bytes 4333568 | tf_op jit(solution)/shard_map/dot_general | solution.py:27
  68.7 1.8 %fusion.117 = bf16[512,128]{1,0:T(8,128)(2,1)S(1)} fusion(pred[1024,512]{1,0:T(32,128)(4,1)S(1)} %pad_add_fusion, f32[1024,128]{0,1:T(8,128)} %fusion.89), kind=kOutput, calls=%fused_computation.80 | convolution fusion | flops 134938624 | bytes 1179648 | tf_op jit(solution)/shard_map/dot_general | solution.py:31
  70.5 1.9 %collective-permute-start.12 = (bf16[128,128]{1,0:T(8,128)(2,1)S(1)}, bf16[128,128]{1,0:T(8,128)(2,1)S(1)}, u32[]{:S(2)}, u32[]{:S(2)}) collective-permute-start(bf16[128,128]{1,0:T(8,128)(2,1)S(1)} %get-tuple-element.21), channel_id=1, source_target_pairs={{1,0},{2,1},{3,2},{4,3},{5,4},{6,5},{7,6},{8,7},{9,8},{10,9},{11,1... | collective-permute-start | bytes 98312 | tf_op jit(solution)/shard_map/ppermute | solution.py:17
  72.4 5.4 %collective-permute-start.15 = (bf16[128,128]{1,0:T(8,128)(2,1)S(1)}, bf16[128,128]{1,0:T(8,128)(2,1)S(1)}, u32[]{:S(2)}, u32[]{:S(2)}) collective-permute-start(bf16[128,128]{1,0:T(8,128)(2,1)S(1)} %get-tuple-element.22), channel_id=1, source_target_pairs={{0,16},{1,17},{2,18},{3,19},{4,20},{5,21},{6,22},{7,23},{8,24},{9,... | collective-permute-start | bytes 98312 | tf_op jit(solution)/shard_map/ppermute | solution.py:17
  79.2 2.1 %collective-permute-start.13 = (bf16[128,128]{1,0:T(8,128)(2,1)S(1)}, bf16[128,128]{1,0:T(8,128)(2,1)S(1)}, u32[]{:S(2)}, u32[]{:S(2)}) collective-permute-start(bf16[128,128]{1,0:T(8,128)(2,1)S(1)} %get-tuple-element.24), channel_id=1, source_target_pairs={{0,1},{1,2},{2,3},{3,4},{4,5},{5,6},{6,7},{7,8},{8,9},{9,10},{10,1... | collective-permute-start | bytes 98312 | tf_op jit(solution)/shard_map/ppermute | solution.py:17
  81.3 3.3 %collective-permute-done.14 = bf16[128,128]{1,0:T(8,128)(2,1)S(1)} collective-permute-done((bf16[128,128]{1,0:T(8,128)(2,1)S(1)}, bf16[128,128]{1,0:T(8,128)(2,1)S(1)}, u32[]{:S(2)}, u32[]{:S(2)}) %collective-permute-start.14) | collective-permute-done | bytes 32800 | tf_op jit(solution)/shard_map/ppermute | solution.py:17
  84.6 1.6 collective-permute-done.13
  87.8 1.9 %collective-permute-start.16 = (bf16[128,128]{1,0:T(8,128)(2,1)S(1)}, bf16[128,128]{1,0:T(8,128)(2,1)S(1)}, u32[]{:S(2)}, u32[]{:S(2)}) collective-permute-start(bf16[128,128]{1,0:T(8,128)(2,1)S(1)} %get-tuple-element.17), channel_id=1, source_target_pairs={{1,0},{2,1},{3,2},{4,3},{5,4},{6,5},{7,6},{8,7},{9,8},{10,9},{11,1... | collective-permute-start | bytes 98312 | tf_op jit(solution)/shard_map/ppermute | solution.py:17
  89.7 5.4 %collective-permute-start.19 = (bf16[128,128]{1,0:T(8,128)(2,1)S(1)}, bf16[128,128]{1,0:T(8,128)(2,1)S(1)}, u32[]{:S(2)}, u32[]{:S(2)}) collective-permute-start(bf16[128,128]{1,0:T(8,128)(2,1)S(1)} %get-tuple-element.18), channel_id=1, source_target_pairs={{0,16},{1,17},{2,18},{3,19},{4,20},{5,21},{6,22},{7,23},{8,24},{9,... | collective-permute-start | bytes 98312 | tf_op jit(solution)/shard_map/ppermute | solution.py:17
  96.5 2.1 %collective-permute-start.17 = (bf16[128,128]{1,0:T(8,128)(2,1)S(1)}, bf16[128,128]{1,0:T(8,128)(2,1)}, u32[]{:S(2)}, u32[]{:S(2)}) collective-permute-start(bf16[128,128]{1,0:T(8,128)(2,1)S(1)} %get-tuple-element.20), channel_id=1, source_target_pairs={{0,1},{1,2},{2,3},{3,4},{4,5},{5,6},{6,7},{7,8},{8,9},{9,10},{10,1... | collective-permute-start | bytes 98312 | tf_op jit(solution)/shard_map/ppermute | solution.py:17
  98.6 3.3 %collective-permute-done.18 = bf16[128,128]{1,0:T(8,128)(2,1)S(1)} collective-permute-done((bf16[128,128]{1,0:T(8,128)(2,1)S(1)}, bf16[128,128]{1,0:T(8,128)(2,1)S(1)}, u32[]{:S(2)}, u32[]{:S(2)}) %collective-permute-start.18) | collective-permute-done | bytes 32800 | tf_op jit(solution)/shard_map/ppermute | solution.py:17
  101.9 1.7 %collective-permute-done.17 = bf16[128,128]{1,0:T(8,128)(2,1)} collective-permute-done((bf16[128,128]{1,0:T(8,128)(2,1)S(1)}, bf16[128,128]{1,0:T(8,128)(2,1)}, u32[]{:S(2)}, u32[]{:S(2)}) %collective-permute-start.17) | collective-permute-done | bytes 32800 | tf_op jit(solution)/shard_map/ppermute | solution.py:17
  103.6 3.9 %fusion.95 = f32[1024,128]{0,1:T(8,128)} fusion(bf16[1,1024,1024]{2,1,0:T(8,128)(2,1)} %param.9, f32[1024,128]{0,1:T(8,128)S(1)} %fusion.65, f32[1024]{0:T(1024)S(1)} %bitcast.117, f32[1024]{0:T(1024)S(1)} %fusion.233, bf16[128,128]{1,0:T(8,128)(2,1)S(1)} %collective-permute-done.19, bf16[128,128]{1,0:T(8,128)(2,1)S(1)} %collective-permute-done.18, ...), kind=kOutput, calls=%fused_computation.70 | convolution fusion | flops 407896064 | bytes 4333568 | tf_op jit(solution)/shard_map/dot_general | solution.py:27
  107.6 1.8 %fusion.123 = bf16[512,128]{1,0:T(8,128)(2,1)S(1)} fusion(pred[1024,512]{1,0:T(32,128)(4,1)S(1)} %pad_add_fusion, f32[1024,128]{0,1:T(8,128)} %fusion.95), kind=kOutput, calls=%fused_computation.82 | convolution fusion | flops 134938624 | bytes 1179648 | tf_op jit(solution)/shard_map/dot_general | solution.py:31
  109.4 1.9 %collective-permute-start.20 = (bf16[128,128]{1,0:T(8,128)(2,1)S(1)}, bf16[128,128]{1,0:T(8,128)(2,1)S(1)}, u32[]{:S(2)}, u32[]{:S(2)}) collective-permute-start(bf16[128,128]{1,0:T(8,128)(2,1)S(1)} %get-tuple-element.13), channel_id=1, source_target_pairs={{1,0},{2,1},{3,2},{4,3},{5,4},{6,5},{7,6},{8,7},{9,8},{10,9},{11,1... | collective-permute-start | bytes 98312 | tf_op jit(solution)/shard_map/ppermute | solution.py:17
  111.4 5.4 %collective-permute-start.23 = (bf16[128,128]{1,0:T(8,128)(2,1)S(1)}, bf16[128,128]{1,0:T(8,128)(2,1)S(1)}, u32[]{:S(2)}, u32[]{:S(2)}) collective-permute-start(bf16[128,128]{1,0:T(8,128)(2,1)S(1)} %get-tuple-element.14), channel_id=1, source_target_pairs={{0,16},{1,17},{2,18},{3,19},{4,20},{5,21},{6,22},{7,23},{8,24},{9,... | collective-permute-start | bytes 98312 | tf_op jit(solution)/shard_map/ppermute | solution.py:17
  118.1 2.1 %collective-permute-start.21 = (bf16[128,128]{1,0:T(8,128)(2,1)S(1)}, bf16[128,128]{1,0:T(8,128)(2,1)S(1)}, u32[]{:S(2)}, u32[]{:S(2)}) collective-permute-start(bf16[128,128]{1,0:T(8,128)(2,1)S(1)} %get-tuple-element.16), channel_id=1, source_target_pairs={{0,1},{1,2},{2,3},{3,4},{4,5},{5,6},{6,7},{7,8},{8,9},{9,10},{10,1... | collective-permute-start | bytes 98312 | tf_op jit(solution)/shard_map/ppermute | solution.py:17
  120.3 3.3 %collective-permute-done.22 = bf16[128,128]{1,0:T(8,128)(2,1)S(1)} collective-permute-done((bf16[128,128]{1,0:T(8,128)(2,1)S(1)}, bf16[128,128]{1,0:T(8,128)(2,1)S(1)}, u32[]{:S(2)}, u32[]{:S(2)}) %collective-permute-start.22) | collective-permute-done | bytes 32800 | tf_op jit(solution)/shard_map/ppermute | solution.py:17
  123.5 1.6 collective-permute-done.21
  127.6 1.9 %collective-permute-start.24 = (bf16[128,128]{1,0:T(8,128)(2,1)S(1)}, bf16[128,128]{1,0:T(8,128)(2,1)S(1)}, u32[]{:S(2)}, u32[]{:S(2)}) collective-permute-start(bf16[128,128]{1,0:T(8,128)(2,1)S(1)} %get-tuple-element.9), channel_id=1, source_target_pairs={{1,0},{2,1},{3,2},{4,3},{5,4},{6,5},{7,6},{8,7},{9,8},{10,9},{11,1... | collective-permute-start | bytes 98312 | tf_op jit(solution)/shard_map/ppermute | solution.py:17
  129.5 5.6 %collective-permute-start.27 = (bf16[128,128]{1,0:T(8,128)(2,1)S(1)}, bf16[128,128]{1,0:T(8,128)(2,1)S(1)}, u32[]{:S(2)}, u32[]{:S(2)}) collective-permute-start(bf16[128,128]{1,0:T(8,128)(2,1)S(1)} %get-tuple-element.10), channel_id=1, source_target_pairs={{0,16},{1,17},{2,18},{3,19},{4,20},{5,21},{6,22},{7,23},{8,24},{9,... | collective-permute-start | bytes 98312 | tf_op jit(solution)/shard_map/ppermute | solution.py:17
  136.3 2.1 %collective-permute-start.25 = (bf16[128,128]{1,0:T(8,128)(2,1)S(1)}, bf16[128,128]{1,0:T(8,128)(2,1)}, u32[]{:S(2)}, u32[]{:S(2)}) collective-permute-start(bf16[128,128]{1,0:T(8,128)(2,1)S(1)} %get-tuple-element.12), channel_id=1, source_target_pairs={{0,1},{1,2},{2,3},{3,4},{4,5},{5,6},{6,7},{7,8},{8,9},{9,10},{10,1... | collective-permute-start | bytes 98312 | tf_op jit(solution)/shard_map/ppermute | solution.py:17
  138.5 3.3 %collective-permute-done.26 = bf16[128,128]{1,0:T(8,128)(2,1)S(1)} collective-permute-done((bf16[128,128]{1,0:T(8,128)(2,1)S(1)}, bf16[128,128]{1,0:T(8,128)(2,1)S(1)}, u32[]{:S(2)}, u32[]{:S(2)}) %collective-permute-start.26) | collective-permute-done | bytes 32800 | tf_op jit(solution)/shard_map/ppermute | solution.py:17
  141.8 1.7 %collective-permute-done.25 = bf16[128,128]{1,0:T(8,128)(2,1)} collective-permute-done((bf16[128,128]{1,0:T(8,128)(2,1)S(1)}, bf16[128,128]{1,0:T(8,128)(2,1)}, u32[]{:S(2)}, u32[]{:S(2)}) %collective-permute-start.25) | collective-permute-done | bytes 32800 | tf_op jit(solution)/shard_map/ppermute | solution.py:17
  143.5 4.0 %fusion.101 = f32[1024,128]{0,1:T(8,128)} fusion(bf16[1,1024,1024]{2,1,0:T(8,128)(2,1)} %param.9, f32[1024,128]{0,1:T(8,128)} %copy-done.3, f32[1024]{0:T(1024)S(1)} %bitcast.118, f32[1024]{0:T(1024)S(1)} %fusion.233, bf16[128,128]{1,0:T(8,128)(2,1)S(1)} %collective-permute-done.27, bf16[128,128]{1,0:T(8,128)(2,1)S(1)} %collective-permute-done.26, ...), kind=kOutput, calls=%fused_computation.72 | convolution fusion | flops 407896064 | bytes 4333568 | tf_op jit(solution)/shard_map/dot_general | solution.py:27
  147.5 1.8 %fusion.129 = bf16[512,128]{1,0:T(8,128)(2,1)S(1)} fusion(pred[1024,512]{1,0:T(32,128)(4,1)S(1)} %pad_add_fusion, f32[1024,128]{0,1:T(8,128)} %fusion.101), kind=kOutput, calls=%fused_computation.84 | convolution fusion | flops 134938624 | bytes 1179648 | tf_op jit(solution)/shard_map/dot_general | solution.py:31
  149.4 1.9 %collective-permute-start.28 = (bf16[128,128]{1,0:T(8,128)(2,1)S(1)}, bf16[128,128]{1,0:T(8,128)(2,1)S(1)}, u32[]{:S(2)}, u32[]{:S(2)}) collective-permute-start(bf16[128,128]{1,0:T(8,128)(2,1)S(1)} %get-tuple-element.5), channel_id=1, source_target_pairs={{1,0},{2,1},{3,2},{4,3},{5,4},{6,5},{7,6},{8,7},{9,8},{10,9},{11,1... | collective-permute-start | bytes 98312 | tf_op jit(solution)/shard_map/ppermute | solution.py:17
  151.3 5.4 %collective-permute-start.31 = (bf16[128,128]{1,0:T(8,128)(2,1)S(1)}, bf16[128,128]{1,0:T(8,128)(2,1)S(1)}, u32[]{:S(2)}, u32[]{:S(2)}) collective-permute-start(bf16[128,128]{1,0:T(8,128)(2,1)S(1)} %get-tuple-element.6), channel_id=1, source_target_pairs={{0,16},{1,17},{2,18},{3,19},{4,20},{5,21},{6,22},{7,23},{8,24},{9,... | collective-permute-start | bytes 98312 | tf_op jit(solution)/shard_map/ppermute | solution.py:17
  158.0 2.1 %collective-permute-start.29 = (bf16[128,128]{1,0:T(8,128)(2,1)S(1)}, bf16[128,128]{1,0:T(8,128)(2,1)S(1)}, u32[]{:S(2)}, u32[]{:S(2)}) collective-permute-start(bf16[128,128]{1,0:T(8,128)(2,1)S(1)} %get-tuple-element.8), channel_id=1, source_target_pairs={{0,1},{1,2},{2,3},{3,4},{4,5},{5,6},{6,7},{7,8},{8,9},{9,10},{10,1... | collective-permute-start | bytes 98312 | tf_op jit(solution)/shard_map/ppermute | solution.py:17
  160.2 3.3 %collective-permute-done.30 = bf16[128,128]{1,0:T(8,128)(2,1)S(1)} collective-permute-done((bf16[128,128]{1,0:T(8,128)(2,1)S(1)}, bf16[128,128]{1,0:T(8,128)(2,1)S(1)}, u32[]{:S(2)}, u32[]{:S(2)}) %collective-permute-start.30) | collective-permute-done | bytes 32800 | tf_op jit(solution)/shard_map/ppermute | solution.py:17
  163.4 1.6 collective-permute-done.29
  (112 shorter events, 22.8 us)
Async XLA Ops:
  4.2 16.5 %collective-permute-start = (bf16[128,128]{1,0:T(8,128)(2,1)S(1)}, bf16[128,128]{1,0:T(8,128)(2,1)S(1)}, u32[]{:S(2)}, u32[]{:S(2)}) collective-permute-start(bf16[128,128]{1,0:T(8,128)(2,1)S(1)} %get-tuple-element.33), channel_id=1, source_target_pairs={{1,0},{2,1},{3,2},{4,3},{5,4},{6,5},{7,6},{8,7},{9,8},{10,9},{11,1... | collective-permute-start | bytes 98312 | tf_op jit(solution)/shard_map/ppermute | solution.py:17
  7.9 12.8 %collective-permute-start.3 = (bf16[128,128]{1,0:T(8,128)(2,1)S(1)}, bf16[128,128]{1,0:T(8,128)(2,1)S(1)}, u32[]{:S(2)}, u32[]{:S(2)}) collective-permute-start(bf16[128,128]{1,0:T(8,128)(2,1)S(1)} %get-tuple-element.34), channel_id=1, source_target_pairs={{0,16},{1,17},{2,18},{3,19},{4,20},{5,21},{6,22},{7,23},{8,24},{9,... | collective-permute-start | bytes 98312 | tf_op jit(solution)/shard_map/ppermute | solution.py:17
  12.4 8.3 %collective-permute-start.2 = (bf16[128,128]{1,0:T(8,128)(2,1)S(1)}, bf16[128,128]{1,0:T(8,128)(2,1)S(1)}, u32[]{:S(2)}, u32[]{:S(2)}) collective-permute-start(bf16[128,128]{1,0:T(8,128)(2,1)S(1)} %get-tuple-element.35), channel_id=1, source_target_pairs={{16,0},{17,1},{18,2},{19,3},{20,4},{21,5},{22,6},{23,7},{24,8},{25... | collective-permute-start | bytes 98312 | tf_op jit(solution)/shard_map/ppermute | solution.py:17
  13.7 7.0 %collective-permute-start.1 = (bf16[128,128]{1,0:T(8,128)(2,1)S(1)}, bf16[128,128]{1,0:T(8,128)(2,1)S(1)}, u32[]{:S(2)}, u32[]{:S(2)}) collective-permute-start(bf16[128,128]{1,0:T(8,128)(2,1)S(1)} %get-tuple-element.36), channel_id=1, source_target_pairs={{0,1},{1,2},{2,3},{3,4},{4,5},{5,6},{6,7},{7,8},{8,9},{9,10},{10,1... | collective-permute-start | bytes 98312 | tf_op jit(solution)/shard_map/ppermute | solution.py:17
  25.3 21.1 %copy-start.5 = (bf16[1024,128]{1,0:T(8,128)(2,1)S(1)}, bf16[1024,128]{1,0:T(8,128)(2,1)}, u32[]{:S(2)}) copy-start(bf16[1024,128]{1,0:T(8,128)(2,1)} %get-tuple-element.49) | copy-start | bytes 786436
  25.3 21.1 %copy-start.9 = (bf16[1024,128]{1,0:T(8,128)(2,1)S(1)}, bf16[1024,128]{1,0:T(8,128)(2,1)}, u32[]{:S(2)}) copy-start(bf16[1024,128]{1,0:T(8,128)(2,1)} %get-tuple-element.50) | copy-start | bytes 786436
  25.3 21.1 %copy-start.13 = (bf16[1024,128]{1,0:T(8,128)(2,1)S(1)}, bf16[1024,128]{1,0:T(8,128)(2,1)}, u32[]{:S(2)}) copy-start(bf16[1024,128]{1,0:T(8,128)(2,1)} %get-tuple-element.51) | copy-start | bytes 786436
  25.3 21.1 %copy-start.17 = (bf16[1024,128]{1,0:T(8,128)(2,1)S(1)}, bf16[1024,128]{1,0:T(8,128)(2,1)}, u32[]{:S(2)}) copy-start(bf16[1024,128]{1,0:T(8,128)(2,1)} %get-tuple-element.52) | copy-start | bytes 786436
  25.3 21.1 %copy-start.27 = (f32[1024,128]{0,1:T(8,128)S(1)}, f32[1024,128]{0,1:T(8,128)}, u32[]{:S(2)}) copy-start(f32[1024,128]{0,1:T(8,128)} %fusion.83) | copy-start | bytes 1572868
  27.1 14.1 %collective-permute-start.4 = (bf16[128,128]{1,0:T(8,128)(2,1)S(1)}, bf16[128,128]{1,0:T(8,128)(2,1)S(1)}, u32[]{:S(2)}, u32[]{:S(2)}) collective-permute-start(bf16[128,128]{1,0:T(8,128)(2,1)S(1)} %get-tuple-element.29), channel_id=1, source_target_pairs={{1,0},{2,1},{3,2},{4,3},{5,4},{6,5},{7,6},{8,7},{9,8},{10,9},{11,1... | collective-permute-start | bytes 98312 | tf_op jit(solution)/shard_map/ppermute | solution.py:17
  32.5 8.7 %collective-permute-start.7 = (bf16[128,128]{1,0:T(8,128)(2,1)S(1)}, bf16[128,128]{1,0:T(8,128)(2,1)S(1)}, u32[]{:S(2)}, u32[]{:S(2)}) collective-permute-start(bf16[128,128]{1,0:T(8,128)(2,1)S(1)} %get-tuple-element.30), channel_id=1, source_target_pairs={{0,16},{1,17},{2,18},{3,19},{4,20},{5,21},{6,22},{7,23},{8,24},{9,... | collective-permute-start | bytes 98312 | tf_op jit(solution)/shard_map/ppermute | solution.py:17
  38.0 6.7 %collective-permute-start.6 = (bf16[128,128]{1,0:T(8,128)(2,1)S(1)}, bf16[128,128]{1,0:T(8,128)(2,1)S(1)}, u32[]{:S(2)}, u32[]{:S(2)}) collective-permute-start(bf16[128,128]{1,0:T(8,128)(2,1)S(1)} %get-tuple-element.31), channel_id=1, source_target_pairs={{16,0},{17,1},{18,2},{19,3},{20,4},{21,5},{22,6},{23,7},{24,8},{25... | collective-permute-start | bytes 98312 | tf_op jit(solution)/shard_map/ppermute | solution.py:17
  39.3 7.0 %collective-permute-start.5 = (bf16[128,128]{1,0:T(8,128)(2,1)S(1)}, bf16[128,128]{1,0:T(8,128)(2,1)S(1)}, u32[]{:S(2)}, u32[]{:S(2)}) collective-permute-start(bf16[128,128]{1,0:T(8,128)(2,1)S(1)} %get-tuple-element.32), channel_id=1, source_target_pairs={{0,1},{1,2},{2,3},{3,4},{4,5},{5,6},{6,7},{7,8},{8,9},{9,10},{10,1... | collective-permute-start | bytes 98312 | tf_op jit(solution)/shard_map/ppermute | solution.py:17
  48.7 10.8 %collective-permute-start.8 = (bf16[128,128]{1,0:T(8,128)(2,1)S(1)}, bf16[128,128]{1,0:T(8,128)(2,1)S(1)}, u32[]{:S(2)}, u32[]{:S(2)}) collective-permute-start(bf16[128,128]{1,0:T(8,128)(2,1)S(1)} %get-tuple-element.25), channel_id=1, source_target_pairs={{1,0},{2,1},{3,2},{4,3},{5,4},{6,5},{7,6},{8,7},{9,8},{10,9},{11,1... | collective-permute-start | bytes 98312 | tf_op jit(solution)/shard_map/ppermute | solution.py:17
  50.6 8.9 %collective-permute-start.11 = (bf16[128,128]{1,0:T(8,128)(2,1)S(1)}, bf16[128,128]{1,0:T(8,128)(2,1)S(1)}, u32[]{:S(2)}, u32[]{:S(2)}) collective-permute-start(bf16[128,128]{1,0:T(8,128)(2,1)S(1)} %get-tuple-element.26), channel_id=1, source_target_pairs={{0,16},{1,17},{2,18},{3,19},{4,20},{5,21},{6,22},{7,23},{8,24},{9,... | collective-permute-start | bytes 98312 | tf_op jit(solution)/shard_map/ppermute | solution.py:17
  56.1 6.7 %collective-permute-start.10 = (bf16[128,128]{1,0:T(8,128)(2,1)S(1)}, bf16[128,128]{1,0:T(8,128)(2,1)S(1)}, u32[]{:S(2)}, u32[]{:S(2)}) collective-permute-start(bf16[128,128]{1,0:T(8,128)(2,1)S(1)} %get-tuple-element.27), channel_id=1, source_target_pairs={{16,0},{17,1},{18,2},{19,3},{20,4},{21,5},{22,6},{23,7},{24,8},{25... | collective-permute-start | bytes 98312 | tf_op jit(solution)/shard_map/ppermute | solution.py:17
  57.4 7.1 %collective-permute-start.9 = (bf16[128,128]{1,0:T(8,128)(2,1)S(1)}, bf16[128,128]{1,0:T(8,128)(2,1)}, u32[]{:S(2)}, u32[]{:S(2)}) collective-permute-start(bf16[128,128]{1,0:T(8,128)(2,1)S(1)} %get-tuple-element.28), channel_id=1, source_target_pairs={{0,1},{1,2},{2,3},{3,4},{4,5},{5,6},{6,7},{7,8},{8,9},{9,10},{10,1... | collective-permute-start | bytes 98312 | tf_op jit(solution)/shard_map/ppermute | solution.py:17
  68.6 17.6 %copy-start.6 = (bf16[1024,128]{1,0:T(8,128)(2,1)S(1)}, bf16[1024,128]{1,0:T(8,128)(2,1)}, u32[]{:S(2)}) copy-start(bf16[1024,128]{1,0:T(8,128)(2,1)} %get-tuple-element.49) | copy-start | bytes 786436
  68.6 17.6 %copy-start.10 = (bf16[1024,128]{1,0:T(8,128)(2,1)S(1)}, bf16[1024,128]{1,0:T(8,128)(2,1)}, u32[]{:S(2)}) copy-start(bf16[1024,128]{1,0:T(8,128)(2,1)} %get-tuple-element.50) | copy-start | bytes 786436
  68.6 17.6 %copy-start.14 = (bf16[1024,128]{1,0:T(8,128)(2,1)S(1)}, bf16[1024,128]{1,0:T(8,128)(2,1)}, u32[]{:S(2)}) copy-start(bf16[1024,128]{1,0:T(8,128)(2,1)} %get-tuple-element.51) | copy-start | bytes 786436
  68.6 17.6 %copy-start.18 = (bf16[1024,128]{1,0:T(8,128)(2,1)S(1)}, bf16[1024,128]{1,0:T(8,128)(2,1)}, u32[]{:S(2)}) copy-start(bf16[1024,128]{1,0:T(8,128)(2,1)} %get-tuple-element.52) | copy-start | bytes 786436
  68.6 17.6 %copy-start.25 = (f32[1024,128]{0,1:T(8,128)S(1)}, f32[1024,128]{0,1:T(8,128)}, u32[]{:S(2)}) copy-start(f32[1024,128]{0,1:T(8,128)} %fusion.89) | copy-start | bytes 1572868
  70.5 10.8 %collective-permute-start.12 = (bf16[128,128]{1,0:T(8,128)(2,1)S(1)}, bf16[128,128]{1,0:T(8,128)(2,1)S(1)}, u32[]{:S(2)}, u32[]{:S(2)}) collective-permute-start(bf16[128,128]{1,0:T(8,128)(2,1)S(1)} %get-tuple-element.21), channel_id=1, source_target_pairs={{1,0},{2,1},{3,2},{4,3},{5,4},{6,5},{7,6},{8,7},{9,8},{10,9},{11,1... | collective-permute-start | bytes 98312 | tf_op jit(solution)/shard_map/ppermute | solution.py:17
  72.4 8.9 %collective-permute-start.15 = (bf16[128,128]{1,0:T(8,128)(2,1)S(1)}, bf16[128,128]{1,0:T(8,128)(2,1)S(1)}, u32[]{:S(2)}, u32[]{:S(2)}) collective-permute-start(bf16[128,128]{1,0:T(8,128)(2,1)S(1)} %get-tuple-element.22), channel_id=1, source_target_pairs={{0,16},{1,17},{2,18},{3,19},{4,20},{5,21},{6,22},{7,23},{8,24},{9,... | collective-permute-start | bytes 98312 | tf_op jit(solution)/shard_map/ppermute | solution.py:17
  77.9 6.7 %collective-permute-start.14 = (bf16[128,128]{1,0:T(8,128)(2,1)S(1)}, bf16[128,128]{1,0:T(8,128)(2,1)S(1)}, u32[]{:S(2)}, u32[]{:S(2)}) collective-permute-start(bf16[128,128]{1,0:T(8,128)(2,1)S(1)} %get-tuple-element.23), channel_id=1, source_target_pairs={{16,0},{17,1},{18,2},{19,3},{20,4},{21,5},{22,6},{23,7},{24,8},{25... | collective-permute-start | bytes 98312 | tf_op jit(solution)/shard_map/ppermute | solution.py:17
  79.2 7.0 %collective-permute-start.13 = (bf16[128,128]{1,0:T(8,128)(2,1)S(1)}, bf16[128,128]{1,0:T(8,128)(2,1)S(1)}, u32[]{:S(2)}, u32[]{:S(2)}) collective-permute-start(bf16[128,128]{1,0:T(8,128)(2,1)S(1)} %get-tuple-element.24), channel_id=1, source_target_pairs={{0,1},{1,2},{2,3},{3,4},{4,5},{5,6},{6,7},{7,8},{8,9},{9,10},{10,1... | collective-permute-start | bytes 98312 | tf_op jit(solution)/shard_map/ppermute | solution.py:17
  87.8 10.8 %collective-permute-start.16 = (bf16[128,128]{1,0:T(8,128)(2,1)S(1)}, bf16[128,128]{1,0:T(8,128)(2,1)S(1)}, u32[]{:S(2)}, u32[]{:S(2)}) collective-permute-start(bf16[128,128]{1,0:T(8,128)(2,1)S(1)} %get-tuple-element.17), channel_id=1, source_target_pairs={{1,0},{2,1},{3,2},{4,3},{5,4},{6,5},{7,6},{8,7},{9,8},{10,9},{11,1... | collective-permute-start | bytes 98312 | tf_op jit(solution)/shard_map/ppermute | solution.py:17
  89.7 8.9 %collective-permute-start.19 = (bf16[128,128]{1,0:T(8,128)(2,1)S(1)}, bf16[128,128]{1,0:T(8,128)(2,1)S(1)}, u32[]{:S(2)}, u32[]{:S(2)}) collective-permute-start(bf16[128,128]{1,0:T(8,128)(2,1)S(1)} %get-tuple-element.18), channel_id=1, source_target_pairs={{0,16},{1,17},{2,18},{3,19},{4,20},{5,21},{6,22},{7,23},{8,24},{9,... | collective-permute-start | bytes 98312 | tf_op jit(solution)/shard_map/ppermute | solution.py:17
  95.2 6.7 %collective-permute-start.18 = (bf16[128,128]{1,0:T(8,128)(2,1)S(1)}, bf16[128,128]{1,0:T(8,128)(2,1)S(1)}, u32[]{:S(2)}, u32[]{:S(2)}) collective-permute-start(bf16[128,128]{1,0:T(8,128)(2,1)S(1)} %get-tuple-element.19), channel_id=1, source_target_pairs={{16,0},{17,1},{18,2},{19,3},{20,4},{21,5},{22,6},{23,7},{24,8},{25... | collective-permute-start | bytes 98312 | tf_op jit(solution)/shard_map/ppermute | solution.py:17
  96.5 7.1 %collective-permute-start.17 = (bf16[128,128]{1,0:T(8,128)(2,1)S(1)}, bf16[128,128]{1,0:T(8,128)(2,1)}, u32[]{:S(2)}, u32[]{:S(2)}) collective-permute-start(bf16[128,128]{1,0:T(8,128)(2,1)S(1)} %get-tuple-element.20), channel_id=1, source_target_pairs={{0,1},{1,2},{2,3},{3,4},{4,5},{5,6},{6,7},{7,8},{8,9},{9,10},{10,1... | collective-permute-start | bytes 98312 | tf_op jit(solution)/shard_map/ppermute | solution.py:17
  107.6 17.6 %copy-start.2 = (f32[1024,128]{0,1:T(8,128)S(1)}, f32[1024,128]{0,1:T(8,128)}, u32[]{:S(2)}) copy-start(f32[1024,128]{0,1:T(8,128)} %copy-done.1) | copy-start | bytes 1572868
  107.6 17.6 %copy-start.7 = (bf16[1024,128]{1,0:T(8,128)(2,1)S(1)}, bf16[1024,128]{1,0:T(8,128)(2,1)}, u32[]{:S(2)}) copy-start(bf16[1024,128]{1,0:T(8,128)(2,1)} %get-tuple-element.49) | copy-start | bytes 786436
  107.6 17.6 %copy-start.11 = (bf16[1024,128]{1,0:T(8,128)(2,1)S(1)}, bf16[1024,128]{1,0:T(8,128)(2,1)}, u32[]{:S(2)}) copy-start(bf16[1024,128]{1,0:T(8,128)(2,1)} %get-tuple-element.50) | copy-start | bytes 786436
  107.6 17.6 %copy-start.15 = (bf16[1024,128]{1,0:T(8,128)(2,1)S(1)}, bf16[1024,128]{1,0:T(8,128)(2,1)}, u32[]{:S(2)}) copy-start(bf16[1024,128]{1,0:T(8,128)(2,1)} %get-tuple-element.51) | copy-start | bytes 786436
  107.6 17.6 %copy-start.19 = (bf16[1024,128]{1,0:T(8,128)(2,1)S(1)}, bf16[1024,128]{1,0:T(8,128)(2,1)}, u32[]{:S(2)}) copy-start(bf16[1024,128]{1,0:T(8,128)(2,1)} %get-tuple-element.52) | copy-start | bytes 786436
  107.6 17.6 %copy-start.26 = (f32[1024,128]{0,1:T(8,128)S(1)}, f32[1024,128]{0,1:T(8,128)}, u32[]{:S(2)}) copy-start(f32[1024,128]{0,1:T(8,128)} %fusion.95) | copy-start | bytes 1572868
  109.4 10.8 %collective-permute-start.20 = (bf16[128,128]{1,0:T(8,128)(2,1)S(1)}, bf16[128,128]{1,0:T(8,128)(2,1)S(1)}, u32[]{:S(2)}, u32[]{:S(2)}) collective-permute-start(bf16[128,128]{1,0:T(8,128)(2,1)S(1)} %get-tuple-element.13), channel_id=1, source_target_pairs={{1,0},{2,1},{3,2},{4,3},{5,4},{6,5},{7,6},{8,7},{9,8},{10,9},{11,1... | collective-permute-start | bytes 98312 | tf_op jit(solution)/shard_map/ppermute | solution.py:17
  111.4 8.9 %collective-permute-start.23 = (bf16[128,128]{1,0:T(8,128)(2,1)S(1)}, bf16[128,128]{1,0:T(8,128)(2,1)S(1)}, u32[]{:S(2)}, u32[]{:S(2)}) collective-permute-start(bf16[128,128]{1,0:T(8,128)(2,1)S(1)} %get-tuple-element.14), channel_id=1, source_target_pairs={{0,16},{1,17},{2,18},{3,19},{4,20},{5,21},{6,22},{7,23},{8,24},{9,... | collective-permute-start | bytes 98312 | tf_op jit(solution)/shard_map/ppermute | solution.py:17
  116.8 6.7 %collective-permute-start.22 = (bf16[128,128]{1,0:T(8,128)(2,1)S(1)}, bf16[128,128]{1,0:T(8,128)(2,1)S(1)}, u32[]{:S(2)}, u32[]{:S(2)}) collective-permute-start(bf16[128,128]{1,0:T(8,128)(2,1)S(1)} %get-tuple-element.15), channel_id=1, source_target_pairs={{16,0},{17,1},{18,2},{19,3},{20,4},{21,5},{22,6},{23,7},{24,8},{25... | collective-permute-start | bytes 98312 | tf_op jit(solution)/shard_map/ppermute | solution.py:17
  118.1 7.0 %collective-permute-start.21 = (bf16[128,128]{1,0:T(8,128)(2,1)S(1)}, bf16[128,128]{1,0:T(8,128)(2,1)S(1)}, u32[]{:S(2)}, u32[]{:S(2)}) collective-permute-start(bf16[128,128]{1,0:T(8,128)(2,1)S(1)} %get-tuple-element.16), channel_id=1, source_target_pairs={{0,1},{1,2},{2,3},{3,4},{4,5},{5,6},{6,7},{7,8},{8,9},{9,10},{10,1... | collective-permute-start | bytes 98312 | tf_op jit(solution)/shard_map/ppermute | solution.py:17
  127.6 10.9 %collective-permute-start.24 = (bf16[128,128]{1,0:T(8,128)(2,1)S(1)}, bf16[128,128]{1,0:T(8,128)(2,1)S(1)}, u32[]{:S(2)}, u32[]{:S(2)}) collective-permute-start(bf16[128,128]{1,0:T(8,128)(2,1)S(1)} %get-tuple-element.9), channel_id=1, source_target_pairs={{1,0},{2,1},{3,2},{4,3},{5,4},{6,5},{7,6},{8,7},{9,8},{10,9},{11,1... | collective-permute-start | bytes 98312 | tf_op jit(solution)/shard_map/ppermute | solution.py:17
  129.5 9.0 %collective-permute-start.27 = (bf16[128,128]{1,0:T(8,128)(2,1)S(1)}, bf16[128,128]{1,0:T(8,128)(2,1)S(1)}, u32[]{:S(2)}, u32[]{:S(2)}) collective-permute-start(bf16[128,128]{1,0:T(8,128)(2,1)S(1)} %get-tuple-element.10), channel_id=1, source_target_pairs={{0,16},{1,17},{2,18},{3,19},{4,20},{5,21},{6,22},{7,23},{8,24},{9,... | collective-permute-start | bytes 98312 | tf_op jit(solution)/shard_map/ppermute | solution.py:17
  135.0 6.7 %collective-permute-start.26 = (bf16[128,128]{1,0:T(8,128)(2,1)S(1)}, bf16[128,128]{1,0:T(8,128)(2,1)S(1)}, u32[]{:S(2)}, u32[]{:S(2)}) collective-permute-start(bf16[128,128]{1,0:T(8,128)(2,1)S(1)} %get-tuple-element.11), channel_id=1, source_target_pairs={{16,0},{17,1},{18,2},{19,3},{20,4},{21,5},{22,6},{23,7},{24,8},{25... | collective-permute-start | bytes 98312 | tf_op jit(solution)/shard_map/ppermute | solution.py:17
  136.3 7.1 %collective-permute-start.25 = (bf16[128,128]{1,0:T(8,128)(2,1)S(1)}, bf16[128,128]{1,0:T(8,128)(2,1)}, u32[]{:S(2)}, u32[]{:S(2)}) collective-permute-start(bf16[128,128]{1,0:T(8,128)(2,1)S(1)} %get-tuple-element.12), channel_id=1, source_target_pairs={{0,1},{1,2},{2,3},{3,4},{4,5},{5,6},{6,7},{7,8},{8,9},{9,10},{10,1... | collective-permute-start | bytes 98312 | tf_op jit(solution)/shard_map/ppermute | solution.py:17
  149.4 10.8 %collective-permute-start.28 = (bf16[128,128]{1,0:T(8,128)(2,1)S(1)}, bf16[128,128]{1,0:T(8,128)(2,1)S(1)}, u32[]{:S(2)}, u32[]{:S(2)}) collective-permute-start(bf16[128,128]{1,0:T(8,128)(2,1)S(1)} %get-tuple-element.5), channel_id=1, source_target_pairs={{1,0},{2,1},{3,2},{4,3},{5,4},{6,5},{7,6},{8,7},{9,8},{10,9},{11,1... | collective-permute-start | bytes 98312 | tf_op jit(solution)/shard_map/ppermute | solution.py:17
  151.3 8.9 %collective-permute-start.31 = (bf16[128,128]{1,0:T(8,128)(2,1)S(1)}, bf16[128,128]{1,0:T(8,128)(2,1)S(1)}, u32[]{:S(2)}, u32[]{:S(2)}) collective-permute-start(bf16[128,128]{1,0:T(8,128)(2,1)S(1)} %get-tuple-element.6), channel_id=1, source_target_pairs={{0,16},{1,17},{2,18},{3,19},{4,20},{5,21},{6,22},{7,23},{8,24},{9,... | collective-permute-start | bytes 98312 | tf_op jit(solution)/shard_map/ppermute | solution.py:17
  156.7 6.7 %collective-permute-start.30 = (bf16[128,128]{1,0:T(8,128)(2,1)S(1)}, bf16[128,128]{1,0:T(8,128)(2,1)S(1)}, u32[]{:S(2)}, u32[]{:S(2)}) collective-permute-start(bf16[128,128]{1,0:T(8,128)(2,1)S(1)} %get-tuple-element.7), channel_id=1, source_target_pairs={{16,0},{17,1},{18,2},{19,3},{20,4},{21,5},{22,6},{23,7},{24,8},{25... | collective-permute-start | bytes 98312 | tf_op jit(solution)/shard_map/ppermute | solution.py:17
  158.0 7.0 %collective-permute-start.29 = (bf16[128,128]{1,0:T(8,128)(2,1)S(1)}, bf16[128,128]{1,0:T(8,128)(2,1)S(1)}, u32[]{:S(2)}, u32[]{:S(2)}) collective-permute-start(bf16[128,128]{1,0:T(8,128)(2,1)S(1)} %get-tuple-element.8), channel_id=1, source_target_pairs={{0,1},{1,2},{2,3},{3,4},{4,5},{5,6},{6,7},{7,8},{8,9},{9,10},{10,1... | collective-permute-start | bytes 98312 | tf_op jit(solution)/shard_map/ppermute | solution.py:17
  (12 other events, 122.3 us)
where the time goes:
time: 169 us; the launch traced here: 167 us
  starting transfers between devices  90.3 us (53%)
  waiting for transfers between devices  34.7 us (21%)
  matrix products  29.3 us (17%)
  local copies, waits for them, and re-layouts  5.97 us (4%)
  other arithmetic  4.7 us (3%)
    ppermute x32, starting transfers between devices, from_behind(): return lax.ppermute(block, axis, route)  90.3 us
    ppermute x32, waiting for transfers between devices, from_behind(): return lax.ppermute(block, axis, route)  34.7 us
    dot_general x4, matrix products, neumann_product(): return jnp.dot(n_mat, scaled, preferred_element_type=jnp.float32)  16 us
    dot_general x8, matrix products, select_rows(): lax.dot_general(picker, block, (((0,), (0,)), ((), ())), preferred_elemen...  9.55 us
    mul x2, other arithmetic, body(): one_hot(links[slot]) * live[slot]  4.34 us
  transfers between devices with their start and end apart: 32, of which 14 were waited for; matrix products, arithmetic and copies ran while one was open for 3% of the time, Pallas kernels for 0%

commit v1 on v0

v1 whole, which is shorter than its diff:
```python
import jax
import jax.numpy as jnp
from jax import lax
from jax.sharding import PartitionSpec as P

ITERS = 4
FAR = 16
DAMPING = 0.7


def swaps(count):
    near = [(i, i ^ 1) for i in range(count)]
    cross = [(i, ((i + 1) ^ 1) - 1) for i in range(count)]
    cross = [(i, j % count) for i, j in cross]
    blocks = count // FAR
    far = [(i, i ^ FAR) for i in range(count)] if blocks > 1 else []
    pairs = [far, near, cross]
    if blocks > 2:
        again = [(i, (((i // FAR + 1) ^ 1) - 1) % blocks * FAR + i % FAR) for i in range(count)]
        pairs = [far, again, near, cross]
    return [p for p in pairs if p]


def slots_of(index, count):
    odd = index % 2
    block = index // FAR % 2
    far, again = 2 + block, 3 - block
    if count // FAR > 2:
        return [far, again, odd, 1 - odd]
    return [far, odd, 1 - odd]


def body(right_side, schur, neumann, weights, neighbours, counts, shared_rows):
    rhs16 = right_side[0]
    rhs = rhs16.astype(jnp.float32)
    s_mat = schur[0]
    n_mat = neumann[0]
    weight = weights[0][:, None]
    count = counts[0]
    width = s_mat.shape[0]
    share = shared_rows.shape[2]
    subs = lax.axis_size("sub")
    routes = swaps(subs)
    slots = slots_of(lax.axis_index("sub"), subs)
    rows = jnp.concatenate([lax.dynamic_index_in_dim(shared_rows[0], k, 0, False) for k in slots])
    live = jnp.concatenate(
        [jnp.broadcast_to(lax.dynamic_index_in_dim(neighbours[0], k, 0, True) >= 0, (share,)) for k in slots]
    )
    mask = (jnp.arange(width) < count).astype(jnp.float32)[:, None]
    hot = (jnp.arange(width)[:, None] == rows[None, :]) & live[None, :]
    placer = hot.astype(jnp.bfloat16)
    picked_weight = jnp.sum(jnp.where(hot, weight, 0.0), 0)[:, None]
    picked_rhs = lax.dot_general(placer, rhs16, (((0,), (0,)), ((), ())), preferred_element_type=jnp.float32)
    picked_s = jnp.dot(s_mat, placer, preferred_element_type=jnp.float32).astype(jnp.bfloat16)
    picked_n = lax.dot_general(
        placer, n_mat, (((0,), (0,)), ((), ())), preferred_element_type=jnp.float32
    ).astype(jnp.bfloat16)
    mask_weight = mask * weight

    def exchange(packed):
        parts = [
            lax.ppermute(packed[k * share : (k + 1) * share], "sub", route) for k, route in enumerate(routes)
        ]
        return jnp.dot(placer, jnp.concatenate(parts, 0), preferred_element_type=jnp.float32)

    def transposed(mat, block):
        return lax.dot_general(mat, block, (((0,), (0,)), ((), ())), preferred_element_type=jnp.float32)

    solution = jnp.zeros(rhs.shape, jnp.float32)
    for step in range(ITERS):
        current = solution.astype(jnp.bfloat16)
        arrived = exchange((picked_rhs - transposed(picked_s, current)).astype(jnp.bfloat16))
        local = mask * (rhs - transposed(s_mat, current))
        scaled = (weight * (local + arrived)).astype(jnp.bfloat16)
        sent = picked_weight * jnp.dot(picked_n, scaled, preferred_element_type=jnp.float32)
        arrived = exchange(sent.astype(jnp.bfloat16))
        weighted = mask_weight * jnp.dot(n_mat, scaled, preferred_element_type=jnp.float32)
        solution = solution + DAMPING * (weighted + arrived)
    return solution[None]


def solution(mesh):
    in_specs = (
        P("sub", None, None),
        P("sub", None, None),
        P("sub", None, None),
        P("sub", None),
        P("sub", None),
        P("sub"),
        P("sub", None, None),
    )
    out_specs = P("sub", None, None)
    return jax.shard_map(body, mesh=mesh, in_specs=in_specs, out_specs=out_specs, check_vma=False)
```

time: 169 us -> 81.7 us (0.48)
  the two profiles are of different devices: /device:TPU:8 before, /device:TPU:0 now
where the time goes in v1:
time: 81.7 us; the launch traced here: 81.5 us
  waiting for transfers between devices  35 us (43%)
  starting transfers between devices  21.2 us (26%)
  matrix products  17.5 us (21%)
  local copies, waits for them, and re-layouts  4.48 us (5%)
  between operations  2.94 us (4%)
    ppermute x24, waiting for transfers between devices, exchange(): lax.ppermute(packed[k * share:(k + 1) * share], 'sub', route)  35 us
    ppermute x24, starting transfers between devices, exchange(): lax.ppermute(packed[k * share:(k + 1) * share], 'sub', route)  21.2 us
    dot_general x8, matrix products, exchange(): jnp.dot(placer, jnp.concatenate(parts, 0), preferred_element_type=jnp.flo...  4.28 us
    dot_general x8, matrix products, transposed(): lax.dot_general(mat, block, (((0,), (0,)), ((), ())), preferred_element_t...  3.32 us
    dot_general x4, matrix products, body(): jnp.dot(n_mat, scaled, preferred_element_type=jnp.float32)  3.32 us
    dot_general x1, matrix products, body(): lax.dot_general(placer, n_mat, (((0,), (0,)), ((), ())), preferred_elemen...  2.62 us
  transfers between devices with their start and end apart: 24, of which 14 were waited for; matrix products, arithmetic and copies ran while one was open for 11% of the time, Pallas kernels for 0%

profile of v1, /device:TPU:0, one launch (start us, length us, event | category | flops | bytes accessed | tf_op | source)
XLA Modules:
  0.0 81.5 jit_solution(13852377290205355177)
XLA Ops:
  0.0 1.5 %constant_dynamic-slice_fusion.2 = (s32[1,1]{1,0:T(1,128)}, s32[1,1]{1,0:T(1,128)}, s32[1,1]{1,0:T(1,128)}) fusion(s32[1,4]{1,0:T(1,128)} %param.11, s32[]{:T(128)S(6)} %select_n.35, s32[]{:T(128)S(6)} %select_n.38, s32[]{:T(128)S(6)} %select_n.37), kind=kLoop, calls=%fused_computation.173 | loop fusion | bytes 36 | tf_op jit(solution)/shard_map/jit(dynamic_index_in_dim)/dynamic_slice | solution.py:47
  3.4 0.8 fusion.263
  4.2 1.4 %fusion.188 = f32[384,128]{1,0:T(8,128)S(1)} fusion(s32[384]{0:T(512)S(1)} %pad_add_fusion, pred[384]{0:T(512)(128)(4,1)S(1)} %pad_add_fusion.1, bf16[1,1024,128]{2,1,0:T(8,128)(2,1)} %param.7), kind=kOutput, calls=%fused_computation.94 | convolution fusion | flops 101842944 | bytes 460672 | tf_op jit(solution)/shard_map/dot_general | solution.py:53
  5.7 1.0 %fusion.44 = bf16[384,1024]{1,0:T(8,128)(2,1)S(1)} fusion(bf16[1,1024,1024]{2,1,0:T(8,128)(2,1)S(1)} %copy-done, s32[384]{0:T(512)S(1)} %pad_add_fusion, pred[384]{0:T(512)(128)(4,1)S(1)} %pad_add_fusion.1), kind=kOutput, calls=%fused_computation.33 | convolution fusion | flops 806879232 | bytes 2885504 | tf_op jit(solution)/shard_map/dot_general | solution.py:54
  7.1 4.1 %collective-permute-start = (bf16[128,128]{1,0:T(8,128)(2,1)S(1)}, bf16[128,128]{1,0:T(8,128)(2,1)S(1)}, u32[]{:S(2)}, u32[]{:S(2)}) collective-permute-start(bf16[128,128]{1,0:T(8,128)(2,1)S(1)} %get-tuple-element.26), channel_id=1, source_target_pairs={{0,16},{1,17},{2,18},{3,19},{4,20},{5,21},{6,22},{7,23},{8,24},{9,... | collective-permute-start | bytes 98312 | tf_op jit(solution)/shard_map/ppermute | solution.py:62
  11.2 2.4 %collective-permute-start.2 = (bf16[128,128]{1,0:T(8,128)(2,1)S(1)}, bf16[128,128]{1,0:T(8,128)(2,1)S(1)}, u32[]{:S(2)}, u32[]{:S(2)}) collective-permute-start(bf16[128,128]{1,0:T(8,128)(2,1)S(1)} %get-tuple-element.27), channel_id=1, source_target_pairs={{0,31},{1,2},{2,1},{3,4},{4,3},{5,6},{6,5},{7,8},{8,7},{9,10},{10,... | collective-permute-start | bytes 98312 | tf_op jit(solution)/shard_map/ppermute | solution.py:62
  13.6 1.1 %copy.18 = bf16[1,1024,128]{1,2,0:T(8,128)(2,1)S(1)} copy(bf16[1,1024,128]{2,1,0:T(8,128)(2,1)} %param.7) | data formatting | bytes 524288 | tf_op args[0]
  15.3 2.6 %fusion.39 = bf16[384,1024]{1,0:T(8,128)(2,1)S(1)} fusion(bf16[1,1024,1024]{2,1,0:T(8,128)(2,1)} %param.9, s32[384]{0:T(512)S(1)} %pad_add_fusion, pred[384]{0:T(512)(128)(4,1)S(1)} %pad_add_fusion.1), kind=kOutput, calls=%fused_computation.32 | convolution fusion | flops 806486016 | bytes 2885504 | tf_op jit(solution)/shard_map/dot_general | solution.py:55
  18.9 0.5 fusion.167
  19.8 1.7 %collective-permute-start.3 = (bf16[128,128]{1,0:T(8,128)(2,1)S(1)}, bf16[128,128]{1,0:T(8,128)(2,1)S(1)}, u32[]{:S(2)}, u32[]{:S(2)}) collective-permute-start(bf16[128,128]{1,0:T(8,128)(2,1)S(1)} %get-tuple-element.23), channel_id=1, source_target_pairs={{0,16},{1,17},{2,18},{3,19},{4,20},{5,21},{6,22},{7,23},{8,24},{9,... | collective-permute-start | bytes 98312 | tf_op jit(solution)/shard_map/ppermute | solution.py:62
  21.5 1.6 %collective-permute-start.5 = (bf16[128,128]{1,0:T(8,128)(2,1)S(1)}, bf16[128,128]{1,0:T(8,128)(2,1)S(1)}, u32[]{:S(2)}, u32[]{:S(2)}) collective-permute-start(bf16[128,128]{1,0:T(8,128)(2,1)S(1)} %get-tuple-element.24), channel_id=1, source_target_pairs={{0,31},{1,2},{2,1},{3,4},{4,3},{5,6},{6,5},{7,8},{8,7},{9,10},{10,... | collective-permute-start | bytes 98312 | tf_op jit(solution)/shard_map/ppermute | solution.py:62
  23.1 0.8 %fusion.146 = f32[1024,128]{0,1:T(8,128)S(1)} fusion(bf16[1024,128]{0,1:T(8,128)(2,1)S(1)} %fusion.167, bf16[1,1024,1024]{2,1,0:T(8,128)(2,1)S(1)} %copy-done.1, f32[1024]{0:T(1024)S(1)} %fusion.262), kind=kOutput, calls=%fused_computation.67 | convolution fusion | flops 268566528 | bytes 2887680 | tf_op jit(solution)/shard_map/dot_general | solution.py:77
  24.0 1.3 %collective-permute-done.3 = bf16[128,128]{1,0:T(8,128)(2,1)S(1)} collective-permute-done((bf16[128,128]{1,0:T(8,128)(2,1)S(1)}, bf16[128,128]{1,0:T(8,128)(2,1)S(1)}, u32[]{:S(2)}, u32[]{:S(2)}) %collective-permute-start.3) | collective-permute-done | bytes 32800 | tf_op jit(solution)/shard_map/ppermute | solution.py:62
  25.3 3.2 %collective-permute-done.5 = bf16[128,128]{1,0:T(8,128)(2,1)S(1)} collective-permute-done((bf16[128,128]{1,0:T(8,128)(2,1)S(1)}, bf16[128,128]{1,0:T(8,128)(2,1)S(1)}, u32[]{:S(2)}, u32[]{:S(2)}) %collective-permute-start.5) | collective-permute-done | bytes 32800 | tf_op jit(solution)/shard_map/ppermute | solution.py:62
  28.5 0.5 fusion.128
  29.5 1.8 %collective-permute-start.8 = (bf16[128,128]{1,0:T(8,128)(2,1)S(1)}, bf16[128,128]{1,0:T(8,128)(2,1)S(1)}, u32[]{:S(2)}, u32[]{:S(2)}) collective-permute-start(bf16[128,128]{1,0:T(8,128)(2,1)S(1)} %get-tuple-element.21), channel_id=1, source_target_pairs={{0,31},{1,2},{2,1},{3,4},{4,3},{5,6},{6,5},{7,8},{8,7},{9,10},{10,... | collective-permute-start | bytes 98312 | tf_op jit(solution)/shard_map/ppermute | solution.py:62
  31.3 0.5 fusion.98
  31.8 2.5 %collective-permute-done.6 = bf16[128,128]{1,0:T(8,128)(2,1)S(1)} collective-permute-done((bf16[128,128]{1,0:T(8,128)(2,1)S(1)}, bf16[128,128]{1,0:T(8,128)(2,1)S(1)}, u32[]{:S(2)}, u32[]{:S(2)}) %collective-permute-start.6) | collective-permute-done | bytes 32800 | tf_op jit(solution)/shard_map/ppermute | solution.py:62
  34.3 2.2 %collective-permute-done.8 = bf16[128,128]{1,0:T(8,128)(2,1)S(1)} collective-permute-done((bf16[128,128]{1,0:T(8,128)(2,1)S(1)}, bf16[128,128]{1,0:T(8,128)(2,1)S(1)}, u32[]{:S(2)}, u32[]{:S(2)}) %collective-permute-start.8) | collective-permute-done | bytes 32800 | tf_op jit(solution)/shard_map/ppermute | solution.py:62
  36.5 0.5 fusion.170
  37.4 1.1 %collective-permute-start.9 = (bf16[128,128]{1,0:T(8,128)(2,1)S(1)}, bf16[128,128]{1,0:T(8,128)(2,1)S(1)}, u32[]{:S(2)}, u32[]{:S(2)}) collective-permute-start(bf16[128,128]{1,0:T(8,128)(2,1)S(1)} %get-tuple-element.17), channel_id=1, source_target_pairs={{0,16},{1,17},{2,18},{3,19},{4,20},{5,21},{6,22},{7,23},{8,24},{9,... | collective-permute-start | bytes 98312 | tf_op jit(solution)/shard_map/ppermute | solution.py:62
  38.5 1.0 %collective-permute-start.11 = (bf16[128,128]{1,0:T(8,128)(2,1)S(1)}, bf16[128,128]{1,0:T(8,128)(2,1)S(1)}, u32[]{:S(2)}, u32[]{:S(2)}) collective-permute-start(bf16[128,128]{1,0:T(8,128)(2,1)S(1)} %get-tuple-element.18), channel_id=1, source_target_pairs={{0,31},{1,2},{2,1},{3,4},{4,3},{5,6},{6,5},{7,8},{8,7},{9,10},{10,... | collective-permute-start | bytes 98312 | tf_op jit(solution)/shard_map/ppermute | solution.py:62
  39.6 0.8 %fusion.152 = f32[1024,128]{0,1:T(8,128)S(1)} fusion(bf16[1024,128]{0,1:T(8,128)(2,1)S(1)} %fusion.170, bf16[1,1024,1024]{2,1,0:T(8,128)(2,1)S(1)} %copy-done.1, f32[1024]{0:T(1024)S(1)} %fusion.262), kind=kOutput, calls=%fused_computation.69 | convolution fusion | flops 268566528 | bytes 2887680 | tf_op jit(solution)/shard_map/dot_general | solution.py:77
  40.4 1.9 %collective-permute-done.9 = bf16[128,128]{1,0:T(8,128)(2,1)S(1)} collective-permute-done((bf16[128,128]{1,0:T(8,128)(2,1)S(1)}, bf16[128,128]{1,0:T(8,128)(2,1)S(1)}, u32[]{:S(2)}, u32[]{:S(2)}) %collective-permute-start.9) | collective-permute-done | bytes 32800 | tf_op jit(solution)/shard_map/ppermute | solution.py:62
  42.3 3.3 %collective-permute-done.11 = bf16[128,128]{1,0:T(8,128)(2,1)S(1)} collective-permute-done((bf16[128,128]{1,0:T(8,128)(2,1)S(1)}, bf16[128,128]{1,0:T(8,128)(2,1)S(1)}, u32[]{:S(2)}, u32[]{:S(2)}) %collective-permute-start.11) | collective-permute-done | bytes 32800 | tf_op jit(solution)/shard_map/ppermute | solution.py:62
  45.6 0.5 fusion.122
  46.7 1.6 %collective-permute-start.14 = (bf16[128,128]{1,0:T(8,128)(2,1)S(1)}, bf16[128,128]{1,0:T(8,128)(2,1)S(1)}, u32[]{:S(2)}, u32[]{:S(2)}) collective-permute-start(bf16[128,128]{1,0:T(8,128)(2,1)S(1)} %get-tuple-element.15), channel_id=1, source_target_pairs={{0,31},{1,2},{2,1},{3,4},{4,3},{5,6},{6,5},{7,8},{8,7},{9,10},{10,... | collective-permute-start | bytes 98312 | tf_op jit(solution)/shard_map/ppermute | solution.py:62
  48.3 0.5 fusion.92
  48.7 3.0 %collective-permute-done.12 = bf16[128,128]{1,0:T(8,128)(2,1)S(1)} collective-permute-done((bf16[128,128]{1,0:T(8,128)(2,1)S(1)}, bf16[128,128]{1,0:T(8,128)(2,1)S(1)}, u32[]{:S(2)}, u32[]{:S(2)}) %collective-permute-start.12) | collective-permute-done | bytes 32800 | tf_op jit(solution)/shard_map/ppermute | solution.py:62
  51.8 1.9 %collective-permute-done.14 = bf16[128,128]{1,0:T(8,128)(2,1)S(1)} collective-permute-done((bf16[128,128]{1,0:T(8,128)(2,1)S(1)}, bf16[128,128]{1,0:T(8,128)(2,1)S(1)}, u32[]{:S(2)}, u32[]{:S(2)}) %collective-permute-start.14) | collective-permute-done | bytes 32800 | tf_op jit(solution)/shard_map/ppermute | solution.py:62
  53.6 0.5 fusion.173
  54.6 1.4 %collective-permute-start.15 = (bf16[128,128]{1,0:T(8,128)(2,1)S(1)}, bf16[128,128]{1,0:T(8,128)(2,1)S(1)}, u32[]{:S(2)}, u32[]{:S(2)}) collective-permute-start(bf16[128,128]{1,0:T(8,128)(2,1)S(1)} %get-tuple-element.11), channel_id=1, source_target_pairs={{0,16},{1,17},{2,18},{3,19},{4,20},{5,21},{6,22},{7,23},{8,24},{9,... | collective-permute-start | bytes 98312 | tf_op jit(solution)/shard_map/ppermute | solution.py:62
  56.0 1.0 %collective-permute-start.17 = (bf16[128,128]{1,0:T(8,128)(2,1)S(1)}, bf16[128,128]{1,0:T(8,128)(2,1)S(1)}, u32[]{:S(2)}, u32[]{:S(2)}) collective-permute-start(bf16[128,128]{1,0:T(8,128)(2,1)S(1)} %get-tuple-element.12), channel_id=1, source_target_pairs={{0,31},{1,2},{2,1},{3,4},{4,3},{5,6},{6,5},{7,8},{8,7},{9,10},{10,... | collective-permute-start | bytes 98312 | tf_op jit(solution)/shard_map/ppermute | solution.py:62
  57.0 0.8 %fusion.158 = f32[1024,128]{0,1:T(8,128)S(1)} fusion(bf16[1024,128]{0,1:T(8,128)(2,1)S(1)} %fusion.173, bf16[1,1024,1024]{2,1,0:T(8,128)(2,1)S(1)} %copy-done.1, f32[1024]{0:T(1024)S(1)} %fusion.262), kind=kOutput, calls=%fused_computation.71 | convolution fusion | flops 268566528 | bytes 2887680 | tf_op jit(solution)/shard_map/dot_general | solution.py:77
  57.8 1.6 %collective-permute-done.15 = bf16[128,128]{1,0:T(8,128)(2,1)S(1)} collective-permute-done((bf16[128,128]{1,0:T(8,128)(2,1)S(1)}, bf16[128,128]{1,0:T(8,128)(2,1)S(1)}, u32[]{:S(2)}, u32[]{:S(2)}) %collective-permute-start.15) | collective-permute-done | bytes 32800 | tf_op jit(solution)/shard_map/ppermute | solution.py:62
  59.4 3.4 %collective-permute-done.17 = bf16[128,128]{1,0:T(8,128)(2,1)S(1)} collective-permute-done((bf16[128,128]{1,0:T(8,128)(2,1)S(1)}, bf16[128,128]{1,0:T(8,128)(2,1)S(1)}, u32[]{:S(2)}, u32[]{:S(2)}) %collective-permute-start.17) | collective-permute-done | bytes 32800 | tf_op jit(solution)/shard_map/ppermute | solution.py:62
  62.9 0.5 fusion.113
  63.9 1.3 %collective-permute-start.20 = (bf16[128,128]{1,0:T(8,128)(2,1)S(1)}, bf16[128,128]{1,0:T(8,128)(2,1)S(1)}, u32[]{:S(2)}, u32[]{:S(2)}) collective-permute-start(bf16[128,128]{1,0:T(8,128)(2,1)S(1)} %get-tuple-element.9), channel_id=1, source_target_pairs={{0,31},{1,2},{2,1},{3,4},{4,3},{5,6},{6,5},{7,8},{8,7},{9,10},{10,... | collective-permute-start | bytes 98312 | tf_op jit(solution)/shard_map/ppermute | solution.py:62
  65.7 3.1 %collective-permute-done.18 = bf16[128,128]{1,0:T(8,128)(2,1)S(1)} collective-permute-done((bf16[128,128]{1,0:T(8,128)(2,1)S(1)}, bf16[128,128]{1,0:T(8,128)(2,1)S(1)}, u32[]{:S(2)}, u32[]{:S(2)}) %collective-permute-start.18) | collective-permute-done | bytes 32800 | tf_op jit(solution)/shard_map/ppermute | solution.py:62
  68.7 2.4 %collective-permute-done.20 = bf16[128,128]{1,0:T(8,128)(2,1)S(1)} collective-permute-done((bf16[128,128]{1,0:T(8,128)(2,1)S(1)}, bf16[128,128]{1,0:T(8,128)(2,1)S(1)}, u32[]{:S(2)}, u32[]{:S(2)}) %collective-permute-start.20) | collective-permute-done | bytes 32800 | tf_op jit(solution)/shard_map/ppermute | solution.py:62
  71.1 0.5 fusion.176
  72.0 0.9 %collective-permute-start.21 = (bf16[128,128]{1,0:T(8,128)(2,1)S(1)}, bf16[128,128]{1,0:T(8,128)(2,1)S(1)}, u32[]{:S(2)}, u32[]{:S(2)}) collective-permute-start(bf16[128,128]{1,0:T(8,128)(2,1)S(1)} %get-tuple-element.5), channel_id=1, source_target_pairs={{0,16},{1,17},{2,18},{3,19},{4,20},{5,21},{6,22},{7,23},{8,24},{9,... | collective-permute-start | bytes 98312 | tf_op jit(solution)/shard_map/ppermute | solution.py:62
  73.0 1.0 %collective-permute-start.23 = (bf16[128,128]{1,0:T(8,128)(2,1)S(1)}, bf16[128,128]{1,0:T(8,128)(2,1)S(1)}, u32[]{:S(2)}, u32[]{:S(2)}) collective-permute-start(bf16[128,128]{1,0:T(8,128)(2,1)S(1)} %get-tuple-element.6), channel_id=1, source_target_pairs={{0,31},{1,2},{2,1},{3,4},{4,3},{5,6},{6,5},{7,8},{8,7},{9,10},{10,... | collective-permute-start | bytes 98312 | tf_op jit(solution)/shard_map/ppermute | solution.py:62
  74.0 0.8 %fusion.164 = f32[1024,128]{0,1:T(8,128)S(1)} fusion(bf16[1024,128]{0,1:T(8,128)(2,1)S(1)} %fusion.176, bf16[1,1024,1024]{2,1,0:T(8,128)(2,1)S(1)} %copy-done.1, f32[1024]{0:T(1024)S(1)} %fusion.262), kind=kOutput, calls=%fused_computation.73 | convolution fusion | flops 268566528 | bytes 2887680 | tf_op jit(solution)/shard_map/dot_general | solution.py:77
  74.8 2.1 %collective-permute-done.21 = bf16[128,128]{1,0:T(8,128)(2,1)S(1)} collective-permute-done((bf16[128,128]{1,0:T(8,128)(2,1)S(1)}, bf16[128,128]{1,0:T(8,128)(2,1)S(1)}, u32[]{:S(2)}, u32[]{:S(2)}) %collective-permute-start.21) | collective-permute-done | bytes 32800 | tf_op jit(solution)/shard_map/ppermute | solution.py:62
  76.9 3.0 %collective-permute-done.23 = bf16[128,128]{1,0:T(8,128)(2,1)S(1)} collective-permute-done((bf16[128,128]{1,0:T(8,128)(2,1)S(1)}, bf16[128,128]{1,0:T(8,128)(2,1)S(1)}, u32[]{:S(2)}, u32[]{:S(2)}) %collective-permute-start.23) | collective-permute-done | bytes 32800 | tf_op jit(solution)/shard_map/ppermute | solution.py:62
  79.9 0.5 fusion.140
  80.5 1.0 %copy.27 = f32[1,1024,128]{2,1,0:T(8,128)} copy(f32[1,1024,128]{1,2,0:T(8,128)S(1)} %fusion.140) | data formatting | bytes 1048576 | tf_op jit(solution)/shard_map/broadcast_in_dim | solution.py:79
  (53 shorter events, 4.7 us)
Async XLA Ops:
  0.0 5.7 %copy-start = (bf16[1,1024,1024]{2,1,0:T(8,128)(2,1)S(1)}, bf16[1,1024,1024]{2,1,0:T(8,128)(2,1)}, u32[]{:S(2)}) copy-start(bf16[1,1024,1024]{2,1,0:T(8,128)(2,1)} %param.8) | copy-start | bytes 6291460
  7.1 11.8 %collective-permute-start = (bf16[128,128]{1,0:T(8,128)(2,1)S(1)}, bf16[128,128]{1,0:T(8,128)(2,1)S(1)}, u32[]{:S(2)}, u32[]{:S(2)}) collective-permute-start(bf16[128,128]{1,0:T(8,128)(2,1)S(1)} %get-tuple-element.26), channel_id=1, source_target_pairs={{0,16},{1,17},{2,18},{3,19},{4,20},{5,21},{6,22},{7,23},{8,24},{9,... | collective-permute-start | bytes 98312 | tf_op jit(solution)/shard_map/ppermute | solution.py:62
  11.2 7.7 %collective-permute-start.2 = (bf16[128,128]{1,0:T(8,128)(2,1)S(1)}, bf16[128,128]{1,0:T(8,128)(2,1)S(1)}, u32[]{:S(2)}, u32[]{:S(2)}) collective-permute-start(bf16[128,128]{1,0:T(8,128)(2,1)S(1)} %get-tuple-element.27), channel_id=1, source_target_pairs={{0,31},{1,2},{2,1},{3,4},{4,3},{5,6},{6,5},{7,8},{8,7},{9,10},{10,... | collective-permute-start | bytes 98312 | tf_op jit(solution)/shard_map/ppermute | solution.py:62
  13.6 5.3 %collective-permute-start.1 = (bf16[128,128]{1,0:T(8,128)(2,1)S(1)}, bf16[128,128]{1,0:T(8,128)(2,1)S(1)}, u32[]{:S(2)}, u32[]{:S(2)}) collective-permute-start(bf16[128,128]{1,0:T(8,128)(2,1)S(1)} %get-tuple-element.28), channel_id=1, source_target_pairs={{0,1},{1,0},{2,3},{3,2},{4,5},{5,4},{6,7},{7,6},{8,9},{9,8},{10,11... | collective-permute-start | bytes 98312 | tf_op jit(solution)/shard_map/ppermute | solution.py:62
  15.3 2.6 %copy-start.2 = (f32[1,1024]{1,0:T(1,128)S(1)}, f32[1,1024]{1,0:T(1,128)}, u32[]{:S(2)}) copy-start(f32[1,1024]{1,0:T(1,128)} %param.10) | copy-start | bytes 12292
  18.4 4.7 %copy-start.1 = (bf16[1,1024,1024]{2,1,0:T(8,128)(2,1)S(1)}, bf16[1,1024,1024]{2,1,0:T(8,128)(2,1)}, u32[]{:S(2)}) copy-start(bf16[1,1024,1024]{2,1,0:T(8,128)(2,1)} %param.9) | copy-start | bytes 6291460
  19.8 5.5 %collective-permute-start.3 = (bf16[128,128]{1,0:T(8,128)(2,1)S(1)}, bf16[128,128]{1,0:T(8,128)(2,1)S(1)}, u32[]{:S(2)}, u32[]{:S(2)}) collective-permute-start(bf16[128,128]{1,0:T(8,128)(2,1)S(1)} %get-tuple-element.23), channel_id=1, source_target_pairs={{0,16},{1,17},{2,18},{3,19},{4,20},{5,21},{6,22},{7,23},{8,24},{9,... | collective-permute-start | bytes 98312 | tf_op jit(solution)/shard_map/ppermute | solution.py:62
  21.5 6.9 %collective-permute-start.5 = (bf16[128,128]{1,0:T(8,128)(2,1)S(1)}, bf16[128,128]{1,0:T(8,128)(2,1)S(1)}, u32[]{:S(2)}, u32[]{:S(2)}) collective-permute-start(bf16[128,128]{1,0:T(8,128)(2,1)S(1)} %get-tuple-element.24), channel_id=1, source_target_pairs={{0,31},{1,2},{2,1},{3,4},{4,3},{5,6},{6,5},{7,8},{8,7},{9,10},{10,... | collective-permute-start | bytes 98312 | tf_op jit(solution)/shard_map/ppermute | solution.py:62
  23.1 5.4 %collective-permute-start.4 = (bf16[128,128]{1,0:T(8,128)(2,1)S(1)}, bf16[128,128]{1,0:T(8,128)(2,1)S(1)}, u32[]{:S(2)}, u32[]{:S(2)}) collective-permute-start(bf16[128,128]{1,0:T(8,128)(2,1)S(1)} %get-tuple-element.25), channel_id=1, source_target_pairs={{0,1},{1,0},{2,3},{3,2},{4,5},{5,4},{6,7},{7,6},{8,9},{9,8},{10,11... | collective-permute-start | bytes 98312 | tf_op jit(solution)/shard_map/ppermute | solution.py:62
  29.4 4.9 %collective-permute-start.6 = (bf16[128,128]{1,0:T(8,128)(2,1)S(1)}, bf16[128,128]{1,0:T(8,128)(2,1)S(1)}, u32[]{:S(2)}, u32[]{:S(2)}) collective-permute-start(bf16[128,128]{1,0:T(8,128)(2,1)S(1)} %get-tuple-element.20), channel_id=1, source_target_pairs={{0,16},{1,17},{2,18},{3,19},{4,20},{5,21},{6,22},{7,23},{8,24},{9,... | collective-permute-start | bytes 98312 | tf_op jit(solution)/shard_map/ppermute | solution.py:62
  29.5 7.0 %collective-permute-start.8 = (bf16[128,128]{1,0:T(8,128)(2,1)S(1)}, bf16[128,128]{1,0:T(8,128)(2,1)S(1)}, u32[]{:S(2)}, u32[]{:S(2)}) collective-permute-start(bf16[128,128]{1,0:T(8,128)(2,1)S(1)} %get-tuple-element.21), channel_id=1, source_target_pairs={{0,31},{1,2},{2,1},{3,4},{4,3},{5,6},{6,5},{7,8},{8,7},{9,10},{10,... | collective-permute-start | bytes 98312 | tf_op jit(solution)/shard_map/ppermute | solution.py:62
  31.3 5.2 %collective-permute-start.7 = (bf16[128,128]{1,0:T(8,128)(2,1)S(1)}, bf16[128,128]{1,0:T(8,128)(2,1)S(1)}, u32[]{:S(2)}, u32[]{:S(2)}) collective-permute-start(bf16[128,128]{1,0:T(8,128)(2,1)S(1)} %get-tuple-element.22), channel_id=1, source_target_pairs={{0,1},{1,0},{2,3},{3,2},{4,5},{5,4},{6,7},{7,6},{8,9},{9,8},{10,11... | collective-permute-start | bytes 98312 | tf_op jit(solution)/shard_map/ppermute | solution.py:62
  37.4 4.9 %collective-permute-start.9 = (bf16[128,128]{1,0:T(8,128)(2,1)S(1)}, bf16[128,128]{1,0:T(8,128)(2,1)S(1)}, u32[]{:S(2)}, u32[]{:S(2)}) collective-permute-start(bf16[128,128]{1,0:T(8,128)(2,1)S(1)} %get-tuple-element.17), channel_id=1, source_target_pairs={{0,16},{1,17},{2,18},{3,19},{4,20},{5,21},{6,22},{7,23},{8,24},{9,... | collective-permute-start | bytes 98312 | tf_op jit(solution)/shard_map/ppermute | solution.py:62
  38.5 7.0 %collective-permute-start.11 = (bf16[128,128]{1,0:T(8,128)(2,1)S(1)}, bf16[128,128]{1,0:T(8,128)(2,1)S(1)}, u32[]{:S(2)}, u32[]{:S(2)}) collective-permute-start(bf16[128,128]{1,0:T(8,128)(2,1)S(1)} %get-tuple-element.18), channel_id=1, source_target_pairs={{0,31},{1,2},{2,1},{3,4},{4,3},{5,6},{6,5},{7,8},{8,7},{9,10},{10,... | collective-permute-start | bytes 98312 | tf_op jit(solution)/shard_map/ppermute | solution.py:62
  39.6 6.0 %collective-permute-start.10 = (bf16[128,128]{1,0:T(8,128)(2,1)S(1)}, bf16[128,128]{1,0:T(8,128)(2,1)S(1)}, u32[]{:S(2)}, u32[]{:S(2)}) collective-permute-start(bf16[128,128]{1,0:T(8,128)(2,1)S(1)} %get-tuple-element.19), channel_id=1, source_target_pairs={{0,1},{1,0},{2,3},{3,2},{4,5},{5,4},{6,7},{7,6},{8,9},{9,8},{10,11... | collective-permute-start | bytes 98312 | tf_op jit(solution)/shard_map/ppermute | solution.py:62
  46.5 5.2 %collective-permute-start.12 = (bf16[128,128]{1,0:T(8,128)(2,1)S(1)}, bf16[128,128]{1,0:T(8,128)(2,1)S(1)}, u32[]{:S(2)}, u32[]{:S(2)}) collective-permute-start(bf16[128,128]{1,0:T(8,128)(2,1)S(1)} %get-tuple-element.14), channel_id=1, source_target_pairs={{0,16},{1,17},{2,18},{3,19},{4,20},{5,21},{6,22},{7,23},{8,24},{9,... | collective-permute-start | bytes 98312 | tf_op jit(solution)/shard_map/ppermute | solution.py:62
  46.7 6.9 %collective-permute-start.14 = (bf16[128,128]{1,0:T(8,128)(2,1)S(1)}, bf16[128,128]{1,0:T(8,128)(2,1)S(1)}, u32[]{:S(2)}, u32[]{:S(2)}) collective-permute-start(bf16[128,128]{1,0:T(8,128)(2,1)S(1)} %get-tuple-element.15), channel_id=1, source_target_pairs={{0,31},{1,2},{2,1},{3,4},{4,3},{5,6},{6,5},{7,8},{8,7},{9,10},{10,... | collective-permute-start | bytes 98312 | tf_op jit(solution)/shard_map/ppermute | solution.py:62
  48.3 5.4 %collective-permute-start.13 = (bf16[128,128]{1,0:T(8,128)(2,1)S(1)}, bf16[128,128]{1,0:T(8,128)(2,1)S(1)}, u32[]{:S(2)}, u32[]{:S(2)}) collective-permute-start(bf16[128,128]{1,0:T(8,128)(2,1)S(1)} %get-tuple-element.16), channel_id=1, source_target_pairs={{0,1},{1,0},{2,3},{3,2},{4,5},{5,4},{6,7},{7,6},{8,9},{9,8},{10,11... | collective-permute-start | bytes 98312 | tf_op jit(solution)/shard_map/ppermute | solution.py:62
  54.6 4.9 %collective-permute-start.15 = (bf16[128,128]{1,0:T(8,128)(2,1)S(1)}, bf16[128,128]{1,0:T(8,128)(2,1)S(1)}, u32[]{:S(2)}, u32[]{:S(2)}) collective-permute-start(bf16[128,128]{1,0:T(8,128)(2,1)S(1)} %get-tuple-element.11), channel_id=1, source_target_pairs={{0,16},{1,17},{2,18},{3,19},{4,20},{5,21},{6,22},{7,23},{8,24},{9,... | collective-permute-start | bytes 98312 | tf_op jit(solution)/shard_map/ppermute | solution.py:62
  56.0 6.9 %collective-permute-start.17 = (bf16[128,128]{1,0:T(8,128)(2,1)S(1)}, bf16[128,128]{1,0:T(8,128)(2,1)S(1)}, u32[]{:S(2)}, u32[]{:S(2)}) collective-permute-start(bf16[128,128]{1,0:T(8,128)(2,1)S(1)} %get-tuple-element.12), channel_id=1, source_target_pairs={{0,31},{1,2},{2,1},{3,4},{4,3},{5,6},{6,5},{7,8},{8,7},{9,10},{10,... | collective-permute-start | bytes 98312 | tf_op jit(solution)/shard_map/ppermute | solution.py:62
  57.0 5.9 %collective-permute-start.16 = (bf16[128,128]{1,0:T(8,128)(2,1)S(1)}, bf16[128,128]{1,0:T(8,128)(2,1)S(1)}, u32[]{:S(2)}, u32[]{:S(2)}) collective-permute-start(bf16[128,128]{1,0:T(8,128)(2,1)S(1)} %get-tuple-element.13), channel_id=1, source_target_pairs={{0,1},{1,0},{2,3},{3,2},{4,5},{5,4},{6,7},{7,6},{8,9},{9,8},{10,11... | collective-permute-start | bytes 98312 | tf_op jit(solution)/shard_map/ppermute | solution.py:62
  63.8 4.9 %collective-permute-start.18 = (bf16[128,128]{1,0:T(8,128)(2,1)S(1)}, bf16[128,128]{1,0:T(8,128)(2,1)S(1)}, u32[]{:S(2)}, u32[]{:S(2)}) collective-permute-start(bf16[128,128]{1,0:T(8,128)(2,1)S(1)} %get-tuple-element.8), channel_id=1, source_target_pairs={{0,16},{1,17},{2,18},{3,19},{4,20},{5,21},{6,22},{7,23},{8,24},{9,... | collective-permute-start | bytes 98312 | tf_op jit(solution)/shard_map/ppermute | solution.py:62
  63.9 7.2 %collective-permute-start.20 = (bf16[128,128]{1,0:T(8,128)(2,1)S(1)}, bf16[128,128]{1,0:T(8,128)(2,1)S(1)}, u32[]{:S(2)}, u32[]{:S(2)}) collective-permute-start(bf16[128,128]{1,0:T(8,128)(2,1)S(1)} %get-tuple-element.9), channel_id=1, source_target_pairs={{0,31},{1,2},{2,1},{3,4},{4,3},{5,6},{6,5},{7,8},{8,7},{9,10},{10,... | collective-permute-start | bytes 98312 | tf_op jit(solution)/shard_map/ppermute | solution.py:62
  65.2 5.9 %collective-permute-start.19 = (bf16[128,128]{1,0:T(8,128)(2,1)S(1)}, bf16[128,128]{1,0:T(8,128)(2,1)S(1)}, u32[]{:S(2)}, u32[]{:S(2)}) collective-permute-start(bf16[128,128]{1,0:T(8,128)(2,1)S(1)} %get-tuple-element.10), channel_id=1, source_target_pairs={{0,1},{1,0},{2,3},{3,2},{4,5},{5,4},{6,7},{7,6},{8,9},{9,8},{10,11... | collective-permute-start | bytes 98312 | tf_op jit(solution)/shard_map/ppermute | solution.py:62
  72.0 4.9 %collective-permute-start.21 = (bf16[128,128]{1,0:T(8,128)(2,1)S(1)}, bf16[128,128]{1,0:T(8,128)(2,1)S(1)}, u32[]{:S(2)}, u32[]{:S(2)}) collective-permute-start(bf16[128,128]{1,0:T(8,128)(2,1)S(1)} %get-tuple-element.5), channel_id=1, source_target_pairs={{0,16},{1,17},{2,18},{3,19},{4,20},{5,21},{6,22},{7,23},{8,24},{9,... | collective-permute-start | bytes 98312 | tf_op jit(solution)/shard_map/ppermute | solution.py:62
  73.0 6.9 %collective-permute-start.23 = (bf16[128,128]{1,0:T(8,128)(2,1)S(1)}, bf16[128,128]{1,0:T(8,128)(2,1)S(1)}, u32[]{:S(2)}, u32[]{:S(2)}) collective-permute-start(bf16[128,128]{1,0:T(8,128)(2,1)S(1)} %get-tuple-element.6), channel_id=1, source_target_pairs={{0,31},{1,2},{2,1},{3,4},{4,3},{5,6},{6,5},{7,8},{8,7},{9,10},{10,... | collective-permute-start | bytes 98312 | tf_op jit(solution)/shard_map/ppermute | solution.py:62
  73.9 6.0 %collective-permute-start.22 = (bf16[128,128]{1,0:T(8,128)(2,1)S(1)}, bf16[128,128]{1,0:T(8,128)(2,1)S(1)}, u32[]{:S(2)}, u32[]{:S(2)}) collective-permute-start(bf16[128,128]{1,0:T(8,128)(2,1)S(1)} %get-tuple-element.7), channel_id=1, source_target_pairs={{0,1},{1,0},{2,3},{3,2},{4,5},{5,4},{6,7},{7,6},{8,9},{9,8},{10,11... | collective-permute-start | bytes 98312 | tf_op jit(solution)/shard_map/ppermute | solution.py:62

commit v2 on v1

--- a/solution.py
+++ b/solution.py
@@ -10,8 +10,7 @@
 
 def swaps(count):
     near = [(i, i ^ 1) for i in range(count)]
-    cross = [(i, ((i + 1) ^ 1) - 1) for i in range(count)]
-    cross = [(i, j % count) for i, j in cross]
+    cross = [(i, ((i + 1) ^ 1) - 1) for i in range(1, count - 1)]
     blocks = count // FAR
     far = [(i, i ^ FAR) for i in range(count)] if blocks > 1 else []
     pairs = [far, near, cross]

time: 81.7 us -> 86.5 us (1.059)
  the two profiles are of different devices: /device:TPU:0 before, /device:TPU:8 now
where the time goes in v2:
time: 86.5 us; the launch traced here: 86 us
  starting transfers between devices  35 us (40%)
  waiting for transfers between devices  25.6 us (30%)
  matrix products  17.5 us (20%)
  local copies, waits for them, and re-layouts  4.48 us (5%)
  between operations  3.07 us (4%)
    ppermute x24, starting transfers between devices, exchange(): lax.ppermute(packed[k * share:(k + 1) * share], 'sub', route)  35 us
    ppermute x24, waiting for transfers between devices, exchange(): lax.ppermute(packed[k * share:(k + 1) * share], 'sub', route)  25.6 us
    dot_general x8, matrix products, exchange(): jnp.dot(placer, jnp.concatenate(parts, 0), preferred_element_type=jnp.flo...  4.27 us
    dot_general x4, matrix products, body(): jnp.dot(n_mat, scaled, preferred_element_type=jnp.float32)  3.32 us
    dot_general x8, matrix products, transposed(): lax.dot_general(mat, block, (((0,), (0,)), ((), ())), preferred_element_t...  3.32 us
    dot_general x1, matrix products, body(): lax.dot_general(placer, n_mat, (((0,), (0,)), ((), ())), preferred_elemen...  2.62 us
  transfers between devices with their start and end apart: 24, of which 10 were waited for; matrix products, arithmetic and copies ran while one was open for 11% of the time, Pallas kernels for 0%

profile of v2, /device:TPU:8, one launch (start us, length us, event | category | flops | bytes accessed | tf_op | source)
XLA Modules:
  0.0 86.0 jit_solution(5913420078785991385)
XLA Ops:
  0.0 1.5 %constant_dynamic-slice_fusion.2 = (s32[1,1]{1,0:T(1,128)}, s32[1,1]{1,0:T(1,128)}, s32[1,1]{1,0:T(1,128)}) fusion(s32[1,4]{1,0:T(1,128)} %param.11, s32[]{:T(128)S(6)} %select_n.35, s32[]{:T(128)S(6)} %select_n.38, s32[]{:T(128)S(6)} %select_n.37), kind=kLoop, calls=%fused_computation.173 | loop fusion | bytes 36 | tf_op jit(solution)/shard_map/jit(dynamic_index_in_dim)/dynamic_slice | solution.py:46
  3.4 0.8 fusion.263
  4.2 1.4 %fusion.188 = f32[384,128]{1,0:T(8,128)S(1)} fusion(s32[384]{0:T(512)S(1)} %pad_add_fusion, pred[384]{0:T(512)(128)(4,1)S(1)} %pad_add_fusion.1, bf16[1,1024,128]{2,1,0:T(8,128)(2,1)} %param.7), kind=kOutput, calls=%fused_computation.94 | convolution fusion | flops 101842944 | bytes 460672 | tf_op jit(solution)/shard_map/dot_general | solution.py:52
  5.7 1.0 %fusion.44 = bf16[384,1024]{1,0:T(8,128)(2,1)S(1)} fusion(bf16[1,1024,1024]{2,1,0:T(8,128)(2,1)S(1)} %copy-done, s32[384]{0:T(512)S(1)} %pad_add_fusion, pred[384]{0:T(512)(128)(4,1)S(1)} %pad_add_fusion.1), kind=kOutput, calls=%fused_computation.33 | convolution fusion | flops 806879232 | bytes 2885504 | tf_op jit(solution)/shard_map/dot_general | solution.py:53
  7.1 2.7 %collective-permute-start = (bf16[128,128]{1,0:T(8,128)(2,1)S(1)}, bf16[128,128]{1,0:T(8,128)(2,1)S(1)}, u32[]{:S(2)}, u32[]{:S(2)}) collective-permute-start(bf16[128,128]{1,0:T(8,128)(2,1)S(1)} %get-tuple-element.26), channel_id=1, source_target_pairs={{0,16},{1,17},{2,18},{3,19},{4,20},{5,21},{6,22},{7,23},{8,24},{9,... | collective-permute-start | bytes 98312 | tf_op jit(solution)/shard_map/ppermute | solution.py:61
  9.7 3.4 %collective-permute-start.2 = (bf16[128,128]{1,0:T(8,128)(2,1)S(1)}, bf16[128,128]{1,0:T(8,128)(2,1)S(1)}, u32[]{:S(2)}, u32[]{:S(2)}) collective-permute-start(bf16[128,128]{1,0:T(8,128)(2,1)S(1)} %get-tuple-element.27), channel_id=1, source_target_pairs={{1,2},{2,1},{3,4},{4,3},{5,6},{6,5},{7,8},{8,7},{9,10},{10,9},{11,... | collective-permute-start | bytes 98312 | tf_op jit(solution)/shard_map/ppermute | solution.py:61
  13.3 1.1 %copy.18 = bf16[1,1024,128]{1,2,0:T(8,128)(2,1)S(1)} copy(bf16[1,1024,128]{2,1,0:T(8,128)(2,1)} %param.7) | data formatting | bytes 524288 | tf_op args[0]
  15.1 2.6 %fusion.39 = bf16[384,1024]{1,0:T(8,128)(2,1)S(1)} fusion(bf16[1,1024,1024]{2,1,0:T(8,128)(2,1)} %param.9, s32[384]{0:T(512)S(1)} %pad_add_fusion, pred[384]{0:T(512)(128)(4,1)S(1)} %pad_add_fusion.1), kind=kOutput, calls=%fused_computation.32 | convolution fusion | flops 806486016 | bytes 2885504 | tf_op jit(solution)/shard_map/dot_general | solution.py:54
  17.7 0.4 fusion.104
  18.6 0.5 fusion.167
  19.9 3.5 %collective-permute-start.5 = (bf16[128,128]{1,0:T(8,128)(2,1)S(1)}, bf16[128,128]{1,0:T(8,128)(2,1)S(1)}, u32[]{:S(2)}, u32[]{:S(2)}) collective-permute-start(bf16[128,128]{1,0:T(8,128)(2,1)S(1)} %get-tuple-element.24), channel_id=1, source_target_pairs={{1,2},{2,1},{3,4},{4,3},{5,6},{6,5},{7,8},{8,7},{9,10},{10,9},{11,... | collective-permute-start | bytes 98312 | tf_op jit(solution)/shard_map/ppermute | solution.py:61
  23.6 0.8 fusion.146
  24.4 2.5 %collective-permute-done.5 = bf16[128,128]{1,0:T(8,128)(2,1)S(1)} collective-permute-done((bf16[128,128]{1,0:T(8,128)(2,1)S(1)}, bf16[128,128]{1,0:T(8,128)(2,1)S(1)}, u32[]{:S(2)}, u32[]{:S(2)}) %collective-permute-start.5) | collective-permute-done | bytes 32800 | tf_op jit(solution)/shard_map/ppermute | solution.py:61
  27.0 0.5 fusion.128
  27.9 2.6 %collective-permute-start.6 = (bf16[128,128]{1,0:T(8,128)(2,1)S(1)}, bf16[128,128]{1,0:T(8,128)(2,1)S(1)}, u32[]{:S(2)}, u32[]{:S(2)}) collective-permute-start(bf16[128,128]{1,0:T(8,128)(2,1)S(1)} %get-tuple-element.20), channel_id=1, source_target_pairs={{0,16},{1,17},{2,18},{3,19},{4,20},{5,21},{6,22},{7,23},{8,24},{9,... | collective-permute-start | bytes 98312 | tf_op jit(solution)/shard_map/ppermute | solution.py:61
  30.5 3.3 %collective-permute-start.8 = (bf16[128,128]{1,0:T(8,128)(2,1)S(1)}, bf16[128,128]{1,0:T(8,128)(2,1)S(1)}, u32[]{:S(2)}, u32[]{:S(2)}) collective-permute-start(bf16[128,128]{1,0:T(8,128)(2,1)S(1)} %get-tuple-element.21), channel_id=1, source_target_pairs={{1,2},{2,1},{3,4},{4,3},{5,6},{6,5},{7,8},{8,7},{9,10},{10,9},{11,... | collective-permute-start | bytes 98312 | tf_op jit(solution)/shard_map/ppermute | solution.py:61
  33.9 0.5 fusion.98
  34.4 3.2 %collective-permute-done.8 = bf16[128,128]{1,0:T(8,128)(2,1)S(1)} collective-permute-done((bf16[128,128]{1,0:T(8,128)(2,1)S(1)}, bf16[128,128]{1,0:T(8,128)(2,1)S(1)}, u32[]{:S(2)}, u32[]{:S(2)}) %collective-permute-start.8) | collective-permute-done | bytes 32800 | tf_op jit(solution)/shard_map/ppermute | solution.py:61
  37.6 0.5 fusion.170
  38.5 0.4 collective-permute-start.9
  38.9 3.0 %collective-permute-start.11 = (bf16[128,128]{1,0:T(8,128)(2,1)S(1)}, bf16[128,128]{1,0:T(8,128)(2,1)S(1)}, u32[]{:S(2)}, u32[]{:S(2)}) collective-permute-start(bf16[128,128]{1,0:T(8,128)(2,1)S(1)} %get-tuple-element.18), channel_id=1, source_target_pairs={{1,2},{2,1},{3,4},{4,3},{5,6},{6,5},{7,8},{8,7},{9,10},{10,9},{11,... | collective-permute-start | bytes 98312 | tf_op jit(solution)/shard_map/ppermute | solution.py:61
  42.0 0.8 fusion.152
  42.8 0.5 collective-permute-done.9
  43.4 2.6 %collective-permute-done.11 = bf16[128,128]{1,0:T(8,128)(2,1)S(1)} collective-permute-done((bf16[128,128]{1,0:T(8,128)(2,1)S(1)}, bf16[128,128]{1,0:T(8,128)(2,1)S(1)}, u32[]{:S(2)}, u32[]{:S(2)}) %collective-permute-start.11) | collective-permute-done | bytes 32800 | tf_op jit(solution)/shard_map/ppermute | solution.py:61
  46.0 0.5 fusion.122
  46.9 3.0 %collective-permute-start.12 = (bf16[128,128]{1,0:T(8,128)(2,1)S(1)}, bf16[128,128]{1,0:T(8,128)(2,1)S(1)}, u32[]{:S(2)}, u32[]{:S(2)}) collective-permute-start(bf16[128,128]{1,0:T(8,128)(2,1)S(1)} %get-tuple-element.14), channel_id=1, source_target_pairs={{0,16},{1,17},{2,18},{3,19},{4,20},{5,21},{6,22},{7,23},{8,24},{9,... | collective-permute-start | bytes 98312 | tf_op jit(solution)/shard_map/ppermute | solution.py:61
  49.9 2.4 %collective-permute-start.14 = (bf16[128,128]{1,0:T(8,128)(2,1)S(1)}, bf16[128,128]{1,0:T(8,128)(2,1)S(1)}, u32[]{:S(2)}, u32[]{:S(2)}) collective-permute-start(bf16[128,128]{1,0:T(8,128)(2,1)S(1)} %get-tuple-element.15), channel_id=1, source_target_pairs={{1,2},{2,1},{3,4},{4,3},{5,6},{6,5},{7,8},{8,7},{9,10},{10,9},{11,... | collective-permute-start | bytes 98312 | tf_op jit(solution)/shard_map/ppermute | solution.py:61
  52.3 0.5 fusion.92
  52.8 4.1 %collective-permute-done.14 = bf16[128,128]{1,0:T(8,128)(2,1)S(1)} collective-permute-done((bf16[128,128]{1,0:T(8,128)(2,1)S(1)}, bf16[128,128]{1,0:T(8,128)(2,1)S(1)}, u32[]{:S(2)}, u32[]{:S(2)}) %collective-permute-start.14) | collective-permute-done | bytes 32800 | tf_op jit(solution)/shard_map/ppermute | solution.py:61
  56.9 0.5 fusion.173
  57.8 0.7 collective-permute-start.15
  58.5 2.1 %collective-permute-start.17 = (bf16[128,128]{1,0:T(8,128)(2,1)S(1)}, bf16[128,128]{1,0:T(8,128)(2,1)S(1)}, u32[]{:S(2)}, u32[]{:S(2)}) collective-permute-start(bf16[128,128]{1,0:T(8,128)(2,1)S(1)} %get-tuple-element.12), channel_id=1, source_target_pairs={{1,2},{2,1},{3,4},{4,3},{5,6},{6,5},{7,8},{8,7},{9,10},{10,9},{11,... | collective-permute-start | bytes 98312 | tf_op jit(solution)/shard_map/ppermute | solution.py:61
  60.7 0.8 fusion.158
  61.5 1.2 %collective-permute-done.15 = bf16[128,128]{1,0:T(8,128)(2,1)S(1)} collective-permute-done((bf16[128,128]{1,0:T(8,128)(2,1)S(1)}, bf16[128,128]{1,0:T(8,128)(2,1)S(1)}, u32[]{:S(2)}, u32[]{:S(2)}) %collective-permute-start.15) | collective-permute-done | bytes 32800 | tf_op jit(solution)/shard_map/ppermute | solution.py:61
  62.7 2.8 %collective-permute-done.17 = bf16[128,128]{1,0:T(8,128)(2,1)S(1)} collective-permute-done((bf16[128,128]{1,0:T(8,128)(2,1)S(1)}, bf16[128,128]{1,0:T(8,128)(2,1)S(1)}, u32[]{:S(2)}, u32[]{:S(2)}) %collective-permute-start.17) | collective-permute-done | bytes 32800 | tf_op jit(solution)/shard_map/ppermute | solution.py:61
  65.5 0.5 fusion.113
  66.5 2.5 %collective-permute-start.18 = (bf16[128,128]{1,0:T(8,128)(2,1)S(1)}, bf16[128,128]{1,0:T(8,128)(2,1)S(1)}, u32[]{:S(2)}, u32[]{:S(2)}) collective-permute-start(bf16[128,128]{1,0:T(8,128)(2,1)S(1)} %get-tuple-element.8), channel_id=1, source_target_pairs={{0,16},{1,17},{2,18},{3,19},{4,20},{5,21},{6,22},{7,23},{8,24},{9,... | collective-permute-start | bytes 98312 | tf_op jit(solution)/shard_map/ppermute | solution.py:61
  69.0 1.9 %collective-permute-start.20 = (bf16[128,128]{1,0:T(8,128)(2,1)S(1)}, bf16[128,128]{1,0:T(8,128)(2,1)S(1)}, u32[]{:S(2)}, u32[]{:S(2)}) collective-permute-start(bf16[128,128]{1,0:T(8,128)(2,1)S(1)} %get-tuple-element.9), channel_id=1, source_target_pairs={{1,2},{2,1},{3,4},{4,3},{5,6},{6,5},{7,8},{8,7},{9,10},{10,9},{11,... | collective-permute-start | bytes 98312 | tf_op jit(solution)/shard_map/ppermute | solution.py:61
  71.0 0.5 fusion.86
  71.4 4.5 %collective-permute-done.20 = bf16[128,128]{1,0:T(8,128)(2,1)S(1)} collective-permute-done((bf16[128,128]{1,0:T(8,128)(2,1)S(1)}, bf16[128,128]{1,0:T(8,128)(2,1)S(1)}, u32[]{:S(2)}, u32[]{:S(2)}) %collective-permute-start.20) | collective-permute-done | bytes 32800 | tf_op jit(solution)/shard_map/ppermute | solution.py:61
  76.0 0.5 fusion.176
  76.9 0.6 collective-permute-start.21
  77.5 1.9 %collective-permute-start.23 = (bf16[128,128]{1,0:T(8,128)(2,1)S(1)}, bf16[128,128]{1,0:T(8,128)(2,1)S(1)}, u32[]{:S(2)}, u32[]{:S(2)}) collective-permute-start(bf16[128,128]{1,0:T(8,128)(2,1)S(1)} %get-tuple-element.6), channel_id=1, source_target_pairs={{1,2},{2,1},{3,4},{4,3},{5,6},{6,5},{7,8},{8,7},{9,10},{10,9},{11,... | collective-permute-start | bytes 98312 | tf_op jit(solution)/shard_map/ppermute | solution.py:61
  79.5 0.8 fusion.164
  80.3 1.5 %collective-permute-done.21 = bf16[128,128]{1,0:T(8,128)(2,1)S(1)} collective-permute-done((bf16[128,128]{1,0:T(8,128)(2,1)S(1)}, bf16[128,128]{1,0:T(8,128)(2,1)S(1)}, u32[]{:S(2)}, u32[]{:S(2)}) %collective-permute-start.21) | collective-permute-done | bytes 32800 | tf_op jit(solution)/shard_map/ppermute | solution.py:61
  81.8 2.7 %collective-permute-done.23 = bf16[128,128]{1,0:T(8,128)(2,1)S(1)} collective-permute-done((bf16[128,128]{1,0:T(8,128)(2,1)S(1)}, bf16[128,128]{1,0:T(8,128)(2,1)S(1)}, u32[]{:S(2)}, u32[]{:S(2)}) %collective-permute-start.23) | collective-permute-done | bytes 32800 | tf_op jit(solution)/shard_map/ppermute | solution.py:61
  84.5 0.5 fusion.140
  85.0 1.0 %copy.27 = f32[1,1024,128]{2,1,0:T(8,128)} copy(f32[1,1024,128]{1,2,0:T(8,128)S(1)} %fusion.140) | data formatting | bytes 1048576 | tf_op jit(solution)/shard_map/broadcast_in_dim | solution.py:78
  (53 shorter events, 4.6 us)
Async XLA Ops:
  0.0 5.7 %copy-start = (bf16[1,1024,1024]{2,1,0:T(8,128)(2,1)S(1)}, bf16[1,1024,1024]{2,1,0:T(8,128)(2,1)}, u32[]{:S(2)}) copy-start(bf16[1,1024,1024]{2,1,0:T(8,128)(2,1)} %param.8) | copy-start | bytes 6291460
  7.1 11.5 %collective-permute-start = (bf16[128,128]{1,0:T(8,128)(2,1)S(1)}, bf16[128,128]{1,0:T(8,128)(2,1)S(1)}, u32[]{:S(2)}, u32[]{:S(2)}) collective-permute-start(bf16[128,128]{1,0:T(8,128)(2,1)S(1)} %get-tuple-element.26), channel_id=1, source_target_pairs={{0,16},{1,17},{2,18},{3,19},{4,20},{5,21},{6,22},{7,23},{8,24},{9,... | collective-permute-start | bytes 98312 | tf_op jit(solution)/shard_map/ppermute | solution.py:61
  9.7 8.8 %collective-permute-start.2 = (bf16[128,128]{1,0:T(8,128)(2,1)S(1)}, bf16[128,128]{1,0:T(8,128)(2,1)S(1)}, u32[]{:S(2)}, u32[]{:S(2)}) collective-permute-start(bf16[128,128]{1,0:T(8,128)(2,1)S(1)} %get-tuple-element.27), channel_id=1, source_target_pairs={{1,2},{2,1},{3,4},{4,3},{5,6},{6,5},{7,8},{8,7},{9,10},{10,9},{11,... | collective-permute-start | bytes 98312 | tf_op jit(solution)/shard_map/ppermute | solution.py:61
  13.1 5.4 %collective-permute-start.1 = (bf16[128,128]{1,0:T(8,128)(2,1)S(1)}, bf16[128,128]{1,0:T(8,128)(2,1)S(1)}, u32[]{:S(2)}, u32[]{:S(2)}) collective-permute-start(bf16[128,128]{1,0:T(8,128)(2,1)S(1)} %get-tuple-element.28), channel_id=1, source_target_pairs={{0,1},{1,0},{2,3},{3,2},{4,5},{5,4},{6,7},{7,6},{8,9},{9,8},{10,11... | collective-permute-start | bytes 98312 | tf_op jit(solution)/shard_map/ppermute | solution.py:61
  15.0 2.6 %copy-start.2 = (f32[1,1024]{1,0:T(1,128)S(1)}, f32[1,1024]{1,0:T(1,128)}, u32[]{:S(2)}) copy-start(f32[1,1024]{1,0:T(1,128)} %param.10) | copy-start | bytes 12292
  18.2 5.4 %copy-start.1 = (bf16[1,1024,1024]{2,1,0:T(8,128)(2,1)S(1)}, bf16[1,1024,1024]{2,1,0:T(8,128)(2,1)}, u32[]{:S(2)}) copy-start(bf16[1,1024,1024]{2,1,0:T(8,128)(2,1)} %param.9) | copy-start | bytes 6291460
  19.5 4.9 %collective-permute-start.3 = (bf16[128,128]{1,0:T(8,128)(2,1)S(1)}, bf16[128,128]{1,0:T(8,128)(2,1)S(1)}, u32[]{:S(2)}, u32[]{:S(2)}) collective-permute-start(bf16[128,128]{1,0:T(8,128)(2,1)S(1)} %get-tuple-element.23), channel_id=1, source_target_pairs={{0,16},{1,17},{2,18},{3,19},{4,20},{5,21},{6,22},{7,23},{8,24},{9,... | collective-permute-start | bytes 98312 | tf_op jit(solution)/shard_map/ppermute | solution.py:61
  19.9 7.0 %collective-permute-start.5 = (bf16[128,128]{1,0:T(8,128)(2,1)S(1)}, bf16[128,128]{1,0:T(8,128)(2,1)S(1)}, u32[]{:S(2)}, u32[]{:S(2)}) collective-permute-start(bf16[128,128]{1,0:T(8,128)(2,1)S(1)} %get-tuple-element.24), channel_id=1, source_target_pairs={{1,2},{2,1},{3,4},{4,3},{5,6},{6,5},{7,8},{8,7},{9,10},{10,9},{11,... | collective-permute-start | bytes 98312 | tf_op jit(solution)/shard_map/ppermute | solution.py:61
  23.5 3.5 %collective-permute-start.4 = (bf16[128,128]{1,0:T(8,128)(2,1)S(1)}, bf16[128,128]{1,0:T(8,128)(2,1)S(1)}, u32[]{:S(2)}, u32[]{:S(2)}) collective-permute-start(bf16[128,128]{1,0:T(8,128)(2,1)S(1)} %get-tuple-element.25), channel_id=1, source_target_pairs={{0,1},{1,0},{2,3},{3,2},{4,5},{5,4},{6,7},{7,6},{8,9},{9,8},{10,11... | collective-permute-start | bytes 98312 | tf_op jit(solution)/shard_map/ppermute | solution.py:61
  27.9 6.5 %collective-permute-start.6 = (bf16[128,128]{1,0:T(8,128)(2,1)S(1)}, bf16[128,128]{1,0:T(8,128)(2,1)S(1)}, u32[]{:S(2)}, u32[]{:S(2)}) collective-permute-start(bf16[128,128]{1,0:T(8,128)(2,1)S(1)} %get-tuple-element.20), channel_id=1, source_target_pairs={{0,16},{1,17},{2,18},{3,19},{4,20},{5,21},{6,22},{7,23},{8,24},{9,... | collective-permute-start | bytes 98312 | tf_op jit(solution)/shard_map/ppermute | solution.py:61
  30.5 7.0 %collective-permute-start.8 = (bf16[128,128]{1,0:T(8,128)(2,1)S(1)}, bf16[128,128]{1,0:T(8,128)(2,1)S(1)}, u32[]{:S(2)}, u32[]{:S(2)}) collective-permute-start(bf16[128,128]{1,0:T(8,128)(2,1)S(1)} %get-tuple-element.21), channel_id=1, source_target_pairs={{1,2},{2,1},{3,4},{4,3},{5,6},{6,5},{7,8},{8,7},{9,10},{10,9},{11,... | collective-permute-start | bytes 98312 | tf_op jit(solution)/shard_map/ppermute | solution.py:61
  33.8 3.7 %collective-permute-start.7 = (bf16[128,128]{1,0:T(8,128)(2,1)S(1)}, bf16[128,128]{1,0:T(8,128)(2,1)S(1)}, u32[]{:S(2)}, u32[]{:S(2)}) collective-permute-start(bf16[128,128]{1,0:T(8,128)(2,1)S(1)} %get-tuple-element.22), channel_id=1, source_target_pairs={{0,1},{1,0},{2,3},{3,2},{4,5},{5,4},{6,7},{7,6},{8,9},{9,8},{10,11... | collective-permute-start | bytes 98312 | tf_op jit(solution)/shard_map/ppermute | solution.py:61
  38.5 4.9 %collective-permute-start.9 = (bf16[128,128]{1,0:T(8,128)(2,1)S(1)}, bf16[128,128]{1,0:T(8,128)(2,1)S(1)}, u32[]{:S(2)}, u32[]{:S(2)}) collective-permute-start(bf16[128,128]{1,0:T(8,128)(2,1)S(1)} %get-tuple-element.17), channel_id=1, source_target_pairs={{0,16},{1,17},{2,18},{3,19},{4,20},{5,21},{6,22},{7,23},{8,24},{9,... | collective-permute-start | bytes 98312 | tf_op jit(solution)/shard_map/ppermute | solution.py:61
  38.9 7.0 %collective-permute-start.11 = (bf16[128,128]{1,0:T(8,128)(2,1)S(1)}, bf16[128,128]{1,0:T(8,128)(2,1)S(1)}, u32[]{:S(2)}, u32[]{:S(2)}) collective-permute-start(bf16[128,128]{1,0:T(8,128)(2,1)S(1)} %get-tuple-element.18), channel_id=1, source_target_pairs={{1,2},{2,1},{3,4},{4,3},{5,6},{6,5},{7,8},{8,7},{9,10},{10,9},{11,... | collective-permute-start | bytes 98312 | tf_op jit(solution)/shard_map/ppermute | solution.py:61
  41.9 4.0 %collective-permute-start.10 = (bf16[128,128]{1,0:T(8,128)(2,1)S(1)}, bf16[128,128]{1,0:T(8,128)(2,1)S(1)}, u32[]{:S(2)}, u32[]{:S(2)}) collective-permute-start(bf16[128,128]{1,0:T(8,128)(2,1)S(1)} %get-tuple-element.19), channel_id=1, source_target_pairs={{0,1},{1,0},{2,3},{3,2},{4,5},{5,4},{6,7},{7,6},{8,9},{9,8},{10,11... | collective-permute-start | bytes 98312 | tf_op jit(solution)/shard_map/ppermute | solution.py:61
  46.9 5.9 %collective-permute-start.12 = (bf16[128,128]{1,0:T(8,128)(2,1)S(1)}, bf16[128,128]{1,0:T(8,128)(2,1)S(1)}, u32[]{:S(2)}, u32[]{:S(2)}) collective-permute-start(bf16[128,128]{1,0:T(8,128)(2,1)S(1)} %get-tuple-element.14), channel_id=1, source_target_pairs={{0,16},{1,17},{2,18},{3,19},{4,20},{5,21},{6,22},{7,23},{8,24},{9,... | collective-permute-start | bytes 98312 | tf_op jit(solution)/shard_map/ppermute | solution.py:61
  49.9 7.0 %collective-permute-start.14 = (bf16[128,128]{1,0:T(8,128)(2,1)S(1)}, bf16[128,128]{1,0:T(8,128)(2,1)S(1)}, u32[]{:S(2)}, u32[]{:S(2)}) collective-permute-start(bf16[128,128]{1,0:T(8,128)(2,1)S(1)} %get-tuple-element.15), channel_id=1, source_target_pairs={{1,2},{2,1},{3,4},{4,3},{5,6},{6,5},{7,8},{8,7},{9,10},{10,9},{11,... | collective-permute-start | bytes 98312 | tf_op jit(solution)/shard_map/ppermute | solution.py:61
  52.3 4.6 %collective-permute-start.13 = (bf16[128,128]{1,0:T(8,128)(2,1)S(1)}, bf16[128,128]{1,0:T(8,128)(2,1)S(1)}, u32[]{:S(2)}, u32[]{:S(2)}) collective-permute-start(bf16[128,128]{1,0:T(8,128)(2,1)S(1)} %get-tuple-element.16), channel_id=1, source_target_pairs={{0,1},{1,0},{2,3},{3,2},{4,5},{5,4},{6,7},{7,6},{8,9},{9,8},{10,11... | collective-permute-start | bytes 98312 | tf_op jit(solution)/shard_map/ppermute | solution.py:61
  57.8 4.9 %collective-permute-start.15 = (bf16[128,128]{1,0:T(8,128)(2,1)S(1)}, bf16[128,128]{1,0:T(8,128)(2,1)S(1)}, u32[]{:S(2)}, u32[]{:S(2)}) collective-permute-start(bf16[128,128]{1,0:T(8,128)(2,1)S(1)} %get-tuple-element.11), channel_id=1, source_target_pairs={{0,16},{1,17},{2,18},{3,19},{4,20},{5,21},{6,22},{7,23},{8,24},{9,... | collective-permute-start | bytes 98312 | tf_op jit(solution)/shard_map/ppermute | solution.py:61
  58.5 7.0 %collective-permute-start.17 = (bf16[128,128]{1,0:T(8,128)(2,1)S(1)}, bf16[128,128]{1,0:T(8,128)(2,1)S(1)}, u32[]{:S(2)}, u32[]{:S(2)}) collective-permute-start(bf16[128,128]{1,0:T(8,128)(2,1)S(1)} %get-tuple-element.12), channel_id=1, source_target_pairs={{1,2},{2,1},{3,4},{4,3},{5,6},{6,5},{7,8},{8,7},{9,10},{10,9},{11,... | collective-permute-start | bytes 98312 | tf_op jit(solution)/shard_map/ppermute | solution.py:61
  60.6 4.9 %collective-permute-start.16 = (bf16[128,128]{1,0:T(8,128)(2,1)S(1)}, bf16[128,128]{1,0:T(8,128)(2,1)S(1)}, u32[]{:S(2)}, u32[]{:S(2)}) collective-permute-start(bf16[128,128]{1,0:T(8,128)(2,1)S(1)} %get-tuple-element.13), channel_id=1, source_target_pairs={{0,1},{1,0},{2,3},{3,2},{4,5},{5,4},{6,7},{7,6},{8,9},{9,8},{10,11... | collective-permute-start | bytes 98312 | tf_op jit(solution)/shard_map/ppermute | solution.py:61
  66.5 5.0 %collective-permute-start.18 = (bf16[128,128]{1,0:T(8,128)(2,1)S(1)}, bf16[128,128]{1,0:T(8,128)(2,1)S(1)}, u32[]{:S(2)}, u32[]{:S(2)}) collective-permute-start(bf16[128,128]{1,0:T(8,128)(2,1)S(1)} %get-tuple-element.8), channel_id=1, source_target_pairs={{0,16},{1,17},{2,18},{3,19},{4,20},{5,21},{6,22},{7,23},{8,24},{9,... | collective-permute-start | bytes 98312 | tf_op jit(solution)/shard_map/ppermute | solution.py:61
  69.0 7.0 %collective-permute-start.20 = (bf16[128,128]{1,0:T(8,128)(2,1)S(1)}, bf16[128,128]{1,0:T(8,128)(2,1)S(1)}, u32[]{:S(2)}, u32[]{:S(2)}) collective-permute-start(bf16[128,128]{1,0:T(8,128)(2,1)S(1)} %get-tuple-element.9), channel_id=1, source_target_pairs={{1,2},{2,1},{3,4},{4,3},{5,6},{6,5},{7,8},{8,7},{9,10},{10,9},{11,... | collective-permute-start | bytes 98312 | tf_op jit(solution)/shard_map/ppermute | solution.py:61
  70.9 5.1 %collective-permute-start.19 = (bf16[128,128]{1,0:T(8,128)(2,1)S(1)}, bf16[128,128]{1,0:T(8,128)(2,1)S(1)}, u32[]{:S(2)}, u32[]{:S(2)}) collective-permute-start(bf16[128,128]{1,0:T(8,128)(2,1)S(1)} %get-tuple-element.10), channel_id=1, source_target_pairs={{0,1},{1,0},{2,3},{3,2},{4,5},{5,4},{6,7},{7,6},{8,9},{9,8},{10,11... | collective-permute-start | bytes 98312 | tf_op jit(solution)/shard_map/ppermute | solution.py:61
  76.9 4.9 %collective-permute-start.21 = (bf16[128,128]{1,0:T(8,128)(2,1)S(1)}, bf16[128,128]{1,0:T(8,128)(2,1)S(1)}, u32[]{:S(2)}, u32[]{:S(2)}) collective-permute-start(bf16[128,128]{1,0:T(8,128)(2,1)S(1)} %get-tuple-element.5), channel_id=1, source_target_pairs={{0,16},{1,17},{2,18},{3,19},{4,20},{5,21},{6,22},{7,23},{8,24},{9,... | collective-permute-start | bytes 98312 | tf_op jit(solution)/shard_map/ppermute | solution.py:61
  77.5 7.0 %collective-permute-start.23 = (bf16[128,128]{1,0:T(8,128)(2,1)S(1)}, bf16[128,128]{1,0:T(8,128)(2,1)S(1)}, u32[]{:S(2)}, u32[]{:S(2)}) collective-permute-start(bf16[128,128]{1,0:T(8,128)(2,1)S(1)} %get-tuple-element.6), channel_id=1, source_target_pairs={{1,2},{2,1},{3,4},{4,3},{5,6},{6,5},{7,8},{8,7},{9,10},{10,9},{11,... | collective-permute-start | bytes 98312 | tf_op jit(solution)/shard_map/ppermute | solution.py:61
  79.4 5.1 %collective-permute-start.22 = (bf16[128,128]{1,0:T(8,128)(2,1)S(1)}, bf16[128,128]{1,0:T(8,128)(2,1)S(1)}, u32[]{:S(2)}, u32[]{:S(2)}) collective-permute-start(bf16[128,128]{1,0:T(8,128)(2,1)S(1)} %get-tuple-element.7), channel_id=1, source_target_pairs={{0,1},{1,0},{2,3},{3,2},{4,5},{5,4},{6,7},{7,6},{8,9},{9,8},{10,11... | collective-permute-start | bytes 98312 | tf_op jit(solution)/shard_map/ppermute | solution.py:61

commit v3 on v2

--- a/solution.py
+++ b/solution.py
@@ -6,27 +6,6 @@
 ITERS = 4
 FAR = 16
 DAMPING = 0.7
-
-
-def swaps(count):
-    near = [(i, i ^ 1) for i in range(count)]
-    cross = [(i, ((i + 1) ^ 1) - 1) for i in range(1, count - 1)]
-    blocks = count // FAR
-    far = [(i, i ^ FAR) for i in range(count)] if blocks > 1 else []
-    pairs = [far, near, cross]
-    if blocks > 2:
-        again = [(i, (((i // FAR + 1) ^ 1) - 1) % blocks * FAR + i % FAR) for i in range(count)]
-        pairs = [far, again, near, cross]
-    return [p for p in pairs if p]
-
-
-def slots_of(index, count):
-    odd = index % 2
-    block = index // FAR % 2
-    far, again = 2 + block, 3 - block
-    if count // FAR > 2:
-        return [far, again, odd, 1 - odd]
-    return [far, odd, 1 - odd]
 
 
 def body(right_side, schur, neumann, weights, neighbours, counts, shared_rows):
@@ -39,11 +18,29 @@
     width = s_mat.shape[0]
     share = shared_rows.shape[2]
     subs = lax.axis_size("sub")
-    routes = swaps(subs)
-    slots = slots_of(lax.axis_index("sub"), subs)
-    rows = jnp.concatenate([lax.dynamic_index_in_dim(shared_rows[0], k, 0, False) for k in slots])
+    index = lax.axis_index("sub")
+    near = [(i, i ^ 1) for i in range(subs)]
+    blocks = subs // FAR
+    again = [(i, (((i // FAR + 1) ^ 1) - 1) % blocks * FAR + i % FAR) for i in range(subs)] if blocks > 2 else []
+    span = 2 * FAR
+    teams = []
+    for base in range(0, subs, span):
+        for j in range(0, FAR, 2):
+            teams.append([base + (j + 1) % span, base + (j + 2) % span, base + (j + 1 + FAR) % span, base + (j + 2 + FAR) % span])
+    turned = (index + span - 1) % span
+    place = turned % 2 + 2 * (turned // FAR)
+    odd = index % 2
+    block = index // FAR % 2
+    slots = []
+    for q in range(4):
+        gap = q ^ place
+        slots.append(jnp.where(gap == 1, 1 - odd, jnp.where(gap == 2, 2 + block, -1)))
+    slots.append(odd)
+    if again:
+        slots.append(3 - block)
+    rows = jnp.concatenate([lax.dynamic_index_in_dim(shared_rows[0], jnp.maximum(k, 0), 0, False) for k in slots])
     live = jnp.concatenate(
-        [jnp.broadcast_to(lax.dynamic_index_in_dim(neighbours[0], k, 0, True) >= 0, (share,)) for k in slots]
+        [jnp.broadcast_to((lax.dynamic_index_in_dim(neighbours[0], jnp.maximum(k, 0), 0, True) >= 0) & (k >= 0), (share,)) for k in slots]
     )
     mask = (jnp.arange(width) < count).astype(jnp.float32)[:, None]
     hot = (jnp.arange(width)[:, None] == rows[None, :]) & live[None, :]
@@ -57,9 +54,11 @@
     mask_weight = mask * weight
 
     def exchange(packed):
-        parts = [
-            lax.ppermute(packed[k * share : (k + 1) * share], "sub", route) for k, route in enumerate(routes)
-        ]
+        parts = [lax.ppermute(packed[4 * share : 5 * share], "sub", near)]
+        if again:
+            parts.append(lax.ppermute(packed[5 * share : 6 * share], "sub", again))
+        out = lax.all_to_all(packed[: 4 * share].reshape(4, share, -1), "sub", 0, 0, axis_index_groups=teams)
+        parts = [out.reshape(4 * share, -1)] + parts
         return jnp.dot(placer, jnp.concatenate(parts, 0), preferred_element_type=jnp.float32)
 
     def transposed(mat, block):

time: 86.5 us -> 137 us (1.58)
  matrix products: 17.5 us -> 47.5 us
  local copies, waits for them, and re-layouts: 4.48 us -> 21.9 us
  starting transfers between devices: 35 us -> 45.3 us
  waiting for transfers between devices: 25.6 us -> 15.8 us
    all_to_all x0 -> x8, starting transfers between devices: none -> 45.3 us  [exchange(): lax.all_to_all(packed[:4 * share].reshape(4, share, -1), 'sub', 0, 0, axi...]
    ppermute x24 -> x8, starting transfers between devices: 35 us -> 0.02 us  [exchange(): parts = [lax.ppermute(packed[4 * share:5 * share], 'sub', near)]]
    ppermute x24 -> x8, waiting for transfers between devices: 25.6 us -> 0.02 us  [exchange(): parts = [lax.ppermute(packed[4 * share:5 * share], 'sub', near)]]
    all_to_all x0 -> x8, waiting for transfers between devices: none -> 15.8 us  [exchange(): lax.all_to_all(packed[:4 * share].reshape(4, share, -1), 'sub', 0, 0, axi...]
    dot_general x8, matrix products: 4.27 us -> 15.6 us  [exchange(): jnp.dot(placer, jnp.concatenate(parts, 0), preferred_element_type=jnp.flo...]
    dot_general x4, matrix products: 3.32 us -> 13.3 us  [body(): jnp.dot(n_mat, scaled, preferred_element_type=jnp.float32)]
    slice x8 -> x16, local copies, waits for them, and re-layouts: 0.07 us -> 9.59 us  [the longest x8 5.3 us: exchange(): packed[:4 * share].reshape(4, share, -1)]
    unnamed x7 -> x61, local copies, waits for them, and re-layouts: 1.1 us -> 8.85 us
  transfers between devices with their start and end apart: 24 -> 16, of which waited for: 10 -> 7; matrix products, arithmetic and copies ran while one was open for 11% -> 20% of each run, Pallas kernels for 0% -> 0%
where the time goes in v3:
time: 137 us; the launch traced here: 135 us
  matrix products  47.5 us (35%)
  starting transfers between devices  45.3 us (33%)
  local copies, waits for them, and re-layouts  21.9 us (16%)
  waiting for transfers between devices  15.8 us (12%)
  between operations  4.22 us (3%)
    all_to_all x8, starting transfers between devices, exchange(): lax.all_to_all(packed[:4 * share].reshape(4, share, -1), 'sub', 0, 0, axi...  45.3 us
    all_to_all x8, waiting for transfers between devices, exchange(): lax.all_to_all(packed[:4 * share].reshape(4, share, -1), 'sub', 0, 0, axi...  15.8 us
    dot_general x8, matrix products, exchange(): jnp.dot(placer, jnp.concatenate(parts, 0), preferred_element_type=jnp.flo...  15.6 us
    dot_general x4, matrix products, body(): jnp.dot(n_mat, scaled, preferred_element_type=jnp.float32)  13.3 us
    dot_general x8, matrix products, transposed(): lax.dot_general(mat, block, (((0,), (0,)), ((), ())), preferred_element_t...  10.3 us
    unnamed x61, local copies, waits for them, and re-layouts  8.85 us
    slice x8, local copies, waits for them, and re-layouts, exchange(): packed[:4 * share].reshape(4, share, -1)  5.3 us
    slice x8, local copies, waits for them, and re-layouts, exchange(): parts = [lax.ppermute(packed[4 * share:5 * share], 'sub', near)]  4.29 us
  transfers between devices with their start and end apart: 16, of which 7 were waited for; matrix products, arithmetic and copies ran while one was open for 20% of the time, Pallas kernels for 0%

profile of v3, /device:TPU:8, one launch (start us, length us, event | category | flops | bytes accessed | tf_op | source)
XLA Modules:
  0.0 135.3 jit_solution(11744343289116991545)
XLA Ops:
  0.0 1.5 %constant_dynamic-slice_fusion = (s32[1,1]{1,0:T(1,128)}, s32[1,1]{1,0:T(1,128)}, s32[1,1]{1,0:T(1,128)}, s32[1,1]{1,0:T(1,128)}, s32[1,1]{1,0:T(1,128)}) fusion(s32[1,4]{1,0:T(1,128)} %param.11, s32[]{:T(128)S(6)} %max.24, s32[]{:T(128)S(6)} %max.22, s32[]{:T(128)S(6)} %max.21, s32[]{:T(128)S(6)} %max.20, s32[]{:T(128)S(6)} %max.23), kind=kLoop, calls=%fused_computation.153 | loop fusion | bytes 60 | tf_op jit(solution)/shard_map/jit(dynamic_index_in_dim)/dynamic_slice | solution.py:43
  4.7 0.7 constant_dynamic-update-slice_fusion.4
  5.4 0.7 constant_dynamic-update-slice_fusion.3
  6.1 0.7 constant_dynamic-update-slice_fusion.2
  6.8 0.7 constant_dynamic-update-slice_fusion.1
  7.5 0.7 constant_dynamic-update-slice_fusion
  9.3 1.6 %fusion.40 = f32[640,128]{1,0:T(8,128)S(1)} fusion(s32[640]{0:T(1024)S(1)} %constant_dynamic-update-slice_fusion, pred[640]{0:T(1024)(128)(4,1)S(1)} %dynamic-update-slice.4, bf16[1,1024,128]{2,1,0:T(8,128)(2,1)} %param.7), kind=kOutput, calls=%fused_computation.32 | convolution fusion | flops 169738240 | bytes 593024 | tf_op jit(solution)/shard_map/dot_general | solution.py:49
  10.9 1.6 %fusion.42 = bf16[640,1024]{1,0:T(8,128)(2,1)S(1)} fusion(bf16[1,1024,1024]{2,1,0:T(8,128)(2,1)S(1)} %copy-done, s32[640]{0:T(1024)S(1)} %constant_dynamic-update-slice_fusion, pred[640]{0:T(1024)(128)(4,1)S(1)} %dynamic-update-slice.4), kind=kOutput, calls=%fused_computation.33 | convolution fusion | flops 1344798720 | bytes 3411072 | tf_op jit(solution)/shard_map/dot_general | solution.py:50
  12.5 1.1 copy-done.1
  14.1 0.7 slice.64
  14.7 6.8 %all-to-all-start = ((bf16[4,128,128]{2,1,0:T(8,128)(2,1)}), bf16[4,128,128]{2,1,0:T(8,128)(2,1)S(1)}, u32[]{:S(2)}, u32[]{:S(2)}) async-start(bf16[4,128,128]{2,1,0:T(8,128)(2,1)} %bitcast.25), calls=%async_computation | async-start | bytes 262144 | tf_op jit(solution)/shard_map/all_to_all | solution.py:60
  22.2 0.9 copy.18
  23.8 3.2 %fusion.47 = bf16[640,1024]{1,0:T(8,128)(2,1)S(1)} fusion(bf16[1,1024,1024]{2,1,0:T(8,128)(2,1)} %param.9, s32[640]{0:T(1024)S(1)} %constant_dynamic-update-slice_fusion, pred[640]{0:T(1024)(128)(4,1)S(1)} %dynamic-update-slice.4), kind=kOutput, calls=%fused_computation.34 | convolution fusion | flops 1344143360 | bytes 3411072 | tf_op jit(solution)/shard_map/dot_general | solution.py:51
  27.0 1.2 fusion.155
  28.9 1.9 %fusion.203 = bf16[1024,128]{0,1:T(8,128)(2,1)S(1)} fusion(f32[1024,128]{0,1:T(8,128)} %fusion.155, s32[640]{0:T(1024)} %copy-done.20, pred[640]{0:T(1024)(128)(4,1)} %copy-done.23, f32[1024]{0:T(1024)S(1)} %bitcast.189, bf16[128,128]{1,0:T(8,128)(2,1)} %collective-permute-done, bf16[512,128]{1,0:T(8,128)(2,1)S(1)} %bitcast.179), kind=kOutput, calls=%fused_computation.100 | convolution fusion | flops 169803776 | bytes 957568 | tf_op jit(solution)/shard_map/dot_general | solution.py:62
  30.8 0.7 copy-done.15
  33.3 6.6 %all-to-all-start.1 = ((bf16[4,128,128]{2,1,0:T(8,128)(2,1)}), bf16[4,128,128]{2,1,0:T(8,128)(2,1)S(1)}, u32[]{:S(2)}, u32[]{:S(2)}) async-start(bf16[4,128,128]{2,1,0:T(8,128)(2,1)} %bitcast.29), calls=%async_computation.1 | async-start | bytes 262144 | tf_op jit(solution)/shard_map/all_to_all | solution.py:60
  39.9 3.3 %fusion.161 = f32[1024,128]{0,1:T(8,128)} fusion(bf16[1024,128]{0,1:T(8,128)(2,1)} %copy-done.15, bf16[1,1024,1024]{2,1,0:T(8,128)(2,1)} %param.9, f32[1024]{0:T(1024)S(1)} %fusion.248), kind=kOutput, calls=%fused_computation.86 | convolution fusion | flops 268566528 | bytes 2887680 | tf_op jit(solution)/shard_map/dot_general | solution.py:75
  43.2 1.8 %all-to-all-done.1 = bf16[4,128,128]{2,1,0:T(8,128)(2,1)S(1)} async-done(((bf16[4,128,128]{2,1,0:T(8,128)(2,1)}), bf16[4,128,128]{2,1,0:T(8,128)(2,1)S(1)}, u32[]{:S(2)}, u32[]{:S(2)}) %all-to-all-start.1) | async-done | bytes 131104 | tf_op jit(solution)/shard_map/all_to_all | solution.py:60
  45.1 2.0 %fusion.101 = f32[1024,128]{0,1:T(8,128)S(1)} fusion(f32[1024,128]{0,1:T(8,128)} %fusion.161, s32[640]{0:T(1024)} %copy-done.20, pred[640]{0:T(1024)(128)(4,1)} %copy-done.23, bf16[128,128]{1,0:T(8,128)(2,1)} %collective-permute-done.1, bf16[512,128]{1,0:T(8,128)(2,1)S(1)} %bitcast.184), kind=kOutput, calls=%fused_computation.66 | convolution fusion | flops 169672704 | bytes 1215616 | tf_op jit(solution)/shard_map/dot_general | solution.py:62
  49.1 5.3 %all-to-all-start.2 = ((bf16[4,128,128]{2,1,0:T(8,128)(2,1)}), bf16[4,128,128]{2,1,0:T(8,128)(2,1)S(1)}, u32[]{:S(2)}, u32[]{:S(2)}) async-start(bf16[4,128,128]{2,1,0:T(8,128)(2,1)} %bitcast.32), calls=%async_computation.2 | async-start | bytes 262144 | tf_op jit(solution)/shard_map/all_to_all | solution.py:60
  54.4 2.4 %fusion.149 = f32[1024,128]{0,1:T(8,128)} fusion(bf16[1,1024,1024]{2,1,0:T(8,128)(2,1)S(1)} %copy-done, bf16[1,1024,128]{1,2,0:T(8,128)(2,1)} %copy.18, f32[1024]{0:T(1024)S(1)} %fusion.247, f32[1024,128]{0,1:T(8,128)} %copy-done.13), kind=kOutput, calls=%fused_computation.82 | convolution fusion | flops 268959744 | bytes 3411968 | tf_op jit(solution)/shard_map/dot_general | solution.py:65
  56.8 2.8 %all-to-all-done.2 = bf16[4,128,128]{2,1,0:T(8,128)(2,1)S(1)} async-done(((bf16[4,128,128]{2,1,0:T(8,128)(2,1)}), bf16[4,128,128]{2,1,0:T(8,128)(2,1)S(1)}, u32[]{:S(2)}, u32[]{:S(2)}) %all-to-all-start.2) | async-done | bytes 131104 | tf_op jit(solution)/shard_map/all_to_all | solution.py:60
  59.6 1.9 %fusion.200 = bf16[1024,128]{0,1:T(8,128)(2,1)S(1)} fusion(f32[1024,128]{0,1:T(8,128)} %fusion.149, s32[640]{0:T(1024)} %copy-done.20, pred[640]{0:T(1024)(128)(4,1)} %copy-done.23, f32[1024]{0:T(1024)S(1)} %bitcast.190, bf16[128,128]{1,0:T(8,128)(2,1)} %collective-permute-done.2, bf16[512,128]{1,0:T(8,128)(2,1)S(1)} %bitcast.185), kind=kOutput, calls=%fused_computation.99 | convolution fusion | flops 169803776 | bytes 957568 | tf_op jit(solution)/shard_map/dot_general | solution.py:62
  61.5 0.7 copy-done.16
  63.9 5.5 %all-to-all-start.3 = ((bf16[4,128,128]{2,1,0:T(8,128)(2,1)}), bf16[4,128,128]{2,1,0:T(8,128)(2,1)S(1)}, u32[]{:S(2)}, u32[]{:S(2)}) async-start(bf16[4,128,128]{2,1,0:T(8,128)(2,1)} %bitcast.35), calls=%async_computation.3 | async-start | bytes 262144 | tf_op jit(solution)/shard_map/all_to_all | solution.py:60
  69.4 3.3 %fusion.167 = f32[1024,128]{0,1:T(8,128)} fusion(bf16[1024,128]{0,1:T(8,128)(2,1)} %copy-done.16, bf16[1,1024,1024]{2,1,0:T(8,128)(2,1)} %param.9, f32[1024]{0:T(1024)S(1)} %fusion.248), kind=kOutput, calls=%fused_computation.88 | convolution fusion | flops 268566528 | bytes 2887680 | tf_op jit(solution)/shard_map/dot_general | solution.py:75
  72.7 1.8 %all-to-all-done.3 = bf16[4,128,128]{2,1,0:T(8,128)(2,1)S(1)} async-done(((bf16[4,128,128]{2,1,0:T(8,128)(2,1)}), bf16[4,128,128]{2,1,0:T(8,128)(2,1)S(1)}, u32[]{:S(2)}, u32[]{:S(2)}) %all-to-all-start.3) | async-done | bytes 131104 | tf_op jit(solution)/shard_map/all_to_all | solution.py:60
  74.6 2.1 %fusion.185 = f32[1024,128]{0,1:T(8,128)S(1)} fusion(f32[1024,128]{0,1:T(8,128)} %copy-done.13, f32[1024,128]{0,1:T(8,128)} %fusion.167, s32[640]{0:T(1024)} %copy-done.20, pred[640]{0:T(1024)(128)(4,1)} %copy-done.23, bf16[128,128]{1,0:T(8,128)(2,1)} %collective-permute-done.3, bf16[512,128]{1,0:T(8,128)(2,1)S(1)} %bitcast.181), kind=kOutput, calls=%fused_computation.94 | convolution fusion | flops 169803776 | bytes 1739904 | tf_op jit(solution)/shard_map/dot_general | solution.py:62
  78.8 5.3 %all-to-all-start.4 = ((bf16[4,128,128]{2,1,0:T(8,128)(2,1)}), bf16[4,128,128]{2,1,0:T(8,128)(2,1)S(1)}, u32[]{:S(2)}, u32[]{:S(2)}) async-start(bf16[4,128,128]{2,1,0:T(8,128)(2,1)} %bitcast.38), calls=%async_computation.4 | async-start | bytes 262144 | tf_op jit(solution)/shard_map/all_to_all | solution.py:60
  84.1 2.4 %fusion.143 = f32[1024,128]{0,1:T(8,128)} fusion(bf16[1,1024,1024]{2,1,0:T(8,128)(2,1)S(1)} %copy-done, bf16[1,1024,128]{1,2,0:T(8,128)(2,1)} %copy.18, f32[1024]{0:T(1024)S(1)} %fusion.247, f32[1024,128]{0,1:T(8,128)} %copy-done.12), kind=kOutput, calls=%fused_computation.80 | convolution fusion | flops 268959744 | bytes 3411968 | tf_op jit(solution)/shard_map/dot_general | solution.py:65
  86.4 2.8 %all-to-all-done.4 = bf16[4,128,128]{2,1,0:T(8,128)(2,1)S(1)} async-done(((bf16[4,128,128]{2,1,0:T(8,128)(2,1)}), bf16[4,128,128]{2,1,0:T(8,128)(2,1)S(1)}, u32[]{:S(2)}, u32[]{:S(2)}) %all-to-all-start.4) | async-done | bytes 131104 | tf_op jit(solution)/shard_map/all_to_all | solution.py:60
  89.2 1.9 %fusion.197 = bf16[1024,128]{0,1:T(8,128)(2,1)S(1)} fusion(f32[1024,128]{0,1:T(8,128)} %fusion.143, s32[640]{0:T(1024)} %copy-done.20, pred[640]{0:T(1024)(128)(4,1)} %copy-done.23, f32[1024]{0:T(1024)S(1)} %bitcast.191, bf16[128,128]{1,0:T(8,128)(2,1)} %collective-permute-done.4, bf16[512,128]{1,0:T(8,128)(2,1)S(1)} %bitcast.186), kind=kOutput, calls=%fused_computation.98 | convolution fusion | flops 169803776 | bytes 957568 | tf_op jit(solution)/shard_map/dot_general | solution.py:62
  91.1 0.7 copy-done.17
  93.6 5.3 %all-to-all-start.5 = ((bf16[4,128,128]{2,1,0:T(8,128)(2,1)}), bf16[4,128,128]{2,1,0:T(8,128)(2,1)S(1)}, u32[]{:S(2)}, u32[]{:S(2)}) async-start(bf16[4,128,128]{2,1,0:T(8,128)(2,1)} %bitcast.41), calls=%async_computation.5 | async-start | bytes 262144 | tf_op jit(solution)/shard_map/all_to_all | solution.py:60
  98.9 3.3 %fusion.173 = f32[1024,128]{0,1:T(8,128)} fusion(bf16[1024,128]{0,1:T(8,128)(2,1)} %copy-done.17, bf16[1,1024,1024]{2,1,0:T(8,128)(2,1)} %param.9, f32[1024]{0:T(1024)S(1)} %fusion.248), kind=kOutput, calls=%fused_computation.90 | convolution fusion | flops 268566528 | bytes 2887680 | tf_op jit(solution)/shard_map/dot_general | solution.py:75
  102.2 1.8 %all-to-all-done.5 = bf16[4,128,128]{2,1,0:T(8,128)(2,1)S(1)} async-done(((bf16[4,128,128]{2,1,0:T(8,128)(2,1)}), bf16[4,128,128]{2,1,0:T(8,128)(2,1)S(1)}, u32[]{:S(2)}, u32[]{:S(2)}) %all-to-all-start.5) | async-done | bytes 131104 | tf_op jit(solution)/shard_map/all_to_all | solution.py:60
  104.0 2.1 %fusion.182 = f32[1024,128]{0,1:T(8,128)S(1)} fusion(f32[1024,128]{0,1:T(8,128)} %copy-done.12, f32[1024,128]{0,1:T(8,128)} %fusion.173, s32[640]{0:T(1024)} %copy-done.20, pred[640]{0:T(1024)(128)(4,1)} %copy-done.23, bf16[128,128]{1,0:T(8,128)(2,1)} %collective-permute-done.5, bf16[512,128]{1,0:T(8,128)(2,1)S(1)} %bitcast.182), kind=kOutput, calls=%fused_computation.93 | convolution fusion | flops 169803776 | bytes 1739904 | tf_op jit(solution)/shard_map/dot_general | solution.py:62
  107.6 0.7 slice.76
  108.3 5.3 %all-to-all-start.6 = ((bf16[4,128,128]{2,1,0:T(8,128)(2,1)}), bf16[4,128,128]{2,1,0:T(8,128)(2,1)S(1)}, u32[]{:S(2)}, u32[]{:S(2)}) async-start(bf16[4,128,128]{2,1,0:T(8,128)(2,1)} %bitcast.44), calls=%async_computation.6 | async-start | bytes 262144 | tf_op jit(solution)/shard_map/all_to_all | solution.py:60
  113.6 2.4 %fusion.137 = f32[1024,128]{0,1:T(8,128)} fusion(bf16[1,1024,1024]{2,1,0:T(8,128)(2,1)S(1)} %copy-done, bf16[1,1024,128]{1,2,0:T(8,128)(2,1)} %copy.18, f32[1024]{0:T(1024)S(1)} %fusion.247, f32[1024,128]{0,1:T(8,128)} %copy-done.10), kind=kOutput, calls=%fused_computation.78 | convolution fusion | flops 268959744 | bytes 3411968 | tf_op jit(solution)/shard_map/dot_general | solution.py:65
  115.9 2.8 %all-to-all-done.6 = bf16[4,128,128]{2,1,0:T(8,128)(2,1)S(1)} async-done(((bf16[4,128,128]{2,1,0:T(8,128)(2,1)}), bf16[4,128,128]{2,1,0:T(8,128)(2,1)S(1)}, u32[]{:S(2)}, u32[]{:S(2)}) %all-to-all-start.6) | async-done | bytes 131104 | tf_op jit(solution)/shard_map/all_to_all | solution.py:60
  118.7 1.9 %fusion.194 = bf16[1024,128]{0,1:T(8,128)(2,1)S(1)} fusion(f32[1024,128]{0,1:T(8,128)} %fusion.137, s32[640]{0:T(1024)} %copy-done.20, pred[640]{0:T(1024)(128)(4,1)} %copy-done.23, f32[1024]{0:T(1024)S(1)} %bitcast.192, bf16[128,128]{1,0:T(8,128)(2,1)} %collective-permute-done.6, bf16[512,128]{1,0:T(8,128)(2,1)S(1)} %bitcast.183), kind=kOutput, calls=%fused_computation.97 | convolution fusion | flops 169803776 | bytes 957568 | tf_op jit(solution)/shard_map/dot_general | solution.py:62
  122.0 5.3 %all-to-all-start.7 = ((bf16[4,128,128]{2,1,0:T(8,128)(2,1)}), bf16[4,128,128]{2,1,0:T(8,128)(2,1)S(1)}, u32[]{:S(2)}, u32[]{:S(2)}) async-start(bf16[4,128,128]{2,1,0:T(8,128)(2,1)} %bitcast.47), calls=%async_computation.7 | async-start | bytes 262144 | tf_op jit(solution)/shard_map/all_to_all | solution.py:60
  127.3 3.3 %fusion.179 = f32[1024,128]{0,1:T(8,128)} fusion(bf16[1024,128]{0,1:T(8,128)(2,1)} %copy-done.14, bf16[1,1024,1024]{2,1,0:T(8,128)(2,1)} %param.9, f32[1024]{0:T(1024)S(1)} %fusion.248), kind=kOutput, calls=%fused_computation.92 | convolution fusion | flops 268566528 | bytes 2887680 | tf_op jit(solution)/shard_map/dot_general | solution.py:75
  130.6 1.8 %all-to-all-done.7 = bf16[4,128,128]{2,1,0:T(8,128)(2,1)S(1)} async-done(((bf16[4,128,128]{2,1,0:T(8,128)(2,1)}), bf16[4,128,128]{2,1,0:T(8,128)(2,1)S(1)}, u32[]{:S(2)}, u32[]{:S(2)}) %all-to-all-start.7) | async-done | bytes 131104 | tf_op jit(solution)/shard_map/all_to_all | solution.py:60
  132.4 1.8 %fusion.191 = f32[1,1024,128]{1,2,0:T(8,128)S(1)} fusion(f32[1024,128]{0,1:T(8,128)S(1)} %copy-done.11, f32[1024,128]{0,1:T(8,128)} %fusion.179, s32[640]{0:T(1024)S(1)} %copy-done.22, pred[640]{0:T(1024)(128)(4,1)S(1)} %copy-done.25, bf16[128,128]{1,0:T(8,128)(2,1)S(1)} %collective-permute-done.7, bf16[512,128]{1,0:T(8,128)(2,1)S(1)} %bitcast.180), kind=kOutput, calls=%fused_computation.96 | convolution fusion | flops 169803776 | bytes 1739904 | tf_op jit(solution)/shard_map/dot_general | solution.py:62
  134.3 1.0 copy.27
  (102 shorter events, 15.1 us)
Async XLA Ops:
  0.0 10.9 %copy-start = (bf16[1,1024,1024]{2,1,0:T(8,128)(2,1)S(1)}, bf16[1,1024,1024]{2,1,0:T(8,128)(2,1)}, u32[]{:S(2)}) copy-start(bf16[1,1024,1024]{2,1,0:T(8,128)(2,1)} %param.8) | copy-start | bytes 6291460
  8.2 15.6 %copy-start.20 = (s32[640]{0:T(1024)}, s32[640]{0:T(1024)S(1)}, u32[]{:S(2)}) copy-start(s32[640]{0:T(1024)S(1)} %constant_dynamic-update-slice_fusion) | copy-start | bytes 7684
  9.3 14.5 %copy-start.23 = (pred[640]{0:T(1024)(128)(4,1)}, pred[640]{0:T(1024)(128)(4,1)S(1)}, u32[]{:S(2)}) copy-start(pred[640]{0:T(1024)(128)(4,1)S(1)} %dynamic-update-slice.4) | copy-start | bytes 1924
  10.9 1.6 %copy-start.6 = (f32[640,128]{1,0:T(8,128)}, f32[640,128]{1,0:T(8,128)S(1)}, u32[]{:S(2)}) copy-start(f32[640,128]{1,0:T(8,128)S(1)} %fusion.40) | copy-start | bytes 983044
  12.5 1.1 copy-start.1
  13.6 8.6 %copy-start.18 = (bf16[1,1024,128]{2,1,0:T(8,128)(2,1)S(1)}, bf16[1,1024,128]{2,1,0:T(8,128)(2,1)}, u32[]{:S(2)}) copy-start(bf16[1,1024,128]{2,1,0:T(8,128)(2,1)} %param.7) | copy-start | bytes 786436
  14.7 14.1 %all-to-all-start = ((bf16[4,128,128]{2,1,0:T(8,128)(2,1)}), bf16[4,128,128]{2,1,0:T(8,128)(2,1)S(1)}, u32[]{:S(2)}, u32[]{:S(2)}) async-start(bf16[4,128,128]{2,1,0:T(8,128)(2,1)} %bitcast.25), calls=%async_computation | async-start | bytes 262144 | tf_op jit(solution)/shard_map/all_to_all | solution.py:60
  22.2 6.7 %collective-permute-start = (bf16[128,128]{1,0:T(8,128)(2,1)}, bf16[128,128]{1,0:T(8,128)(2,1)}, u32[]{:S(2)}, u32[]{:S(2)}) collective-permute-start(bf16[128,128]{1,0:T(8,128)(2,1)} %slice.65), channel_id=1, source_target_pairs={{0,1},{1,0},{2,3},{3,2},{4,5},{5,4},{6,7},{7,6},{8,9},{9,8},{10,11... | collective-permute-start | bytes 98312 | tf_op jit(solution)/shard_map/ppermute | solution.py:57
  23.8 3.2 %copy-start.5 = (bf16[1,1024,128]{1,2,0:T(8,128)(2,1)S(1)}, bf16[1,1024,128]{1,2,0:T(8,128)(2,1)}, u32[]{:S(2)}) copy-start(bf16[1,1024,128]{1,2,0:T(8,128)(2,1)} %copy.18) | copy-start | bytes 786436
  27.0 1.3 copy-start.19
  27.0 1.3 copy-start.21
  27.0 1.3 copy-start.24
  30.8 0.7 copy-start.15
  33.3 11.8 %all-to-all-start.1 = ((bf16[4,128,128]{2,1,0:T(8,128)(2,1)}), bf16[4,128,128]{2,1,0:T(8,128)(2,1)S(1)}, u32[]{:S(2)}, u32[]{:S(2)}) async-start(bf16[4,128,128]{2,1,0:T(8,128)(2,1)} %bitcast.29), calls=%async_computation.1 | async-start | bytes 262144 | tf_op jit(solution)/shard_map/all_to_all | solution.py:60
  39.9 3.3 %collective-permute-start.1 = (bf16[128,128]{1,0:T(8,128)(2,1)}, bf16[128,128]{1,0:T(8,128)(2,1)}, u32[]{:S(2)}, u32[]{:S(2)}) collective-permute-start(bf16[128,128]{1,0:T(8,128)(2,1)} %slice.67), channel_id=1, source_target_pairs={{0,1},{1,0},{2,3},{3,2},{4,5},{5,4},{6,7},{7,6},{8,9},{9,8},{10,11... | collective-permute-start | bytes 98312 | tf_op jit(solution)/shard_map/ppermute | solution.py:57
  45.0 2.0 %copy-start.2 = (bf16[640,1024]{1,0:T(8,128)(2,1)S(1)}, bf16[640,1024]{1,0:T(8,128)(2,1)}, u32[]{:S(2)}) copy-start(bf16[640,1024]{1,0:T(8,128)(2,1)} %copy-done.1) | copy-start | bytes 3932164
  45.1 2.0 %copy-start.7 = (f32[640,128]{1,0:T(8,128)S(1)}, f32[640,128]{1,0:T(8,128)}, u32[]{:S(2)}) copy-start(f32[640,128]{1,0:T(8,128)} %copy-done.6) | copy-start | bytes 983044
  47.1 0.8 copy-start.13
  49.1 10.4 %all-to-all-start.2 = ((bf16[4,128,128]{2,1,0:T(8,128)(2,1)}), bf16[4,128,128]{2,1,0:T(8,128)(2,1)S(1)}, u32[]{:S(2)}, u32[]{:S(2)}) async-start(bf16[4,128,128]{2,1,0:T(8,128)(2,1)} %bitcast.32), calls=%async_computation.2 | async-start | bytes 262144 | tf_op jit(solution)/shard_map/all_to_all | solution.py:60
  54.4 2.4 %collective-permute-start.2 = (bf16[128,128]{1,0:T(8,128)(2,1)}, bf16[128,128]{1,0:T(8,128)(2,1)}, u32[]{:S(2)}, u32[]{:S(2)}) collective-permute-start(bf16[128,128]{1,0:T(8,128)(2,1)} %slice.69), channel_id=1, source_target_pairs={{0,1},{1,0},{2,3},{3,2},{4,5},{5,4},{6,7},{7,6},{8,9},{9,8},{10,11... | collective-permute-start | bytes 98312 | tf_op jit(solution)/shard_map/ppermute | solution.py:57
  61.5 0.7 copy-start.16
  63.9 10.6 %all-to-all-start.3 = ((bf16[4,128,128]{2,1,0:T(8,128)(2,1)}), bf16[4,128,128]{2,1,0:T(8,128)(2,1)S(1)}, u32[]{:S(2)}, u32[]{:S(2)}) async-start(bf16[4,128,128]{2,1,0:T(8,128)(2,1)} %bitcast.35), calls=%async_computation.3 | async-start | bytes 262144 | tf_op jit(solution)/shard_map/all_to_all | solution.py:60
  69.4 3.3 %collective-permute-start.3 = (bf16[128,128]{1,0:T(8,128)(2,1)}, bf16[128,128]{1,0:T(8,128)(2,1)}, u32[]{:S(2)}, u32[]{:S(2)}) collective-permute-start(bf16[128,128]{1,0:T(8,128)(2,1)} %slice.71), channel_id=1, source_target_pairs={{0,1},{1,0},{2,3},{3,2},{4,5},{5,4},{6,7},{7,6},{8,9},{9,8},{10,11... | collective-permute-start | bytes 98312 | tf_op jit(solution)/shard_map/ppermute | solution.py:57
  74.6 2.2 %copy-start.3 = (bf16[640,1024]{1,0:T(8,128)(2,1)S(1)}, bf16[640,1024]{1,0:T(8,128)(2,1)}, u32[]{:S(2)}) copy-start(bf16[640,1024]{1,0:T(8,128)(2,1)} %copy-done.1) | copy-start | bytes 3932164
  74.6 2.2 %copy-start.8 = (f32[640,128]{1,0:T(8,128)S(1)}, f32[640,128]{1,0:T(8,128)}, u32[]{:S(2)}) copy-start(f32[640,128]{1,0:T(8,128)} %copy-done.6) | copy-start | bytes 983044
  76.7 0.8 copy-start.12
  78.8 10.4 %all-to-all-start.4 = ((bf16[4,128,128]{2,1,0:T(8,128)(2,1)}), bf16[4,128,128]{2,1,0:T(8,128)(2,1)S(1)}, u32[]{:S(2)}, u32[]{:S(2)}) async-start(bf16[4,128,128]{2,1,0:T(8,128)(2,1)} %bitcast.38), calls=%async_computation.4 | async-start | bytes 262144 | tf_op jit(solution)/shard_map/all_to_all | solution.py:60
  84.1 2.4 %collective-permute-start.4 = (bf16[128,128]{1,0:T(8,128)(2,1)}, bf16[128,128]{1,0:T(8,128)(2,1)}, u32[]{:S(2)}, u32[]{:S(2)}) collective-permute-start(bf16[128,128]{1,0:T(8,128)(2,1)} %slice.73), channel_id=1, source_target_pairs={{0,1},{1,0},{2,3},{3,2},{4,5},{5,4},{6,7},{7,6},{8,9},{9,8},{10,11... | collective-permute-start | bytes 98312 | tf_op jit(solution)/shard_map/ppermute | solution.py:57
  91.1 0.7 copy-start.17
  93.6 10.4 %all-to-all-start.5 = ((bf16[4,128,128]{2,1,0:T(8,128)(2,1)}), bf16[4,128,128]{2,1,0:T(8,128)(2,1)S(1)}, u32[]{:S(2)}, u32[]{:S(2)}) async-start(bf16[4,128,128]{2,1,0:T(8,128)(2,1)} %bitcast.41), calls=%async_computation.5 | async-start | bytes 262144 | tf_op jit(solution)/shard_map/all_to_all | solution.py:60
  98.9 3.3 %collective-permute-start.5 = (bf16[128,128]{1,0:T(8,128)(2,1)}, bf16[128,128]{1,0:T(8,128)(2,1)}, u32[]{:S(2)}, u32[]{:S(2)}) collective-permute-start(bf16[128,128]{1,0:T(8,128)(2,1)} %slice.75), channel_id=1, source_target_pairs={{0,1},{1,0},{2,3},{3,2},{4,5},{5,4},{6,7},{7,6},{8,9},{9,8},{10,11... | collective-permute-start | bytes 98312 | tf_op jit(solution)/shard_map/ppermute | solution.py:57
  104.0 2.2 %copy-start.4 = (bf16[640,1024]{1,0:T(8,128)(2,1)S(1)}, bf16[640,1024]{1,0:T(8,128)(2,1)}, u32[]{:S(2)}) copy-start(bf16[640,1024]{1,0:T(8,128)(2,1)} %copy-done.1) | copy-start | bytes 3932164
  104.0 2.2 %copy-start.9 = (f32[640,128]{1,0:T(8,128)S(1)}, f32[640,128]{1,0:T(8,128)}, u32[]{:S(2)}) copy-start(f32[640,128]{1,0:T(8,128)} %copy-done.6) | copy-start | bytes 983044
  106.2 0.8 copy-start.10
  108.3 10.4 %all-to-all-start.6 = ((bf16[4,128,128]{2,1,0:T(8,128)(2,1)}), bf16[4,128,128]{2,1,0:T(8,128)(2,1)S(1)}, u32[]{:S(2)}, u32[]{:S(2)}) async-start(bf16[4,128,128]{2,1,0:T(8,128)(2,1)} %bitcast.44), calls=%async_computation.6 | async-start | bytes 262144 | tf_op jit(solution)/shard_map/all_to_all | solution.py:60
  113.6 2.4 %collective-permute-start.6 = (bf16[128,128]{1,0:T(8,128)(2,1)}, bf16[128,128]{1,0:T(8,128)(2,1)}, u32[]{:S(2)}, u32[]{:S(2)}) collective-permute-start(bf16[128,128]{1,0:T(8,128)(2,1)} %slice.77), channel_id=1, source_target_pairs={{0,1},{1,0},{2,3},{3,2},{4,5},{5,4},{6,7},{7,6},{8,9},{9,8},{10,11... | collective-permute-start | bytes 98312 | tf_op jit(solution)/shard_map/ppermute | solution.py:57
  120.6 0.7 copy-start.14
  121.3 11.1 %copy-start.11 = (f32[1024,128]{0,1:T(8,128)S(1)}, f32[1024,128]{0,1:T(8,128)}, u32[]{:S(2)}) copy-start(f32[1024,128]{0,1:T(8,128)} %copy-done.10) | copy-start | bytes 1572868
  121.3 11.1 %copy-start.22 = (s32[640]{0:T(1024)S(1)}, s32[640]{0:T(1024)}, u32[]{:S(2)}) copy-start(s32[640]{0:T(1024)} %copy-done.20) | copy-start | bytes 7684
  121.3 11.1 %copy-start.25 = (pred[640]{0:T(1024)(128)(4,1)S(1)}, pred[640]{0:T(1024)(128)(4,1)}, u32[]{:S(2)}) copy-start(pred[640]{0:T(1024)(128)(4,1)} %copy-done.23) | copy-start | bytes 1924
  122.0 10.4 %all-to-all-start.7 = ((bf16[4,128,128]{2,1,0:T(8,128)(2,1)}), bf16[4,128,128]{2,1,0:T(8,128)(2,1)S(1)}, u32[]{:S(2)}, u32[]{:S(2)}) async-start(bf16[4,128,128]{2,1,0:T(8,128)(2,1)} %bitcast.47), calls=%async_computation.7 | async-start | bytes 262144 | tf_op jit(solution)/shard_map/all_to_all | solution.py:60
  127.3 3.3 %collective-permute-start.7 = (bf16[128,128]{1,0:T(8,128)(2,1)S(1)}, bf16[128,128]{1,0:T(8,128)(2,1)S(1)}, u32[]{:S(2)}, u32[]{:S(2)}) collective-permute-start(bf16[128,128]{1,0:T(8,128)(2,1)S(1)} %slice.79), channel_id=1, source_target_pairs={{0,1},{1,0},{2,3},{3,2},{4,5},{5,4},{6,7},{7,6},{8,9},{9,8},{10,11... | collective-permute-start | bytes 98312 | tf_op jit(solution)/shard_map/ppermute | solution.py:57

commit v4 on v1

--- a/solution.py
+++ b/solution.py
@@ -14,10 +14,10 @@
     cross = [(i, j % count) for i, j in cross]
     blocks = count // FAR
     far = [(i, i ^ FAR) for i in range(count)] if blocks > 1 else []
-    pairs = [far, near, cross]
+    pairs = [cross, near, far]
     if blocks > 2:
         again = [(i, (((i // FAR + 1) ^ 1) - 1) % blocks * FAR + i % FAR) for i in range(count)]
-        pairs = [far, again, near, cross]
+        pairs = [cross, near, far, again]
     return [p for p in pairs if p]
 
 
@@ -26,8 +26,8 @@
     block = index // FAR % 2
     far, again = 2 + block, 3 - block
     if count // FAR > 2:
-        return [far, again, odd, 1 - odd]
-    return [far, odd, 1 - odd]
+        return [1 - odd, odd, far, again]
+    return [1 - odd, odd, far]
 
 
 def body(right_side, schur, neumann, weights, neighbours, counts, shared_rows):

time: 81.7 us -> 76.8 us (0.940)
  waiting for transfers between devices: 35 us -> 28 us
  starting transfers between devices: 21.2 us -> 23.2 us
    ppermute x24, waiting for transfers between devices: 35 us -> 28 us  [exchange(): lax.ppermute(packed[k * share:(k + 1) * share], 'sub', route)]
    ppermute x24, starting transfers between devices: 21.2 us -> 23.2 us  [exchange(): lax.ppermute(packed[k * share:(k + 1) * share], 'sub', route)]
  transfers between devices with their start and end apart: 24 -> 24, of which waited for: 14 -> 7; matrix products, arithmetic and copies ran while one was open for 11% -> 12% of each run, Pallas kernels for 0% -> 0%
where the time goes in v4:
time: 76.8 us; the launch traced here: 76.5 us
  waiting for transfers between devices  28 us (36%)
  starting transfers between devices  23.2 us (30%)
  matrix products  17.5 us (23%)
  local copies, waits for them, and re-layouts  4.48 us (6%)
  between operations  2.92 us (4%)
    ppermute x24, waiting for transfers between devices, exchange(): lax.ppermute(packed[k * share:(k + 1) * share], 'sub', route)  28 us
    ppermute x24, starting transfers between devices, exchange(): lax.ppermute(packed[k * share:(k + 1) * share], 'sub', route)  23.2 us
    dot_general x8, matrix products, exchange(): jnp.dot(placer, jnp.concatenate(parts, 0), preferred_element_type=jnp.flo...  4.28 us
    dot_general x8, matrix products, transposed(): lax.dot_general(mat, block, (((0,), (0,)), ((), ())), preferred_element_t...  3.33 us
    dot_general x4, matrix products, body(): jnp.dot(n_mat, scaled, preferred_element_type=jnp.float32)  3.32 us
    dot_general x1, matrix products, body(): lax.dot_general(placer, n_mat, (((0,), (0,)), ((), ())), preferred_elemen...  2.62 us
  transfers between devices with their start and end apart: 24, of which 7 were waited for; matrix products, arithmetic and copies ran while one was open for 12% of the time, Pallas kernels for 0%

profile of v4, /device:TPU:0, one launch (start us, length us, event | category | flops | bytes accessed | tf_op | source)
XLA Modules:
  0.0 76.5 jit_solution(3300631686968190888)
XLA Ops:
  0.0 1.5 %constant_dynamic-slice_fusion.2 = (s32[1,1]{1,0:T(1,128)}, s32[1,1]{1,0:T(1,128)}, s32[1,1]{1,0:T(1,128)}) fusion(s32[1,4]{1,0:T(1,128)} %param.11, s32[]{:T(128)S(6)} %select_n.34, s32[]{:T(128)S(6)} %select_n.38, s32[]{:T(128)S(6)} %select_n.35), kind=kLoop, calls=%fused_computation.173 | loop fusion | bytes 36 | tf_op jit(solution)/shard_map/jit(dynamic_index_in_dim)/dynamic_slice | solution.py:47
  3.4 0.8 %fusion.263 = (s32[128]{0:T(128)S(1)}, s32[128]{0:T(128)S(1)}, s32[128]{0:T(128)S(1)}) fusion(s32[1,4,128]{2,1,0:T(4,128)} %param.13, s32[]{:T(128)S(6)} %select_n.34, s32[]{:T(128)S(6)} %select_n.38, s32[]{:T(128)S(6)} %select_n.35), kind=kLoop, calls=%fused_computation.177 | loop fusion | bytes 3084 | tf_op jit(solution)/shard_map/jit(dynamic_index_in_dim)/squeeze | solution.py:45
  4.2 1.4 %fusion.188 = f32[384,128]{1,0:T(8,128)S(1)} fusion(s32[384]{0:T(512)S(1)} %pad_add_fusion, pred[384]{0:T(512)(128)(4,1)S(1)} %pad_add_fusion.1, bf16[1,1024,128]{2,1,0:T(8,128)(2,1)} %param.7), kind=kOutput, calls=%fused_computation.94 | convolution fusion | flops 101842944 | bytes 460672 | tf_op jit(solution)/shard_map/dot_general | solution.py:53
  5.7 1.0 %fusion.44 = bf16[384,1024]{1,0:T(8,128)(2,1)S(1)} fusion(bf16[1,1024,1024]{2,1,0:T(8,128)(2,1)S(1)} %copy-done, s32[384]{0:T(512)S(1)} %pad_add_fusion, pred[384]{0:T(512)(128)(4,1)S(1)} %pad_add_fusion.1), kind=kOutput, calls=%fused_computation.33 | convolution fusion | flops 806879232 | bytes 2885504 | tf_op jit(solution)/shard_map/dot_general | solution.py:54
  7.1 6.4 %collective-permute-start = (bf16[128,128]{1,0:T(8,128)(2,1)S(1)}, bf16[128,128]{1,0:T(8,128)(2,1)S(1)}, u32[]{:S(2)}, u32[]{:S(2)}) collective-permute-start(bf16[128,128]{1,0:T(8,128)(2,1)S(1)} %get-tuple-element.26), channel_id=1, source_target_pairs={{0,31},{1,2},{2,1},{3,4},{4,3},{5,6},{6,5},{7,8},{8,7},{9,10},{10,... | collective-permute-start | bytes 98312 | tf_op jit(solution)/shard_map/ppermute | solution.py:62
  13.5 1.1 %copy.18 = bf16[1,1024,128]{1,2,0:T(8,128)(2,1)S(1)} copy(bf16[1,1024,128]{2,1,0:T(8,128)(2,1)} %param.7) | data formatting | bytes 524288 | tf_op args[0]
  15.3 2.6 %fusion.39 = bf16[384,1024]{1,0:T(8,128)(2,1)S(1)} fusion(bf16[1,1024,1024]{2,1,0:T(8,128)(2,1)} %param.9, s32[384]{0:T(512)S(1)} %pad_add_fusion, pred[384]{0:T(512)(128)(4,1)S(1)} %pad_add_fusion.1), kind=kOutput, calls=%fused_computation.32 | convolution fusion | flops 806486016 | bytes 2885504 | tf_op jit(solution)/shard_map/dot_general | solution.py:55
  17.9 0.4 fusion.104
  18.4 0.4 select_reduce_fusion
  18.8 0.5 fusion.167
  19.3 0.4 fusion.180
  19.7 1.9 %collective-permute-start.3 = (bf16[128,128]{1,0:T(8,128)(2,1)S(1)}, bf16[128,128]{1,0:T(8,128)(2,1)S(1)}, u32[]{:S(2)}, u32[]{:S(2)}) collective-permute-start(bf16[128,128]{1,0:T(8,128)(2,1)S(1)} %get-tuple-element.23), channel_id=1, source_target_pairs={{0,31},{1,2},{2,1},{3,4},{4,3},{5,6},{6,5},{7,8},{8,7},{9,10},{10,... | collective-permute-start | bytes 98312 | tf_op jit(solution)/shard_map/ppermute | solution.py:62
  21.6 1.2 %collective-permute-start.5 = (bf16[128,128]{1,0:T(8,128)(2,1)S(1)}, bf16[128,128]{1,0:T(8,128)(2,1)S(1)}, u32[]{:S(2)}, u32[]{:S(2)}) collective-permute-start(bf16[128,128]{1,0:T(8,128)(2,1)S(1)} %get-tuple-element.24), channel_id=1, source_target_pairs={{0,16},{1,17},{2,18},{3,19},{4,20},{5,21},{6,22},{7,23},{8,24},{9,... | collective-permute-start | bytes 98312 | tf_op jit(solution)/shard_map/ppermute | solution.py:62
  23.0 0.8 %fusion.146 = f32[1024,128]{0,1:T(8,128)S(1)} fusion(bf16[1024,128]{0,1:T(8,128)(2,1)S(1)} %fusion.167, bf16[1,1024,1024]{2,1,0:T(8,128)(2,1)S(1)} %copy-done.1, f32[1024]{0:T(1024)S(1)} %fusion.262), kind=kOutput, calls=%fused_computation.67 | convolution fusion | flops 268566528 | bytes 2887680 | tf_op jit(solution)/shard_map/dot_general | solution.py:77
  23.9 3.3 %collective-permute-done.3 = bf16[128,128]{1,0:T(8,128)(2,1)S(1)} collective-permute-done((bf16[128,128]{1,0:T(8,128)(2,1)S(1)}, bf16[128,128]{1,0:T(8,128)(2,1)S(1)}, u32[]{:S(2)}, u32[]{:S(2)}) %collective-permute-start.3) | collective-permute-done | bytes 32800 | tf_op jit(solution)/shard_map/ppermute | solution.py:62
  27.1 0.5 fusion.128
  27.7 0.4 fusion.181
  28.1 1.7 %collective-permute-start.6 = (bf16[128,128]{1,0:T(8,128)(2,1)S(1)}, bf16[128,128]{1,0:T(8,128)(2,1)S(1)}, u32[]{:S(2)}, u32[]{:S(2)}) collective-permute-start(bf16[128,128]{1,0:T(8,128)(2,1)S(1)} %get-tuple-element.20), channel_id=1, source_target_pairs={{0,31},{1,2},{2,1},{3,4},{4,3},{5,6},{6,5},{7,8},{8,7},{9,10},{10,... | collective-permute-start | bytes 98312 | tf_op jit(solution)/shard_map/ppermute | solution.py:62
  29.8 1.1 %collective-permute-start.8 = (bf16[128,128]{1,0:T(8,128)(2,1)S(1)}, bf16[128,128]{1,0:T(8,128)(2,1)S(1)}, u32[]{:S(2)}, u32[]{:S(2)}) collective-permute-start(bf16[128,128]{1,0:T(8,128)(2,1)S(1)} %get-tuple-element.21), channel_id=1, source_target_pairs={{0,16},{1,17},{2,18},{3,19},{4,20},{5,21},{6,22},{7,23},{8,24},{9,... | collective-permute-start | bytes 98312 | tf_op jit(solution)/shard_map/ppermute | solution.py:62
  30.9 0.5 fusion.98
  31.4 3.7 %collective-permute-done.6 = bf16[128,128]{1,0:T(8,128)(2,1)S(1)} collective-permute-done((bf16[128,128]{1,0:T(8,128)(2,1)S(1)}, bf16[128,128]{1,0:T(8,128)(2,1)S(1)}, u32[]{:S(2)}, u32[]{:S(2)}) %collective-permute-start.6) | collective-permute-done | bytes 32800 | tf_op jit(solution)/shard_map/ppermute | solution.py:62
  35.1 0.5 fusion.170
  35.6 0.4 fusion.182
  36.0 2.1 %collective-permute-start.9 = (bf16[128,128]{1,0:T(8,128)(2,1)S(1)}, bf16[128,128]{1,0:T(8,128)(2,1)S(1)}, u32[]{:S(2)}, u32[]{:S(2)}) collective-permute-start(bf16[128,128]{1,0:T(8,128)(2,1)S(1)} %get-tuple-element.17), channel_id=1, source_target_pairs={{0,31},{1,2},{2,1},{3,4},{4,3},{5,6},{6,5},{7,8},{8,7},{9,10},{10,... | collective-permute-start | bytes 98312 | tf_op jit(solution)/shard_map/ppermute | solution.py:62
  38.2 0.8 %fusion.152 = f32[1024,128]{0,1:T(8,128)S(1)} fusion(bf16[1024,128]{0,1:T(8,128)(2,1)S(1)} %fusion.170, bf16[1,1024,1024]{2,1,0:T(8,128)(2,1)S(1)} %copy-done.1, f32[1024]{0:T(1024)S(1)} %fusion.262), kind=kOutput, calls=%fused_computation.69 | convolution fusion | flops 268566528 | bytes 2887680 | tf_op jit(solution)/shard_map/dot_general | solution.py:77
  39.0 4.0 %collective-permute-done.9 = bf16[128,128]{1,0:T(8,128)(2,1)S(1)} collective-permute-done((bf16[128,128]{1,0:T(8,128)(2,1)S(1)}, bf16[128,128]{1,0:T(8,128)(2,1)S(1)}, u32[]{:S(2)}, u32[]{:S(2)}) %collective-permute-start.9) | collective-permute-done | bytes 32800 | tf_op jit(solution)/shard_map/ppermute | solution.py:62
  43.0 0.5 fusion.122
  43.6 0.4 fusion.183
  44.0 2.2 %collective-permute-start.12 = (bf16[128,128]{1,0:T(8,128)(2,1)S(1)}, bf16[128,128]{1,0:T(8,128)(2,1)S(1)}, u32[]{:S(2)}, u32[]{:S(2)}) collective-permute-start(bf16[128,128]{1,0:T(8,128)(2,1)S(1)} %get-tuple-element.14), channel_id=1, source_target_pairs={{0,31},{1,2},{2,1},{3,4},{4,3},{5,6},{6,5},{7,8},{8,7},{9,10},{10,... | collective-permute-start | bytes 98312 | tf_op jit(solution)/shard_map/ppermute | solution.py:62
  46.2 0.5 fusion.92
  46.6 4.4 %collective-permute-done.12 = bf16[128,128]{1,0:T(8,128)(2,1)S(1)} collective-permute-done((bf16[128,128]{1,0:T(8,128)(2,1)S(1)}, bf16[128,128]{1,0:T(8,128)(2,1)S(1)}, u32[]{:S(2)}, u32[]{:S(2)}) %collective-permute-start.12) | collective-permute-done | bytes 32800 | tf_op jit(solution)/shard_map/ppermute | solution.py:62
  51.0 0.5 fusion.173
  51.5 0.4 fusion.184
  51.9 2.2 %collective-permute-start.15 = (bf16[128,128]{1,0:T(8,128)(2,1)S(1)}, bf16[128,128]{1,0:T(8,128)(2,1)S(1)}, u32[]{:S(2)}, u32[]{:S(2)}) collective-permute-start(bf16[128,128]{1,0:T(8,128)(2,1)S(1)} %get-tuple-element.11), channel_id=1, source_target_pairs={{0,31},{1,2},{2,1},{3,4},{4,3},{5,6},{6,5},{7,8},{8,7},{9,10},{10,... | collective-permute-start | bytes 98312 | tf_op jit(solution)/shard_map/ppermute | solution.py:62
  54.1 0.8 %fusion.158 = f32[1024,128]{0,1:T(8,128)S(1)} fusion(bf16[1024,128]{0,1:T(8,128)(2,1)S(1)} %fusion.173, bf16[1,1024,1024]{2,1,0:T(8,128)(2,1)S(1)} %copy-done.1, f32[1024]{0:T(1024)S(1)} %fusion.262), kind=kOutput, calls=%fused_computation.71 | convolution fusion | flops 268566528 | bytes 2887680 | tf_op jit(solution)/shard_map/dot_general | solution.py:77
  54.9 4.1 %collective-permute-done.15 = bf16[128,128]{1,0:T(8,128)(2,1)S(1)} collective-permute-done((bf16[128,128]{1,0:T(8,128)(2,1)S(1)}, bf16[128,128]{1,0:T(8,128)(2,1)S(1)}, u32[]{:S(2)}, u32[]{:S(2)}) %collective-permute-start.15) | collective-permute-done | bytes 32800 | tf_op jit(solution)/shard_map/ppermute | solution.py:62
  59.0 0.5 fusion.113
  59.6 0.4 fusion.185
  60.0 2.1 %collective-permute-start.18 = (bf16[128,128]{1,0:T(8,128)(2,1)S(1)}, bf16[128,128]{1,0:T(8,128)(2,1)S(1)}, u32[]{:S(2)}, u32[]{:S(2)}) collective-permute-start(bf16[128,128]{1,0:T(8,128)(2,1)S(1)} %get-tuple-element.8), channel_id=1, source_target_pairs={{0,31},{1,2},{2,1},{3,4},{4,3},{5,6},{6,5},{7,8},{8,7},{9,10},{10,... | collective-permute-start | bytes 98312 | tf_op jit(solution)/shard_map/ppermute | solution.py:62
  62.1 0.5 fusion.86
  62.5 4.5 %collective-permute-done.18 = bf16[128,128]{1,0:T(8,128)(2,1)S(1)} collective-permute-done((bf16[128,128]{1,0:T(8,128)(2,1)S(1)}, bf16[128,128]{1,0:T(8,128)(2,1)S(1)}, u32[]{:S(2)}, u32[]{:S(2)}) %collective-permute-start.18) | collective-permute-done | bytes 32800 | tf_op jit(solution)/shard_map/ppermute | solution.py:62
  67.0 0.5 fusion.176
  67.5 0.4 fusion.186
  67.9 2.1 %collective-permute-start.21 = (bf16[128,128]{1,0:T(8,128)(2,1)S(1)}, bf16[128,128]{1,0:T(8,128)(2,1)S(1)}, u32[]{:S(2)}, u32[]{:S(2)}) collective-permute-start(bf16[128,128]{1,0:T(8,128)(2,1)S(1)} %get-tuple-element.5), channel_id=1, source_target_pairs={{0,31},{1,2},{2,1},{3,4},{4,3},{5,6},{6,5},{7,8},{8,7},{9,10},{10,... | collective-permute-start | bytes 98312 | tf_op jit(solution)/shard_map/ppermute | solution.py:62
  70.1 0.8 %fusion.164 = f32[1024,128]{0,1:T(8,128)S(1)} fusion(bf16[1024,128]{0,1:T(8,128)(2,1)S(1)} %fusion.176, bf16[1,1024,1024]{2,1,0:T(8,128)(2,1)S(1)} %copy-done.1, f32[1024]{0:T(1024)S(1)} %fusion.262), kind=kOutput, calls=%fused_computation.73 | convolution fusion | flops 268566528 | bytes 2887680 | tf_op jit(solution)/shard_map/dot_general | solution.py:77
  70.9 4.0 %collective-permute-done.21 = bf16[128,128]{1,0:T(8,128)(2,1)S(1)} collective-permute-done((bf16[128,128]{1,0:T(8,128)(2,1)S(1)}, bf16[128,128]{1,0:T(8,128)(2,1)S(1)}, u32[]{:S(2)}, u32[]{:S(2)}) %collective-permute-start.21) | collective-permute-done | bytes 32800 | tf_op jit(solution)/shard_map/ppermute | solution.py:62
  75.0 0.5 fusion.140
  75.5 1.0 %copy.27 = f32[1,1024,128]{2,1,0:T(8,128)} copy(f32[1,1024,128]{1,2,0:T(8,128)S(1)} %fusion.140) | data formatting | bytes 1048576 | tf_op jit(solution)/shard_map/broadcast_in_dim | solution.py:79
  (53 shorter events, 0.8 us)
Async XLA Ops:
  0.0 5.7 %copy-start = (bf16[1,1024,1024]{2,1,0:T(8,128)(2,1)S(1)}, bf16[1,1024,1024]{2,1,0:T(8,128)(2,1)}, u32[]{:S(2)}) copy-start(bf16[1,1024,1024]{2,1,0:T(8,128)(2,1)} %param.8) | copy-start | bytes 6291460
  7.1 11.7 %collective-permute-start = (bf16[128,128]{1,0:T(8,128)(2,1)S(1)}, bf16[128,128]{1,0:T(8,128)(2,1)S(1)}, u32[]{:S(2)}, u32[]{:S(2)}) collective-permute-start(bf16[128,128]{1,0:T(8,128)(2,1)S(1)} %get-tuple-element.26), channel_id=1, source_target_pairs={{0,31},{1,2},{2,1},{3,4},{4,3},{5,6},{6,5},{7,8},{8,7},{9,10},{10,... | collective-permute-start | bytes 98312 | tf_op jit(solution)/shard_map/ppermute | solution.py:62
  13.5 5.3 %collective-permute-start.2 = (bf16[128,128]{1,0:T(8,128)(2,1)S(1)}, bf16[128,128]{1,0:T(8,128)(2,1)S(1)}, u32[]{:S(2)}, u32[]{:S(2)}) collective-permute-start(bf16[128,128]{1,0:T(8,128)(2,1)S(1)} %get-tuple-element.27), channel_id=1, source_target_pairs={{0,16},{1,17},{2,18},{3,19},{4,20},{5,21},{6,22},{7,23},{8,24},{9,... | collective-permute-start | bytes 98312 | tf_op jit(solution)/shard_map/ppermute | solution.py:62
  13.5 5.3 %collective-permute-start.1 = (bf16[128,128]{1,0:T(8,128)(2,1)S(1)}, bf16[128,128]{1,0:T(8,128)(2,1)S(1)}, u32[]{:S(2)}, u32[]{:S(2)}) collective-permute-start(bf16[128,128]{1,0:T(8,128)(2,1)S(1)} %get-tuple-element.28), channel_id=1, source_target_pairs={{0,1},{1,0},{2,3},{3,2},{4,5},{5,4},{6,7},{7,6},{8,9},{9,8},{10,11... | collective-permute-start | bytes 98312 | tf_op jit(solution)/shard_map/ppermute | solution.py:62
  15.3 2.6 %copy-start.2 = (f32[1,1024]{1,0:T(1,128)S(1)}, f32[1,1024]{1,0:T(1,128)}, u32[]{:S(2)}) copy-start(f32[1,1024]{1,0:T(1,128)} %param.10) | copy-start | bytes 12292
  18.4 4.6 %copy-start.1 = (bf16[1,1024,1024]{2,1,0:T(8,128)(2,1)S(1)}, bf16[1,1024,1024]{2,1,0:T(8,128)(2,1)}, u32[]{:S(2)}) copy-start(bf16[1,1024,1024]{2,1,0:T(8,128)(2,1)} %param.9) | copy-start | bytes 6291460
  19.7 7.4 %collective-permute-start.3 = (bf16[128,128]{1,0:T(8,128)(2,1)S(1)}, bf16[128,128]{1,0:T(8,128)(2,1)S(1)}, u32[]{:S(2)}, u32[]{:S(2)}) collective-permute-start(bf16[128,128]{1,0:T(8,128)(2,1)S(1)} %get-tuple-element.23), channel_id=1, source_target_pairs={{0,31},{1,2},{2,1},{3,4},{4,3},{5,6},{6,5},{7,8},{8,7},{9,10},{10,... | collective-permute-start | bytes 98312 | tf_op jit(solution)/shard_map/ppermute | solution.py:62
  21.6 5.5 %collective-permute-start.5 = (bf16[128,128]{1,0:T(8,128)(2,1)S(1)}, bf16[128,128]{1,0:T(8,128)(2,1)S(1)}, u32[]{:S(2)}, u32[]{:S(2)}) collective-permute-start(bf16[128,128]{1,0:T(8,128)(2,1)S(1)} %get-tuple-element.24), channel_id=1, source_target_pairs={{0,16},{1,17},{2,18},{3,19},{4,20},{5,21},{6,22},{7,23},{8,24},{9,... | collective-permute-start | bytes 98312 | tf_op jit(solution)/shard_map/ppermute | solution.py:62
  22.8 4.3 %collective-permute-start.4 = (bf16[128,128]{1,0:T(8,128)(2,1)S(1)}, bf16[128,128]{1,0:T(8,128)(2,1)S(1)}, u32[]{:S(2)}, u32[]{:S(2)}) collective-permute-start(bf16[128,128]{1,0:T(8,128)(2,1)S(1)} %get-tuple-element.25), channel_id=1, source_target_pairs={{0,1},{1,0},{2,3},{3,2},{4,5},{5,4},{6,7},{7,6},{8,9},{9,8},{10,11... | collective-permute-start | bytes 98312 | tf_op jit(solution)/shard_map/ppermute | solution.py:62
  28.1 7.0 %collective-permute-start.6 = (bf16[128,128]{1,0:T(8,128)(2,1)S(1)}, bf16[128,128]{1,0:T(8,128)(2,1)S(1)}, u32[]{:S(2)}, u32[]{:S(2)}) collective-permute-start(bf16[128,128]{1,0:T(8,128)(2,1)S(1)} %get-tuple-element.20), channel_id=1, source_target_pairs={{0,31},{1,2},{2,1},{3,4},{4,3},{5,6},{6,5},{7,8},{8,7},{9,10},{10,... | collective-permute-start | bytes 98312 | tf_op jit(solution)/shard_map/ppermute | solution.py:62
  29.8 5.3 %collective-permute-start.8 = (bf16[128,128]{1,0:T(8,128)(2,1)S(1)}, bf16[128,128]{1,0:T(8,128)(2,1)S(1)}, u32[]{:S(2)}, u32[]{:S(2)}) collective-permute-start(bf16[128,128]{1,0:T(8,128)(2,1)S(1)} %get-tuple-element.21), channel_id=1, source_target_pairs={{0,16},{1,17},{2,18},{3,19},{4,20},{5,21},{6,22},{7,23},{8,24},{9,... | collective-permute-start | bytes 98312 | tf_op jit(solution)/shard_map/ppermute | solution.py:62
  30.9 4.2 %collective-permute-start.7 = (bf16[128,128]{1,0:T(8,128)(2,1)S(1)}, bf16[128,128]{1,0:T(8,128)(2,1)S(1)}, u32[]{:S(2)}, u32[]{:S(2)}) collective-permute-start(bf16[128,128]{1,0:T(8,128)(2,1)S(1)} %get-tuple-element.22), channel_id=1, source_target_pairs={{0,1},{1,0},{2,3},{3,2},{4,5},{5,4},{6,7},{7,6},{8,9},{9,8},{10,11... | collective-permute-start | bytes 98312 | tf_op jit(solution)/shard_map/ppermute | solution.py:62
  36.0 7.0 %collective-permute-start.9 = (bf16[128,128]{1,0:T(8,128)(2,1)S(1)}, bf16[128,128]{1,0:T(8,128)(2,1)S(1)}, u32[]{:S(2)}, u32[]{:S(2)}) collective-permute-start(bf16[128,128]{1,0:T(8,128)(2,1)S(1)} %get-tuple-element.17), channel_id=1, source_target_pairs={{0,31},{1,2},{2,1},{3,4},{4,3},{5,6},{6,5},{7,8},{8,7},{9,10},{10,... | collective-permute-start | bytes 98312 | tf_op jit(solution)/shard_map/ppermute | solution.py:62
  38.2 4.9 %collective-permute-start.11 = (bf16[128,128]{1,0:T(8,128)(2,1)S(1)}, bf16[128,128]{1,0:T(8,128)(2,1)S(1)}, u32[]{:S(2)}, u32[]{:S(2)}) collective-permute-start(bf16[128,128]{1,0:T(8,128)(2,1)S(1)} %get-tuple-element.18), channel_id=1, source_target_pairs={{0,16},{1,17},{2,18},{3,19},{4,20},{5,21},{6,22},{7,23},{8,24},{9,... | collective-permute-start | bytes 98312 | tf_op jit(solution)/shard_map/ppermute | solution.py:62
  38.2 4.9 %collective-permute-start.10 = (bf16[128,128]{1,0:T(8,128)(2,1)S(1)}, bf16[128,128]{1,0:T(8,128)(2,1)S(1)}, u32[]{:S(2)}, u32[]{:S(2)}) collective-permute-start(bf16[128,128]{1,0:T(8,128)(2,1)S(1)} %get-tuple-element.19), channel_id=1, source_target_pairs={{0,1},{1,0},{2,3},{3,2},{4,5},{5,4},{6,7},{7,6},{8,9},{9,8},{10,11... | collective-permute-start | bytes 98312 | tf_op jit(solution)/shard_map/ppermute | solution.py:62
  44.0 7.0 %collective-permute-start.12 = (bf16[128,128]{1,0:T(8,128)(2,1)S(1)}, bf16[128,128]{1,0:T(8,128)(2,1)S(1)}, u32[]{:S(2)}, u32[]{:S(2)}) collective-permute-start(bf16[128,128]{1,0:T(8,128)(2,1)S(1)} %get-tuple-element.14), channel_id=1, source_target_pairs={{0,31},{1,2},{2,1},{3,4},{4,3},{5,6},{6,5},{7,8},{8,7},{9,10},{10,... | collective-permute-start | bytes 98312 | tf_op jit(solution)/shard_map/ppermute | solution.py:62
  46.2 4.8 %collective-permute-start.14 = (bf16[128,128]{1,0:T(8,128)(2,1)S(1)}, bf16[128,128]{1,0:T(8,128)(2,1)S(1)}, u32[]{:S(2)}, u32[]{:S(2)}) collective-permute-start(bf16[128,128]{1,0:T(8,128)(2,1)S(1)} %get-tuple-element.15), channel_id=1, source_target_pairs={{0,16},{1,17},{2,18},{3,19},{4,20},{5,21},{6,22},{7,23},{8,24},{9,... | collective-permute-start | bytes 98312 | tf_op jit(solution)/shard_map/ppermute | solution.py:62
  46.2 4.8 %collective-permute-start.13 = (bf16[128,128]{1,0:T(8,128)(2,1)S(1)}, bf16[128,128]{1,0:T(8,128)(2,1)S(1)}, u32[]{:S(2)}, u32[]{:S(2)}) collective-permute-start(bf16[128,128]{1,0:T(8,128)(2,1)S(1)} %get-tuple-element.16), channel_id=1, source_target_pairs={{0,1},{1,0},{2,3},{3,2},{4,5},{5,4},{6,7},{7,6},{8,9},{9,8},{10,11... | collective-permute-start | bytes 98312 | tf_op jit(solution)/shard_map/ppermute | solution.py:62
  51.9 7.1 %collective-permute-start.15 = (bf16[128,128]{1,0:T(8,128)(2,1)S(1)}, bf16[128,128]{1,0:T(8,128)(2,1)S(1)}, u32[]{:S(2)}, u32[]{:S(2)}) collective-permute-start(bf16[128,128]{1,0:T(8,128)(2,1)S(1)} %get-tuple-element.11), channel_id=1, source_target_pairs={{0,31},{1,2},{2,1},{3,4},{4,3},{5,6},{6,5},{7,8},{8,7},{9,10},{10,... | collective-permute-start | bytes 98312 | tf_op jit(solution)/shard_map/ppermute | solution.py:62
  54.1 4.9 %collective-permute-start.17 = (bf16[128,128]{1,0:T(8,128)(2,1)S(1)}, bf16[128,128]{1,0:T(8,128)(2,1)S(1)}, u32[]{:S(2)}, u32[]{:S(2)}) collective-permute-start(bf16[128,128]{1,0:T(8,128)(2,1)S(1)} %get-tuple-element.12), channel_id=1, source_target_pairs={{0,16},{1,17},{2,18},{3,19},{4,20},{5,21},{6,22},{7,23},{8,24},{9,... | collective-permute-start | bytes 98312 | tf_op jit(solution)/shard_map/ppermute | solution.py:62
  54.1 4.9 %collective-permute-start.16 = (bf16[128,128]{1,0:T(8,128)(2,1)S(1)}, bf16[128,128]{1,0:T(8,128)(2,1)S(1)}, u32[]{:S(2)}, u32[]{:S(2)}) collective-permute-start(bf16[128,128]{1,0:T(8,128)(2,1)S(1)} %get-tuple-element.13), channel_id=1, source_target_pairs={{0,1},{1,0},{2,3},{3,2},{4,5},{5,4},{6,7},{7,6},{8,9},{9,8},{10,11... | collective-permute-start | bytes 98312 | tf_op jit(solution)/shard_map/ppermute | solution.py:62
  60.0 7.0 %collective-permute-start.18 = (bf16[128,128]{1,0:T(8,128)(2,1)S(1)}, bf16[128,128]{1,0:T(8,128)(2,1)S(1)}, u32[]{:S(2)}, u32[]{:S(2)}) collective-permute-start(bf16[128,128]{1,0:T(8,128)(2,1)S(1)} %get-tuple-element.8), channel_id=1, source_target_pairs={{0,31},{1,2},{2,1},{3,4},{4,3},{5,6},{6,5},{7,8},{8,7},{9,10},{10,... | collective-permute-start | bytes 98312 | tf_op jit(solution)/shard_map/ppermute | solution.py:62
  62.1 4.9 %collective-permute-start.20 = (bf16[128,128]{1,0:T(8,128)(2,1)S(1)}, bf16[128,128]{1,0:T(8,128)(2,1)S(1)}, u32[]{:S(2)}, u32[]{:S(2)}) collective-permute-start(bf16[128,128]{1,0:T(8,128)(2,1)S(1)} %get-tuple-element.9), channel_id=1, source_target_pairs={{0,16},{1,17},{2,18},{3,19},{4,20},{5,21},{6,22},{7,23},{8,24},{9,... | collective-permute-start | bytes 98312 | tf_op jit(solution)/shard_map/ppermute | solution.py:62
  62.1 4.9 %collective-permute-start.19 = (bf16[128,128]{1,0:T(8,128)(2,1)S(1)}, bf16[128,128]{1,0:T(8,128)(2,1)S(1)}, u32[]{:S(2)}, u32[]{:S(2)}) collective-permute-start(bf16[128,128]{1,0:T(8,128)(2,1)S(1)} %get-tuple-element.10), channel_id=1, source_target_pairs={{0,1},{1,0},{2,3},{3,2},{4,5},{5,4},{6,7},{7,6},{8,9},{9,8},{10,11... | collective-permute-start | bytes 98312 | tf_op jit(solution)/shard_map/ppermute | solution.py:62
  67.9 7.0 %collective-permute-start.21 = (bf16[128,128]{1,0:T(8,128)(2,1)S(1)}, bf16[128,128]{1,0:T(8,128)(2,1)S(1)}, u32[]{:S(2)}, u32[]{:S(2)}) collective-permute-start(bf16[128,128]{1,0:T(8,128)(2,1)S(1)} %get-tuple-element.5), channel_id=1, source_target_pairs={{0,31},{1,2},{2,1},{3,4},{4,3},{5,6},{6,5},{7,8},{8,7},{9,10},{10,... | collective-permute-start | bytes 98312 | tf_op jit(solution)/shard_map/ppermute | solution.py:62
  70.1 4.9 %collective-permute-start.23 = (bf16[128,128]{1,0:T(8,128)(2,1)S(1)}, bf16[128,128]{1,0:T(8,128)(2,1)S(1)}, u32[]{:S(2)}, u32[]{:S(2)}) collective-permute-start(bf16[128,128]{1,0:T(8,128)(2,1)S(1)} %get-tuple-element.6), channel_id=1, source_target_pairs={{0,16},{1,17},{2,18},{3,19},{4,20},{5,21},{6,22},{7,23},{8,24},{9,... | collective-permute-start | bytes 98312 | tf_op jit(solution)/shard_map/ppermute | solution.py:62
  70.1 4.9 %collective-permute-start.22 = (bf16[128,128]{1,0:T(8,128)(2,1)S(1)}, bf16[128,128]{1,0:T(8,128)(2,1)S(1)}, u32[]{:S(2)}, u32[]{:S(2)}) collective-permute-start(bf16[128,128]{1,0:T(8,128)(2,1)S(1)} %get-tuple-element.7), channel_id=1, source_target_pairs={{0,1},{1,0},{2,3},{3,2},{4,5},{5,4},{6,7},{7,6},{8,9},{9,8},{10,11... | collective-permute-start | bytes 98312 | tf_op jit(solution)/shard_map/ppermute | solution.py:62

commit v5 on v4

--- a/solution.py
+++ b/solution.py
@@ -10,8 +10,7 @@
 
 def swaps(count):
     near = [(i, i ^ 1) for i in range(count)]
-    cross = [(i, ((i + 1) ^ 1) - 1) for i in range(count)]
-    cross = [(i, j % count) for i, j in cross]
+    cross = [(i, ((i + 1) ^ 1) - 1) for i in range(1, count - 1)] + [(0, 0), (count - 1, count - 1)]
     blocks = count // FAR
     far = [(i, i ^ FAR) for i in range(count)] if blocks > 1 else []
     pairs = [cross, near, far]

time: 76.8 us -> 84.5 us (1.10)
  the two profiles are of different devices: /device:TPU:0 before, /device:TPU:8 now
where the time goes in v5:
time: 84.5 us; the launch traced here: 84 us
  starting transfers between devices  32.3 us (38%)
  waiting for transfers between devices  26.4 us (31%)
  matrix products  17.4 us (21%)
  local copies, waits for them, and re-layouts  4.48 us (5%)
  between operations  2.98 us (4%)
    ppermute x24, starting transfers between devices, exchange(): lax.ppermute(packed[k * share:(k + 1) * share], 'sub', route)  32.3 us
    ppermute x24, waiting for transfers between devices, exchange(): lax.ppermute(packed[k * share:(k + 1) * share], 'sub', route)  26.4 us
    dot_general x8, matrix products, exchange(): jnp.dot(placer, jnp.concatenate(parts, 0), preferred_element_type=jnp.flo...  4.27 us
    dot_general x4, matrix products, body(): jnp.dot(n_mat, scaled, preferred_element_type=jnp.float32)  3.32 us
    dot_general x8, matrix products, transposed(): lax.dot_general(mat, block, (((0,), (0,)), ((), ())), preferred_element_t...  3.31 us
    dot_general x1, matrix products, body(): lax.dot_general(placer, n_mat, (((0,), (0,)), ((), ())), preferred_elemen...  2.62 us
  transfers between devices with their start and end apart: 24, of which 14 were waited for; matrix products, arithmetic and copies ran while one was open for 11% of the time, Pallas kernels for 0%

profile of v5, /device:TPU:8, one launch (start us, length us, event | category | flops | bytes accessed | tf_op | source)
XLA Modules:
  0.0 84.0 jit_solution(5326934129642807154)
XLA Ops:
  0.0 1.5 %constant_dynamic-slice_fusion.2 = (s32[1,1]{1,0:T(1,128)}, s32[1,1]{1,0:T(1,128)}, s32[1,1]{1,0:T(1,128)}) fusion(s32[1,4]{1,0:T(1,128)} %param.11, s32[]{:T(128)S(6)} %select_n.34, s32[]{:T(128)S(6)} %select_n.38, s32[]{:T(128)S(6)} %select_n.35), kind=kLoop, calls=%fused_computation.173 | loop fusion | bytes 36 | tf_op jit(solution)/shard_map/jit(dynamic_index_in_dim)/dynamic_slice | solution.py:46
  3.4 0.8 fusion.263
  4.2 1.4 %fusion.188 = f32[384,128]{1,0:T(8,128)S(1)} fusion(s32[384]{0:T(512)S(1)} %pad_add_fusion, pred[384]{0:T(512)(128)(4,1)S(1)} %pad_add_fusion.1, bf16[1,1024,128]{2,1,0:T(8,128)(2,1)} %param.7), kind=kOutput, calls=%fused_computation.94 | convolution fusion | flops 101842944 | bytes 460672 | tf_op jit(solution)/shard_map/dot_general | solution.py:52
  5.7 1.0 %fusion.44 = bf16[384,1024]{1,0:T(8,128)(2,1)S(1)} fusion(bf16[1,1024,1024]{2,1,0:T(8,128)(2,1)S(1)} %copy-done, s32[384]{0:T(512)S(1)} %pad_add_fusion, pred[384]{0:T(512)(128)(4,1)S(1)} %pad_add_fusion.1), kind=kOutput, calls=%fused_computation.33 | convolution fusion | flops 806879232 | bytes 2885504 | tf_op jit(solution)/shard_map/dot_general | solution.py:53
  7.1 3.7 %collective-permute-start = (bf16[128,128]{1,0:T(8,128)(2,1)S(1)}, bf16[128,128]{1,0:T(8,128)(2,1)S(1)}, u32[]{:S(2)}, u32[]{:S(2)}) collective-permute-start(bf16[128,128]{1,0:T(8,128)(2,1)S(1)} %get-tuple-element.26), channel_id=1, source_target_pairs={{1,2},{2,1},{3,4},{4,3},{5,6},{6,5},{7,8},{8,7},{9,10},{10,9},{11,... | collective-permute-start | bytes 98312 | tf_op jit(solution)/shard_map/ppermute | solution.py:61
  10.8 2.7 %collective-permute-start.2 = (bf16[128,128]{1,0:T(8,128)(2,1)S(1)}, bf16[128,128]{1,0:T(8,128)(2,1)S(1)}, u32[]{:S(2)}, u32[]{:S(2)}) collective-permute-start(bf16[128,128]{1,0:T(8,128)(2,1)S(1)} %get-tuple-element.27), channel_id=1, source_target_pairs={{0,16},{1,17},{2,18},{3,19},{4,20},{5,21},{6,22},{7,23},{8,24},{9,... | collective-permute-start | bytes 98312 | tf_op jit(solution)/shard_map/ppermute | solution.py:61
  13.4 1.1 %copy.18 = bf16[1,1024,128]{1,2,0:T(8,128)(2,1)S(1)} copy(bf16[1,1024,128]{2,1,0:T(8,128)(2,1)} %param.7) | data formatting | bytes 524288 | tf_op args[0]
  15.2 2.6 %fusion.39 = bf16[384,1024]{1,0:T(8,128)(2,1)S(1)} fusion(bf16[1,1024,1024]{2,1,0:T(8,128)(2,1)} %param.9, s32[384]{0:T(512)S(1)} %pad_add_fusion, pred[384]{0:T(512)(128)(4,1)S(1)} %pad_add_fusion.1), kind=kOutput, calls=%fused_computation.32 | convolution fusion | flops 806486016 | bytes 2885504 | tf_op jit(solution)/shard_map/dot_general | solution.py:54
  17.8 0.4 fusion.104
  18.7 0.5 fusion.167
  19.6 3.4 %collective-permute-start.3 = (bf16[128,128]{1,0:T(8,128)(2,1)S(1)}, bf16[128,128]{1,0:T(8,128)(2,1)S(1)}, u32[]{:S(2)}, u32[]{:S(2)}) collective-permute-start(bf16[128,128]{1,0:T(8,128)(2,1)S(1)} %get-tuple-element.23), channel_id=1, source_target_pairs={{1,2},{2,1},{3,4},{4,3},{5,6},{6,5},{7,8},{8,7},{9,10},{10,9},{11,... | collective-permute-start | bytes 98312 | tf_op jit(solution)/shard_map/ppermute | solution.py:61
  23.5 0.8 fusion.146
  24.3 2.3 %collective-permute-done.3 = bf16[128,128]{1,0:T(8,128)(2,1)S(1)} collective-permute-done((bf16[128,128]{1,0:T(8,128)(2,1)S(1)}, bf16[128,128]{1,0:T(8,128)(2,1)S(1)}, u32[]{:S(2)}, u32[]{:S(2)}) %collective-permute-start.3) | collective-permute-done | bytes 32800 | tf_op jit(solution)/shard_map/ppermute | solution.py:61
  26.7 1.3 %collective-permute-done.5 = bf16[128,128]{1,0:T(8,128)(2,1)S(1)} collective-permute-done((bf16[128,128]{1,0:T(8,128)(2,1)S(1)}, bf16[128,128]{1,0:T(8,128)(2,1)S(1)}, u32[]{:S(2)}, u32[]{:S(2)}) %collective-permute-start.5) | collective-permute-done | bytes 32800 | tf_op jit(solution)/shard_map/ppermute | solution.py:61
  27.9 0.5 fusion.128
  28.9 3.2 %collective-permute-start.6 = (bf16[128,128]{1,0:T(8,128)(2,1)S(1)}, bf16[128,128]{1,0:T(8,128)(2,1)S(1)}, u32[]{:S(2)}, u32[]{:S(2)}) collective-permute-start(bf16[128,128]{1,0:T(8,128)(2,1)S(1)} %get-tuple-element.20), channel_id=1, source_target_pairs={{1,2},{2,1},{3,4},{4,3},{5,6},{6,5},{7,8},{8,7},{9,10},{10,9},{11,... | collective-permute-start | bytes 98312 | tf_op jit(solution)/shard_map/ppermute | solution.py:61
  32.3 0.5 fusion.98
  32.8 3.1 %collective-permute-done.6 = bf16[128,128]{1,0:T(8,128)(2,1)S(1)} collective-permute-done((bf16[128,128]{1,0:T(8,128)(2,1)S(1)}, bf16[128,128]{1,0:T(8,128)(2,1)S(1)}, u32[]{:S(2)}, u32[]{:S(2)}) %collective-permute-start.6) | collective-permute-done | bytes 32800 | tf_op jit(solution)/shard_map/ppermute | solution.py:61
  35.9 1.0 %collective-permute-done.8 = bf16[128,128]{1,0:T(8,128)(2,1)S(1)} collective-permute-done((bf16[128,128]{1,0:T(8,128)(2,1)S(1)}, bf16[128,128]{1,0:T(8,128)(2,1)S(1)}, u32[]{:S(2)}, u32[]{:S(2)}) %collective-permute-start.8) | collective-permute-done | bytes 32800 | tf_op jit(solution)/shard_map/ppermute | solution.py:61
  36.9 0.5 fusion.170
  37.9 3.4 %collective-permute-start.9 = (bf16[128,128]{1,0:T(8,128)(2,1)S(1)}, bf16[128,128]{1,0:T(8,128)(2,1)S(1)}, u32[]{:S(2)}, u32[]{:S(2)}) collective-permute-start(bf16[128,128]{1,0:T(8,128)(2,1)S(1)} %get-tuple-element.17), channel_id=1, source_target_pairs={{1,2},{2,1},{3,4},{4,3},{5,6},{6,5},{7,8},{8,7},{9,10},{10,9},{11,... | collective-permute-start | bytes 98312 | tf_op jit(solution)/shard_map/ppermute | solution.py:61
  41.5 0.8 fusion.152
  42.4 2.5 %collective-permute-done.9 = bf16[128,128]{1,0:T(8,128)(2,1)S(1)} collective-permute-done((bf16[128,128]{1,0:T(8,128)(2,1)S(1)}, bf16[128,128]{1,0:T(8,128)(2,1)S(1)}, u32[]{:S(2)}, u32[]{:S(2)}) %collective-permute-start.9) | collective-permute-done | bytes 32800 | tf_op jit(solution)/shard_map/ppermute | solution.py:61
  44.9 1.3 %collective-permute-done.11 = bf16[128,128]{1,0:T(8,128)(2,1)S(1)} collective-permute-done((bf16[128,128]{1,0:T(8,128)(2,1)S(1)}, bf16[128,128]{1,0:T(8,128)(2,1)S(1)}, u32[]{:S(2)}, u32[]{:S(2)}) %collective-permute-start.11) | collective-permute-done | bytes 32800 | tf_op jit(solution)/shard_map/ppermute | solution.py:61
  46.1 0.5 fusion.122
  47.1 2.8 %collective-permute-start.12 = (bf16[128,128]{1,0:T(8,128)(2,1)S(1)}, bf16[128,128]{1,0:T(8,128)(2,1)S(1)}, u32[]{:S(2)}, u32[]{:S(2)}) collective-permute-start(bf16[128,128]{1,0:T(8,128)(2,1)S(1)} %get-tuple-element.14), channel_id=1, source_target_pairs={{1,2},{2,1},{3,4},{4,3},{5,6},{6,5},{7,8},{8,7},{9,10},{10,9},{11,... | collective-permute-start | bytes 98312 | tf_op jit(solution)/shard_map/ppermute | solution.py:61
  49.9 0.6 collective-permute-start.14
  50.5 0.5 fusion.92
  51.0 3.1 %collective-permute-done.12 = bf16[128,128]{1,0:T(8,128)(2,1)S(1)} collective-permute-done((bf16[128,128]{1,0:T(8,128)(2,1)S(1)}, bf16[128,128]{1,0:T(8,128)(2,1)S(1)}, u32[]{:S(2)}, u32[]{:S(2)}) %collective-permute-start.12) | collective-permute-done | bytes 32800 | tf_op jit(solution)/shard_map/ppermute | solution.py:61
  54.1 0.7 collective-permute-done.14
  54.8 0.5 fusion.173
  55.7 3.7 %collective-permute-start.15 = (bf16[128,128]{1,0:T(8,128)(2,1)S(1)}, bf16[128,128]{1,0:T(8,128)(2,1)S(1)}, u32[]{:S(2)}, u32[]{:S(2)}) collective-permute-start(bf16[128,128]{1,0:T(8,128)(2,1)S(1)} %get-tuple-element.11), channel_id=1, source_target_pairs={{1,2},{2,1},{3,4},{4,3},{5,6},{6,5},{7,8},{8,7},{9,10},{10,9},{11,... | collective-permute-start | bytes 98312 | tf_op jit(solution)/shard_map/ppermute | solution.py:61
  59.7 0.8 fusion.158
  60.6 2.2 %collective-permute-done.15 = bf16[128,128]{1,0:T(8,128)(2,1)S(1)} collective-permute-done((bf16[128,128]{1,0:T(8,128)(2,1)S(1)}, bf16[128,128]{1,0:T(8,128)(2,1)S(1)}, u32[]{:S(2)}, u32[]{:S(2)}) %collective-permute-start.15) | collective-permute-done | bytes 32800 | tf_op jit(solution)/shard_map/ppermute | solution.py:61
  62.8 1.6 %collective-permute-done.17 = bf16[128,128]{1,0:T(8,128)(2,1)S(1)} collective-permute-done((bf16[128,128]{1,0:T(8,128)(2,1)S(1)}, bf16[128,128]{1,0:T(8,128)(2,1)S(1)}, u32[]{:S(2)}, u32[]{:S(2)}) %collective-permute-start.17) | collective-permute-done | bytes 32800 | tf_op jit(solution)/shard_map/ppermute | solution.py:61
  64.3 0.5 fusion.113
  65.3 2.7 %collective-permute-start.18 = (bf16[128,128]{1,0:T(8,128)(2,1)S(1)}, bf16[128,128]{1,0:T(8,128)(2,1)S(1)}, u32[]{:S(2)}, u32[]{:S(2)}) collective-permute-start(bf16[128,128]{1,0:T(8,128)(2,1)S(1)} %get-tuple-element.8), channel_id=1, source_target_pairs={{1,2},{2,1},{3,4},{4,3},{5,6},{6,5},{7,8},{8,7},{9,10},{10,9},{11,... | collective-permute-start | bytes 98312 | tf_op jit(solution)/shard_map/ppermute | solution.py:61
  68.0 0.6 collective-permute-start.20
  68.6 0.5 fusion.86
  69.0 3.4 %collective-permute-done.18 = bf16[128,128]{1,0:T(8,128)(2,1)S(1)} collective-permute-done((bf16[128,128]{1,0:T(8,128)(2,1)S(1)}, bf16[128,128]{1,0:T(8,128)(2,1)S(1)}, u32[]{:S(2)}, u32[]{:S(2)}) %collective-permute-start.18) | collective-permute-done | bytes 32800 | tf_op jit(solution)/shard_map/ppermute | solution.py:61
  72.8 0.5 fusion.176
  73.8 3.7 %collective-permute-start.21 = (bf16[128,128]{1,0:T(8,128)(2,1)S(1)}, bf16[128,128]{1,0:T(8,128)(2,1)S(1)}, u32[]{:S(2)}, u32[]{:S(2)}) collective-permute-start(bf16[128,128]{1,0:T(8,128)(2,1)S(1)} %get-tuple-element.5), channel_id=1, source_target_pairs={{1,2},{2,1},{3,4},{4,3},{5,6},{6,5},{7,8},{8,7},{9,10},{10,9},{11,... | collective-permute-start | bytes 98312 | tf_op jit(solution)/shard_map/ppermute | solution.py:61
  77.5 0.6 collective-permute-start.23
  78.1 0.8 fusion.164
  79.0 1.9 %collective-permute-done.21 = bf16[128,128]{1,0:T(8,128)(2,1)S(1)} collective-permute-done((bf16[128,128]{1,0:T(8,128)(2,1)S(1)}, bf16[128,128]{1,0:T(8,128)(2,1)S(1)}, u32[]{:S(2)}, u32[]{:S(2)}) %collective-permute-start.21) | collective-permute-done | bytes 32800 | tf_op jit(solution)/shard_map/ppermute | solution.py:61
  80.8 1.6 %collective-permute-done.23 = bf16[128,128]{1,0:T(8,128)(2,1)S(1)} collective-permute-done((bf16[128,128]{1,0:T(8,128)(2,1)S(1)}, bf16[128,128]{1,0:T(8,128)(2,1)S(1)}, u32[]{:S(2)}, u32[]{:S(2)}) %collective-permute-start.23) | collective-permute-done | bytes 32800 | tf_op jit(solution)/shard_map/ppermute | solution.py:61
  82.4 0.5 fusion.140
  83.0 1.0 %copy.27 = f32[1,1024,128]{2,1,0:T(8,128)} copy(f32[1,1024,128]{1,2,0:T(8,128)S(1)} %fusion.140) | data formatting | bytes 1048576 | tf_op jit(solution)/shard_map/broadcast_in_dim | solution.py:78
  (53 shorter events, 5.1 us)
Async XLA Ops:
  0.0 5.7 %copy-start = (bf16[1,1024,1024]{2,1,0:T(8,128)(2,1)S(1)}, bf16[1,1024,1024]{2,1,0:T(8,128)(2,1)}, u32[]{:S(2)}) copy-start(bf16[1,1024,1024]{2,1,0:T(8,128)(2,1)} %param.8) | copy-start | bytes 6291460
  7.1 11.6 %collective-permute-start = (bf16[128,128]{1,0:T(8,128)(2,1)S(1)}, bf16[128,128]{1,0:T(8,128)(2,1)S(1)}, u32[]{:S(2)}, u32[]{:S(2)}) collective-permute-start(bf16[128,128]{1,0:T(8,128)(2,1)S(1)} %get-tuple-element.26), channel_id=1, source_target_pairs={{1,2},{2,1},{3,4},{4,3},{5,6},{6,5},{7,8},{8,7},{9,10},{10,9},{11,... | collective-permute-start | bytes 98312 | tf_op jit(solution)/shard_map/ppermute | solution.py:61
  10.8 7.9 %collective-permute-start.2 = (bf16[128,128]{1,0:T(8,128)(2,1)S(1)}, bf16[128,128]{1,0:T(8,128)(2,1)S(1)}, u32[]{:S(2)}, u32[]{:S(2)}) collective-permute-start(bf16[128,128]{1,0:T(8,128)(2,1)S(1)} %get-tuple-element.27), channel_id=1, source_target_pairs={{0,16},{1,17},{2,18},{3,19},{4,20},{5,21},{6,22},{7,23},{8,24},{9,... | collective-permute-start | bytes 98312 | tf_op jit(solution)/shard_map/ppermute | solution.py:61
  13.4 5.3 %collective-permute-start.1 = (bf16[128,128]{1,0:T(8,128)(2,1)S(1)}, bf16[128,128]{1,0:T(8,128)(2,1)S(1)}, u32[]{:S(2)}, u32[]{:S(2)}) collective-permute-start(bf16[128,128]{1,0:T(8,128)(2,1)S(1)} %get-tuple-element.28), channel_id=1, source_target_pairs={{0,1},{1,0},{2,3},{3,2},{4,5},{5,4},{6,7},{7,6},{8,9},{9,8},{10,11... | collective-permute-start | bytes 98312 | tf_op jit(solution)/shard_map/ppermute | solution.py:61
  15.2 2.6 %copy-start.2 = (f32[1,1024]{1,0:T(1,128)S(1)}, f32[1,1024]{1,0:T(1,128)}, u32[]{:S(2)}) copy-start(f32[1,1024]{1,0:T(1,128)} %param.10) | copy-start | bytes 12292
  18.3 5.2 %copy-start.1 = (bf16[1,1024,1024]{2,1,0:T(8,128)(2,1)S(1)}, bf16[1,1024,1024]{2,1,0:T(8,128)(2,1)}, u32[]{:S(2)}) copy-start(bf16[1,1024,1024]{2,1,0:T(8,128)(2,1)} %param.9) | copy-start | bytes 6291460
  19.6 7.0 %collective-permute-start.3 = (bf16[128,128]{1,0:T(8,128)(2,1)S(1)}, bf16[128,128]{1,0:T(8,128)(2,1)S(1)}, u32[]{:S(2)}, u32[]{:S(2)}) collective-permute-start(bf16[128,128]{1,0:T(8,128)(2,1)S(1)} %get-tuple-element.23), channel_id=1, source_target_pairs={{1,2},{2,1},{3,4},{4,3},{5,6},{6,5},{7,8},{8,7},{9,10},{10,9},{11,... | collective-permute-start | bytes 98312 | tf_op jit(solution)/shard_map/ppermute | solution.py:61
  23.0 4.9 %collective-permute-start.5 = (bf16[128,128]{1,0:T(8,128)(2,1)S(1)}, bf16[128,128]{1,0:T(8,128)(2,1)S(1)}, u32[]{:S(2)}, u32[]{:S(2)}) collective-permute-start(bf16[128,128]{1,0:T(8,128)(2,1)S(1)} %get-tuple-element.24), channel_id=1, source_target_pairs={{0,16},{1,17},{2,18},{3,19},{4,20},{5,21},{6,22},{7,23},{8,24},{9,... | collective-permute-start | bytes 98312 | tf_op jit(solution)/shard_map/ppermute | solution.py:61
  23.5 4.4 %collective-permute-start.4 = (bf16[128,128]{1,0:T(8,128)(2,1)S(1)}, bf16[128,128]{1,0:T(8,128)(2,1)S(1)}, u32[]{:S(2)}, u32[]{:S(2)}) collective-permute-start(bf16[128,128]{1,0:T(8,128)(2,1)S(1)} %get-tuple-element.25), channel_id=1, source_target_pairs={{0,1},{1,0},{2,3},{3,2},{4,5},{5,4},{6,7},{7,6},{8,9},{9,8},{10,11... | collective-permute-start | bytes 98312 | tf_op jit(solution)/shard_map/ppermute | solution.py:61
  28.9 7.0 %collective-permute-start.6 = (bf16[128,128]{1,0:T(8,128)(2,1)S(1)}, bf16[128,128]{1,0:T(8,128)(2,1)S(1)}, u32[]{:S(2)}, u32[]{:S(2)}) collective-permute-start(bf16[128,128]{1,0:T(8,128)(2,1)S(1)} %get-tuple-element.20), channel_id=1, source_target_pairs={{1,2},{2,1},{3,4},{4,3},{5,6},{6,5},{7,8},{8,7},{9,10},{10,9},{11,... | collective-permute-start | bytes 98312 | tf_op jit(solution)/shard_map/ppermute | solution.py:61
  32.0 4.9 %collective-permute-start.8 = (bf16[128,128]{1,0:T(8,128)(2,1)S(1)}, bf16[128,128]{1,0:T(8,128)(2,1)S(1)}, u32[]{:S(2)}, u32[]{:S(2)}) collective-permute-start(bf16[128,128]{1,0:T(8,128)(2,1)S(1)} %get-tuple-element.21), channel_id=1, source_target_pairs={{0,16},{1,17},{2,18},{3,19},{4,20},{5,21},{6,22},{7,23},{8,24},{9,... | collective-permute-start | bytes 98312 | tf_op jit(solution)/shard_map/ppermute | solution.py:61
  32.3 4.6 %collective-permute-start.7 = (bf16[128,128]{1,0:T(8,128)(2,1)S(1)}, bf16[128,128]{1,0:T(8,128)(2,1)S(1)}, u32[]{:S(2)}, u32[]{:S(2)}) collective-permute-start(bf16[128,128]{1,0:T(8,128)(2,1)S(1)} %get-tuple-element.22), channel_id=1, source_target_pairs={{0,1},{1,0},{2,3},{3,2},{4,5},{5,4},{6,7},{7,6},{8,9},{9,8},{10,11... | collective-permute-start | bytes 98312 | tf_op jit(solution)/shard_map/ppermute | solution.py:61
  37.9 7.0 %collective-permute-start.9 = (bf16[128,128]{1,0:T(8,128)(2,1)S(1)}, bf16[128,128]{1,0:T(8,128)(2,1)S(1)}, u32[]{:S(2)}, u32[]{:S(2)}) collective-permute-start(bf16[128,128]{1,0:T(8,128)(2,1)S(1)} %get-tuple-element.17), channel_id=1, source_target_pairs={{1,2},{2,1},{3,4},{4,3},{5,6},{6,5},{7,8},{8,7},{9,10},{10,9},{11,... | collective-permute-start | bytes 98312 | tf_op jit(solution)/shard_map/ppermute | solution.py:61
  41.3 4.9 %collective-permute-start.11 = (bf16[128,128]{1,0:T(8,128)(2,1)S(1)}, bf16[128,128]{1,0:T(8,128)(2,1)S(1)}, u32[]{:S(2)}, u32[]{:S(2)}) collective-permute-start(bf16[128,128]{1,0:T(8,128)(2,1)S(1)} %get-tuple-element.18), channel_id=1, source_target_pairs={{0,16},{1,17},{2,18},{3,19},{4,20},{5,21},{6,22},{7,23},{8,24},{9,... | collective-permute-start | bytes 98312 | tf_op jit(solution)/shard_map/ppermute | solution.py:61
  41.5 4.6 %collective-permute-start.10 = (bf16[128,128]{1,0:T(8,128)(2,1)S(1)}, bf16[128,128]{1,0:T(8,128)(2,1)S(1)}, u32[]{:S(2)}, u32[]{:S(2)}) collective-permute-start(bf16[128,128]{1,0:T(8,128)(2,1)S(1)} %get-tuple-element.19), channel_id=1, source_target_pairs={{0,1},{1,0},{2,3},{3,2},{4,5},{5,4},{6,7},{7,6},{8,9},{9,8},{10,11... | collective-permute-start | bytes 98312 | tf_op jit(solution)/shard_map/ppermute | solution.py:61
  47.1 7.0 %collective-permute-start.12 = (bf16[128,128]{1,0:T(8,128)(2,1)S(1)}, bf16[128,128]{1,0:T(8,128)(2,1)S(1)}, u32[]{:S(2)}, u32[]{:S(2)}) collective-permute-start(bf16[128,128]{1,0:T(8,128)(2,1)S(1)} %get-tuple-element.14), channel_id=1, source_target_pairs={{1,2},{2,1},{3,4},{4,3},{5,6},{6,5},{7,8},{8,7},{9,10},{10,9},{11,... | collective-permute-start | bytes 98312 | tf_op jit(solution)/shard_map/ppermute | solution.py:61
  49.9 4.9 %collective-permute-start.14 = (bf16[128,128]{1,0:T(8,128)(2,1)S(1)}, bf16[128,128]{1,0:T(8,128)(2,1)S(1)}, u32[]{:S(2)}, u32[]{:S(2)}) collective-permute-start(bf16[128,128]{1,0:T(8,128)(2,1)S(1)} %get-tuple-element.15), channel_id=1, source_target_pairs={{0,16},{1,17},{2,18},{3,19},{4,20},{5,21},{6,22},{7,23},{8,24},{9,... | collective-permute-start | bytes 98312 | tf_op jit(solution)/shard_map/ppermute | solution.py:61
  50.5 4.3 %collective-permute-start.13 = (bf16[128,128]{1,0:T(8,128)(2,1)S(1)}, bf16[128,128]{1,0:T(8,128)(2,1)S(1)}, u32[]{:S(2)}, u32[]{:S(2)}) collective-permute-start(bf16[128,128]{1,0:T(8,128)(2,1)S(1)} %get-tuple-element.16), channel_id=1, source_target_pairs={{0,1},{1,0},{2,3},{3,2},{4,5},{5,4},{6,7},{7,6},{8,9},{9,8},{10,11... | collective-permute-start | bytes 98312 | tf_op jit(solution)/shard_map/ppermute | solution.py:61
  55.7 7.0 %collective-permute-start.15 = (bf16[128,128]{1,0:T(8,128)(2,1)S(1)}, bf16[128,128]{1,0:T(8,128)(2,1)S(1)}, u32[]{:S(2)}, u32[]{:S(2)}) collective-permute-start(bf16[128,128]{1,0:T(8,128)(2,1)S(1)} %get-tuple-element.11), channel_id=1, source_target_pairs={{1,2},{2,1},{3,4},{4,3},{5,6},{6,5},{7,8},{8,7},{9,10},{10,9},{11,... | collective-permute-start | bytes 98312 | tf_op jit(solution)/shard_map/ppermute | solution.py:61
  59.4 4.9 %collective-permute-start.17 = (bf16[128,128]{1,0:T(8,128)(2,1)S(1)}, bf16[128,128]{1,0:T(8,128)(2,1)S(1)}, u32[]{:S(2)}, u32[]{:S(2)}) collective-permute-start(bf16[128,128]{1,0:T(8,128)(2,1)S(1)} %get-tuple-element.12), channel_id=1, source_target_pairs={{0,16},{1,17},{2,18},{3,19},{4,20},{5,21},{6,22},{7,23},{8,24},{9,... | collective-permute-start | bytes 98312 | tf_op jit(solution)/shard_map/ppermute | solution.py:61
  59.7 4.6 %collective-permute-start.16 = (bf16[128,128]{1,0:T(8,128)(2,1)S(1)}, bf16[128,128]{1,0:T(8,128)(2,1)S(1)}, u32[]{:S(2)}, u32[]{:S(2)}) collective-permute-start(bf16[128,128]{1,0:T(8,128)(2,1)S(1)} %get-tuple-element.13), channel_id=1, source_target_pairs={{0,1},{1,0},{2,3},{3,2},{4,5},{5,4},{6,7},{7,6},{8,9},{9,8},{10,11... | collective-permute-start | bytes 98312 | tf_op jit(solution)/shard_map/ppermute | solution.py:61
  65.3 7.2 %collective-permute-start.18 = (bf16[128,128]{1,0:T(8,128)(2,1)S(1)}, bf16[128,128]{1,0:T(8,128)(2,1)S(1)}, u32[]{:S(2)}, u32[]{:S(2)}) collective-permute-start(bf16[128,128]{1,0:T(8,128)(2,1)S(1)} %get-tuple-element.8), channel_id=1, source_target_pairs={{1,2},{2,1},{3,4},{4,3},{5,6},{6,5},{7,8},{8,7},{9,10},{10,9},{11,... | collective-permute-start | bytes 98312 | tf_op jit(solution)/shard_map/ppermute | solution.py:61
  68.0 4.9 %collective-permute-start.20 = (bf16[128,128]{1,0:T(8,128)(2,1)S(1)}, bf16[128,128]{1,0:T(8,128)(2,1)S(1)}, u32[]{:S(2)}, u32[]{:S(2)}) collective-permute-start(bf16[128,128]{1,0:T(8,128)(2,1)S(1)} %get-tuple-element.9), channel_id=1, source_target_pairs={{0,16},{1,17},{2,18},{3,19},{4,20},{5,21},{6,22},{7,23},{8,24},{9,... | collective-permute-start | bytes 98312 | tf_op jit(solution)/shard_map/ppermute | solution.py:61
  68.6 4.3 %collective-permute-start.19 = (bf16[128,128]{1,0:T(8,128)(2,1)S(1)}, bf16[128,128]{1,0:T(8,128)(2,1)S(1)}, u32[]{:S(2)}, u32[]{:S(2)}) collective-permute-start(bf16[128,128]{1,0:T(8,128)(2,1)S(1)} %get-tuple-element.10), channel_id=1, source_target_pairs={{0,1},{1,0},{2,3},{3,2},{4,5},{5,4},{6,7},{7,6},{8,9},{9,8},{10,11... | collective-permute-start | bytes 98312 | tf_op jit(solution)/shard_map/ppermute | solution.py:61
  73.8 7.0 %collective-permute-start.21 = (bf16[128,128]{1,0:T(8,128)(2,1)S(1)}, bf16[128,128]{1,0:T(8,128)(2,1)S(1)}, u32[]{:S(2)}, u32[]{:S(2)}) collective-permute-start(bf16[128,128]{1,0:T(8,128)(2,1)S(1)} %get-tuple-element.5), channel_id=1, source_target_pairs={{1,2},{2,1},{3,4},{4,3},{5,6},{6,5},{7,8},{8,7},{9,10},{10,9},{11,... | collective-permute-start | bytes 98312 | tf_op jit(solution)/shard_map/ppermute | solution.py:61
  77.5 4.9 %collective-permute-start.23 = (bf16[128,128]{1,0:T(8,128)(2,1)S(1)}, bf16[128,128]{1,0:T(8,128)(2,1)S(1)}, u32[]{:S(2)}, u32[]{:S(2)}) collective-permute-start(bf16[128,128]{1,0:T(8,128)(2,1)S(1)} %get-tuple-element.6), channel_id=1, source_target_pairs={{0,16},{1,17},{2,18},{3,19},{4,20},{5,21},{6,22},{7,23},{8,24},{9,... | collective-permute-start | bytes 98312 | tf_op jit(solution)/shard_map/ppermute | solution.py:61
  78.1 4.3 %collective-permute-start.22 = (bf16[128,128]{1,0:T(8,128)(2,1)S(1)}, bf16[128,128]{1,0:T(8,128)(2,1)S(1)}, u32[]{:S(2)}, u32[]{:S(2)}) collective-permute-start(bf16[128,128]{1,0:T(8,128)(2,1)S(1)} %get-tuple-element.7), channel_id=1, source_target_pairs={{0,1},{1,0},{2,3},{3,2},{4,5},{5,4},{6,7},{7,6},{8,9},{9,8},{10,11... | collective-permute-start | bytes 98312 | tf_op jit(solution)/shard_map/ppermute | solution.py:61

commit v6 on v4

--- a/solution.py
+++ b/solution.py
@@ -50,33 +50,46 @@
     hot = (jnp.arange(width)[:, None] == rows[None, :]) & live[None, :]
     placer = hot.astype(jnp.bfloat16)
     picked_weight = jnp.sum(jnp.where(hot, weight, 0.0), 0)[:, None]
-    picked_rhs = lax.dot_general(placer, rhs16, (((0,), (0,)), ((), ())), preferred_element_type=jnp.float32)
-    picked_s = jnp.dot(s_mat, placer, preferred_element_type=jnp.float32).astype(jnp.bfloat16)
-    picked_n = lax.dot_general(
-        placer, n_mat, (((0,), (0,)), ((), ())), preferred_element_type=jnp.float32
-    ).astype(jnp.bfloat16)
-    mask_weight = mask * weight
+
+    def transposed(mat, block):
+        return lax.dot_general(mat, block, (((0,), (0,)), ((), ())), preferred_element_type=jnp.float32)
+
+    def times(mat, block):
+        return jnp.dot(mat, block, preferred_element_type=jnp.float32)
 
     def exchange(packed):
         parts = [
             lax.ppermute(packed[k * share : (k + 1) * share], "sub", route) for k, route in enumerate(routes)
         ]
-        return jnp.dot(placer, jnp.concatenate(parts, 0), preferred_element_type=jnp.float32)
+        return jnp.concatenate(parts, 0)
 
-    def transposed(mat, block):
-        return lax.dot_general(mat, block, (((0,), (0,)), ((), ())), preferred_element_type=jnp.float32)
+    picked_rhs = transposed(placer, rhs16)
+    arrived = exchange(picked_rhs.astype(jnp.bfloat16))
 
+    picked_n = transposed(placer, n_mat).astype(jnp.bfloat16)
+    picked_s = times(s_mat, placer).astype(jnp.bfloat16)
+    small_n = times(picked_n, placer).astype(jnp.bfloat16)
+    small_s = transposed(picked_s, placer).astype(jnp.bfloat16)
+    mask_weight = mask * weight
+
+    local = mask * rhs
     solution = jnp.zeros(rhs.shape, jnp.float32)
     for step in range(ITERS):
-        current = solution.astype(jnp.bfloat16)
-        arrived = exchange((picked_rhs - transposed(picked_s, current)).astype(jnp.bfloat16))
-        local = mask * (rhs - transposed(s_mat, current))
-        scaled = (weight * (local + arrived)).astype(jnp.bfloat16)
-        sent = picked_weight * jnp.dot(picked_n, scaled, preferred_element_type=jnp.float32)
+        if step:
+            sent = sent_base - DAMPING * times(small_s, arrived)
+            came = arrived
+            arrived = exchange(sent.astype(jnp.bfloat16))
+            solution = solution + DAMPING * times(placer, came)
+            local = mask * (rhs - transposed(s_mat, solution.astype(jnp.bfloat16)))
+        sent_base = picked_weight * times(picked_n, (weight * local).astype(jnp.bfloat16))
+        sent = sent_base + picked_weight * times(small_n, (picked_weight * arrived).astype(jnp.bfloat16))
+        came = arrived
         arrived = exchange(sent.astype(jnp.bfloat16))
-        weighted = mask_weight * jnp.dot(n_mat, scaled, preferred_element_type=jnp.float32)
-        solution = solution + DAMPING * (weighted + arrived)
-    return solution[None]
+        scaled = (weight * (local + times(placer, came))).astype(jnp.bfloat16)
+        solution = solution + DAMPING * (mask_weight * times(n_mat, scaled))
+        if step < ITERS - 1:
+            sent_base = picked_rhs - transposed(picked_s, solution.astype(jnp.bfloat16))
+    return (solution + DAMPING * times(placer, arrived))[None]
 
 
 def solution(mesh):

time: 76.8 us -> 99.1 us (1.29)
  matrix products: 17.5 us -> 37.5 us
  local copies, waits for them, and re-layouts: 4.48 us -> 6.96 us
  waiting for transfers between devices: 28 us -> 26.7 us
    dot_general x19 -> x21, matrix products: 14.1 us -> 26.5 us  [times(): return jnp.dot(mat, block, preferred_element_type=jnp.float32)]
    dot_general x8 -> x9, matrix products: 3.33 us -> 10.9 us  [transposed(): lax.dot_general(mat, block, (((0,), (0,)), ((), ())), preferred_element_t...]
    ppermute x24, waiting for transfers between devices: 28 us -> 26.7 us  [exchange(): lax.ppermute(packed[k * share:(k + 1) * share], 'sub', route)]
    unnamed x7 -> x59, local copies, waits for them, and re-layouts: 1.1 us -> 2.3 us
  transfers between devices with their start and end apart: 24 -> 24, of which waited for: 7 -> 11; matrix products, arithmetic and copies ran while one was open for 12% -> 18% of each run, Pallas kernels for 0% -> 0%
where the time goes in v6:
time: 99.1 us; the launch traced here: 98.5 us
  matrix products  37.5 us (38%)
  waiting for transfers between devices  26.7 us (27%)
  starting transfers between devices  23.8 us (24%)
  local copies, waits for them, and re-layouts  6.96 us (7%)
  between operations  3.17 us (3%)
    ppermute x24, waiting for transfers between devices, exchange(): lax.ppermute(packed[k * share:(k + 1) * share], 'sub', route)  26.7 us
    dot_general x21, matrix products, times(): return jnp.dot(mat, block, preferred_element_type=jnp.float32)  26.5 us
    ppermute x24, starting transfers between devices, exchange(): lax.ppermute(packed[k * share:(k + 1) * share], 'sub', route)  23.8 us
    dot_general x9, matrix products, transposed(): lax.dot_general(mat, block, (((0,), (0,)), ((), ())), preferred_element_t...  10.9 us
    unnamed x59, local copies, waits for them, and re-layouts  2.3 us
  transfers between devices with their start and end apart: 24, of which 11 were waited for; matrix products, arithmetic and copies ran while one was open for 18% of the time, Pallas kernels for 0%

profile of v6, /device:TPU:0, one launch (start us, length us, event | category | flops | bytes accessed | tf_op | source)
XLA Modules:
  0.0 98.5 jit_solution(3373099364838281714)
XLA Ops:
  0.0 1.5 %constant_dynamic-slice_fusion.2 = (s32[1,1]{1,0:T(1,128)}, s32[1,1]{1,0:T(1,128)}, s32[1,1]{1,0:T(1,128)}) fusion(s32[1,4]{1,0:T(1,128)} %param.11, s32[]{:T(128)S(6)} %select_n.34, s32[]{:T(128)S(6)} %select_n.38, s32[]{:T(128)S(6)} %select_n.35), kind=kLoop, calls=%fused_computation.202 | loop fusion | bytes 36 | tf_op jit(solution)/shard_map/jit(dynamic_index_in_dim)/dynamic_slice | solution.py:47
  3.4 0.8 fusion.290
  4.3 2.1 %fusion.302 = (bf16[384,128]{1,0:T(8,128)(2,1)S(1)}, f32[384,128]{1,0:T(8,128)}) fusion(bf16[1,1024,128]{2,1,0:T(8,128)(2,1)} %param.7, s32[384]{0:T(512)S(1)} %pad_add_fusion, pred[384]{0:T(512)(128)(4,1)S(1)} %pad_add_fusion.1), kind=kOutput, calls=%fused_computation.218 | convolution fusion | flops 101892096 | bytes 558976 | tf_op jit(solution)/shard_map/dot_general | solution.py:55
  6.4 0.6 fusion.301
  7.0 6.4 %collective-permute-start = (bf16[128,128]{1,0:T(8,128)(2,1)}, bf16[128,128]{1,0:T(8,128)(2,1)}, u32[]{:S(2)}, u32[]{:S(2)}) collective-permute-start(bf16[128,128]{1,0:T(8,128)(2,1)} %get-tuple-element.28), channel_id=1, source_target_pairs={{0,31},{1,2},{2,1},{3,4},{4,3},{5,6},{6,5},{7,8},{8,7},{9,10},{10,... | collective-permute-start | bytes 98312 | tf_op jit(solution)/shard_map/ppermute | solution.py:62
  14.2 2.6 %fusion.46 = bf16[384,1024]{1,0:T(8,128)(2,1)S(1)} fusion(bf16[1,1024,1024]{2,1,0:T(8,128)(2,1)} %param.8, s32[384]{0:T(512)S(1)} %pad_add_fusion, pred[384]{0:T(512)(128)(4,1)S(1)} %pad_add_fusion.1), kind=kOutput, calls=%fused_computation.33 | convolution fusion | flops 806879232 | bytes 2885504 | tf_op jit(solution)/shard_map/dot_general | solution.py:58
  16.9 1.0 %fusion.41 = bf16[384,1024]{1,0:T(8,128)(2,1)S(1)} fusion(bf16[1,1024,1024]{2,1,0:T(8,128)(2,1)S(1)} %copy-done, s32[384]{0:T(512)S(1)} %pad_add_fusion, pred[384]{0:T(512)(128)(4,1)S(1)} %pad_add_fusion.1), kind=kOutput, calls=%fused_computation.32 | convolution fusion | flops 806486016 | bytes 2885504 | tf_op jit(solution)/shard_map/dot_general | solution.py:55
  17.9 0.6 fusion.166
  18.6 1.4 %fusion.169 = bf16[384,384]{1,0:T(8,128)(2,1)} fusion(bf16[384,1024]{1,0:T(8,128)(2,1)S(1)} %fusion.46, s32[384]{0:T(512)S(1)} %pad_add_fusion, pred[384]{0:T(512)(128)(4,1)S(1)} %pad_add_fusion.1), kind=kOutput, calls=%fused_computation.74 | convolution fusion | flops 302923776 | bytes 1083264 | tf_op jit(solution)/shard_map/dot_general | solution.py:55
  19.9 1.1 %fusion.258 = f32[384,128]{1,0:T(8,128)} fusion(bf16[384,1024]{1,0:T(8,128)(2,1)S(1)} %fusion.41, bf16[1,1024,128]{1,2,0:T(8,128)(2,1)S(1)} %copy.14, f32[1024]{0:T(1024)S(1)} %fusion.288, f32[1024]{0:T(1024)S(1)} %bitcast.171), kind=kOutput, calls=%fused_computation.141 | convolution fusion | flops 101187584 | bytes 1253376 | tf_op jit(solution)/shard_map/dot_general | solution.py:58
  21.4 1.4 %constant_dynamic-update-slice_fusion.2 = bf16[384,128]{1,0:T(8,128)(2,1)} fusion(bf16[128,128]{1,0:T(8,128)(2,1)} %collective-permute-done), kind=kLoop, calls=%fused_computation.176 | loop fusion | bytes 65536
  22.7 0.6 constant_dynamic-update-slice_fusion.1
  23.4 0.6 constant_dynamic-update-slice_fusion
  24.0 2.9 %fusion.127 = f32[1024,128]{0,1:T(8,128)} fusion(bf16[1,1024,1024]{2,1,0:T(8,128)(2,1)S(1)} %copy-done, bf16[384,128]{1,0:T(8,128)(2,1)} %constant_dynamic-update-slice_fusion, s32[384]{0:T(512)S(1)} %pad_add_fusion, pred[384]{0:T(512)(128)(4,1)S(1)} %pad_add_fusion.1, bf16[1,1024,128]{1,2,0:T(8,128)(2,1)S(1)} %copy.14, f32[1024]{0:T(1024)S(1)} %fusion.288, ...), kind=kOutput, calls=%fused_computation.60 | convolution fusion | flops 370802688 | bytes 2996096 | tf_op jit(solution)/shard_map/dot_general | solution.py:58
  26.9 1.4 %fusion.209 = bf16[384,128]{1,0:T(8,128)(2,1)S(1)} fusion(f32[384,128]{1,0:T(8,128)} %fusion.258, bf16[384,384]{1,0:T(8,128)(2,1)S(1)} %fusion.166, bf16[384,128]{1,0:T(8,128)(2,1)} %constant_dynamic-update-slice_fusion, f32[384]{0:T(512)S(1)} %select_reduce_fusion), kind=kOutput, calls=%fused_computation.98 | convolution fusion | flops 38043648 | bytes 689664 | tf_op jit(solution)/shard_map/dot_general | solution.py:58
  28.3 1.9 %collective-permute-start.3 = (bf16[128,128]{1,0:T(8,128)(2,1)S(1)}, bf16[128,128]{1,0:T(8,128)(2,1)S(1)}, u32[]{:S(2)}, u32[]{:S(2)}) collective-permute-start(bf16[128,128]{1,0:T(8,128)(2,1)S(1)} %get-tuple-element.25), channel_id=1, source_target_pairs={{0,31},{1,2},{2,1},{3,4},{4,3},{5,6},{6,5},{7,8},{8,7},{9,10},{10,... | collective-permute-start | bytes 98312 | tf_op jit(solution)/shard_map/ppermute | solution.py:62
  30.2 1.4 %collective-permute-start.5 = (bf16[128,128]{1,0:T(8,128)(2,1)S(1)}, bf16[128,128]{1,0:T(8,128)(2,1)S(1)}, u32[]{:S(2)}, u32[]{:S(2)}) collective-permute-start(bf16[128,128]{1,0:T(8,128)(2,1)S(1)} %get-tuple-element.23), channel_id=1, source_target_pairs={{0,16},{1,17},{2,18},{3,19},{4,20},{5,21},{6,22},{7,23},{8,24},{9,... | collective-permute-start | bytes 98312 | tf_op jit(solution)/shard_map/ppermute | solution.py:62
  31.6 1.7 %convolution_subtract_fusion.2 = f32[384,128]{1,0:T(8,128)S(1)} fusion(f32[384,128]{1,0:T(8,128)} %get-tuple-element.36, bf16[384,1024]{1,0:T(8,128)(2,1)} %copy-done.4, f32[1024,128]{0,1:T(8,128)} %fusion.127), kind=kOutput, calls=%fused_computation.97 | convolution fusion | flops 100843520 | bytes 1703936 | tf_op jit(solution)/shard_map/dot_general | solution.py:55
  33.3 2.0 %collective-permute-done.3 = bf16[128,128]{1,0:T(8,128)(2,1)S(1)} collective-permute-done((bf16[128,128]{1,0:T(8,128)(2,1)S(1)}, bf16[128,128]{1,0:T(8,128)(2,1)S(1)}, u32[]{:S(2)}, u32[]{:S(2)}) %collective-permute-start.3) | collective-permute-done | bytes 32800 | tf_op jit(solution)/shard_map/ppermute | solution.py:62
  35.6 0.5 fusion.115
  36.4 1.9 %collective-permute-start.6 = (bf16[128,128]{1,0:T(8,128)(2,1)S(1)}, bf16[128,128]{1,0:T(8,128)(2,1)S(1)}, u32[]{:S(2)}, u32[]{:S(2)}) collective-permute-start(bf16[128,128]{1,0:T(8,128)(2,1)S(1)} %get-tuple-element.22), channel_id=1, source_target_pairs={{0,31},{1,2},{2,1},{3,4},{4,3},{5,6},{6,5},{7,8},{8,7},{9,10},{10,... | collective-permute-start | bytes 98312 | tf_op jit(solution)/shard_map/ppermute | solution.py:62
  38.3 1.0 %collective-permute-start.8 = (bf16[128,128]{1,0:T(8,128)(2,1)S(1)}, bf16[128,128]{1,0:T(8,128)(2,1)S(1)}, u32[]{:S(2)}, u32[]{:S(2)}) collective-permute-start(bf16[128,128]{1,0:T(8,128)(2,1)S(1)} %get-tuple-element.20), channel_id=1, source_target_pairs={{0,16},{1,17},{2,18},{3,19},{4,20},{5,21},{6,22},{7,23},{8,24},{9,... | collective-permute-start | bytes 98312 | tf_op jit(solution)/shard_map/ppermute | solution.py:62
  39.8 1.1 %fusion.255 = f32[384,128]{1,0:T(8,128)} fusion(bf16[384,1024]{1,0:T(8,128)(2,1)S(1)} %fusion.41, f32[1024,128]{0,1:T(8,128)S(1)} %fusion.97, f32[1024]{0:T(1024)S(1)} %bitcast.174), kind=kOutput, calls=%fused_computation.138 | convolution fusion | flops 100925440 | bytes 1511424 | tf_op jit(solution)/shard_map/dot_general | solution.py:58
  40.9 2.6 %collective-permute-done.6 = bf16[128,128]{1,0:T(8,128)(2,1)S(1)} collective-permute-done((bf16[128,128]{1,0:T(8,128)(2,1)S(1)}, bf16[128,128]{1,0:T(8,128)(2,1)S(1)}, u32[]{:S(2)}, u32[]{:S(2)}) %collective-permute-start.6) | collective-permute-done | bytes 32800 | tf_op jit(solution)/shard_map/ppermute | solution.py:62
  43.6 3.1 %fusion.139 = f32[1024,128]{0,1:T(8,128)} fusion(f32[1024,128]{0,1:T(8,128)} %copy-done.16, bf16[1,1024,1024]{2,1,0:T(8,128)(2,1)S(1)} %copy-done, f32[1024,128]{0,1:T(8,128)S(1)} %fusion.97, bf16[384,128]{1,0:T(8,128)(2,1)S(1)} %constant_dynamic-update-slice_fusion.6, s32[384]{0:T(512)S(1)} %pad_add_fusion, pred[384]{0:T(512)(128)(4,1)S(1)} %pad_add_fusion.1, ...), kind=kOutput, calls=%fused_computation.64 | convolution fusion | flops 370671616 | bytes 3778432 | tf_op jit(solution)/shard_map/dot_general | solution.py:58
  46.6 1.4 %fusion.211 = bf16[384,128]{1,0:T(8,128)(2,1)S(1)} fusion(f32[384,128]{1,0:T(8,128)} %fusion.255, bf16[384,384]{1,0:T(8,128)(2,1)} %copy-done.5, bf16[384,128]{1,0:T(8,128)(2,1)S(1)} %constant_dynamic-update-slice_fusion.6, f32[384]{0:T(512)S(1)} %select_reduce_fusion), kind=kOutput, calls=%fused_computation.100 | convolution fusion | flops 38043648 | bytes 689664 | tf_op jit(solution)/shard_map/dot_general | solution.py:58
  48.0 2.0 %collective-permute-start.9 = (bf16[128,128]{1,0:T(8,128)(2,1)S(1)}, bf16[128,128]{1,0:T(8,128)(2,1)S(1)}, u32[]{:S(2)}, u32[]{:S(2)}) collective-permute-start(bf16[128,128]{1,0:T(8,128)(2,1)S(1)} %get-tuple-element.19), channel_id=1, source_target_pairs={{0,31},{1,2},{2,1},{3,4},{4,3},{5,6},{6,5},{7,8},{8,7},{9,10},{10,... | collective-permute-start | bytes 98312 | tf_op jit(solution)/shard_map/ppermute | solution.py:62
  50.1 1.7 %convolution_subtract_fusion.1 = f32[384,128]{1,0:T(8,128)S(1)} fusion(f32[384,128]{1,0:T(8,128)} %get-tuple-element.36, bf16[384,1024]{1,0:T(8,128)(2,1)} %copy-done.4, f32[1024,128]{0,1:T(8,128)} %fusion.139), kind=kOutput, calls=%fused_computation.96 | convolution fusion | flops 100843520 | bytes 1703936 | tf_op jit(solution)/shard_map/dot_general | solution.py:55
  51.9 3.2 %collective-permute-done.9 = bf16[128,128]{1,0:T(8,128)(2,1)S(1)} collective-permute-done((bf16[128,128]{1,0:T(8,128)(2,1)S(1)}, bf16[128,128]{1,0:T(8,128)(2,1)S(1)}, u32[]{:S(2)}, u32[]{:S(2)}) %collective-permute-start.9) | collective-permute-done | bytes 32800 | tf_op jit(solution)/shard_map/ppermute | solution.py:62
  55.1 1.6 %collective-permute-done.11 = bf16[128,128]{1,0:T(8,128)(2,1)S(1)} collective-permute-done((bf16[128,128]{1,0:T(8,128)(2,1)S(1)}, bf16[128,128]{1,0:T(8,128)(2,1)S(1)}, u32[]{:S(2)}, u32[]{:S(2)}) %collective-permute-start.11) | collective-permute-done | bytes 32800 | tf_op jit(solution)/shard_map/ppermute | solution.py:62
  56.7 0.5 fusion.109
  57.6 2.3 %collective-permute-start.12 = (bf16[128,128]{1,0:T(8,128)(2,1)S(1)}, bf16[128,128]{1,0:T(8,128)(2,1)S(1)}, u32[]{:S(2)}, u32[]{:S(2)}) collective-permute-start(bf16[128,128]{1,0:T(8,128)(2,1)S(1)} %get-tuple-element.16), channel_id=1, source_target_pairs={{0,31},{1,2},{2,1},{3,4},{4,3},{5,6},{6,5},{7,8},{8,7},{9,10},{10,... | collective-permute-start | bytes 98312 | tf_op jit(solution)/shard_map/ppermute | solution.py:62
  60.4 1.1 %fusion.256 = f32[384,128]{1,0:T(8,128)} fusion(bf16[384,1024]{1,0:T(8,128)(2,1)S(1)} %fusion.41, f32[1024,128]{0,1:T(8,128)S(1)} %fusion.91, f32[1024]{0:T(1024)S(1)} %bitcast.176), kind=kOutput, calls=%fused_computation.139 | convolution fusion | flops 100925440 | bytes 1511424 | tf_op jit(solution)/shard_map/dot_general | solution.py:58
  61.4 3.1 %collective-permute-done.12 = bf16[128,128]{1,0:T(8,128)(2,1)S(1)} collective-permute-done((bf16[128,128]{1,0:T(8,128)(2,1)S(1)}, bf16[128,128]{1,0:T(8,128)(2,1)S(1)}, u32[]{:S(2)}, u32[]{:S(2)}) %collective-permute-start.12) | collective-permute-done | bytes 32800 | tf_op jit(solution)/shard_map/ppermute | solution.py:62
  64.7 3.2 %fusion.151 = f32[1024,128]{0,1:T(8,128)} fusion(f32[1024,128]{0,1:T(8,128)} %copy-done.17, bf16[1,1024,1024]{2,1,0:T(8,128)(2,1)S(1)} %copy-done, f32[1024,128]{0,1:T(8,128)S(1)} %fusion.91, bf16[384,128]{1,0:T(8,128)(2,1)S(1)} %constant_dynamic-update-slice_fusion.12, s32[384]{0:T(512)S(1)} %pad_add_fusion, pred[384]{0:T(512)(128)(4,1)S(1)} %pad_add_fusion.1, ...), kind=kOutput, calls=%fused_computation.68 | convolution fusion | flops 370671616 | bytes 3778432 | tf_op jit(solution)/shard_map/dot_general | solution.py:58
  68.0 1.4 %fusion.213 = bf16[384,128]{1,0:T(8,128)(2,1)S(1)} fusion(f32[384,128]{1,0:T(8,128)} %fusion.256, bf16[384,384]{1,0:T(8,128)(2,1)} %copy-done.5, bf16[384,128]{1,0:T(8,128)(2,1)S(1)} %constant_dynamic-update-slice_fusion.12, f32[384]{0:T(512)S(1)} %select_reduce_fusion), kind=kOutput, calls=%fused_computation.102 | convolution fusion | flops 38043648 | bytes 689664 | tf_op jit(solution)/shard_map/dot_general | solution.py:58
  69.4 2.4 %collective-permute-start.15 = (bf16[128,128]{1,0:T(8,128)(2,1)S(1)}, bf16[128,128]{1,0:T(8,128)(2,1)S(1)}, u32[]{:S(2)}, u32[]{:S(2)}) collective-permute-start(bf16[128,128]{1,0:T(8,128)(2,1)S(1)} %get-tuple-element.13), channel_id=1, source_target_pairs={{0,31},{1,2},{2,1},{3,4},{4,3},{5,6},{6,5},{7,8},{8,7},{9,10},{10,... | collective-permute-start | bytes 98312 | tf_op jit(solution)/shard_map/ppermute | solution.py:62
  71.8 1.7 %convolution_subtract_fusion = f32[384,128]{1,0:T(8,128)S(1)} fusion(f32[384,128]{1,0:T(8,128)} %get-tuple-element.36, bf16[384,1024]{1,0:T(8,128)(2,1)} %copy-done.4, f32[1024,128]{0,1:T(8,128)} %fusion.151), kind=kOutput, calls=%fused_computation.95 | convolution fusion | flops 100843520 | bytes 1703936 | tf_op jit(solution)/shard_map/dot_general | solution.py:55
  73.7 2.8 %collective-permute-done.15 = bf16[128,128]{1,0:T(8,128)(2,1)S(1)} collective-permute-done((bf16[128,128]{1,0:T(8,128)(2,1)S(1)}, bf16[128,128]{1,0:T(8,128)(2,1)S(1)}, u32[]{:S(2)}, u32[]{:S(2)}) %collective-permute-start.15) | collective-permute-done | bytes 32800 | tf_op jit(solution)/shard_map/ppermute | solution.py:62
  76.4 2.0 %collective-permute-done.17 = bf16[128,128]{1,0:T(8,128)(2,1)S(1)} collective-permute-done((bf16[128,128]{1,0:T(8,128)(2,1)S(1)}, bf16[128,128]{1,0:T(8,128)(2,1)S(1)}, u32[]{:S(2)}, u32[]{:S(2)}) %collective-permute-start.17) | collective-permute-done | bytes 32800 | tf_op jit(solution)/shard_map/ppermute | solution.py:62
  78.5 0.5 fusion.103
  79.3 1.9 %collective-permute-start.18 = (bf16[128,128]{1,0:T(8,128)(2,1)S(1)}, bf16[128,128]{1,0:T(8,128)(2,1)S(1)}, u32[]{:S(2)}, u32[]{:S(2)}) collective-permute-start(bf16[128,128]{1,0:T(8,128)(2,1)S(1)} %get-tuple-element.10), channel_id=1, source_target_pairs={{0,31},{1,2},{2,1},{3,4},{4,3},{5,6},{6,5},{7,8},{8,7},{9,10},{10,... | collective-permute-start | bytes 98312 | tf_op jit(solution)/shard_map/ppermute | solution.py:62
  82.1 4.2 %collective-permute-done.18 = bf16[128,128]{1,0:T(8,128)(2,1)S(1)} collective-permute-done((bf16[128,128]{1,0:T(8,128)(2,1)S(1)}, bf16[128,128]{1,0:T(8,128)(2,1)S(1)}, u32[]{:S(2)}, u32[]{:S(2)}) %collective-permute-start.18) | collective-permute-done | bytes 32800 | tf_op jit(solution)/shard_map/ppermute | solution.py:62
  86.7 2.1 %collective-permute-start.21 = (bf16[128,128]{1,0:T(8,128)(2,1)S(1)}, bf16[128,128]{1,0:T(8,128)(2,1)S(1)}, u32[]{:S(2)}, u32[]{:S(2)}) collective-permute-start(bf16[128,128]{1,0:T(8,128)(2,1)S(1)} %get-tuple-element.5), channel_id=1, source_target_pairs={{0,31},{1,2},{2,1},{3,4},{4,3},{5,6},{6,5},{7,8},{8,7},{9,10},{10,... | collective-permute-start | bytes 98312 | tf_op jit(solution)/shard_map/ppermute | solution.py:62
  88.9 4.8 %collective-permute-done.21 = bf16[128,128]{1,0:T(8,128)(2,1)S(1)} collective-permute-done((bf16[128,128]{1,0:T(8,128)(2,1)S(1)}, bf16[128,128]{1,0:T(8,128)(2,1)S(1)}, u32[]{:S(2)}, u32[]{:S(2)}) %collective-permute-start.21) | collective-permute-done | bytes 32800 | tf_op jit(solution)/shard_map/ppermute | solution.py:62
  93.7 1.3 %fusion.55 = f32[1024,128]{0,1:T(8,128)} fusion(s32[384]{0:T(512)S(1)} %pad_add_fusion, pred[384]{0:T(512)(128)(4,1)S(1)} %pad_add_fusion.1, bf16[128,128]{1,0:T(8,128)(2,1)S(1)} %collective-permute-done.23, bf16[128,128]{1,0:T(8,128)(2,1)S(1)} %collective-permute-done.22, bf16[128,128]{1,0:T(8,128)(2,1)S(1)} %collective-permute-done.21), kind=kOutput, calls=%fused_computation.36 | convolution fusion | flops 101875712 | bytes 624512 | tf_op jit(solution)/shard_map/dot_general | solution.py:58
  95.0 2.4 %fusion.191 = f32[1,1024,128]{1,2,0:T(8,128)S(1)} fusion(f32[1024,128]{0,1:T(8,128)} %fusion.55, f32[1024,128]{0,1:T(8,128)} %copy-done.18, bf16[1,1024,1024]{2,1,0:T(8,128)(2,1)S(1)} %copy-done, f32[1024,128]{0,1:T(8,128)S(1)} %fusion.85, bf16[384,128]{1,0:T(8,128)(2,1)S(1)} %constant_dynamic-update-slice_fusion.18, s32[384]{0:T(512)S(1)} %pad_add_fusion, ...), kind=kOutput, calls=%fused_computation.80 | convolution fusion | flops 370802688 | bytes 4302720 | tf_op jit(solution)/shard_map/dot_general | solution.py:58
  97.5 1.0 %copy.19 = f32[1,1024,128]{2,1,0:T(8,128)} copy(f32[1,1024,128]{1,2,0:T(8,128)S(1)} %fusion.191) | data formatting | bytes 1048576 | tf_op jit(solution)/shard_map/broadcast_in_dim | solution.py:92
  (115 shorter events, 4.3 us)
Async XLA Ops:
  0.0 16.9 %copy-start = (bf16[1,1024,1024]{2,1,0:T(8,128)(2,1)S(1)}, bf16[1,1024,1024]{2,1,0:T(8,128)(2,1)}, u32[]{:S(2)}) copy-start(bf16[1,1024,1024]{2,1,0:T(8,128)(2,1)} %param.9) | copy-start | bytes 6291460
  0.0 13.4 %copy-start.20 = (bf16[1,1024,128]{2,1,0:T(8,128)(2,1)S(1)}, bf16[1,1024,128]{2,1,0:T(8,128)(2,1)}, u32[]{:S(2)}) copy-start(bf16[1,1024,128]{2,1,0:T(8,128)(2,1)} %param.7) | copy-start | bytes 786436
  7.0 14.3 %collective-permute-start = (bf16[128,128]{1,0:T(8,128)(2,1)}, bf16[128,128]{1,0:T(8,128)(2,1)}, u32[]{:S(2)}, u32[]{:S(2)}) collective-permute-start(bf16[128,128]{1,0:T(8,128)(2,1)} %get-tuple-element.28), channel_id=1, source_target_pairs={{0,31},{1,2},{2,1},{3,4},{4,3},{5,6},{6,5},{7,8},{8,7},{9,10},{10,... | collective-permute-start | bytes 98312 | tf_op jit(solution)/shard_map/ppermute | solution.py:62
  13.4 9.3 %collective-permute-start.1 = (bf16[128,128]{1,0:T(8,128)(2,1)}, bf16[128,128]{1,0:T(8,128)(2,1)S(1)}, u32[]{:S(2)}, u32[]{:S(2)}) collective-permute-start(bf16[128,128]{1,0:T(8,128)(2,1)} %get-tuple-element.27), channel_id=1, source_target_pairs={{0,1},{1,0},{2,3},{3,2},{4,5},{5,4},{6,7},{7,6},{8,9},{9,8},{10,11... | collective-permute-start | bytes 98312 | tf_op jit(solution)/shard_map/ppermute | solution.py:62
  13.4 10.0 %collective-permute-start.2 = (bf16[128,128]{1,0:T(8,128)(2,1)}, bf16[128,128]{1,0:T(8,128)(2,1)S(1)}, u32[]{:S(2)}, u32[]{:S(2)}) collective-permute-start(bf16[128,128]{1,0:T(8,128)(2,1)} %get-tuple-element.26), channel_id=1, source_target_pairs={{0,16},{1,17},{2,18},{3,19},{4,20},{5,21},{6,22},{7,23},{8,24},{9,... | collective-permute-start | bytes 98312 | tf_op jit(solution)/shard_map/ppermute | solution.py:62
  13.6 10.4 %copy-start.7 = (bf16[1,1024,128]{1,2,0:T(8,128)(2,1)}, bf16[1,1024,128]{1,2,0:T(8,128)(2,1)S(1)}, u32[]{:S(2)}) copy-start(bf16[1,1024,128]{1,2,0:T(8,128)(2,1)S(1)} %copy.14) | copy-start | bytes 786436
  16.9 1.7 %copy-start.4 = (bf16[384,1024]{1,0:T(8,128)(2,1)}, bf16[384,1024]{1,0:T(8,128)(2,1)S(1)}, u32[]{:S(2)}) copy-start(bf16[384,1024]{1,0:T(8,128)(2,1)S(1)} %fusion.46) | copy-start | bytes 2359300
  18.6 8.3 %copy-start.5 = (bf16[384,384]{1,0:T(8,128)(2,1)}, bf16[384,384]{1,0:T(8,128)(2,1)S(1)}, u32[]{:S(2)}) copy-start(bf16[384,384]{1,0:T(8,128)(2,1)S(1)} %fusion.166) | copy-start | bytes 884740
  18.6 1.4 %copy-start.21 = (f32[1,1024]{1,0:T(1,128)S(1)}, f32[1,1024]{1,0:T(1,128)}, u32[]{:S(2)}) copy-start(f32[1,1024]{1,0:T(1,128)} %param.10) | copy-start | bytes 12292
  26.9 8.7 %copy-start.19 = (f32[1024,128]{0,1:T(8,128)S(1)}, f32[1024,128]{0,1:T(8,128)}, u32[]{:S(2)}) copy-start(f32[1024,128]{0,1:T(8,128)} %fusion.127) | copy-start | bytes 1572868
  28.3 7.1 %collective-permute-start.3 = (bf16[128,128]{1,0:T(8,128)(2,1)S(1)}, bf16[128,128]{1,0:T(8,128)(2,1)S(1)}, u32[]{:S(2)}, u32[]{:S(2)}) collective-permute-start(bf16[128,128]{1,0:T(8,128)(2,1)S(1)} %get-tuple-element.25), channel_id=1, source_target_pairs={{0,31},{1,2},{2,1},{3,4},{4,3},{5,6},{6,5},{7,8},{8,7},{9,10},{10,... | collective-permute-start | bytes 98312 | tf_op jit(solution)/shard_map/ppermute | solution.py:62
  30.2 5.2 %collective-permute-start.4 = (bf16[128,128]{1,0:T(8,128)(2,1)S(1)}, bf16[128,128]{1,0:T(8,128)(2,1)S(1)}, u32[]{:S(2)}, u32[]{:S(2)}) collective-permute-start(bf16[128,128]{1,0:T(8,128)(2,1)S(1)} %get-tuple-element.24), channel_id=1, source_target_pairs={{0,1},{1,0},{2,3},{3,2},{4,5},{5,4},{6,7},{7,6},{8,9},{9,8},{10,11... | collective-permute-start | bytes 98312 | tf_op jit(solution)/shard_map/ppermute | solution.py:62
  30.2 5.4 %collective-permute-start.5 = (bf16[128,128]{1,0:T(8,128)(2,1)S(1)}, bf16[128,128]{1,0:T(8,128)(2,1)S(1)}, u32[]{:S(2)}, u32[]{:S(2)}) collective-permute-start(bf16[128,128]{1,0:T(8,128)(2,1)S(1)} %get-tuple-element.23), channel_id=1, source_target_pairs={{0,16},{1,17},{2,18},{3,19},{4,20},{5,21},{6,22},{7,23},{8,24},{9,... | collective-permute-start | bytes 98312 | tf_op jit(solution)/shard_map/ppermute | solution.py:62
  31.6 4.6 %copy-start.11 = (bf16[384,384]{1,0:T(8,128)(2,1)S(1)}, bf16[384,384]{1,0:T(8,128)(2,1)}, u32[]{:S(2)}) copy-start(bf16[384,384]{1,0:T(8,128)(2,1)} %fusion.169) | copy-start | bytes 884740
  33.3 6.1 %copy-start.1 = (bf16[1,1024,1024]{2,1,0:T(8,128)(2,1)S(1)}, bf16[1,1024,1024]{2,1,0:T(8,128)(2,1)}, u32[]{:S(2)}) copy-start(bf16[1,1024,1024]{2,1,0:T(8,128)(2,1)} %param.8) | copy-start | bytes 6291460
  33.3 6.1 %copy-start.8 = (bf16[1,1024,128]{1,2,0:T(8,128)(2,1)S(1)}, bf16[1,1024,128]{1,2,0:T(8,128)(2,1)}, u32[]{:S(2)}) copy-start(bf16[1,1024,128]{1,2,0:T(8,128)(2,1)} %copy-done.7) | copy-start | bytes 786436
  36.1 3.7 %copy-start.16 = (f32[1024,128]{0,1:T(8,128)}, f32[1024,128]{0,1:T(8,128)S(1)}, u32[]{:S(2)}) copy-start(f32[1024,128]{0,1:T(8,128)S(1)} %fusion.115) | copy-start | bytes 1572868
  36.4 7.1 %collective-permute-start.6 = (bf16[128,128]{1,0:T(8,128)(2,1)S(1)}, bf16[128,128]{1,0:T(8,128)(2,1)S(1)}, u32[]{:S(2)}, u32[]{:S(2)}) collective-permute-start(bf16[128,128]{1,0:T(8,128)(2,1)S(1)} %get-tuple-element.22), channel_id=1, source_target_pairs={{0,31},{1,2},{2,1},{3,4},{4,3},{5,6},{6,5},{7,8},{8,7},{9,10},{10,... | collective-permute-start | bytes 98312 | tf_op jit(solution)/shard_map/ppermute | solution.py:62
  38.3 5.2 %collective-permute-start.7 = (bf16[128,128]{1,0:T(8,128)(2,1)S(1)}, bf16[128,128]{1,0:T(8,128)(2,1)S(1)}, u32[]{:S(2)}, u32[]{:S(2)}) collective-permute-start(bf16[128,128]{1,0:T(8,128)(2,1)S(1)} %get-tuple-element.21), channel_id=1, source_target_pairs={{0,1},{1,0},{2,3},{3,2},{4,5},{5,4},{6,7},{7,6},{8,9},{9,8},{10,11... | collective-permute-start | bytes 98312 | tf_op jit(solution)/shard_map/ppermute | solution.py:62
  38.3 5.2 %collective-permute-start.8 = (bf16[128,128]{1,0:T(8,128)(2,1)S(1)}, bf16[128,128]{1,0:T(8,128)(2,1)S(1)}, u32[]{:S(2)}, u32[]{:S(2)}) collective-permute-start(bf16[128,128]{1,0:T(8,128)(2,1)S(1)} %get-tuple-element.20), channel_id=1, source_target_pairs={{0,16},{1,17},{2,18},{3,19},{4,20},{5,21},{6,22},{7,23},{8,24},{9,... | collective-permute-start | bytes 98312 | tf_op jit(solution)/shard_map/ppermute | solution.py:62
  46.6 10.1 %copy-start.15 = (f32[1024,128]{0,1:T(8,128)S(1)}, f32[1024,128]{0,1:T(8,128)}, u32[]{:S(2)}) copy-start(f32[1024,128]{0,1:T(8,128)} %fusion.139) | copy-start | bytes 1572868
  48.0 9.2 %copy-start.12 = (bf16[384,384]{1,0:T(8,128)(2,1)S(1)}, bf16[384,384]{1,0:T(8,128)(2,1)}, u32[]{:S(2)}) copy-start(bf16[384,384]{1,0:T(8,128)(2,1)} %fusion.169) | copy-start | bytes 884740
  48.0 7.0 %collective-permute-start.9 = (bf16[128,128]{1,0:T(8,128)(2,1)S(1)}, bf16[128,128]{1,0:T(8,128)(2,1)S(1)}, u32[]{:S(2)}, u32[]{:S(2)}) collective-permute-start(bf16[128,128]{1,0:T(8,128)(2,1)S(1)} %get-tuple-element.19), channel_id=1, source_target_pairs={{0,31},{1,2},{2,1},{3,4},{4,3},{5,6},{6,5},{7,8},{8,7},{9,10},{10,... | collective-permute-start | bytes 98312 | tf_op jit(solution)/shard_map/ppermute | solution.py:62
  51.7 8.2 %copy-start.2 = (bf16[1,1024,1024]{2,1,0:T(8,128)(2,1)S(1)}, bf16[1,1024,1024]{2,1,0:T(8,128)(2,1)}, u32[]{:S(2)}) copy-start(bf16[1,1024,1024]{2,1,0:T(8,128)(2,1)} %param.8) | copy-start | bytes 6291460
  51.8 8.2 %copy-start.9 = (bf16[1,1024,128]{1,2,0:T(8,128)(2,1)S(1)}, bf16[1,1024,128]{1,2,0:T(8,128)(2,1)}, u32[]{:S(2)}) copy-start(bf16[1,1024,128]{1,2,0:T(8,128)(2,1)} %copy-done.7) | copy-start | bytes 786436
  51.8 3.3 %collective-permute-start.10 = (bf16[128,128]{1,0:T(8,128)(2,1)S(1)}, bf16[128,128]{1,0:T(8,128)(2,1)S(1)}, u32[]{:S(2)}, u32[]{:S(2)}) collective-permute-start(bf16[128,128]{1,0:T(8,128)(2,1)S(1)} %get-tuple-element.18), channel_id=1, source_target_pairs={{0,1},{1,0},{2,3},{3,2},{4,5},{5,4},{6,7},{7,6},{8,9},{9,8},{10,11... | collective-permute-start | bytes 98312 | tf_op jit(solution)/shard_map/ppermute | solution.py:62
  51.8 4.9 %collective-permute-start.11 = (bf16[128,128]{1,0:T(8,128)(2,1)S(1)}, bf16[128,128]{1,0:T(8,128)(2,1)S(1)}, u32[]{:S(2)}, u32[]{:S(2)}) collective-permute-start(bf16[128,128]{1,0:T(8,128)(2,1)S(1)} %get-tuple-element.17), channel_id=1, source_target_pairs={{0,16},{1,17},{2,18},{3,19},{4,20},{5,21},{6,22},{7,23},{8,24},{9,... | collective-permute-start | bytes 98312 | tf_op jit(solution)/shard_map/ppermute | solution.py:62
  57.3 3.1 %copy-start.17 = (f32[1024,128]{0,1:T(8,128)}, f32[1024,128]{0,1:T(8,128)S(1)}, u32[]{:S(2)}) copy-start(f32[1024,128]{0,1:T(8,128)S(1)} %fusion.109) | copy-start | bytes 1572868
  57.6 7.0 %collective-permute-start.12 = (bf16[128,128]{1,0:T(8,128)(2,1)S(1)}, bf16[128,128]{1,0:T(8,128)(2,1)S(1)}, u32[]{:S(2)}, u32[]{:S(2)}) collective-permute-start(bf16[128,128]{1,0:T(8,128)(2,1)S(1)} %get-tuple-element.16), channel_id=1, source_target_pairs={{0,31},{1,2},{2,1},{3,4},{4,3},{5,6},{6,5},{7,8},{8,7},{9,10},{10,... | collective-permute-start | bytes 98312 | tf_op jit(solution)/shard_map/ppermute | solution.py:62
  59.9 4.7 %collective-permute-start.13 = (bf16[128,128]{1,0:T(8,128)(2,1)S(1)}, bf16[128,128]{1,0:T(8,128)(2,1)S(1)}, u32[]{:S(2)}, u32[]{:S(2)}) collective-permute-start(bf16[128,128]{1,0:T(8,128)(2,1)S(1)} %get-tuple-element.15), channel_id=1, source_target_pairs={{0,1},{1,0},{2,3},{3,2},{4,5},{5,4},{6,7},{7,6},{8,9},{9,8},{10,11... | collective-permute-start | bytes 98312 | tf_op jit(solution)/shard_map/ppermute | solution.py:62
  59.9 4.8 %collective-permute-start.14 = (bf16[128,128]{1,0:T(8,128)(2,1)S(1)}, bf16[128,128]{1,0:T(8,128)(2,1)S(1)}, u32[]{:S(2)}, u32[]{:S(2)}) collective-permute-start(bf16[128,128]{1,0:T(8,128)(2,1)S(1)} %get-tuple-element.14), channel_id=1, source_target_pairs={{0,16},{1,17},{2,18},{3,19},{4,20},{5,21},{6,22},{7,23},{8,24},{9,... | collective-permute-start | bytes 98312 | tf_op jit(solution)/shard_map/ppermute | solution.py:62
  68.0 10.5 %copy-start.14 = (f32[1024,128]{0,1:T(8,128)S(1)}, f32[1024,128]{0,1:T(8,128)}, u32[]{:S(2)}) copy-start(f32[1024,128]{0,1:T(8,128)} %fusion.151) | copy-start | bytes 1572868
  69.4 9.6 %copy-start.13 = (bf16[384,384]{1,0:T(8,128)(2,1)S(1)}, bf16[384,384]{1,0:T(8,128)(2,1)}, u32[]{:S(2)}) copy-start(bf16[384,384]{1,0:T(8,128)(2,1)} %fusion.169) | copy-start | bytes 884740
  69.4 7.0 %collective-permute-start.15 = (bf16[128,128]{1,0:T(8,128)(2,1)S(1)}, bf16[128,128]{1,0:T(8,128)(2,1)S(1)}, u32[]{:S(2)}, u32[]{:S(2)}) collective-permute-start(bf16[128,128]{1,0:T(8,128)(2,1)S(1)} %get-tuple-element.13), channel_id=1, source_target_pairs={{0,31},{1,2},{2,1},{3,4},{4,3},{5,6},{6,5},{7,8},{8,7},{9,10},{10,... | collective-permute-start | bytes 98312 | tf_op jit(solution)/shard_map/ppermute | solution.py:62
  73.5 7.8 %copy-start.3 = (bf16[1,1024,1024]{2,1,0:T(8,128)(2,1)S(1)}, bf16[1,1024,1024]{2,1,0:T(8,128)(2,1)}, u32[]{:S(2)}) copy-start(bf16[1,1024,1024]{2,1,0:T(8,128)(2,1)} %param.8) | copy-start | bytes 6291460
  73.5 7.8 %copy-start.10 = (bf16[1,1024,128]{1,2,0:T(8,128)(2,1)S(1)}, bf16[1,1024,128]{1,2,0:T(8,128)(2,1)}, u32[]{:S(2)}) copy-start(bf16[1,1024,128]{1,2,0:T(8,128)(2,1)} %copy-done.7) | copy-start | bytes 786436
  73.5 2.9 %collective-permute-start.16 = (bf16[128,128]{1,0:T(8,128)(2,1)S(1)}, bf16[128,128]{1,0:T(8,128)(2,1)S(1)}, u32[]{:S(2)}, u32[]{:S(2)}) collective-permute-start(bf16[128,128]{1,0:T(8,128)(2,1)S(1)} %get-tuple-element.12), channel_id=1, source_target_pairs={{0,1},{1,0},{2,3},{3,2},{4,5},{5,4},{6,7},{7,6},{8,9},{9,8},{10,11... | collective-permute-start | bytes 98312 | tf_op jit(solution)/shard_map/ppermute | solution.py:62
  73.6 4.9 %collective-permute-start.17 = (bf16[128,128]{1,0:T(8,128)(2,1)S(1)}, bf16[128,128]{1,0:T(8,128)(2,1)S(1)}, u32[]{:S(2)}, u32[]{:S(2)}) collective-permute-start(bf16[128,128]{1,0:T(8,128)(2,1)S(1)} %get-tuple-element.11), channel_id=1, source_target_pairs={{0,16},{1,17},{2,18},{3,19},{4,20},{5,21},{6,22},{7,23},{8,24},{9,... | collective-permute-start | bytes 98312 | tf_op jit(solution)/shard_map/ppermute | solution.py:62
  79.0 2.7 %copy-start.18 = (f32[1024,128]{0,1:T(8,128)}, f32[1024,128]{0,1:T(8,128)S(1)}, u32[]{:S(2)}) copy-start(f32[1024,128]{0,1:T(8,128)S(1)} %fusion.103) | copy-start | bytes 1572868
  79.3 7.0 %collective-permute-start.18 = (bf16[128,128]{1,0:T(8,128)(2,1)S(1)}, bf16[128,128]{1,0:T(8,128)(2,1)S(1)}, u32[]{:S(2)}, u32[]{:S(2)}) collective-permute-start(bf16[128,128]{1,0:T(8,128)(2,1)S(1)} %get-tuple-element.10), channel_id=1, source_target_pairs={{0,31},{1,2},{2,1},{3,4},{4,3},{5,6},{6,5},{7,8},{8,7},{9,10},{10,... | collective-permute-start | bytes 98312 | tf_op jit(solution)/shard_map/ppermute | solution.py:62
  81.2 5.1 %collective-permute-start.19 = (bf16[128,128]{1,0:T(8,128)(2,1)S(1)}, bf16[128,128]{1,0:T(8,128)(2,1)S(1)}, u32[]{:S(2)}, u32[]{:S(2)}) collective-permute-start(bf16[128,128]{1,0:T(8,128)(2,1)S(1)} %get-tuple-element.9), channel_id=1, source_target_pairs={{0,1},{1,0},{2,3},{3,2},{4,5},{5,4},{6,7},{7,6},{8,9},{9,8},{10,11... | collective-permute-start | bytes 98312 | tf_op jit(solution)/shard_map/ppermute | solution.py:62
  81.2 5.1 %collective-permute-start.20 = (bf16[128,128]{1,0:T(8,128)(2,1)S(1)}, bf16[128,128]{1,0:T(8,128)(2,1)S(1)}, u32[]{:S(2)}, u32[]{:S(2)}) collective-permute-start(bf16[128,128]{1,0:T(8,128)(2,1)S(1)} %get-tuple-element.8), channel_id=1, source_target_pairs={{0,16},{1,17},{2,18},{3,19},{4,20},{5,21},{6,22},{7,23},{8,24},{9,... | collective-permute-start | bytes 98312 | tf_op jit(solution)/shard_map/ppermute | solution.py:62
  81.7 4.6 %copy-start.6 = (bf16[384,384]{1,0:T(8,128)(2,1)S(1)}, bf16[384,384]{1,0:T(8,128)(2,1)}, u32[]{:S(2)}) copy-start(bf16[384,384]{1,0:T(8,128)(2,1)} %copy-done.5) | copy-start | bytes 884740
  86.7 7.0 %collective-permute-start.21 = (bf16[128,128]{1,0:T(8,128)(2,1)S(1)}, bf16[128,128]{1,0:T(8,128)(2,1)S(1)}, u32[]{:S(2)}, u32[]{:S(2)}) collective-permute-start(bf16[128,128]{1,0:T(8,128)(2,1)S(1)} %get-tuple-element.5), channel_id=1, source_target_pairs={{0,31},{1,2},{2,1},{3,4},{4,3},{5,6},{6,5},{7,8},{8,7},{9,10},{10,... | collective-permute-start | bytes 98312 | tf_op jit(solution)/shard_map/ppermute | solution.py:62
  88.8 4.9 %collective-permute-start.22 = (bf16[128,128]{1,0:T(8,128)(2,1)S(1)}, bf16[128,128]{1,0:T(8,128)(2,1)S(1)}, u32[]{:S(2)}, u32[]{:S(2)}) collective-permute-start(bf16[128,128]{1,0:T(8,128)(2,1)S(1)} %get-tuple-element.7), channel_id=1, source_target_pairs={{0,1},{1,0},{2,3},{3,2},{4,5},{5,4},{6,7},{7,6},{8,9},{9,8},{10,11... | collective-permute-start | bytes 98312 | tf_op jit(solution)/shard_map/ppermute | solution.py:62
  88.8 4.9 %collective-permute-start.23 = (bf16[128,128]{1,0:T(8,128)(2,1)S(1)}, bf16[128,128]{1,0:T(8,128)(2,1)S(1)}, u32[]{:S(2)}, u32[]{:S(2)}) collective-permute-start(bf16[128,128]{1,0:T(8,128)(2,1)S(1)} %get-tuple-element.6), channel_id=1, source_target_pairs={{0,16},{1,17},{2,18},{3,19},{4,20},{5,21},{6,22},{7,23},{8,24},{9,... | collective-permute-start | bytes 98312 | tf_op jit(solution)/shard_map/ppermute | solution.py:62

commit v7 on v5

v7 whole, which is shorter than its diff:
```python
import functools

import jax
import jax.numpy as jnp
from jax import lax
from jax.experimental import pallas as pl
from jax.experimental.pallas import tpu as pltpu
from jax.sharding import PartitionSpec as P

ITERS = 4
FAR = 16
DAMPING = 0.7
LIMIT = 16 * 2**20
F32 = jnp.float32
BF16 = jnp.bfloat16


def swaps(count):
    near = [(i, i ^ 1) for i in range(count)]
    cross = [(i, (((i + 1) ^ 1) - 1) % count) for i in range(count)]
    blocks = count // FAR
    far = [(i, i ^ FAR) for i in range(count)] if blocks > 1 else []
    again = [(i, (((i // FAR + 1) ^ 1) - 1) % blocks * FAR + i % FAR) for i in range(count)] if blocks > 2 else []
    return [pairs for pairs in (cross, near, far, again) if pairs]


def slots_of(index, count):
    odd = lax.rem(index, 2)
    block = lax.rem(lax.div(index, FAR), 2)
    slots = [1 - odd, odd, 2 + block, 3 - block]
    return slots[: 2 + (count // FAR > 1) + (count // FAR > 2)]


def times(a, b):
    return jnp.dot(a, b, preferred_element_type=F32)


def times_t(a, b):
    return lax.dot_general(a, b, (((1,), (1,)), ((), ())), preferred_element_type=F32)


def gather(refs):
    return jnp.concatenate([ref[...] for ref in refs], 1)


def scatter(refs, block):
    share = refs[0].shape[1]
    for k, ref in enumerate(refs):
        ref[...] = block[:, k * share : (k + 1) * share].astype(ref.dtype)


def open_kernel(subs, links, rows_ref, live_ref, rhs_ref, hot_ref, turned_ref, picked_ref, *out_refs):
    width, share = rhs_ref.shape[1], rows_ref.shape[2]
    slots = slots_of(lax.axis_index("sub"), subs)
    place = lax.broadcasted_iota(jnp.int32, (width, share), 0)
    turned = rhs_ref[0].T
    turned_ref[...] = turned
    for k, slot in enumerate(slots):
        row = jnp.where(live_ref[0, slot] >= 0, rows_ref[0, pl.ds(slot, 1), :], -1)
        hot = jnp.where(place == row, 1.0, 0.0).astype(BF16)
        part = pl.ds(k * share, share)
        hot_ref[:, part] = hot
        message = times(turned, hot).astype(BF16)
        picked_ref[:, part] = message
        out_refs[k][...] = message


def pick_n_kernel(
    hot_ref, turned_ref, n_ref, weight_ref, count_ref, n_pick_ref, n_small_ref, same_ref, inner_ref, mask_ref, local_ref, base_ref, first_ref, chosen_ref
):
    hot = hot_ref[...]
    width, total = hot.shape
    weight = weight_ref[...]
    hot_t = hot.T
    n_pick = times(hot_t, n_ref[0]).astype(BF16)
    n_pick_ref[...] = n_pick
    same = times(hot_t, hot)
    same_ref[...] = same.astype(BF16)
    earlier = lax.broadcasted_iota(jnp.int32, same.shape, 0) < lax.broadcasted_iota(jnp.int32, same.shape, 1)
    repeats = jnp.sum(jnp.where(earlier, same, 0.0), 0, keepdims=True)
    first = jnp.where(repeats > 0.0, 0.0, 1.0)
    first_ref[...] = jnp.broadcast_to(first, first_ref.shape)
    n_small_ref[...] = (times(n_pick, hot) * first).astype(BF16)
    hits = times_t(jnp.ones((8, total), BF16), hot)[:1]
    inner = jnp.where(hits > 0.0, 0.0, 1.0)
    inner_ref[...] = jnp.broadcast_to(inner, inner_ref.shape)
    place = lax.broadcasted_iota(jnp.int32, (1, width), 1)
    mask = jnp.where(place < count_ref[0], 1.0, 0.0)
    mask_ref[...] = jnp.broadcast_to(mask, mask_ref.shape)
    high = weight.astype(BF16)
    rest = weight - high.astype(F32)
    middle = rest.astype(BF16)
    low = (rest - middle.astype(F32)).astype(BF16)
    pieces = [times(jnp.broadcast_to(piece, (8, width)), hot) for piece in (high, middle, low)]
    chosen = (pieces[0] + pieces[1]) + pieces[2]
    chosen_ref[...] = chosen
    local = mask * turned_ref[...].astype(F32)
    local_ref[...] = local
    base_ref[...] = times_t((weight * local * inner).astype(BF16), n_pick)


def update_path_kernel(links, *refs):
    arrived_refs, refs = refs[:links], refs[links:]
    same_ref, n_small_ref, chosen_ref, local_ref, base_ref, state_ref, state_out_ref = refs[:7]
    chosen = chosen_ref[:1]
    residual = local_ref[...].astype(F32) + times(gather(arrived_refs), same_ref[...])
    scaled = (chosen * residual).astype(BF16)
    sent = chosen * (base_ref[...] + times_t(scaled, n_small_ref[...]))
    scatter(refs[7:], sent)
    state_out_ref[...] = state_ref[...] + DAMPING * sent


def first_update_path_kernel(links, *refs):
    arrived_refs, refs = refs[:links], refs[links:]
    same_ref, n_small_ref, chosen_ref, local_ref, base_ref, state_out_ref = refs[:6]
    chosen = chosen_ref[:1]
    residual = local_ref[...].astype(F32) + times(gather(arrived_refs), same_ref[...])
    scaled = (chosen * residual).astype(BF16)
    sent = chosen * (base_ref[...] + times_t(scaled, n_small_ref[...]))
    scatter(refs[6:], sent)
    state_out_ref[...] = DAMPING * sent


def residual_path_kernel(links, *refs):
    arrived_refs, refs = refs[:links], refs[links:]
    same_ref, s_small_ref, base_ref, state_ref, state_out_ref, local_ref = refs[:6]
    state = state_ref[...] + DAMPING * times(gather(arrived_refs), same_ref[...])
    state_out_ref[...] = state
    local = base_ref[...] - times(state.astype(BF16), s_small_ref[...])
    local_ref[...] = local
    scatter(refs[6:], local)


def corrected(links, arrived_refs, hot_ref, n_ref, weight_ref, mask_ref, local_ref):
    weight = weight_ref[...]
    residual = local_ref[...] + times_t(gather(arrived_refs), hot_ref[...])
    scaled = (weight * residual).astype(BF16)
    return mask_ref[:1] * weight * times_t(scaled, n_ref[0])


def first_update_kernel(links, *refs):
    arrived_refs, refs = refs[:links], refs[links:]
    hot_ref, n_ref, s_ref, weight_ref, mask_ref, inner_ref, first_ref, local_ref, picked_ref = refs[:9]
    state_out_ref, base_ref, s_pick_ref, s_small_ref = refs[9:]
    state = DAMPING * corrected(links, arrived_refs, hot_ref, n_ref, weight_ref, mask_ref, local_ref)
    state_out_ref[...] = state
    hot = hot_ref[...]
    s_pick = times(s_ref[0], hot).astype(BF16)
    s_pick_ref[...] = s_pick
    alone = (hot.astype(F32) * first_ref[:1]).astype(BF16)
    s_small_ref[...] = times(alone.T, s_pick).astype(BF16)
    base_ref[...] = picked_ref[...].astype(F32) - times((state * inner_ref[:1]).astype(BF16), s_pick)


def update_kernel(links, *refs):
    arrived_refs, refs = refs[:links], refs[links:]
    hot_ref, n_ref, weight_ref, mask_ref, inner_ref, local_ref, picked_ref, s_pick_ref, state_ref = refs[:9]
    state_out_ref, base_ref = refs[9:]
    state = state_ref[...] + DAMPING * corrected(links, arrived_refs, hot_ref, n_ref, weight_ref, mask_ref, local_ref)
    state_out_ref[...] = state
    base_ref[...] = picked_ref[...].astype(F32) - times((state * inner_ref[:1]).astype(BF16), s_pick_ref[...])


def last_update_kernel(links, *refs):
    arrived_refs, refs = refs[:links], refs[links:]
    hot_ref, n_ref, weight_ref, mask_ref, local_ref, state_ref, state_out_ref = refs
    state_out_ref[...] = state_ref[...] + DAMPING * corrected(
        links, arrived_refs, hot_ref, n_ref, weight_ref, mask_ref, local_ref
    )


def residual_kernel(links, *refs):
    arrived_refs, refs = refs[:links], refs[links:]
    hot_ref, s_ref, turned_ref, weight_ref, mask_ref, inner_ref, n_pick_ref, state_ref = refs[:8]
    state_out_ref, local_ref, base_ref = refs[8:]
    state = state_ref[...] + DAMPING * times_t(gather(arrived_refs), hot_ref[...])
    state_out_ref[...] = state
    local = mask_ref[:1] * (turned_ref[...].astype(F32) - times(state.astype(BF16), s_ref[0]))
    local_ref[...] = local
    base_ref[...] = times_t((weight_ref[...] * local * inner_ref[:1]).astype(BF16), n_pick_ref[...])


def close_kernel(links, *refs):
    arrived_refs, (hot_ref, state_ref, out_ref) = refs[:links], refs[links:]
    state = state_ref[...] + DAMPING * times_t(gather(arrived_refs), hot_ref[...])
    out_ref[0] = state.T


def run(kernel, operands, results, flops, scalars=()):
    specs = [
        pl.BlockSpec(memory_space=pltpu.SMEM if k in scalars else pltpu.VMEM) for k in range(len(operands))
    ]
    moved = sum(a.size * a.dtype.itemsize for a in (*operands, *results))
    return pl.pallas_call(
        kernel,
        out_shape=results,
        in_specs=specs,
        out_specs=[pl.BlockSpec(memory_space=pltpu.VMEM)] * len(results),
        compiler_params=pltpu.CompilerParams(vmem_limit_bytes=LIMIT),
        cost_estimate=pl.CostEstimate(flops=flops, bytes_accessed=moved, transcendentals=0),
    )(*operands)


def body(right_side, schur, neumann, weights, neighbours, counts, shared_rows):
    width, leads = right_side.shape[1:]
    share = shared_rows.shape[2]
    subs = lax.axis_size("sub")
    routes = swaps(subs)
    links = len(routes)
    total = links * share

    def array(rows, columns, kind=F32):
        return jax.ShapeDtypeStruct((rows, columns), kind)

    messages = [array(leads, share, BF16)] * links
    full, some = array(leads, width), array(leads, total)
    small = array(total, total, BF16)
    row = array(8, width)
    picks = 2 * leads * total * width
    whole = 2 * leads * width * width
    path = 4 * leads * total * total

    def exchange(parts):
        return [lax.ppermute(part, "sub", route) for part, route in zip(parts, routes)]

    hot, turned, picked, *sent = run(
        functools.partial(open_kernel, subs, links),
        [shared_rows, neighbours, right_side],
        [array(width, total, BF16), array(leads, width, BF16), array(leads, total, BF16), *messages],
        picks,
        scalars=(1,),
    )
    arrived = exchange(sent)
    n_pick, n_small, same, inner, mask, local, base, first, chosen = run(
        pick_n_kernel,
        [hot, turned, neumann, weights, counts],
        [array(total, width, BF16), small, small, row, row, full, some, array(8, total), array(8, total)],
        2 * total * width * width + 4 * total * total * width + picks,
        scalars=(4,),
    )
    near = picked
    for step in range(ITERS):
        came = arrived
        if step == 0:
            near_state, *sent = run(
                functools.partial(first_update_path_kernel, links),
                [*came, same, n_small, chosen, near, base],
                [some, *messages],
                path,
            )
        else:
            near_state, *sent = run(
                functools.partial(update_path_kernel, links),
                [*came, same, n_small, chosen, near, base, near_state],
                [some, *messages],
                path,
            )
        arrived = exchange(sent)
        if step == 0:
            state, base, s_pick, s_small = run(
                functools.partial(first_update_kernel, links),
                [*came, hot, neumann, schur, weights, mask, inner, first, local, picked],
                [full, some, array(width, total, BF16), small],
                whole + 2 * picks + 2 * total * width * (width + total),
            )
        elif step < ITERS - 1:
            state, base = run(
                functools.partial(update_kernel, links),
                [*came, hot, neumann, weights, mask, inner, local, picked, s_pick, state],
                [full, some],
                whole + 2 * picks,
            )
        else:
            (state,) = run(
                functools.partial(last_update_kernel, links),
                [*came, hot, neumann, weights, mask, local, state],
                [full],
                whole + picks,
            )
            break
        came = arrived
        near_state, near, *sent = run(
            functools.partial(residual_path_kernel, links),
            [*came, same, s_small, base, near_state],
            [some, some, *messages],
            path,
        )
        arrived = exchange(sent)
        state, local, base = run(
            functools.partial(residual_kernel, links),
            [*came, hot, schur, turned, weights, mask, inner, n_pick, state],
            [full, full, some],
            whole + 2 * picks,
        )
    (out,) = run(
        functools.partial(close_kernel, links),
        [*arrived, hot, state],
        [jax.ShapeDtypeStruct((1, width, leads), F32)],
        picks,
    )
    return out


def solution(mesh):
    in_specs = (
        P("sub", None, None),
        P("sub", None, None),
        P("sub", None, None),
        P("sub", None),
        P("sub", None),
        P("sub"),
        P("sub", None, None),
    )
    out_specs = P("sub", None, None)
    return jax.shard_map(body, mesh=mesh, in_specs=in_specs, out_specs=out_specs, check_vma=False)
```

time: 84.5 us -> 71 us (0.84)
  the two profiles are of different devices: /device:TPU:8 before, /device:TPU:0 now
where the time goes in v7:
time: 71 us; the launch traced here: 70.7 us
  starting transfers between devices  24.5 us (35%)
  waiting for transfers between devices  23.2 us (33%)
  Pallas kernels  17.6 us (25%)
  local copies, waits for them, and re-layouts  4.57 us (6%)
  between operations  0.82 us (1%)
    ppermute x24, starting transfers between devices, exchange(): lax.ppermute(part, 'sub', route)  24.5 us
    ppermute x24, waiting for transfers between devices, exchange(): lax.ppermute(part, 'sub', route)  23.2 us
    pallas_call x17, Pallas kernels, run(): pl.pallas_call(kernel, out_shape=results, in_specs=specs, out_specs=[pl.B...  17.6 us
    unnamed x16, local copies, waits for them, and re-layouts  4.57 us
  transfers between devices with their start and end apart: 24, of which 14 were waited for; matrix products, arithmetic and copies ran while one was open for 0% of the time, Pallas kernels for 17%

profile of v7, /device:TPU:0, one launch (start us, length us, event | category | flops | bytes accessed | tf_op | source)
XLA Modules:
  0.0 70.7 jit_solution(12435919081113516995)
XLA Ops:
  0.0 0.9 %copy-done.5 = bf16[1,1024,128]{2,1,0:T(8,128)(2,1)S(1)} copy-done((bf16[1,1024,128]{2,1,0:T(8,128)(2,1)S(1)}, bf16[1,1024,128]{2,1,0:T(8,128)(2,1)}, u32[]{:S(2)}) %copy-start.5) | copy-done | bytes 262168
  1.0 0.7 copy-done.6
  1.6 0.7 copy-done.7
  2.3 1.0 %shard_map.73 = (bf16[1024,384]{1,0:T(8,128)(2,1)S(1)}, bf16[128,1024]{1,0:T(8,128)(2,1)S(1)}, bf16[128,384]{1,0:T(8,128)(2,1)S(1)}, bf16[128,128]{1,0:T(8,128)(...) custom-call(s32[1,4,128]{2,1,0:T(4,128)S(1)} %copy-done.6, s32[1,4]{1,0:T(1,128)S(1)} %copy-done.7, ...), custom_call_target="tpu_custom_call" | custom-call | flops 100663296 | bytes 1509392 | tf_op jit(solution)/shard_map/pallas_call | solution.py:194
  3.3 6.4 %collective-permute-start = (bf16[128,128]{1,0:T(8,128)(2,1)S(1)}, bf16[128,128]{1,0:T(8,128)(2,1)S(1)}, u32[]{:S(2)}, u32[]{:S(2)}) collective-permute-start(bf16[128,128]{1,0:T(8,128)(2,1)S(1)} %get-tuple-element.67), channel_id=1, source_target_pairs={{0,31},{1,2},{2,1},{3,4},{4,3},{5,6},{6,5},{7,8},{8,7},{9,10},{10,... | collective-permute-start | bytes 98312 | tf_op jit(solution)/shard_map/ppermute | solution.py:224
  9.7 0.0 collective-permute-start.1
  10.4 0.0 copy-start.1
  10.4 1.6 %copy-done.1 = bf16[1,1024,1024]{2,1,0:T(8,128)(2,1)S(1)} copy-done((bf16[1,1024,1024]{2,1,0:T(8,128)(2,1)S(1)}, bf16[1,1024,1024]{2,1,0:T(8,128)(2,1)}, u32[]{:S(2)}) %copy-start.1) | copy-done | bytes 2097176
  12.0 0.7 copy-done.3
  12.7 2.6 %shard_map.74 = (bf16[384,1024]{1,0:T(8,128)(2,1)S(1)}, bf16[384,384]{1,0:T(8,128)(2,1)S(1)}, bf16[384,384]{1,0:T(8,128)(2,1)S(1)}, f32[8,1024]{1,0:T(8,128)S(1)...) custom-call(bf16[1024,384]{1,0:T(8,128)(2,1)S(1)} %get-tuple-element, ...), custom_call_target="tpu_custom_call" | custom-call | flops 1509949440 | bytes 5337092 | tf_op jit(solution)/shard_map/pallas_call | solution.py:194
  15.3 0.4 shard_map.75
  15.7 1.9 %collective-permute-start.3 = (bf16[128,128]{1,0:T(8,128)(2,1)S(1)}, bf16[128,128]{1,0:T(8,128)(2,1)S(1)}, u32[]{:S(2)}, u32[]{:S(2)}) collective-permute-start(bf16[128,128]{1,0:T(8,128)(2,1)S(1)} %get-tuple-element.77), channel_id=1, source_target_pairs={{0,31},{1,2},{2,1},{3,4},{4,3},{5,6},{6,5},{7,8},{8,7},{9,10},{10,... | collective-permute-start | bytes 98312 | tf_op jit(solution)/shard_map/ppermute | solution.py:224
  17.6 1.4 %collective-permute-start.5 = (bf16[128,128]{1,0:T(8,128)(2,1)S(1)}, bf16[128,128]{1,0:T(8,128)(2,1)S(1)}, u32[]{:S(2)}, u32[]{:S(2)}) collective-permute-start(bf16[128,128]{1,0:T(8,128)(2,1)S(1)} %get-tuple-element.79), channel_id=1, source_target_pairs={{0,16},{1,17},{2,18},{3,19},{4,20},{5,21},{6,22},{7,23},{8,24},{9,... | collective-permute-start | bytes 98312 | tf_op jit(solution)/shard_map/ppermute | solution.py:224
  19.0 2.7 %shard_map.76 = (f32[128,1024]{1,0:T(8,128)S(1)}, f32[128,384]{1,0:T(8,128)S(1)}, bf16[1024,384]{1,0:T(8,128)(2,1)S(1)}, bf16[384,384]{1,0:T(8,128)(2,1)S(1)}) custom-call(bf16[128,128]{1,0:T(8,128)(2,1)S(1)} %collective-permute-done.refs_0_, bf16[128,128]{1,0:T(8,128)(2,1)S(1)} %collective-permute-done.1.refs_1_, ...), custom_call_target="tpu_custom_call" | custom-call | flops 1577058304 | bytes 7585792 | tf_op jit(solution)/shard_map/pallas_call | solution.py:194
  21.7 1.1 %collective-permute-done.3.refs_0_ = bf16[128,128]{1,0:T(8,128)(2,1)S(1)} collective-permute-done((bf16[128,128]{1,0:T(8,128)(2,1)S(1)}, bf16[128,128]{1,0:T(8,128)(2,1)S(1)}, u32[]{:S(2)}, u32[]{:S(2)}) %collective-permute-start.3) | collective-permute-done | bytes 32800 | tf_op jit(solution)/shard_map/ppermute | solution.py:224
  22.8 0.2 collective-permute-done.5.refs_2_
  23.0 0.4 shard_map.77
  23.4 2.7 %collective-permute-start.6 = (bf16[128,128]{1,0:T(8,128)(2,1)S(1)}, bf16[128,128]{1,0:T(8,128)(2,1)S(1)}, u32[]{:S(2)}, u32[]{:S(2)}) collective-permute-start(bf16[128,128]{1,0:T(8,128)(2,1)S(1)} %get-tuple-element.87), channel_id=1, source_target_pairs={{0,31},{1,2},{2,1},{3,4},{4,3},{5,6},{6,5},{7,8},{8,7},{9,10},{10,... | collective-permute-start | bytes 98312 | tf_op jit(solution)/shard_map/ppermute | solution.py:224
  26.0 0.3 collective-permute-start.8
  26.3 1.0 %shard_map.78 = (f32[128,1024]{1,0:T(8,128)S(1)}, f32[128,1024]{1,0:T(8,128)S(1)}, f32[128,384]{1,0:T(8,128)S(1)}) custom-call(bf16[128,128]{1,0:T(8,128)(2,1)S(1)} %collective-permute-done.3.refs_0_, bf16[128,128]{1,0:T(8,128)(2,1)S(1)} %collective-permute-done.4.refs_1_, bf16[128,128]{1,0:T(8,128)(2,1)S(1)} %collective-permute-done.5.refs_2_, ...), custom_call_target="tpu_custom_call" | custom-call | flops 469762048 | bytes 5869568 | tf_op jit(solution)/shard_map/pallas_call | solution.py:194
  27.3 3.1 %collective-permute-done.6.refs_0_ = bf16[128,128]{1,0:T(8,128)(2,1)S(1)} collective-permute-done((bf16[128,128]{1,0:T(8,128)(2,1)S(1)}, bf16[128,128]{1,0:T(8,128)(2,1)S(1)}, u32[]{:S(2)}, u32[]{:S(2)}) %collective-permute-start.6) | collective-permute-done | bytes 32800 | tf_op jit(solution)/shard_map/ppermute | solution.py:224
  30.5 0.4 collective-permute-done.8.refs_2_
  30.8 0.4 shard_map.79
  31.3 2.4 %collective-permute-start.9 = (bf16[128,128]{1,0:T(8,128)(2,1)S(1)}, bf16[128,128]{1,0:T(8,128)(2,1)S(1)}, u32[]{:S(2)}, u32[]{:S(2)}) collective-permute-start(bf16[128,128]{1,0:T(8,128)(2,1)S(1)} %get-tuple-element.95), channel_id=1, source_target_pairs={{0,31},{1,2},{2,1},{3,4},{4,3},{5,6},{6,5},{7,8},{8,7},{9,10},{10,... | collective-permute-start | bytes 98312 | tf_op jit(solution)/shard_map/ppermute | solution.py:224
  33.7 1.3 %shard_map.80 = (f32[128,1024]{1,0:T(8,128)S(1)}, f32[128,384]{1,0:T(8,128)S(1)}) custom-call(bf16[128,128]{1,0:T(8,128)(2,1)S(1)} %collective-permute-done.6.refs_0_, bf16[128,128]{1,0:T(8,128)(2,1)S(1)} %collective-permute-done.7.refs_1_, bf16[128,128]{1,0:T(8,128)(2,1)S(1)} %collective-permute-done.8.refs_2_, ...), custom_call_target="tpu_custom_call" | custom-call | flops 469762048 | bytes 5705728 | tf_op jit(solution)/shard_map/pallas_call | solution.py:194
  34.9 3.3 %collective-permute-done.9.refs_0_ = bf16[128,128]{1,0:T(8,128)(2,1)S(1)} collective-permute-done((bf16[128,128]{1,0:T(8,128)(2,1)S(1)}, bf16[128,128]{1,0:T(8,128)(2,1)S(1)}, u32[]{:S(2)}, u32[]{:S(2)}) %collective-permute-start.9) | collective-permute-done | bytes 32800 | tf_op jit(solution)/shard_map/ppermute | solution.py:224
  38.3 0.2 collective-permute-done.11.refs_2_
  38.5 0.4 shard_map.81
  38.9 2.4 %collective-permute-start.12 = (bf16[128,128]{1,0:T(8,128)(2,1)S(1)}, bf16[128,128]{1,0:T(8,128)(2,1)S(1)}, u32[]{:S(2)}, u32[]{:S(2)}) collective-permute-start(bf16[128,128]{1,0:T(8,128)(2,1)S(1)} %get-tuple-element.103), channel_id=1, source_target_pairs={{0,31},{1,2},{2,1},{3,4},{4,3},{5,6},{6,5},{7,8},{8,7},{9,10},{10,... | collective-permute-start | bytes 98312 | tf_op jit(solution)/shard_map/ppermute | solution.py:224
  41.2 1.0 %shard_map.82 = (f32[128,1024]{1,0:T(8,128)S(1)}, f32[128,1024]{1,0:T(8,128)S(1)}, f32[128,384]{1,0:T(8,128)S(1)}) custom-call(bf16[128,128]{1,0:T(8,128)(2,1)S(1)} %collective-permute-done.9.refs_0_, bf16[128,128]{1,0:T(8,128)(2,1)S(1)} %collective-permute-done.10.refs_1_, bf16[128,128]{1,0:T(8,128)(2,1)S(1)} %collective-permute-done.11.refs_2_, ...), custom_call_target="tpu_custom_call" | custom-call | flops 469762048 | bytes 5869568 | tf_op jit(solution)/shard_map/pallas_call | solution.py:194
  42.2 3.6 %collective-permute-done.12.refs_0_ = bf16[128,128]{1,0:T(8,128)(2,1)S(1)} collective-permute-done((bf16[128,128]{1,0:T(8,128)(2,1)S(1)}, bf16[128,128]{1,0:T(8,128)(2,1)S(1)}, u32[]{:S(2)}, u32[]{:S(2)}) %collective-permute-start.12) | collective-permute-done | bytes 32800 | tf_op jit(solution)/shard_map/ppermute | solution.py:224
  45.9 0.2 collective-permute-done.14.refs_2_
  46.1 0.4 shard_map.83
  46.5 2.4 %collective-permute-start.15 = (bf16[128,128]{1,0:T(8,128)(2,1)S(1)}, bf16[128,128]{1,0:T(8,128)(2,1)S(1)}, u32[]{:S(2)}, u32[]{:S(2)}) collective-permute-start(bf16[128,128]{1,0:T(8,128)(2,1)S(1)} %get-tuple-element.110), channel_id=1, source_target_pairs={{0,31},{1,2},{2,1},{3,4},{4,3},{5,6},{6,5},{7,8},{8,7},{9,10},{10,... | collective-permute-start | bytes 98312 | tf_op jit(solution)/shard_map/ppermute | solution.py:224
  48.8 1.3 %shard_map.84 = (f32[128,1024]{1,0:T(8,128)S(1)}, f32[128,384]{1,0:T(8,128)S(1)}) custom-call(bf16[128,128]{1,0:T(8,128)(2,1)S(1)} %collective-permute-done.12.refs_0_, bf16[128,128]{1,0:T(8,128)(2,1)S(1)} %collective-permute-done.13.refs_1_, bf16[128,128]{1,0:T(8,128)(2,1)S(1)} %collective-permute-done.14.refs_2_, ...), custom_call_target="tpu_custom_call" | custom-call | flops 469762048 | bytes 5705728 | tf_op jit(solution)/shard_map/pallas_call | solution.py:194
  50.1 3.4 %collective-permute-done.15.refs_0_ = bf16[128,128]{1,0:T(8,128)(2,1)S(1)} collective-permute-done((bf16[128,128]{1,0:T(8,128)(2,1)S(1)}, bf16[128,128]{1,0:T(8,128)(2,1)S(1)}, u32[]{:S(2)}, u32[]{:S(2)}) %collective-permute-start.15) | collective-permute-done | bytes 32800 | tf_op jit(solution)/shard_map/ppermute | solution.py:224
  53.5 0.2 collective-permute-done.17.refs_2_
  53.6 0.4 shard_map.85
  54.1 2.4 %collective-permute-start.18 = (bf16[128,128]{1,0:T(8,128)(2,1)S(1)}, bf16[128,128]{1,0:T(8,128)(2,1)S(1)}, u32[]{:S(2)}, u32[]{:S(2)}) collective-permute-start(bf16[128,128]{1,0:T(8,128)(2,1)S(1)} %get-tuple-element.117), channel_id=1, source_target_pairs={{0,31},{1,2},{2,1},{3,4},{4,3},{5,6},{6,5},{7,8},{8,7},{9,10},{10,... | collective-permute-start | bytes 98312 | tf_op jit(solution)/shard_map/ppermute | solution.py:224
  56.4 1.0 %shard_map.86 = (f32[128,1024]{1,0:T(8,128)S(1)}, f32[128,1024]{1,0:T(8,128)S(1)}, f32[128,384]{1,0:T(8,128)S(1)}) custom-call(bf16[128,128]{1,0:T(8,128)(2,1)S(1)} %collective-permute-done.15.refs_0_, bf16[128,128]{1,0:T(8,128)(2,1)S(1)} %collective-permute-done.16.refs_1_, bf16[128,128]{1,0:T(8,128)(2,1)S(1)} %collective-permute-done.17.refs_2_, ...), custom_call_target="tpu_custom_call" | custom-call | flops 469762048 | bytes 5869568 | tf_op jit(solution)/shard_map/pallas_call | solution.py:194
  57.4 3.6 %collective-permute-done.18.refs_0_ = bf16[128,128]{1,0:T(8,128)(2,1)S(1)} collective-permute-done((bf16[128,128]{1,0:T(8,128)(2,1)S(1)}, bf16[128,128]{1,0:T(8,128)(2,1)S(1)}, u32[]{:S(2)}, u32[]{:S(2)}) %collective-permute-start.18) | collective-permute-done | bytes 32800 | tf_op jit(solution)/shard_map/ppermute | solution.py:224
  61.1 0.2 collective-permute-done.20.refs_2_
  61.2 1.1 %shard_map.87 = (f32[128,384]{1,0:T(8,128)}, bf16[128,128]{1,0:T(8,128)(2,1)S(1)}, bf16[128,128]{1,0:T(8,128)(2,1)S(1)}, bf16[128,128]{1,0:T(8,128)(2,1)S(1)}) custom-call(bf16[128,128]{1,0:T(8,128)(2,1)S(1)} %collective-permute-done.18.refs_0_, bf16[128,128]{1,0:T(8,128)(2,1)S(1)} %collective-permute-done.19.refs_1_, ...), custom_call_target="tpu_custom_call" | custom-call | flops 75497472 | bytes 1585152 | tf_op jit(solution)/shard_map/pallas_call | solution.py:194
  62.3 2.3 %collective-permute-start.21 = (bf16[128,128]{1,0:T(8,128)(2,1)S(1)}, bf16[128,128]{1,0:T(8,128)(2,1)S(1)}, u32[]{:S(2)}, u32[]{:S(2)}) collective-permute-start(bf16[128,128]{1,0:T(8,128)(2,1)S(1)} %get-tuple-element.124), channel_id=1, source_target_pairs={{0,31},{1,2},{2,1},{3,4},{4,3},{5,6},{6,5},{7,8},{8,7},{9,10},{10,... | collective-permute-start | bytes 98312 | tf_op jit(solution)/shard_map/ppermute | solution.py:224
  64.6 1.1 %shard_map.88.refs_4_ = f32[128,1024]{1,0:T(8,128)S(1)} custom-call(bf16[128,128]{1,0:T(8,128)(2,1)S(1)} %collective-permute-done.18.refs_0_, bf16[128,128]{1,0:T(8,128)(2,1)S(1)} %collective-permute-done.19.refs_1_, bf16[128,128]{1,0:T(8,128)(2,1)S(1)} %collective-permute-done.20.refs_2_, bf16[1024,384]{1,0:T(8,128)(2,1)S(1)} %get-tuple-element.70.hot_ref.refs_3_, ...), custom_call_target="tpu_custom_call" | custom-call | flops 369098752 | bytes 4591616 | tf_op jit(solution)/shard_map/pallas_call | solution.py:194
  65.7 3.6 %collective-permute-done.21.refs_0_ = bf16[128,128]{1,0:T(8,128)(2,1)S(1)} collective-permute-done((bf16[128,128]{1,0:T(8,128)(2,1)S(1)}, bf16[128,128]{1,0:T(8,128)(2,1)S(1)}, u32[]{:S(2)}, u32[]{:S(2)}) %collective-permute-start.21) | collective-permute-done | bytes 32800 | tf_op jit(solution)/shard_map/ppermute | solution.py:224
  69.3 0.2 collective-permute-done.23.refs_2_
  69.4 1.3 %shard_map.89 = f32[1,1024,128]{2,1,0:T(8,128)} custom-call(bf16[128,128]{1,0:T(8,128)(2,1)S(1)} %collective-permute-done.21.refs_0_, bf16[128,128]{1,0:T(8,128)(2,1)S(1)} %collective-permute-done.22.refs_1_, bf16[128,128]{1,0:T(8,128)(2,1)S(1)} %collective-permute-done.23.refs_2_, bf16[1024,384]{1,0:T(8,128)(2,1)S(1)} %get-tuple-element.70.hot_ref.refs_3_, ...), custom_call_target="tpu_custom_call" | custom-call | flops 100663296 | bytes 1933312 | tf_op jit(solution)/shard_map/pallas_call | solution.py:194
  (33 shorter events, 0.1 us)
Async XLA Ops:
  0.0 0.9 %copy-start.5 = (bf16[1,1024,128]{2,1,0:T(8,128)(2,1)S(1)}, bf16[1,1024,128]{2,1,0:T(8,128)(2,1)}, u32[]{:S(2)}) copy-start(bf16[1,1024,128]{2,1,0:T(8,128)(2,1)} %rhs_ref.1) | copy-start | bytes 786436
  1.0 0.7 copy-start.6
  1.6 0.7 copy-start.7
  3.3 11.9 %collective-permute-start = (bf16[128,128]{1,0:T(8,128)(2,1)S(1)}, bf16[128,128]{1,0:T(8,128)(2,1)S(1)}, u32[]{:S(2)}, u32[]{:S(2)}) collective-permute-start(bf16[128,128]{1,0:T(8,128)(2,1)S(1)} %get-tuple-element.67), channel_id=1, source_target_pairs={{0,31},{1,2},{2,1},{3,4},{4,3},{5,6},{6,5},{7,8},{8,7},{9,10},{10,... | collective-permute-start | bytes 98312 | tf_op jit(solution)/shard_map/ppermute | solution.py:224
  9.7 5.5 %collective-permute-start.1 = (bf16[128,128]{1,0:T(8,128)(2,1)S(1)}, bf16[128,128]{1,0:T(8,128)(2,1)S(1)}, u32[]{:S(2)}, u32[]{:S(2)}) collective-permute-start(bf16[128,128]{1,0:T(8,128)(2,1)S(1)} %get-tuple-element.68), channel_id=1, source_target_pairs={{0,1},{1,0},{2,3},{3,2},{4,5},{5,4},{6,7},{7,6},{8,9},{9,8},{10,11... | collective-permute-start | bytes 98312 | tf_op jit(solution)/shard_map/ppermute | solution.py:224
  9.7 5.5 %collective-permute-start.2 = (bf16[128,128]{1,0:T(8,128)(2,1)S(1)}, bf16[128,128]{1,0:T(8,128)(2,1)S(1)}, u32[]{:S(2)}, u32[]{:S(2)}) collective-permute-start(bf16[128,128]{1,0:T(8,128)(2,1)S(1)} %get-tuple-element.69), channel_id=1, source_target_pairs={{0,16},{1,17},{2,18},{3,19},{4,20},{5,21},{6,22},{7,23},{8,24},{9,... | collective-permute-start | bytes 98312 | tf_op jit(solution)/shard_map/ppermute | solution.py:224
  10.4 1.6 %copy-start.1 = (bf16[1,1024,1024]{2,1,0:T(8,128)(2,1)S(1)}, bf16[1,1024,1024]{2,1,0:T(8,128)(2,1)}, u32[]{:S(2)}) copy-start(bf16[1,1024,1024]{2,1,0:T(8,128)(2,1)} %refs_4_.13) | copy-start | bytes 6291460
  12.0 0.7 copy-start.3
  12.7 6.3 %copy-start = (bf16[1,1024,1024]{2,1,0:T(8,128)(2,1)S(1)}, bf16[1,1024,1024]{2,1,0:T(8,128)(2,1)}, u32[]{:S(2)}) copy-start(bf16[1,1024,1024]{2,1,0:T(8,128)(2,1)} %refs_4_.12) | copy-start | bytes 6291460
  12.7 6.3 %copy-start.2 = (bf16[1,1024,1024]{2,1,0:T(8,128)(2,1)S(1)}, bf16[1,1024,1024]{2,1,0:T(8,128)(2,1)}, u32[]{:S(2)}) copy-start(bf16[1,1024,1024]{2,1,0:T(8,128)(2,1)} %refs_4_.13) | copy-start | bytes 6291460
  15.7 7.1 %collective-permute-start.3 = (bf16[128,128]{1,0:T(8,128)(2,1)S(1)}, bf16[128,128]{1,0:T(8,128)(2,1)S(1)}, u32[]{:S(2)}, u32[]{:S(2)}) collective-permute-start(bf16[128,128]{1,0:T(8,128)(2,1)S(1)} %get-tuple-element.77), channel_id=1, source_target_pairs={{0,31},{1,2},{2,1},{3,4},{4,3},{5,6},{6,5},{7,8},{8,7},{9,10},{10,... | collective-permute-start | bytes 98312 | tf_op jit(solution)/shard_map/ppermute | solution.py:224
  17.6 5.2 %collective-permute-start.4 = (bf16[128,128]{1,0:T(8,128)(2,1)S(1)}, bf16[128,128]{1,0:T(8,128)(2,1)S(1)}, u32[]{:S(2)}, u32[]{:S(2)}) collective-permute-start(bf16[128,128]{1,0:T(8,128)(2,1)S(1)} %get-tuple-element.78), channel_id=1, source_target_pairs={{0,1},{1,0},{2,3},{3,2},{4,5},{5,4},{6,7},{7,6},{8,9},{9,8},{10,11... | collective-permute-start | bytes 98312 | tf_op jit(solution)/shard_map/ppermute | solution.py:224
  17.6 5.4 %collective-permute-start.5 = (bf16[128,128]{1,0:T(8,128)(2,1)S(1)}, bf16[128,128]{1,0:T(8,128)(2,1)S(1)}, u32[]{:S(2)}, u32[]{:S(2)}) collective-permute-start(bf16[128,128]{1,0:T(8,128)(2,1)S(1)} %get-tuple-element.79), channel_id=1, source_target_pairs={{0,16},{1,17},{2,18},{3,19},{4,20},{5,21},{6,22},{7,23},{8,24},{9,... | collective-permute-start | bytes 98312 | tf_op jit(solution)/shard_map/ppermute | solution.py:224
  23.4 7.1 %collective-permute-start.6 = (bf16[128,128]{1,0:T(8,128)(2,1)S(1)}, bf16[128,128]{1,0:T(8,128)(2,1)S(1)}, u32[]{:S(2)}, u32[]{:S(2)}) collective-permute-start(bf16[128,128]{1,0:T(8,128)(2,1)S(1)} %get-tuple-element.87), channel_id=1, source_target_pairs={{0,31},{1,2},{2,1},{3,4},{4,3},{5,6},{6,5},{7,8},{8,7},{9,10},{10,... | collective-permute-start | bytes 98312 | tf_op jit(solution)/shard_map/ppermute | solution.py:224
  26.0 4.4 %collective-permute-start.7 = (bf16[128,128]{1,0:T(8,128)(2,1)S(1)}, bf16[128,128]{1,0:T(8,128)(2,1)S(1)}, u32[]{:S(2)}, u32[]{:S(2)}) collective-permute-start(bf16[128,128]{1,0:T(8,128)(2,1)S(1)} %get-tuple-element.88), channel_id=1, source_target_pairs={{0,1},{1,0},{2,3},{3,2},{4,5},{5,4},{6,7},{7,6},{8,9},{9,8},{10,11... | collective-permute-start | bytes 98312 | tf_op jit(solution)/shard_map/ppermute | solution.py:224
  26.0 4.8 %collective-permute-start.8 = (bf16[128,128]{1,0:T(8,128)(2,1)S(1)}, bf16[128,128]{1,0:T(8,128)(2,1)S(1)}, u32[]{:S(2)}, u32[]{:S(2)}) collective-permute-start(bf16[128,128]{1,0:T(8,128)(2,1)S(1)} %get-tuple-element.89), channel_id=1, source_target_pairs={{0,16},{1,17},{2,18},{3,19},{4,20},{5,21},{6,22},{7,23},{8,24},{9,... | collective-permute-start | bytes 98312 | tf_op jit(solution)/shard_map/ppermute | solution.py:224
  26.3 7.3 %copy-start.4 = (f32[1,1024]{1,0:T(1,128)S(1)}, f32[1,1024]{1,0:T(1,128)}, u32[]{:S(2)}) copy-start(f32[1,1024]{1,0:T(1,128)} %refs_5_.7) | copy-start | bytes 12292
  31.3 7.0 %collective-permute-start.9 = (bf16[128,128]{1,0:T(8,128)(2,1)S(1)}, bf16[128,128]{1,0:T(8,128)(2,1)S(1)}, u32[]{:S(2)}, u32[]{:S(2)}) collective-permute-start(bf16[128,128]{1,0:T(8,128)(2,1)S(1)} %get-tuple-element.95), channel_id=1, source_target_pairs={{0,31},{1,2},{2,1},{3,4},{4,3},{5,6},{6,5},{7,8},{8,7},{9,10},{10,... | collective-permute-start | bytes 98312 | tf_op jit(solution)/shard_map/ppermute | solution.py:224
  33.6 4.6 %collective-permute-start.10 = (bf16[128,128]{1,0:T(8,128)(2,1)S(1)}, bf16[128,128]{1,0:T(8,128)(2,1)S(1)}, u32[]{:S(2)}, u32[]{:S(2)}) collective-permute-start(bf16[128,128]{1,0:T(8,128)(2,1)S(1)} %get-tuple-element.96), channel_id=1, source_target_pairs={{0,1},{1,0},{2,3},{3,2},{4,5},{5,4},{6,7},{7,6},{8,9},{9,8},{10,11... | collective-permute-start | bytes 98312 | tf_op jit(solution)/shard_map/ppermute | solution.py:224
  33.7 4.8 %collective-permute-start.11 = (bf16[128,128]{1,0:T(8,128)(2,1)S(1)}, bf16[128,128]{1,0:T(8,128)(2,1)S(1)}, u32[]{:S(2)}, u32[]{:S(2)}) collective-permute-start(bf16[128,128]{1,0:T(8,128)(2,1)S(1)} %get-tuple-element.97), channel_id=1, source_target_pairs={{0,16},{1,17},{2,18},{3,19},{4,20},{5,21},{6,22},{7,23},{8,24},{9,... | collective-permute-start | bytes 98312 | tf_op jit(solution)/shard_map/ppermute | solution.py:224
  38.9 7.0 %collective-permute-start.12 = (bf16[128,128]{1,0:T(8,128)(2,1)S(1)}, bf16[128,128]{1,0:T(8,128)(2,1)S(1)}, u32[]{:S(2)}, u32[]{:S(2)}) collective-permute-start(bf16[128,128]{1,0:T(8,128)(2,1)S(1)} %get-tuple-element.103), channel_id=1, source_target_pairs={{0,31},{1,2},{2,1},{3,4},{4,3},{5,6},{6,5},{7,8},{8,7},{9,10},{10,... | collective-permute-start | bytes 98312 | tf_op jit(solution)/shard_map/ppermute | solution.py:224
  41.2 4.6 %collective-permute-start.13 = (bf16[128,128]{1,0:T(8,128)(2,1)S(1)}, bf16[128,128]{1,0:T(8,128)(2,1)S(1)}, u32[]{:S(2)}, u32[]{:S(2)}) collective-permute-start(bf16[128,128]{1,0:T(8,128)(2,1)S(1)} %get-tuple-element.104), channel_id=1, source_target_pairs={{0,1},{1,0},{2,3},{3,2},{4,5},{5,4},{6,7},{7,6},{8,9},{9,8},{10,11... | collective-permute-start | bytes 98312 | tf_op jit(solution)/shard_map/ppermute | solution.py:224
  41.2 4.8 %collective-permute-start.14 = (bf16[128,128]{1,0:T(8,128)(2,1)S(1)}, bf16[128,128]{1,0:T(8,128)(2,1)S(1)}, u32[]{:S(2)}, u32[]{:S(2)}) collective-permute-start(bf16[128,128]{1,0:T(8,128)(2,1)S(1)} %get-tuple-element.105), channel_id=1, source_target_pairs={{0,16},{1,17},{2,18},{3,19},{4,20},{5,21},{6,22},{7,23},{8,24},{9,... | collective-permute-start | bytes 98312 | tf_op jit(solution)/shard_map/ppermute | solution.py:224
  46.5 7.0 %collective-permute-start.15 = (bf16[128,128]{1,0:T(8,128)(2,1)S(1)}, bf16[128,128]{1,0:T(8,128)(2,1)S(1)}, u32[]{:S(2)}, u32[]{:S(2)}) collective-permute-start(bf16[128,128]{1,0:T(8,128)(2,1)S(1)} %get-tuple-element.110), channel_id=1, source_target_pairs={{0,31},{1,2},{2,1},{3,4},{4,3},{5,6},{6,5},{7,8},{8,7},{9,10},{10,... | collective-permute-start | bytes 98312 | tf_op jit(solution)/shard_map/ppermute | solution.py:224
  48.8 4.6 %collective-permute-start.16 = (bf16[128,128]{1,0:T(8,128)(2,1)S(1)}, bf16[128,128]{1,0:T(8,128)(2,1)S(1)}, u32[]{:S(2)}, u32[]{:S(2)}) collective-permute-start(bf16[128,128]{1,0:T(8,128)(2,1)S(1)} %get-tuple-element.111), channel_id=1, source_target_pairs={{0,1},{1,0},{2,3},{3,2},{4,5},{5,4},{6,7},{7,6},{8,9},{9,8},{10,11... | collective-permute-start | bytes 98312 | tf_op jit(solution)/shard_map/ppermute | solution.py:224
  48.8 4.8 %collective-permute-start.17 = (bf16[128,128]{1,0:T(8,128)(2,1)S(1)}, bf16[128,128]{1,0:T(8,128)(2,1)S(1)}, u32[]{:S(2)}, u32[]{:S(2)}) collective-permute-start(bf16[128,128]{1,0:T(8,128)(2,1)S(1)} %get-tuple-element.112), channel_id=1, source_target_pairs={{0,16},{1,17},{2,18},{3,19},{4,20},{5,21},{6,22},{7,23},{8,24},{9,... | collective-permute-start | bytes 98312 | tf_op jit(solution)/shard_map/ppermute | solution.py:224
  54.1 7.0 %collective-permute-start.18 = (bf16[128,128]{1,0:T(8,128)(2,1)S(1)}, bf16[128,128]{1,0:T(8,128)(2,1)S(1)}, u32[]{:S(2)}, u32[]{:S(2)}) collective-permute-start(bf16[128,128]{1,0:T(8,128)(2,1)S(1)} %get-tuple-element.117), channel_id=1, source_target_pairs={{0,31},{1,2},{2,1},{3,4},{4,3},{5,6},{6,5},{7,8},{8,7},{9,10},{10,... | collective-permute-start | bytes 98312 | tf_op jit(solution)/shard_map/ppermute | solution.py:224
  56.4 4.6 %collective-permute-start.19 = (bf16[128,128]{1,0:T(8,128)(2,1)S(1)}, bf16[128,128]{1,0:T(8,128)(2,1)S(1)}, u32[]{:S(2)}, u32[]{:S(2)}) collective-permute-start(bf16[128,128]{1,0:T(8,128)(2,1)S(1)} %get-tuple-element.118), channel_id=1, source_target_pairs={{0,1},{1,0},{2,3},{3,2},{4,5},{5,4},{6,7},{7,6},{8,9},{9,8},{10,11... | collective-permute-start | bytes 98312 | tf_op jit(solution)/shard_map/ppermute | solution.py:224
  56.4 4.8 %collective-permute-start.20 = (bf16[128,128]{1,0:T(8,128)(2,1)S(1)}, bf16[128,128]{1,0:T(8,128)(2,1)S(1)}, u32[]{:S(2)}, u32[]{:S(2)}) collective-permute-start(bf16[128,128]{1,0:T(8,128)(2,1)S(1)} %get-tuple-element.119), channel_id=1, source_target_pairs={{0,16},{1,17},{2,18},{3,19},{4,20},{5,21},{6,22},{7,23},{8,24},{9,... | collective-permute-start | bytes 98312 | tf_op jit(solution)/shard_map/ppermute | solution.py:224
  62.3 6.9 %collective-permute-start.21 = (bf16[128,128]{1,0:T(8,128)(2,1)S(1)}, bf16[128,128]{1,0:T(8,128)(2,1)S(1)}, u32[]{:S(2)}, u32[]{:S(2)}) collective-permute-start(bf16[128,128]{1,0:T(8,128)(2,1)S(1)} %get-tuple-element.124), channel_id=1, source_target_pairs={{0,31},{1,2},{2,1},{3,4},{4,3},{5,6},{6,5},{7,8},{8,7},{9,10},{10,... | collective-permute-start | bytes 98312 | tf_op jit(solution)/shard_map/ppermute | solution.py:224
  64.6 4.6 %collective-permute-start.22 = (bf16[128,128]{1,0:T(8,128)(2,1)S(1)}, bf16[128,128]{1,0:T(8,128)(2,1)S(1)}, u32[]{:S(2)}, u32[]{:S(2)}) collective-permute-start(bf16[128,128]{1,0:T(8,128)(2,1)S(1)} %get-tuple-element.125), channel_id=1, source_target_pairs={{0,1},{1,0},{2,3},{3,2},{4,5},{5,4},{6,7},{7,6},{8,9},{9,8},{10,11... | collective-permute-start | bytes 98312 | tf_op jit(solution)/shard_map/ppermute | solution.py:224
  64.6 4.8 %collective-permute-start.23 = (bf16[128,128]{1,0:T(8,128)(2,1)S(1)}, bf16[128,128]{1,0:T(8,128)(2,1)S(1)}, u32[]{:S(2)}, u32[]{:S(2)}) collective-permute-start(bf16[128,128]{1,0:T(8,128)(2,1)S(1)} %get-tuple-element.126), channel_id=1, source_target_pairs={{0,16},{1,17},{2,18},{3,19},{4,20},{5,21},{6,22},{7,23},{8,24},{9,... | collective-permute-start | bytes 98312 | tf_op jit(solution)/shard_map/ppermute | solution.py:224

commit v8 on v7

--- a/solution.py
+++ b/solution.py
@@ -15,20 +15,46 @@
 BF16 = jnp.bfloat16
 
 
+TURNS = (1, 5, 9, 13)
+
+
 def swaps(count):
-    near = [(i, i ^ 1) for i in range(count)]
-    cross = [(i, (((i + 1) ^ 1) - 1) % count) for i in range(count)]
     blocks = count // FAR
-    far = [(i, i ^ FAR) for i in range(count)] if blocks > 1 else []
-    again = [(i, (((i // FAR + 1) ^ 1) - 1) % blocks * FAR + i % FAR) for i in range(count)] if blocks > 2 else []
-    return [pairs for pairs in (cross, near, far, again) if pairs]
+    near = [i ^ 1 for i in range(count)]
+    far = [i ^ FAR for i in range(count)]
+    if blocks != 2:
+        cross = [(((i + 1) ^ 1) - 1) % count for i in range(count)]
+        again = [(((i // FAR + 1) ^ 1) - 1) % blocks * FAR + i % FAR for i in range(count)]
+        pairings = [far, again, cross, near] if blocks > 2 else [cross, near]
+    else:
+        split = [[None] * count, [None] * count]
+        for i in range(1, count - 1):
+            split[cross_half(i)][i] = ((i + 1) ^ 1) - 1
+        for half in split:
+            free = [i for i in range(count) if half[i] is None]
+            alone = [i for i in free if i ^ 1 not in free]
+            mates = dict(zip(alone[::2], alone[1::2])) | dict(zip(alone[1::2], alone[::2]))
+            for i in free:
+                half[i] = mates.get(i, i ^ 1)
+        pairings = [far, *split, near]
+    return [list(enumerate(pairing)) for pairing in pairings]
+
+
+def cross_half(index):
+    edge = (index - 1) // 2 if isinstance(index, int) else lax.div(index - 1, 2)
+    half = 0
+    for turn in TURNS:
+        half = half + (edge >= turn) * 1 if isinstance(index, int) else half + jnp.where(edge >= turn, 1, 0)
+    return half % 2 if isinstance(index, int) else lax.rem(half, 2)
 
 
 def slots_of(index, count):
     odd = lax.rem(index, 2)
     block = lax.rem(lax.div(index, FAR), 2)
-    slots = [1 - odd, odd, 2 + block, 3 - block]
-    return slots[: 2 + (count // FAR > 1) + (count // FAR > 2)]
+    blocks = count // FAR
+    far = [2 + block] if blocks > 1 else []
+    again = [3 - block] if blocks > 2 else []
+    return [*far, *again, 1 - odd, odd]
 
 
 def times(a, b):
@@ -39,13 +65,19 @@
     return lax.dot_general(a, b, (((1,), (1,)), ((), ())), preferred_element_type=F32)
 
 
-def gather(refs):
-    return jnp.concatenate([ref[...] for ref in refs], 1)
-
-
-def scatter(refs, block):
+def gather(links, refs):
+    parts = [ref[...] for ref in refs]
+    if len(parts) > links:
+        half = cross_half(lax.axis_index("sub"))
+        mine = jnp.where(half == 0, parts[1].astype(F32), parts[2].astype(F32))
+        parts[1:3] = [mine.astype(BF16)]
+    return jnp.concatenate(parts, 1)
+
+
+def scatter(links, refs, block):
     share = refs[0].shape[1]
-    for k, ref in enumerate(refs):
+    columns = [0, 1, 1, 2] if len(refs) > links else range(links)
+    for k, ref in zip(columns, refs):
         ref[...] = block[:, k * share : (k + 1) * share].astype(ref.dtype)
 
 
@@ -60,9 +92,8 @@
         hot = jnp.where(place == row, 1.0, 0.0).astype(BF16)
         part = pl.ds(k * share, share)
         hot_ref[:, part] = hot
-        message = times(turned, hot).astype(BF16)
-        picked_ref[:, part] = message
-        out_refs[k][...] = message
+        picked_ref[:, part] = times(turned, hot).astype(BF16)
+    scatter(links, out_refs, picked_ref[...])
 
 
 def pick_n_kernel(
@@ -99,47 +130,47 @@
     base_ref[...] = times_t((weight * local * inner).astype(BF16), n_pick)
 
 
-def update_path_kernel(links, *refs):
-    arrived_refs, refs = refs[:links], refs[links:]
+def update_path_kernel(trips, links, *refs):
+    arrived_refs, refs = refs[:trips], refs[trips:]
     same_ref, n_small_ref, chosen_ref, local_ref, base_ref, state_ref, state_out_ref = refs[:7]
     chosen = chosen_ref[:1]
-    residual = local_ref[...].astype(F32) + times(gather(arrived_refs), same_ref[...])
+    residual = local_ref[...].astype(F32) + times(gather(links, arrived_refs), same_ref[...])
     scaled = (chosen * residual).astype(BF16)
     sent = chosen * (base_ref[...] + times_t(scaled, n_small_ref[...]))
-    scatter(refs[7:], sent)
+    scatter(links, refs[7:], sent)
     state_out_ref[...] = state_ref[...] + DAMPING * sent
 
 
-def first_update_path_kernel(links, *refs):
-    arrived_refs, refs = refs[:links], refs[links:]
+def first_update_path_kernel(trips, links, *refs):
+    arrived_refs, refs = refs[:trips], refs[trips:]
     same_ref, n_small_ref, chosen_ref, local_ref, base_ref, state_out_ref = refs[:6]
     chosen = chosen_ref[:1]
-    residual = local_ref[...].astype(F32) + times(gather(arrived_refs), same_ref[...])
+    residual = local_ref[...].astype(F32) + times(gather(links, arrived_refs), same_ref[...])
     scaled = (chosen * residual).astype(BF16)
     sent = chosen * (base_ref[...] + times_t(scaled, n_small_ref[...]))
-    scatter(refs[6:], sent)
+    scatter(links, refs[6:], sent)
     state_out_ref[...] = DAMPING * sent
 
 
-def residual_path_kernel(links, *refs):
-    arrived_refs, refs = refs[:links], refs[links:]
+def residual_path_kernel(trips, links, *refs):
+    arrived_refs, refs = refs[:trips], refs[trips:]
     same_ref, s_small_ref, base_ref, state_ref, state_out_ref, local_ref = refs[:6]
-    state = state_ref[...] + DAMPING * times(gather(arrived_refs), same_ref[...])
+    state = state_ref[...] + DAMPING * times(gather(links, arrived_refs), same_ref[...])
     state_out_ref[...] = state
     local = base_ref[...] - times(state.astype(BF16), s_small_ref[...])
     local_ref[...] = local
-    scatter(refs[6:], local)
+    scatter(links, refs[6:], local)
 
 
 def corrected(links, arrived_refs, hot_ref, n_ref, weight_ref, mask_ref, local_ref):
     weight = weight_ref[...]
-    residual = local_ref[...] + times_t(gather(arrived_refs), hot_ref[...])
+    residual = local_ref[...] + times_t(gather(links, arrived_refs), hot_ref[...])
     scaled = (weight * residual).astype(BF16)
     return mask_ref[:1] * weight * times_t(scaled, n_ref[0])
 
 
-def first_update_kernel(links, *refs):
-    arrived_refs, refs = refs[:links], refs[links:]
+def first_update_kernel(trips, links, *refs):
+    arrived_refs, refs = refs[:trips], refs[trips:]
     hot_ref, n_ref, s_ref, weight_ref, mask_ref, inner_ref, first_ref, local_ref, picked_ref = refs[:9]
     state_out_ref, base_ref, s_pick_ref, s_small_ref = refs[9:]
     state = DAMPING * corrected(links, arrived_refs, hot_ref, n_ref, weight_ref, mask_ref, local_ref)
@@ -152,8 +183,8 @@
     base_ref[...] = picked_ref[...].astype(F32) - times((state * inner_ref[:1]).astype(BF16), s_pick)
 
 
-def update_kernel(links, *refs):
-    arrived_refs, refs = refs[:links], refs[links:]
+def update_kernel(trips, links, *refs):
+    arrived_refs, refs = refs[:trips], refs[trips:]
     hot_ref, n_ref, weight_ref, mask_ref, inner_ref, local_ref, picked_ref, s_pick_ref, state_ref = refs[:9]
     state_out_ref, base_ref = refs[9:]
     state = state_ref[...] + DAMPING * corrected(links, arrived_refs, hot_ref, n_ref, weight_ref, mask_ref, local_ref)
@@ -161,28 +192,28 @@
     base_ref[...] = picked_ref[...].astype(F32) - times((state * inner_ref[:1]).astype(BF16), s_pick_ref[...])
 
 
-def last_update_kernel(links, *refs):
-    arrived_refs, refs = refs[:links], refs[links:]
+def last_update_kernel(trips, links, *refs):
+    arrived_refs, refs = refs[:trips], refs[trips:]
     hot_ref, n_ref, weight_ref, mask_ref, local_ref, state_ref, state_out_ref = refs
     state_out_ref[...] = state_ref[...] + DAMPING * corrected(
         links, arrived_refs, hot_ref, n_ref, weight_ref, mask_ref, local_ref
     )
 
 
-def residual_kernel(links, *refs):
-    arrived_refs, refs = refs[:links], refs[links:]
+def residual_kernel(trips, links, *refs):
+    arrived_refs, refs = refs[:trips], refs[trips:]
     hot_ref, s_ref, turned_ref, weight_ref, mask_ref, inner_ref, n_pick_ref, state_ref = refs[:8]
     state_out_ref, local_ref, base_ref = refs[8:]
-    state = state_ref[...] + DAMPING * times_t(gather(arrived_refs), hot_ref[...])
+    state = state_ref[...] + DAMPING * times_t(gather(links, arrived_refs), hot_ref[...])
     state_out_ref[...] = state
     local = mask_ref[:1] * (turned_ref[...].astype(F32) - times(state.astype(BF16), s_ref[0]))
     local_ref[...] = local
     base_ref[...] = times_t((weight_ref[...] * local * inner_ref[:1]).astype(BF16), n_pick_ref[...])
 
 
-def close_kernel(links, *refs):
-    arrived_refs, (hot_ref, state_ref, out_ref) = refs[:links], refs[links:]
-    state = state_ref[...] + DAMPING * times_t(gather(arrived_refs), hot_ref[...])
+def close_kernel(trips, links, *refs):
+    arrived_refs, (hot_ref, state_ref, out_ref) = refs[:trips], refs[trips:]
+    state = state_ref[...] + DAMPING * times_t(gather(links, arrived_refs), hot_ref[...])
     out_ref[0] = state.T
 
 
@@ -206,13 +237,14 @@
     share = shared_rows.shape[2]
     subs = lax.axis_size("sub")
     routes = swaps(subs)
-    links = len(routes)
+    trips = len(routes)
+    links = len(slots_of(0, subs))
     total = links * share
 
     def array(rows, columns, kind=F32):
         return jax.ShapeDtypeStruct((rows, columns), kind)
 
-    messages = [array(leads, share, BF16)] * links
+    messages = [array(leads, share, BF16)] * trips
     full, some = array(leads, width), array(leads, total)
     small = array(total, total, BF16)
     row = array(8, width)
@@ -243,14 +275,14 @@
         came = arrived
         if step == 0:
             near_state, *sent = run(
-                functools.partial(first_update_path_kernel, links),
+                functools.partial(first_update_path_kernel, trips, links),
                 [*came, same, n_small, chosen, near, base],
                 [some, *messages],
                 path,
             )
         else:
             near_state, *sent = run(
-                functools.partial(update_path_kernel, links),
+                functools.partial(update_path_kernel, trips, links),
                 [*came, same, n_small, chosen, near, base, near_state],
                 [some, *messages],
                 path,
@@ -258,21 +290,21 @@
         arrived = exchange(sent)
         if step == 0:
             state, base, s_pick, s_small = run(
-                functools.partial(first_update_kernel, links),
+                functools.partial(first_update_kernel, trips, links),
                 [*came, hot, neumann, schur, weights, mask, inner, first, local, picked],
                 [full, some, array(width, total, BF16), small],
                 whole + 2 * picks + 2 * total * width * (width + total),
             )
         elif step < ITERS - 1:
             state, base = run(
-                functools.partial(update_kernel, links),
+                functools.partial(update_kernel, trips, links),
                 [*came, hot, neumann, weights, mask, inner, local, picked, s_pick, state],
                 [full, some],
                 whole + 2 * picks,
             )
         else:
             (state,) = run(
-                functools.partial(last_update_kernel, links),
+                functools.partial(last_update_kernel, trips, links),
                 [*came, hot, neumann, weights, mask, local, state],
                 [full],
                 whole + picks,
@@ -280,20 +312,20 @@
             break
         came = arrived
         near_state, near, *sent = run(
-            functools.partial(residual_path_kernel, links),
+            functools.partial(residual_path_kernel, trips, links),
             [*came, same, s_small, base, near_state],
             [some, some, *messages],
             path,
         )
         arrived = exchange(sent)
         state, local, base = run(
-            functools.partial(residual_kernel, links),
+            functools.partial(residual_kernel, trips, links),
             [*came, hot, schur, turned, weights, mask, inner, n_pick, state],
             [full, full, some],
             whole + 2 * picks,
         )
     (out,) = run(
-        functools.partial(close_kernel, links),
+        functools.partial(close_kernel, trips, links),
         [*arrived, hot, state],
         [jax.ShapeDtypeStruct((1, width, leads), F32)],
         picks,

time: 71 us -> 65.5 us (0.923)
  the two profiles are of different devices: /device:TPU:0 before, /device:TPU:8 now
where the time goes in v8:
time: 65.5 us; the launch traced here: 65.3 us
  starting transfers between devices  23.6 us (36%)
  waiting for transfers between devices  18.7 us (29%)
  Pallas kernels  17.6 us (27%)
  local copies, waits for them, and re-layouts  4.57 us (7%)
  between operations  0.86 us (1%)
    ppermute x32, starting transfers between devices, exchange(): lax.ppermute(part, 'sub', route)  23.6 us
    ppermute x32, waiting for transfers between devices, exchange(): lax.ppermute(part, 'sub', route)  18.7 us
    pallas_call x17, Pallas kernels, run(): pl.pallas_call(kernel, out_shape=results, in_specs=specs, out_specs=[pl.B...  17.6 us
    unnamed x14, local copies, waits for them, and re-layouts  4.57 us
  transfers between devices with their start and end apart: 32, of which 12 were waited for; matrix products, arithmetic and copies ran while one was open for 0% of the time, Pallas kernels for 18%

profile of v8, /device:TPU:8, one launch (start us, length us, event | category | flops | bytes accessed | tf_op | source)
XLA Modules:
  0.0 65.3 jit_solution(3287720476876634387)
XLA Ops:
  0.0 0.9 %copy-done.4 = bf16[1,1024,128]{2,1,0:T(8,128)(2,1)S(1)} copy-done((bf16[1,1024,128]{2,1,0:T(8,128)(2,1)S(1)}, bf16[1,1024,128]{2,1,0:T(8,128)(2,1)}, u32[]{:S(2)}) %copy-start.4) | copy-done | bytes 262168
  1.0 0.7 %copy-done.5 = s32[1,4,128]{2,1,0:T(4,128)S(1)} copy-done((s32[1,4,128]{2,1,0:T(4,128)S(1)}, s32[1,4,128]{2,1,0:T(4,128)}, u32[]{:S(2)}) %copy-start.5) | copy-done | bytes 2072
  1.6 0.7 %copy-done.6 = s32[1,4]{1,0:T(1,128)S(1)} copy-done((s32[1,4]{1,0:T(1,128)S(1)}, s32[1,4]{1,0:T(1,128)}, u32[]{:S(2)}) %copy-start.6) | copy-done | bytes 40
  2.3 1.0 %shard_map.73 = (bf16[1024,384]{1,0:T(8,128)(2,1)S(1)}, bf16[128,1024]{1,0:T(8,128)(2,1)S(1)}, bf16[128,384]{1,0:T(8,128)(2,1)S(1)}, bf16[128,128]{1,0:T(8,128)(...) custom-call(s32[1,4,128]{2,1,0:T(4,128)S(1)} %copy-done.5, ...), custom_call_target="tpu_custom_call" | custom-call | flops 100663296 | bytes 1542160 | tf_op jit(solution)/shard_map/pallas_call | solution.py:225
  3.3 2.7 %collective-permute-start = (bf16[128,128]{1,0:T(8,128)(2,1)S(1)}, bf16[128,128]{1,0:T(8,128)(2,1)S(1)}, u32[]{:S(2)}, u32[]{:S(2)}) collective-permute-start(bf16[128,128]{1,0:T(8,128)(2,1)S(1)} %get-tuple-element.75), channel_id=1, source_target_pairs={{0,16},{1,17},{2,18},{3,19},{4,20},{5,21},{6,22},{7,23},{8,24},{9,... | collective-permute-start | bytes 98312 | tf_op jit(solution)/shard_map/ppermute | solution.py:256
  6.0 2.4 %collective-permute-start.2 = (bf16[128,128]{1,0:T(8,128)(2,1)S(1)}, bf16[128,128]{1,0:T(8,128)(2,1)S(1)}, u32[]{:S(2)}, u32[]{:S(2)}) collective-permute-start(bf16[128,128]{1,0:T(8,128)(2,1)S(1)} %get-tuple-element.77), channel_id=1, source_target_pairs={{0,1},{1,0},{2,11},{3,4},{4,3},{5,6},{6,5},{7,8},{8,7},{9,10},{10,... | collective-permute-start | bytes 98312 | tf_op jit(solution)/shard_map/ppermute | solution.py:256
  9.1 1.6 %copy-done.1 = bf16[1,1024,1024]{2,1,0:T(8,128)(2,1)S(1)} copy-done((bf16[1,1024,1024]{2,1,0:T(8,128)(2,1)S(1)}, bf16[1,1024,1024]{2,1,0:T(8,128)(2,1)}, u32[]{:S(2)}) %copy-start.1) | copy-done | bytes 2097176
  10.7 0.7 %copy-done.3 = f32[1,1024]{1,0:T(1,128)S(1)} copy-done((f32[1,1024]{1,0:T(1,128)S(1)}, f32[1,1024]{1,0:T(1,128)}, u32[]{:S(2)}) %copy-start.3) | copy-done | bytes 4120
  11.4 2.6 %shard_map.74 = (bf16[384,1024]{1,0:T(8,128)(2,1)S(1)}, bf16[384,384]{1,0:T(8,128)(2,1)S(1)}, bf16[384,384]{1,0:T(8,128)(2,1)S(1)}, f32[8,1024]{1,0:T(8,128)S(1)...) custom-call(bf16[1024,384]{1,0:T(8,128)(2,1)S(1)} %get-tuple-element, ...), custom_call_target="tpu_custom_call" | custom-call | flops 1509949440 | bytes 5337092 | tf_op jit(solution)/shard_map/pallas_call | solution.py:225
  14.0 0.4 shard_map.75
  15.0 1.4 %collective-permute-start.6 = (bf16[128,128]{1,0:T(8,128)(2,1)S(1)}, bf16[128,128]{1,0:T(8,128)(2,1)S(1)}, u32[]{:S(2)}, u32[]{:S(2)}) collective-permute-start(bf16[128,128]{1,0:T(8,128)(2,1)S(1)} %get-tuple-element.88), channel_id=1, source_target_pairs={{0,1},{1,0},{2,11},{3,4},{4,3},{5,6},{6,5},{7,8},{8,7},{9,10},{10,... | collective-permute-start | bytes 98312 | tf_op jit(solution)/shard_map/ppermute | solution.py:256
  16.4 1.8 %collective-permute-start.7 = (bf16[128,128]{1,0:T(8,128)(2,1)S(1)}, bf16[128,128]{1,0:T(8,128)(2,1)S(1)}, u32[]{:S(2)}, u32[]{:S(2)}) collective-permute-start(bf16[128,128]{1,0:T(8,128)(2,1)S(1)} %get-tuple-element.89), channel_id=1, source_target_pairs={{0,1},{1,0},{2,3},{3,2},{4,5},{5,4},{6,7},{7,6},{8,9},{9,8},{10,11... | collective-permute-start | bytes 98312 | tf_op jit(solution)/shard_map/ppermute | solution.py:256
  18.1 2.7 %shard_map.76 = (f32[128,1024]{1,0:T(8,128)S(1)}, f32[128,384]{1,0:T(8,128)S(1)}, bf16[1024,384]{1,0:T(8,128)(2,1)S(1)}, bf16[384,384]{1,0:T(8,128)(2,1)S(1)}) custom-call(bf16[128,128]{1,0:T(8,128)(2,1)S(1)} %collective-permute-done.refs_0_, bf16[128,128]{1,0:T(8,128)(2,1)S(1)} %collective-permute-done.1.refs_1_, ...), custom_call_target="tpu_custom_call" | custom-call | flops 1577058304 | bytes 7618560 | tf_op jit(solution)/shard_map/pallas_call | solution.py:225
  20.9 0.4 shard_map.77
  21.3 1.9 %collective-permute-start.8 = (bf16[128,128]{1,0:T(8,128)(2,1)S(1)}, bf16[128,128]{1,0:T(8,128)(2,1)S(1)}, u32[]{:S(2)}, u32[]{:S(2)}) collective-permute-start(bf16[128,128]{1,0:T(8,128)(2,1)S(1)} %get-tuple-element.97), channel_id=1, source_target_pairs={{0,16},{1,17},{2,18},{3,19},{4,20},{5,21},{6,22},{7,23},{8,24},{9,... | collective-permute-start | bytes 98312 | tf_op jit(solution)/shard_map/ppermute | solution.py:256
  23.2 1.7 %collective-permute-start.10 = (bf16[128,128]{1,0:T(8,128)(2,1)S(1)}, bf16[128,128]{1,0:T(8,128)(2,1)S(1)}, u32[]{:S(2)}, u32[]{:S(2)}) collective-permute-start(bf16[128,128]{1,0:T(8,128)(2,1)S(1)} %get-tuple-element.99), channel_id=1, source_target_pairs={{0,1},{1,0},{2,11},{3,4},{4,3},{5,6},{6,5},{7,8},{8,7},{9,10},{10,... | collective-permute-start | bytes 98312 | tf_op jit(solution)/shard_map/ppermute | solution.py:256
  24.9 1.0 %shard_map.78 = (f32[128,1024]{1,0:T(8,128)S(1)}, f32[128,1024]{1,0:T(8,128)S(1)}, f32[128,384]{1,0:T(8,128)S(1)}) custom-call(bf16[128,128]{1,0:T(8,128)(2,1)S(1)} %collective-permute-done.4.refs_0_, bf16[128,128]{1,0:T(8,128)(2,1)S(1)} %collective-permute-done.5.refs_1_, bf16[128,128]{1,0:T(8,128)(2,1)S(1)} %collective-permute-done.6.refs_2_, ...), custom_call_target="tpu_custom_call" | custom-call | flops 469762048 | bytes 5902336 | tf_op jit(solution)/shard_map/pallas_call | solution.py:225
  25.9 0.4 collective-permute-done.8.refs_0_
  26.3 2.1 %collective-permute-done.10.refs_2_ = bf16[128,128]{1,0:T(8,128)(2,1)S(1)} collective-permute-done((bf16[128,128]{1,0:T(8,128)(2,1)S(1)}, bf16[128,128]{1,0:T(8,128)(2,1)S(1)}, u32[]{:S(2)}, u32[]{:S(2)}) %collective-permute-start.10) | collective-permute-done | bytes 32800 | tf_op jit(solution)/shard_map/ppermute | solution.py:256
  28.4 0.4 shard_map.79
  28.8 1.2 %collective-permute-start.12 = (bf16[128,128]{1,0:T(8,128)(2,1)S(1)}, bf16[128,128]{1,0:T(8,128)(2,1)S(1)}, u32[]{:S(2)}, u32[]{:S(2)}) collective-permute-start(bf16[128,128]{1,0:T(8,128)(2,1)S(1)} %get-tuple-element.106), channel_id=1, source_target_pairs={{0,16},{1,17},{2,18},{3,19},{4,20},{5,21},{6,22},{7,23},{8,24},{9,... | collective-permute-start | bytes 98312 | tf_op jit(solution)/shard_map/ppermute | solution.py:256
  29.9 0.9 %collective-permute-start.14 = (bf16[128,128]{1,0:T(8,128)(2,1)S(1)}, bf16[128,128]{1,0:T(8,128)(2,1)S(1)}, u32[]{:S(2)}, u32[]{:S(2)}) collective-permute-start(bf16[128,128]{1,0:T(8,128)(2,1)S(1)} %get-tuple-element.108), channel_id=1, source_target_pairs={{0,1},{1,0},{2,11},{3,4},{4,3},{5,6},{6,5},{7,8},{8,7},{9,10},{10,... | collective-permute-start | bytes 98312 | tf_op jit(solution)/shard_map/ppermute | solution.py:256
  30.8 1.3 %shard_map.80 = (f32[128,1024]{1,0:T(8,128)S(1)}, f32[128,384]{1,0:T(8,128)S(1)}) custom-call(bf16[128,128]{1,0:T(8,128)(2,1)S(1)} %collective-permute-done.8.refs_0_, bf16[128,128]{1,0:T(8,128)(2,1)S(1)} %collective-permute-done.9.refs_1_, bf16[128,128]{1,0:T(8,128)(2,1)S(1)} %collective-permute-done.10.refs_2_, ...), custom_call_target="tpu_custom_call" | custom-call | flops 469762048 | bytes 5738496 | tf_op jit(solution)/shard_map/pallas_call | solution.py:225
  32.1 1.6 %collective-permute-done.12.refs_0_ = bf16[128,128]{1,0:T(8,128)(2,1)S(1)} collective-permute-done((bf16[128,128]{1,0:T(8,128)(2,1)S(1)}, bf16[128,128]{1,0:T(8,128)(2,1)S(1)}, u32[]{:S(2)}, u32[]{:S(2)}) %collective-permute-start.12) | collective-permute-done | bytes 32800 | tf_op jit(solution)/shard_map/ppermute | solution.py:256
  33.6 1.4 %collective-permute-done.14.refs_2_ = bf16[128,128]{1,0:T(8,128)(2,1)S(1)} collective-permute-done((bf16[128,128]{1,0:T(8,128)(2,1)S(1)}, bf16[128,128]{1,0:T(8,128)(2,1)S(1)}, u32[]{:S(2)}, u32[]{:S(2)}) %collective-permute-start.14) | collective-permute-done | bytes 32800 | tf_op jit(solution)/shard_map/ppermute | solution.py:256
  35.5 1.9 %collective-permute-start.16 = (bf16[128,128]{1,0:T(8,128)(2,1)S(1)}, bf16[128,128]{1,0:T(8,128)(2,1)S(1)}, u32[]{:S(2)}, u32[]{:S(2)}) collective-permute-start(bf16[128,128]{1,0:T(8,128)(2,1)S(1)} %get-tuple-element.115), channel_id=1, source_target_pairs={{0,16},{1,17},{2,18},{3,19},{4,20},{5,21},{6,22},{7,23},{8,24},{9,... | collective-permute-start | bytes 98312 | tf_op jit(solution)/shard_map/ppermute | solution.py:256
  37.4 1.1 %collective-permute-start.18 = (bf16[128,128]{1,0:T(8,128)(2,1)S(1)}, bf16[128,128]{1,0:T(8,128)(2,1)S(1)}, u32[]{:S(2)}, u32[]{:S(2)}) collective-permute-start(bf16[128,128]{1,0:T(8,128)(2,1)S(1)} %get-tuple-element.117), channel_id=1, source_target_pairs={{0,1},{1,0},{2,11},{3,4},{4,3},{5,6},{6,5},{7,8},{8,7},{9,10},{10,... | collective-permute-start | bytes 98312 | tf_op jit(solution)/shard_map/ppermute | solution.py:256
  38.5 1.0 %shard_map.82 = (f32[128,1024]{1,0:T(8,128)S(1)}, f32[128,1024]{1,0:T(8,128)S(1)}, f32[128,384]{1,0:T(8,128)S(1)}) custom-call(bf16[128,128]{1,0:T(8,128)(2,1)S(1)} %collective-permute-done.12.refs_0_, bf16[128,128]{1,0:T(8,128)(2,1)S(1)} %collective-permute-done.13.refs_1_, bf16[128,128]{1,0:T(8,128)(2,1)S(1)} %collective-permute-done.14.refs_2_, ...), custom_call_target="tpu_custom_call" | custom-call | flops 469762048 | bytes 5902336 | tf_op jit(solution)/shard_map/pallas_call | solution.py:225
  39.5 0.9 %collective-permute-done.16.refs_0_ = bf16[128,128]{1,0:T(8,128)(2,1)S(1)} collective-permute-done((bf16[128,128]{1,0:T(8,128)(2,1)S(1)}, bf16[128,128]{1,0:T(8,128)(2,1)S(1)}, u32[]{:S(2)}, u32[]{:S(2)}) %collective-permute-start.16) | collective-permute-done | bytes 32800 | tf_op jit(solution)/shard_map/ppermute | solution.py:256
  40.3 2.2 %collective-permute-done.18.refs_2_ = bf16[128,128]{1,0:T(8,128)(2,1)S(1)} collective-permute-done((bf16[128,128]{1,0:T(8,128)(2,1)S(1)}, bf16[128,128]{1,0:T(8,128)(2,1)S(1)}, u32[]{:S(2)}, u32[]{:S(2)}) %collective-permute-start.18) | collective-permute-done | bytes 32800 | tf_op jit(solution)/shard_map/ppermute | solution.py:256
  42.9 1.2 %collective-permute-start.20 = (bf16[128,128]{1,0:T(8,128)(2,1)S(1)}, bf16[128,128]{1,0:T(8,128)(2,1)S(1)}, u32[]{:S(2)}, u32[]{:S(2)}) collective-permute-start(bf16[128,128]{1,0:T(8,128)(2,1)S(1)} %get-tuple-element.123), channel_id=1, source_target_pairs={{0,16},{1,17},{2,18},{3,19},{4,20},{5,21},{6,22},{7,23},{8,24},{9,... | collective-permute-start | bytes 98312 | tf_op jit(solution)/shard_map/ppermute | solution.py:256
  44.1 0.5 collective-permute-start.22
  44.6 1.3 %shard_map.84 = (f32[128,1024]{1,0:T(8,128)S(1)}, f32[128,384]{1,0:T(8,128)S(1)}) custom-call(bf16[128,128]{1,0:T(8,128)(2,1)S(1)} %collective-permute-done.16.refs_0_, bf16[128,128]{1,0:T(8,128)(2,1)S(1)} %collective-permute-done.17.refs_1_, bf16[128,128]{1,0:T(8,128)(2,1)S(1)} %collective-permute-done.18.refs_2_, ...), custom_call_target="tpu_custom_call" | custom-call | flops 469762048 | bytes 5738496 | tf_op jit(solution)/shard_map/pallas_call | solution.py:225
  45.9 1.9 %collective-permute-done.20.refs_0_ = bf16[128,128]{1,0:T(8,128)(2,1)S(1)} collective-permute-done((bf16[128,128]{1,0:T(8,128)(2,1)S(1)}, bf16[128,128]{1,0:T(8,128)(2,1)S(1)}, u32[]{:S(2)}, u32[]{:S(2)}) %collective-permute-start.20) | collective-permute-done | bytes 32800 | tf_op jit(solution)/shard_map/ppermute | solution.py:256
  47.8 1.4 %collective-permute-done.22.refs_2_ = bf16[128,128]{1,0:T(8,128)(2,1)S(1)} collective-permute-done((bf16[128,128]{1,0:T(8,128)(2,1)S(1)}, bf16[128,128]{1,0:T(8,128)(2,1)S(1)}, u32[]{:S(2)}, u32[]{:S(2)}) %collective-permute-start.22) | collective-permute-done | bytes 32800 | tf_op jit(solution)/shard_map/ppermute | solution.py:256
  49.2 0.4 shard_map.85
  49.6 1.9 %collective-permute-start.24 = (bf16[128,128]{1,0:T(8,128)(2,1)S(1)}, bf16[128,128]{1,0:T(8,128)(2,1)S(1)}, u32[]{:S(2)}, u32[]{:S(2)}) collective-permute-start(bf16[128,128]{1,0:T(8,128)(2,1)S(1)} %get-tuple-element.131), channel_id=1, source_target_pairs={{0,16},{1,17},{2,18},{3,19},{4,20},{5,21},{6,22},{7,23},{8,24},{9,... | collective-permute-start | bytes 98312 | tf_op jit(solution)/shard_map/ppermute | solution.py:256
  51.5 0.9 %collective-permute-start.26 = (bf16[128,128]{1,0:T(8,128)(2,1)S(1)}, bf16[128,128]{1,0:T(8,128)(2,1)S(1)}, u32[]{:S(2)}, u32[]{:S(2)}) collective-permute-start(bf16[128,128]{1,0:T(8,128)(2,1)S(1)} %get-tuple-element.133), channel_id=1, source_target_pairs={{0,1},{1,0},{2,11},{3,4},{4,3},{5,6},{6,5},{7,8},{8,7},{9,10},{10,... | collective-permute-start | bytes 98312 | tf_op jit(solution)/shard_map/ppermute | solution.py:256
  52.4 1.0 %shard_map.86 = (f32[128,1024]{1,0:T(8,128)S(1)}, f32[128,1024]{1,0:T(8,128)S(1)}, f32[128,384]{1,0:T(8,128)S(1)}) custom-call(bf16[128,128]{1,0:T(8,128)(2,1)S(1)} %collective-permute-done.20.refs_0_, bf16[128,128]{1,0:T(8,128)(2,1)S(1)} %collective-permute-done.21.refs_1_, bf16[128,128]{1,0:T(8,128)(2,1)S(1)} %collective-permute-done.22.refs_2_, ...), custom_call_target="tpu_custom_call" | custom-call | flops 469762048 | bytes 5902336 | tf_op jit(solution)/shard_map/pallas_call | solution.py:225
  53.4 1.1 %collective-permute-done.24.refs_0_ = bf16[128,128]{1,0:T(8,128)(2,1)S(1)} collective-permute-done((bf16[128,128]{1,0:T(8,128)(2,1)S(1)}, bf16[128,128]{1,0:T(8,128)(2,1)S(1)}, u32[]{:S(2)}, u32[]{:S(2)}) %collective-permute-start.24) | collective-permute-done | bytes 32800 | tf_op jit(solution)/shard_map/ppermute | solution.py:256
  54.5 2.2 %collective-permute-done.26.refs_2_ = bf16[128,128]{1,0:T(8,128)(2,1)S(1)} collective-permute-done((bf16[128,128]{1,0:T(8,128)(2,1)S(1)}, bf16[128,128]{1,0:T(8,128)(2,1)S(1)}, u32[]{:S(2)}, u32[]{:S(2)}) %collective-permute-start.26) | collective-permute-done | bytes 32800 | tf_op jit(solution)/shard_map/ppermute | solution.py:256
  56.7 1.1 %shard_map.87 = (f32[128,384]{1,0:T(8,128)}, bf16[128,128]{1,0:T(8,128)(2,1)S(1)}, bf16[128,128]{1,0:T(8,128)(2,1)S(1)}, bf16[128,128]{1,0:T(8,128)(2,1)S(1)}, bf16[128,128]{1,0:T(8,128)(2,1)S(1)}) custom-call(bf16[128,128]{1,0:T(8,128)(2,1)S(1)} %collective-permute-done.24.refs_0_, bf16[128,128]{1,0:T(8,128)(2,1)S(1)} %collective-permute-done.25.refs_1_, ...), custom_call_target="tpu_custom_call" | custom-call | flops 75497472 | bytes 1650688 | tf_op jit(solution)/shard_map/pallas_call | solution.py:225
  57.8 1.1 %collective-permute-start.28 = (bf16[128,128]{1,0:T(8,128)(2,1)S(1)}, bf16[128,128]{1,0:T(8,128)(2,1)S(1)}, u32[]{:S(2)}, u32[]{:S(2)}) collective-permute-start(bf16[128,128]{1,0:T(8,128)(2,1)S(1)} %get-tuple-element.139), channel_id=1, source_target_pairs={{0,16},{1,17},{2,18},{3,19},{4,20},{5,21},{6,22},{7,23},{8,24},{9,... | collective-permute-start | bytes 98312 | tf_op jit(solution)/shard_map/ppermute | solution.py:256
  58.9 0.4 collective-permute-start.31
  59.3 1.1 %shard_map.88.refs_5_ = f32[128,1024]{1,0:T(8,128)S(1)} custom-call(bf16[128,128]{1,0:T(8,128)(2,1)S(1)} %collective-permute-done.24.refs_0_, bf16[128,128]{1,0:T(8,128)(2,1)S(1)} %collective-permute-done.25.refs_1_, bf16[128,128]{1,0:T(8,128)(2,1)S(1)} %collective-permute-done.26.refs_2_, bf16[128,128]{1,0:T(8,128)(2,1)S(1)} %collective-permute-done.27.refs_3_, ...), custom_call_target="tpu_custom_call" | custom-call | flops 369098752 | bytes 4624384 | tf_op jit(solution)/shard_map/pallas_call | solution.py:225
  60.4 2.1 %collective-permute-done.28.refs_0_ = bf16[128,128]{1,0:T(8,128)(2,1)S(1)} collective-permute-done((bf16[128,128]{1,0:T(8,128)(2,1)S(1)}, bf16[128,128]{1,0:T(8,128)(2,1)S(1)}, u32[]{:S(2)}, u32[]{:S(2)}) %collective-permute-start.28) | collective-permute-done | bytes 32800 | tf_op jit(solution)/shard_map/ppermute | solution.py:256
  62.6 1.4 %collective-permute-done.30.refs_2_ = bf16[128,128]{1,0:T(8,128)(2,1)S(1)} collective-permute-done((bf16[128,128]{1,0:T(8,128)(2,1)S(1)}, bf16[128,128]{1,0:T(8,128)(2,1)S(1)}, u32[]{:S(2)}, u32[]{:S(2)}) %collective-permute-start.30) | collective-permute-done | bytes 32800 | tf_op jit(solution)/shard_map/ppermute | solution.py:256
  64.0 1.3 %shard_map.89 = f32[1,1024,128]{2,1,0:T(8,128)} custom-call(bf16[128,128]{1,0:T(8,128)(2,1)S(1)} %collective-permute-done.28.refs_0_, bf16[128,128]{1,0:T(8,128)(2,1)S(1)} %collective-permute-done.29.refs_1_, bf16[128,128]{1,0:T(8,128)(2,1)S(1)} %collective-permute-done.30.refs_2_, bf16[128,128]{1,0:T(8,128)(2,1)S(1)} %collective-permute-done.31.refs_3_, ...), custom_call_target="tpu_custom_call" | custom-call | flops 100663296 | bytes 1966080 | tf_op jit(solution)/shard_map/pallas_call | solution.py:225
  (47 shorter events, 1.6 us)
Async XLA Ops:
  0.0 0.9 %copy-start.4 = (bf16[1,1024,128]{2,1,0:T(8,128)(2,1)S(1)}, bf16[1,1024,128]{2,1,0:T(8,128)(2,1)}, u32[]{:S(2)}) copy-start(bf16[1,1024,128]{2,1,0:T(8,128)(2,1)} %rhs_ref.1) | copy-start | bytes 786436
  1.0 0.7 %copy-start.5 = (s32[1,4,128]{2,1,0:T(4,128)S(1)}, s32[1,4,128]{2,1,0:T(4,128)}, u32[]{:S(2)}) copy-start(s32[1,4,128]{2,1,0:T(4,128)} %rows_ref.1) | copy-start | bytes 6148
  1.6 0.7 %copy-start.6 = (s32[1,4]{1,0:T(1,128)S(1)}, s32[1,4]{1,0:T(1,128)}, u32[]{:S(2)}) copy-start(s32[1,4]{1,0:T(1,128)} %live_ref.1) | copy-start | bytes 52
  3.3 10.6 %collective-permute-start = (bf16[128,128]{1,0:T(8,128)(2,1)S(1)}, bf16[128,128]{1,0:T(8,128)(2,1)S(1)}, u32[]{:S(2)}, u32[]{:S(2)}) collective-permute-start(bf16[128,128]{1,0:T(8,128)(2,1)S(1)} %get-tuple-element.75), channel_id=1, source_target_pairs={{0,16},{1,17},{2,18},{3,19},{4,20},{5,21},{6,22},{7,23},{8,24},{9,... | collective-permute-start | bytes 98312 | tf_op jit(solution)/shard_map/ppermute | solution.py:256
  6.0 8.0 %collective-permute-start.1 = (bf16[128,128]{1,0:T(8,128)(2,1)S(1)}, bf16[128,128]{1,0:T(8,128)(2,1)S(1)}, u32[]{:S(2)}, u32[]{:S(2)}) collective-permute-start(bf16[128,128]{1,0:T(8,128)(2,1)S(1)} %get-tuple-element.76), channel_id=1, source_target_pairs={{0,3},{1,2},{2,1},{3,0},{4,5},{5,4},{6,7},{7,6},{8,9},{9,8},{10,19... | collective-permute-start | bytes 98312 | tf_op jit(solution)/shard_map/ppermute | solution.py:256
  6.0 8.0 %collective-permute-start.2 = (bf16[128,128]{1,0:T(8,128)(2,1)S(1)}, bf16[128,128]{1,0:T(8,128)(2,1)S(1)}, u32[]{:S(2)}, u32[]{:S(2)}) collective-permute-start(bf16[128,128]{1,0:T(8,128)(2,1)S(1)} %get-tuple-element.77), channel_id=1, source_target_pairs={{0,1},{1,0},{2,11},{3,4},{4,3},{5,6},{6,5},{7,8},{8,7},{9,10},{10,... | collective-permute-start | bytes 98312 | tf_op jit(solution)/shard_map/ppermute | solution.py:256
  8.4 5.5 %collective-permute-start.3 = (bf16[128,128]{1,0:T(8,128)(2,1)S(1)}, bf16[128,128]{1,0:T(8,128)(2,1)S(1)}, u32[]{:S(2)}, u32[]{:S(2)}) collective-permute-start(bf16[128,128]{1,0:T(8,128)(2,1)S(1)} %get-tuple-element.78), channel_id=1, source_target_pairs={{0,1},{1,0},{2,3},{3,2},{4,5},{5,4},{6,7},{7,6},{8,9},{9,8},{10,11... | collective-permute-start | bytes 98312 | tf_op jit(solution)/shard_map/ppermute | solution.py:256
  9.1 1.6 %copy-start.1 = (bf16[1,1024,1024]{2,1,0:T(8,128)(2,1)S(1)}, bf16[1,1024,1024]{2,1,0:T(8,128)(2,1)}, u32[]{:S(2)}) copy-start(bf16[1,1024,1024]{2,1,0:T(8,128)(2,1)} %refs_5_.13) | copy-start | bytes 6291460
  10.7 0.7 %copy-start.3 = (f32[1,1024]{1,0:T(1,128)S(1)}, f32[1,1024]{1,0:T(1,128)}, u32[]{:S(2)}) copy-start(f32[1,1024]{1,0:T(1,128)} %refs_6_.7) | copy-start | bytes 12292
  11.4 6.8 %copy-start = (bf16[1,1024,1024]{2,1,0:T(8,128)(2,1)S(1)}, bf16[1,1024,1024]{2,1,0:T(8,128)(2,1)}, u32[]{:S(2)}) copy-start(bf16[1,1024,1024]{2,1,0:T(8,128)(2,1)} %refs_5_.12) | copy-start | bytes 6291460
  11.4 6.8 %copy-start.2 = (bf16[1,1024,1024]{2,1,0:T(8,128)(2,1)S(1)}, bf16[1,1024,1024]{2,1,0:T(8,128)(2,1)}, u32[]{:S(2)}) copy-start(bf16[1,1024,1024]{2,1,0:T(8,128)(2,1)} %refs_5_.13) | copy-start | bytes 6291460
  14.4 6.5 %collective-permute-start.4 = (bf16[128,128]{1,0:T(8,128)(2,1)S(1)}, bf16[128,128]{1,0:T(8,128)(2,1)S(1)}, u32[]{:S(2)}, u32[]{:S(2)}) collective-permute-start(bf16[128,128]{1,0:T(8,128)(2,1)S(1)} %get-tuple-element.86), channel_id=1, source_target_pairs={{0,16},{1,17},{2,18},{3,19},{4,20},{5,21},{6,22},{7,23},{8,24},{9,... | collective-permute-start | bytes 98312 | tf_op jit(solution)/shard_map/ppermute | solution.py:256
  14.8 6.1 %collective-permute-start.5 = (bf16[128,128]{1,0:T(8,128)(2,1)S(1)}, bf16[128,128]{1,0:T(8,128)(2,1)S(1)}, u32[]{:S(2)}, u32[]{:S(2)}) collective-permute-start(bf16[128,128]{1,0:T(8,128)(2,1)S(1)} %get-tuple-element.87), channel_id=1, source_target_pairs={{0,3},{1,2},{2,1},{3,0},{4,5},{5,4},{6,7},{7,6},{8,9},{9,8},{10,19... | collective-permute-start | bytes 98312 | tf_op jit(solution)/shard_map/ppermute | solution.py:256
  15.0 5.8 %collective-permute-start.6 = (bf16[128,128]{1,0:T(8,128)(2,1)S(1)}, bf16[128,128]{1,0:T(8,128)(2,1)S(1)}, u32[]{:S(2)}, u32[]{:S(2)}) collective-permute-start(bf16[128,128]{1,0:T(8,128)(2,1)S(1)} %get-tuple-element.88), channel_id=1, source_target_pairs={{0,1},{1,0},{2,11},{3,4},{4,3},{5,6},{6,5},{7,8},{8,7},{9,10},{10,... | collective-permute-start | bytes 98312 | tf_op jit(solution)/shard_map/ppermute | solution.py:256
  16.4 4.5 %collective-permute-start.7 = (bf16[128,128]{1,0:T(8,128)(2,1)S(1)}, bf16[128,128]{1,0:T(8,128)(2,1)S(1)}, u32[]{:S(2)}, u32[]{:S(2)}) collective-permute-start(bf16[128,128]{1,0:T(8,128)(2,1)S(1)} %get-tuple-element.89), channel_id=1, source_target_pairs={{0,1},{1,0},{2,3},{3,2},{4,5},{5,4},{6,7},{7,6},{8,9},{9,8},{10,11... | collective-permute-start | bytes 98312 | tf_op jit(solution)/shard_map/ppermute | solution.py:256
  21.3 5.0 %collective-permute-start.8 = (bf16[128,128]{1,0:T(8,128)(2,1)S(1)}, bf16[128,128]{1,0:T(8,128)(2,1)S(1)}, u32[]{:S(2)}, u32[]{:S(2)}) collective-permute-start(bf16[128,128]{1,0:T(8,128)(2,1)S(1)} %get-tuple-element.97), channel_id=1, source_target_pairs={{0,16},{1,17},{2,18},{3,19},{4,20},{5,21},{6,22},{7,23},{8,24},{9,... | collective-permute-start | bytes 98312 | tf_op jit(solution)/shard_map/ppermute | solution.py:256
  23.2 3.1 %collective-permute-start.9 = (bf16[128,128]{1,0:T(8,128)(2,1)S(1)}, bf16[128,128]{1,0:T(8,128)(2,1)S(1)}, u32[]{:S(2)}, u32[]{:S(2)}) collective-permute-start(bf16[128,128]{1,0:T(8,128)(2,1)S(1)} %get-tuple-element.98), channel_id=1, source_target_pairs={{0,3},{1,2},{2,1},{3,0},{4,5},{5,4},{6,7},{7,6},{8,9},{9,8},{10,19... | collective-permute-start | bytes 98312 | tf_op jit(solution)/shard_map/ppermute | solution.py:256
  23.2 5.1 %collective-permute-start.10 = (bf16[128,128]{1,0:T(8,128)(2,1)S(1)}, bf16[128,128]{1,0:T(8,128)(2,1)S(1)}, u32[]{:S(2)}, u32[]{:S(2)}) collective-permute-start(bf16[128,128]{1,0:T(8,128)(2,1)S(1)} %get-tuple-element.99), channel_id=1, source_target_pairs={{0,1},{1,0},{2,11},{3,4},{4,3},{5,6},{6,5},{7,8},{8,7},{9,10},{10,... | collective-permute-start | bytes 98312 | tf_op jit(solution)/shard_map/ppermute | solution.py:256
  24.9 3.5 %collective-permute-start.11 = (bf16[128,128]{1,0:T(8,128)(2,1)S(1)}, bf16[128,128]{1,0:T(8,128)(2,1)S(1)}, u32[]{:S(2)}, u32[]{:S(2)}) collective-permute-start(bf16[128,128]{1,0:T(8,128)(2,1)S(1)} %get-tuple-element.100), channel_id=1, source_target_pairs={{0,1},{1,0},{2,3},{3,2},{4,5},{5,4},{6,7},{7,6},{8,9},{9,8},{10,11... | collective-permute-start | bytes 98312 | tf_op jit(solution)/shard_map/ppermute | solution.py:256
  28.8 4.9 %collective-permute-start.12 = (bf16[128,128]{1,0:T(8,128)(2,1)S(1)}, bf16[128,128]{1,0:T(8,128)(2,1)S(1)}, u32[]{:S(2)}, u32[]{:S(2)}) collective-permute-start(bf16[128,128]{1,0:T(8,128)(2,1)S(1)} %get-tuple-element.106), channel_id=1, source_target_pairs={{0,16},{1,17},{2,18},{3,19},{4,20},{5,21},{6,22},{7,23},{8,24},{9,... | collective-permute-start | bytes 98312 | tf_op jit(solution)/shard_map/ppermute | solution.py:256
  29.9 3.7 %collective-permute-start.13 = (bf16[128,128]{1,0:T(8,128)(2,1)S(1)}, bf16[128,128]{1,0:T(8,128)(2,1)S(1)}, u32[]{:S(2)}, u32[]{:S(2)}) collective-permute-start(bf16[128,128]{1,0:T(8,128)(2,1)S(1)} %get-tuple-element.107), channel_id=1, source_target_pairs={{0,3},{1,2},{2,1},{3,0},{4,5},{5,4},{6,7},{7,6},{8,9},{9,8},{10,19... | collective-permute-start | bytes 98312 | tf_op jit(solution)/shard_map/ppermute | solution.py:256
  29.9 5.1 %collective-permute-start.14 = (bf16[128,128]{1,0:T(8,128)(2,1)S(1)}, bf16[128,128]{1,0:T(8,128)(2,1)S(1)}, u32[]{:S(2)}, u32[]{:S(2)}) collective-permute-start(bf16[128,128]{1,0:T(8,128)(2,1)S(1)} %get-tuple-element.108), channel_id=1, source_target_pairs={{0,1},{1,0},{2,11},{3,4},{4,3},{5,6},{6,5},{7,8},{8,7},{9,10},{10,... | collective-permute-start | bytes 98312 | tf_op jit(solution)/shard_map/ppermute | solution.py:256
  30.8 4.3 %collective-permute-start.15 = (bf16[128,128]{1,0:T(8,128)(2,1)S(1)}, bf16[128,128]{1,0:T(8,128)(2,1)S(1)}, u32[]{:S(2)}, u32[]{:S(2)}) collective-permute-start(bf16[128,128]{1,0:T(8,128)(2,1)S(1)} %get-tuple-element.109), channel_id=1, source_target_pairs={{0,1},{1,0},{2,3},{3,2},{4,5},{5,4},{6,7},{7,6},{8,9},{9,8},{10,11... | collective-permute-start | bytes 98312 | tf_op jit(solution)/shard_map/ppermute | solution.py:256
  35.5 4.9 %collective-permute-start.16 = (bf16[128,128]{1,0:T(8,128)(2,1)S(1)}, bf16[128,128]{1,0:T(8,128)(2,1)S(1)}, u32[]{:S(2)}, u32[]{:S(2)}) collective-permute-start(bf16[128,128]{1,0:T(8,128)(2,1)S(1)} %get-tuple-element.115), channel_id=1, source_target_pairs={{0,16},{1,17},{2,18},{3,19},{4,20},{5,21},{6,22},{7,23},{8,24},{9,... | collective-permute-start | bytes 98312 | tf_op jit(solution)/shard_map/ppermute | solution.py:256
  37.4 3.0 %collective-permute-start.17 = (bf16[128,128]{1,0:T(8,128)(2,1)S(1)}, bf16[128,128]{1,0:T(8,128)(2,1)S(1)}, u32[]{:S(2)}, u32[]{:S(2)}) collective-permute-start(bf16[128,128]{1,0:T(8,128)(2,1)S(1)} %get-tuple-element.116), channel_id=1, source_target_pairs={{0,3},{1,2},{2,1},{3,0},{4,5},{5,4},{6,7},{7,6},{8,9},{9,8},{10,19... | collective-permute-start | bytes 98312 | tf_op jit(solution)/shard_map/ppermute | solution.py:256
  37.4 5.1 %collective-permute-start.18 = (bf16[128,128]{1,0:T(8,128)(2,1)S(1)}, bf16[128,128]{1,0:T(8,128)(2,1)S(1)}, u32[]{:S(2)}, u32[]{:S(2)}) collective-permute-start(bf16[128,128]{1,0:T(8,128)(2,1)S(1)} %get-tuple-element.117), channel_id=1, source_target_pairs={{0,1},{1,0},{2,11},{3,4},{4,3},{5,6},{6,5},{7,8},{8,7},{9,10},{10,... | collective-permute-start | bytes 98312 | tf_op jit(solution)/shard_map/ppermute | solution.py:256
  38.5 4.0 %collective-permute-start.19 = (bf16[128,128]{1,0:T(8,128)(2,1)S(1)}, bf16[128,128]{1,0:T(8,128)(2,1)S(1)}, u32[]{:S(2)}, u32[]{:S(2)}) collective-permute-start(bf16[128,128]{1,0:T(8,128)(2,1)S(1)} %get-tuple-element.118), channel_id=1, source_target_pairs={{0,1},{1,0},{2,3},{3,2},{4,5},{5,4},{6,7},{7,6},{8,9},{9,8},{10,11... | collective-permute-start | bytes 98312 | tf_op jit(solution)/shard_map/ppermute | solution.py:256
  42.9 4.9 %collective-permute-start.20 = (bf16[128,128]{1,0:T(8,128)(2,1)S(1)}, bf16[128,128]{1,0:T(8,128)(2,1)S(1)}, u32[]{:S(2)}, u32[]{:S(2)}) collective-permute-start(bf16[128,128]{1,0:T(8,128)(2,1)S(1)} %get-tuple-element.123), channel_id=1, source_target_pairs={{0,16},{1,17},{2,18},{3,19},{4,20},{5,21},{6,22},{7,23},{8,24},{9,... | collective-permute-start | bytes 98312 | tf_op jit(solution)/shard_map/ppermute | solution.py:256
  44.1 3.7 %collective-permute-start.21 = (bf16[128,128]{1,0:T(8,128)(2,1)S(1)}, bf16[128,128]{1,0:T(8,128)(2,1)S(1)}, u32[]{:S(2)}, u32[]{:S(2)}) collective-permute-start(bf16[128,128]{1,0:T(8,128)(2,1)S(1)} %get-tuple-element.124), channel_id=1, source_target_pairs={{0,3},{1,2},{2,1},{3,0},{4,5},{5,4},{6,7},{7,6},{8,9},{9,8},{10,19... | collective-permute-start | bytes 98312 | tf_op jit(solution)/shard_map/ppermute | solution.py:256
  44.1 5.1 %collective-permute-start.22 = (bf16[128,128]{1,0:T(8,128)(2,1)S(1)}, bf16[128,128]{1,0:T(8,128)(2,1)S(1)}, u32[]{:S(2)}, u32[]{:S(2)}) collective-permute-start(bf16[128,128]{1,0:T(8,128)(2,1)S(1)} %get-tuple-element.125), channel_id=1, source_target_pairs={{0,1},{1,0},{2,11},{3,4},{4,3},{5,6},{6,5},{7,8},{8,7},{9,10},{10,... | collective-permute-start | bytes 98312 | tf_op jit(solution)/shard_map/ppermute | solution.py:256
  44.6 4.6 %collective-permute-start.23 = (bf16[128,128]{1,0:T(8,128)(2,1)S(1)}, bf16[128,128]{1,0:T(8,128)(2,1)S(1)}, u32[]{:S(2)}, u32[]{:S(2)}) collective-permute-start(bf16[128,128]{1,0:T(8,128)(2,1)S(1)} %get-tuple-element.126), channel_id=1, source_target_pairs={{0,1},{1,0},{2,3},{3,2},{4,5},{5,4},{6,7},{7,6},{8,9},{9,8},{10,11... | collective-permute-start | bytes 98312 | tf_op jit(solution)/shard_map/ppermute | solution.py:256
  49.6 4.9 %collective-permute-start.24 = (bf16[128,128]{1,0:T(8,128)(2,1)S(1)}, bf16[128,128]{1,0:T(8,128)(2,1)S(1)}, u32[]{:S(2)}, u32[]{:S(2)}) collective-permute-start(bf16[128,128]{1,0:T(8,128)(2,1)S(1)} %get-tuple-element.131), channel_id=1, source_target_pairs={{0,16},{1,17},{2,18},{3,19},{4,20},{5,21},{6,22},{7,23},{8,24},{9,... | collective-permute-start | bytes 98312 | tf_op jit(solution)/shard_map/ppermute | solution.py:256
  51.5 3.0 %collective-permute-start.25 = (bf16[128,128]{1,0:T(8,128)(2,1)S(1)}, bf16[128,128]{1,0:T(8,128)(2,1)S(1)}, u32[]{:S(2)}, u32[]{:S(2)}) collective-permute-start(bf16[128,128]{1,0:T(8,128)(2,1)S(1)} %get-tuple-element.132), channel_id=1, source_target_pairs={{0,3},{1,2},{2,1},{3,0},{4,5},{5,4},{6,7},{7,6},{8,9},{9,8},{10,19... | collective-permute-start | bytes 98312 | tf_op jit(solution)/shard_map/ppermute | solution.py:256
  51.5 5.1 %collective-permute-start.26 = (bf16[128,128]{1,0:T(8,128)(2,1)S(1)}, bf16[128,128]{1,0:T(8,128)(2,1)S(1)}, u32[]{:S(2)}, u32[]{:S(2)}) collective-permute-start(bf16[128,128]{1,0:T(8,128)(2,1)S(1)} %get-tuple-element.133), channel_id=1, source_target_pairs={{0,1},{1,0},{2,11},{3,4},{4,3},{5,6},{6,5},{7,8},{8,7},{9,10},{10,... | collective-permute-start | bytes 98312 | tf_op jit(solution)/shard_map/ppermute | solution.py:256
  52.4 4.2 %collective-permute-start.27 = (bf16[128,128]{1,0:T(8,128)(2,1)S(1)}, bf16[128,128]{1,0:T(8,128)(2,1)S(1)}, u32[]{:S(2)}, u32[]{:S(2)}) collective-permute-start(bf16[128,128]{1,0:T(8,128)(2,1)S(1)} %get-tuple-element.134), channel_id=1, source_target_pairs={{0,1},{1,0},{2,3},{3,2},{4,5},{5,4},{6,7},{7,6},{8,9},{9,8},{10,11... | collective-permute-start | bytes 98312 | tf_op jit(solution)/shard_map/ppermute | solution.py:256
  57.8 4.8 %collective-permute-start.28 = (bf16[128,128]{1,0:T(8,128)(2,1)S(1)}, bf16[128,128]{1,0:T(8,128)(2,1)S(1)}, u32[]{:S(2)}, u32[]{:S(2)}) collective-permute-start(bf16[128,128]{1,0:T(8,128)(2,1)S(1)} %get-tuple-element.139), channel_id=1, source_target_pairs={{0,16},{1,17},{2,18},{3,19},{4,20},{5,21},{6,22},{7,23},{8,24},{9,... | collective-permute-start | bytes 98312 | tf_op jit(solution)/shard_map/ppermute | solution.py:256
  58.8 3.7 %collective-permute-start.29 = (bf16[128,128]{1,0:T(8,128)(2,1)S(1)}, bf16[128,128]{1,0:T(8,128)(2,1)S(1)}, u32[]{:S(2)}, u32[]{:S(2)}) collective-permute-start(bf16[128,128]{1,0:T(8,128)(2,1)S(1)} %get-tuple-element.140), channel_id=1, source_target_pairs={{0,3},{1,2},{2,1},{3,0},{4,5},{5,4},{6,7},{7,6},{8,9},{9,8},{10,19... | collective-permute-start | bytes 98312 | tf_op jit(solution)/shard_map/ppermute | solution.py:256
  58.8 5.1 %collective-permute-start.30 = (bf16[128,128]{1,0:T(8,128)(2,1)S(1)}, bf16[128,128]{1,0:T(8,128)(2,1)S(1)}, u32[]{:S(2)}, u32[]{:S(2)}) collective-permute-start(bf16[128,128]{1,0:T(8,128)(2,1)S(1)} %get-tuple-element.141), channel_id=1, source_target_pairs={{0,1},{1,0},{2,11},{3,4},{4,3},{5,6},{6,5},{7,8},{8,7},{9,10},{10,... | collective-permute-start | bytes 98312 | tf_op jit(solution)/shard_map/ppermute | solution.py:256
  58.9 5.1 %collective-permute-start.31 = (bf16[128,128]{1,0:T(8,128)(2,1)S(1)}, bf16[128,128]{1,0:T(8,128)(2,1)S(1)}, u32[]{:S(2)}, u32[]{:S(2)}) collective-permute-start(bf16[128,128]{1,0:T(8,128)(2,1)S(1)} %get-tuple-element.142), channel_id=1, source_target_pairs={{0,1},{1,0},{2,3},{3,2},{4,5},{5,4},{6,7},{7,6},{8,9},{9,8},{10,11... | collective-permute-start | bytes 98312 | tf_op jit(solution)/shard_map/ppermute | solution.py:256

commit v9 on v8

v9 whole, which is shorter than its diff:
```python
import functools

import jax
import jax.numpy as jnp
from jax import lax
from jax.experimental import pallas as pl
from jax.experimental.pallas import tpu as pltpu
from jax.sharding import PartitionSpec as P

ITERS = 4
FAR = 16
DAMPING = 0.7
LIMIT = 16 * 2**20
PIECES = 4
F32 = jnp.float32
BF16 = jnp.bfloat16


TURNS = (1, 5, 9, 13)


def swaps(count):
    blocks = count // FAR
    near = [i ^ 1 for i in range(count)]
    far = [i ^ FAR for i in range(count)]
    if blocks != 2:
        cross = [(((i + 1) ^ 1) - 1) % count for i in range(count)]
        again = [(((i // FAR + 1) ^ 1) - 1) % blocks * FAR + i % FAR for i in range(count)]
        pairings = [far, again, cross, near] if blocks > 2 else [cross, near]
    else:
        split = [[None] * count, [None] * count]
        for i in range(1, count - 1):
            split[cross_half(i)][i] = ((i + 1) ^ 1) - 1
        for half in split:
            free = [i for i in range(count) if half[i] is None]
            alone = [i for i in free if i ^ 1 not in free]
            mates = dict(zip(alone[::2], alone[1::2])) | dict(zip(alone[1::2], alone[::2]))
            for i in free:
                half[i] = mates.get(i, i ^ 1)
        pairings = [far, *split, near]
    return [list(enumerate(pairing)) for pairing in pairings]


def cross_half(index):
    edge = (index - 1) // 2 if isinstance(index, int) else lax.div(index - 1, 2)
    half = 0
    for turn in TURNS:
        half = half + (edge >= turn) * 1 if isinstance(index, int) else half + jnp.where(edge >= turn, 1, 0)
    return half % 2 if isinstance(index, int) else lax.rem(half, 2)


def slots_of(index, count):
    odd = lax.rem(index, 2)
    block = lax.rem(lax.div(index, FAR), 2)
    blocks = count // FAR
    far = [2 + block] if blocks > 1 else []
    again = [3 - block] if blocks > 2 else []
    return [*far, *again, 1 - odd, odd]


def times(a, b):
    return jnp.dot(a, b, preferred_element_type=F32)


def times_t(a, b):
    return lax.dot_general(a, b, (((1,), (1,)), ((), ())), preferred_element_type=F32)


def gather(links, refs):
    parts = [ref[...] for ref in refs]
    if len(parts) > links:
        half = cross_half(lax.axis_index("sub"))
        mine = jnp.where(half == 0, parts[1].astype(F32), parts[2].astype(F32))
        parts[1:3] = [mine.astype(BF16)]
    return jnp.concatenate(parts, 1)


def scatter(links, refs, block):
    share = refs[0].shape[1]
    columns = [0, 1, 1, 2] if len(refs) > links else range(links)
    for k, ref in zip(columns, refs):
        ref[...] = block[:, k * share : (k + 1) * share].astype(ref.dtype)


def open_kernel(
    trips,
    links,
    subs,
    rows_in,
    near_in,
    rhs_in,
    weight_in,
    n_in,
    s_in,
    hot_ref,
    turned_ref,
    picked_ref,
    weight_ref,
    n_ref,
    s_ref,
    *refs,
):
    out_refs, (rows_ref, near_ref, rhs_ref, sems) = refs[:trips], refs[trips:]
    pairs = [
        (rows_in, rows_ref),
        (near_in, near_ref),
        (rhs_in, rhs_ref),
        (weight_in, weight_ref),
        (n_in, n_ref),
        (s_in, s_ref),
    ]
    copies = [pltpu.make_async_copy(source, target, sems.at[k]) for k, (source, target) in enumerate(pairs)]
    for copy in copies:
        copy.start()
    width, share = rhs_ref.shape[1], rows_ref.shape[2]
    slots = slots_of(lax.axis_index("sub"), subs)
    place = lax.broadcasted_iota(jnp.int32, (width, share), 0)
    copies[0].wait()
    copies[1].wait()
    near = near_ref[...].astype(F32)
    lane = lax.broadcasted_iota(jnp.int32, near.shape, 1)
    for k, slot in enumerate(slots):
        partner = jnp.sum(jnp.where(lane == slot, near, 0.0), 1, keepdims=True)
        row = jnp.where(partner >= 0.0, rows_ref[0, pl.ds(slot, 1), :], -1)
        hot_ref[:, pl.ds(k * share, share)] = jnp.where(place == row, 1.0, 0.0).astype(BF16)
    copies[2].wait()
    turned = rhs_ref[0].T
    turned_ref[...] = turned
    picked = times(turned, hot_ref[...]).astype(BF16)
    picked_ref[...] = picked
    scatter(links, out_refs, picked)
    for copy in copies[3:]:
        copy.wait()


def pick_n_kernel(
    hot_ref,
    turned_ref,
    n_ref,
    weight_ref,
    count_ref,
    hot_t_ref,
    n_pick_ref,
    n_small_ref,
    same_ref,
    inner_ref,
    mask_ref,
    local_ref,
    base_ref,
    row_ref,
):
    hot = hot_ref[...]
    width, total = hot.shape
    weight = weight_ref[...]
    hot_t = hot.T
    hot_t_ref[...] = hot_t
    n_pick = times(hot_t, n_ref[0]).astype(BF16)
    n_pick_ref[...] = n_pick
    n_small_ref[...] = times(n_pick, hot).astype(BF16)
    same = times(hot_t, hot)
    same_ref[...] = same.astype(BF16)
    earlier = lax.broadcasted_iota(jnp.int32, same.shape, 0) < lax.broadcasted_iota(jnp.int32, same.shape, 1)
    repeats = jnp.sum(jnp.where(earlier, same, 0.0), 0, keepdims=True)
    first = jnp.where(repeats > 0.0, 0.0, 1.0)
    hits = jnp.sum(hot_t.astype(F32), 0, keepdims=True)
    inner = jnp.where(hits > 0.0, 0.0, 1.0)
    inner_ref[...] = jnp.broadcast_to(inner, inner_ref.shape)
    high = weight.astype(BF16).astype(F32)
    middle = (weight - high).astype(BF16).astype(F32)
    low = weight - high - middle
    level = lax.broadcasted_iota(jnp.int32, (8, width), 0)
    pieces = jnp.where(level == 0, high, jnp.where(level == 1, middle, jnp.where(level == 2, low, 0.0)))
    pieces = times(pieces.astype(BF16), hot)
    chosen = (pieces[0:1] + pieces[1:2]) + pieces[2:3]
    row_ref[0:1] = chosen
    row_ref[1:2] = chosen * first
    row_ref[2:3] = first
    row_ref[3:8] = jnp.zeros((5, total), F32)
    mask = jnp.where(lax.broadcasted_iota(jnp.int32, mask_ref.shape, 1) < count_ref[0], 1.0, 0.0)
    mask_ref[...] = mask
    local = mask[:1] * turned_ref[...].astype(F32)
    local_ref[...] = local
    base_ref[...] = times_t((weight * local * inner).astype(BF16), n_pick)


def update_path_kernel(trips, links, step, last, *refs):
    arrived_refs, refs = refs[:trips], refs[trips:]
    same_ref, n_small_ref, row_ref, local_ref, base_ref = refs[:5]
    refs = refs[5:]
    residual = local_ref[...].astype(F32) + times(gather(links, arrived_refs), same_ref[...])
    scaled = (row_ref[1:2] * residual).astype(BF16)
    sent = row_ref[0:1] * (base_ref[...] + times_t(scaled, n_small_ref[...]))
    if last:
        scatter(links, refs, sent)
    elif step == 0:
        scatter(links, refs[1:], sent)
        refs[0][...] = DAMPING * sent
    else:
        scatter(links, refs[2:], sent)
        refs[1][...] = refs[0][...] + DAMPING * sent


def residual_path_kernel(trips, links, *refs):
    arrived_refs, refs = refs[:trips], refs[trips:]
    same_ref, s_small_ref, row_ref, base_ref, state_ref, state_out_ref, local_ref = refs[:7]
    state = state_ref[...] + DAMPING * times(gather(links, arrived_refs), same_ref[...])
    state_out_ref[...] = state
    local = base_ref[...] - times((state * row_ref[2:3]).astype(BF16), s_small_ref[...])
    local_ref[...] = local
    scatter(links, refs[7:], local)


def corrected(links, arrived_refs, hot_ref, n_ref, weight_ref, mask_ref, local_ref):
    weight = weight_ref[...]
    residual = local_ref[...] + times_t(gather(links, arrived_refs), hot_ref[...])
    scaled = (weight * residual).astype(BF16)
    return mask_ref[:1] * weight * times_t(scaled, n_ref[0])


def first_update_kernel(trips, links, *refs):
    arrived_refs, refs = refs[:trips], refs[trips:]
    hot_ref, hot_t_ref, n_ref, s_ref, weight_ref, mask_ref, inner_ref, local_ref, picked_ref = refs[:9]
    state_out_ref, base_ref, s_pick_ref, s_small_ref = refs[9:]
    state = DAMPING * corrected(links, arrived_refs, hot_ref, n_ref, weight_ref, mask_ref, local_ref)
    state_out_ref[...] = state
    s_pick = times(s_ref[0], hot_ref[...]).astype(BF16)
    s_pick_ref[...] = s_pick
    s_small_ref[...] = times(hot_t_ref[...], s_pick).astype(BF16)
    base_ref[...] = picked_ref[...].astype(F32) - times((state * inner_ref[:1]).astype(BF16), s_pick)


def update_kernel(trips, links, *refs):
    arrived_refs, refs = refs[:trips], refs[trips:]
    hot_ref, n_ref, weight_ref, mask_ref, inner_ref, local_ref, picked_ref, s_pick_ref, state_ref = refs[:9]
    state_out_ref, base_ref = refs[9:]
    state = state_ref[...] + DAMPING * corrected(links, arrived_refs, hot_ref, n_ref, weight_ref, mask_ref, local_ref)
    state_out_ref[...] = state
    base_ref[...] = picked_ref[...].astype(F32) - times((state * inner_ref[:1]).astype(BF16), s_pick_ref[...])


def last_update_kernel(trips, links, *refs):
    arrived_refs, refs = refs[:trips], refs[trips:]
    hot_ref, n_ref, weight_ref, mask_ref, local_ref, state_ref, state_out_ref = refs
    update = corrected(links, arrived_refs, hot_ref, n_ref, weight_ref, mask_ref, local_ref)
    state_out_ref[...] = (state_ref[...] + DAMPING * update).T


def residual_kernel(trips, links, *refs):
    arrived_refs, refs = refs[:trips], refs[trips:]
    hot_ref, s_ref, turned_ref, weight_ref, mask_ref, inner_ref, n_pick_ref, state_ref = refs[:8]
    state_out_ref, local_ref, base_ref = refs[8:]
    state = state_ref[...] + DAMPING * times_t(gather(links, arrived_refs), hot_ref[...])
    state_out_ref[...] = state
    local = mask_ref[:1] * (turned_ref[...].astype(F32) - times(state.astype(BF16), s_ref[0]))
    local_ref[...] = local
    base_ref[...] = times_t((weight_ref[...] * local * inner_ref[:1]).astype(BF16), n_pick_ref[...])


def close_kernel(trips, links, *refs):
    arrived_refs, (hot_ref, state_ref, out_ref, piece_ref, sems) = refs[:trips], refs[trips:]
    arrived = gather(links, arrived_refs)
    rows = state_ref.shape[0] // PIECES
    copies = []
    for k in range(PIECES):
        part = pl.ds(k * rows, rows)
        piece_ref[part, :] = state_ref[part, :] + DAMPING * times_t(hot_ref[part, :], arrived)
        copies.append(pltpu.make_async_copy(piece_ref.at[part, :], out_ref.at[0, part, :], sems.at[k]))
        copies[k].start()
    for copy in copies:
        copy.wait()


def run(kernel, operands, results, flops, inputs=pltpu.VMEM, outputs=pltpu.VMEM, scalars=(), scratch=()):
    if inputs is pltpu.HBM:
        operands = [pltpu.with_memory_space_constraint(a, inputs) for a in operands]
    moved = sum(a.size * a.dtype.itemsize for a in (*operands, *results))
    return pl.pallas_call(
        kernel,
        out_shape=results,
        in_specs=[pl.BlockSpec(memory_space=pltpu.SMEM if k in scalars else inputs) for k in range(len(operands))],
        out_specs=[pl.BlockSpec(memory_space=outputs)] * len(results),
        scratch_shapes=scratch,
        compiler_params=pltpu.CompilerParams(vmem_limit_bytes=LIMIT),
        cost_estimate=pl.CostEstimate(flops=flops, bytes_accessed=moved, transcendentals=0),
    )(*operands)


def body(right_side, schur, neumann, weights, neighbours, counts, shared_rows):
    width, leads = right_side.shape[1:]
    share = shared_rows.shape[2]
    subs = lax.axis_size("sub")
    routes = swaps(subs)
    trips = len(routes)
    links = len(slots_of(0, subs))
    total = links * share

    def array(rows, columns, kind=F32):
        return jax.ShapeDtypeStruct((rows, columns), kind)

    def same_as(a):
        return jax.ShapeDtypeStruct(a.shape, a.dtype)

    messages = [array(leads, share, BF16)] * trips
    full, some = array(leads, width), array(leads, total)
    small = array(total, total, BF16)
    row = array(8, width)
    picks = 2 * leads * total * width
    whole = 2 * leads * width * width
    path = 4 * leads * total * total

    def exchange(parts):
        return [lax.ppermute(part, "sub", route) for part, route in zip(parts, routes)]

    def bound(kernel, *settings):
        return functools.partial(kernel, trips, links, *settings)

    hot, turned, picked, weight, n_mat, s_mat, *sent = run(
        bound(open_kernel, subs),
        [shared_rows, neighbours, right_side, weights, neumann, schur],
        [
            array(width, total, BF16),
            array(leads, width, BF16),
            array(leads, total, BF16),
            same_as(weights),
            same_as(neumann),
            same_as(schur),
            *messages,
        ],
        picks,
        inputs=pltpu.HBM,
        scratch=[
            pltpu.VMEM(shared_rows.shape, jnp.int32),
            pltpu.VMEM(neighbours.shape, jnp.int32),
            pltpu.VMEM(right_side.shape, BF16),
            pltpu.SemaphoreType.DMA((6,)),
        ],
    )
    arrived = exchange(sent)
    hot_t, n_pick, n_small, same, inner, mask, local, base, rows = run(
        pick_n_kernel,
        [hot, turned, n_mat, weight, counts],
        [array(total, width, BF16), array(total, width, BF16), small, small, row, row, full, some, array(8, total)],
        2 * total * width * width + 4 * total * total * width + picks,
        scalars=(4,),
    )
    near = picked
    near_state = None
    for step in range(ITERS):
        came, last = arrived, step == ITERS - 1
        operands = [*came, same, n_small, rows, near, base]
        if step and not last:
            operands.append(near_state)
        kernel = bound(update_path_kernel, step, last)
        if last:
            sent = run(kernel, operands, messages, path)
            arrived = exchange(sent)
            (state,) = run(
                bound(last_update_kernel),
                [*came, hot, n_mat, weight, mask, local, state],
                [array(width, leads)],
                whole + picks,
            )
            break
        near_state, *sent = run(kernel, operands, [some, *messages], path)
        arrived = exchange(sent)
        if step == 0:
            state, base, s_pick, s_small = run(
                bound(first_update_kernel),
                [*came, hot, hot_t, n_mat, s_mat, weight, mask, inner, local, picked],
                [full, some, array(width, total, BF16), small],
                whole + 2 * picks + 2 * total * width * (width + total),
            )
        else:
            state, base = run(
                bound(update_kernel),
                [*came, hot, n_mat, weight, mask, inner, local, picked, s_pick, state],
                [full, some],
                whole + 2 * picks,
            )
        came = arrived
        near_state, near, *sent = run(
            bound(residual_path_kernel),
            [*came, same, s_small, rows, base, near_state],
            [some, some, *messages],
            path,
        )
        arrived = exchange(sent)
        state, local, base = run(
            bound(residual_kernel),
            [*came, hot, s_mat, turned, weight, mask, inner, n_pick, state],
            [full, full, some],
            whole + 2 * picks,
        )
    (out,) = run(
        bound(close_kernel),
        [*arrived, hot, state],
        [jax.ShapeDtypeStruct((1, width, leads), F32)],
        picks,
        outputs=pltpu.HBM,
        scratch=[pltpu.VMEM((width, leads), F32), pltpu.SemaphoreType.DMA((PIECES,))],
    )
    return out


def solution(mesh):
    in_specs = (
        P("sub", None, None),
        P("sub", None, None),
        P("sub", None, None),
        P("sub", None),
        P("sub", None),
        P("sub"),
        P("sub", None, None),
    )
    out_specs = P("sub", None, None)
    return jax.shard_map(body, mesh=mesh, in_specs=in_specs, out_specs=out_specs, check_vma=False)
```

time: 65.5 us -> 61.5 us (0.939)
  local copies, waits for them, and re-layouts: 4.57 us -> 0 us
  Pallas kernels: 17.6 us -> 18.4 us
    unnamed x14 -> x0, local copies, waits for them, and re-layouts: 4.57 us -> none
    pallas_call x17, Pallas kernels: 17.6 us -> 18.4 us  [run(): pl.pallas_call(kernel, out_shape=results, in_specs=[pl.BlockSpec(memory_s...]
  transfers between devices with their start and end apart: 32 -> 32, of which waited for: 12 -> 12; matrix products, arithmetic and copies ran while one was open for 0% -> 0% of each run, Pallas kernels for 18% -> 19%
where the time goes in v9:
time: 61.5 us; the launch traced here: 61.4 us
  starting transfers between devices  23.2 us (38%)
  waiting for transfers between devices  18.9 us (31%)
  Pallas kernels  18.4 us (30%)
  between operations  0.85 us (1%)
    ppermute x32, starting transfers between devices, exchange(): lax.ppermute(part, 'sub', route)  23.2 us
    ppermute x32, waiting for transfers between devices, exchange(): lax.ppermute(part, 'sub', route)  18.9 us
    pallas_call x17, Pallas kernels, run(): pl.pallas_call(kernel, out_shape=results, in_specs=[pl.BlockSpec(memory_s...  18.4 us
  transfers between devices with their start and end apart: 32, of which 12 were waited for; matrix products, arithmetic and copies ran while one was open for 0% of the time, Pallas kernels for 19%

profile of v9, /device:TPU:8, one launch (start us, length us, event | category | flops | bytes accessed | tf_op | source)
XLA Modules:
  0.0 61.4 jit_solution(5924369894483552004)
XLA Ops:
  0.0 2.4 %shard_map.73 = (bf16[1024,384]{1,0:T(8,128)(2,1)S(1)}, bf16[128,1024]{1,0:T(8,128)(2,1)S(1)}, bf16[128,384]{1,0:T(8,128)(2,1)S(1)}, f32[1,1024]{1,0:T(1,128)S(1...) custom-call(s32[1,4,128]{2,1,0:T(4,128)} %rows_in.1, ...), custom_call_target="tpu_custom_call" | custom-call | flops 100663296 | bytes 9938960 | tf_op jit(solution)/shard_map/pallas_call | solution.py:277
  2.4 2.7 %collective-permute-start = (bf16[128,128]{1,0:T(8,128)(2,1)S(1)}, bf16[128,128]{1,0:T(8,128)(2,1)S(1)}, u32[]{:S(2)}, u32[]{:S(2)}) collective-permute-start(bf16[128,128]{1,0:T(8,128)(2,1)S(1)} %get-tuple-element.77), channel_id=1, source_target_pairs={{0,16},{1,17},{2,18},{3,19},{4,20},{5,21},{6,22},{7,23},{8,24},{9,... | collective-permute-start | bytes 98312 | tf_op jit(solution)/shard_map/ppermute | solution.py:312
  5.1 2.4 %collective-permute-start.2 = (bf16[128,128]{1,0:T(8,128)(2,1)S(1)}, bf16[128,128]{1,0:T(8,128)(2,1)S(1)}, u32[]{:S(2)}, u32[]{:S(2)}) collective-permute-start(bf16[128,128]{1,0:T(8,128)(2,1)S(1)} %get-tuple-element.79), channel_id=1, source_target_pairs={{0,1},{1,0},{2,11},{3,4},{4,3},{5,6},{6,5},{7,8},{8,7},{9,10},{10,... | collective-permute-start | bytes 98312 | tf_op jit(solution)/shard_map/ppermute | solution.py:312
  8.2 2.2 %shard_map.74 = (bf16[384,1024]{1,0:T(8,128)(2,1)S(1)}, bf16[384,1024]{1,0:T(8,128)(2,1)S(1)}, bf16[384,384]{1,0:T(8,128)(2,1)S(1)}, bf16[384,384]{1,0:T(8,128)(...) custom-call(bf16[1024,384]{1,0:T(8,128)(2,1)S(1)} %get-tuple-element, ...), custom_call_target="tpu_custom_call" | custom-call | flops 1509949440 | bytes 6111236 | tf_op jit(solution)/shard_map/pallas_call | solution.py:277
  10.5 0.4 shard_map.75
  10.9 0.4 collective-permute-start.4
  11.3 0.3 collective-permute-start.5
  11.5 1.8 %collective-permute-start.6 = (bf16[128,128]{1,0:T(8,128)(2,1)S(1)}, bf16[128,128]{1,0:T(8,128)(2,1)S(1)}, u32[]{:S(2)}, u32[]{:S(2)}) collective-permute-start(bf16[128,128]{1,0:T(8,128)(2,1)S(1)} %get-tuple-element.92), channel_id=1, source_target_pairs={{0,1},{1,0},{2,11},{3,4},{4,3},{5,6},{6,5},{7,8},{8,7},{9,10},{10,... | collective-permute-start | bytes 98312 | tf_op jit(solution)/shard_map/ppermute | solution.py:312
  13.3 1.3 %collective-permute-start.7 = (bf16[128,128]{1,0:T(8,128)(2,1)S(1)}, bf16[128,128]{1,0:T(8,128)(2,1)S(1)}, u32[]{:S(2)}, u32[]{:S(2)}) collective-permute-start(bf16[128,128]{1,0:T(8,128)(2,1)S(1)} %get-tuple-element.93), channel_id=1, source_target_pairs={{0,1},{1,0},{2,3},{3,2},{4,5},{5,4},{6,7},{7,6},{8,9},{9,8},{10,11... | collective-permute-start | bytes 98312 | tf_op jit(solution)/shard_map/ppermute | solution.py:312
  14.6 2.7 %shard_map.76 = (f32[128,1024]{1,0:T(8,128)S(1)}, f32[128,384]{1,0:T(8,128)S(1)}, bf16[1024,384]{1,0:T(8,128)(2,1)S(1)}, bf16[384,384]{1,0:T(8,128)(2,1)S(1)}) custom-call(bf16[128,128]{1,0:T(8,128)(2,1)S(1)} %collective-permute-done.refs_0_, bf16[128,128]{1,0:T(8,128)(2,1)S(1)} %collective-permute-done.1.refs_1_, ...), custom_call_target="tpu_custom_call" | custom-call | flops 1577058304 | bytes 8392704 | tf_op jit(solution)/shard_map/pallas_call | solution.py:277
  17.4 0.4 shard_map.77
  17.8 1.9 %collective-permute-start.8 = (bf16[128,128]{1,0:T(8,128)(2,1)S(1)}, bf16[128,128]{1,0:T(8,128)(2,1)S(1)}, u32[]{:S(2)}, u32[]{:S(2)}) collective-permute-start(bf16[128,128]{1,0:T(8,128)(2,1)S(1)} %get-tuple-element.102), channel_id=1, source_target_pairs={{0,16},{1,17},{2,18},{3,19},{4,20},{5,21},{6,22},{7,23},{8,24},{9,... | collective-permute-start | bytes 98312 | tf_op jit(solution)/shard_map/ppermute | solution.py:312
  19.7 1.7 %collective-permute-start.10 = (bf16[128,128]{1,0:T(8,128)(2,1)S(1)}, bf16[128,128]{1,0:T(8,128)(2,1)S(1)}, u32[]{:S(2)}, u32[]{:S(2)}) collective-permute-start(bf16[128,128]{1,0:T(8,128)(2,1)S(1)} %get-tuple-element.104), channel_id=1, source_target_pairs={{0,1},{1,0},{2,11},{3,4},{4,3},{5,6},{6,5},{7,8},{8,7},{9,10},{10,... | collective-permute-start | bytes 98312 | tf_op jit(solution)/shard_map/ppermute | solution.py:312
  21.4 1.0 %shard_map.78 = (f32[128,1024]{1,0:T(8,128)S(1)}, f32[128,1024]{1,0:T(8,128)S(1)}, f32[128,384]{1,0:T(8,128)S(1)}) custom-call(bf16[128,128]{1,0:T(8,128)(2,1)S(1)} %collective-permute-done.4.refs_0_, bf16[128,128]{1,0:T(8,128)(2,1)S(1)} %collective-permute-done.5.refs_1_, bf16[128,128]{1,0:T(8,128)(2,1)S(1)} %collective-permute-done.6.refs_2_, ...), custom_call_target="tpu_custom_call" | custom-call | flops 469762048 | bytes 5902336 | tf_op jit(solution)/shard_map/pallas_call | solution.py:277
  22.4 0.4 collective-permute-done.8.refs_0_
  22.8 2.1 %collective-permute-done.10.refs_2_ = bf16[128,128]{1,0:T(8,128)(2,1)S(1)} collective-permute-done((bf16[128,128]{1,0:T(8,128)(2,1)S(1)}, bf16[128,128]{1,0:T(8,128)(2,1)S(1)}, u32[]{:S(2)}, u32[]{:S(2)}) %collective-permute-start.10) | collective-permute-done | bytes 32800 | tf_op jit(solution)/shard_map/ppermute | solution.py:312
  24.8 0.4 shard_map.79
  25.2 1.1 %collective-permute-start.12 = (bf16[128,128]{1,0:T(8,128)(2,1)S(1)}, bf16[128,128]{1,0:T(8,128)(2,1)S(1)}, u32[]{:S(2)}, u32[]{:S(2)}) collective-permute-start(bf16[128,128]{1,0:T(8,128)(2,1)S(1)} %get-tuple-element.111), channel_id=1, source_target_pairs={{0,16},{1,17},{2,18},{3,19},{4,20},{5,21},{6,22},{7,23},{8,24},{9,... | collective-permute-start | bytes 98312 | tf_op jit(solution)/shard_map/ppermute | solution.py:312
  26.4 0.9 %collective-permute-start.14 = (bf16[128,128]{1,0:T(8,128)(2,1)S(1)}, bf16[128,128]{1,0:T(8,128)(2,1)S(1)}, u32[]{:S(2)}, u32[]{:S(2)}) collective-permute-start(bf16[128,128]{1,0:T(8,128)(2,1)S(1)} %get-tuple-element.113), channel_id=1, source_target_pairs={{0,1},{1,0},{2,11},{3,4},{4,3},{5,6},{6,5},{7,8},{8,7},{9,10},{10,... | collective-permute-start | bytes 98312 | tf_op jit(solution)/shard_map/ppermute | solution.py:312
  27.3 1.2 %shard_map.80 = (f32[128,1024]{1,0:T(8,128)S(1)}, f32[128,384]{1,0:T(8,128)S(1)}) custom-call(bf16[128,128]{1,0:T(8,128)(2,1)S(1)} %collective-permute-done.8.refs_0_, bf16[128,128]{1,0:T(8,128)(2,1)S(1)} %collective-permute-done.9.refs_1_, bf16[128,128]{1,0:T(8,128)(2,1)S(1)} %collective-permute-done.10.refs_2_, ...), custom_call_target="tpu_custom_call" | custom-call | flops 469762048 | bytes 5738496 | tf_op jit(solution)/shard_map/pallas_call | solution.py:277
  28.5 1.6 %collective-permute-done.12.refs_0_ = bf16[128,128]{1,0:T(8,128)(2,1)S(1)} collective-permute-done((bf16[128,128]{1,0:T(8,128)(2,1)S(1)}, bf16[128,128]{1,0:T(8,128)(2,1)S(1)}, u32[]{:S(2)}, u32[]{:S(2)}) %collective-permute-start.12) | collective-permute-done | bytes 32800 | tf_op jit(solution)/shard_map/ppermute | solution.py:312
  30.1 1.4 %collective-permute-done.14.refs_2_ = bf16[128,128]{1,0:T(8,128)(2,1)S(1)} collective-permute-done((bf16[128,128]{1,0:T(8,128)(2,1)S(1)}, bf16[128,128]{1,0:T(8,128)(2,1)S(1)}, u32[]{:S(2)}, u32[]{:S(2)}) %collective-permute-start.14) | collective-permute-done | bytes 32800 | tf_op jit(solution)/shard_map/ppermute | solution.py:312
  31.5 0.4 shard_map.81
  31.9 1.9 %collective-permute-start.16 = (bf16[128,128]{1,0:T(8,128)(2,1)S(1)}, bf16[128,128]{1,0:T(8,128)(2,1)S(1)}, u32[]{:S(2)}, u32[]{:S(2)}) collective-permute-start(bf16[128,128]{1,0:T(8,128)(2,1)S(1)} %get-tuple-element.120), channel_id=1, source_target_pairs={{0,16},{1,17},{2,18},{3,19},{4,20},{5,21},{6,22},{7,23},{8,24},{9,... | collective-permute-start | bytes 98312 | tf_op jit(solution)/shard_map/ppermute | solution.py:312
  33.8 1.1 %collective-permute-start.18 = (bf16[128,128]{1,0:T(8,128)(2,1)S(1)}, bf16[128,128]{1,0:T(8,128)(2,1)S(1)}, u32[]{:S(2)}, u32[]{:S(2)}) collective-permute-start(bf16[128,128]{1,0:T(8,128)(2,1)S(1)} %get-tuple-element.122), channel_id=1, source_target_pairs={{0,1},{1,0},{2,11},{3,4},{4,3},{5,6},{6,5},{7,8},{8,7},{9,10},{10,... | collective-permute-start | bytes 98312 | tf_op jit(solution)/shard_map/ppermute | solution.py:312
  35.0 1.0 %shard_map.82 = (f32[128,1024]{1,0:T(8,128)S(1)}, f32[128,1024]{1,0:T(8,128)S(1)}, f32[128,384]{1,0:T(8,128)S(1)}) custom-call(bf16[128,128]{1,0:T(8,128)(2,1)S(1)} %collective-permute-done.12.refs_0_, bf16[128,128]{1,0:T(8,128)(2,1)S(1)} %collective-permute-done.13.refs_1_, bf16[128,128]{1,0:T(8,128)(2,1)S(1)} %collective-permute-done.14.refs_2_, ...), custom_call_target="tpu_custom_call" | custom-call | flops 469762048 | bytes 5902336 | tf_op jit(solution)/shard_map/pallas_call | solution.py:277
  36.0 0.8 %collective-permute-done.16.refs_0_ = bf16[128,128]{1,0:T(8,128)(2,1)S(1)} collective-permute-done((bf16[128,128]{1,0:T(8,128)(2,1)S(1)}, bf16[128,128]{1,0:T(8,128)(2,1)S(1)}, u32[]{:S(2)}, u32[]{:S(2)}) %collective-permute-start.16) | collective-permute-done | bytes 32800 | tf_op jit(solution)/shard_map/ppermute | solution.py:312
  36.8 2.2 %collective-permute-done.18.refs_2_ = bf16[128,128]{1,0:T(8,128)(2,1)S(1)} collective-permute-done((bf16[128,128]{1,0:T(8,128)(2,1)S(1)}, bf16[128,128]{1,0:T(8,128)(2,1)S(1)}, u32[]{:S(2)}, u32[]{:S(2)}) %collective-permute-start.18) | collective-permute-done | bytes 32800 | tf_op jit(solution)/shard_map/ppermute | solution.py:312
  39.0 0.4 shard_map.83
  39.4 1.1 %collective-permute-start.20 = (bf16[128,128]{1,0:T(8,128)(2,1)S(1)}, bf16[128,128]{1,0:T(8,128)(2,1)S(1)}, u32[]{:S(2)}, u32[]{:S(2)}) collective-permute-start(bf16[128,128]{1,0:T(8,128)(2,1)S(1)} %get-tuple-element.128), channel_id=1, source_target_pairs={{0,16},{1,17},{2,18},{3,19},{4,20},{5,21},{6,22},{7,23},{8,24},{9,... | collective-permute-start | bytes 98312 | tf_op jit(solution)/shard_map/ppermute | solution.py:312
  40.5 0.3 collective-permute-start.22
  40.9 0.2 collective-permute-start.23
  41.0 1.2 %shard_map.84 = (f32[128,1024]{1,0:T(8,128)S(1)}, f32[128,384]{1,0:T(8,128)S(1)}) custom-call(bf16[128,128]{1,0:T(8,128)(2,1)S(1)} %collective-permute-done.16.refs_0_, bf16[128,128]{1,0:T(8,128)(2,1)S(1)} %collective-permute-done.17.refs_1_, bf16[128,128]{1,0:T(8,128)(2,1)S(1)} %collective-permute-done.18.refs_2_, ...), custom_call_target="tpu_custom_call" | custom-call | flops 469762048 | bytes 5738496 | tf_op jit(solution)/shard_map/pallas_call | solution.py:277
  42.3 2.0 %collective-permute-done.20.refs_0_ = bf16[128,128]{1,0:T(8,128)(2,1)S(1)} collective-permute-done((bf16[128,128]{1,0:T(8,128)(2,1)S(1)}, bf16[128,128]{1,0:T(8,128)(2,1)S(1)}, u32[]{:S(2)}, u32[]{:S(2)}) %collective-permute-start.20) | collective-permute-done | bytes 32800 | tf_op jit(solution)/shard_map/ppermute | solution.py:312
  44.3 1.4 %collective-permute-done.22.refs_2_ = bf16[128,128]{1,0:T(8,128)(2,1)S(1)} collective-permute-done((bf16[128,128]{1,0:T(8,128)(2,1)S(1)}, bf16[128,128]{1,0:T(8,128)(2,1)S(1)}, u32[]{:S(2)}, u32[]{:S(2)}) %collective-permute-start.22) | collective-permute-done | bytes 32800 | tf_op jit(solution)/shard_map/ppermute | solution.py:312
  45.7 0.9 %shard_map.85 = (f32[128,384]{1,0:T(8,128)}, f32[128,384]{1,0:T(8,128)S(1)}, bf16[128,128]{1,0:T(8,128)(2,1)S(1)}, bf16[128,128]{1,0:T(8,128)(2,1)S(1)}, bf16[12...) custom-call(bf16[128,128]{1,0:T(8,128)(2,1)S(1)} %collective-permute-done.20.refs_0_, ...), custom_call_target="tpu_custom_call" | custom-call | flops 75497472 | bytes 1650688 | tf_op jit(solution)/shard_map/pallas_call | solution.py:277
  46.6 1.8 %collective-permute-start.24 = (bf16[128,128]{1,0:T(8,128)(2,1)S(1)}, bf16[128,128]{1,0:T(8,128)(2,1)S(1)}, u32[]{:S(2)}, u32[]{:S(2)}) collective-permute-start(bf16[128,128]{1,0:T(8,128)(2,1)S(1)} %get-tuple-element.136), channel_id=1, source_target_pairs={{0,16},{1,17},{2,18},{3,19},{4,20},{5,21},{6,22},{7,23},{8,24},{9,... | collective-permute-start | bytes 98312 | tf_op jit(solution)/shard_map/ppermute | solution.py:312
  48.4 0.6 collective-permute-start.26
  49.0 1.0 %shard_map.86 = (f32[128,1024]{1,0:T(8,128)S(1)}, f32[128,1024]{1,0:T(8,128)S(1)}, f32[128,384]{1,0:T(8,128)S(1)}) custom-call(bf16[128,128]{1,0:T(8,128)(2,1)S(1)} %collective-permute-done.20.refs_0_, bf16[128,128]{1,0:T(8,128)(2,1)S(1)} %collective-permute-done.21.refs_1_, bf16[128,128]{1,0:T(8,128)(2,1)S(1)} %collective-permute-done.22.refs_2_, ...), custom_call_target="tpu_custom_call" | custom-call | flops 469762048 | bytes 5902336 | tf_op jit(solution)/shard_map/pallas_call | solution.py:277
  50.0 1.4 %collective-permute-done.24.refs_0_ = bf16[128,128]{1,0:T(8,128)(2,1)S(1)} collective-permute-done((bf16[128,128]{1,0:T(8,128)(2,1)S(1)}, bf16[128,128]{1,0:T(8,128)(2,1)S(1)}, u32[]{:S(2)}, u32[]{:S(2)}) %collective-permute-start.24) | collective-permute-done | bytes 32800 | tf_op jit(solution)/shard_map/ppermute | solution.py:312
  51.4 2.2 %collective-permute-done.26.refs_2_ = bf16[128,128]{1,0:T(8,128)(2,1)S(1)} collective-permute-done((bf16[128,128]{1,0:T(8,128)(2,1)S(1)}, bf16[128,128]{1,0:T(8,128)(2,1)S(1)}, u32[]{:S(2)}, u32[]{:S(2)}) %collective-permute-start.26) | collective-permute-done | bytes 32800 | tf_op jit(solution)/shard_map/ppermute | solution.py:312
  53.6 0.4 shard_map.87
  54.0 1.1 %collective-permute-start.28 = (bf16[128,128]{1,0:T(8,128)(2,1)S(1)}, bf16[128,128]{1,0:T(8,128)(2,1)S(1)}, u32[]{:S(2)}, u32[]{:S(2)}) collective-permute-start(bf16[128,128]{1,0:T(8,128)(2,1)S(1)} %get-tuple-element.143), channel_id=1, source_target_pairs={{0,16},{1,17},{2,18},{3,19},{4,20},{5,21},{6,22},{7,23},{8,24},{9,... | collective-permute-start | bytes 98312 | tf_op jit(solution)/shard_map/ppermute | solution.py:312
  55.2 0.4 collective-permute-start.31
  55.6 1.2 %shard_map.88.refs_5_ = f32[1024,128]{1,0:T(8,128)S(1)} custom-call(bf16[128,128]{1,0:T(8,128)(2,1)S(1)} %collective-permute-done.24.refs_0_, bf16[128,128]{1,0:T(8,128)(2,1)S(1)} %collective-permute-done.25.refs_1_, bf16[128,128]{1,0:T(8,128)(2,1)S(1)} %collective-permute-done.26.refs_2_, bf16[128,128]{1,0:T(8,128)(2,1)S(1)} %collective-permute-done.27.refs_3_, ...), custom_call_target="tpu_custom_call" | custom-call | flops 369098752 | bytes 4624384 | tf_op jit(solution)/shard_map/pallas_call | solution.py:277
  56.8 2.0 %collective-permute-done.28.refs_0_ = bf16[128,128]{1,0:T(8,128)(2,1)S(1)} collective-permute-done((bf16[128,128]{1,0:T(8,128)(2,1)S(1)}, bf16[128,128]{1,0:T(8,128)(2,1)S(1)}, u32[]{:S(2)}, u32[]{:S(2)}) %collective-permute-start.28) | collective-permute-done | bytes 32800 | tf_op jit(solution)/shard_map/ppermute | solution.py:312
  58.9 1.4 %collective-permute-done.30.refs_2_ = bf16[128,128]{1,0:T(8,128)(2,1)S(1)} collective-permute-done((bf16[128,128]{1,0:T(8,128)(2,1)S(1)}, bf16[128,128]{1,0:T(8,128)(2,1)S(1)}, u32[]{:S(2)}, u32[]{:S(2)}) %collective-permute-start.30) | collective-permute-done | bytes 32800 | tf_op jit(solution)/shard_map/ppermute | solution.py:312
  60.3 1.1 %shard_map.89 = f32[1,1024,128]{2,1,0:T(8,128)} custom-call(bf16[128,128]{1,0:T(8,128)(2,1)S(1)} %collective-permute-done.28.refs_0_, bf16[128,128]{1,0:T(8,128)(2,1)S(1)} %collective-permute-done.29.refs_1_, bf16[128,128]{1,0:T(8,128)(2,1)S(1)} %collective-permute-done.30.refs_2_, bf16[128,128]{1,0:T(8,128)(2,1)S(1)} %collective-permute-done.31.refs_3_, ...), custom_call_target="tpu_custom_call" | custom-call | flops 100663296 | bytes 1966080 | tf_op jit(solution)/shard_map/pallas_call | solution.py:277
  (33 shorter events, 0.2 us)
Async XLA Ops:
  2.4 8.0 %collective-permute-start = (bf16[128,128]{1,0:T(8,128)(2,1)S(1)}, bf16[128,128]{1,0:T(8,128)(2,1)S(1)}, u32[]{:S(2)}, u32[]{:S(2)}) collective-permute-start(bf16[128,128]{1,0:T(8,128)(2,1)S(1)} %get-tuple-element.77), channel_id=1, source_target_pairs={{0,16},{1,17},{2,18},{3,19},{4,20},{5,21},{6,22},{7,23},{8,24},{9,... | collective-permute-start | bytes 98312 | tf_op jit(solution)/shard_map/ppermute | solution.py:312
  5.1 5.3 %collective-permute-start.1 = (bf16[128,128]{1,0:T(8,128)(2,1)S(1)}, bf16[128,128]{1,0:T(8,128)(2,1)S(1)}, u32[]{:S(2)}, u32[]{:S(2)}) collective-permute-start(bf16[128,128]{1,0:T(8,128)(2,1)S(1)} %get-tuple-element.78), channel_id=1, source_target_pairs={{0,3},{1,2},{2,1},{3,0},{4,5},{5,4},{6,7},{7,6},{8,9},{9,8},{10,19... | collective-permute-start | bytes 98312 | tf_op jit(solution)/shard_map/ppermute | solution.py:312
  5.1 5.4 %collective-permute-start.2 = (bf16[128,128]{1,0:T(8,128)(2,1)S(1)}, bf16[128,128]{1,0:T(8,128)(2,1)S(1)}, u32[]{:S(2)}, u32[]{:S(2)}) collective-permute-start(bf16[128,128]{1,0:T(8,128)(2,1)S(1)} %get-tuple-element.79), channel_id=1, source_target_pairs={{0,1},{1,0},{2,11},{3,4},{4,3},{5,6},{6,5},{7,8},{8,7},{9,10},{10,... | collective-permute-start | bytes 98312 | tf_op jit(solution)/shard_map/ppermute | solution.py:312
  7.5 2.9 %collective-permute-start.3 = (bf16[128,128]{1,0:T(8,128)(2,1)S(1)}, bf16[128,128]{1,0:T(8,128)(2,1)S(1)}, u32[]{:S(2)}, u32[]{:S(2)}) collective-permute-start(bf16[128,128]{1,0:T(8,128)(2,1)S(1)} %get-tuple-element.80), channel_id=1, source_target_pairs={{0,1},{1,0},{2,3},{3,2},{4,5},{5,4},{6,7},{7,6},{8,9},{9,8},{10,11... | collective-permute-start | bytes 98312 | tf_op jit(solution)/shard_map/ppermute | solution.py:312
  10.9 6.5 %collective-permute-start.4 = (bf16[128,128]{1,0:T(8,128)(2,1)S(1)}, bf16[128,128]{1,0:T(8,128)(2,1)S(1)}, u32[]{:S(2)}, u32[]{:S(2)}) collective-permute-start(bf16[128,128]{1,0:T(8,128)(2,1)S(1)} %get-tuple-element.90), channel_id=1, source_target_pairs={{0,16},{1,17},{2,18},{3,19},{4,20},{5,21},{6,22},{7,23},{8,24},{9,... | collective-permute-start | bytes 98312 | tf_op jit(solution)/shard_map/ppermute | solution.py:312
  11.3 6.1 %collective-permute-start.5 = (bf16[128,128]{1,0:T(8,128)(2,1)S(1)}, bf16[128,128]{1,0:T(8,128)(2,1)S(1)}, u32[]{:S(2)}, u32[]{:S(2)}) collective-permute-start(bf16[128,128]{1,0:T(8,128)(2,1)S(1)} %get-tuple-element.91), channel_id=1, source_target_pairs={{0,3},{1,2},{2,1},{3,0},{4,5},{5,4},{6,7},{7,6},{8,9},{9,8},{10,19... | collective-permute-start | bytes 98312 | tf_op jit(solution)/shard_map/ppermute | solution.py:312
  11.5 5.8 %collective-permute-start.6 = (bf16[128,128]{1,0:T(8,128)(2,1)S(1)}, bf16[128,128]{1,0:T(8,128)(2,1)S(1)}, u32[]{:S(2)}, u32[]{:S(2)}) collective-permute-start(bf16[128,128]{1,0:T(8,128)(2,1)S(1)} %get-tuple-element.92), channel_id=1, source_target_pairs={{0,1},{1,0},{2,11},{3,4},{4,3},{5,6},{6,5},{7,8},{8,7},{9,10},{10,... | collective-permute-start | bytes 98312 | tf_op jit(solution)/shard_map/ppermute | solution.py:312
  13.3 4.1 %collective-permute-start.7 = (bf16[128,128]{1,0:T(8,128)(2,1)S(1)}, bf16[128,128]{1,0:T(8,128)(2,1)S(1)}, u32[]{:S(2)}, u32[]{:S(2)}) collective-permute-start(bf16[128,128]{1,0:T(8,128)(2,1)S(1)} %get-tuple-element.93), channel_id=1, source_target_pairs={{0,1},{1,0},{2,3},{3,2},{4,5},{5,4},{6,7},{7,6},{8,9},{9,8},{10,11... | collective-permute-start | bytes 98312 | tf_op jit(solution)/shard_map/ppermute | solution.py:312
  17.8 5.0 %collective-permute-start.8 = (bf16[128,128]{1,0:T(8,128)(2,1)S(1)}, bf16[128,128]{1,0:T(8,128)(2,1)S(1)}, u32[]{:S(2)}, u32[]{:S(2)}) collective-permute-start(bf16[128,128]{1,0:T(8,128)(2,1)S(1)} %get-tuple-element.102), channel_id=1, source_target_pairs={{0,16},{1,17},{2,18},{3,19},{4,20},{5,21},{6,22},{7,23},{8,24},{9,... | collective-permute-start | bytes 98312 | tf_op jit(solution)/shard_map/ppermute | solution.py:312
  19.7 3.1 %collective-permute-start.9 = (bf16[128,128]{1,0:T(8,128)(2,1)S(1)}, bf16[128,128]{1,0:T(8,128)(2,1)S(1)}, u32[]{:S(2)}, u32[]{:S(2)}) collective-permute-start(bf16[128,128]{1,0:T(8,128)(2,1)S(1)} %get-tuple-element.103), channel_id=1, source_target_pairs={{0,3},{1,2},{2,1},{3,0},{4,5},{5,4},{6,7},{7,6},{8,9},{9,8},{10,19... | collective-permute-start | bytes 98312 | tf_op jit(solution)/shard_map/ppermute | solution.py:312
  19.7 5.1 %collective-permute-start.10 = (bf16[128,128]{1,0:T(8,128)(2,1)S(1)}, bf16[128,128]{1,0:T(8,128)(2,1)S(1)}, u32[]{:S(2)}, u32[]{:S(2)}) collective-permute-start(bf16[128,128]{1,0:T(8,128)(2,1)S(1)} %get-tuple-element.104), channel_id=1, source_target_pairs={{0,1},{1,0},{2,11},{3,4},{4,3},{5,6},{6,5},{7,8},{8,7},{9,10},{10,... | collective-permute-start | bytes 98312 | tf_op jit(solution)/shard_map/ppermute | solution.py:312
  21.4 3.5 %collective-permute-start.11 = (bf16[128,128]{1,0:T(8,128)(2,1)S(1)}, bf16[128,128]{1,0:T(8,128)(2,1)S(1)}, u32[]{:S(2)}, u32[]{:S(2)}) collective-permute-start(bf16[128,128]{1,0:T(8,128)(2,1)S(1)} %get-tuple-element.105), channel_id=1, source_target_pairs={{0,1},{1,0},{2,3},{3,2},{4,5},{5,4},{6,7},{7,6},{8,9},{9,8},{10,11... | collective-permute-start | bytes 98312 | tf_op jit(solution)/shard_map/ppermute | solution.py:312
  25.2 4.9 %collective-permute-start.12 = (bf16[128,128]{1,0:T(8,128)(2,1)S(1)}, bf16[128,128]{1,0:T(8,128)(2,1)S(1)}, u32[]{:S(2)}, u32[]{:S(2)}) collective-permute-start(bf16[128,128]{1,0:T(8,128)(2,1)S(1)} %get-tuple-element.111), channel_id=1, source_target_pairs={{0,16},{1,17},{2,18},{3,19},{4,20},{5,21},{6,22},{7,23},{8,24},{9,... | collective-permute-start | bytes 98312 | tf_op jit(solution)/shard_map/ppermute | solution.py:312
  26.4 3.7 %collective-permute-start.13 = (bf16[128,128]{1,0:T(8,128)(2,1)S(1)}, bf16[128,128]{1,0:T(8,128)(2,1)S(1)}, u32[]{:S(2)}, u32[]{:S(2)}) collective-permute-start(bf16[128,128]{1,0:T(8,128)(2,1)S(1)} %get-tuple-element.112), channel_id=1, source_target_pairs={{0,3},{1,2},{2,1},{3,0},{4,5},{5,4},{6,7},{7,6},{8,9},{9,8},{10,19... | collective-permute-start | bytes 98312 | tf_op jit(solution)/shard_map/ppermute | solution.py:312
  26.4 5.1 %collective-permute-start.14 = (bf16[128,128]{1,0:T(8,128)(2,1)S(1)}, bf16[128,128]{1,0:T(8,128)(2,1)S(1)}, u32[]{:S(2)}, u32[]{:S(2)}) collective-permute-start(bf16[128,128]{1,0:T(8,128)(2,1)S(1)} %get-tuple-element.113), channel_id=1, source_target_pairs={{0,1},{1,0},{2,11},{3,4},{4,3},{5,6},{6,5},{7,8},{8,7},{9,10},{10,... | collective-permute-start | bytes 98312 | tf_op jit(solution)/shard_map/ppermute | solution.py:312
  27.3 4.3 %collective-permute-start.15 = (bf16[128,128]{1,0:T(8,128)(2,1)S(1)}, bf16[128,128]{1,0:T(8,128)(2,1)S(1)}, u32[]{:S(2)}, u32[]{:S(2)}) collective-permute-start(bf16[128,128]{1,0:T(8,128)(2,1)S(1)} %get-tuple-element.114), channel_id=1, source_target_pairs={{0,1},{1,0},{2,3},{3,2},{4,5},{5,4},{6,7},{7,6},{8,9},{9,8},{10,11... | collective-permute-start | bytes 98312 | tf_op jit(solution)/shard_map/ppermute | solution.py:312
  31.9 4.9 %collective-permute-start.16 = (bf16[128,128]{1,0:T(8,128)(2,1)S(1)}, bf16[128,128]{1,0:T(8,128)(2,1)S(1)}, u32[]{:S(2)}, u32[]{:S(2)}) collective-permute-start(bf16[128,128]{1,0:T(8,128)(2,1)S(1)} %get-tuple-element.120), channel_id=1, source_target_pairs={{0,16},{1,17},{2,18},{3,19},{4,20},{5,21},{6,22},{7,23},{8,24},{9,... | collective-permute-start | bytes 98312 | tf_op jit(solution)/shard_map/ppermute | solution.py:312
  33.8 3.0 %collective-permute-start.17 = (bf16[128,128]{1,0:T(8,128)(2,1)S(1)}, bf16[128,128]{1,0:T(8,128)(2,1)S(1)}, u32[]{:S(2)}, u32[]{:S(2)}) collective-permute-start(bf16[128,128]{1,0:T(8,128)(2,1)S(1)} %get-tuple-element.121), channel_id=1, source_target_pairs={{0,3},{1,2},{2,1},{3,0},{4,5},{5,4},{6,7},{7,6},{8,9},{9,8},{10,19... | collective-permute-start | bytes 98312 | tf_op jit(solution)/shard_map/ppermute | solution.py:312
  33.8 5.1 %collective-permute-start.18 = (bf16[128,128]{1,0:T(8,128)(2,1)S(1)}, bf16[128,128]{1,0:T(8,128)(2,1)S(1)}, u32[]{:S(2)}, u32[]{:S(2)}) collective-permute-start(bf16[128,128]{1,0:T(8,128)(2,1)S(1)} %get-tuple-element.122), channel_id=1, source_target_pairs={{0,1},{1,0},{2,11},{3,4},{4,3},{5,6},{6,5},{7,8},{8,7},{9,10},{10,... | collective-permute-start | bytes 98312 | tf_op jit(solution)/shard_map/ppermute | solution.py:312
  34.9 4.0 %collective-permute-start.19 = (bf16[128,128]{1,0:T(8,128)(2,1)S(1)}, bf16[128,128]{1,0:T(8,128)(2,1)S(1)}, u32[]{:S(2)}, u32[]{:S(2)}) collective-permute-start(bf16[128,128]{1,0:T(8,128)(2,1)S(1)} %get-tuple-element.123), channel_id=1, source_target_pairs={{0,1},{1,0},{2,3},{3,2},{4,5},{5,4},{6,7},{7,6},{8,9},{9,8},{10,11... | collective-permute-start | bytes 98312 | tf_op jit(solution)/shard_map/ppermute | solution.py:312
  39.4 4.9 %collective-permute-start.20 = (bf16[128,128]{1,0:T(8,128)(2,1)S(1)}, bf16[128,128]{1,0:T(8,128)(2,1)S(1)}, u32[]{:S(2)}, u32[]{:S(2)}) collective-permute-start(bf16[128,128]{1,0:T(8,128)(2,1)S(1)} %get-tuple-element.128), channel_id=1, source_target_pairs={{0,16},{1,17},{2,18},{3,19},{4,20},{5,21},{6,22},{7,23},{8,24},{9,... | collective-permute-start | bytes 98312 | tf_op jit(solution)/shard_map/ppermute | solution.py:312
  40.5 3.7 %collective-permute-start.21 = (bf16[128,128]{1,0:T(8,128)(2,1)S(1)}, bf16[128,128]{1,0:T(8,128)(2,1)S(1)}, u32[]{:S(2)}, u32[]{:S(2)}) collective-permute-start(bf16[128,128]{1,0:T(8,128)(2,1)S(1)} %get-tuple-element.129), channel_id=1, source_target_pairs={{0,3},{1,2},{2,1},{3,0},{4,5},{5,4},{6,7},{7,6},{8,9},{9,8},{10,19... | collective-permute-start | bytes 98312 | tf_op jit(solution)/shard_map/ppermute | solution.py:312
  40.5 5.1 %collective-permute-start.22 = (bf16[128,128]{1,0:T(8,128)(2,1)S(1)}, bf16[128,128]{1,0:T(8,128)(2,1)S(1)}, u32[]{:S(2)}, u32[]{:S(2)}) collective-permute-start(bf16[128,128]{1,0:T(8,128)(2,1)S(1)} %get-tuple-element.130), channel_id=1, source_target_pairs={{0,1},{1,0},{2,11},{3,4},{4,3},{5,6},{6,5},{7,8},{8,7},{9,10},{10,... | collective-permute-start | bytes 98312 | tf_op jit(solution)/shard_map/ppermute | solution.py:312
  40.9 4.8 %collective-permute-start.23 = (bf16[128,128]{1,0:T(8,128)(2,1)S(1)}, bf16[128,128]{1,0:T(8,128)(2,1)S(1)}, u32[]{:S(2)}, u32[]{:S(2)}) collective-permute-start(bf16[128,128]{1,0:T(8,128)(2,1)S(1)} %get-tuple-element.131), channel_id=1, source_target_pairs={{0,1},{1,0},{2,3},{3,2},{4,5},{5,4},{6,7},{7,6},{8,9},{9,8},{10,11... | collective-permute-start | bytes 98312 | tf_op jit(solution)/shard_map/ppermute | solution.py:312
  46.6 4.8 %collective-permute-start.24 = (bf16[128,128]{1,0:T(8,128)(2,1)S(1)}, bf16[128,128]{1,0:T(8,128)(2,1)S(1)}, u32[]{:S(2)}, u32[]{:S(2)}) collective-permute-start(bf16[128,128]{1,0:T(8,128)(2,1)S(1)} %get-tuple-element.136), channel_id=1, source_target_pairs={{0,16},{1,17},{2,18},{3,19},{4,20},{5,21},{6,22},{7,23},{8,24},{9,... | collective-permute-start | bytes 98312 | tf_op jit(solution)/shard_map/ppermute | solution.py:312
  48.4 3.0 %collective-permute-start.25 = (bf16[128,128]{1,0:T(8,128)(2,1)S(1)}, bf16[128,128]{1,0:T(8,128)(2,1)S(1)}, u32[]{:S(2)}, u32[]{:S(2)}) collective-permute-start(bf16[128,128]{1,0:T(8,128)(2,1)S(1)} %get-tuple-element.137), channel_id=1, source_target_pairs={{0,3},{1,2},{2,1},{3,0},{4,5},{5,4},{6,7},{7,6},{8,9},{9,8},{10,19... | collective-permute-start | bytes 98312 | tf_op jit(solution)/shard_map/ppermute | solution.py:312
  48.4 5.1 %collective-permute-start.26 = (bf16[128,128]{1,0:T(8,128)(2,1)S(1)}, bf16[128,128]{1,0:T(8,128)(2,1)S(1)}, u32[]{:S(2)}, u32[]{:S(2)}) collective-permute-start(bf16[128,128]{1,0:T(8,128)(2,1)S(1)} %get-tuple-element.138), channel_id=1, source_target_pairs={{0,1},{1,0},{2,11},{3,4},{4,3},{5,6},{6,5},{7,8},{8,7},{9,10},{10,... | collective-permute-start | bytes 98312 | tf_op jit(solution)/shard_map/ppermute | solution.py:312
  49.0 4.6 %collective-permute-start.27 = (bf16[128,128]{1,0:T(8,128)(2,1)S(1)}, bf16[128,128]{1,0:T(8,128)(2,1)S(1)}, u32[]{:S(2)}, u32[]{:S(2)}) collective-permute-start(bf16[128,128]{1,0:T(8,128)(2,1)S(1)} %get-tuple-element.139), channel_id=1, source_target_pairs={{0,1},{1,0},{2,3},{3,2},{4,5},{5,4},{6,7},{7,6},{8,9},{9,8},{10,11... | collective-permute-start | bytes 98312 | tf_op jit(solution)/shard_map/ppermute | solution.py:312
  54.0 4.9 %collective-permute-start.28 = (bf16[128,128]{1,0:T(8,128)(2,1)S(1)}, bf16[128,128]{1,0:T(8,128)(2,1)S(1)}, u32[]{:S(2)}, u32[]{:S(2)}) collective-permute-start(bf16[128,128]{1,0:T(8,128)(2,1)S(1)} %get-tuple-element.143), channel_id=1, source_target_pairs={{0,16},{1,17},{2,18},{3,19},{4,20},{5,21},{6,22},{7,23},{8,24},{9,... | collective-permute-start | bytes 98312 | tf_op jit(solution)/shard_map/ppermute | solution.py:312
  55.1 3.7 %collective-permute-start.29 = (bf16[128,128]{1,0:T(8,128)(2,1)S(1)}, bf16[128,128]{1,0:T(8,128)(2,1)S(1)}, u32[]{:S(2)}, u32[]{:S(2)}) collective-permute-start(bf16[128,128]{1,0:T(8,128)(2,1)S(1)} %get-tuple-element.144), channel_id=1, source_target_pairs={{0,3},{1,2},{2,1},{3,0},{4,5},{5,4},{6,7},{7,6},{8,9},{9,8},{10,19... | collective-permute-start | bytes 98312 | tf_op jit(solution)/shard_map/ppermute | solution.py:312
  55.1 5.1 %collective-permute-start.30 = (bf16[128,128]{1,0:T(8,128)(2,1)S(1)}, bf16[128,128]{1,0:T(8,128)(2,1)S(1)}, u32[]{:S(2)}, u32[]{:S(2)}) collective-permute-start(bf16[128,128]{1,0:T(8,128)(2,1)S(1)} %get-tuple-element.145), channel_id=1, source_target_pairs={{0,1},{1,0},{2,11},{3,4},{4,3},{5,6},{6,5},{7,8},{8,7},{9,10},{10,... | collective-permute-start | bytes 98312 | tf_op jit(solution)/shard_map/ppermute | solution.py:312
  55.2 5.1 %collective-permute-start.31 = (bf16[128,128]{1,0:T(8,128)(2,1)S(1)}, bf16[128,128]{1,0:T(8,128)(2,1)S(1)}, u32[]{:S(2)}, u32[]{:S(2)}) collective-permute-start(bf16[128,128]{1,0:T(8,128)(2,1)S(1)} %get-tuple-element.146), channel_id=1, source_target_pairs={{0,1},{1,0},{2,3},{3,2},{4,5},{5,4},{6,7},{7,6},{8,9},{9,8},{10,11... | collective-permute-start | bytes 98312 | tf_op jit(solution)/shard_map/ppermute | solution.py:312

commit v10 on v9

--- a/solution.py
+++ b/solution.py
@@ -16,37 +16,52 @@
 BF16 = jnp.bfloat16
 
 
-TURNS = (1, 5, 9, 13)
+FAR_TURNS = (0, 0, 0, 2, 1, 0, 0, 1, 1, 0, 0, 0, 0, 0, 0, 0)
+ODD_TURNS = (1, 0, 1, 0, 1, 1, 1, 1, 1, 0, 2, 0, 2, 1, 1)
+FILL = ((), ((0, 3), (19, 21), (22, 31), (25, 26)), ((2, 18), (20, 23), (24, 27)))
+
+
+def turns(count):
+    far = [FAR_TURNS[i % FAR] for i in range(count)]
+    odd = [ODD_TURNS[(i - 1) // 2] if 0 < i < count - 1 else -1 for i in range(count)]
+    return far, odd
+
+
+def mixed(count):
+    return count == 2 * FAR
 
 
 def swaps(count):
     blocks = count // FAR
     near = [i ^ 1 for i in range(count)]
     far = [i ^ FAR for i in range(count)]
-    if blocks != 2:
-        cross = [(((i + 1) ^ 1) - 1) % count for i in range(count)]
+    odd = [(((i + 1) ^ 1) - 1) % count for i in range(count)]
+    if mixed(count):
+        far_turns, odd_turns = turns(count)
+        pairings = []
+        for turn, fill in enumerate(FILL):
+            pairing = list(near)
+            for i, j in fill:
+                pairing[i], pairing[j] = j, i
+            for i in range(count):
+                if far_turns[i] == turn:
+                    pairing[i] = far[i]
+                elif odd_turns[i] == turn:
+                    pairing[i] = odd[i]
+            pairings.append(pairing)
+        pairings.append(near)
+    else:
         again = [(((i // FAR + 1) ^ 1) - 1) % blocks * FAR + i % FAR for i in range(count)]
-        pairings = [far, again, cross, near] if blocks > 2 else [cross, near]
-    else:
-        split = [[None] * count, [None] * count]
-        for i in range(1, count - 1):
-            split[cross_half(i)][i] = ((i + 1) ^ 1) - 1
-        for half in split:
-            free = [i for i in range(count) if half[i] is None]
-            alone = [i for i in free if i ^ 1 not in free]
-            mates = dict(zip(alone[::2], alone[1::2])) | dict(zip(alone[1::2], alone[::2]))
-            for i in free:
-                half[i] = mates.get(i, i ^ 1)
-        pairings = [far, *split, near]
+        pairings = ([far] if blocks > 1 else []) + ([again] if blocks > 2 else []) + [odd, near]
+    for pairing in pairings:
+        assert all(pairing[j] == i != j for i, j in enumerate(pairing))
     return [list(enumerate(pairing)) for pairing in pairings]
 
 
-def cross_half(index):
-    edge = (index - 1) // 2 if isinstance(index, int) else lax.div(index - 1, 2)
-    half = 0
-    for turn in TURNS:
-        half = half + (edge >= turn) * 1 if isinstance(index, int) else half + jnp.where(edge >= turn, 1, 0)
-    return half % 2 if isinstance(index, int) else lax.rem(half, 2)
+def is_turn(own_turns, turn):
+    bits = sum(1 << i for i, own in enumerate(own_turns) if own == turn)
+    bits = bits - (1 << 32) if bits >> 31 else bits
+    return lax.shift_right_logical(jnp.int32(bits), lax.axis_index("sub")) & 1 == 1
 
 
 def slots_of(index, count):
@@ -69,17 +84,24 @@
 def gather(links, refs):
     parts = [ref[...] for ref in refs]
     if len(parts) > links:
-        half = cross_half(lax.axis_index("sub"))
-        mine = jnp.where(half == 0, parts[1].astype(F32), parts[2].astype(F32))
-        parts[1:3] = [mine.astype(BF16)]
+        values = [part.astype(F32) for part in parts[:3]]
+        picked = []
+        for own in turns(2 * FAR):
+            later = jnp.where(is_turn(own, 1), values[1], values[2])
+            picked.append(jnp.where(is_turn(own, 0), values[0], later).astype(BF16))
+        parts = [*picked, parts[3]]
     return jnp.concatenate(parts, 1)
 
 
 def scatter(links, refs, block):
     share = refs[0].shape[1]
-    columns = [0, 1, 1, 2] if len(refs) > links else range(links)
-    for k, ref in zip(columns, refs):
-        ref[...] = block[:, k * share : (k + 1) * share].astype(ref.dtype)
+    parts = [block[:, k * share : (k + 1) * share].astype(F32) for k in range(links)]
+    if len(refs) > links:
+        far, odd, near = parts
+        own, _ = turns(2 * FAR)
+        parts = [*(jnp.where(is_turn(own, turn), far, odd) for turn in range(3)), near]
+    for ref, part in zip(refs, parts):
+        ref[...] = part.astype(BF16)
 
 
 def open_kernel(
@@ -200,14 +222,18 @@
         refs[1][...] = refs[0][...] + DAMPING * sent
 
 
-def residual_path_kernel(trips, links, *refs):
-    arrived_refs, refs = refs[:trips], refs[trips:]
-    same_ref, s_small_ref, row_ref, base_ref, state_ref, state_out_ref, local_ref = refs[:7]
+def residual_path_kernel(trips, links, last, *refs):
+    arrived_refs, refs = refs[:trips], refs[trips:]
+    same_ref, s_small_ref, row_ref, base_ref, state_ref, local_ref = refs[:6]
     state = state_ref[...] + DAMPING * times(gather(links, arrived_refs), same_ref[...])
-    state_out_ref[...] = state
+    if last:
+        refs = refs[6:]
+    else:
+        refs[6][...] = state
+        refs = refs[7:]
     local = base_ref[...] - times((state * row_ref[2:3]).astype(BF16), s_small_ref[...])
     local_ref[...] = local
-    scatter(links, refs[7:], local)
+    scatter(links, refs, local)
 
 
 def corrected(links, arrived_refs, hot_ref, n_ref, weight_ref, mask_ref, local_ref):
@@ -378,12 +404,15 @@
                 whole + 2 * picks,
             )
         came = arrived
-        near_state, near, *sent = run(
-            bound(residual_path_kernel),
+        ends = step == ITERS - 2
+        near, *sent = run(
+            bound(residual_path_kernel, ends),
             [*came, same, s_small, rows, base, near_state],
-            [some, some, *messages],
+            [some, *([] if ends else [some]), *messages],
             path,
         )
+        if not ends:
+            near_state, *sent = sent
         arrived = exchange(sent)
         state, local, base = run(
             bound(residual_kernel),

time: 61.5 us -> 59.7 us (0.971)
  the two profiles are of different devices: /device:TPU:8 before, /device:TPU:2 now
where the time goes in v10:
time: 59.7 us; the launch traced here: 59.5 us
  starting transfers between devices  25.8 us (43%)
  Pallas kernels  17.8 us (30%)
  waiting for transfers between devices  15.1 us (25%)
  between operations  0.83 us (1%)
    ppermute x32, starting transfers between devices, exchange(): lax.ppermute(part, 'sub', route)  25.8 us
    pallas_call x17, Pallas kernels, run(): pl.pallas_call(kernel, out_shape=results, in_specs=[pl.BlockSpec(memory_s...  17.8 us
    ppermute x32, waiting for transfers between devices, exchange(): lax.ppermute(part, 'sub', route)  15.1 us
  transfers between devices with their start and end apart: 32, of which 17 were waited for; matrix products, arithmetic and copies ran while one was open for 0% of the time, Pallas kernels for 19%

profile of v10, /device:TPU:2, one launch (start us, length us, event | category | flops | bytes accessed | tf_op | source)
XLA Modules:
  0.0 59.5 jit_solution(278316070983679441)
XLA Ops:
  0.0 2.4 %shard_map.73 = (bf16[1024,384]{1,0:T(8,128)(2,1)S(1)}, bf16[128,1024]{1,0:T(8,128)(2,1)S(1)}, bf16[128,384]{1,0:T(8,128)(2,1)S(1)}, f32[1,1024]{1,0:T(1,128)S(1...) custom-call(s32[1,4,128]{2,1,0:T(4,128)} %rows_in.1, ...), custom_call_target="tpu_custom_call" | custom-call | flops 100663296 | bytes 9938960 | tf_op jit(solution)/shard_map/pallas_call | solution.py:303
  2.4 2.7 %collective-permute-start = (bf16[128,128]{1,0:T(8,128)(2,1)S(1)}, bf16[128,128]{1,0:T(8,128)(2,1)S(1)}, u32[]{:S(2)}, u32[]{:S(2)}) collective-permute-start(bf16[128,128]{1,0:T(8,128)(2,1)S(1)} %get-tuple-element.77), channel_id=1, source_target_pairs={{0,16},{1,17},{2,18},{3,4},{4,3},{5,21},{6,22},{7,8},{8,7},{9,25},... | collective-permute-start | bytes 98312 | tf_op jit(solution)/shard_map/ppermute | solution.py:338
  5.4 1.0 %collective-permute-start.3 = (bf16[128,128]{1,0:T(8,128)(2,1)S(1)}, bf16[128,128]{1,0:T(8,128)(2,1)S(1)}, u32[]{:S(2)}, u32[]{:S(2)}) collective-permute-start(bf16[128,128]{1,0:T(8,128)(2,1)S(1)} %get-tuple-element.80), channel_id=1, source_target_pairs={{0,1},{1,0},{2,3},{3,2},{4,5},{5,4},{6,7},{7,6},{8,9},{9,8},{10,11... | collective-permute-start | bytes 98312 | tf_op jit(solution)/shard_map/ppermute | solution.py:338
  7.1 2.2 %shard_map.74 = (bf16[384,1024]{1,0:T(8,128)(2,1)S(1)}, bf16[384,1024]{1,0:T(8,128)(2,1)S(1)}, bf16[384,384]{1,0:T(8,128)(2,1)S(1)}, bf16[384,384]{1,0:T(8,128)(...) custom-call(bf16[1024,384]{1,0:T(8,128)(2,1)S(1)} %get-tuple-element, ...), custom_call_target="tpu_custom_call" | custom-call | flops 1509949440 | bytes 6111236 | tf_op jit(solution)/shard_map/pallas_call | solution.py:303
  9.3 0.6 %collective-permute-done.2.refs_2_ = bf16[128,128]{1,0:T(8,128)(2,1)S(1)} collective-permute-done((bf16[128,128]{1,0:T(8,128)(2,1)S(1)}, bf16[128,128]{1,0:T(8,128)(2,1)S(1)}, u32[]{:S(2)}, u32[]{:S(2)}) %collective-permute-start.2) | collective-permute-done | bytes 32800 | tf_op jit(solution)/shard_map/ppermute | solution.py:338
  9.9 0.4 shard_map.75
  10.3 1.4 %collective-permute-start.4 = (bf16[128,128]{1,0:T(8,128)(2,1)S(1)}, bf16[128,128]{1,0:T(8,128)(2,1)S(1)}, u32[]{:S(2)}, u32[]{:S(2)}) collective-permute-start(bf16[128,128]{1,0:T(8,128)(2,1)S(1)} %get-tuple-element.90), channel_id=1, source_target_pairs={{0,16},{1,17},{2,18},{3,4},{4,3},{5,21},{6,22},{7,8},{8,7},{9,25},... | collective-permute-start | bytes 98312 | tf_op jit(solution)/shard_map/ppermute | solution.py:338
  11.8 1.2 %collective-permute-start.5 = (bf16[128,128]{1,0:T(8,128)(2,1)S(1)}, bf16[128,128]{1,0:T(8,128)(2,1)S(1)}, u32[]{:S(2)}, u32[]{:S(2)}) collective-permute-start(bf16[128,128]{1,0:T(8,128)(2,1)S(1)} %get-tuple-element.91), channel_id=1, source_target_pairs={{0,3},{1,2},{2,1},{3,0},{4,20},{5,6},{6,5},{7,23},{8,24},{9,10},{1... | collective-permute-start | bytes 98312 | tf_op jit(solution)/shard_map/ppermute | solution.py:338
  12.9 0.4 collective-permute-start.6
  13.4 0.8 %collective-permute-start.7 = (bf16[128,128]{1,0:T(8,128)(2,1)S(1)}, bf16[128,128]{1,0:T(8,128)(2,1)S(1)}, u32[]{:S(2)}, u32[]{:S(2)}) collective-permute-start(bf16[128,128]{1,0:T(8,128)(2,1)S(1)} %get-tuple-element.93), channel_id=1, source_target_pairs={{0,1},{1,0},{2,3},{3,2},{4,5},{5,4},{6,7},{7,6},{8,9},{9,8},{10,11... | collective-permute-start | bytes 98312 | tf_op jit(solution)/shard_map/ppermute | solution.py:338
  14.2 2.7 %shard_map.76 = (f32[128,1024]{1,0:T(8,128)S(1)}, f32[128,384]{1,0:T(8,128)S(1)}, bf16[1024,384]{1,0:T(8,128)(2,1)S(1)}, bf16[384,384]{1,0:T(8,128)(2,1)S(1)}) custom-call(bf16[128,128]{1,0:T(8,128)(2,1)S(1)} %collective-permute-done.refs_0_, bf16[128,128]{1,0:T(8,128)(2,1)S(1)} %collective-permute-done.1.refs_1_, ...), custom_call_target="tpu_custom_call" | custom-call | flops 1577058304 | bytes 8392704 | tf_op jit(solution)/shard_map/pallas_call | solution.py:303
  16.9 1.0 %collective-permute-done.6.refs_2_ = bf16[128,128]{1,0:T(8,128)(2,1)S(1)} collective-permute-done((bf16[128,128]{1,0:T(8,128)(2,1)S(1)}, bf16[128,128]{1,0:T(8,128)(2,1)S(1)}, u32[]{:S(2)}, u32[]{:S(2)}) %collective-permute-start.6) | collective-permute-done | bytes 32800 | tf_op jit(solution)/shard_map/ppermute | solution.py:338
  17.9 0.4 shard_map.77
  18.3 1.3 %collective-permute-start.8 = (bf16[128,128]{1,0:T(8,128)(2,1)S(1)}, bf16[128,128]{1,0:T(8,128)(2,1)S(1)}, u32[]{:S(2)}, u32[]{:S(2)}) collective-permute-start(bf16[128,128]{1,0:T(8,128)(2,1)S(1)} %get-tuple-element.102), channel_id=1, source_target_pairs={{0,16},{1,17},{2,18},{3,4},{4,3},{5,21},{6,22},{7,8},{8,7},{9,25},... | collective-permute-start | bytes 98312 | tf_op jit(solution)/shard_map/ppermute | solution.py:338
  19.6 1.7 %collective-permute-start.10 = (bf16[128,128]{1,0:T(8,128)(2,1)S(1)}, bf16[128,128]{1,0:T(8,128)(2,1)S(1)}, u32[]{:S(2)}, u32[]{:S(2)}) collective-permute-start(bf16[128,128]{1,0:T(8,128)(2,1)S(1)} %get-tuple-element.104), channel_id=1, source_target_pairs={{0,1},{1,0},{2,18},{3,19},{4,5},{5,4},{6,7},{7,6},{8,9},{9,8},{10,... | collective-permute-start | bytes 98312 | tf_op jit(solution)/shard_map/ppermute | solution.py:338
  21.3 1.0 %shard_map.78 = (f32[128,1024]{1,0:T(8,128)S(1)}, f32[128,1024]{1,0:T(8,128)S(1)}, f32[128,384]{1,0:T(8,128)S(1)}) custom-call(bf16[128,128]{1,0:T(8,128)(2,1)S(1)} %collective-permute-done.4.refs_0_, bf16[128,128]{1,0:T(8,128)(2,1)S(1)} %collective-permute-done.5.refs_1_, bf16[128,128]{1,0:T(8,128)(2,1)S(1)} %collective-permute-done.6.refs_2_, ...), custom_call_target="tpu_custom_call" | custom-call | flops 469762048 | bytes 5902336 | tf_op jit(solution)/shard_map/pallas_call | solution.py:303
  22.3 0.9 %collective-permute-done.8.refs_0_ = bf16[128,128]{1,0:T(8,128)(2,1)S(1)} collective-permute-done((bf16[128,128]{1,0:T(8,128)(2,1)S(1)}, bf16[128,128]{1,0:T(8,128)(2,1)S(1)}, u32[]{:S(2)}, u32[]{:S(2)}) %collective-permute-start.8) | collective-permute-done | bytes 32800 | tf_op jit(solution)/shard_map/ppermute | solution.py:338
  23.2 1.2 %collective-permute-done.10.refs_2_ = bf16[128,128]{1,0:T(8,128)(2,1)S(1)} collective-permute-done((bf16[128,128]{1,0:T(8,128)(2,1)S(1)}, bf16[128,128]{1,0:T(8,128)(2,1)S(1)}, u32[]{:S(2)}, u32[]{:S(2)}) %collective-permute-start.10) | collective-permute-done | bytes 32800 | tf_op jit(solution)/shard_map/ppermute | solution.py:338
  24.4 0.4 shard_map.79
  24.8 1.8 %collective-permute-start.12 = (bf16[128,128]{1,0:T(8,128)(2,1)S(1)}, bf16[128,128]{1,0:T(8,128)(2,1)S(1)}, u32[]{:S(2)}, u32[]{:S(2)}) collective-permute-start(bf16[128,128]{1,0:T(8,128)(2,1)S(1)} %get-tuple-element.111), channel_id=1, source_target_pairs={{0,16},{1,17},{2,18},{3,4},{4,3},{5,21},{6,22},{7,8},{8,7},{9,25},... | collective-permute-start | bytes 98312 | tf_op jit(solution)/shard_map/ppermute | solution.py:338
  26.6 1.2 %collective-permute-start.14 = (bf16[128,128]{1,0:T(8,128)(2,1)S(1)}, bf16[128,128]{1,0:T(8,128)(2,1)S(1)}, u32[]{:S(2)}, u32[]{:S(2)}) collective-permute-start(bf16[128,128]{1,0:T(8,128)(2,1)S(1)} %get-tuple-element.113), channel_id=1, source_target_pairs={{0,1},{1,0},{2,18},{3,19},{4,5},{5,4},{6,7},{7,6},{8,9},{9,8},{10,... | collective-permute-start | bytes 98312 | tf_op jit(solution)/shard_map/ppermute | solution.py:338
  27.8 1.2 %shard_map.80 = (f32[128,1024]{1,0:T(8,128)S(1)}, f32[128,384]{1,0:T(8,128)S(1)}) custom-call(bf16[128,128]{1,0:T(8,128)(2,1)S(1)} %collective-permute-done.8.refs_0_, bf16[128,128]{1,0:T(8,128)(2,1)S(1)} %collective-permute-done.9.refs_1_, bf16[128,128]{1,0:T(8,128)(2,1)S(1)} %collective-permute-done.10.refs_2_, ...), custom_call_target="tpu_custom_call" | custom-call | flops 469762048 | bytes 5738496 | tf_op jit(solution)/shard_map/pallas_call | solution.py:303
  29.1 0.6 %collective-permute-done.12.refs_0_ = bf16[128,128]{1,0:T(8,128)(2,1)S(1)} collective-permute-done((bf16[128,128]{1,0:T(8,128)(2,1)S(1)}, bf16[128,128]{1,0:T(8,128)(2,1)S(1)}, u32[]{:S(2)}, u32[]{:S(2)}) %collective-permute-start.12) | collective-permute-done | bytes 32800 | tf_op jit(solution)/shard_map/ppermute | solution.py:338
  29.7 0.4 collective-permute-done.13.refs_1_
  30.1 1.3 %collective-permute-done.14.refs_2_ = bf16[128,128]{1,0:T(8,128)(2,1)S(1)} collective-permute-done((bf16[128,128]{1,0:T(8,128)(2,1)S(1)}, bf16[128,128]{1,0:T(8,128)(2,1)S(1)}, u32[]{:S(2)}, u32[]{:S(2)}) %collective-permute-start.14) | collective-permute-done | bytes 32800 | tf_op jit(solution)/shard_map/ppermute | solution.py:338
  31.4 0.4 shard_map.81
  31.8 1.3 %collective-permute-start.16 = (bf16[128,128]{1,0:T(8,128)(2,1)S(1)}, bf16[128,128]{1,0:T(8,128)(2,1)S(1)}, u32[]{:S(2)}, u32[]{:S(2)}) collective-permute-start(bf16[128,128]{1,0:T(8,128)(2,1)S(1)} %get-tuple-element.120), channel_id=1, source_target_pairs={{0,16},{1,17},{2,18},{3,4},{4,3},{5,21},{6,22},{7,8},{8,7},{9,25},... | collective-permute-start | bytes 98312 | tf_op jit(solution)/shard_map/ppermute | solution.py:338
  33.1 1.7 %collective-permute-start.18 = (bf16[128,128]{1,0:T(8,128)(2,1)S(1)}, bf16[128,128]{1,0:T(8,128)(2,1)S(1)}, u32[]{:S(2)}, u32[]{:S(2)}) collective-permute-start(bf16[128,128]{1,0:T(8,128)(2,1)S(1)} %get-tuple-element.122), channel_id=1, source_target_pairs={{0,1},{1,0},{2,18},{3,19},{4,5},{5,4},{6,7},{7,6},{8,9},{9,8},{10,... | collective-permute-start | bytes 98312 | tf_op jit(solution)/shard_map/ppermute | solution.py:338
  34.8 1.0 %shard_map.82 = (f32[128,1024]{1,0:T(8,128)S(1)}, f32[128,1024]{1,0:T(8,128)S(1)}, f32[128,384]{1,0:T(8,128)S(1)}) custom-call(bf16[128,128]{1,0:T(8,128)(2,1)S(1)} %collective-permute-done.12.refs_0_, bf16[128,128]{1,0:T(8,128)(2,1)S(1)} %collective-permute-done.13.refs_1_, bf16[128,128]{1,0:T(8,128)(2,1)S(1)} %collective-permute-done.14.refs_2_, ...), custom_call_target="tpu_custom_call" | custom-call | flops 469762048 | bytes 5902336 | tf_op jit(solution)/shard_map/pallas_call | solution.py:303
  35.8 0.9 %collective-permute-done.16.refs_0_ = bf16[128,128]{1,0:T(8,128)(2,1)S(1)} collective-permute-done((bf16[128,128]{1,0:T(8,128)(2,1)S(1)}, bf16[128,128]{1,0:T(8,128)(2,1)S(1)}, u32[]{:S(2)}, u32[]{:S(2)}) %collective-permute-start.16) | collective-permute-done | bytes 32800 | tf_op jit(solution)/shard_map/ppermute | solution.py:338
  36.7 1.2 %collective-permute-done.18.refs_2_ = bf16[128,128]{1,0:T(8,128)(2,1)S(1)} collective-permute-done((bf16[128,128]{1,0:T(8,128)(2,1)S(1)}, bf16[128,128]{1,0:T(8,128)(2,1)S(1)}, u32[]{:S(2)}, u32[]{:S(2)}) %collective-permute-start.18) | collective-permute-done | bytes 32800 | tf_op jit(solution)/shard_map/ppermute | solution.py:338
  37.9 0.4 shard_map.83
  38.3 1.8 %collective-permute-start.20 = (bf16[128,128]{1,0:T(8,128)(2,1)S(1)}, bf16[128,128]{1,0:T(8,128)(2,1)S(1)}, u32[]{:S(2)}, u32[]{:S(2)}) collective-permute-start(bf16[128,128]{1,0:T(8,128)(2,1)S(1)} %get-tuple-element.128), channel_id=1, source_target_pairs={{0,16},{1,17},{2,18},{3,4},{4,3},{5,21},{6,22},{7,8},{8,7},{9,25},... | collective-permute-start | bytes 98312 | tf_op jit(solution)/shard_map/ppermute | solution.py:338
  40.1 1.2 %collective-permute-start.22 = (bf16[128,128]{1,0:T(8,128)(2,1)S(1)}, bf16[128,128]{1,0:T(8,128)(2,1)S(1)}, u32[]{:S(2)}, u32[]{:S(2)}) collective-permute-start(bf16[128,128]{1,0:T(8,128)(2,1)S(1)} %get-tuple-element.130), channel_id=1, source_target_pairs={{0,1},{1,0},{2,18},{3,19},{4,5},{5,4},{6,7},{7,6},{8,9},{9,8},{10,... | collective-permute-start | bytes 98312 | tf_op jit(solution)/shard_map/ppermute | solution.py:338
  41.3 1.2 %shard_map.84 = (f32[128,1024]{1,0:T(8,128)S(1)}, f32[128,384]{1,0:T(8,128)S(1)}) custom-call(bf16[128,128]{1,0:T(8,128)(2,1)S(1)} %collective-permute-done.16.refs_0_, bf16[128,128]{1,0:T(8,128)(2,1)S(1)} %collective-permute-done.17.refs_1_, bf16[128,128]{1,0:T(8,128)(2,1)S(1)} %collective-permute-done.18.refs_2_, ...), custom_call_target="tpu_custom_call" | custom-call | flops 469762048 | bytes 5738496 | tf_op jit(solution)/shard_map/pallas_call | solution.py:303
  42.6 0.8 %collective-permute-done.20.refs_0_ = bf16[128,128]{1,0:T(8,128)(2,1)S(1)} collective-permute-done((bf16[128,128]{1,0:T(8,128)(2,1)S(1)}, bf16[128,128]{1,0:T(8,128)(2,1)S(1)}, u32[]{:S(2)}, u32[]{:S(2)}) %collective-permute-start.20) | collective-permute-done | bytes 32800 | tf_op jit(solution)/shard_map/ppermute | solution.py:338
  43.5 1.5 %collective-permute-done.22.refs_2_ = bf16[128,128]{1,0:T(8,128)(2,1)S(1)} collective-permute-done((bf16[128,128]{1,0:T(8,128)(2,1)S(1)}, bf16[128,128]{1,0:T(8,128)(2,1)S(1)}, u32[]{:S(2)}, u32[]{:S(2)}) %collective-permute-start.22) | collective-permute-done | bytes 32800 | tf_op jit(solution)/shard_map/ppermute | solution.py:338
  45.3 1.3 %collective-permute-start.24 = (bf16[128,128]{1,0:T(8,128)(2,1)S(1)}, bf16[128,128]{1,0:T(8,128)(2,1)S(1)}, u32[]{:S(2)}, u32[]{:S(2)}) collective-permute-start(bf16[128,128]{1,0:T(8,128)(2,1)S(1)} %get-tuple-element.136), channel_id=1, source_target_pairs={{0,16},{1,17},{2,18},{3,4},{4,3},{5,21},{6,22},{7,8},{8,7},{9,25},... | collective-permute-start | bytes 98312 | tf_op jit(solution)/shard_map/ppermute | solution.py:338
  46.6 1.7 %collective-permute-start.26 = (bf16[128,128]{1,0:T(8,128)(2,1)S(1)}, bf16[128,128]{1,0:T(8,128)(2,1)S(1)}, u32[]{:S(2)}, u32[]{:S(2)}) collective-permute-start(bf16[128,128]{1,0:T(8,128)(2,1)S(1)} %get-tuple-element.138), channel_id=1, source_target_pairs={{0,1},{1,0},{2,18},{3,19},{4,5},{5,4},{6,7},{7,6},{8,9},{9,8},{10,... | collective-permute-start | bytes 98312 | tf_op jit(solution)/shard_map/ppermute | solution.py:338
  48.3 1.0 %shard_map.86 = (f32[128,1024]{1,0:T(8,128)S(1)}, f32[128,1024]{1,0:T(8,128)S(1)}, f32[128,384]{1,0:T(8,128)S(1)}) custom-call(bf16[128,128]{1,0:T(8,128)(2,1)S(1)} %collective-permute-done.20.refs_0_, bf16[128,128]{1,0:T(8,128)(2,1)S(1)} %collective-permute-done.21.refs_1_, bf16[128,128]{1,0:T(8,128)(2,1)S(1)} %collective-permute-done.22.refs_2_, ...), custom_call_target="tpu_custom_call" | custom-call | flops 469762048 | bytes 5902336 | tf_op jit(solution)/shard_map/pallas_call | solution.py:303
  49.3 0.9 %collective-permute-done.24.refs_0_ = bf16[128,128]{1,0:T(8,128)(2,1)S(1)} collective-permute-done((bf16[128,128]{1,0:T(8,128)(2,1)S(1)}, bf16[128,128]{1,0:T(8,128)(2,1)S(1)}, u32[]{:S(2)}, u32[]{:S(2)}) %collective-permute-start.24) | collective-permute-done | bytes 32800 | tf_op jit(solution)/shard_map/ppermute | solution.py:338
  50.2 1.2 %collective-permute-done.26.refs_2_ = bf16[128,128]{1,0:T(8,128)(2,1)S(1)} collective-permute-done((bf16[128,128]{1,0:T(8,128)(2,1)S(1)}, bf16[128,128]{1,0:T(8,128)(2,1)S(1)}, u32[]{:S(2)}, u32[]{:S(2)}) %collective-permute-start.26) | collective-permute-done | bytes 32800 | tf_op jit(solution)/shard_map/ppermute | solution.py:338
  51.8 1.8 %collective-permute-start.28 = (bf16[128,128]{1,0:T(8,128)(2,1)S(1)}, bf16[128,128]{1,0:T(8,128)(2,1)S(1)}, u32[]{:S(2)}, u32[]{:S(2)}) collective-permute-start(bf16[128,128]{1,0:T(8,128)(2,1)S(1)} %get-tuple-element.143), channel_id=1, source_target_pairs={{0,16},{1,17},{2,18},{3,4},{4,3},{5,21},{6,22},{7,8},{8,7},{9,25},... | collective-permute-start | bytes 98312 | tf_op jit(solution)/shard_map/ppermute | solution.py:338
  53.6 1.2 %collective-permute-start.30 = (bf16[128,128]{1,0:T(8,128)(2,1)S(1)}, bf16[128,128]{1,0:T(8,128)(2,1)S(1)}, u32[]{:S(2)}, u32[]{:S(2)}) collective-permute-start(bf16[128,128]{1,0:T(8,128)(2,1)S(1)} %get-tuple-element.145), channel_id=1, source_target_pairs={{0,1},{1,0},{2,18},{3,19},{4,5},{5,4},{6,7},{7,6},{8,9},{9,8},{10,... | collective-permute-start | bytes 98312 | tf_op jit(solution)/shard_map/ppermute | solution.py:338
  54.8 1.2 %shard_map.88.refs_5_ = f32[1024,128]{1,0:T(8,128)S(1)} custom-call(bf16[128,128]{1,0:T(8,128)(2,1)S(1)} %collective-permute-done.24.refs_0_, bf16[128,128]{1,0:T(8,128)(2,1)S(1)} %collective-permute-done.25.refs_1_, bf16[128,128]{1,0:T(8,128)(2,1)S(1)} %collective-permute-done.26.refs_2_, bf16[128,128]{1,0:T(8,128)(2,1)S(1)} %collective-permute-done.27.refs_3_, ...), custom_call_target="tpu_custom_call" | custom-call | flops 369098752 | bytes 4624384 | tf_op jit(solution)/shard_map/pallas_call | solution.py:303
  56.0 0.9 %collective-permute-done.28.refs_0_ = bf16[128,128]{1,0:T(8,128)(2,1)S(1)} collective-permute-done((bf16[128,128]{1,0:T(8,128)(2,1)S(1)}, bf16[128,128]{1,0:T(8,128)(2,1)S(1)}, u32[]{:S(2)}, u32[]{:S(2)}) %collective-permute-start.28) | collective-permute-done | bytes 32800 | tf_op jit(solution)/shard_map/ppermute | solution.py:338
  56.9 1.5 %collective-permute-done.30.refs_2_ = bf16[128,128]{1,0:T(8,128)(2,1)S(1)} collective-permute-done((bf16[128,128]{1,0:T(8,128)(2,1)S(1)}, bf16[128,128]{1,0:T(8,128)(2,1)S(1)}, u32[]{:S(2)}, u32[]{:S(2)}) %collective-permute-start.30) | collective-permute-done | bytes 32800 | tf_op jit(solution)/shard_map/ppermute | solution.py:338
  58.4 1.1 %shard_map.89 = f32[1,1024,128]{2,1,0:T(8,128)} custom-call(bf16[128,128]{1,0:T(8,128)(2,1)S(1)} %collective-permute-done.28.refs_0_, bf16[128,128]{1,0:T(8,128)(2,1)S(1)} %collective-permute-done.29.refs_1_, bf16[128,128]{1,0:T(8,128)(2,1)S(1)} %collective-permute-done.30.refs_2_, bf16[128,128]{1,0:T(8,128)(2,1)S(1)} %collective-permute-done.31.refs_3_, ...), custom_call_target="tpu_custom_call" | custom-call | flops 100663296 | bytes 1966080 | tf_op jit(solution)/shard_map/pallas_call | solution.py:303
  (33 shorter events, 1.3 us)
Async XLA Ops:
  2.4 6.9 %collective-permute-start = (bf16[128,128]{1,0:T(8,128)(2,1)S(1)}, bf16[128,128]{1,0:T(8,128)(2,1)S(1)}, u32[]{:S(2)}, u32[]{:S(2)}) collective-permute-start(bf16[128,128]{1,0:T(8,128)(2,1)S(1)} %get-tuple-element.77), channel_id=1, source_target_pairs={{0,16},{1,17},{2,18},{3,4},{4,3},{5,21},{6,22},{7,8},{8,7},{9,25},... | collective-permute-start | bytes 98312 | tf_op jit(solution)/shard_map/ppermute | solution.py:338
  5.1 4.2 %collective-permute-start.1 = (bf16[128,128]{1,0:T(8,128)(2,1)S(1)}, bf16[128,128]{1,0:T(8,128)(2,1)S(1)}, u32[]{:S(2)}, u32[]{:S(2)}) collective-permute-start(bf16[128,128]{1,0:T(8,128)(2,1)S(1)} %get-tuple-element.78), channel_id=1, source_target_pairs={{0,3},{1,2},{2,1},{3,0},{4,20},{5,6},{6,5},{7,23},{8,24},{9,10},{1... | collective-permute-start | bytes 98312 | tf_op jit(solution)/shard_map/ppermute | solution.py:338
  5.1 4.8 %collective-permute-start.2 = (bf16[128,128]{1,0:T(8,128)(2,1)S(1)}, bf16[128,128]{1,0:T(8,128)(2,1)S(1)}, u32[]{:S(2)}, u32[]{:S(2)}) collective-permute-start(bf16[128,128]{1,0:T(8,128)(2,1)S(1)} %get-tuple-element.79), channel_id=1, source_target_pairs={{0,1},{1,0},{2,18},{3,19},{4,5},{5,4},{6,7},{7,6},{8,9},{9,8},{10,... | collective-permute-start | bytes 98312 | tf_op jit(solution)/shard_map/ppermute | solution.py:338
  5.4 4.5 %collective-permute-start.3 = (bf16[128,128]{1,0:T(8,128)(2,1)S(1)}, bf16[128,128]{1,0:T(8,128)(2,1)S(1)}, u32[]{:S(2)}, u32[]{:S(2)}) collective-permute-start(bf16[128,128]{1,0:T(8,128)(2,1)S(1)} %get-tuple-element.80), channel_id=1, source_target_pairs={{0,1},{1,0},{2,3},{3,2},{4,5},{5,4},{6,7},{7,6},{8,9},{9,8},{10,11... | collective-permute-start | bytes 98312 | tf_op jit(solution)/shard_map/ppermute | solution.py:338
  10.3 6.6 %collective-permute-start.4 = (bf16[128,128]{1,0:T(8,128)(2,1)S(1)}, bf16[128,128]{1,0:T(8,128)(2,1)S(1)}, u32[]{:S(2)}, u32[]{:S(2)}) collective-permute-start(bf16[128,128]{1,0:T(8,128)(2,1)S(1)} %get-tuple-element.90), channel_id=1, source_target_pairs={{0,16},{1,17},{2,18},{3,4},{4,3},{5,21},{6,22},{7,8},{8,7},{9,25},... | collective-permute-start | bytes 98312 | tf_op jit(solution)/shard_map/ppermute | solution.py:338
  11.8 5.1 %collective-permute-start.5 = (bf16[128,128]{1,0:T(8,128)(2,1)S(1)}, bf16[128,128]{1,0:T(8,128)(2,1)S(1)}, u32[]{:S(2)}, u32[]{:S(2)}) collective-permute-start(bf16[128,128]{1,0:T(8,128)(2,1)S(1)} %get-tuple-element.91), channel_id=1, source_target_pairs={{0,3},{1,2},{2,1},{3,0},{4,20},{5,6},{6,5},{7,23},{8,24},{9,10},{1... | collective-permute-start | bytes 98312 | tf_op jit(solution)/shard_map/ppermute | solution.py:338
  12.9 5.0 %collective-permute-start.6 = (bf16[128,128]{1,0:T(8,128)(2,1)S(1)}, bf16[128,128]{1,0:T(8,128)(2,1)S(1)}, u32[]{:S(2)}, u32[]{:S(2)}) collective-permute-start(bf16[128,128]{1,0:T(8,128)(2,1)S(1)} %get-tuple-element.92), channel_id=1, source_target_pairs={{0,1},{1,0},{2,18},{3,19},{4,5},{5,4},{6,7},{7,6},{8,9},{9,8},{10,... | collective-permute-start | bytes 98312 | tf_op jit(solution)/shard_map/ppermute | solution.py:338
  13.4 4.5 %collective-permute-start.7 = (bf16[128,128]{1,0:T(8,128)(2,1)S(1)}, bf16[128,128]{1,0:T(8,128)(2,1)S(1)}, u32[]{:S(2)}, u32[]{:S(2)}) collective-permute-start(bf16[128,128]{1,0:T(8,128)(2,1)S(1)} %get-tuple-element.93), channel_id=1, source_target_pairs={{0,1},{1,0},{2,3},{3,2},{4,5},{5,4},{6,7},{7,6},{8,9},{9,8},{10,11... | collective-permute-start | bytes 98312 | tf_op jit(solution)/shard_map/ppermute | solution.py:338
  18.3 4.9 %collective-permute-start.8 = (bf16[128,128]{1,0:T(8,128)(2,1)S(1)}, bf16[128,128]{1,0:T(8,128)(2,1)S(1)}, u32[]{:S(2)}, u32[]{:S(2)}) collective-permute-start(bf16[128,128]{1,0:T(8,128)(2,1)S(1)} %get-tuple-element.102), channel_id=1, source_target_pairs={{0,16},{1,17},{2,18},{3,4},{4,3},{5,21},{6,22},{7,8},{8,7},{9,25},... | collective-permute-start | bytes 98312 | tf_op jit(solution)/shard_map/ppermute | solution.py:338
  19.6 3.6 %collective-permute-start.9 = (bf16[128,128]{1,0:T(8,128)(2,1)S(1)}, bf16[128,128]{1,0:T(8,128)(2,1)S(1)}, u32[]{:S(2)}, u32[]{:S(2)}) collective-permute-start(bf16[128,128]{1,0:T(8,128)(2,1)S(1)} %get-tuple-element.103), channel_id=1, source_target_pairs={{0,3},{1,2},{2,1},{3,0},{4,20},{5,6},{6,5},{7,23},{8,24},{9,10},{1... | collective-permute-start | bytes 98312 | tf_op jit(solution)/shard_map/ppermute | solution.py:338
  19.6 4.8 %collective-permute-start.10 = (bf16[128,128]{1,0:T(8,128)(2,1)S(1)}, bf16[128,128]{1,0:T(8,128)(2,1)S(1)}, u32[]{:S(2)}, u32[]{:S(2)}) collective-permute-start(bf16[128,128]{1,0:T(8,128)(2,1)S(1)} %get-tuple-element.104), channel_id=1, source_target_pairs={{0,1},{1,0},{2,18},{3,19},{4,5},{5,4},{6,7},{7,6},{8,9},{9,8},{10,... | collective-permute-start | bytes 98312 | tf_op jit(solution)/shard_map/ppermute | solution.py:338
  21.3 3.1 %collective-permute-start.11 = (bf16[128,128]{1,0:T(8,128)(2,1)S(1)}, bf16[128,128]{1,0:T(8,128)(2,1)S(1)}, u32[]{:S(2)}, u32[]{:S(2)}) collective-permute-start(bf16[128,128]{1,0:T(8,128)(2,1)S(1)} %get-tuple-element.105), channel_id=1, source_target_pairs={{0,1},{1,0},{2,3},{3,2},{4,5},{5,4},{6,7},{7,6},{8,9},{9,8},{10,11... | collective-permute-start | bytes 98312 | tf_op jit(solution)/shard_map/ppermute | solution.py:338
  24.8 4.9 %collective-permute-start.12 = (bf16[128,128]{1,0:T(8,128)(2,1)S(1)}, bf16[128,128]{1,0:T(8,128)(2,1)S(1)}, u32[]{:S(2)}, u32[]{:S(2)}) collective-permute-start(bf16[128,128]{1,0:T(8,128)(2,1)S(1)} %get-tuple-element.111), channel_id=1, source_target_pairs={{0,16},{1,17},{2,18},{3,4},{4,3},{5,21},{6,22},{7,8},{8,7},{9,25},... | collective-permute-start | bytes 98312 | tf_op jit(solution)/shard_map/ppermute | solution.py:338
  26.6 3.5 %collective-permute-start.13 = (bf16[128,128]{1,0:T(8,128)(2,1)S(1)}, bf16[128,128]{1,0:T(8,128)(2,1)S(1)}, u32[]{:S(2)}, u32[]{:S(2)}) collective-permute-start(bf16[128,128]{1,0:T(8,128)(2,1)S(1)} %get-tuple-element.112), channel_id=1, source_target_pairs={{0,3},{1,2},{2,1},{3,0},{4,20},{5,6},{6,5},{7,23},{8,24},{9,10},{1... | collective-permute-start | bytes 98312 | tf_op jit(solution)/shard_map/ppermute | solution.py:338
  26.6 4.8 %collective-permute-start.14 = (bf16[128,128]{1,0:T(8,128)(2,1)S(1)}, bf16[128,128]{1,0:T(8,128)(2,1)S(1)}, u32[]{:S(2)}, u32[]{:S(2)}) collective-permute-start(bf16[128,128]{1,0:T(8,128)(2,1)S(1)} %get-tuple-element.113), channel_id=1, source_target_pairs={{0,1},{1,0},{2,18},{3,19},{4,5},{5,4},{6,7},{7,6},{8,9},{9,8},{10,... | collective-permute-start | bytes 98312 | tf_op jit(solution)/shard_map/ppermute | solution.py:338
  27.8 3.6 %collective-permute-start.15 = (bf16[128,128]{1,0:T(8,128)(2,1)S(1)}, bf16[128,128]{1,0:T(8,128)(2,1)S(1)}, u32[]{:S(2)}, u32[]{:S(2)}) collective-permute-start(bf16[128,128]{1,0:T(8,128)(2,1)S(1)} %get-tuple-element.114), channel_id=1, source_target_pairs={{0,1},{1,0},{2,3},{3,2},{4,5},{5,4},{6,7},{7,6},{8,9},{9,8},{10,11... | collective-permute-start | bytes 98312 | tf_op jit(solution)/shard_map/ppermute | solution.py:338
  31.8 4.9 %collective-permute-start.16 = (bf16[128,128]{1,0:T(8,128)(2,1)S(1)}, bf16[128,128]{1,0:T(8,128)(2,1)S(1)}, u32[]{:S(2)}, u32[]{:S(2)}) collective-permute-start(bf16[128,128]{1,0:T(8,128)(2,1)S(1)} %get-tuple-element.120), channel_id=1, source_target_pairs={{0,16},{1,17},{2,18},{3,4},{4,3},{5,21},{6,22},{7,8},{8,7},{9,25},... | collective-permute-start | bytes 98312 | tf_op jit(solution)/shard_map/ppermute | solution.py:338
  33.1 3.6 %collective-permute-start.17 = (bf16[128,128]{1,0:T(8,128)(2,1)S(1)}, bf16[128,128]{1,0:T(8,128)(2,1)S(1)}, u32[]{:S(2)}, u32[]{:S(2)}) collective-permute-start(bf16[128,128]{1,0:T(8,128)(2,1)S(1)} %get-tuple-element.121), channel_id=1, source_target_pairs={{0,3},{1,2},{2,1},{3,0},{4,20},{5,6},{6,5},{7,23},{8,24},{9,10},{1... | collective-permute-start | bytes 98312 | tf_op jit(solution)/shard_map/ppermute | solution.py:338
  33.1 4.8 %collective-permute-start.18 = (bf16[128,128]{1,0:T(8,128)(2,1)S(1)}, bf16[128,128]{1,0:T(8,128)(2,1)S(1)}, u32[]{:S(2)}, u32[]{:S(2)}) collective-permute-start(bf16[128,128]{1,0:T(8,128)(2,1)S(1)} %get-tuple-element.122), channel_id=1, source_target_pairs={{0,1},{1,0},{2,18},{3,19},{4,5},{5,4},{6,7},{7,6},{8,9},{9,8},{10,... | collective-permute-start | bytes 98312 | tf_op jit(solution)/shard_map/ppermute | solution.py:338
  34.8 3.1 %collective-permute-start.19 = (bf16[128,128]{1,0:T(8,128)(2,1)S(1)}, bf16[128,128]{1,0:T(8,128)(2,1)S(1)}, u32[]{:S(2)}, u32[]{:S(2)}) collective-permute-start(bf16[128,128]{1,0:T(8,128)(2,1)S(1)} %get-tuple-element.123), channel_id=1, source_target_pairs={{0,1},{1,0},{2,3},{3,2},{4,5},{5,4},{6,7},{7,6},{8,9},{9,8},{10,11... | collective-permute-start | bytes 98312 | tf_op jit(solution)/shard_map/ppermute | solution.py:338
  38.3 5.0 %collective-permute-start.20 = (bf16[128,128]{1,0:T(8,128)(2,1)S(1)}, bf16[128,128]{1,0:T(8,128)(2,1)S(1)}, u32[]{:S(2)}, u32[]{:S(2)}) collective-permute-start(bf16[128,128]{1,0:T(8,128)(2,1)S(1)} %get-tuple-element.128), channel_id=1, source_target_pairs={{0,16},{1,17},{2,18},{3,4},{4,3},{5,21},{6,22},{7,8},{8,7},{9,25},... | collective-permute-start | bytes 98312 | tf_op jit(solution)/shard_map/ppermute | solution.py:338
  40.1 3.3 %collective-permute-start.21 = (bf16[128,128]{1,0:T(8,128)(2,1)S(1)}, bf16[128,128]{1,0:T(8,128)(2,1)S(1)}, u32[]{:S(2)}, u32[]{:S(2)}) collective-permute-start(bf16[128,128]{1,0:T(8,128)(2,1)S(1)} %get-tuple-element.129), channel_id=1, source_target_pairs={{0,3},{1,2},{2,1},{3,0},{4,20},{5,6},{6,5},{7,23},{8,24},{9,10},{1... | collective-permute-start | bytes 98312 | tf_op jit(solution)/shard_map/ppermute | solution.py:338
  40.1 4.8 %collective-permute-start.22 = (bf16[128,128]{1,0:T(8,128)(2,1)S(1)}, bf16[128,128]{1,0:T(8,128)(2,1)S(1)}, u32[]{:S(2)}, u32[]{:S(2)}) collective-permute-start(bf16[128,128]{1,0:T(8,128)(2,1)S(1)} %get-tuple-element.130), channel_id=1, source_target_pairs={{0,1},{1,0},{2,18},{3,19},{4,5},{5,4},{6,7},{7,6},{8,9},{9,8},{10,... | collective-permute-start | bytes 98312 | tf_op jit(solution)/shard_map/ppermute | solution.py:338
  41.3 3.6 %collective-permute-start.23 = (bf16[128,128]{1,0:T(8,128)(2,1)S(1)}, bf16[128,128]{1,0:T(8,128)(2,1)S(1)}, u32[]{:S(2)}, u32[]{:S(2)}) collective-permute-start(bf16[128,128]{1,0:T(8,128)(2,1)S(1)} %get-tuple-element.131), channel_id=1, source_target_pairs={{0,1},{1,0},{2,3},{3,2},{4,5},{5,4},{6,7},{7,6},{8,9},{9,8},{10,11... | collective-permute-start | bytes 98312 | tf_op jit(solution)/shard_map/ppermute | solution.py:338
  45.3 4.9 %collective-permute-start.24 = (bf16[128,128]{1,0:T(8,128)(2,1)S(1)}, bf16[128,128]{1,0:T(8,128)(2,1)S(1)}, u32[]{:S(2)}, u32[]{:S(2)}) collective-permute-start(bf16[128,128]{1,0:T(8,128)(2,1)S(1)} %get-tuple-element.136), channel_id=1, source_target_pairs={{0,16},{1,17},{2,18},{3,4},{4,3},{5,21},{6,22},{7,8},{8,7},{9,25},... | collective-permute-start | bytes 98312 | tf_op jit(solution)/shard_map/ppermute | solution.py:338
  46.6 3.6 %collective-permute-start.25 = (bf16[128,128]{1,0:T(8,128)(2,1)S(1)}, bf16[128,128]{1,0:T(8,128)(2,1)S(1)}, u32[]{:S(2)}, u32[]{:S(2)}) collective-permute-start(bf16[128,128]{1,0:T(8,128)(2,1)S(1)} %get-tuple-element.137), channel_id=1, source_target_pairs={{0,3},{1,2},{2,1},{3,0},{4,20},{5,6},{6,5},{7,23},{8,24},{9,10},{1... | collective-permute-start | bytes 98312 | tf_op jit(solution)/shard_map/ppermute | solution.py:338
  46.6 4.8 %collective-permute-start.26 = (bf16[128,128]{1,0:T(8,128)(2,1)S(1)}, bf16[128,128]{1,0:T(8,128)(2,1)S(1)}, u32[]{:S(2)}, u32[]{:S(2)}) collective-permute-start(bf16[128,128]{1,0:T(8,128)(2,1)S(1)} %get-tuple-element.138), channel_id=1, source_target_pairs={{0,1},{1,0},{2,18},{3,19},{4,5},{5,4},{6,7},{7,6},{8,9},{9,8},{10,... | collective-permute-start | bytes 98312 | tf_op jit(solution)/shard_map/ppermute | solution.py:338
  48.3 3.1 %collective-permute-start.27 = (bf16[128,128]{1,0:T(8,128)(2,1)S(1)}, bf16[128,128]{1,0:T(8,128)(2,1)S(1)}, u32[]{:S(2)}, u32[]{:S(2)}) collective-permute-start(bf16[128,128]{1,0:T(8,128)(2,1)S(1)} %get-tuple-element.139), channel_id=1, source_target_pairs={{0,1},{1,0},{2,3},{3,2},{4,5},{5,4},{6,7},{7,6},{8,9},{9,8},{10,11... | collective-permute-start | bytes 98312 | tf_op jit(solution)/shard_map/ppermute | solution.py:338
  51.8 5.0 %collective-permute-start.28 = (bf16[128,128]{1,0:T(8,128)(2,1)S(1)}, bf16[128,128]{1,0:T(8,128)(2,1)S(1)}, u32[]{:S(2)}, u32[]{:S(2)}) collective-permute-start(bf16[128,128]{1,0:T(8,128)(2,1)S(1)} %get-tuple-element.143), channel_id=1, source_target_pairs={{0,16},{1,17},{2,18},{3,4},{4,3},{5,21},{6,22},{7,8},{8,7},{9,25},... | collective-permute-start | bytes 98312 | tf_op jit(solution)/shard_map/ppermute | solution.py:338
  53.6 3.3 %collective-permute-start.29 = (bf16[128,128]{1,0:T(8,128)(2,1)S(1)}, bf16[128,128]{1,0:T(8,128)(2,1)S(1)}, u32[]{:S(2)}, u32[]{:S(2)}) collective-permute-start(bf16[128,128]{1,0:T(8,128)(2,1)S(1)} %get-tuple-element.144), channel_id=1, source_target_pairs={{0,3},{1,2},{2,1},{3,0},{4,20},{5,6},{6,5},{7,23},{8,24},{9,10},{1... | collective-permute-start | bytes 98312 | tf_op jit(solution)/shard_map/ppermute | solution.py:338
  53.6 4.8 %collective-permute-start.30 = (bf16[128,128]{1,0:T(8,128)(2,1)S(1)}, bf16[128,128]{1,0:T(8,128)(2,1)S(1)}, u32[]{:S(2)}, u32[]{:S(2)}) collective-permute-start(bf16[128,128]{1,0:T(8,128)(2,1)S(1)} %get-tuple-element.145), channel_id=1, source_target_pairs={{0,1},{1,0},{2,18},{3,19},{4,5},{5,4},{6,7},{7,6},{8,9},{9,8},{10,... | collective-permute-start | bytes 98312 | tf_op jit(solution)/shard_map/ppermute | solution.py:338
  54.8 3.6 %collective-permute-start.31 = (bf16[128,128]{1,0:T(8,128)(2,1)S(1)}, bf16[128,128]{1,0:T(8,128)(2,1)S(1)}, u32[]{:S(2)}, u32[]{:S(2)}) collective-permute-start(bf16[128,128]{1,0:T(8,128)(2,1)S(1)} %get-tuple-element.146), channel_id=1, source_target_pairs={{0,1},{1,0},{2,3},{3,2},{4,5},{5,4},{6,7},{7,6},{8,9},{9,8},{10,11... | collective-permute-start | bytes 98312 | tf_op jit(solution)/shard_map/ppermute | solution.py:338

commit v11 on v10

--- a/solution.py
+++ b/solution.py
@@ -16,9 +16,9 @@
 BF16 = jnp.bfloat16
 
 
-FAR_TURNS = (0, 0, 0, 2, 1, 0, 0, 1, 1, 0, 0, 0, 0, 0, 0, 0)
-ODD_TURNS = (1, 0, 1, 0, 1, 1, 1, 1, 1, 0, 2, 0, 2, 1, 1)
-FILL = ((), ((0, 3), (19, 21), (22, 31), (25, 26)), ((2, 18), (20, 23), (24, 27)))
+FAR_TURNS = (0, 0, 0, 0, 0, 2, 1, 1, 1, 0, 0, 0, 0, 0, 1, 2)
+ODD_TURNS = (1, 1, 0, 0, 1, 1, 2, 1, 1, 1, 0, 0, 1, 1, 2)
+FILL = ((), ((0, 5), (13, 21), (29, 31)), ((4, 12), (20, 28)))
 
 
 def turns(count):

time: 59.7 us -> 57.7 us (0.966)
  the two profiles are of different devices: /device:TPU:2 before, /device:TPU:8 now
where the time goes in v11:
time: 57.7 us; the launch traced here: 57.5 us
  starting transfers between devices  27.3 us (47%)
  Pallas kernels  17.8 us (31%)
  waiting for transfers between devices  11.6 us (20%)
  between operations  0.83 us (1%)
    ppermute x32, starting transfers between devices, exchange(): lax.ppermute(part, 'sub', route)  27.3 us
    pallas_call x17, Pallas kernels, run(): pl.pallas_call(kernel, out_shape=results, in_specs=[pl.BlockSpec(memory_s...  17.8 us
    ppermute x32, waiting for transfers between devices, exchange(): lax.ppermute(part, 'sub', route)  11.6 us
  transfers between devices with their start and end apart: 32, of which 13 were waited for; matrix products, arithmetic and copies ran while one was open for 0% of the time, Pallas kernels for 20%

profile of v11, /device:TPU:8, one launch (start us, length us, event | category | flops | bytes accessed | tf_op | source)
XLA Modules:
  0.0 57.5 jit_solution(3910663541245100253)
XLA Ops:
  0.0 2.4 %shard_map.73 = (bf16[1024,384]{1,0:T(8,128)(2,1)S(1)}, bf16[128,1024]{1,0:T(8,128)(2,1)S(1)}, bf16[128,384]{1,0:T(8,128)(2,1)S(1)}, f32[1,1024]{1,0:T(1,128)S(1...) custom-call(s32[1,4,128]{2,1,0:T(4,128)} %rows_in.1, ...), custom_call_target="tpu_custom_call" | custom-call | flops 100663296 | bytes 9938960 | tf_op jit(solution)/shard_map/pallas_call | solution.py:303
  2.4 1.8 %collective-permute-start = (bf16[128,128]{1,0:T(8,128)(2,1)S(1)}, bf16[128,128]{1,0:T(8,128)(2,1)S(1)}, u32[]{:S(2)}, u32[]{:S(2)}) collective-permute-start(bf16[128,128]{1,0:T(8,128)(2,1)S(1)} %get-tuple-element.77), channel_id=1, source_target_pairs={{0,16},{1,17},{2,18},{3,19},{4,20},{5,6},{6,5},{7,8},{8,7},{9,25},... | collective-permute-start | bytes 98312 | tf_op jit(solution)/shard_map/ppermute | solution.py:338
  4.3 2.6 %collective-permute-start.1 = (bf16[128,128]{1,0:T(8,128)(2,1)S(1)}, bf16[128,128]{1,0:T(8,128)(2,1)S(1)}, u32[]{:S(2)}, u32[]{:S(2)}) collective-permute-start(bf16[128,128]{1,0:T(8,128)(2,1)S(1)} %get-tuple-element.78), channel_id=1, source_target_pairs={{0,5},{1,2},{2,1},{3,4},{4,3},{5,0},{6,22},{7,23},{8,24},{9,10},{1... | collective-permute-start | bytes 98312 | tf_op jit(solution)/shard_map/ppermute | solution.py:338
  6.9 0.5 collective-permute-start.3
  8.0 2.2 %shard_map.74 = (bf16[384,1024]{1,0:T(8,128)(2,1)S(1)}, bf16[384,1024]{1,0:T(8,128)(2,1)S(1)}, bf16[384,384]{1,0:T(8,128)(2,1)S(1)}, bf16[384,384]{1,0:T(8,128)(...) custom-call(bf16[1024,384]{1,0:T(8,128)(2,1)S(1)} %get-tuple-element, ...), custom_call_target="tpu_custom_call" | custom-call | flops 1509949440 | bytes 6111236 | tf_op jit(solution)/shard_map/pallas_call | solution.py:303
  10.7 1.6 %collective-permute-start.4 = (bf16[128,128]{1,0:T(8,128)(2,1)S(1)}, bf16[128,128]{1,0:T(8,128)(2,1)S(1)}, u32[]{:S(2)}, u32[]{:S(2)}) collective-permute-start(bf16[128,128]{1,0:T(8,128)(2,1)S(1)} %get-tuple-element.90), channel_id=1, source_target_pairs={{0,16},{1,17},{2,18},{3,19},{4,20},{5,6},{6,5},{7,8},{8,7},{9,25},... | collective-permute-start | bytes 98312 | tf_op jit(solution)/shard_map/ppermute | solution.py:338
  12.3 0.5 collective-permute-start.5
  12.8 0.5 collective-permute-start.7
  13.3 2.7 %shard_map.76 = (f32[128,1024]{1,0:T(8,128)S(1)}, f32[128,384]{1,0:T(8,128)S(1)}, bf16[1024,384]{1,0:T(8,128)(2,1)S(1)}, bf16[384,384]{1,0:T(8,128)(2,1)S(1)}) custom-call(bf16[128,128]{1,0:T(8,128)(2,1)S(1)} %collective-permute-done.refs_0_, bf16[128,128]{1,0:T(8,128)(2,1)S(1)} %collective-permute-done.1.refs_1_, ...), custom_call_target="tpu_custom_call" | custom-call | flops 1577058304 | bytes 8392704 | tf_op jit(solution)/shard_map/pallas_call | solution.py:303
  16.0 1.0 %collective-permute-done.5.refs_1_ = bf16[128,128]{1,0:T(8,128)(2,1)S(1)} collective-permute-done((bf16[128,128]{1,0:T(8,128)(2,1)S(1)}, bf16[128,128]{1,0:T(8,128)(2,1)S(1)}, u32[]{:S(2)}, u32[]{:S(2)}) %collective-permute-start.5) | collective-permute-done | bytes 32800 | tf_op jit(solution)/shard_map/ppermute | solution.py:338
  17.5 1.7 %collective-permute-start.8 = (bf16[128,128]{1,0:T(8,128)(2,1)S(1)}, bf16[128,128]{1,0:T(8,128)(2,1)S(1)}, u32[]{:S(2)}, u32[]{:S(2)}) collective-permute-start(bf16[128,128]{1,0:T(8,128)(2,1)S(1)} %get-tuple-element.102), channel_id=1, source_target_pairs={{0,16},{1,17},{2,18},{3,19},{4,20},{5,6},{6,5},{7,8},{8,7},{9,25},... | collective-permute-start | bytes 98312 | tf_op jit(solution)/shard_map/ppermute | solution.py:338
  19.1 1.5 %collective-permute-start.9 = (bf16[128,128]{1,0:T(8,128)(2,1)S(1)}, bf16[128,128]{1,0:T(8,128)(2,1)S(1)}, u32[]{:S(2)}, u32[]{:S(2)}) collective-permute-start(bf16[128,128]{1,0:T(8,128)(2,1)S(1)} %get-tuple-element.103), channel_id=1, source_target_pairs={{0,5},{1,2},{2,1},{3,4},{4,3},{5,0},{6,22},{7,23},{8,24},{9,10},{1... | collective-permute-start | bytes 98312 | tf_op jit(solution)/shard_map/ppermute | solution.py:338
  20.7 0.5 collective-permute-start.11
  21.2 1.0 %shard_map.78 = (f32[128,1024]{1,0:T(8,128)S(1)}, f32[128,1024]{1,0:T(8,128)S(1)}, f32[128,384]{1,0:T(8,128)S(1)}) custom-call(bf16[128,128]{1,0:T(8,128)(2,1)S(1)} %collective-permute-done.4.refs_0_, bf16[128,128]{1,0:T(8,128)(2,1)S(1)} %collective-permute-done.5.refs_1_, bf16[128,128]{1,0:T(8,128)(2,1)S(1)} %collective-permute-done.6.refs_2_, ...), custom_call_target="tpu_custom_call" | custom-call | flops 469762048 | bytes 5902336 | tf_op jit(solution)/shard_map/pallas_call | solution.py:303
  22.2 0.5 collective-permute-done.8.refs_0_
  22.7 1.3 %collective-permute-done.9.refs_1_ = bf16[128,128]{1,0:T(8,128)(2,1)S(1)} collective-permute-done((bf16[128,128]{1,0:T(8,128)(2,1)S(1)}, bf16[128,128]{1,0:T(8,128)(2,1)S(1)}, u32[]{:S(2)}, u32[]{:S(2)}) %collective-permute-start.9) | collective-permute-done | bytes 32800 | tf_op jit(solution)/shard_map/ppermute | solution.py:338
  24.0 0.4 shard_map.79
  24.4 1.2 %collective-permute-start.12 = (bf16[128,128]{1,0:T(8,128)(2,1)S(1)}, bf16[128,128]{1,0:T(8,128)(2,1)S(1)}, u32[]{:S(2)}, u32[]{:S(2)}) collective-permute-start(bf16[128,128]{1,0:T(8,128)(2,1)S(1)} %get-tuple-element.111), channel_id=1, source_target_pairs={{0,16},{1,17},{2,18},{3,19},{4,20},{5,6},{6,5},{7,8},{8,7},{9,25},... | collective-permute-start | bytes 98312 | tf_op jit(solution)/shard_map/ppermute | solution.py:338
  25.6 1.5 %collective-permute-start.13 = (bf16[128,128]{1,0:T(8,128)(2,1)S(1)}, bf16[128,128]{1,0:T(8,128)(2,1)S(1)}, u32[]{:S(2)}, u32[]{:S(2)}) collective-permute-start(bf16[128,128]{1,0:T(8,128)(2,1)S(1)} %get-tuple-element.112), channel_id=1, source_target_pairs={{0,5},{1,2},{2,1},{3,4},{4,3},{5,0},{6,22},{7,23},{8,24},{9,10},{1... | collective-permute-start | bytes 98312 | tf_op jit(solution)/shard_map/ppermute | solution.py:338
  27.1 0.5 collective-permute-start.15
  27.6 1.2 %shard_map.80 = (f32[128,1024]{1,0:T(8,128)S(1)}, f32[128,384]{1,0:T(8,128)S(1)}) custom-call(bf16[128,128]{1,0:T(8,128)(2,1)S(1)} %collective-permute-done.8.refs_0_, bf16[128,128]{1,0:T(8,128)(2,1)S(1)} %collective-permute-done.9.refs_1_, bf16[128,128]{1,0:T(8,128)(2,1)S(1)} %collective-permute-done.10.refs_2_, ...), custom_call_target="tpu_custom_call" | custom-call | flops 469762048 | bytes 5738496 | tf_op jit(solution)/shard_map/pallas_call | solution.py:303
  28.8 1.1 %collective-permute-done.12.refs_0_ = bf16[128,128]{1,0:T(8,128)(2,1)S(1)} collective-permute-done((bf16[128,128]{1,0:T(8,128)(2,1)S(1)}, bf16[128,128]{1,0:T(8,128)(2,1)S(1)}, u32[]{:S(2)}, u32[]{:S(2)}) %collective-permute-start.12) | collective-permute-done | bytes 32800 | tf_op jit(solution)/shard_map/ppermute | solution.py:338
  30.0 0.5 collective-permute-done.13.refs_1_
  30.8 1.3 %collective-permute-start.16 = (bf16[128,128]{1,0:T(8,128)(2,1)S(1)}, bf16[128,128]{1,0:T(8,128)(2,1)S(1)}, u32[]{:S(2)}, u32[]{:S(2)}) collective-permute-start(bf16[128,128]{1,0:T(8,128)(2,1)S(1)} %get-tuple-element.120), channel_id=1, source_target_pairs={{0,16},{1,17},{2,18},{3,19},{4,20},{5,6},{6,5},{7,8},{8,7},{9,25},... | collective-permute-start | bytes 98312 | tf_op jit(solution)/shard_map/ppermute | solution.py:338
  32.1 1.5 %collective-permute-start.17 = (bf16[128,128]{1,0:T(8,128)(2,1)S(1)}, bf16[128,128]{1,0:T(8,128)(2,1)S(1)}, u32[]{:S(2)}, u32[]{:S(2)}) collective-permute-start(bf16[128,128]{1,0:T(8,128)(2,1)S(1)} %get-tuple-element.121), channel_id=1, source_target_pairs={{0,5},{1,2},{2,1},{3,4},{4,3},{5,0},{6,22},{7,23},{8,24},{9,10},{1... | collective-permute-start | bytes 98312 | tf_op jit(solution)/shard_map/ppermute | solution.py:338
  33.7 0.5 collective-permute-start.19
  34.2 1.0 %shard_map.82 = (f32[128,1024]{1,0:T(8,128)S(1)}, f32[128,1024]{1,0:T(8,128)S(1)}, f32[128,384]{1,0:T(8,128)S(1)}) custom-call(bf16[128,128]{1,0:T(8,128)(2,1)S(1)} %collective-permute-done.12.refs_0_, bf16[128,128]{1,0:T(8,128)(2,1)S(1)} %collective-permute-done.13.refs_1_, bf16[128,128]{1,0:T(8,128)(2,1)S(1)} %collective-permute-done.14.refs_2_, ...), custom_call_target="tpu_custom_call" | custom-call | flops 469762048 | bytes 5902336 | tf_op jit(solution)/shard_map/pallas_call | solution.py:303
  35.2 0.8 %collective-permute-done.16.refs_0_ = bf16[128,128]{1,0:T(8,128)(2,1)S(1)} collective-permute-done((bf16[128,128]{1,0:T(8,128)(2,1)S(1)}, bf16[128,128]{1,0:T(8,128)(2,1)S(1)}, u32[]{:S(2)}, u32[]{:S(2)}) %collective-permute-start.16) | collective-permute-done | bytes 32800 | tf_op jit(solution)/shard_map/ppermute | solution.py:338
  36.0 0.9 %collective-permute-done.17.refs_1_ = bf16[128,128]{1,0:T(8,128)(2,1)S(1)} collective-permute-done((bf16[128,128]{1,0:T(8,128)(2,1)S(1)}, bf16[128,128]{1,0:T(8,128)(2,1)S(1)}, u32[]{:S(2)}, u32[]{:S(2)}) %collective-permute-start.17) | collective-permute-done | bytes 32800 | tf_op jit(solution)/shard_map/ppermute | solution.py:338
  37.4 1.2 %collective-permute-start.20 = (bf16[128,128]{1,0:T(8,128)(2,1)S(1)}, bf16[128,128]{1,0:T(8,128)(2,1)S(1)}, u32[]{:S(2)}, u32[]{:S(2)}) collective-permute-start(bf16[128,128]{1,0:T(8,128)(2,1)S(1)} %get-tuple-element.128), channel_id=1, source_target_pairs={{0,16},{1,17},{2,18},{3,19},{4,20},{5,6},{6,5},{7,8},{8,7},{9,25},... | collective-permute-start | bytes 98312 | tf_op jit(solution)/shard_map/ppermute | solution.py:338
  38.6 1.5 %collective-permute-start.21 = (bf16[128,128]{1,0:T(8,128)(2,1)S(1)}, bf16[128,128]{1,0:T(8,128)(2,1)S(1)}, u32[]{:S(2)}, u32[]{:S(2)}) collective-permute-start(bf16[128,128]{1,0:T(8,128)(2,1)S(1)} %get-tuple-element.129), channel_id=1, source_target_pairs={{0,5},{1,2},{2,1},{3,4},{4,3},{5,0},{6,22},{7,23},{8,24},{9,10},{1... | collective-permute-start | bytes 98312 | tf_op jit(solution)/shard_map/ppermute | solution.py:338
  40.1 0.5 collective-permute-start.23
  40.6 1.2 %shard_map.84 = (f32[128,1024]{1,0:T(8,128)S(1)}, f32[128,384]{1,0:T(8,128)S(1)}) custom-call(bf16[128,128]{1,0:T(8,128)(2,1)S(1)} %collective-permute-done.16.refs_0_, bf16[128,128]{1,0:T(8,128)(2,1)S(1)} %collective-permute-done.17.refs_1_, bf16[128,128]{1,0:T(8,128)(2,1)S(1)} %collective-permute-done.18.refs_2_, ...), custom_call_target="tpu_custom_call" | custom-call | flops 469762048 | bytes 5738496 | tf_op jit(solution)/shard_map/pallas_call | solution.py:303
  41.8 0.8 %collective-permute-done.20.refs_0_ = bf16[128,128]{1,0:T(8,128)(2,1)S(1)} collective-permute-done((bf16[128,128]{1,0:T(8,128)(2,1)S(1)}, bf16[128,128]{1,0:T(8,128)(2,1)S(1)}, u32[]{:S(2)}, u32[]{:S(2)}) %collective-permute-start.20) | collective-permute-done | bytes 32800 | tf_op jit(solution)/shard_map/ppermute | solution.py:338
  42.6 0.9 %collective-permute-done.21.refs_1_ = bf16[128,128]{1,0:T(8,128)(2,1)S(1)} collective-permute-done((bf16[128,128]{1,0:T(8,128)(2,1)S(1)}, bf16[128,128]{1,0:T(8,128)(2,1)S(1)}, u32[]{:S(2)}, u32[]{:S(2)}) %collective-permute-start.21) | collective-permute-done | bytes 32800 | tf_op jit(solution)/shard_map/ppermute | solution.py:338
  43.9 1.2 %collective-permute-start.24 = (bf16[128,128]{1,0:T(8,128)(2,1)S(1)}, bf16[128,128]{1,0:T(8,128)(2,1)S(1)}, u32[]{:S(2)}, u32[]{:S(2)}) collective-permute-start(bf16[128,128]{1,0:T(8,128)(2,1)S(1)} %get-tuple-element.136), channel_id=1, source_target_pairs={{0,16},{1,17},{2,18},{3,19},{4,20},{5,6},{6,5},{7,8},{8,7},{9,25},... | collective-permute-start | bytes 98312 | tf_op jit(solution)/shard_map/ppermute | solution.py:338
  45.1 1.5 %collective-permute-start.25 = (bf16[128,128]{1,0:T(8,128)(2,1)S(1)}, bf16[128,128]{1,0:T(8,128)(2,1)S(1)}, u32[]{:S(2)}, u32[]{:S(2)}) collective-permute-start(bf16[128,128]{1,0:T(8,128)(2,1)S(1)} %get-tuple-element.137), channel_id=1, source_target_pairs={{0,5},{1,2},{2,1},{3,4},{4,3},{5,0},{6,22},{7,23},{8,24},{9,10},{1... | collective-permute-start | bytes 98312 | tf_op jit(solution)/shard_map/ppermute | solution.py:338
  46.6 0.5 collective-permute-start.27
  47.2 1.0 %shard_map.86 = (f32[128,1024]{1,0:T(8,128)S(1)}, f32[128,1024]{1,0:T(8,128)S(1)}, f32[128,384]{1,0:T(8,128)S(1)}) custom-call(bf16[128,128]{1,0:T(8,128)(2,1)S(1)} %collective-permute-done.20.refs_0_, bf16[128,128]{1,0:T(8,128)(2,1)S(1)} %collective-permute-done.21.refs_1_, bf16[128,128]{1,0:T(8,128)(2,1)S(1)} %collective-permute-done.22.refs_2_, ...), custom_call_target="tpu_custom_call" | custom-call | flops 469762048 | bytes 5902336 | tf_op jit(solution)/shard_map/pallas_call | solution.py:303
  48.2 0.9 %collective-permute-done.24.refs_0_ = bf16[128,128]{1,0:T(8,128)(2,1)S(1)} collective-permute-done((bf16[128,128]{1,0:T(8,128)(2,1)S(1)}, bf16[128,128]{1,0:T(8,128)(2,1)S(1)}, u32[]{:S(2)}, u32[]{:S(2)}) %collective-permute-start.24) | collective-permute-done | bytes 32800 | tf_op jit(solution)/shard_map/ppermute | solution.py:338
  49.1 0.9 %collective-permute-done.25.refs_1_ = bf16[128,128]{1,0:T(8,128)(2,1)S(1)} collective-permute-done((bf16[128,128]{1,0:T(8,128)(2,1)S(1)}, bf16[128,128]{1,0:T(8,128)(2,1)S(1)}, u32[]{:S(2)}, u32[]{:S(2)}) %collective-permute-start.25) | collective-permute-done | bytes 32800 | tf_op jit(solution)/shard_map/ppermute | solution.py:338
  50.5 1.2 %collective-permute-start.28 = (bf16[128,128]{1,0:T(8,128)(2,1)S(1)}, bf16[128,128]{1,0:T(8,128)(2,1)S(1)}, u32[]{:S(2)}, u32[]{:S(2)}) collective-permute-start(bf16[128,128]{1,0:T(8,128)(2,1)S(1)} %get-tuple-element.143), channel_id=1, source_target_pairs={{0,16},{1,17},{2,18},{3,19},{4,20},{5,6},{6,5},{7,8},{8,7},{9,25},... | collective-permute-start | bytes 98312 | tf_op jit(solution)/shard_map/ppermute | solution.py:338
  51.6 1.4 %collective-permute-start.29 = (bf16[128,128]{1,0:T(8,128)(2,1)S(1)}, bf16[128,128]{1,0:T(8,128)(2,1)S(1)}, u32[]{:S(2)}, u32[]{:S(2)}) collective-permute-start(bf16[128,128]{1,0:T(8,128)(2,1)S(1)} %get-tuple-element.144), channel_id=1, source_target_pairs={{0,5},{1,2},{2,1},{3,4},{4,3},{5,0},{6,22},{7,23},{8,24},{9,10},{1... | collective-permute-start | bytes 98312 | tf_op jit(solution)/shard_map/ppermute | solution.py:338
  53.0 0.5 collective-permute-start.31
  53.5 1.2 %shard_map.88.refs_5_ = f32[1024,128]{1,0:T(8,128)S(1)} custom-call(bf16[128,128]{1,0:T(8,128)(2,1)S(1)} %collective-permute-done.24.refs_0_, bf16[128,128]{1,0:T(8,128)(2,1)S(1)} %collective-permute-done.25.refs_1_, bf16[128,128]{1,0:T(8,128)(2,1)S(1)} %collective-permute-done.26.refs_2_, bf16[128,128]{1,0:T(8,128)(2,1)S(1)} %collective-permute-done.27.refs_3_, ...), custom_call_target="tpu_custom_call" | custom-call | flops 369098752 | bytes 4624384 | tf_op jit(solution)/shard_map/pallas_call | solution.py:303
  54.7 1.0 %collective-permute-done.28.refs_0_ = bf16[128,128]{1,0:T(8,128)(2,1)S(1)} collective-permute-done((bf16[128,128]{1,0:T(8,128)(2,1)S(1)}, bf16[128,128]{1,0:T(8,128)(2,1)S(1)}, u32[]{:S(2)}, u32[]{:S(2)}) %collective-permute-start.28) | collective-permute-done | bytes 32800 | tf_op jit(solution)/shard_map/ppermute | solution.py:338
  55.7 0.8 %collective-permute-done.29.refs_1_ = bf16[128,128]{1,0:T(8,128)(2,1)S(1)} collective-permute-done((bf16[128,128]{1,0:T(8,128)(2,1)S(1)}, bf16[128,128]{1,0:T(8,128)(2,1)S(1)}, u32[]{:S(2)}, u32[]{:S(2)}) %collective-permute-start.29) | collective-permute-done | bytes 32800 | tf_op jit(solution)/shard_map/ppermute | solution.py:338
  56.5 1.1 %shard_map.89 = f32[1,1024,128]{2,1,0:T(8,128)} custom-call(bf16[128,128]{1,0:T(8,128)(2,1)S(1)} %collective-permute-done.28.refs_0_, bf16[128,128]{1,0:T(8,128)(2,1)S(1)} %collective-permute-done.29.refs_1_, bf16[128,128]{1,0:T(8,128)(2,1)S(1)} %collective-permute-done.30.refs_2_, bf16[128,128]{1,0:T(8,128)(2,1)S(1)} %collective-permute-done.31.refs_3_, ...), custom_call_target="tpu_custom_call" | custom-call | flops 100663296 | bytes 1966080 | tf_op jit(solution)/shard_map/pallas_call | solution.py:303
  (33 shorter events, 2.5 us)
Async XLA Ops:
  2.4 7.8 %collective-permute-start = (bf16[128,128]{1,0:T(8,128)(2,1)S(1)}, bf16[128,128]{1,0:T(8,128)(2,1)S(1)}, u32[]{:S(2)}, u32[]{:S(2)}) collective-permute-start(bf16[128,128]{1,0:T(8,128)(2,1)S(1)} %get-tuple-element.77), channel_id=1, source_target_pairs={{0,16},{1,17},{2,18},{3,19},{4,20},{5,6},{6,5},{7,8},{8,7},{9,25},... | collective-permute-start | bytes 98312 | tf_op jit(solution)/shard_map/ppermute | solution.py:338
  4.3 6.0 %collective-permute-start.1 = (bf16[128,128]{1,0:T(8,128)(2,1)S(1)}, bf16[128,128]{1,0:T(8,128)(2,1)S(1)}, u32[]{:S(2)}, u32[]{:S(2)}) collective-permute-start(bf16[128,128]{1,0:T(8,128)(2,1)S(1)} %get-tuple-element.78), channel_id=1, source_target_pairs={{0,5},{1,2},{2,1},{3,4},{4,3},{5,0},{6,22},{7,23},{8,24},{9,10},{1... | collective-permute-start | bytes 98312 | tf_op jit(solution)/shard_map/ppermute | solution.py:338
  6.9 3.4 %collective-permute-start.2 = (bf16[128,128]{1,0:T(8,128)(2,1)S(1)}, bf16[128,128]{1,0:T(8,128)(2,1)S(1)}, u32[]{:S(2)}, u32[]{:S(2)}) collective-permute-start(bf16[128,128]{1,0:T(8,128)(2,1)S(1)} %get-tuple-element.79), channel_id=1, source_target_pairs={{0,1},{1,0},{2,3},{3,2},{4,12},{5,21},{6,7},{7,6},{8,9},{9,8},{10,... | collective-permute-start | bytes 98312 | tf_op jit(solution)/shard_map/ppermute | solution.py:338
  6.9 3.4 %collective-permute-start.3 = (bf16[128,128]{1,0:T(8,128)(2,1)S(1)}, bf16[128,128]{1,0:T(8,128)(2,1)S(1)}, u32[]{:S(2)}, u32[]{:S(2)}) collective-permute-start(bf16[128,128]{1,0:T(8,128)(2,1)S(1)} %get-tuple-element.80), channel_id=1, source_target_pairs={{0,1},{1,0},{2,3},{3,2},{4,5},{5,4},{6,7},{7,6},{8,9},{9,8},{10,11... | collective-permute-start | bytes 98312 | tf_op jit(solution)/shard_map/ppermute | solution.py:338
  10.7 5.3 %collective-permute-start.4 = (bf16[128,128]{1,0:T(8,128)(2,1)S(1)}, bf16[128,128]{1,0:T(8,128)(2,1)S(1)}, u32[]{:S(2)}, u32[]{:S(2)}) collective-permute-start(bf16[128,128]{1,0:T(8,128)(2,1)S(1)} %get-tuple-element.90), channel_id=1, source_target_pairs={{0,16},{1,17},{2,18},{3,19},{4,20},{5,6},{6,5},{7,8},{8,7},{9,25},... | collective-permute-start | bytes 98312 | tf_op jit(solution)/shard_map/ppermute | solution.py:338
  12.3 4.8 %collective-permute-start.5 = (bf16[128,128]{1,0:T(8,128)(2,1)S(1)}, bf16[128,128]{1,0:T(8,128)(2,1)S(1)}, u32[]{:S(2)}, u32[]{:S(2)}) collective-permute-start(bf16[128,128]{1,0:T(8,128)(2,1)S(1)} %get-tuple-element.91), channel_id=1, source_target_pairs={{0,5},{1,2},{2,1},{3,4},{4,3},{5,0},{6,22},{7,23},{8,24},{9,10},{1... | collective-permute-start | bytes 98312 | tf_op jit(solution)/shard_map/ppermute | solution.py:338
  12.8 4.3 %collective-permute-start.6 = (bf16[128,128]{1,0:T(8,128)(2,1)S(1)}, bf16[128,128]{1,0:T(8,128)(2,1)S(1)}, u32[]{:S(2)}, u32[]{:S(2)}) collective-permute-start(bf16[128,128]{1,0:T(8,128)(2,1)S(1)} %get-tuple-element.92), channel_id=1, source_target_pairs={{0,1},{1,0},{2,3},{3,2},{4,12},{5,21},{6,7},{7,6},{8,9},{9,8},{10,... | collective-permute-start | bytes 98312 | tf_op jit(solution)/shard_map/ppermute | solution.py:338
  12.8 4.3 %collective-permute-start.7 = (bf16[128,128]{1,0:T(8,128)(2,1)S(1)}, bf16[128,128]{1,0:T(8,128)(2,1)S(1)}, u32[]{:S(2)}, u32[]{:S(2)}) collective-permute-start(bf16[128,128]{1,0:T(8,128)(2,1)S(1)} %get-tuple-element.93), channel_id=1, source_target_pairs={{0,1},{1,0},{2,3},{3,2},{4,5},{5,4},{6,7},{7,6},{8,9},{9,8},{10,11... | collective-permute-start | bytes 98312 | tf_op jit(solution)/shard_map/ppermute | solution.py:338
  17.5 5.2 %collective-permute-start.8 = (bf16[128,128]{1,0:T(8,128)(2,1)S(1)}, bf16[128,128]{1,0:T(8,128)(2,1)S(1)}, u32[]{:S(2)}, u32[]{:S(2)}) collective-permute-start(bf16[128,128]{1,0:T(8,128)(2,1)S(1)} %get-tuple-element.102), channel_id=1, source_target_pairs={{0,16},{1,17},{2,18},{3,19},{4,20},{5,6},{6,5},{7,8},{8,7},{9,25},... | collective-permute-start | bytes 98312 | tf_op jit(solution)/shard_map/ppermute | solution.py:338
  19.1 4.8 %collective-permute-start.9 = (bf16[128,128]{1,0:T(8,128)(2,1)S(1)}, bf16[128,128]{1,0:T(8,128)(2,1)S(1)}, u32[]{:S(2)}, u32[]{:S(2)}) collective-permute-start(bf16[128,128]{1,0:T(8,128)(2,1)S(1)} %get-tuple-element.103), channel_id=1, source_target_pairs={{0,5},{1,2},{2,1},{3,4},{4,3},{5,0},{6,22},{7,23},{8,24},{9,10},{1... | collective-permute-start | bytes 98312 | tf_op jit(solution)/shard_map/ppermute | solution.py:338
  20.7 3.3 %collective-permute-start.10 = (bf16[128,128]{1,0:T(8,128)(2,1)S(1)}, bf16[128,128]{1,0:T(8,128)(2,1)S(1)}, u32[]{:S(2)}, u32[]{:S(2)}) collective-permute-start(bf16[128,128]{1,0:T(8,128)(2,1)S(1)} %get-tuple-element.104), channel_id=1, source_target_pairs={{0,1},{1,0},{2,3},{3,2},{4,12},{5,21},{6,7},{7,6},{8,9},{9,8},{10,... | collective-permute-start | bytes 98312 | tf_op jit(solution)/shard_map/ppermute | solution.py:338
  20.7 3.3 %collective-permute-start.11 = (bf16[128,128]{1,0:T(8,128)(2,1)S(1)}, bf16[128,128]{1,0:T(8,128)(2,1)S(1)}, u32[]{:S(2)}, u32[]{:S(2)}) collective-permute-start(bf16[128,128]{1,0:T(8,128)(2,1)S(1)} %get-tuple-element.105), channel_id=1, source_target_pairs={{0,1},{1,0},{2,3},{3,2},{4,5},{5,4},{6,7},{7,6},{8,9},{9,8},{10,11... | collective-permute-start | bytes 98312 | tf_op jit(solution)/shard_map/ppermute | solution.py:338
  24.4 5.6 %collective-permute-start.12 = (bf16[128,128]{1,0:T(8,128)(2,1)S(1)}, bf16[128,128]{1,0:T(8,128)(2,1)S(1)}, u32[]{:S(2)}, u32[]{:S(2)}) collective-permute-start(bf16[128,128]{1,0:T(8,128)(2,1)S(1)} %get-tuple-element.111), channel_id=1, source_target_pairs={{0,16},{1,17},{2,18},{3,19},{4,20},{5,6},{6,5},{7,8},{8,7},{9,25},... | collective-permute-start | bytes 98312 | tf_op jit(solution)/shard_map/ppermute | solution.py:338
  25.6 4.8 %collective-permute-start.13 = (bf16[128,128]{1,0:T(8,128)(2,1)S(1)}, bf16[128,128]{1,0:T(8,128)(2,1)S(1)}, u32[]{:S(2)}, u32[]{:S(2)}) collective-permute-start(bf16[128,128]{1,0:T(8,128)(2,1)S(1)} %get-tuple-element.112), channel_id=1, source_target_pairs={{0,5},{1,2},{2,1},{3,4},{4,3},{5,0},{6,22},{7,23},{8,24},{9,10},{1... | collective-permute-start | bytes 98312 | tf_op jit(solution)/shard_map/ppermute | solution.py:338
  27.1 3.3 %collective-permute-start.14 = (bf16[128,128]{1,0:T(8,128)(2,1)S(1)}, bf16[128,128]{1,0:T(8,128)(2,1)S(1)}, u32[]{:S(2)}, u32[]{:S(2)}) collective-permute-start(bf16[128,128]{1,0:T(8,128)(2,1)S(1)} %get-tuple-element.113), channel_id=1, source_target_pairs={{0,1},{1,0},{2,3},{3,2},{4,12},{5,21},{6,7},{7,6},{8,9},{9,8},{10,... | collective-permute-start | bytes 98312 | tf_op jit(solution)/shard_map/ppermute | solution.py:338
  27.1 3.3 %collective-permute-start.15 = (bf16[128,128]{1,0:T(8,128)(2,1)S(1)}, bf16[128,128]{1,0:T(8,128)(2,1)S(1)}, u32[]{:S(2)}, u32[]{:S(2)}) collective-permute-start(bf16[128,128]{1,0:T(8,128)(2,1)S(1)} %get-tuple-element.114), channel_id=1, source_target_pairs={{0,1},{1,0},{2,3},{3,2},{4,5},{5,4},{6,7},{7,6},{8,9},{9,8},{10,11... | collective-permute-start | bytes 98312 | tf_op jit(solution)/shard_map/ppermute | solution.py:338
  30.8 5.2 %collective-permute-start.16 = (bf16[128,128]{1,0:T(8,128)(2,1)S(1)}, bf16[128,128]{1,0:T(8,128)(2,1)S(1)}, u32[]{:S(2)}, u32[]{:S(2)}) collective-permute-start(bf16[128,128]{1,0:T(8,128)(2,1)S(1)} %get-tuple-element.120), channel_id=1, source_target_pairs={{0,16},{1,17},{2,18},{3,19},{4,20},{5,6},{6,5},{7,8},{8,7},{9,25},... | collective-permute-start | bytes 98312 | tf_op jit(solution)/shard_map/ppermute | solution.py:338
  32.1 4.8 %collective-permute-start.17 = (bf16[128,128]{1,0:T(8,128)(2,1)S(1)}, bf16[128,128]{1,0:T(8,128)(2,1)S(1)}, u32[]{:S(2)}, u32[]{:S(2)}) collective-permute-start(bf16[128,128]{1,0:T(8,128)(2,1)S(1)} %get-tuple-element.121), channel_id=1, source_target_pairs={{0,5},{1,2},{2,1},{3,4},{4,3},{5,0},{6,22},{7,23},{8,24},{9,10},{1... | collective-permute-start | bytes 98312 | tf_op jit(solution)/shard_map/ppermute | solution.py:338
  33.7 3.3 %collective-permute-start.18 = (bf16[128,128]{1,0:T(8,128)(2,1)S(1)}, bf16[128,128]{1,0:T(8,128)(2,1)S(1)}, u32[]{:S(2)}, u32[]{:S(2)}) collective-permute-start(bf16[128,128]{1,0:T(8,128)(2,1)S(1)} %get-tuple-element.122), channel_id=1, source_target_pairs={{0,1},{1,0},{2,3},{3,2},{4,12},{5,21},{6,7},{7,6},{8,9},{9,8},{10,... | collective-permute-start | bytes 98312 | tf_op jit(solution)/shard_map/ppermute | solution.py:338
  33.7 3.3 %collective-permute-start.19 = (bf16[128,128]{1,0:T(8,128)(2,1)S(1)}, bf16[128,128]{1,0:T(8,128)(2,1)S(1)}, u32[]{:S(2)}, u32[]{:S(2)}) collective-permute-start(bf16[128,128]{1,0:T(8,128)(2,1)S(1)} %get-tuple-element.123), channel_id=1, source_target_pairs={{0,1},{1,0},{2,3},{3,2},{4,5},{5,4},{6,7},{7,6},{8,9},{9,8},{10,11... | collective-permute-start | bytes 98312 | tf_op jit(solution)/shard_map/ppermute | solution.py:338
  37.4 5.2 %collective-permute-start.20 = (bf16[128,128]{1,0:T(8,128)(2,1)S(1)}, bf16[128,128]{1,0:T(8,128)(2,1)S(1)}, u32[]{:S(2)}, u32[]{:S(2)}) collective-permute-start(bf16[128,128]{1,0:T(8,128)(2,1)S(1)} %get-tuple-element.128), channel_id=1, source_target_pairs={{0,16},{1,17},{2,18},{3,19},{4,20},{5,6},{6,5},{7,8},{8,7},{9,25},... | collective-permute-start | bytes 98312 | tf_op jit(solution)/shard_map/ppermute | solution.py:338
  38.6 4.9 %collective-permute-start.21 = (bf16[128,128]{1,0:T(8,128)(2,1)S(1)}, bf16[128,128]{1,0:T(8,128)(2,1)S(1)}, u32[]{:S(2)}, u32[]{:S(2)}) collective-permute-start(bf16[128,128]{1,0:T(8,128)(2,1)S(1)} %get-tuple-element.129), channel_id=1, source_target_pairs={{0,5},{1,2},{2,1},{3,4},{4,3},{5,0},{6,22},{7,23},{8,24},{9,10},{1... | collective-permute-start | bytes 98312 | tf_op jit(solution)/shard_map/ppermute | solution.py:338
  40.1 3.4 %collective-permute-start.22 = (bf16[128,128]{1,0:T(8,128)(2,1)S(1)}, bf16[128,128]{1,0:T(8,128)(2,1)S(1)}, u32[]{:S(2)}, u32[]{:S(2)}) collective-permute-start(bf16[128,128]{1,0:T(8,128)(2,1)S(1)} %get-tuple-element.130), channel_id=1, source_target_pairs={{0,1},{1,0},{2,3},{3,2},{4,12},{5,21},{6,7},{7,6},{8,9},{9,8},{10,... | collective-permute-start | bytes 98312 | tf_op jit(solution)/shard_map/ppermute | solution.py:338
  40.1 3.4 %collective-permute-start.23 = (bf16[128,128]{1,0:T(8,128)(2,1)S(1)}, bf16[128,128]{1,0:T(8,128)(2,1)S(1)}, u32[]{:S(2)}, u32[]{:S(2)}) collective-permute-start(bf16[128,128]{1,0:T(8,128)(2,1)S(1)} %get-tuple-element.131), channel_id=1, source_target_pairs={{0,1},{1,0},{2,3},{3,2},{4,5},{5,4},{6,7},{7,6},{8,9},{9,8},{10,11... | collective-permute-start | bytes 98312 | tf_op jit(solution)/shard_map/ppermute | solution.py:338
  43.9 5.2 %collective-permute-start.24 = (bf16[128,128]{1,0:T(8,128)(2,1)S(1)}, bf16[128,128]{1,0:T(8,128)(2,1)S(1)}, u32[]{:S(2)}, u32[]{:S(2)}) collective-permute-start(bf16[128,128]{1,0:T(8,128)(2,1)S(1)} %get-tuple-element.136), channel_id=1, source_target_pairs={{0,16},{1,17},{2,18},{3,19},{4,20},{5,6},{6,5},{7,8},{8,7},{9,25},... | collective-permute-start | bytes 98312 | tf_op jit(solution)/shard_map/ppermute | solution.py:338
  45.1 4.9 %collective-permute-start.25 = (bf16[128,128]{1,0:T(8,128)(2,1)S(1)}, bf16[128,128]{1,0:T(8,128)(2,1)S(1)}, u32[]{:S(2)}, u32[]{:S(2)}) collective-permute-start(bf16[128,128]{1,0:T(8,128)(2,1)S(1)} %get-tuple-element.137), channel_id=1, source_target_pairs={{0,5},{1,2},{2,1},{3,4},{4,3},{5,0},{6,22},{7,23},{8,24},{9,10},{1... | collective-permute-start | bytes 98312 | tf_op jit(solution)/shard_map/ppermute | solution.py:338
  46.6 3.4 %collective-permute-start.26 = (bf16[128,128]{1,0:T(8,128)(2,1)S(1)}, bf16[128,128]{1,0:T(8,128)(2,1)S(1)}, u32[]{:S(2)}, u32[]{:S(2)}) collective-permute-start(bf16[128,128]{1,0:T(8,128)(2,1)S(1)} %get-tuple-element.138), channel_id=1, source_target_pairs={{0,1},{1,0},{2,3},{3,2},{4,12},{5,21},{6,7},{7,6},{8,9},{9,8},{10,... | collective-permute-start | bytes 98312 | tf_op jit(solution)/shard_map/ppermute | solution.py:338
  46.6 3.4 %collective-permute-start.27 = (bf16[128,128]{1,0:T(8,128)(2,1)S(1)}, bf16[128,128]{1,0:T(8,128)(2,1)S(1)}, u32[]{:S(2)}, u32[]{:S(2)}) collective-permute-start(bf16[128,128]{1,0:T(8,128)(2,1)S(1)} %get-tuple-element.139), channel_id=1, source_target_pairs={{0,1},{1,0},{2,3},{3,2},{4,5},{5,4},{6,7},{7,6},{8,9},{9,8},{10,11... | collective-permute-start | bytes 98312 | tf_op jit(solution)/shard_map/ppermute | solution.py:338
  50.5 5.2 %collective-permute-start.28 = (bf16[128,128]{1,0:T(8,128)(2,1)S(1)}, bf16[128,128]{1,0:T(8,128)(2,1)S(1)}, u32[]{:S(2)}, u32[]{:S(2)}) collective-permute-start(bf16[128,128]{1,0:T(8,128)(2,1)S(1)} %get-tuple-element.143), channel_id=1, source_target_pairs={{0,16},{1,17},{2,18},{3,19},{4,20},{5,6},{6,5},{7,8},{8,7},{9,25},... | collective-permute-start | bytes 98312 | tf_op jit(solution)/shard_map/ppermute | solution.py:338
  51.6 4.8 %collective-permute-start.29 = (bf16[128,128]{1,0:T(8,128)(2,1)S(1)}, bf16[128,128]{1,0:T(8,128)(2,1)S(1)}, u32[]{:S(2)}, u32[]{:S(2)}) collective-permute-start(bf16[128,128]{1,0:T(8,128)(2,1)S(1)} %get-tuple-element.144), channel_id=1, source_target_pairs={{0,5},{1,2},{2,1},{3,4},{4,3},{5,0},{6,22},{7,23},{8,24},{9,10},{1... | collective-permute-start | bytes 98312 | tf_op jit(solution)/shard_map/ppermute | solution.py:338
  53.0 3.4 %collective-permute-start.30 = (bf16[128,128]{1,0:T(8,128)(2,1)S(1)}, bf16[128,128]{1,0:T(8,128)(2,1)S(1)}, u32[]{:S(2)}, u32[]{:S(2)}) collective-permute-start(bf16[128,128]{1,0:T(8,128)(2,1)S(1)} %get-tuple-element.145), channel_id=1, source_target_pairs={{0,1},{1,0},{2,3},{3,2},{4,12},{5,21},{6,7},{7,6},{8,9},{9,8},{10,... | collective-permute-start | bytes 98312 | tf_op jit(solution)/shard_map/ppermute | solution.py:338
  53.0 3.4 %collective-permute-start.31 = (bf16[128,128]{1,0:T(8,128)(2,1)S(1)}, bf16[128,128]{1,0:T(8,128)(2,1)S(1)}, u32[]{:S(2)}, u32[]{:S(2)}) collective-permute-start(bf16[128,128]{1,0:T(8,128)(2,1)S(1)} %get-tuple-element.146), channel_id=1, source_target_pairs={{0,1},{1,0},{2,3},{3,2},{4,5},{5,4},{6,7},{7,6},{8,9},{9,8},{10,11... | collective-permute-start | bytes 98312 | tf_op jit(solution)/shard_map/ppermute | solution.py:338

commit v12 on v11

--- a/solution.py
+++ b/solution.py
@@ -113,13 +113,12 @@
     rhs_in,
     weight_in,
     n_in,
-    s_in,
     hot_ref,
     turned_ref,
     picked_ref,
+    list_ref,
     weight_ref,
     n_ref,
-    s_ref,
     *refs,
 ):
     out_refs, (rows_ref, near_ref, rhs_ref, sems) = refs[:trips], refs[trips:]
@@ -129,7 +128,6 @@
         (rhs_in, rhs_ref),
         (weight_in, weight_ref),
         (n_in, n_ref),
-        (s_in, s_ref),
     ]
     copies = [pltpu.make_async_copy(source, target, sems.at[k]) for k, (source, target) in enumerate(pairs)]
     for copy in copies:
@@ -144,6 +142,7 @@
     for k, slot in enumerate(slots):
         partner = jnp.sum(jnp.where(lane == slot, near, 0.0), 1, keepdims=True)
         row = jnp.where(partner >= 0.0, rows_ref[0, pl.ds(slot, 1), :], -1)
+        list_ref[:, pl.ds(k * share, share)] = jnp.broadcast_to(row.astype(F32), (list_ref.shape[0], share))
         hot_ref[:, pl.ds(k * share, share)] = jnp.where(place == row, 1.0, 0.0).astype(BF16)
     copies[2].wait()
     turned = rhs_ref[0].T
@@ -158,9 +157,11 @@
 def pick_n_kernel(
     hot_ref,
     turned_ref,
+    list_ref,
     n_ref,
     weight_ref,
     count_ref,
+    s_in,
     hot_t_ref,
     n_pick_ref,
     n_small_ref,
@@ -170,23 +171,37 @@
     local_ref,
     base_ref,
     row_ref,
+    s_ref,
+    sem,
 ):
+    copy = pltpu.make_async_copy(s_in, s_ref, sem)
+    copy.start()
     hot = hot_ref[...]
     width, total = hot.shape
     weight = weight_ref[...]
-    hot_t = hot.T
-    hot_t_ref[...] = hot_t
-    n_pick = times(hot_t, n_ref[0]).astype(BF16)
+    side = 128
+    listed = list_ref[:1]
+    lane = lax.broadcasted_iota(jnp.int32, (side, side), 1).astype(F32)
+    hits = [jnp.zeros((1, side), F32)] * (width // side)
+    same = []
+    for k in range(0, total, side):
+        down = jnp.broadcast_to(listed[:, k : k + side], (side, side)).T
+        for m in range(width // side):
+            block = jnp.where(down == lane + float(m * side), 1.0, 0.0)
+            hits[m] = hits[m] + jnp.sum(block, 0, keepdims=True)
+            hot_t_ref[k : k + side, m * side : (m + 1) * side] = block.astype(BF16)
+        wide = jnp.concatenate([down] * (total // side), 1)
+        same.append(jnp.where((wide == listed) & (wide >= 0.0), 1.0, 0.0))
+    same = jnp.concatenate(same, 0)
+    same_ref[...] = same.astype(BF16)
+    inner = jnp.where(jnp.concatenate(hits, 1) > 0.0, 0.0, 1.0)
+    inner_ref[...] = jnp.broadcast_to(inner, inner_ref.shape)
+    n_pick = times(hot_t_ref[...], n_ref[0]).astype(BF16)
     n_pick_ref[...] = n_pick
     n_small_ref[...] = times(n_pick, hot).astype(BF16)
-    same = times(hot_t, hot)
-    same_ref[...] = same.astype(BF16)
     earlier = lax.broadcasted_iota(jnp.int32, same.shape, 0) < lax.broadcasted_iota(jnp.int32, same.shape, 1)
     repeats = jnp.sum(jnp.where(earlier, same, 0.0), 0, keepdims=True)
     first = jnp.where(repeats > 0.0, 0.0, 1.0)
-    hits = jnp.sum(hot_t.astype(F32), 0, keepdims=True)
-    inner = jnp.where(hits > 0.0, 0.0, 1.0)
-    inner_ref[...] = jnp.broadcast_to(inner, inner_ref.shape)
     high = weight.astype(BF16).astype(F32)
     middle = (weight - high).astype(BF16).astype(F32)
     low = weight - high - middle
@@ -203,6 +218,7 @@
     local = mask[:1] * turned_ref[...].astype(F32)
     local_ref[...] = local
     base_ref[...] = times_t((weight * local * inner).astype(BF16), n_pick)
+    copy.wait()
 
 
 def update_path_kernel(trips, links, step, last, *refs):
@@ -296,14 +312,16 @@
         copy.wait()
 
 
-def run(kernel, operands, results, flops, inputs=pltpu.VMEM, outputs=pltpu.VMEM, scalars=(), scratch=()):
-    if inputs is pltpu.HBM:
-        operands = [pltpu.with_memory_space_constraint(a, inputs) for a in operands]
+def run(kernel, operands, results, flops, spaces=(), outputs=pltpu.VMEM, scratch=()):
+    spaces = [dict(spaces).get(k, pltpu.VMEM) for k in range(len(operands))]
     moved = sum(a.size * a.dtype.itemsize for a in (*operands, *results))
+    operands = [
+        pltpu.with_memory_space_constraint(a, space) if space is pltpu.HBM else a for a, space in zip(operands, spaces)
+    ]
     return pl.pallas_call(
         kernel,
         out_shape=results,
-        in_specs=[pl.BlockSpec(memory_space=pltpu.SMEM if k in scalars else inputs) for k in range(len(operands))],
+        in_specs=[pl.BlockSpec(memory_space=space) for space in spaces],
         out_specs=[pl.BlockSpec(memory_space=outputs)] * len(results),
         scratch_shapes=scratch,
         compiler_params=pltpu.CompilerParams(vmem_limit_bytes=LIMIT),
@@ -340,34 +358,46 @@
     def bound(kernel, *settings):
         return functools.partial(kernel, trips, links, *settings)
 
-    hot, turned, picked, weight, n_mat, s_mat, *sent = run(
+    hot, turned, picked, listed, weight, n_mat, *sent = run(
         bound(open_kernel, subs),
-        [shared_rows, neighbours, right_side, weights, neumann, schur],
+        [shared_rows, neighbours, right_side, weights, neumann],
         [
             array(width, total, BF16),
             array(leads, width, BF16),
             array(leads, total, BF16),
+            array(8, total),
             same_as(weights),
             same_as(neumann),
-            same_as(schur),
             *messages,
         ],
         picks,
-        inputs=pltpu.HBM,
+        spaces={k: pltpu.HBM for k in range(5)},
         scratch=[
             pltpu.VMEM(shared_rows.shape, jnp.int32),
             pltpu.VMEM(neighbours.shape, jnp.int32),
             pltpu.VMEM(right_side.shape, BF16),
-            pltpu.SemaphoreType.DMA((6,)),
+            pltpu.SemaphoreType.DMA((5,)),
         ],
     )
     arrived = exchange(sent)
-    hot_t, n_pick, n_small, same, inner, mask, local, base, rows = run(
+    hot_t, n_pick, n_small, same, inner, mask, local, base, rows, s_mat = run(
         pick_n_kernel,
-        [hot, turned, n_mat, weight, counts],
-        [array(total, width, BF16), array(total, width, BF16), small, small, row, row, full, some, array(8, total)],
-        2 * total * width * width + 4 * total * total * width + picks,
-        scalars=(4,),
+        [hot, turned, listed, n_mat, weight, counts, schur],
+        [
+            array(total, width, BF16),
+            array(total, width, BF16),
+            small,
+            small,
+            row,
+            row,
+            full,
+            some,
+            array(8, total),
+            same_as(schur),
+        ],
+        2 * total * width * width + 2 * total * total * width + picks,
+        spaces={5: pltpu.SMEM, 6: pltpu.HBM},
+        scratch=[pltpu.SemaphoreType.DMA],
     )
     near = picked
     near_state = None

time: 57.7 us -> 57 us (0.988)
  Pallas kernels: 17.8 us -> 17.1 us
    pallas_call x17, Pallas kernels: 17.8 us -> 17.1 us  [run(): pl.pallas_call(kernel, out_shape=results, in_specs=[pl.BlockSpec(memory_s...]
where the time goes in v12:
time: 57 us; the launch traced here: 56.8 us
  starting transfers between devices  27.2 us (48%)
  Pallas kernels  17.1 us (30%)
  waiting for transfers between devices  11.7 us (21%)
  between operations  0.83 us (1%)
    ppermute x32, starting transfers between devices, exchange(): lax.ppermute(part, 'sub', route)  27.2 us
    pallas_call x17, Pallas kernels, run(): pl.pallas_call(kernel, out_shape=results, in_specs=[pl.BlockSpec(memory_s...  17.1 us
    ppermute x32, waiting for transfers between devices, exchange(): lax.ppermute(part, 'sub', route)  11.7 us
  transfers between devices with their start and end apart: 32, of which 13 were waited for; matrix products, arithmetic and copies ran while one was open for 0% of the time, Pallas kernels for 20%

profile of v12, /device:TPU:8, one launch (start us, length us, event | category | flops | bytes accessed | tf_op | source)
XLA Modules:
  0.0 56.8 jit_solution(13503145075490615810)
XLA Ops:
  0.0 1.8 %shard_map.73 = (bf16[1024,384]{1,0:T(8,128)(2,1)S(1)}, bf16[128,1024]{1,0:T(8,128)(2,1)S(1)}, bf16[128,384]{1,0:T(8,128)(2,1)S(1)}, f32[8,384]{1,0:T(8,128)S(1)...) custom-call(s32[1,4,128]{2,1,0:T(4,128)} %rows_in.1, ...), custom_call_target="tpu_custom_call" | custom-call | flops 100663296 | bytes 5756944 | tf_op jit(solution)/shard_map/pallas_call | solution.py:321
  1.8 1.8 %collective-permute-start = (bf16[128,128]{1,0:T(8,128)(2,1)S(1)}, bf16[128,128]{1,0:T(8,128)(2,1)S(1)}, u32[]{:S(2)}, u32[]{:S(2)}) collective-permute-start(bf16[128,128]{1,0:T(8,128)(2,1)S(1)} %get-tuple-element.78), channel_id=1, source_target_pairs={{0,16},{1,17},{2,18},{3,19},{4,20},{5,6},{6,5},{7,8},{8,7},{9,25},... | collective-permute-start | bytes 98312 | tf_op jit(solution)/shard_map/ppermute | solution.py:356
  3.6 2.6 %collective-permute-start.1 = (bf16[128,128]{1,0:T(8,128)(2,1)S(1)}, bf16[128,128]{1,0:T(8,128)(2,1)S(1)}, u32[]{:S(2)}, u32[]{:S(2)}) collective-permute-start(bf16[128,128]{1,0:T(8,128)(2,1)S(1)} %get-tuple-element.79), channel_id=1, source_target_pairs={{0,5},{1,2},{2,1},{3,4},{4,3},{5,0},{6,22},{7,23},{8,24},{9,10},{1... | collective-permute-start | bytes 98312 | tf_op jit(solution)/shard_map/ppermute | solution.py:356
  6.2 0.5 collective-permute-start.3
  7.4 2.1 %shard_map.74 = (bf16[384,1024]{1,0:T(8,128)(2,1)S(1)}, bf16[384,1024]{1,0:T(8,128)(2,1)S(1)}, bf16[384,384]{1,0:T(8,128)(2,1)S(1)}, bf16[384,384]{1,0:T(8,128)(...) custom-call(bf16[1024,384]{1,0:T(8,128)(2,1)S(1)} %get-tuple-element, ...), custom_call_target="tpu_custom_call" | custom-call | flops 1207959552 | bytes 10317828 | tf_op jit(solution)/shard_map/pallas_call | solution.py:321
  9.6 0.4 shard_map.75
  10.0 1.6 %collective-permute-start.4 = (bf16[128,128]{1,0:T(8,128)(2,1)S(1)}, bf16[128,128]{1,0:T(8,128)(2,1)S(1)}, u32[]{:S(2)}, u32[]{:S(2)}) collective-permute-start(bf16[128,128]{1,0:T(8,128)(2,1)S(1)} %get-tuple-element.92), channel_id=1, source_target_pairs={{0,16},{1,17},{2,18},{3,19},{4,20},{5,6},{6,5},{7,8},{8,7},{9,25},... | collective-permute-start | bytes 98312 | tf_op jit(solution)/shard_map/ppermute | solution.py:356
  11.5 0.6 %collective-permute-start.5 = (bf16[128,128]{1,0:T(8,128)(2,1)S(1)}, bf16[128,128]{1,0:T(8,128)(2,1)S(1)}, u32[]{:S(2)}, u32[]{:S(2)}) collective-permute-start(bf16[128,128]{1,0:T(8,128)(2,1)S(1)} %get-tuple-element.93), channel_id=1, source_target_pairs={{0,5},{1,2},{2,1},{3,4},{4,3},{5,0},{6,22},{7,23},{8,24},{9,10},{1... | collective-permute-start | bytes 98312 | tf_op jit(solution)/shard_map/ppermute | solution.py:356
  12.1 0.5 collective-permute-start.7
  12.6 2.7 %shard_map.76 = (f32[128,1024]{1,0:T(8,128)S(1)}, f32[128,384]{1,0:T(8,128)S(1)}, bf16[1024,384]{1,0:T(8,128)(2,1)S(1)}, bf16[384,384]{1,0:T(8,128)(2,1)S(1)}) custom-call(bf16[128,128]{1,0:T(8,128)(2,1)S(1)} %collective-permute-done.refs_0_, bf16[128,128]{1,0:T(8,128)(2,1)S(1)} %collective-permute-done.1.refs_1_, ...), custom_call_target="tpu_custom_call" | custom-call | flops 1577058304 | bytes 8392704 | tf_op jit(solution)/shard_map/pallas_call | solution.py:321
  15.4 1.0 %collective-permute-done.5.refs_1_ = bf16[128,128]{1,0:T(8,128)(2,1)S(1)} collective-permute-done((bf16[128,128]{1,0:T(8,128)(2,1)S(1)}, bf16[128,128]{1,0:T(8,128)(2,1)S(1)}, u32[]{:S(2)}, u32[]{:S(2)}) %collective-permute-start.5) | collective-permute-done | bytes 32800 | tf_op jit(solution)/shard_map/ppermute | solution.py:356
  16.7 1.8 %collective-permute-start.8 = (bf16[128,128]{1,0:T(8,128)(2,1)S(1)}, bf16[128,128]{1,0:T(8,128)(2,1)S(1)}, u32[]{:S(2)}, u32[]{:S(2)}) collective-permute-start(bf16[128,128]{1,0:T(8,128)(2,1)S(1)} %get-tuple-element.104), channel_id=1, source_target_pairs={{0,16},{1,17},{2,18},{3,19},{4,20},{5,6},{6,5},{7,8},{8,7},{9,25},... | collective-permute-start | bytes 98312 | tf_op jit(solution)/shard_map/ppermute | solution.py:356
  18.5 1.5 %collective-permute-start.9 = (bf16[128,128]{1,0:T(8,128)(2,1)S(1)}, bf16[128,128]{1,0:T(8,128)(2,1)S(1)}, u32[]{:S(2)}, u32[]{:S(2)}) collective-permute-start(bf16[128,128]{1,0:T(8,128)(2,1)S(1)} %get-tuple-element.105), channel_id=1, source_target_pairs={{0,5},{1,2},{2,1},{3,4},{4,3},{5,0},{6,22},{7,23},{8,24},{9,10},{1... | collective-permute-start | bytes 98312 | tf_op jit(solution)/shard_map/ppermute | solution.py:356
  20.0 0.5 collective-permute-start.11
  20.5 1.0 %shard_map.78 = (f32[128,1024]{1,0:T(8,128)S(1)}, f32[128,1024]{1,0:T(8,128)S(1)}, f32[128,384]{1,0:T(8,128)S(1)}) custom-call(bf16[128,128]{1,0:T(8,128)(2,1)S(1)} %collective-permute-done.4.refs_0_, bf16[128,128]{1,0:T(8,128)(2,1)S(1)} %collective-permute-done.5.refs_1_, bf16[128,128]{1,0:T(8,128)(2,1)S(1)} %collective-permute-done.6.refs_2_, ...), custom_call_target="tpu_custom_call" | custom-call | flops 469762048 | bytes 5902336 | tf_op jit(solution)/shard_map/pallas_call | solution.py:321
  21.5 0.5 collective-permute-done.8.refs_0_
  22.0 1.4 %collective-permute-done.9.refs_1_ = bf16[128,128]{1,0:T(8,128)(2,1)S(1)} collective-permute-done((bf16[128,128]{1,0:T(8,128)(2,1)S(1)}, bf16[128,128]{1,0:T(8,128)(2,1)S(1)}, u32[]{:S(2)}, u32[]{:S(2)}) %collective-permute-start.9) | collective-permute-done | bytes 32800 | tf_op jit(solution)/shard_map/ppermute | solution.py:356
  23.7 1.1 %collective-permute-start.12 = (bf16[128,128]{1,0:T(8,128)(2,1)S(1)}, bf16[128,128]{1,0:T(8,128)(2,1)S(1)}, u32[]{:S(2)}, u32[]{:S(2)}) collective-permute-start(bf16[128,128]{1,0:T(8,128)(2,1)S(1)} %get-tuple-element.113), channel_id=1, source_target_pairs={{0,16},{1,17},{2,18},{3,19},{4,20},{5,6},{6,5},{7,8},{8,7},{9,25},... | collective-permute-start | bytes 98312 | tf_op jit(solution)/shard_map/ppermute | solution.py:356
  24.9 1.5 %collective-permute-start.13 = (bf16[128,128]{1,0:T(8,128)(2,1)S(1)}, bf16[128,128]{1,0:T(8,128)(2,1)S(1)}, u32[]{:S(2)}, u32[]{:S(2)}) collective-permute-start(bf16[128,128]{1,0:T(8,128)(2,1)S(1)} %get-tuple-element.114), channel_id=1, source_target_pairs={{0,5},{1,2},{2,1},{3,4},{4,3},{5,0},{6,22},{7,23},{8,24},{9,10},{1... | collective-permute-start | bytes 98312 | tf_op jit(solution)/shard_map/ppermute | solution.py:356
  26.3 0.5 collective-permute-start.15
  26.9 1.2 %shard_map.80 = (f32[128,1024]{1,0:T(8,128)S(1)}, f32[128,384]{1,0:T(8,128)S(1)}) custom-call(bf16[128,128]{1,0:T(8,128)(2,1)S(1)} %collective-permute-done.8.refs_0_, bf16[128,128]{1,0:T(8,128)(2,1)S(1)} %collective-permute-done.9.refs_1_, bf16[128,128]{1,0:T(8,128)(2,1)S(1)} %collective-permute-done.10.refs_2_, ...), custom_call_target="tpu_custom_call" | custom-call | flops 469762048 | bytes 5738496 | tf_op jit(solution)/shard_map/pallas_call | solution.py:321
  28.1 1.1 %collective-permute-done.12.refs_0_ = bf16[128,128]{1,0:T(8,128)(2,1)S(1)} collective-permute-done((bf16[128,128]{1,0:T(8,128)(2,1)S(1)}, bf16[128,128]{1,0:T(8,128)(2,1)S(1)}, u32[]{:S(2)}, u32[]{:S(2)}) %collective-permute-start.12) | collective-permute-done | bytes 32800 | tf_op jit(solution)/shard_map/ppermute | solution.py:356
  29.2 0.4 collective-permute-done.13.refs_1_
  30.1 1.4 %collective-permute-start.16 = (bf16[128,128]{1,0:T(8,128)(2,1)S(1)}, bf16[128,128]{1,0:T(8,128)(2,1)S(1)}, u32[]{:S(2)}, u32[]{:S(2)}) collective-permute-start(bf16[128,128]{1,0:T(8,128)(2,1)S(1)} %get-tuple-element.122), channel_id=1, source_target_pairs={{0,16},{1,17},{2,18},{3,19},{4,20},{5,6},{6,5},{7,8},{8,7},{9,25},... | collective-permute-start | bytes 98312 | tf_op jit(solution)/shard_map/ppermute | solution.py:356
  31.5 1.5 %collective-permute-start.17 = (bf16[128,128]{1,0:T(8,128)(2,1)S(1)}, bf16[128,128]{1,0:T(8,128)(2,1)S(1)}, u32[]{:S(2)}, u32[]{:S(2)}) collective-permute-start(bf16[128,128]{1,0:T(8,128)(2,1)S(1)} %get-tuple-element.123), channel_id=1, source_target_pairs={{0,5},{1,2},{2,1},{3,4},{4,3},{5,0},{6,22},{7,23},{8,24},{9,10},{1... | collective-permute-start | bytes 98312 | tf_op jit(solution)/shard_map/ppermute | solution.py:356
  32.9 0.5 collective-permute-start.19
  33.5 1.0 %shard_map.82 = (f32[128,1024]{1,0:T(8,128)S(1)}, f32[128,1024]{1,0:T(8,128)S(1)}, f32[128,384]{1,0:T(8,128)S(1)}) custom-call(bf16[128,128]{1,0:T(8,128)(2,1)S(1)} %collective-permute-done.12.refs_0_, bf16[128,128]{1,0:T(8,128)(2,1)S(1)} %collective-permute-done.13.refs_1_, bf16[128,128]{1,0:T(8,128)(2,1)S(1)} %collective-permute-done.14.refs_2_, ...), custom_call_target="tpu_custom_call" | custom-call | flops 469762048 | bytes 5902336 | tf_op jit(solution)/shard_map/pallas_call | solution.py:321
  34.5 0.8 %collective-permute-done.16.refs_0_ = bf16[128,128]{1,0:T(8,128)(2,1)S(1)} collective-permute-done((bf16[128,128]{1,0:T(8,128)(2,1)S(1)}, bf16[128,128]{1,0:T(8,128)(2,1)S(1)}, u32[]{:S(2)}, u32[]{:S(2)}) %collective-permute-start.16) | collective-permute-done | bytes 32800 | tf_op jit(solution)/shard_map/ppermute | solution.py:356
  35.3 1.0 %collective-permute-done.17.refs_1_ = bf16[128,128]{1,0:T(8,128)(2,1)S(1)} collective-permute-done((bf16[128,128]{1,0:T(8,128)(2,1)S(1)}, bf16[128,128]{1,0:T(8,128)(2,1)S(1)}, u32[]{:S(2)}, u32[]{:S(2)}) %collective-permute-start.17) | collective-permute-done | bytes 32800 | tf_op jit(solution)/shard_map/ppermute | solution.py:356
  36.7 1.1 %collective-permute-start.20 = (bf16[128,128]{1,0:T(8,128)(2,1)S(1)}, bf16[128,128]{1,0:T(8,128)(2,1)S(1)}, u32[]{:S(2)}, u32[]{:S(2)}) collective-permute-start(bf16[128,128]{1,0:T(8,128)(2,1)S(1)} %get-tuple-element.130), channel_id=1, source_target_pairs={{0,16},{1,17},{2,18},{3,19},{4,20},{5,6},{6,5},{7,8},{8,7},{9,25},... | collective-permute-start | bytes 98312 | tf_op jit(solution)/shard_map/ppermute | solution.py:356
  37.8 1.5 %collective-permute-start.21 = (bf16[128,128]{1,0:T(8,128)(2,1)S(1)}, bf16[128,128]{1,0:T(8,128)(2,1)S(1)}, u32[]{:S(2)}, u32[]{:S(2)}) collective-permute-start(bf16[128,128]{1,0:T(8,128)(2,1)S(1)} %get-tuple-element.131), channel_id=1, source_target_pairs={{0,5},{1,2},{2,1},{3,4},{4,3},{5,0},{6,22},{7,23},{8,24},{9,10},{1... | collective-permute-start | bytes 98312 | tf_op jit(solution)/shard_map/ppermute | solution.py:356
  39.3 0.5 collective-permute-start.23
  39.8 1.3 %shard_map.84 = (f32[128,1024]{1,0:T(8,128)S(1)}, f32[128,384]{1,0:T(8,128)S(1)}) custom-call(bf16[128,128]{1,0:T(8,128)(2,1)S(1)} %collective-permute-done.16.refs_0_, bf16[128,128]{1,0:T(8,128)(2,1)S(1)} %collective-permute-done.17.refs_1_, bf16[128,128]{1,0:T(8,128)(2,1)S(1)} %collective-permute-done.18.refs_2_, ...), custom_call_target="tpu_custom_call" | custom-call | flops 469762048 | bytes 5738496 | tf_op jit(solution)/shard_map/pallas_call | solution.py:321
  41.1 0.8 %collective-permute-done.20.refs_0_ = bf16[128,128]{1,0:T(8,128)(2,1)S(1)} collective-permute-done((bf16[128,128]{1,0:T(8,128)(2,1)S(1)}, bf16[128,128]{1,0:T(8,128)(2,1)S(1)}, u32[]{:S(2)}, u32[]{:S(2)}) %collective-permute-start.20) | collective-permute-done | bytes 32800 | tf_op jit(solution)/shard_map/ppermute | solution.py:356
  41.9 0.8 %collective-permute-done.21.refs_1_ = bf16[128,128]{1,0:T(8,128)(2,1)S(1)} collective-permute-done((bf16[128,128]{1,0:T(8,128)(2,1)S(1)}, bf16[128,128]{1,0:T(8,128)(2,1)S(1)}, u32[]{:S(2)}, u32[]{:S(2)}) %collective-permute-start.21) | collective-permute-done | bytes 32800 | tf_op jit(solution)/shard_map/ppermute | solution.py:356
  43.2 1.3 %collective-permute-start.24 = (bf16[128,128]{1,0:T(8,128)(2,1)S(1)}, bf16[128,128]{1,0:T(8,128)(2,1)S(1)}, u32[]{:S(2)}, u32[]{:S(2)}) collective-permute-start(bf16[128,128]{1,0:T(8,128)(2,1)S(1)} %get-tuple-element.138), channel_id=1, source_target_pairs={{0,16},{1,17},{2,18},{3,19},{4,20},{5,6},{6,5},{7,8},{8,7},{9,25},... | collective-permute-start | bytes 98312 | tf_op jit(solution)/shard_map/ppermute | solution.py:356
  44.5 1.4 %collective-permute-start.25 = (bf16[128,128]{1,0:T(8,128)(2,1)S(1)}, bf16[128,128]{1,0:T(8,128)(2,1)S(1)}, u32[]{:S(2)}, u32[]{:S(2)}) collective-permute-start(bf16[128,128]{1,0:T(8,128)(2,1)S(1)} %get-tuple-element.139), channel_id=1, source_target_pairs={{0,5},{1,2},{2,1},{3,4},{4,3},{5,0},{6,22},{7,23},{8,24},{9,10},{1... | collective-permute-start | bytes 98312 | tf_op jit(solution)/shard_map/ppermute | solution.py:356
  45.9 0.5 collective-permute-start.27
  46.4 1.0 %shard_map.86 = (f32[128,1024]{1,0:T(8,128)S(1)}, f32[128,1024]{1,0:T(8,128)S(1)}, f32[128,384]{1,0:T(8,128)S(1)}) custom-call(bf16[128,128]{1,0:T(8,128)(2,1)S(1)} %collective-permute-done.20.refs_0_, bf16[128,128]{1,0:T(8,128)(2,1)S(1)} %collective-permute-done.21.refs_1_, bf16[128,128]{1,0:T(8,128)(2,1)S(1)} %collective-permute-done.22.refs_2_, ...), custom_call_target="tpu_custom_call" | custom-call | flops 469762048 | bytes 5902336 | tf_op jit(solution)/shard_map/pallas_call | solution.py:321
  47.4 0.9 %collective-permute-done.24.refs_0_ = bf16[128,128]{1,0:T(8,128)(2,1)S(1)} collective-permute-done((bf16[128,128]{1,0:T(8,128)(2,1)S(1)}, bf16[128,128]{1,0:T(8,128)(2,1)S(1)}, u32[]{:S(2)}, u32[]{:S(2)}) %collective-permute-start.24) | collective-permute-done | bytes 32800 | tf_op jit(solution)/shard_map/ppermute | solution.py:356
  48.4 1.0 %collective-permute-done.25.refs_1_ = bf16[128,128]{1,0:T(8,128)(2,1)S(1)} collective-permute-done((bf16[128,128]{1,0:T(8,128)(2,1)S(1)}, bf16[128,128]{1,0:T(8,128)(2,1)S(1)}, u32[]{:S(2)}, u32[]{:S(2)}) %collective-permute-start.25) | collective-permute-done | bytes 32800 | tf_op jit(solution)/shard_map/ppermute | solution.py:356
  49.8 1.1 %collective-permute-start.28 = (bf16[128,128]{1,0:T(8,128)(2,1)S(1)}, bf16[128,128]{1,0:T(8,128)(2,1)S(1)}, u32[]{:S(2)}, u32[]{:S(2)}) collective-permute-start(bf16[128,128]{1,0:T(8,128)(2,1)S(1)} %get-tuple-element.145), channel_id=1, source_target_pairs={{0,16},{1,17},{2,18},{3,19},{4,20},{5,6},{6,5},{7,8},{8,7},{9,25},... | collective-permute-start | bytes 98312 | tf_op jit(solution)/shard_map/ppermute | solution.py:356
  50.9 1.4 %collective-permute-start.29 = (bf16[128,128]{1,0:T(8,128)(2,1)S(1)}, bf16[128,128]{1,0:T(8,128)(2,1)S(1)}, u32[]{:S(2)}, u32[]{:S(2)}) collective-permute-start(bf16[128,128]{1,0:T(8,128)(2,1)S(1)} %get-tuple-element.146), channel_id=1, source_target_pairs={{0,5},{1,2},{2,1},{3,4},{4,3},{5,0},{6,22},{7,23},{8,24},{9,10},{1... | collective-permute-start | bytes 98312 | tf_op jit(solution)/shard_map/ppermute | solution.py:356
  52.3 0.5 collective-permute-start.31
  52.8 1.2 %shard_map.88.refs_5_ = f32[1024,128]{1,0:T(8,128)S(1)} custom-call(bf16[128,128]{1,0:T(8,128)(2,1)S(1)} %collective-permute-done.24.refs_0_, bf16[128,128]{1,0:T(8,128)(2,1)S(1)} %collective-permute-done.25.refs_1_, bf16[128,128]{1,0:T(8,128)(2,1)S(1)} %collective-permute-done.26.refs_2_, bf16[128,128]{1,0:T(8,128)(2,1)S(1)} %collective-permute-done.27.refs_3_, ...), custom_call_target="tpu_custom_call" | custom-call | flops 369098752 | bytes 4624384 | tf_op jit(solution)/shard_map/pallas_call | solution.py:321
  54.0 1.0 %collective-permute-done.28.refs_0_ = bf16[128,128]{1,0:T(8,128)(2,1)S(1)} collective-permute-done((bf16[128,128]{1,0:T(8,128)(2,1)S(1)}, bf16[128,128]{1,0:T(8,128)(2,1)S(1)}, u32[]{:S(2)}, u32[]{:S(2)}) %collective-permute-start.28) | collective-permute-done | bytes 32800 | tf_op jit(solution)/shard_map/ppermute | solution.py:356
  55.0 0.7 %collective-permute-done.29.refs_1_ = bf16[128,128]{1,0:T(8,128)(2,1)S(1)} collective-permute-done((bf16[128,128]{1,0:T(8,128)(2,1)S(1)}, bf16[128,128]{1,0:T(8,128)(2,1)S(1)}, u32[]{:S(2)}, u32[]{:S(2)}) %collective-permute-start.29) | collective-permute-done | bytes 32800 | tf_op jit(solution)/shard_map/ppermute | solution.py:356
  55.7 1.1 %shard_map.89 = f32[1,1024,128]{2,1,0:T(8,128)} custom-call(bf16[128,128]{1,0:T(8,128)(2,1)S(1)} %collective-permute-done.28.refs_0_, bf16[128,128]{1,0:T(8,128)(2,1)S(1)} %collective-permute-done.29.refs_1_, bf16[128,128]{1,0:T(8,128)(2,1)S(1)} %collective-permute-done.30.refs_2_, bf16[128,128]{1,0:T(8,128)(2,1)S(1)} %collective-permute-done.31.refs_3_, ...), custom_call_target="tpu_custom_call" | custom-call | flops 100663296 | bytes 1966080 | tf_op jit(solution)/shard_map/pallas_call | solution.py:321
  (33 shorter events, 2.4 us)
Async XLA Ops:
  1.8 7.7 %collective-permute-start = (bf16[128,128]{1,0:T(8,128)(2,1)S(1)}, bf16[128,128]{1,0:T(8,128)(2,1)S(1)}, u32[]{:S(2)}, u32[]{:S(2)}) collective-permute-start(bf16[128,128]{1,0:T(8,128)(2,1)S(1)} %get-tuple-element.78), channel_id=1, source_target_pairs={{0,16},{1,17},{2,18},{3,19},{4,20},{5,6},{6,5},{7,8},{8,7},{9,25},... | collective-permute-start | bytes 98312 | tf_op jit(solution)/shard_map/ppermute | solution.py:356
  3.6 5.9 %collective-permute-start.1 = (bf16[128,128]{1,0:T(8,128)(2,1)S(1)}, bf16[128,128]{1,0:T(8,128)(2,1)S(1)}, u32[]{:S(2)}, u32[]{:S(2)}) collective-permute-start(bf16[128,128]{1,0:T(8,128)(2,1)S(1)} %get-tuple-element.79), channel_id=1, source_target_pairs={{0,5},{1,2},{2,1},{3,4},{4,3},{5,0},{6,22},{7,23},{8,24},{9,10},{1... | collective-permute-start | bytes 98312 | tf_op jit(solution)/shard_map/ppermute | solution.py:356
  6.2 3.3 %collective-permute-start.2 = (bf16[128,128]{1,0:T(8,128)(2,1)S(1)}, bf16[128,128]{1,0:T(8,128)(2,1)S(1)}, u32[]{:S(2)}, u32[]{:S(2)}) collective-permute-start(bf16[128,128]{1,0:T(8,128)(2,1)S(1)} %get-tuple-element.80), channel_id=1, source_target_pairs={{0,1},{1,0},{2,3},{3,2},{4,12},{5,21},{6,7},{7,6},{8,9},{9,8},{10,... | collective-permute-start | bytes 98312 | tf_op jit(solution)/shard_map/ppermute | solution.py:356
  6.2 3.3 %collective-permute-start.3 = (bf16[128,128]{1,0:T(8,128)(2,1)S(1)}, bf16[128,128]{1,0:T(8,128)(2,1)S(1)}, u32[]{:S(2)}, u32[]{:S(2)}) collective-permute-start(bf16[128,128]{1,0:T(8,128)(2,1)S(1)} %get-tuple-element.81), channel_id=1, source_target_pairs={{0,1},{1,0},{2,3},{3,2},{4,5},{5,4},{6,7},{7,6},{8,9},{9,8},{10,11... | collective-permute-start | bytes 98312 | tf_op jit(solution)/shard_map/ppermute | solution.py:356
  10.0 5.4 %collective-permute-start.4 = (bf16[128,128]{1,0:T(8,128)(2,1)S(1)}, bf16[128,128]{1,0:T(8,128)(2,1)S(1)}, u32[]{:S(2)}, u32[]{:S(2)}) collective-permute-start(bf16[128,128]{1,0:T(8,128)(2,1)S(1)} %get-tuple-element.92), channel_id=1, source_target_pairs={{0,16},{1,17},{2,18},{3,19},{4,20},{5,6},{6,5},{7,8},{8,7},{9,25},... | collective-permute-start | bytes 98312 | tf_op jit(solution)/shard_map/ppermute | solution.py:356
  11.5 4.8 %collective-permute-start.5 = (bf16[128,128]{1,0:T(8,128)(2,1)S(1)}, bf16[128,128]{1,0:T(8,128)(2,1)S(1)}, u32[]{:S(2)}, u32[]{:S(2)}) collective-permute-start(bf16[128,128]{1,0:T(8,128)(2,1)S(1)} %get-tuple-element.93), channel_id=1, source_target_pairs={{0,5},{1,2},{2,1},{3,4},{4,3},{5,0},{6,22},{7,23},{8,24},{9,10},{1... | collective-permute-start | bytes 98312 | tf_op jit(solution)/shard_map/ppermute | solution.py:356
  12.1 4.2 %collective-permute-start.6 = (bf16[128,128]{1,0:T(8,128)(2,1)S(1)}, bf16[128,128]{1,0:T(8,128)(2,1)S(1)}, u32[]{:S(2)}, u32[]{:S(2)}) collective-permute-start(bf16[128,128]{1,0:T(8,128)(2,1)S(1)} %get-tuple-element.94), channel_id=1, source_target_pairs={{0,1},{1,0},{2,3},{3,2},{4,12},{5,21},{6,7},{7,6},{8,9},{9,8},{10,... | collective-permute-start | bytes 98312 | tf_op jit(solution)/shard_map/ppermute | solution.py:356
  12.1 4.2 %collective-permute-start.7 = (bf16[128,128]{1,0:T(8,128)(2,1)S(1)}, bf16[128,128]{1,0:T(8,128)(2,1)S(1)}, u32[]{:S(2)}, u32[]{:S(2)}) collective-permute-start(bf16[128,128]{1,0:T(8,128)(2,1)S(1)} %get-tuple-element.95), channel_id=1, source_target_pairs={{0,1},{1,0},{2,3},{3,2},{4,5},{5,4},{6,7},{7,6},{8,9},{9,8},{10,11... | collective-permute-start | bytes 98312 | tf_op jit(solution)/shard_map/ppermute | solution.py:356
  16.7 5.2 %collective-permute-start.8 = (bf16[128,128]{1,0:T(8,128)(2,1)S(1)}, bf16[128,128]{1,0:T(8,128)(2,1)S(1)}, u32[]{:S(2)}, u32[]{:S(2)}) collective-permute-start(bf16[128,128]{1,0:T(8,128)(2,1)S(1)} %get-tuple-element.104), channel_id=1, source_target_pairs={{0,16},{1,17},{2,18},{3,19},{4,20},{5,6},{6,5},{7,8},{8,7},{9,25},... | collective-permute-start | bytes 98312 | tf_op jit(solution)/shard_map/ppermute | solution.py:356
  18.5 4.8 %collective-permute-start.9 = (bf16[128,128]{1,0:T(8,128)(2,1)S(1)}, bf16[128,128]{1,0:T(8,128)(2,1)S(1)}, u32[]{:S(2)}, u32[]{:S(2)}) collective-permute-start(bf16[128,128]{1,0:T(8,128)(2,1)S(1)} %get-tuple-element.105), channel_id=1, source_target_pairs={{0,5},{1,2},{2,1},{3,4},{4,3},{5,0},{6,22},{7,23},{8,24},{9,10},{1... | collective-permute-start | bytes 98312 | tf_op jit(solution)/shard_map/ppermute | solution.py:356
  20.0 3.4 %collective-permute-start.10 = (bf16[128,128]{1,0:T(8,128)(2,1)S(1)}, bf16[128,128]{1,0:T(8,128)(2,1)S(1)}, u32[]{:S(2)}, u32[]{:S(2)}) collective-permute-start(bf16[128,128]{1,0:T(8,128)(2,1)S(1)} %get-tuple-element.106), channel_id=1, source_target_pairs={{0,1},{1,0},{2,3},{3,2},{4,12},{5,21},{6,7},{7,6},{8,9},{9,8},{10,... | collective-permute-start | bytes 98312 | tf_op jit(solution)/shard_map/ppermute | solution.py:356
  20.0 3.4 %collective-permute-start.11 = (bf16[128,128]{1,0:T(8,128)(2,1)S(1)}, bf16[128,128]{1,0:T(8,128)(2,1)S(1)}, u32[]{:S(2)}, u32[]{:S(2)}) collective-permute-start(bf16[128,128]{1,0:T(8,128)(2,1)S(1)} %get-tuple-element.107), channel_id=1, source_target_pairs={{0,1},{1,0},{2,3},{3,2},{4,5},{5,4},{6,7},{7,6},{8,9},{9,8},{10,11... | collective-permute-start | bytes 98312 | tf_op jit(solution)/shard_map/ppermute | solution.py:356
  23.7 5.5 %collective-permute-start.12 = (bf16[128,128]{1,0:T(8,128)(2,1)S(1)}, bf16[128,128]{1,0:T(8,128)(2,1)S(1)}, u32[]{:S(2)}, u32[]{:S(2)}) collective-permute-start(bf16[128,128]{1,0:T(8,128)(2,1)S(1)} %get-tuple-element.113), channel_id=1, source_target_pairs={{0,16},{1,17},{2,18},{3,19},{4,20},{5,6},{6,5},{7,8},{8,7},{9,25},... | collective-permute-start | bytes 98312 | tf_op jit(solution)/shard_map/ppermute | solution.py:356
  24.9 4.8 %collective-permute-start.13 = (bf16[128,128]{1,0:T(8,128)(2,1)S(1)}, bf16[128,128]{1,0:T(8,128)(2,1)S(1)}, u32[]{:S(2)}, u32[]{:S(2)}) collective-permute-start(bf16[128,128]{1,0:T(8,128)(2,1)S(1)} %get-tuple-element.114), channel_id=1, source_target_pairs={{0,5},{1,2},{2,1},{3,4},{4,3},{5,0},{6,22},{7,23},{8,24},{9,10},{1... | collective-permute-start | bytes 98312 | tf_op jit(solution)/shard_map/ppermute | solution.py:356
  26.3 3.3 %collective-permute-start.14 = (bf16[128,128]{1,0:T(8,128)(2,1)S(1)}, bf16[128,128]{1,0:T(8,128)(2,1)S(1)}, u32[]{:S(2)}, u32[]{:S(2)}) collective-permute-start(bf16[128,128]{1,0:T(8,128)(2,1)S(1)} %get-tuple-element.115), channel_id=1, source_target_pairs={{0,1},{1,0},{2,3},{3,2},{4,12},{5,21},{6,7},{7,6},{8,9},{9,8},{10,... | collective-permute-start | bytes 98312 | tf_op jit(solution)/shard_map/ppermute | solution.py:356
  26.3 3.3 %collective-permute-start.15 = (bf16[128,128]{1,0:T(8,128)(2,1)S(1)}, bf16[128,128]{1,0:T(8,128)(2,1)S(1)}, u32[]{:S(2)}, u32[]{:S(2)}) collective-permute-start(bf16[128,128]{1,0:T(8,128)(2,1)S(1)} %get-tuple-element.116), channel_id=1, source_target_pairs={{0,1},{1,0},{2,3},{3,2},{4,5},{5,4},{6,7},{7,6},{8,9},{9,8},{10,11... | collective-permute-start | bytes 98312 | tf_op jit(solution)/shard_map/ppermute | solution.py:356
  30.1 5.2 %collective-permute-start.16 = (bf16[128,128]{1,0:T(8,128)(2,1)S(1)}, bf16[128,128]{1,0:T(8,128)(2,1)S(1)}, u32[]{:S(2)}, u32[]{:S(2)}) collective-permute-start(bf16[128,128]{1,0:T(8,128)(2,1)S(1)} %get-tuple-element.122), channel_id=1, source_target_pairs={{0,16},{1,17},{2,18},{3,19},{4,20},{5,6},{6,5},{7,8},{8,7},{9,25},... | collective-permute-start | bytes 98312 | tf_op jit(solution)/shard_map/ppermute | solution.py:356
  31.5 4.8 %collective-permute-start.17 = (bf16[128,128]{1,0:T(8,128)(2,1)S(1)}, bf16[128,128]{1,0:T(8,128)(2,1)S(1)}, u32[]{:S(2)}, u32[]{:S(2)}) collective-permute-start(bf16[128,128]{1,0:T(8,128)(2,1)S(1)} %get-tuple-element.123), channel_id=1, source_target_pairs={{0,5},{1,2},{2,1},{3,4},{4,3},{5,0},{6,22},{7,23},{8,24},{9,10},{1... | collective-permute-start | bytes 98312 | tf_op jit(solution)/shard_map/ppermute | solution.py:356
  32.9 3.4 %collective-permute-start.18 = (bf16[128,128]{1,0:T(8,128)(2,1)S(1)}, bf16[128,128]{1,0:T(8,128)(2,1)S(1)}, u32[]{:S(2)}, u32[]{:S(2)}) collective-permute-start(bf16[128,128]{1,0:T(8,128)(2,1)S(1)} %get-tuple-element.124), channel_id=1, source_target_pairs={{0,1},{1,0},{2,3},{3,2},{4,12},{5,21},{6,7},{7,6},{8,9},{9,8},{10,... | collective-permute-start | bytes 98312 | tf_op jit(solution)/shard_map/ppermute | solution.py:356
  32.9 3.4 %collective-permute-start.19 = (bf16[128,128]{1,0:T(8,128)(2,1)S(1)}, bf16[128,128]{1,0:T(8,128)(2,1)S(1)}, u32[]{:S(2)}, u32[]{:S(2)}) collective-permute-start(bf16[128,128]{1,0:T(8,128)(2,1)S(1)} %get-tuple-element.125), channel_id=1, source_target_pairs={{0,1},{1,0},{2,3},{3,2},{4,5},{5,4},{6,7},{7,6},{8,9},{9,8},{10,11... | collective-permute-start | bytes 98312 | tf_op jit(solution)/shard_map/ppermute | solution.py:356
  36.7 5.2 %collective-permute-start.20 = (bf16[128,128]{1,0:T(8,128)(2,1)S(1)}, bf16[128,128]{1,0:T(8,128)(2,1)S(1)}, u32[]{:S(2)}, u32[]{:S(2)}) collective-permute-start(bf16[128,128]{1,0:T(8,128)(2,1)S(1)} %get-tuple-element.130), channel_id=1, source_target_pairs={{0,16},{1,17},{2,18},{3,19},{4,20},{5,6},{6,5},{7,8},{8,7},{9,25},... | collective-permute-start | bytes 98312 | tf_op jit(solution)/shard_map/ppermute | solution.py:356
  37.8 4.9 %collective-permute-start.21 = (bf16[128,128]{1,0:T(8,128)(2,1)S(1)}, bf16[128,128]{1,0:T(8,128)(2,1)S(1)}, u32[]{:S(2)}, u32[]{:S(2)}) collective-permute-start(bf16[128,128]{1,0:T(8,128)(2,1)S(1)} %get-tuple-element.131), channel_id=1, source_target_pairs={{0,5},{1,2},{2,1},{3,4},{4,3},{5,0},{6,22},{7,23},{8,24},{9,10},{1... | collective-permute-start | bytes 98312 | tf_op jit(solution)/shard_map/ppermute | solution.py:356
  39.3 3.4 %collective-permute-start.22 = (bf16[128,128]{1,0:T(8,128)(2,1)S(1)}, bf16[128,128]{1,0:T(8,128)(2,1)S(1)}, u32[]{:S(2)}, u32[]{:S(2)}) collective-permute-start(bf16[128,128]{1,0:T(8,128)(2,1)S(1)} %get-tuple-element.132), channel_id=1, source_target_pairs={{0,1},{1,0},{2,3},{3,2},{4,12},{5,21},{6,7},{7,6},{8,9},{9,8},{10,... | collective-permute-start | bytes 98312 | tf_op jit(solution)/shard_map/ppermute | solution.py:356
  39.3 3.4 %collective-permute-start.23 = (bf16[128,128]{1,0:T(8,128)(2,1)S(1)}, bf16[128,128]{1,0:T(8,128)(2,1)S(1)}, u32[]{:S(2)}, u32[]{:S(2)}) collective-permute-start(bf16[128,128]{1,0:T(8,128)(2,1)S(1)} %get-tuple-element.133), channel_id=1, source_target_pairs={{0,1},{1,0},{2,3},{3,2},{4,5},{5,4},{6,7},{7,6},{8,9},{9,8},{10,11... | collective-permute-start | bytes 98312 | tf_op jit(solution)/shard_map/ppermute | solution.py:356
  43.2 5.2 %collective-permute-start.24 = (bf16[128,128]{1,0:T(8,128)(2,1)S(1)}, bf16[128,128]{1,0:T(8,128)(2,1)S(1)}, u32[]{:S(2)}, u32[]{:S(2)}) collective-permute-start(bf16[128,128]{1,0:T(8,128)(2,1)S(1)} %get-tuple-element.138), channel_id=1, source_target_pairs={{0,16},{1,17},{2,18},{3,19},{4,20},{5,6},{6,5},{7,8},{8,7},{9,25},... | collective-permute-start | bytes 98312 | tf_op jit(solution)/shard_map/ppermute | solution.py:356
  44.5 4.9 %collective-permute-start.25 = (bf16[128,128]{1,0:T(8,128)(2,1)S(1)}, bf16[128,128]{1,0:T(8,128)(2,1)S(1)}, u32[]{:S(2)}, u32[]{:S(2)}) collective-permute-start(bf16[128,128]{1,0:T(8,128)(2,1)S(1)} %get-tuple-element.139), channel_id=1, source_target_pairs={{0,5},{1,2},{2,1},{3,4},{4,3},{5,0},{6,22},{7,23},{8,24},{9,10},{1... | collective-permute-start | bytes 98312 | tf_op jit(solution)/shard_map/ppermute | solution.py:356
  45.9 3.5 %collective-permute-start.26 = (bf16[128,128]{1,0:T(8,128)(2,1)S(1)}, bf16[128,128]{1,0:T(8,128)(2,1)S(1)}, u32[]{:S(2)}, u32[]{:S(2)}) collective-permute-start(bf16[128,128]{1,0:T(8,128)(2,1)S(1)} %get-tuple-element.140), channel_id=1, source_target_pairs={{0,1},{1,0},{2,3},{3,2},{4,12},{5,21},{6,7},{7,6},{8,9},{9,8},{10,... | collective-permute-start | bytes 98312 | tf_op jit(solution)/shard_map/ppermute | solution.py:356
  45.9 3.5 %collective-permute-start.27 = (bf16[128,128]{1,0:T(8,128)(2,1)S(1)}, bf16[128,128]{1,0:T(8,128)(2,1)S(1)}, u32[]{:S(2)}, u32[]{:S(2)}) collective-permute-start(bf16[128,128]{1,0:T(8,128)(2,1)S(1)} %get-tuple-element.141), channel_id=1, source_target_pairs={{0,1},{1,0},{2,3},{3,2},{4,5},{5,4},{6,7},{7,6},{8,9},{9,8},{10,11... | collective-permute-start | bytes 98312 | tf_op jit(solution)/shard_map/ppermute | solution.py:356
  49.8 5.2 %collective-permute-start.28 = (bf16[128,128]{1,0:T(8,128)(2,1)S(1)}, bf16[128,128]{1,0:T(8,128)(2,1)S(1)}, u32[]{:S(2)}, u32[]{:S(2)}) collective-permute-start(bf16[128,128]{1,0:T(8,128)(2,1)S(1)} %get-tuple-element.145), channel_id=1, source_target_pairs={{0,16},{1,17},{2,18},{3,19},{4,20},{5,6},{6,5},{7,8},{8,7},{9,25},... | collective-permute-start | bytes 98312 | tf_op jit(solution)/shard_map/ppermute | solution.py:356
  50.9 4.8 %collective-permute-start.29 = (bf16[128,128]{1,0:T(8,128)(2,1)S(1)}, bf16[128,128]{1,0:T(8,128)(2,1)S(1)}, u32[]{:S(2)}, u32[]{:S(2)}) collective-permute-start(bf16[128,128]{1,0:T(8,128)(2,1)S(1)} %get-tuple-element.146), channel_id=1, source_target_pairs={{0,5},{1,2},{2,1},{3,4},{4,3},{5,0},{6,22},{7,23},{8,24},{9,10},{1... | collective-permute-start | bytes 98312 | tf_op jit(solution)/shard_map/ppermute | solution.py:356
  52.3 3.4 %collective-permute-start.30 = (bf16[128,128]{1,0:T(8,128)(2,1)S(1)}, bf16[128,128]{1,0:T(8,128)(2,1)S(1)}, u32[]{:S(2)}, u32[]{:S(2)}) collective-permute-start(bf16[128,128]{1,0:T(8,128)(2,1)S(1)} %get-tuple-element.147), channel_id=1, source_target_pairs={{0,1},{1,0},{2,3},{3,2},{4,12},{5,21},{6,7},{7,6},{8,9},{9,8},{10,... | collective-permute-start | bytes 98312 | tf_op jit(solution)/shard_map/ppermute | solution.py:356
  52.3 3.4 %collective-permute-start.31 = (bf16[128,128]{1,0:T(8,128)(2,1)S(1)}, bf16[128,128]{1,0:T(8,128)(2,1)S(1)}, u32[]{:S(2)}, u32[]{:S(2)}) collective-permute-start(bf16[128,128]{1,0:T(8,128)(2,1)S(1)} %get-tuple-element.148), channel_id=1, source_target_pairs={{0,1},{1,0},{2,3},{3,2},{4,5},{5,4},{6,7},{7,6},{8,9},{9,8},{10,11... | collective-permute-start | bytes 98312 | tf_op jit(solution)/shard_map/ppermute | solution.py:356

commit v13 on v12

--- a/solution.py
+++ b/solution.py
@@ -81,6 +81,10 @@
     return lax.dot_general(a, b, (((1,), (1,)), ((), ())), preferred_element_type=F32)
 
 
+def together(refs):
+    return jnp.concatenate([ref[...] for ref in refs], 1)
+
+
 def gather(links, refs):
     parts = [ref[...] for ref in refs]
     if len(parts) > links:
@@ -91,6 +95,18 @@
             picked.append(jnp.where(is_turn(own, 0), values[0], later).astype(BF16))
         parts = [*picked, parts[3]]
     return jnp.concatenate(parts, 1)
+
+
+def by_pairing(trips, links, blocks):
+    if trips == links:
+        return blocks
+    far, odd, near = blocks
+    far_turns, odd_turns = turns(2 * FAR)
+    picked = []
+    for turn in range(3):
+        other = jnp.where(is_turn(odd_turns, turn), odd, jnp.zeros_like(odd))
+        picked.append(jnp.where(is_turn(far_turns, turn), far, other))
+    return [*picked, near]
 
 
 def scatter(links, refs, block):
@@ -135,8 +151,10 @@
     width, share = rhs_ref.shape[1], rows_ref.shape[2]
     slots = slots_of(lax.axis_index("sub"), subs)
     place = lax.broadcasted_iota(jnp.int32, (width, share), 0)
-    copies[0].wait()
-    copies[1].wait()
+    for copy in copies[:3]:
+        copy.wait()
+    turned = rhs_ref[0].T
+    turned_ref[...] = turned
     near = near_ref[...].astype(F32)
     lane = lax.broadcasted_iota(jnp.int32, near.shape, 1)
     for k, slot in enumerate(slots):
@@ -144,9 +162,6 @@
         row = jnp.where(partner >= 0.0, rows_ref[0, pl.ds(slot, 1), :], -1)
         list_ref[:, pl.ds(k * share, share)] = jnp.broadcast_to(row.astype(F32), (list_ref.shape[0], share))
         hot_ref[:, pl.ds(k * share, share)] = jnp.where(place == row, 1.0, 0.0).astype(BF16)
-    copies[2].wait()
-    turned = rhs_ref[0].T
-    turned_ref[...] = turned
     picked = times(turned, hot_ref[...]).astype(BF16)
     picked_ref[...] = picked
     scatter(links, out_refs, picked)
@@ -155,6 +170,8 @@
 
 
 def pick_n_kernel(
+    trips,
+    links,
     hot_ref,
     turned_ref,
     list_ref,
@@ -192,22 +209,23 @@
             hot_t_ref[k : k + side, m * side : (m + 1) * side] = block.astype(BF16)
         wide = jnp.concatenate([down] * (total // side), 1)
         same.append(jnp.where((wide == listed) & (wide >= 0.0), 1.0, 0.0))
+    same_ref[...] = jnp.concatenate(by_pairing(trips, links, same), 0).astype(BF16)
     same = jnp.concatenate(same, 0)
-    same_ref[...] = same.astype(BF16)
     inner = jnp.where(jnp.concatenate(hits, 1) > 0.0, 0.0, 1.0)
     inner_ref[...] = jnp.broadcast_to(inner, inner_ref.shape)
     n_pick = times(hot_t_ref[...], n_ref[0]).astype(BF16)
     n_pick_ref[...] = n_pick
-    n_small_ref[...] = times(n_pick, hot).astype(BF16)
     earlier = lax.broadcasted_iota(jnp.int32, same.shape, 0) < lax.broadcasted_iota(jnp.int32, same.shape, 1)
     repeats = jnp.sum(jnp.where(earlier, same, 0.0), 0, keepdims=True)
     first = jnp.where(repeats > 0.0, 0.0, 1.0)
     high = weight.astype(BF16).astype(F32)
     middle = (weight - high).astype(BF16).astype(F32)
     low = weight - high - middle
-    level = lax.broadcasted_iota(jnp.int32, (8, width), 0)
+    level = lax.broadcasted_iota(jnp.int32, (16, width), 0)
     pieces = jnp.where(level == 0, high, jnp.where(level == 1, middle, jnp.where(level == 2, low, 0.0)))
-    pieces = times(pieces.astype(BF16), hot)
+    chosen = times(jnp.concatenate([n_pick, pieces.astype(BF16)], 0), hot)
+    n_small_ref[...] = chosen[:total].astype(BF16)
+    pieces = chosen[total:]
     chosen = (pieces[0:1] + pieces[1:2]) + pieces[2:3]
     row_ref[0:1] = chosen
     row_ref[1:2] = chosen * first
@@ -225,7 +243,7 @@
     arrived_refs, refs = refs[:trips], refs[trips:]
     same_ref, n_small_ref, row_ref, local_ref, base_ref = refs[:5]
     refs = refs[5:]
-    residual = local_ref[...].astype(F32) + times(gather(links, arrived_refs), same_ref[...])
+    residual = local_ref[...].astype(F32) + times(together(arrived_refs), same_ref[...])
     scaled = (row_ref[1:2] * residual).astype(BF16)
     sent = row_ref[0:1] * (base_ref[...] + times_t(scaled, n_small_ref[...]))
     if last:
@@ -241,7 +259,7 @@
 def residual_path_kernel(trips, links, last, *refs):
     arrived_refs, refs = refs[:trips], refs[trips:]
     same_ref, s_small_ref, row_ref, base_ref, state_ref, local_ref = refs[:6]
-    state = state_ref[...] + DAMPING * times(gather(links, arrived_refs), same_ref[...])
+    state = state_ref[...] + DAMPING * times(together(arrived_refs), same_ref[...])
     if last:
         refs = refs[6:]
     else:
@@ -267,8 +285,11 @@
     state_out_ref[...] = state
     s_pick = times(s_ref[0], hot_ref[...]).astype(BF16)
     s_pick_ref[...] = s_pick
-    s_small_ref[...] = times(hot_t_ref[...], s_pick).astype(BF16)
-    base_ref[...] = picked_ref[...].astype(F32) - times((state * inner_ref[:1]).astype(BF16), s_pick)
+    outer = jnp.concatenate([hot_t_ref[...], (state * inner_ref[:1]).astype(BF16)], 0)
+    product = times(outer, s_pick)
+    total = s_small_ref.shape[0]
+    s_small_ref[...] = product[:total].astype(BF16)
+    base_ref[...] = picked_ref[...].astype(F32) - product[total:]
 
 
 def update_kernel(trips, links, *refs):
@@ -381,13 +402,13 @@
     )
     arrived = exchange(sent)
     hot_t, n_pick, n_small, same, inner, mask, local, base, rows, s_mat = run(
-        pick_n_kernel,
+        bound(pick_n_kernel),
         [hot, turned, listed, n_mat, weight, counts, schur],
         [
             array(total, width, BF16),
             array(total, width, BF16),
             small,
-            small,
+            array(trips * share, total, BF16),
             row,
             row,
             full,

time: 57 us -> 58.2 us (1.021)
  Pallas kernels: 17.1 us -> 18.3 us
  waiting for transfers between devices: 11.7 us -> 10.8 us
  starting transfers between devices: 27.2 us -> 28 us
    pallas_call x17, Pallas kernels: 17.1 us -> 18.3 us  [run(): pl.pallas_call(kernel, out_shape=results, in_specs=[pl.BlockSpec(memory_s...]
    ppermute x32, waiting for transfers between devices: 11.7 us -> 10.8 us  [exchange(): lax.ppermute(part, 'sub', route)]
    ppermute x32, starting transfers between devices: 27.2 us -> 28 us  [exchange(): lax.ppermute(part, 'sub', route)]
  transfers between devices with their start and end apart: 32 -> 32, of which waited for: 13 -> 14; matrix products, arithmetic and copies ran while one was open for 0% -> 0% of each run, Pallas kernels for 20% -> 22%
where the time goes in v13:
time: 58.2 us; the launch traced here: 58 us
  starting transfers between devices  28 us (48%)
  Pallas kernels  18.3 us (31%)
  waiting for transfers between devices  10.8 us (19%)
  between operations  0.83 us (1%)
    ppermute x32, starting transfers between devices, exchange(): lax.ppermute(part, 'sub', route)  28 us
    pallas_call x17, Pallas kernels, run(): pl.pallas_call(kernel, out_shape=results, in_specs=[pl.BlockSpec(memory_s...  18.3 us
    ppermute x32, waiting for transfers between devices, exchange(): lax.ppermute(part, 'sub', route)  10.8 us
  transfers between devices with their start and end apart: 32, of which 14 were waited for; matrix products, arithmetic and copies ran while one was open for 0% of the time, Pallas kernels for 22%

profile of v13, /device:TPU:8, one launch (start us, length us, event | category | flops | bytes accessed | tf_op | source)
XLA Modules:
  0.0 58.0 jit_solution(18190534323836922344)
XLA Ops:
  0.0 1.8 %shard_map.73 = (bf16[1024,384]{1,0:T(8,128)(2,1)S(1)}, bf16[128,1024]{1,0:T(8,128)(2,1)S(1)}, bf16[128,384]{1,0:T(8,128)(2,1)S(1)}, f32[8,384]{1,0:T(8,128)S(1)...) custom-call(s32[1,4,128]{2,1,0:T(4,128)} %rows_in.1, ...), custom_call_target="tpu_custom_call" | custom-call | flops 100663296 | bytes 5756944 | tf_op jit(solution)/shard_map/pallas_call | solution.py:342
  1.8 1.8 %collective-permute-start = (bf16[128,128]{1,0:T(8,128)(2,1)S(1)}, bf16[128,128]{1,0:T(8,128)(2,1)S(1)}, u32[]{:S(2)}, u32[]{:S(2)}) collective-permute-start(bf16[128,128]{1,0:T(8,128)(2,1)S(1)} %get-tuple-element.78), channel_id=1, source_target_pairs={{0,16},{1,17},{2,18},{3,19},{4,20},{5,6},{6,5},{7,8},{8,7},{9,25},... | collective-permute-start | bytes 98312 | tf_op jit(solution)/shard_map/ppermute | solution.py:377
  3.6 2.6 %collective-permute-start.1 = (bf16[128,128]{1,0:T(8,128)(2,1)S(1)}, bf16[128,128]{1,0:T(8,128)(2,1)S(1)}, u32[]{:S(2)}, u32[]{:S(2)}) collective-permute-start(bf16[128,128]{1,0:T(8,128)(2,1)S(1)} %get-tuple-element.79), channel_id=1, source_target_pairs={{0,5},{1,2},{2,1},{3,4},{4,3},{5,0},{6,22},{7,23},{8,24},{9,10},{1... | collective-permute-start | bytes 98312 | tf_op jit(solution)/shard_map/ppermute | solution.py:377
  6.2 0.5 collective-permute-start.3
  7.4 3.3 %shard_map.74 = (bf16[384,1024]{1,0:T(8,128)(2,1)S(1)}, bf16[384,1024]{1,0:T(8,128)(2,1)S(1)}, bf16[384,384]{1,0:T(8,128)(2,1)S(1)}, bf16[512,384]{1,0:T(8,128)(...) custom-call(bf16[1024,384]{1,0:T(8,128)(2,1)S(1)} %get-tuple-element, ...), custom_call_target="tpu_custom_call" | custom-call | flops 1207959552 | bytes 10416132 | tf_op jit(solution)/shard_map/pallas_call | solution.py:342
  11.1 1.6 %collective-permute-start.4 = (bf16[128,128]{1,0:T(8,128)(2,1)S(1)}, bf16[128,128]{1,0:T(8,128)(2,1)S(1)}, u32[]{:S(2)}, u32[]{:S(2)}) collective-permute-start(bf16[128,128]{1,0:T(8,128)(2,1)S(1)} %get-tuple-element.92), channel_id=1, source_target_pairs={{0,16},{1,17},{2,18},{3,19},{4,20},{5,6},{6,5},{7,8},{8,7},{9,25},... | collective-permute-start | bytes 98312 | tf_op jit(solution)/shard_map/ppermute | solution.py:377
  13.0 0.5 collective-permute-start.7
  13.5 2.7 %shard_map.76 = (f32[128,1024]{1,0:T(8,128)S(1)}, f32[128,384]{1,0:T(8,128)S(1)}, bf16[1024,384]{1,0:T(8,128)(2,1)S(1)}, bf16[384,384]{1,0:T(8,128)(2,1)S(1)}) custom-call(bf16[128,128]{1,0:T(8,128)(2,1)S(1)} %collective-permute-done.refs_0_, bf16[128,128]{1,0:T(8,128)(2,1)S(1)} %collective-permute-done.1.refs_1_, ...), custom_call_target="tpu_custom_call" | custom-call | flops 1577058304 | bytes 8392704 | tf_op jit(solution)/shard_map/pallas_call | solution.py:342
  16.5 1.0 %collective-permute-done.5.refs_1_ = bf16[128,128]{1,0:T(8,128)(2,1)S(1)} collective-permute-done((bf16[128,128]{1,0:T(8,128)(2,1)S(1)}, bf16[128,128]{1,0:T(8,128)(2,1)S(1)}, u32[]{:S(2)}, u32[]{:S(2)}) %collective-permute-start.5) | collective-permute-done | bytes 32800 | tf_op jit(solution)/shard_map/ppermute | solution.py:377
  17.9 1.4 %collective-permute-start.8 = (bf16[128,128]{1,0:T(8,128)(2,1)S(1)}, bf16[128,128]{1,0:T(8,128)(2,1)S(1)}, u32[]{:S(2)}, u32[]{:S(2)}) collective-permute-start(bf16[128,128]{1,0:T(8,128)(2,1)S(1)} %get-tuple-element.104), channel_id=1, source_target_pairs={{0,16},{1,17},{2,18},{3,19},{4,20},{5,6},{6,5},{7,8},{8,7},{9,25},... | collective-permute-start | bytes 98312 | tf_op jit(solution)/shard_map/ppermute | solution.py:377
  19.3 1.8 %collective-permute-start.9 = (bf16[128,128]{1,0:T(8,128)(2,1)S(1)}, bf16[128,128]{1,0:T(8,128)(2,1)S(1)}, u32[]{:S(2)}, u32[]{:S(2)}) collective-permute-start(bf16[128,128]{1,0:T(8,128)(2,1)S(1)} %get-tuple-element.105), channel_id=1, source_target_pairs={{0,5},{1,2},{2,1},{3,4},{4,3},{5,0},{6,22},{7,23},{8,24},{9,10},{1... | collective-permute-start | bytes 98312 | tf_op jit(solution)/shard_map/ppermute | solution.py:377
  21.1 0.5 collective-permute-start.11
  21.6 1.0 %shard_map.78 = (f32[128,1024]{1,0:T(8,128)S(1)}, f32[128,1024]{1,0:T(8,128)S(1)}, f32[128,384]{1,0:T(8,128)S(1)}) custom-call(bf16[128,128]{1,0:T(8,128)(2,1)S(1)} %collective-permute-done.4.refs_0_, bf16[128,128]{1,0:T(8,128)(2,1)S(1)} %collective-permute-done.5.refs_1_, bf16[128,128]{1,0:T(8,128)(2,1)S(1)} %collective-permute-done.6.refs_2_, ...), custom_call_target="tpu_custom_call" | custom-call | flops 469762048 | bytes 5902336 | tf_op jit(solution)/shard_map/pallas_call | solution.py:342
  22.6 0.5 collective-permute-done.8.refs_0_
  23.1 1.0 %collective-permute-done.9.refs_1_ = bf16[128,128]{1,0:T(8,128)(2,1)S(1)} collective-permute-done((bf16[128,128]{1,0:T(8,128)(2,1)S(1)}, bf16[128,128]{1,0:T(8,128)(2,1)S(1)}, u32[]{:S(2)}, u32[]{:S(2)}) %collective-permute-start.9) | collective-permute-done | bytes 32800 | tf_op jit(solution)/shard_map/ppermute | solution.py:377
  24.1 0.4 shard_map.79
  24.6 1.5 %collective-permute-start.12 = (bf16[128,128]{1,0:T(8,128)(2,1)S(1)}, bf16[128,128]{1,0:T(8,128)(2,1)S(1)}, u32[]{:S(2)}, u32[]{:S(2)}) collective-permute-start(bf16[128,128]{1,0:T(8,128)(2,1)S(1)} %get-tuple-element.113), channel_id=1, source_target_pairs={{0,16},{1,17},{2,18},{3,19},{4,20},{5,6},{6,5},{7,8},{8,7},{9,25},... | collective-permute-start | bytes 98312 | tf_op jit(solution)/shard_map/ppermute | solution.py:377
  26.0 1.5 %collective-permute-start.13 = (bf16[128,128]{1,0:T(8,128)(2,1)S(1)}, bf16[128,128]{1,0:T(8,128)(2,1)S(1)}, u32[]{:S(2)}, u32[]{:S(2)}) collective-permute-start(bf16[128,128]{1,0:T(8,128)(2,1)S(1)} %get-tuple-element.114), channel_id=1, source_target_pairs={{0,5},{1,2},{2,1},{3,4},{4,3},{5,0},{6,22},{7,23},{8,24},{9,10},{1... | collective-permute-start | bytes 98312 | tf_op jit(solution)/shard_map/ppermute | solution.py:377
  27.5 0.5 collective-permute-start.15
  28.0 1.2 %shard_map.80 = (f32[128,1024]{1,0:T(8,128)S(1)}, f32[128,384]{1,0:T(8,128)S(1)}) custom-call(bf16[128,128]{1,0:T(8,128)(2,1)S(1)} %collective-permute-done.8.refs_0_, bf16[128,128]{1,0:T(8,128)(2,1)S(1)} %collective-permute-done.9.refs_1_, bf16[128,128]{1,0:T(8,128)(2,1)S(1)} %collective-permute-done.10.refs_2_, ...), custom_call_target="tpu_custom_call" | custom-call | flops 469762048 | bytes 5738496 | tf_op jit(solution)/shard_map/pallas_call | solution.py:342
  29.3 0.7 %collective-permute-done.12.refs_0_ = bf16[128,128]{1,0:T(8,128)(2,1)S(1)} collective-permute-done((bf16[128,128]{1,0:T(8,128)(2,1)S(1)}, bf16[128,128]{1,0:T(8,128)(2,1)S(1)}, u32[]{:S(2)}, u32[]{:S(2)}) %collective-permute-start.12) | collective-permute-done | bytes 32800 | tf_op jit(solution)/shard_map/ppermute | solution.py:377
  29.9 0.9 %collective-permute-done.13.refs_1_ = bf16[128,128]{1,0:T(8,128)(2,1)S(1)} collective-permute-done((bf16[128,128]{1,0:T(8,128)(2,1)S(1)}, bf16[128,128]{1,0:T(8,128)(2,1)S(1)}, u32[]{:S(2)}, u32[]{:S(2)}) %collective-permute-start.13) | collective-permute-done | bytes 32800 | tf_op jit(solution)/shard_map/ppermute | solution.py:377
  31.2 1.1 %collective-permute-start.16 = (bf16[128,128]{1,0:T(8,128)(2,1)S(1)}, bf16[128,128]{1,0:T(8,128)(2,1)S(1)}, u32[]{:S(2)}, u32[]{:S(2)}) collective-permute-start(bf16[128,128]{1,0:T(8,128)(2,1)S(1)} %get-tuple-element.122), channel_id=1, source_target_pairs={{0,16},{1,17},{2,18},{3,19},{4,20},{5,6},{6,5},{7,8},{8,7},{9,25},... | collective-permute-start | bytes 98312 | tf_op jit(solution)/shard_map/ppermute | solution.py:377
  32.3 1.8 %collective-permute-start.17 = (bf16[128,128]{1,0:T(8,128)(2,1)S(1)}, bf16[128,128]{1,0:T(8,128)(2,1)S(1)}, u32[]{:S(2)}, u32[]{:S(2)}) collective-permute-start(bf16[128,128]{1,0:T(8,128)(2,1)S(1)} %get-tuple-element.123), channel_id=1, source_target_pairs={{0,5},{1,2},{2,1},{3,4},{4,3},{5,0},{6,22},{7,23},{8,24},{9,10},{1... | collective-permute-start | bytes 98312 | tf_op jit(solution)/shard_map/ppermute | solution.py:377
  34.1 0.5 collective-permute-start.19
  34.6 1.0 %shard_map.82 = (f32[128,1024]{1,0:T(8,128)S(1)}, f32[128,1024]{1,0:T(8,128)S(1)}, f32[128,384]{1,0:T(8,128)S(1)}) custom-call(bf16[128,128]{1,0:T(8,128)(2,1)S(1)} %collective-permute-done.12.refs_0_, bf16[128,128]{1,0:T(8,128)(2,1)S(1)} %collective-permute-done.13.refs_1_, bf16[128,128]{1,0:T(8,128)(2,1)S(1)} %collective-permute-done.14.refs_2_, ...), custom_call_target="tpu_custom_call" | custom-call | flops 469762048 | bytes 5902336 | tf_op jit(solution)/shard_map/pallas_call | solution.py:342
  35.6 1.1 %collective-permute-done.16.refs_0_ = bf16[128,128]{1,0:T(8,128)(2,1)S(1)} collective-permute-done((bf16[128,128]{1,0:T(8,128)(2,1)S(1)}, bf16[128,128]{1,0:T(8,128)(2,1)S(1)}, u32[]{:S(2)}, u32[]{:S(2)}) %collective-permute-start.16) | collective-permute-done | bytes 32800 | tf_op jit(solution)/shard_map/ppermute | solution.py:377
  36.7 0.4 collective-permute-done.17.refs_1_
  37.1 0.4 shard_map.83
  37.6 1.5 %collective-permute-start.20 = (bf16[128,128]{1,0:T(8,128)(2,1)S(1)}, bf16[128,128]{1,0:T(8,128)(2,1)S(1)}, u32[]{:S(2)}, u32[]{:S(2)}) collective-permute-start(bf16[128,128]{1,0:T(8,128)(2,1)S(1)} %get-tuple-element.130), channel_id=1, source_target_pairs={{0,16},{1,17},{2,18},{3,19},{4,20},{5,6},{6,5},{7,8},{8,7},{9,25},... | collective-permute-start | bytes 98312 | tf_op jit(solution)/shard_map/ppermute | solution.py:377
  39.0 1.5 %collective-permute-start.21 = (bf16[128,128]{1,0:T(8,128)(2,1)S(1)}, bf16[128,128]{1,0:T(8,128)(2,1)S(1)}, u32[]{:S(2)}, u32[]{:S(2)}) collective-permute-start(bf16[128,128]{1,0:T(8,128)(2,1)S(1)} %get-tuple-element.131), channel_id=1, source_target_pairs={{0,5},{1,2},{2,1},{3,4},{4,3},{5,0},{6,22},{7,23},{8,24},{9,10},{1... | collective-permute-start | bytes 98312 | tf_op jit(solution)/shard_map/ppermute | solution.py:377
  40.5 0.5 collective-permute-start.23
  41.0 1.2 %shard_map.84 = (f32[128,1024]{1,0:T(8,128)S(1)}, f32[128,384]{1,0:T(8,128)S(1)}) custom-call(bf16[128,128]{1,0:T(8,128)(2,1)S(1)} %collective-permute-done.16.refs_0_, bf16[128,128]{1,0:T(8,128)(2,1)S(1)} %collective-permute-done.17.refs_1_, bf16[128,128]{1,0:T(8,128)(2,1)S(1)} %collective-permute-done.18.refs_2_, ...), custom_call_target="tpu_custom_call" | custom-call | flops 469762048 | bytes 5738496 | tf_op jit(solution)/shard_map/pallas_call | solution.py:342
  42.3 0.6 collective-permute-done.20.refs_0_
  42.8 1.1 %collective-permute-done.21.refs_1_ = bf16[128,128]{1,0:T(8,128)(2,1)S(1)} collective-permute-done((bf16[128,128]{1,0:T(8,128)(2,1)S(1)}, bf16[128,128]{1,0:T(8,128)(2,1)S(1)}, u32[]{:S(2)}, u32[]{:S(2)}) %collective-permute-start.21) | collective-permute-done | bytes 32800 | tf_op jit(solution)/shard_map/ppermute | solution.py:377
  44.3 1.0 %collective-permute-start.24 = (bf16[128,128]{1,0:T(8,128)(2,1)S(1)}, bf16[128,128]{1,0:T(8,128)(2,1)S(1)}, u32[]{:S(2)}, u32[]{:S(2)}) collective-permute-start(bf16[128,128]{1,0:T(8,128)(2,1)S(1)} %get-tuple-element.138), channel_id=1, source_target_pairs={{0,16},{1,17},{2,18},{3,19},{4,20},{5,6},{6,5},{7,8},{8,7},{9,25},... | collective-permute-start | bytes 98312 | tf_op jit(solution)/shard_map/ppermute | solution.py:377
  45.3 1.8 %collective-permute-start.25 = (bf16[128,128]{1,0:T(8,128)(2,1)S(1)}, bf16[128,128]{1,0:T(8,128)(2,1)S(1)}, u32[]{:S(2)}, u32[]{:S(2)}) collective-permute-start(bf16[128,128]{1,0:T(8,128)(2,1)S(1)} %get-tuple-element.139), channel_id=1, source_target_pairs={{0,5},{1,2},{2,1},{3,4},{4,3},{5,0},{6,22},{7,23},{8,24},{9,10},{1... | collective-permute-start | bytes 98312 | tf_op jit(solution)/shard_map/ppermute | solution.py:377
  47.1 0.5 collective-permute-start.27
  47.6 1.0 %shard_map.86 = (f32[128,1024]{1,0:T(8,128)S(1)}, f32[128,1024]{1,0:T(8,128)S(1)}, f32[128,384]{1,0:T(8,128)S(1)}) custom-call(bf16[128,128]{1,0:T(8,128)(2,1)S(1)} %collective-permute-done.20.refs_0_, bf16[128,128]{1,0:T(8,128)(2,1)S(1)} %collective-permute-done.21.refs_1_, bf16[128,128]{1,0:T(8,128)(2,1)S(1)} %collective-permute-done.22.refs_2_, ...), custom_call_target="tpu_custom_call" | custom-call | flops 469762048 | bytes 5902336 | tf_op jit(solution)/shard_map/pallas_call | solution.py:342
  48.6 0.9 %collective-permute-done.24.refs_0_ = bf16[128,128]{1,0:T(8,128)(2,1)S(1)} collective-permute-done((bf16[128,128]{1,0:T(8,128)(2,1)S(1)}, bf16[128,128]{1,0:T(8,128)(2,1)S(1)}, u32[]{:S(2)}, u32[]{:S(2)}) %collective-permute-start.24) | collective-permute-done | bytes 32800 | tf_op jit(solution)/shard_map/ppermute | solution.py:377
  49.5 0.6 %collective-permute-done.25.refs_1_ = bf16[128,128]{1,0:T(8,128)(2,1)S(1)} collective-permute-done((bf16[128,128]{1,0:T(8,128)(2,1)S(1)}, bf16[128,128]{1,0:T(8,128)(2,1)S(1)}, u32[]{:S(2)}, u32[]{:S(2)}) %collective-permute-start.25) | collective-permute-done | bytes 32800 | tf_op jit(solution)/shard_map/ppermute | solution.py:377
  50.6 1.5 %collective-permute-start.28 = (bf16[128,128]{1,0:T(8,128)(2,1)S(1)}, bf16[128,128]{1,0:T(8,128)(2,1)S(1)}, u32[]{:S(2)}, u32[]{:S(2)}) collective-permute-start(bf16[128,128]{1,0:T(8,128)(2,1)S(1)} %get-tuple-element.145), channel_id=1, source_target_pairs={{0,16},{1,17},{2,18},{3,19},{4,20},{5,6},{6,5},{7,8},{8,7},{9,25},... | collective-permute-start | bytes 98312 | tf_op jit(solution)/shard_map/ppermute | solution.py:377
  52.1 1.4 %collective-permute-start.29 = (bf16[128,128]{1,0:T(8,128)(2,1)S(1)}, bf16[128,128]{1,0:T(8,128)(2,1)S(1)}, u32[]{:S(2)}, u32[]{:S(2)}) collective-permute-start(bf16[128,128]{1,0:T(8,128)(2,1)S(1)} %get-tuple-element.146), channel_id=1, source_target_pairs={{0,5},{1,2},{2,1},{3,4},{4,3},{5,0},{6,22},{7,23},{8,24},{9,10},{1... | collective-permute-start | bytes 98312 | tf_op jit(solution)/shard_map/ppermute | solution.py:377
  53.5 0.5 collective-permute-start.31
  54.0 1.2 %shard_map.88.refs_5_ = f32[1024,128]{1,0:T(8,128)S(1)} custom-call(bf16[128,128]{1,0:T(8,128)(2,1)S(1)} %collective-permute-done.24.refs_0_, bf16[128,128]{1,0:T(8,128)(2,1)S(1)} %collective-permute-done.25.refs_1_, bf16[128,128]{1,0:T(8,128)(2,1)S(1)} %collective-permute-done.26.refs_2_, bf16[128,128]{1,0:T(8,128)(2,1)S(1)} %collective-permute-done.27.refs_3_, ...), custom_call_target="tpu_custom_call" | custom-call | flops 369098752 | bytes 4624384 | tf_op jit(solution)/shard_map/pallas_call | solution.py:342
  55.2 0.6 %collective-permute-done.28.refs_0_ = bf16[128,128]{1,0:T(8,128)(2,1)S(1)} collective-permute-done((bf16[128,128]{1,0:T(8,128)(2,1)S(1)}, bf16[128,128]{1,0:T(8,128)(2,1)S(1)}, u32[]{:S(2)}, u32[]{:S(2)}) %collective-permute-start.28) | collective-permute-done | bytes 32800 | tf_op jit(solution)/shard_map/ppermute | solution.py:377
  55.8 1.1 %collective-permute-done.29.refs_1_ = bf16[128,128]{1,0:T(8,128)(2,1)S(1)} collective-permute-done((bf16[128,128]{1,0:T(8,128)(2,1)S(1)}, bf16[128,128]{1,0:T(8,128)(2,1)S(1)}, u32[]{:S(2)}, u32[]{:S(2)}) %collective-permute-start.29) | collective-permute-done | bytes 32800 | tf_op jit(solution)/shard_map/ppermute | solution.py:377
  56.9 1.1 %shard_map.89 = f32[1,1024,128]{2,1,0:T(8,128)} custom-call(bf16[128,128]{1,0:T(8,128)(2,1)S(1)} %collective-permute-done.28.refs_0_, bf16[128,128]{1,0:T(8,128)(2,1)S(1)} %collective-permute-done.29.refs_1_, bf16[128,128]{1,0:T(8,128)(2,1)S(1)} %collective-permute-done.30.refs_2_, bf16[128,128]{1,0:T(8,128)(2,1)S(1)} %collective-permute-done.31.refs_3_, ...), custom_call_target="tpu_custom_call" | custom-call | flops 100663296 | bytes 1966080 | tf_op jit(solution)/shard_map/pallas_call | solution.py:342
  (33 shorter events, 2.6 us)
Async XLA Ops:
  1.8 8.9 %collective-permute-start = (bf16[128,128]{1,0:T(8,128)(2,1)S(1)}, bf16[128,128]{1,0:T(8,128)(2,1)S(1)}, u32[]{:S(2)}, u32[]{:S(2)}) collective-permute-start(bf16[128,128]{1,0:T(8,128)(2,1)S(1)} %get-tuple-element.78), channel_id=1, source_target_pairs={{0,16},{1,17},{2,18},{3,19},{4,20},{5,6},{6,5},{7,8},{8,7},{9,25},... | collective-permute-start | bytes 98312 | tf_op jit(solution)/shard_map/ppermute | solution.py:377
  3.6 7.0 %collective-permute-start.1 = (bf16[128,128]{1,0:T(8,128)(2,1)S(1)}, bf16[128,128]{1,0:T(8,128)(2,1)S(1)}, u32[]{:S(2)}, u32[]{:S(2)}) collective-permute-start(bf16[128,128]{1,0:T(8,128)(2,1)S(1)} %get-tuple-element.79), channel_id=1, source_target_pairs={{0,5},{1,2},{2,1},{3,4},{4,3},{5,0},{6,22},{7,23},{8,24},{9,10},{1... | collective-permute-start | bytes 98312 | tf_op jit(solution)/shard_map/ppermute | solution.py:377
  6.2 4.5 %collective-permute-start.2 = (bf16[128,128]{1,0:T(8,128)(2,1)S(1)}, bf16[128,128]{1,0:T(8,128)(2,1)S(1)}, u32[]{:S(2)}, u32[]{:S(2)}) collective-permute-start(bf16[128,128]{1,0:T(8,128)(2,1)S(1)} %get-tuple-element.80), channel_id=1, source_target_pairs={{0,1},{1,0},{2,3},{3,2},{4,12},{5,21},{6,7},{7,6},{8,9},{9,8},{10,... | collective-permute-start | bytes 98312 | tf_op jit(solution)/shard_map/ppermute | solution.py:377
  6.2 4.5 %collective-permute-start.3 = (bf16[128,128]{1,0:T(8,128)(2,1)S(1)}, bf16[128,128]{1,0:T(8,128)(2,1)S(1)}, u32[]{:S(2)}, u32[]{:S(2)}) collective-permute-start(bf16[128,128]{1,0:T(8,128)(2,1)S(1)} %get-tuple-element.81), channel_id=1, source_target_pairs={{0,1},{1,0},{2,3},{3,2},{4,5},{5,4},{6,7},{7,6},{8,9},{9,8},{10,11... | collective-permute-start | bytes 98312 | tf_op jit(solution)/shard_map/ppermute | solution.py:377
  11.1 5.3 %collective-permute-start.4 = (bf16[128,128]{1,0:T(8,128)(2,1)S(1)}, bf16[128,128]{1,0:T(8,128)(2,1)S(1)}, u32[]{:S(2)}, u32[]{:S(2)}) collective-permute-start(bf16[128,128]{1,0:T(8,128)(2,1)S(1)} %get-tuple-element.92), channel_id=1, source_target_pairs={{0,16},{1,17},{2,18},{3,19},{4,20},{5,6},{6,5},{7,8},{8,7},{9,25},... | collective-permute-start | bytes 98312 | tf_op jit(solution)/shard_map/ppermute | solution.py:377
  12.7 4.8 %collective-permute-start.5 = (bf16[128,128]{1,0:T(8,128)(2,1)S(1)}, bf16[128,128]{1,0:T(8,128)(2,1)S(1)}, u32[]{:S(2)}, u32[]{:S(2)}) collective-permute-start(bf16[128,128]{1,0:T(8,128)(2,1)S(1)} %get-tuple-element.93), channel_id=1, source_target_pairs={{0,5},{1,2},{2,1},{3,4},{4,3},{5,0},{6,22},{7,23},{8,24},{9,10},{1... | collective-permute-start | bytes 98312 | tf_op jit(solution)/shard_map/ppermute | solution.py:377
  13.0 4.5 %collective-permute-start.6 = (bf16[128,128]{1,0:T(8,128)(2,1)S(1)}, bf16[128,128]{1,0:T(8,128)(2,1)S(1)}, u32[]{:S(2)}, u32[]{:S(2)}) collective-permute-start(bf16[128,128]{1,0:T(8,128)(2,1)S(1)} %get-tuple-element.94), channel_id=1, source_target_pairs={{0,1},{1,0},{2,3},{3,2},{4,12},{5,21},{6,7},{7,6},{8,9},{9,8},{10,... | collective-permute-start | bytes 98312 | tf_op jit(solution)/shard_map/ppermute | solution.py:377
  13.0 4.5 %collective-permute-start.7 = (bf16[128,128]{1,0:T(8,128)(2,1)S(1)}, bf16[128,128]{1,0:T(8,128)(2,1)S(1)}, u32[]{:S(2)}, u32[]{:S(2)}) collective-permute-start(bf16[128,128]{1,0:T(8,128)(2,1)S(1)} %get-tuple-element.95), channel_id=1, source_target_pairs={{0,1},{1,0},{2,3},{3,2},{4,5},{5,4},{6,7},{7,6},{8,9},{9,8},{10,11... | collective-permute-start | bytes 98312 | tf_op jit(solution)/shard_map/ppermute | solution.py:377
  17.9 5.2 %collective-permute-start.8 = (bf16[128,128]{1,0:T(8,128)(2,1)S(1)}, bf16[128,128]{1,0:T(8,128)(2,1)S(1)}, u32[]{:S(2)}, u32[]{:S(2)}) collective-permute-start(bf16[128,128]{1,0:T(8,128)(2,1)S(1)} %get-tuple-element.104), channel_id=1, source_target_pairs={{0,16},{1,17},{2,18},{3,19},{4,20},{5,6},{6,5},{7,8},{8,7},{9,25},... | collective-permute-start | bytes 98312 | tf_op jit(solution)/shard_map/ppermute | solution.py:377
  19.3 4.8 %collective-permute-start.9 = (bf16[128,128]{1,0:T(8,128)(2,1)S(1)}, bf16[128,128]{1,0:T(8,128)(2,1)S(1)}, u32[]{:S(2)}, u32[]{:S(2)}) collective-permute-start(bf16[128,128]{1,0:T(8,128)(2,1)S(1)} %get-tuple-element.105), channel_id=1, source_target_pairs={{0,5},{1,2},{2,1},{3,4},{4,3},{5,0},{6,22},{7,23},{8,24},{9,10},{1... | collective-permute-start | bytes 98312 | tf_op jit(solution)/shard_map/ppermute | solution.py:377
  21.1 3.0 %collective-permute-start.10 = (bf16[128,128]{1,0:T(8,128)(2,1)S(1)}, bf16[128,128]{1,0:T(8,128)(2,1)S(1)}, u32[]{:S(2)}, u32[]{:S(2)}) collective-permute-start(bf16[128,128]{1,0:T(8,128)(2,1)S(1)} %get-tuple-element.106), channel_id=1, source_target_pairs={{0,1},{1,0},{2,3},{3,2},{4,12},{5,21},{6,7},{7,6},{8,9},{9,8},{10,... | collective-permute-start | bytes 98312 | tf_op jit(solution)/shard_map/ppermute | solution.py:377
  21.1 3.0 %collective-permute-start.11 = (bf16[128,128]{1,0:T(8,128)(2,1)S(1)}, bf16[128,128]{1,0:T(8,128)(2,1)S(1)}, u32[]{:S(2)}, u32[]{:S(2)}) collective-permute-start(bf16[128,128]{1,0:T(8,128)(2,1)S(1)} %get-tuple-element.107), channel_id=1, source_target_pairs={{0,1},{1,0},{2,3},{3,2},{4,5},{5,4},{6,7},{7,6},{8,9},{9,8},{10,11... | collective-permute-start | bytes 98312 | tf_op jit(solution)/shard_map/ppermute | solution.py:377
  24.6 5.4 %collective-permute-start.12 = (bf16[128,128]{1,0:T(8,128)(2,1)S(1)}, bf16[128,128]{1,0:T(8,128)(2,1)S(1)}, u32[]{:S(2)}, u32[]{:S(2)}) collective-permute-start(bf16[128,128]{1,0:T(8,128)(2,1)S(1)} %get-tuple-element.113), channel_id=1, source_target_pairs={{0,16},{1,17},{2,18},{3,19},{4,20},{5,6},{6,5},{7,8},{8,7},{9,25},... | collective-permute-start | bytes 98312 | tf_op jit(solution)/shard_map/ppermute | solution.py:377
  26.0 4.8 %collective-permute-start.13 = (bf16[128,128]{1,0:T(8,128)(2,1)S(1)}, bf16[128,128]{1,0:T(8,128)(2,1)S(1)}, u32[]{:S(2)}, u32[]{:S(2)}) collective-permute-start(bf16[128,128]{1,0:T(8,128)(2,1)S(1)} %get-tuple-element.114), channel_id=1, source_target_pairs={{0,5},{1,2},{2,1},{3,4},{4,3},{5,0},{6,22},{7,23},{8,24},{9,10},{1... | collective-permute-start | bytes 98312 | tf_op jit(solution)/shard_map/ppermute | solution.py:377
  27.5 3.3 %collective-permute-start.14 = (bf16[128,128]{1,0:T(8,128)(2,1)S(1)}, bf16[128,128]{1,0:T(8,128)(2,1)S(1)}, u32[]{:S(2)}, u32[]{:S(2)}) collective-permute-start(bf16[128,128]{1,0:T(8,128)(2,1)S(1)} %get-tuple-element.115), channel_id=1, source_target_pairs={{0,1},{1,0},{2,3},{3,2},{4,12},{5,21},{6,7},{7,6},{8,9},{9,8},{10,... | collective-permute-start | bytes 98312 | tf_op jit(solution)/shard_map/ppermute | solution.py:377
  27.5 3.3 %collective-permute-start.15 = (bf16[128,128]{1,0:T(8,128)(2,1)S(1)}, bf16[128,128]{1,0:T(8,128)(2,1)S(1)}, u32[]{:S(2)}, u32[]{:S(2)}) collective-permute-start(bf16[128,128]{1,0:T(8,128)(2,1)S(1)} %get-tuple-element.116), channel_id=1, source_target_pairs={{0,1},{1,0},{2,3},{3,2},{4,5},{5,4},{6,7},{7,6},{8,9},{9,8},{10,11... | collective-permute-start | bytes 98312 | tf_op jit(solution)/shard_map/ppermute | solution.py:377
  31.2 5.5 %collective-permute-start.16 = (bf16[128,128]{1,0:T(8,128)(2,1)S(1)}, bf16[128,128]{1,0:T(8,128)(2,1)S(1)}, u32[]{:S(2)}, u32[]{:S(2)}) collective-permute-start(bf16[128,128]{1,0:T(8,128)(2,1)S(1)} %get-tuple-element.122), channel_id=1, source_target_pairs={{0,16},{1,17},{2,18},{3,19},{4,20},{5,6},{6,5},{7,8},{8,7},{9,25},... | collective-permute-start | bytes 98312 | tf_op jit(solution)/shard_map/ppermute | solution.py:377
  32.3 4.8 %collective-permute-start.17 = (bf16[128,128]{1,0:T(8,128)(2,1)S(1)}, bf16[128,128]{1,0:T(8,128)(2,1)S(1)}, u32[]{:S(2)}, u32[]{:S(2)}) collective-permute-start(bf16[128,128]{1,0:T(8,128)(2,1)S(1)} %get-tuple-element.123), channel_id=1, source_target_pairs={{0,5},{1,2},{2,1},{3,4},{4,3},{5,0},{6,22},{7,23},{8,24},{9,10},{1... | collective-permute-start | bytes 98312 | tf_op jit(solution)/shard_map/ppermute | solution.py:377
  34.1 3.0 %collective-permute-start.18 = (bf16[128,128]{1,0:T(8,128)(2,1)S(1)}, bf16[128,128]{1,0:T(8,128)(2,1)S(1)}, u32[]{:S(2)}, u32[]{:S(2)}) collective-permute-start(bf16[128,128]{1,0:T(8,128)(2,1)S(1)} %get-tuple-element.124), channel_id=1, source_target_pairs={{0,1},{1,0},{2,3},{3,2},{4,12},{5,21},{6,7},{7,6},{8,9},{9,8},{10,... | collective-permute-start | bytes 98312 | tf_op jit(solution)/shard_map/ppermute | solution.py:377
  34.1 3.0 %collective-permute-start.19 = (bf16[128,128]{1,0:T(8,128)(2,1)S(1)}, bf16[128,128]{1,0:T(8,128)(2,1)S(1)}, u32[]{:S(2)}, u32[]{:S(2)}) collective-permute-start(bf16[128,128]{1,0:T(8,128)(2,1)S(1)} %get-tuple-element.125), channel_id=1, source_target_pairs={{0,1},{1,0},{2,3},{3,2},{4,5},{5,4},{6,7},{7,6},{8,9},{9,8},{10,11... | collective-permute-start | bytes 98312 | tf_op jit(solution)/shard_map/ppermute | solution.py:377
  37.6 5.3 %collective-permute-start.20 = (bf16[128,128]{1,0:T(8,128)(2,1)S(1)}, bf16[128,128]{1,0:T(8,128)(2,1)S(1)}, u32[]{:S(2)}, u32[]{:S(2)}) collective-permute-start(bf16[128,128]{1,0:T(8,128)(2,1)S(1)} %get-tuple-element.130), channel_id=1, source_target_pairs={{0,16},{1,17},{2,18},{3,19},{4,20},{5,6},{6,5},{7,8},{8,7},{9,25},... | collective-permute-start | bytes 98312 | tf_op jit(solution)/shard_map/ppermute | solution.py:377
  39.0 4.9 %collective-permute-start.21 = (bf16[128,128]{1,0:T(8,128)(2,1)S(1)}, bf16[128,128]{1,0:T(8,128)(2,1)S(1)}, u32[]{:S(2)}, u32[]{:S(2)}) collective-permute-start(bf16[128,128]{1,0:T(8,128)(2,1)S(1)} %get-tuple-element.131), channel_id=1, source_target_pairs={{0,5},{1,2},{2,1},{3,4},{4,3},{5,0},{6,22},{7,23},{8,24},{9,10},{1... | collective-permute-start | bytes 98312 | tf_op jit(solution)/shard_map/ppermute | solution.py:377
  40.5 3.4 %collective-permute-start.22 = (bf16[128,128]{1,0:T(8,128)(2,1)S(1)}, bf16[128,128]{1,0:T(8,128)(2,1)S(1)}, u32[]{:S(2)}, u32[]{:S(2)}) collective-permute-start(bf16[128,128]{1,0:T(8,128)(2,1)S(1)} %get-tuple-element.132), channel_id=1, source_target_pairs={{0,1},{1,0},{2,3},{3,2},{4,12},{5,21},{6,7},{7,6},{8,9},{9,8},{10,... | collective-permute-start | bytes 98312 | tf_op jit(solution)/shard_map/ppermute | solution.py:377
  40.5 3.4 %collective-permute-start.23 = (bf16[128,128]{1,0:T(8,128)(2,1)S(1)}, bf16[128,128]{1,0:T(8,128)(2,1)S(1)}, u32[]{:S(2)}, u32[]{:S(2)}) collective-permute-start(bf16[128,128]{1,0:T(8,128)(2,1)S(1)} %get-tuple-element.133), channel_id=1, source_target_pairs={{0,1},{1,0},{2,3},{3,2},{4,5},{5,4},{6,7},{7,6},{8,9},{9,8},{10,11... | collective-permute-start | bytes 98312 | tf_op jit(solution)/shard_map/ppermute | solution.py:377
  44.3 5.2 %collective-permute-start.24 = (bf16[128,128]{1,0:T(8,128)(2,1)S(1)}, bf16[128,128]{1,0:T(8,128)(2,1)S(1)}, u32[]{:S(2)}, u32[]{:S(2)}) collective-permute-start(bf16[128,128]{1,0:T(8,128)(2,1)S(1)} %get-tuple-element.138), channel_id=1, source_target_pairs={{0,16},{1,17},{2,18},{3,19},{4,20},{5,6},{6,5},{7,8},{8,7},{9,25},... | collective-permute-start | bytes 98312 | tf_op jit(solution)/shard_map/ppermute | solution.py:377
  45.3 4.8 %collective-permute-start.25 = (bf16[128,128]{1,0:T(8,128)(2,1)S(1)}, bf16[128,128]{1,0:T(8,128)(2,1)S(1)}, u32[]{:S(2)}, u32[]{:S(2)}) collective-permute-start(bf16[128,128]{1,0:T(8,128)(2,1)S(1)} %get-tuple-element.139), channel_id=1, source_target_pairs={{0,5},{1,2},{2,1},{3,4},{4,3},{5,0},{6,22},{7,23},{8,24},{9,10},{1... | collective-permute-start | bytes 98312 | tf_op jit(solution)/shard_map/ppermute | solution.py:377
  47.1 3.1 %collective-permute-start.26 = (bf16[128,128]{1,0:T(8,128)(2,1)S(1)}, bf16[128,128]{1,0:T(8,128)(2,1)S(1)}, u32[]{:S(2)}, u32[]{:S(2)}) collective-permute-start(bf16[128,128]{1,0:T(8,128)(2,1)S(1)} %get-tuple-element.140), channel_id=1, source_target_pairs={{0,1},{1,0},{2,3},{3,2},{4,12},{5,21},{6,7},{7,6},{8,9},{9,8},{10,... | collective-permute-start | bytes 98312 | tf_op jit(solution)/shard_map/ppermute | solution.py:377
  47.1 3.1 %collective-permute-start.27 = (bf16[128,128]{1,0:T(8,128)(2,1)S(1)}, bf16[128,128]{1,0:T(8,128)(2,1)S(1)}, u32[]{:S(2)}, u32[]{:S(2)}) collective-permute-start(bf16[128,128]{1,0:T(8,128)(2,1)S(1)} %get-tuple-element.141), channel_id=1, source_target_pairs={{0,1},{1,0},{2,3},{3,2},{4,5},{5,4},{6,7},{7,6},{8,9},{9,8},{10,11... | collective-permute-start | bytes 98312 | tf_op jit(solution)/shard_map/ppermute | solution.py:377
  50.6 5.2 %collective-permute-start.28 = (bf16[128,128]{1,0:T(8,128)(2,1)S(1)}, bf16[128,128]{1,0:T(8,128)(2,1)S(1)}, u32[]{:S(2)}, u32[]{:S(2)}) collective-permute-start(bf16[128,128]{1,0:T(8,128)(2,1)S(1)} %get-tuple-element.145), channel_id=1, source_target_pairs={{0,16},{1,17},{2,18},{3,19},{4,20},{5,6},{6,5},{7,8},{8,7},{9,25},... | collective-permute-start | bytes 98312 | tf_op jit(solution)/shard_map/ppermute | solution.py:377
  52.1 4.8 %collective-permute-start.29 = (bf16[128,128]{1,0:T(8,128)(2,1)S(1)}, bf16[128,128]{1,0:T(8,128)(2,1)S(1)}, u32[]{:S(2)}, u32[]{:S(2)}) collective-permute-start(bf16[128,128]{1,0:T(8,128)(2,1)S(1)} %get-tuple-element.146), channel_id=1, source_target_pairs={{0,5},{1,2},{2,1},{3,4},{4,3},{5,0},{6,22},{7,23},{8,24},{9,10},{1... | collective-permute-start | bytes 98312 | tf_op jit(solution)/shard_map/ppermute | solution.py:377
  53.5 3.4 %collective-permute-start.30 = (bf16[128,128]{1,0:T(8,128)(2,1)S(1)}, bf16[128,128]{1,0:T(8,128)(2,1)S(1)}, u32[]{:S(2)}, u32[]{:S(2)}) collective-permute-start(bf16[128,128]{1,0:T(8,128)(2,1)S(1)} %get-tuple-element.147), channel_id=1, source_target_pairs={{0,1},{1,0},{2,3},{3,2},{4,12},{5,21},{6,7},{7,6},{8,9},{9,8},{10,... | collective-permute-start | bytes 98312 | tf_op jit(solution)/shard_map/ppermute | solution.py:377
  53.5 3.4 %collective-permute-start.31 = (bf16[128,128]{1,0:T(8,128)(2,1)S(1)}, bf16[128,128]{1,0:T(8,128)(2,1)S(1)}, u32[]{:S(2)}, u32[]{:S(2)}) collective-permute-start(bf16[128,128]{1,0:T(8,128)(2,1)S(1)} %get-tuple-element.148), channel_id=1, source_target_pairs={{0,1},{1,0},{2,3},{3,2},{4,5},{5,4},{6,7},{7,6},{8,9},{9,8},{10,11... | collective-permute-start | bytes 98312 | tf_op jit(solution)/shard_map/ppermute | solution.py:377

commit v14 on v12

--- a/solution.py
+++ b/solution.py
@@ -16,14 +16,29 @@
 BF16 = jnp.bfloat16
 
 
-FAR_TURNS = (0, 0, 0, 0, 0, 2, 1, 1, 1, 0, 0, 0, 0, 0, 1, 2)
-ODD_TURNS = (1, 1, 0, 0, 1, 1, 2, 1, 1, 1, 0, 0, 1, 1, 2)
-FILL = ((), ((0, 5), (13, 21), (29, 31)), ((4, 12), (20, 28)))
-
-
-def turns(count):
-    far = [FAR_TURNS[i % FAR] for i in range(count)]
-    odd = [ODD_TURNS[(i - 1) // 2] if 0 < i < count - 1 else -1 for i in range(count)]
+PLANS = (
+    (
+        (1, 1, 2, 1, 1, 1, 1, 0, 0, 0, 0, 0, 2, 1, 1, 1),
+        (0, 0, 2, 1, 1, 1, 0, 2, 0, 0, 0, 1, 1, 1, 2),
+        (((0, 5), (6, 15), (12, 16)), ((2, 18),), ((3, 7), (4, 13), (14, 31), (17, 19))),
+    ),
+    (
+        (1, 1, 1, 2, 2, 1, 1, 0, 0, 0, 2, 0, 1, 1, 1, 1),
+        (0, 1, 0, 1, 1, 2, 2, 2, 2, 1, 2, 1, 1, 2, 2),
+        (((0, 4), (3, 10), (22, 26)), ((11, 27),), ((2, 5), (23, 31))),
+    ),
+    (
+        (0, 0, 0, 0, 0, 2, 1, 1, 1, 0, 0, 1, 1, 0, 0, 0),
+        (1, 1, 0, 0, 1, 0, 2, 1, 1, 1, 0, 0, 1, 0, 2),
+        ((), ((0, 5), (13, 14), (21, 29)), ((4, 12), (15, 20), (28, 31))),
+    ),
+)
+
+
+def turns(count, plan):
+    far_turns, odd_turns, _ = PLANS[plan]
+    far = [far_turns[i % FAR] for i in range(count)]
+    odd = [odd_turns[(i - 1) // 2] if 0 < i < count - 1 else -1 for i in range(count)]
     return far, odd
 
 
@@ -31,15 +46,15 @@
     return count == 2 * FAR
 
 
-def swaps(count):
+def swaps(count, plan):
     blocks = count // FAR
     near = [i ^ 1 for i in range(count)]
     far = [i ^ FAR for i in range(count)]
     odd = [(((i + 1) ^ 1) - 1) % count for i in range(count)]
     if mixed(count):
-        far_turns, odd_turns = turns(count)
+        far_turns, odd_turns = turns(count, plan)
         pairings = []
-        for turn, fill in enumerate(FILL):
+        for turn, fill in enumerate(PLANS[plan][2]):
             pairing = list(near)
             for i, j in fill:
                 pairing[i], pairing[j] = j, i
@@ -81,24 +96,24 @@
     return lax.dot_general(a, b, (((1,), (1,)), ((), ())), preferred_element_type=F32)
 
 
-def gather(links, refs):
+def gather(links, plan, refs):
     parts = [ref[...] for ref in refs]
     if len(parts) > links:
         values = [part.astype(F32) for part in parts[:3]]
         picked = []
-        for own in turns(2 * FAR):
+        for own in turns(2 * FAR, plan):
             later = jnp.where(is_turn(own, 1), values[1], values[2])
             picked.append(jnp.where(is_turn(own, 0), values[0], later).astype(BF16))
         parts = [*picked, parts[3]]
     return jnp.concatenate(parts, 1)
 
 
-def scatter(links, refs, block):
+def scatter(links, plan, refs, block):
     share = refs[0].shape[1]
     parts = [block[:, k * share : (k + 1) * share].astype(F32) for k in range(links)]
     if len(refs) > links:
         far, odd, near = parts
-        own, _ = turns(2 * FAR)
+        own, _ = turns(2 * FAR, plan)
         parts = [*(jnp.where(is_turn(own, turn), far, odd) for turn in range(3)), near]
     for ref, part in zip(refs, parts):
         ref[...] = part.astype(BF16)
@@ -107,6 +122,7 @@
 def open_kernel(
     trips,
     links,
+    plan_out,
     subs,
     rows_in,
     near_in,
@@ -149,7 +165,7 @@
     turned_ref[...] = turned
     picked = times(turned, hot_ref[...]).astype(BF16)
     picked_ref[...] = picked
-    scatter(links, out_refs, picked)
+    scatter(links, plan_out, out_refs, picked)
     for copy in copies[3:]:
         copy.wait()
 
@@ -221,27 +237,27 @@
     copy.wait()
 
 
-def update_path_kernel(trips, links, step, last, *refs):
+def update_path_kernel(trips, links, plan, plan_out, step, last, *refs):
     arrived_refs, refs = refs[:trips], refs[trips:]
     same_ref, n_small_ref, row_ref, local_ref, base_ref = refs[:5]
     refs = refs[5:]
-    residual = local_ref[...].astype(F32) + times(gather(links, arrived_refs), same_ref[...])
+    residual = local_ref[...].astype(F32) + times(gather(links, plan, arrived_refs), same_ref[...])
     scaled = (row_ref[1:2] * residual).astype(BF16)
     sent = row_ref[0:1] * (base_ref[...] + times_t(scaled, n_small_ref[...]))
     if last:
-        scatter(links, refs, sent)
+        scatter(links, plan_out, refs, sent)
     elif step == 0:
-        scatter(links, refs[1:], sent)
+        scatter(links, plan_out, refs[1:], sent)
         refs[0][...] = DAMPING * sent
     else:
-        scatter(links, refs[2:], sent)
+        scatter(links, plan_out, refs[2:], sent)
         refs[1][...] = refs[0][...] + DAMPING * sent
 
 
-def residual_path_kernel(trips, links, last, *refs):
+def residual_path_kernel(trips, links, plan, plan_out, last, *refs):
     arrived_refs, refs = refs[:trips], refs[trips:]
     same_ref, s_small_ref, row_ref, base_ref, state_ref, local_ref = refs[:6]
-    state = state_ref[...] + DAMPING * times(gather(links, arrived_refs), same_ref[...])
+    state = state_ref[...] + DAMPING * times(gather(links, plan, arrived_refs), same_ref[...])
     if last:
         refs = refs[6:]
     else:
@@ -249,21 +265,21 @@
         refs = refs[7:]
     local = base_ref[...] - times((state * row_ref[2:3]).astype(BF16), s_small_ref[...])
     local_ref[...] = local
-    scatter(links, refs, local)
-
-
-def corrected(links, arrived_refs, hot_ref, n_ref, weight_ref, mask_ref, local_ref):
+    scatter(links, plan_out, refs, local)
+
+
+def corrected(links, plan, arrived_refs, hot_ref, n_ref, weight_ref, mask_ref, local_ref):
     weight = weight_ref[...]
-    residual = local_ref[...] + times_t(gather(links, arrived_refs), hot_ref[...])
+    residual = local_ref[...] + times_t(gather(links, plan, arrived_refs), hot_ref[...])
     scaled = (weight * residual).astype(BF16)
     return mask_ref[:1] * weight * times_t(scaled, n_ref[0])
 
 
-def first_update_kernel(trips, links, *refs):
+def first_update_kernel(trips, links, plan, *refs):
     arrived_refs, refs = refs[:trips], refs[trips:]
     hot_ref, hot_t_ref, n_ref, s_ref, weight_ref, mask_ref, inner_ref, local_ref, picked_ref = refs[:9]
     state_out_ref, base_ref, s_pick_ref, s_small_ref = refs[9:]
-    state = DAMPING * corrected(links, arrived_refs, hot_ref, n_ref, weight_ref, mask_ref, local_ref)
+    state = DAMPING * corrected(links, plan, arrived_refs, hot_ref, n_ref, weight_ref, mask_ref, local_ref)
     state_out_ref[...] = state
     s_pick = times(s_ref[0], hot_ref[...]).astype(BF16)
     s_pick_ref[...] = s_pick
@@ -271,36 +287,36 @@
     base_ref[...] = picked_ref[...].astype(F32) - times((state * inner_ref[:1]).astype(BF16), s_pick)
 
 
-def update_kernel(trips, links, *refs):
+def update_kernel(trips, links, plan, *refs):
     arrived_refs, refs = refs[:trips], refs[trips:]
     hot_ref, n_ref, weight_ref, mask_ref, inner_ref, local_ref, picked_ref, s_pick_ref, state_ref = refs[:9]
     state_out_ref, base_ref = refs[9:]
-    state = state_ref[...] + DAMPING * corrected(links, arrived_refs, hot_ref, n_ref, weight_ref, mask_ref, local_ref)
+    state = state_ref[...] + DAMPING * corrected(links, plan, arrived_refs, hot_ref, n_ref, weight_ref, mask_ref, local_ref)
     state_out_ref[...] = state
     base_ref[...] = picked_ref[...].astype(F32) - times((state * inner_ref[:1]).astype(BF16), s_pick_ref[...])
 
 
-def last_update_kernel(trips, links, *refs):
+def last_update_kernel(trips, links, plan, *refs):
     arrived_refs, refs = refs[:trips], refs[trips:]
     hot_ref, n_ref, weight_ref, mask_ref, local_ref, state_ref, state_out_ref = refs
-    update = corrected(links, arrived_refs, hot_ref, n_ref, weight_ref, mask_ref, local_ref)
+    update = corrected(links, plan, arrived_refs, hot_ref, n_ref, weight_ref, mask_ref, local_ref)
     state_out_ref[...] = (state_ref[...] + DAMPING * update).T
 
 
-def residual_kernel(trips, links, *refs):
+def residual_kernel(trips, links, plan, *refs):
     arrived_refs, refs = refs[:trips], refs[trips:]
     hot_ref, s_ref, turned_ref, weight_ref, mask_ref, inner_ref, n_pick_ref, state_ref = refs[:8]
     state_out_ref, local_ref, base_ref = refs[8:]
-    state = state_ref[...] + DAMPING * times_t(gather(links, arrived_refs), hot_ref[...])
+    state = state_ref[...] + DAMPING * times_t(gather(links, plan, arrived_refs), hot_ref[...])
     state_out_ref[...] = state
     local = mask_ref[:1] * (turned_ref[...].astype(F32) - times(state.astype(BF16), s_ref[0]))
     local_ref[...] = local
     base_ref[...] = times_t((weight_ref[...] * local * inner_ref[:1]).astype(BF16), n_pick_ref[...])
 
 
-def close_kernel(trips, links, *refs):
+def close_kernel(trips, links, plan, *refs):
     arrived_refs, (hot_ref, state_ref, out_ref, piece_ref, sems) = refs[:trips], refs[trips:]
-    arrived = gather(links, arrived_refs)
+    arrived = gather(links, plan, arrived_refs)
     rows = state_ref.shape[0] // PIECES
     copies = []
     for k in range(PIECES):
@@ -333,8 +349,8 @@
     width, leads = right_side.shape[1:]
     share = shared_rows.shape[2]
     subs = lax.axis_size("sub")
-    routes = swaps(subs)
-    trips = len(routes)
+    plans = [min(k, len(PLANS) - 1) for k in range(2 * ITERS)]
+    trips = len(swaps(subs, plans[0]))
     links = len(slots_of(0, subs))
     total = links * share
 
@@ -352,14 +368,14 @@
     whole = 2 * leads * width * width
     path = 4 * leads * total * total
 
-    def exchange(parts):
-        return [lax.ppermute(part, "sub", route) for part, route in zip(parts, routes)]
+    def exchange(parts, plan):
+        return [lax.ppermute(part, "sub", route) for part, route in zip(parts, swaps(subs, plan))]
 
     def bound(kernel, *settings):
         return functools.partial(kernel, trips, links, *settings)
 
     hot, turned, picked, listed, weight, n_mat, *sent = run(
-        bound(open_kernel, subs),
+        bound(open_kernel, plans[0], subs),
         [shared_rows, neighbours, right_side, weights, neumann],
         [
             array(width, total, BF16),
@@ -379,7 +395,7 @@
             pltpu.SemaphoreType.DMA((5,)),
         ],
     )
-    arrived = exchange(sent)
+    arrived = exchange(sent, plans[0])
     hot_t, n_pick, n_small, same, inner, mask, local, base, rows, s_mat = run(
         pick_n_kernel,
         [hot, turned, listed, n_mat, weight, counts, schur],
@@ -403,32 +419,33 @@
     near_state = None
     for step in range(ITERS):
         came, last = arrived, step == ITERS - 1
+        plan, next_plan, after = (*plans[2 * step :], None)[:3]
         operands = [*came, same, n_small, rows, near, base]
         if step and not last:
             operands.append(near_state)
-        kernel = bound(update_path_kernel, step, last)
+        kernel = bound(update_path_kernel, plan, next_plan, step, last)
         if last:
             sent = run(kernel, operands, messages, path)
-            arrived = exchange(sent)
+            arrived = exchange(sent, next_plan)
             (state,) = run(
-                bound(last_update_kernel),
+                bound(last_update_kernel, plan),
                 [*came, hot, n_mat, weight, mask, local, state],
                 [array(width, leads)],
                 whole + picks,
             )
             break
         near_state, *sent = run(kernel, operands, [some, *messages], path)
-        arrived = exchange(sent)
+        arrived = exchange(sent, next_plan)
         if step == 0:
             state, base, s_pick, s_small = run(
-                bound(first_update_kernel),
+                bound(first_update_kernel, plan),
                 [*came, hot, hot_t, n_mat, s_mat, weight, mask, inner, local, picked],
                 [full, some, array(width, total, BF16), small],
                 whole + 2 * picks + 2 * total * width * (width + total),
             )
         else:
             state, base = run(
-                bound(update_kernel),
+                bound(update_kernel, plan),
                 [*came, hot, n_mat, weight, mask, inner, local, picked, s_pick, state],
                 [full, some],
                 whole + 2 * picks,
@@ -436,22 +453,22 @@
         came = arrived
         ends = step == ITERS - 2
         near, *sent = run(
-            bound(residual_path_kernel, ends),
+            bound(residual_path_kernel, next_plan, after, ends),
             [*came, same, s_small, rows, base, near_state],
             [some, *([] if ends else [some]), *messages],
             path,
         )
         if not ends:
             near_state, *sent = sent
-        arrived = exchange(sent)
+        arrived = exchange(sent, after)
         state, local, base = run(
-            bound(residual_kernel),
+            bound(residual_kernel, next_plan),
             [*came, hot, s_mat, turned, weight, mask, inner, n_pick, state],
             [full, full, some],
             whole + 2 * picks,
         )
     (out,) = run(
-        bound(close_kernel),
+        bound(close_kernel, plans[-1]),
         [*arrived, hot, state],
         [jax.ShapeDtypeStruct((1, width, leads), F32)],
         picks,

time: 57 us -> 57.2 us (level)
  starting transfers between devices: 27.2 us -> 29.2 us
  waiting for transfers between devices: 11.7 us -> 9.82 us
    ppermute x32, starting transfers between devices: 27.2 us -> 29.2 us  [exchange(): lax.ppermute(part, 'sub', route)]
    ppermute x32, waiting for transfers between devices: 11.7 us -> 9.82 us  [exchange(): lax.ppermute(part, 'sub', route)]
where the time goes in v14:
time: 57.2 us; the launch traced here: 57 us
  starting transfers between devices  29.2 us (51%)
  Pallas kernels  17.1 us (30%)
  waiting for transfers between devices  9.82 us (17%)
  between operations  0.81 us (1%)
    ppermute x32, starting transfers between devices, exchange(): lax.ppermute(part, 'sub', route)  29.2 us
    pallas_call x17, Pallas kernels, run(): pl.pallas_call(kernel, out_shape=results, in_specs=[pl.BlockSpec(memory_s...  17.1 us
    ppermute x32, waiting for transfers between devices, exchange(): lax.ppermute(part, 'sub', route)  9.82 us
  transfers between devices with their start and end apart: 32, of which 13 were waited for; matrix products, arithmetic and copies ran while one was open for 0% of the time, Pallas kernels for 20%

profile of v14, /device:TPU:8, one launch (start us, length us, event | category | flops | bytes accessed | tf_op | source)
XLA Modules:
  0.0 57.0 jit_solution(11406153654567865709)
XLA Ops:
  0.0 1.8 %shard_map.73 = (bf16[1024,384]{1,0:T(8,128)(2,1)S(1)}, bf16[128,1024]{1,0:T(8,128)(2,1)S(1)}, bf16[128,384]{1,0:T(8,128)(2,1)S(1)}, f32[8,384]{1,0:T(8,128)S(1)...) custom-call(s32[1,4,128]{2,1,0:T(4,128)} %rows_in.1, ...), custom_call_target="tpu_custom_call" | custom-call | flops 100663296 | bytes 5756944 | tf_op jit(solution)/shard_map/pallas_call | solution.py:337
  1.8 2.7 %collective-permute-start = (bf16[128,128]{1,0:T(8,128)(2,1)S(1)}, bf16[128,128]{1,0:T(8,128)(2,1)S(1)}, u32[]{:S(2)}, u32[]{:S(2)}) collective-permute-start(bf16[128,128]{1,0:T(8,128)(2,1)S(1)} %get-tuple-element.78), channel_id=1, source_target_pairs={{0,5},{1,2},{2,1},{3,4},{4,3},{5,0},{6,15},{7,23},{8,24},{9,25},{1... | collective-permute-start | bytes 98312 | tf_op jit(solution)/shard_map/ppermute | solution.py:372
  4.4 1.5 %collective-permute-start.1 = (bf16[128,128]{1,0:T(8,128)(2,1)S(1)}, bf16[128,128]{1,0:T(8,128)(2,1)S(1)}, u32[]{:S(2)}, u32[]{:S(2)}) collective-permute-start(bf16[128,128]{1,0:T(8,128)(2,1)S(1)} %get-tuple-element.79), channel_id=1, source_target_pairs={{0,16},{1,17},{2,18},{3,19},{4,20},{5,21},{6,22},{7,8},{8,7},{9,10... | collective-permute-start | bytes 98312 | tf_op jit(solution)/shard_map/ppermute | solution.py:372
  6.0 0.4 collective-permute-start.3
  7.1 2.1 %shard_map.74 = (bf16[384,1024]{1,0:T(8,128)(2,1)S(1)}, bf16[384,1024]{1,0:T(8,128)(2,1)S(1)}, bf16[384,384]{1,0:T(8,128)(2,1)S(1)}, bf16[384,384]{1,0:T(8,128)(...) custom-call(bf16[1024,384]{1,0:T(8,128)(2,1)S(1)} %get-tuple-element, ...), custom_call_target="tpu_custom_call" | custom-call | flops 1207959552 | bytes 10317828 | tf_op jit(solution)/shard_map/pallas_call | solution.py:337
  9.6 0.4 shard_map.75
  10.0 0.4 collective-permute-start.4
  10.4 1.5 %collective-permute-start.5 = (bf16[128,128]{1,0:T(8,128)(2,1)S(1)}, bf16[128,128]{1,0:T(8,128)(2,1)S(1)}, u32[]{:S(2)}, u32[]{:S(2)}) collective-permute-start(bf16[128,128]{1,0:T(8,128)(2,1)S(1)} %get-tuple-element.93), channel_id=1, source_target_pairs={{0,16},{1,17},{2,18},{3,4},{4,3},{5,21},{6,22},{7,8},{8,7},{9,10},... | collective-permute-start | bytes 98312 | tf_op jit(solution)/shard_map/ppermute | solution.py:372
  11.9 0.4 collective-permute-start.6
  12.4 2.7 %shard_map.76 = (f32[128,1024]{1,0:T(8,128)S(1)}, f32[128,384]{1,0:T(8,128)S(1)}, bf16[1024,384]{1,0:T(8,128)(2,1)S(1)}, bf16[384,384]{1,0:T(8,128)(2,1)S(1)}) custom-call(bf16[128,128]{1,0:T(8,128)(2,1)S(1)} %collective-permute-done.refs_0_, bf16[128,128]{1,0:T(8,128)(2,1)S(1)} %collective-permute-done.1.refs_1_, ...), custom_call_target="tpu_custom_call" | custom-call | flops 1577058304 | bytes 8392704 | tf_op jit(solution)/shard_map/pallas_call | solution.py:337
  15.1 0.4 collective-permute-done.5.refs_1_
  15.9 2.0 %collective-permute-start.8 = (bf16[128,128]{1,0:T(8,128)(2,1)S(1)}, bf16[128,128]{1,0:T(8,128)(2,1)S(1)}, u32[]{:S(2)}, u32[]{:S(2)}) collective-permute-start(bf16[128,128]{1,0:T(8,128)(2,1)S(1)} %get-tuple-element.104), channel_id=1, source_target_pairs={{0,16},{1,17},{2,18},{3,19},{4,20},{5,6},{6,5},{7,8},{8,7},{9,25},... | collective-permute-start | bytes 98312 | tf_op jit(solution)/shard_map/ppermute | solution.py:372
  17.9 2.0 %collective-permute-start.9 = (bf16[128,128]{1,0:T(8,128)(2,1)S(1)}, bf16[128,128]{1,0:T(8,128)(2,1)S(1)}, u32[]{:S(2)}, u32[]{:S(2)}) collective-permute-start(bf16[128,128]{1,0:T(8,128)(2,1)S(1)} %get-tuple-element.105), channel_id=1, source_target_pairs={{0,5},{1,2},{2,1},{3,4},{4,3},{5,0},{6,22},{7,23},{8,24},{9,10},{1... | collective-permute-start | bytes 98312 | tf_op jit(solution)/shard_map/ppermute | solution.py:372
  19.9 0.5 collective-permute-start.11
  20.4 1.0 %shard_map.78 = (f32[128,1024]{1,0:T(8,128)S(1)}, f32[128,1024]{1,0:T(8,128)S(1)}, f32[128,384]{1,0:T(8,128)S(1)}) custom-call(bf16[128,128]{1,0:T(8,128)(2,1)S(1)} %collective-permute-done.4.refs_0_, bf16[128,128]{1,0:T(8,128)(2,1)S(1)} %collective-permute-done.5.refs_1_, bf16[128,128]{1,0:T(8,128)(2,1)S(1)} %collective-permute-done.6.refs_2_, ...), custom_call_target="tpu_custom_call" | custom-call | flops 469762048 | bytes 5902336 | tf_op jit(solution)/shard_map/pallas_call | solution.py:337
  21.4 1.3 %collective-permute-done.9.refs_1_ = bf16[128,128]{1,0:T(8,128)(2,1)S(1)} collective-permute-done((bf16[128,128]{1,0:T(8,128)(2,1)S(1)}, bf16[128,128]{1,0:T(8,128)(2,1)S(1)}, u32[]{:S(2)}, u32[]{:S(2)}) %collective-permute-start.9) | collective-permute-done | bytes 32800 | tf_op jit(solution)/shard_map/ppermute | solution.py:372
  22.8 0.4 shard_map.79
  23.2 1.3 %collective-permute-start.12 = (bf16[128,128]{1,0:T(8,128)(2,1)S(1)}, bf16[128,128]{1,0:T(8,128)(2,1)S(1)}, u32[]{:S(2)}, u32[]{:S(2)}) collective-permute-start(bf16[128,128]{1,0:T(8,128)(2,1)S(1)} %get-tuple-element.113), channel_id=1, source_target_pairs={{0,16},{1,17},{2,18},{3,19},{4,20},{5,6},{6,5},{7,8},{8,7},{9,25},... | collective-permute-start | bytes 98312 | tf_op jit(solution)/shard_map/ppermute | solution.py:372
  24.4 1.9 %collective-permute-start.13 = (bf16[128,128]{1,0:T(8,128)(2,1)S(1)}, bf16[128,128]{1,0:T(8,128)(2,1)S(1)}, u32[]{:S(2)}, u32[]{:S(2)}) collective-permute-start(bf16[128,128]{1,0:T(8,128)(2,1)S(1)} %get-tuple-element.114), channel_id=1, source_target_pairs={{0,5},{1,2},{2,1},{3,4},{4,3},{5,0},{6,22},{7,23},{8,24},{9,10},{1... | collective-permute-start | bytes 98312 | tf_op jit(solution)/shard_map/ppermute | solution.py:372
  26.4 0.5 collective-permute-start.15
  26.9 1.2 %shard_map.80 = (f32[128,1024]{1,0:T(8,128)S(1)}, f32[128,384]{1,0:T(8,128)S(1)}) custom-call(bf16[128,128]{1,0:T(8,128)(2,1)S(1)} %collective-permute-done.8.refs_0_, bf16[128,128]{1,0:T(8,128)(2,1)S(1)} %collective-permute-done.9.refs_1_, bf16[128,128]{1,0:T(8,128)(2,1)S(1)} %collective-permute-done.10.refs_2_, ...), custom_call_target="tpu_custom_call" | custom-call | flops 469762048 | bytes 5738496 | tf_op jit(solution)/shard_map/pallas_call | solution.py:337
  28.5 0.8 %collective-permute-done.13.refs_1_ = bf16[128,128]{1,0:T(8,128)(2,1)S(1)} collective-permute-done((bf16[128,128]{1,0:T(8,128)(2,1)S(1)}, bf16[128,128]{1,0:T(8,128)(2,1)S(1)}, u32[]{:S(2)}, u32[]{:S(2)}) %collective-permute-start.13) | collective-permute-done | bytes 32800 | tf_op jit(solution)/shard_map/ppermute | solution.py:372
  29.3 0.4 shard_map.81
  29.7 1.6 %collective-permute-start.16 = (bf16[128,128]{1,0:T(8,128)(2,1)S(1)}, bf16[128,128]{1,0:T(8,128)(2,1)S(1)}, u32[]{:S(2)}, u32[]{:S(2)}) collective-permute-start(bf16[128,128]{1,0:T(8,128)(2,1)S(1)} %get-tuple-element.122), channel_id=1, source_target_pairs={{0,16},{1,17},{2,18},{3,19},{4,20},{5,6},{6,5},{7,8},{8,7},{9,25},... | collective-permute-start | bytes 98312 | tf_op jit(solution)/shard_map/ppermute | solution.py:372
  31.3 1.7 %collective-permute-start.17 = (bf16[128,128]{1,0:T(8,128)(2,1)S(1)}, bf16[128,128]{1,0:T(8,128)(2,1)S(1)}, u32[]{:S(2)}, u32[]{:S(2)}) collective-permute-start(bf16[128,128]{1,0:T(8,128)(2,1)S(1)} %get-tuple-element.123), channel_id=1, source_target_pairs={{0,5},{1,2},{2,1},{3,4},{4,3},{5,0},{6,22},{7,23},{8,24},{9,10},{1... | collective-permute-start | bytes 98312 | tf_op jit(solution)/shard_map/ppermute | solution.py:372
  33.0 0.5 collective-permute-start.19
  33.5 1.0 %shard_map.82 = (f32[128,1024]{1,0:T(8,128)S(1)}, f32[128,1024]{1,0:T(8,128)S(1)}, f32[128,384]{1,0:T(8,128)S(1)}) custom-call(bf16[128,128]{1,0:T(8,128)(2,1)S(1)} %collective-permute-done.12.refs_0_, bf16[128,128]{1,0:T(8,128)(2,1)S(1)} %collective-permute-done.13.refs_1_, bf16[128,128]{1,0:T(8,128)(2,1)S(1)} %collective-permute-done.14.refs_2_, ...), custom_call_target="tpu_custom_call" | custom-call | flops 469762048 | bytes 5902336 | tf_op jit(solution)/shard_map/pallas_call | solution.py:337
  34.5 0.4 collective-permute-done.16.refs_0_
  34.9 1.2 %collective-permute-done.17.refs_1_ = bf16[128,128]{1,0:T(8,128)(2,1)S(1)} collective-permute-done((bf16[128,128]{1,0:T(8,128)(2,1)S(1)}, bf16[128,128]{1,0:T(8,128)(2,1)S(1)}, u32[]{:S(2)}, u32[]{:S(2)}) %collective-permute-start.17) | collective-permute-done | bytes 32800 | tf_op jit(solution)/shard_map/ppermute | solution.py:372
  36.1 0.4 shard_map.83
  36.5 1.6 %collective-permute-start.20 = (bf16[128,128]{1,0:T(8,128)(2,1)S(1)}, bf16[128,128]{1,0:T(8,128)(2,1)S(1)}, u32[]{:S(2)}, u32[]{:S(2)}) collective-permute-start(bf16[128,128]{1,0:T(8,128)(2,1)S(1)} %get-tuple-element.130), channel_id=1, source_target_pairs={{0,16},{1,17},{2,18},{3,19},{4,20},{5,6},{6,5},{7,8},{8,7},{9,25},... | collective-permute-start | bytes 98312 | tf_op jit(solution)/shard_map/ppermute | solution.py:372
  38.1 1.7 %collective-permute-start.21 = (bf16[128,128]{1,0:T(8,128)(2,1)S(1)}, bf16[128,128]{1,0:T(8,128)(2,1)S(1)}, u32[]{:S(2)}, u32[]{:S(2)}) collective-permute-start(bf16[128,128]{1,0:T(8,128)(2,1)S(1)} %get-tuple-element.131), channel_id=1, source_target_pairs={{0,5},{1,2},{2,1},{3,4},{4,3},{5,0},{6,22},{7,23},{8,24},{9,10},{1... | collective-permute-start | bytes 98312 | tf_op jit(solution)/shard_map/ppermute | solution.py:372
  39.8 0.5 collective-permute-start.23
  40.3 1.3 %shard_map.84 = (f32[128,1024]{1,0:T(8,128)S(1)}, f32[128,384]{1,0:T(8,128)S(1)}) custom-call(bf16[128,128]{1,0:T(8,128)(2,1)S(1)} %collective-permute-done.16.refs_0_, bf16[128,128]{1,0:T(8,128)(2,1)S(1)} %collective-permute-done.17.refs_1_, bf16[128,128]{1,0:T(8,128)(2,1)S(1)} %collective-permute-done.18.refs_2_, ...), custom_call_target="tpu_custom_call" | custom-call | flops 469762048 | bytes 5738496 | tf_op jit(solution)/shard_map/pallas_call | solution.py:337
  41.7 1.2 %collective-permute-done.21.refs_1_ = bf16[128,128]{1,0:T(8,128)(2,1)S(1)} collective-permute-done((bf16[128,128]{1,0:T(8,128)(2,1)S(1)}, bf16[128,128]{1,0:T(8,128)(2,1)S(1)}, u32[]{:S(2)}, u32[]{:S(2)}) %collective-permute-start.21) | collective-permute-done | bytes 32800 | tf_op jit(solution)/shard_map/ppermute | solution.py:372
  43.4 1.5 %collective-permute-start.24 = (bf16[128,128]{1,0:T(8,128)(2,1)S(1)}, bf16[128,128]{1,0:T(8,128)(2,1)S(1)}, u32[]{:S(2)}, u32[]{:S(2)}) collective-permute-start(bf16[128,128]{1,0:T(8,128)(2,1)S(1)} %get-tuple-element.138), channel_id=1, source_target_pairs={{0,16},{1,17},{2,18},{3,19},{4,20},{5,6},{6,5},{7,8},{8,7},{9,25},... | collective-permute-start | bytes 98312 | tf_op jit(solution)/shard_map/ppermute | solution.py:372
  44.9 1.1 %collective-permute-start.25 = (bf16[128,128]{1,0:T(8,128)(2,1)S(1)}, bf16[128,128]{1,0:T(8,128)(2,1)S(1)}, u32[]{:S(2)}, u32[]{:S(2)}) collective-permute-start(bf16[128,128]{1,0:T(8,128)(2,1)S(1)} %get-tuple-element.139), channel_id=1, source_target_pairs={{0,5},{1,2},{2,1},{3,4},{4,3},{5,0},{6,22},{7,23},{8,24},{9,10},{1... | collective-permute-start | bytes 98312 | tf_op jit(solution)/shard_map/ppermute | solution.py:372
  46.0 0.5 collective-permute-start.27
  46.5 1.0 %shard_map.86 = (f32[128,1024]{1,0:T(8,128)S(1)}, f32[128,1024]{1,0:T(8,128)S(1)}, f32[128,384]{1,0:T(8,128)S(1)}) custom-call(bf16[128,128]{1,0:T(8,128)(2,1)S(1)} %collective-permute-done.20.refs_0_, bf16[128,128]{1,0:T(8,128)(2,1)S(1)} %collective-permute-done.21.refs_1_, bf16[128,128]{1,0:T(8,128)(2,1)S(1)} %collective-permute-done.22.refs_2_, ...), custom_call_target="tpu_custom_call" | custom-call | flops 469762048 | bytes 5902336 | tf_op jit(solution)/shard_map/pallas_call | solution.py:337
  47.5 1.3 %collective-permute-done.24.refs_0_ = bf16[128,128]{1,0:T(8,128)(2,1)S(1)} collective-permute-done((bf16[128,128]{1,0:T(8,128)(2,1)S(1)}, bf16[128,128]{1,0:T(8,128)(2,1)S(1)}, u32[]{:S(2)}, u32[]{:S(2)}) %collective-permute-start.24) | collective-permute-done | bytes 32800 | tf_op jit(solution)/shard_map/ppermute | solution.py:372
  48.8 1.0 %collective-permute-done.25.refs_1_ = bf16[128,128]{1,0:T(8,128)(2,1)S(1)} collective-permute-done((bf16[128,128]{1,0:T(8,128)(2,1)S(1)}, bf16[128,128]{1,0:T(8,128)(2,1)S(1)}, u32[]{:S(2)}, u32[]{:S(2)}) %collective-permute-start.25) | collective-permute-done | bytes 32800 | tf_op jit(solution)/shard_map/ppermute | solution.py:372
  49.7 0.4 shard_map.87
  50.1 1.0 %collective-permute-start.28 = (bf16[128,128]{1,0:T(8,128)(2,1)S(1)}, bf16[128,128]{1,0:T(8,128)(2,1)S(1)}, u32[]{:S(2)}, u32[]{:S(2)}) collective-permute-start(bf16[128,128]{1,0:T(8,128)(2,1)S(1)} %get-tuple-element.145), channel_id=1, source_target_pairs={{0,16},{1,17},{2,18},{3,19},{4,20},{5,6},{6,5},{7,8},{8,7},{9,25},... | collective-permute-start | bytes 98312 | tf_op jit(solution)/shard_map/ppermute | solution.py:372
  51.1 1.7 %collective-permute-start.29 = (bf16[128,128]{1,0:T(8,128)(2,1)S(1)}, bf16[128,128]{1,0:T(8,128)(2,1)S(1)}, u32[]{:S(2)}, u32[]{:S(2)}) collective-permute-start(bf16[128,128]{1,0:T(8,128)(2,1)S(1)} %get-tuple-element.146), channel_id=1, source_target_pairs={{0,5},{1,2},{2,1},{3,4},{4,3},{5,0},{6,22},{7,23},{8,24},{9,10},{1... | collective-permute-start | bytes 98312 | tf_op jit(solution)/shard_map/ppermute | solution.py:372
  52.8 0.5 collective-permute-start.31
  53.3 1.2 %shard_map.88.refs_5_ = f32[1024,128]{1,0:T(8,128)S(1)} custom-call(bf16[128,128]{1,0:T(8,128)(2,1)S(1)} %collective-permute-done.24.refs_0_, bf16[128,128]{1,0:T(8,128)(2,1)S(1)} %collective-permute-done.25.refs_1_, bf16[128,128]{1,0:T(8,128)(2,1)S(1)} %collective-permute-done.26.refs_2_, bf16[128,128]{1,0:T(8,128)(2,1)S(1)} %collective-permute-done.27.refs_3_, ...), custom_call_target="tpu_custom_call" | custom-call | flops 369098752 | bytes 4624384 | tf_op jit(solution)/shard_map/pallas_call | solution.py:337
  54.5 1.2 %collective-permute-done.28.refs_0_ = bf16[128,128]{1,0:T(8,128)(2,1)S(1)} collective-permute-done((bf16[128,128]{1,0:T(8,128)(2,1)S(1)}, bf16[128,128]{1,0:T(8,128)(2,1)S(1)}, u32[]{:S(2)}, u32[]{:S(2)}) %collective-permute-start.28) | collective-permute-done | bytes 32800 | tf_op jit(solution)/shard_map/ppermute | solution.py:372
  55.9 1.1 %shard_map.89 = f32[1,1024,128]{2,1,0:T(8,128)} custom-call(bf16[128,128]{1,0:T(8,128)(2,1)S(1)} %collective-permute-done.28.refs_0_, bf16[128,128]{1,0:T(8,128)(2,1)S(1)} %collective-permute-done.29.refs_1_, bf16[128,128]{1,0:T(8,128)(2,1)S(1)} %collective-permute-done.30.refs_2_, bf16[128,128]{1,0:T(8,128)(2,1)S(1)} %collective-permute-done.31.refs_3_, ...), custom_call_target="tpu_custom_call" | custom-call | flops 100663296 | bytes 1966080 | tf_op jit(solution)/shard_map/pallas_call | solution.py:337
  (33 shorter events, 2.1 us)
Async XLA Ops:
  1.8 7.5 %collective-permute-start = (bf16[128,128]{1,0:T(8,128)(2,1)S(1)}, bf16[128,128]{1,0:T(8,128)(2,1)S(1)}, u32[]{:S(2)}, u32[]{:S(2)}) collective-permute-start(bf16[128,128]{1,0:T(8,128)(2,1)S(1)} %get-tuple-element.78), channel_id=1, source_target_pairs={{0,5},{1,2},{2,1},{3,4},{4,3},{5,0},{6,15},{7,23},{8,24},{9,25},{1... | collective-permute-start | bytes 98312 | tf_op jit(solution)/shard_map/ppermute | solution.py:372
  4.4 5.1 %collective-permute-start.1 = (bf16[128,128]{1,0:T(8,128)(2,1)S(1)}, bf16[128,128]{1,0:T(8,128)(2,1)S(1)}, u32[]{:S(2)}, u32[]{:S(2)}) collective-permute-start(bf16[128,128]{1,0:T(8,128)(2,1)S(1)} %get-tuple-element.79), channel_id=1, source_target_pairs={{0,16},{1,17},{2,18},{3,19},{4,20},{5,21},{6,22},{7,8},{8,7},{9,10... | collective-permute-start | bytes 98312 | tf_op jit(solution)/shard_map/ppermute | solution.py:372
  5.9 3.6 %collective-permute-start.2 = (bf16[128,128]{1,0:T(8,128)(2,1)S(1)}, bf16[128,128]{1,0:T(8,128)(2,1)S(1)}, u32[]{:S(2)}, u32[]{:S(2)}) collective-permute-start(bf16[128,128]{1,0:T(8,128)(2,1)S(1)} %get-tuple-element.80), channel_id=1, source_target_pairs={{0,1},{1,0},{2,18},{3,7},{4,13},{5,6},{6,5},{7,3},{8,9},{9,8},{10,... | collective-permute-start | bytes 98312 | tf_op jit(solution)/shard_map/ppermute | solution.py:372
  6.0 3.5 %collective-permute-start.3 = (bf16[128,128]{1,0:T(8,128)(2,1)S(1)}, bf16[128,128]{1,0:T(8,128)(2,1)S(1)}, u32[]{:S(2)}, u32[]{:S(2)}) collective-permute-start(bf16[128,128]{1,0:T(8,128)(2,1)S(1)} %get-tuple-element.81), channel_id=1, source_target_pairs={{0,1},{1,0},{2,3},{3,2},{4,5},{5,4},{6,7},{7,6},{8,9},{9,8},{10,11... | collective-permute-start | bytes 98312 | tf_op jit(solution)/shard_map/ppermute | solution.py:372
  10.0 5.1 %collective-permute-start.4 = (bf16[128,128]{1,0:T(8,128)(2,1)S(1)}, bf16[128,128]{1,0:T(8,128)(2,1)S(1)}, u32[]{:S(2)}, u32[]{:S(2)}) collective-permute-start(bf16[128,128]{1,0:T(8,128)(2,1)S(1)} %get-tuple-element.92), channel_id=1, source_target_pairs={{0,4},{1,2},{2,1},{3,10},{4,0},{5,6},{6,5},{7,23},{8,24},{9,25},{1... | collective-permute-start | bytes 98312 | tf_op jit(solution)/shard_map/ppermute | solution.py:372
  10.4 5.1 %collective-permute-start.5 = (bf16[128,128]{1,0:T(8,128)(2,1)S(1)}, bf16[128,128]{1,0:T(8,128)(2,1)S(1)}, u32[]{:S(2)}, u32[]{:S(2)}) collective-permute-start(bf16[128,128]{1,0:T(8,128)(2,1)S(1)} %get-tuple-element.93), channel_id=1, source_target_pairs={{0,16},{1,17},{2,18},{3,4},{4,3},{5,21},{6,22},{7,8},{8,7},{9,10},... | collective-permute-start | bytes 98312 | tf_op jit(solution)/shard_map/ppermute | solution.py:372
  11.9 3.7 %collective-permute-start.6 = (bf16[128,128]{1,0:T(8,128)(2,1)S(1)}, bf16[128,128]{1,0:T(8,128)(2,1)S(1)}, u32[]{:S(2)}, u32[]{:S(2)}) collective-permute-start(bf16[128,128]{1,0:T(8,128)(2,1)S(1)} %get-tuple-element.94), channel_id=1, source_target_pairs={{0,1},{1,0},{2,5},{3,19},{4,20},{5,2},{6,7},{7,6},{8,9},{9,8},{10,... | collective-permute-start | bytes 98312 | tf_op jit(solution)/shard_map/ppermute | solution.py:372
  12.3 3.3 %collective-permute-start.7 = (bf16[128,128]{1,0:T(8,128)(2,1)S(1)}, bf16[128,128]{1,0:T(8,128)(2,1)S(1)}, u32[]{:S(2)}, u32[]{:S(2)}) collective-permute-start(bf16[128,128]{1,0:T(8,128)(2,1)S(1)} %get-tuple-element.95), channel_id=1, source_target_pairs={{0,1},{1,0},{2,3},{3,2},{4,5},{5,4},{6,7},{7,6},{8,9},{9,8},{10,11... | collective-permute-start | bytes 98312 | tf_op jit(solution)/shard_map/ppermute | solution.py:372
  15.9 5.5 %collective-permute-start.8 = (bf16[128,128]{1,0:T(8,128)(2,1)S(1)}, bf16[128,128]{1,0:T(8,128)(2,1)S(1)}, u32[]{:S(2)}, u32[]{:S(2)}) collective-permute-start(bf16[128,128]{1,0:T(8,128)(2,1)S(1)} %get-tuple-element.104), channel_id=1, source_target_pairs={{0,16},{1,17},{2,18},{3,19},{4,20},{5,6},{6,5},{7,8},{8,7},{9,25},... | collective-permute-start | bytes 98312 | tf_op jit(solution)/shard_map/ppermute | solution.py:372
  17.9 4.8 %collective-permute-start.9 = (bf16[128,128]{1,0:T(8,128)(2,1)S(1)}, bf16[128,128]{1,0:T(8,128)(2,1)S(1)}, u32[]{:S(2)}, u32[]{:S(2)}) collective-permute-start(bf16[128,128]{1,0:T(8,128)(2,1)S(1)} %get-tuple-element.105), channel_id=1, source_target_pairs={{0,5},{1,2},{2,1},{3,4},{4,3},{5,0},{6,22},{7,23},{8,24},{9,10},{1... | collective-permute-start | bytes 98312 | tf_op jit(solution)/shard_map/ppermute | solution.py:372
  19.9 2.8 %collective-permute-start.10 = (bf16[128,128]{1,0:T(8,128)(2,1)S(1)}, bf16[128,128]{1,0:T(8,128)(2,1)S(1)}, u32[]{:S(2)}, u32[]{:S(2)}) collective-permute-start(bf16[128,128]{1,0:T(8,128)(2,1)S(1)} %get-tuple-element.106), channel_id=1, source_target_pairs={{0,1},{1,0},{2,3},{3,2},{4,12},{5,21},{6,7},{7,6},{8,9},{9,8},{10,... | collective-permute-start | bytes 98312 | tf_op jit(solution)/shard_map/ppermute | solution.py:372
  19.9 2.8 %collective-permute-start.11 = (bf16[128,128]{1,0:T(8,128)(2,1)S(1)}, bf16[128,128]{1,0:T(8,128)(2,1)S(1)}, u32[]{:S(2)}, u32[]{:S(2)}) collective-permute-start(bf16[128,128]{1,0:T(8,128)(2,1)S(1)} %get-tuple-element.107), channel_id=1, source_target_pairs={{0,1},{1,0},{2,3},{3,2},{4,5},{5,4},{6,7},{7,6},{8,9},{9,8},{10,11... | collective-permute-start | bytes 98312 | tf_op jit(solution)/shard_map/ppermute | solution.py:372
  23.2 5.3 %collective-permute-start.12 = (bf16[128,128]{1,0:T(8,128)(2,1)S(1)}, bf16[128,128]{1,0:T(8,128)(2,1)S(1)}, u32[]{:S(2)}, u32[]{:S(2)}) collective-permute-start(bf16[128,128]{1,0:T(8,128)(2,1)S(1)} %get-tuple-element.113), channel_id=1, source_target_pairs={{0,16},{1,17},{2,18},{3,19},{4,20},{5,6},{6,5},{7,8},{8,7},{9,25},... | collective-permute-start | bytes 98312 | tf_op jit(solution)/shard_map/ppermute | solution.py:372
  24.4 4.8 %collective-permute-start.13 = (bf16[128,128]{1,0:T(8,128)(2,1)S(1)}, bf16[128,128]{1,0:T(8,128)(2,1)S(1)}, u32[]{:S(2)}, u32[]{:S(2)}) collective-permute-start(bf16[128,128]{1,0:T(8,128)(2,1)S(1)} %get-tuple-element.114), channel_id=1, source_target_pairs={{0,5},{1,2},{2,1},{3,4},{4,3},{5,0},{6,22},{7,23},{8,24},{9,10},{1... | collective-permute-start | bytes 98312 | tf_op jit(solution)/shard_map/ppermute | solution.py:372
  26.4 2.9 %collective-permute-start.14 = (bf16[128,128]{1,0:T(8,128)(2,1)S(1)}, bf16[128,128]{1,0:T(8,128)(2,1)S(1)}, u32[]{:S(2)}, u32[]{:S(2)}) collective-permute-start(bf16[128,128]{1,0:T(8,128)(2,1)S(1)} %get-tuple-element.115), channel_id=1, source_target_pairs={{0,1},{1,0},{2,3},{3,2},{4,12},{5,21},{6,7},{7,6},{8,9},{9,8},{10,... | collective-permute-start | bytes 98312 | tf_op jit(solution)/shard_map/ppermute | solution.py:372
  26.4 2.9 %collective-permute-start.15 = (bf16[128,128]{1,0:T(8,128)(2,1)S(1)}, bf16[128,128]{1,0:T(8,128)(2,1)S(1)}, u32[]{:S(2)}, u32[]{:S(2)}) collective-permute-start(bf16[128,128]{1,0:T(8,128)(2,1)S(1)} %get-tuple-element.116), channel_id=1, source_target_pairs={{0,1},{1,0},{2,3},{3,2},{4,5},{5,4},{6,7},{7,6},{8,9},{9,8},{10,11... | collective-permute-start | bytes 98312 | tf_op jit(solution)/shard_map/ppermute | solution.py:372
  29.7 5.2 %collective-permute-start.16 = (bf16[128,128]{1,0:T(8,128)(2,1)S(1)}, bf16[128,128]{1,0:T(8,128)(2,1)S(1)}, u32[]{:S(2)}, u32[]{:S(2)}) collective-permute-start(bf16[128,128]{1,0:T(8,128)(2,1)S(1)} %get-tuple-element.122), channel_id=1, source_target_pairs={{0,16},{1,17},{2,18},{3,19},{4,20},{5,6},{6,5},{7,8},{8,7},{9,25},... | collective-permute-start | bytes 98312 | tf_op jit(solution)/shard_map/ppermute | solution.py:372
  31.3 4.8 %collective-permute-start.17 = (bf16[128,128]{1,0:T(8,128)(2,1)S(1)}, bf16[128,128]{1,0:T(8,128)(2,1)S(1)}, u32[]{:S(2)}, u32[]{:S(2)}) collective-permute-start(bf16[128,128]{1,0:T(8,128)(2,1)S(1)} %get-tuple-element.123), channel_id=1, source_target_pairs={{0,5},{1,2},{2,1},{3,4},{4,3},{5,0},{6,22},{7,23},{8,24},{9,10},{1... | collective-permute-start | bytes 98312 | tf_op jit(solution)/shard_map/ppermute | solution.py:372
  33.0 3.1 %collective-permute-start.18 = (bf16[128,128]{1,0:T(8,128)(2,1)S(1)}, bf16[128,128]{1,0:T(8,128)(2,1)S(1)}, u32[]{:S(2)}, u32[]{:S(2)}) collective-permute-start(bf16[128,128]{1,0:T(8,128)(2,1)S(1)} %get-tuple-element.124), channel_id=1, source_target_pairs={{0,1},{1,0},{2,3},{3,2},{4,12},{5,21},{6,7},{7,6},{8,9},{9,8},{10,... | collective-permute-start | bytes 98312 | tf_op jit(solution)/shard_map/ppermute | solution.py:372
  33.0 3.1 %collective-permute-start.19 = (bf16[128,128]{1,0:T(8,128)(2,1)S(1)}, bf16[128,128]{1,0:T(8,128)(2,1)S(1)}, u32[]{:S(2)}, u32[]{:S(2)}) collective-permute-start(bf16[128,128]{1,0:T(8,128)(2,1)S(1)} %get-tuple-element.125), channel_id=1, source_target_pairs={{0,1},{1,0},{2,3},{3,2},{4,5},{5,4},{6,7},{7,6},{8,9},{9,8},{10,11... | collective-permute-start | bytes 98312 | tf_op jit(solution)/shard_map/ppermute | solution.py:372
  36.5 5.2 %collective-permute-start.20 = (bf16[128,128]{1,0:T(8,128)(2,1)S(1)}, bf16[128,128]{1,0:T(8,128)(2,1)S(1)}, u32[]{:S(2)}, u32[]{:S(2)}) collective-permute-start(bf16[128,128]{1,0:T(8,128)(2,1)S(1)} %get-tuple-element.130), channel_id=1, source_target_pairs={{0,16},{1,17},{2,18},{3,19},{4,20},{5,6},{6,5},{7,8},{8,7},{9,25},... | collective-permute-start | bytes 98312 | tf_op jit(solution)/shard_map/ppermute | solution.py:372
  38.1 4.8 %collective-permute-start.21 = (bf16[128,128]{1,0:T(8,128)(2,1)S(1)}, bf16[128,128]{1,0:T(8,128)(2,1)S(1)}, u32[]{:S(2)}, u32[]{:S(2)}) collective-permute-start(bf16[128,128]{1,0:T(8,128)(2,1)S(1)} %get-tuple-element.131), channel_id=1, source_target_pairs={{0,5},{1,2},{2,1},{3,4},{4,3},{5,0},{6,22},{7,23},{8,24},{9,10},{1... | collective-permute-start | bytes 98312 | tf_op jit(solution)/shard_map/ppermute | solution.py:372
  39.8 3.1 %collective-permute-start.22 = (bf16[128,128]{1,0:T(8,128)(2,1)S(1)}, bf16[128,128]{1,0:T(8,128)(2,1)S(1)}, u32[]{:S(2)}, u32[]{:S(2)}) collective-permute-start(bf16[128,128]{1,0:T(8,128)(2,1)S(1)} %get-tuple-element.132), channel_id=1, source_target_pairs={{0,1},{1,0},{2,3},{3,2},{4,12},{5,21},{6,7},{7,6},{8,9},{9,8},{10,... | collective-permute-start | bytes 98312 | tf_op jit(solution)/shard_map/ppermute | solution.py:372
  39.8 3.1 %collective-permute-start.23 = (bf16[128,128]{1,0:T(8,128)(2,1)S(1)}, bf16[128,128]{1,0:T(8,128)(2,1)S(1)}, u32[]{:S(2)}, u32[]{:S(2)}) collective-permute-start(bf16[128,128]{1,0:T(8,128)(2,1)S(1)} %get-tuple-element.133), channel_id=1, source_target_pairs={{0,1},{1,0},{2,3},{3,2},{4,5},{5,4},{6,7},{7,6},{8,9},{9,8},{10,11... | collective-permute-start | bytes 98312 | tf_op jit(solution)/shard_map/ppermute | solution.py:372
  43.4 5.4 %collective-permute-start.24 = (bf16[128,128]{1,0:T(8,128)(2,1)S(1)}, bf16[128,128]{1,0:T(8,128)(2,1)S(1)}, u32[]{:S(2)}, u32[]{:S(2)}) collective-permute-start(bf16[128,128]{1,0:T(8,128)(2,1)S(1)} %get-tuple-element.138), channel_id=1, source_target_pairs={{0,16},{1,17},{2,18},{3,19},{4,20},{5,6},{6,5},{7,8},{8,7},{9,25},... | collective-permute-start | bytes 98312 | tf_op jit(solution)/shard_map/ppermute | solution.py:372
  44.9 4.8 %collective-permute-start.25 = (bf16[128,128]{1,0:T(8,128)(2,1)S(1)}, bf16[128,128]{1,0:T(8,128)(2,1)S(1)}, u32[]{:S(2)}, u32[]{:S(2)}) collective-permute-start(bf16[128,128]{1,0:T(8,128)(2,1)S(1)} %get-tuple-element.139), channel_id=1, source_target_pairs={{0,5},{1,2},{2,1},{3,4},{4,3},{5,0},{6,22},{7,23},{8,24},{9,10},{1... | collective-permute-start | bytes 98312 | tf_op jit(solution)/shard_map/ppermute | solution.py:372
  46.0 3.7 %collective-permute-start.26 = (bf16[128,128]{1,0:T(8,128)(2,1)S(1)}, bf16[128,128]{1,0:T(8,128)(2,1)S(1)}, u32[]{:S(2)}, u32[]{:S(2)}) collective-permute-start(bf16[128,128]{1,0:T(8,128)(2,1)S(1)} %get-tuple-element.140), channel_id=1, source_target_pairs={{0,1},{1,0},{2,3},{3,2},{4,12},{5,21},{6,7},{7,6},{8,9},{9,8},{10,... | collective-permute-start | bytes 98312 | tf_op jit(solution)/shard_map/ppermute | solution.py:372
  46.0 3.7 %collective-permute-start.27 = (bf16[128,128]{1,0:T(8,128)(2,1)S(1)}, bf16[128,128]{1,0:T(8,128)(2,1)S(1)}, u32[]{:S(2)}, u32[]{:S(2)}) collective-permute-start(bf16[128,128]{1,0:T(8,128)(2,1)S(1)} %get-tuple-element.141), channel_id=1, source_target_pairs={{0,1},{1,0},{2,3},{3,2},{4,5},{5,4},{6,7},{7,6},{8,9},{9,8},{10,11... | collective-permute-start | bytes 98312 | tf_op jit(solution)/shard_map/ppermute | solution.py:372
  50.1 5.5 %collective-permute-start.28 = (bf16[128,128]{1,0:T(8,128)(2,1)S(1)}, bf16[128,128]{1,0:T(8,128)(2,1)S(1)}, u32[]{:S(2)}, u32[]{:S(2)}) collective-permute-start(bf16[128,128]{1,0:T(8,128)(2,1)S(1)} %get-tuple-element.145), channel_id=1, source_target_pairs={{0,16},{1,17},{2,18},{3,19},{4,20},{5,6},{6,5},{7,8},{8,7},{9,25},... | collective-permute-start | bytes 98312 | tf_op jit(solution)/shard_map/ppermute | solution.py:372
  51.1 4.8 %collective-permute-start.29 = (bf16[128,128]{1,0:T(8,128)(2,1)S(1)}, bf16[128,128]{1,0:T(8,128)(2,1)S(1)}, u32[]{:S(2)}, u32[]{:S(2)}) collective-permute-start(bf16[128,128]{1,0:T(8,128)(2,1)S(1)} %get-tuple-element.146), channel_id=1, source_target_pairs={{0,5},{1,2},{2,1},{3,4},{4,3},{5,0},{6,22},{7,23},{8,24},{9,10},{1... | collective-permute-start | bytes 98312 | tf_op jit(solution)/shard_map/ppermute | solution.py:372
  52.8 3.1 %collective-permute-start.30 = (bf16[128,128]{1,0:T(8,128)(2,1)S(1)}, bf16[128,128]{1,0:T(8,128)(2,1)S(1)}, u32[]{:S(2)}, u32[]{:S(2)}) collective-permute-start(bf16[128,128]{1,0:T(8,128)(2,1)S(1)} %get-tuple-element.147), channel_id=1, source_target_pairs={{0,1},{1,0},{2,3},{3,2},{4,12},{5,21},{6,7},{7,6},{8,9},{9,8},{10,... | collective-permute-start | bytes 98312 | tf_op jit(solution)/shard_map/ppermute | solution.py:372
  52.8 3.1 %collective-permute-start.31 = (bf16[128,128]{1,0:T(8,128)(2,1)S(1)}, bf16[128,128]{1,0:T(8,128)(2,1)S(1)}, u32[]{:S(2)}, u32[]{:S(2)}) collective-permute-start(bf16[128,128]{1,0:T(8,128)(2,1)S(1)} %get-tuple-element.148), channel_id=1, source_target_pairs={{0,1},{1,0},{2,3},{3,2},{4,5},{5,4},{6,7},{7,6},{8,9},{9,8},{10,11... | collective-permute-start | bytes 98312 | tf_op jit(solution)/shard_map/ppermute | solution.py:372

commit v15 on v14

--- a/solution.py
+++ b/solution.py
@@ -18,19 +18,14 @@
 
 PLANS = (
     (
-        (1, 1, 2, 1, 1, 1, 1, 0, 0, 0, 0, 0, 2, 1, 1, 1),
-        (0, 0, 2, 1, 1, 1, 0, 2, 0, 0, 0, 1, 1, 1, 2),
-        (((0, 5), (6, 15), (12, 16)), ((2, 18),), ((3, 7), (4, 13), (14, 31), (17, 19))),
+        (0, 1, 2, 0, 2, 2, 2, 0, 0, 0, 0, 1, 2, 2, 2, 2),
+        (0, 1, 1, 1, 1, 0, 0, 1, 0, 1, 1, 1, 2, 0, 1),
+        (((6, 15), (22, 29)), ((0, 2), (14, 18), (25, 26), (28, 31)), ((3, 7), (19, 23), (24, 27))),
     ),
     (
-        (1, 1, 1, 2, 2, 1, 1, 0, 0, 0, 2, 0, 1, 1, 1, 1),
-        (0, 1, 0, 1, 1, 2, 2, 2, 2, 1, 2, 1, 1, 2, 2),
-        (((0, 4), (3, 10), (22, 26)), ((11, 27),), ((2, 5), (23, 31))),
-    ),
-    (
-        (0, 0, 0, 0, 0, 2, 1, 1, 1, 0, 0, 1, 1, 0, 0, 0),
-        (1, 1, 0, 0, 1, 0, 2, 1, 1, 1, 0, 0, 1, 0, 2),
-        ((), ((0, 5), (13, 14), (21, 29)), ((4, 12), (15, 20), (28, 31))),
+        (0, 1, 1, 0, 0, 0, 0, 1, 1, 1, 1, 0, 0, 0, 0, 0),
+        (0, 2, 1, 0, 0, 1, 2, 1, 0, 1, 1, 0, 0, 1, 1),
+        ((), ((0, 3), (4, 13), (14, 31)), ((2, 5), (12, 15))),
     ),
 )
 
@@ -349,7 +344,7 @@
     width, leads = right_side.shape[1:]
     share = shared_rows.shape[2]
     subs = lax.axis_size("sub")
-    plans = [min(k, len(PLANS) - 1) for k in range(2 * ITERS)]
+    plans = [min(k // 2, len(PLANS) - 1) for k in range(2 * ITERS)]
     trips = len(swaps(subs, plans[0]))
     links = len(slots_of(0, subs))
     total = links * share

time: 57.2 us -> 56.8 us (level)
  no operation moved by 1% of the time
where the time goes in v15:
time: 56.8 us; the launch traced here: 56.6 us
  starting transfers between devices  29.3 us (52%)
  Pallas kernels  17.1 us (30%)
  waiting for transfers between devices  9.35 us (16%)
  between operations  0.81 us (1%)
    ppermute x32, starting transfers between devices, exchange(): lax.ppermute(part, 'sub', route)  29.3 us
    pallas_call x17, Pallas kernels, run(): pl.pallas_call(kernel, out_shape=results, in_specs=[pl.BlockSpec(memory_s...  17.1 us
    ppermute x32, waiting for transfers between devices, exchange(): lax.ppermute(part, 'sub', route)  9.35 us
  transfers between devices with their start and end apart: 32, of which 13 were waited for; matrix products, arithmetic and copies ran while one was open for 0% of the time, Pallas kernels for 20%

profile of v15, /device:TPU:8, one launch (start us, length us, event | category | flops | bytes accessed | tf_op | source)
XLA Modules:
  0.0 56.6 jit_solution(15207486444565932268)
XLA Ops:
  0.0 1.8 %shard_map.73 = (bf16[1024,384]{1,0:T(8,128)(2,1)S(1)}, bf16[128,1024]{1,0:T(8,128)(2,1)S(1)}, bf16[128,384]{1,0:T(8,128)(2,1)S(1)}, f32[8,384]{1,0:T(8,128)S(1)...) custom-call(s32[1,4,128]{2,1,0:T(4,128)} %rows_in.1, ...), custom_call_target="tpu_custom_call" | custom-call | flops 100663296 | bytes 5756944 | tf_op jit(solution)/shard_map/pallas_call | solution.py:332
  1.8 2.7 %collective-permute-start = (bf16[128,128]{1,0:T(8,128)(2,1)S(1)}, bf16[128,128]{1,0:T(8,128)(2,1)S(1)}, u32[]{:S(2)}, u32[]{:S(2)}) collective-permute-start(bf16[128,128]{1,0:T(8,128)(2,1)S(1)} %get-tuple-element.78), channel_id=1, source_target_pairs={{0,16},{1,2},{2,1},{3,19},{4,5},{5,4},{6,15},{7,23},{8,24},{9,25},... | collective-permute-start | bytes 98312 | tf_op jit(solution)/shard_map/ppermute | solution.py:367
  4.4 1.5 %collective-permute-start.1 = (bf16[128,128]{1,0:T(8,128)(2,1)S(1)}, bf16[128,128]{1,0:T(8,128)(2,1)S(1)}, u32[]{:S(2)}, u32[]{:S(2)}) collective-permute-start(bf16[128,128]{1,0:T(8,128)(2,1)S(1)} %get-tuple-element.79), channel_id=1, source_target_pairs={{0,2},{1,17},{2,0},{3,4},{4,3},{5,6},{6,5},{7,8},{8,7},{9,10},{10,... | collective-permute-start | bytes 98312 | tf_op jit(solution)/shard_map/ppermute | solution.py:367
  6.0 0.4 collective-permute-start.3
  7.1 2.1 %shard_map.74 = (bf16[384,1024]{1,0:T(8,128)(2,1)S(1)}, bf16[384,1024]{1,0:T(8,128)(2,1)S(1)}, bf16[384,384]{1,0:T(8,128)(2,1)S(1)}, bf16[384,384]{1,0:T(8,128)(...) custom-call(bf16[1024,384]{1,0:T(8,128)(2,1)S(1)} %get-tuple-element, ...), custom_call_target="tpu_custom_call" | custom-call | flops 1207959552 | bytes 10317828 | tf_op jit(solution)/shard_map/pallas_call | solution.py:332
  9.3 0.6 %collective-permute-done.1.refs_1_ = bf16[128,128]{1,0:T(8,128)(2,1)S(1)} collective-permute-done((bf16[128,128]{1,0:T(8,128)(2,1)S(1)}, bf16[128,128]{1,0:T(8,128)(2,1)S(1)}, u32[]{:S(2)}, u32[]{:S(2)}) %collective-permute-start.1) | collective-permute-done | bytes 32800 | tf_op jit(solution)/shard_map/ppermute | solution.py:367
  9.9 0.4 shard_map.75
  10.6 1.1 %collective-permute-start.5 = (bf16[128,128]{1,0:T(8,128)(2,1)S(1)}, bf16[128,128]{1,0:T(8,128)(2,1)S(1)}, u32[]{:S(2)}, u32[]{:S(2)}) collective-permute-start(bf16[128,128]{1,0:T(8,128)(2,1)S(1)} %get-tuple-element.93), channel_id=1, source_target_pairs={{0,2},{1,17},{2,0},{3,4},{4,3},{5,6},{6,5},{7,8},{8,7},{9,10},{10,... | collective-permute-start | bytes 98312 | tf_op jit(solution)/shard_map/ppermute | solution.py:367
  12.2 2.7 %shard_map.76 = (f32[128,1024]{1,0:T(8,128)S(1)}, f32[128,384]{1,0:T(8,128)S(1)}, bf16[1024,384]{1,0:T(8,128)(2,1)S(1)}, bf16[384,384]{1,0:T(8,128)(2,1)S(1)}) custom-call(bf16[128,128]{1,0:T(8,128)(2,1)S(1)} %collective-permute-done.refs_0_, bf16[128,128]{1,0:T(8,128)(2,1)S(1)} %collective-permute-done.1.refs_1_, ...), custom_call_target="tpu_custom_call" | custom-call | flops 1577058304 | bytes 8392704 | tf_op jit(solution)/shard_map/pallas_call | solution.py:332
  15.2 0.5 collective-permute-done.5.refs_1_
  16.1 1.5 %collective-permute-start.8 = (bf16[128,128]{1,0:T(8,128)(2,1)S(1)}, bf16[128,128]{1,0:T(8,128)(2,1)S(1)}, u32[]{:S(2)}, u32[]{:S(2)}) collective-permute-start(bf16[128,128]{1,0:T(8,128)(2,1)S(1)} %get-tuple-element.104), channel_id=1, source_target_pairs={{0,16},{1,2},{2,1},{3,19},{4,20},{5,21},{6,22},{7,8},{8,7},{9,10},... | collective-permute-start | bytes 98312 | tf_op jit(solution)/shard_map/ppermute | solution.py:367
  17.7 2.5 %collective-permute-start.9 = (bf16[128,128]{1,0:T(8,128)(2,1)S(1)}, bf16[128,128]{1,0:T(8,128)(2,1)S(1)}, u32[]{:S(2)}, u32[]{:S(2)}) collective-permute-start(bf16[128,128]{1,0:T(8,128)(2,1)S(1)} %get-tuple-element.105), channel_id=1, source_target_pairs={{0,3},{1,17},{2,18},{3,0},{4,13},{5,6},{6,5},{7,23},{8,24},{9,25},... | collective-permute-start | bytes 98312 | tf_op jit(solution)/shard_map/ppermute | solution.py:367
  20.2 0.5 collective-permute-start.11
  20.7 1.0 %shard_map.78 = (f32[128,1024]{1,0:T(8,128)S(1)}, f32[128,1024]{1,0:T(8,128)S(1)}, f32[128,384]{1,0:T(8,128)S(1)}) custom-call(bf16[128,128]{1,0:T(8,128)(2,1)S(1)} %collective-permute-done.4.refs_0_, bf16[128,128]{1,0:T(8,128)(2,1)S(1)} %collective-permute-done.5.refs_1_, bf16[128,128]{1,0:T(8,128)(2,1)S(1)} %collective-permute-done.6.refs_2_, ...), custom_call_target="tpu_custom_call" | custom-call | flops 469762048 | bytes 5902336 | tf_op jit(solution)/shard_map/pallas_call | solution.py:332
  21.7 0.9 %collective-permute-done.9.refs_1_ = bf16[128,128]{1,0:T(8,128)(2,1)S(1)} collective-permute-done((bf16[128,128]{1,0:T(8,128)(2,1)S(1)}, bf16[128,128]{1,0:T(8,128)(2,1)S(1)}, u32[]{:S(2)}, u32[]{:S(2)}) %collective-permute-start.9) | collective-permute-done | bytes 32800 | tf_op jit(solution)/shard_map/ppermute | solution.py:367
  22.6 0.4 shard_map.79
  23.0 1.8 %collective-permute-start.12 = (bf16[128,128]{1,0:T(8,128)(2,1)S(1)}, bf16[128,128]{1,0:T(8,128)(2,1)S(1)}, u32[]{:S(2)}, u32[]{:S(2)}) collective-permute-start(bf16[128,128]{1,0:T(8,128)(2,1)S(1)} %get-tuple-element.113), channel_id=1, source_target_pairs={{0,16},{1,2},{2,1},{3,19},{4,20},{5,21},{6,22},{7,8},{8,7},{9,10},... | collective-permute-start | bytes 98312 | tf_op jit(solution)/shard_map/ppermute | solution.py:367
  24.8 1.8 %collective-permute-start.13 = (bf16[128,128]{1,0:T(8,128)(2,1)S(1)}, bf16[128,128]{1,0:T(8,128)(2,1)S(1)}, u32[]{:S(2)}, u32[]{:S(2)}) collective-permute-start(bf16[128,128]{1,0:T(8,128)(2,1)S(1)} %get-tuple-element.114), channel_id=1, source_target_pairs={{0,3},{1,17},{2,18},{3,0},{4,13},{5,6},{6,5},{7,23},{8,24},{9,25},... | collective-permute-start | bytes 98312 | tf_op jit(solution)/shard_map/ppermute | solution.py:367
  26.6 0.5 collective-permute-start.15
  27.1 1.2 %shard_map.80 = (f32[128,1024]{1,0:T(8,128)S(1)}, f32[128,384]{1,0:T(8,128)S(1)}) custom-call(bf16[128,128]{1,0:T(8,128)(2,1)S(1)} %collective-permute-done.8.refs_0_, bf16[128,128]{1,0:T(8,128)(2,1)S(1)} %collective-permute-done.9.refs_1_, bf16[128,128]{1,0:T(8,128)(2,1)S(1)} %collective-permute-done.10.refs_2_, ...), custom_call_target="tpu_custom_call" | custom-call | flops 469762048 | bytes 5738496 | tf_op jit(solution)/shard_map/pallas_call | solution.py:332
  28.4 1.2 %collective-permute-done.13.refs_1_ = bf16[128,128]{1,0:T(8,128)(2,1)S(1)} collective-permute-done((bf16[128,128]{1,0:T(8,128)(2,1)S(1)}, bf16[128,128]{1,0:T(8,128)(2,1)S(1)}, u32[]{:S(2)}, u32[]{:S(2)}) %collective-permute-start.13) | collective-permute-done | bytes 32800 | tf_op jit(solution)/shard_map/ppermute | solution.py:367
  29.6 0.4 shard_map.81
  30.0 1.4 %collective-permute-start.16 = (bf16[128,128]{1,0:T(8,128)(2,1)S(1)}, bf16[128,128]{1,0:T(8,128)(2,1)S(1)}, u32[]{:S(2)}, u32[]{:S(2)}) collective-permute-start(bf16[128,128]{1,0:T(8,128)(2,1)S(1)} %get-tuple-element.122), channel_id=1, source_target_pairs={{0,16},{1,2},{2,1},{3,19},{4,20},{5,21},{6,22},{7,8},{8,7},{9,10},... | collective-permute-start | bytes 98312 | tf_op jit(solution)/shard_map/ppermute | solution.py:367
  31.4 1.8 %collective-permute-start.17 = (bf16[128,128]{1,0:T(8,128)(2,1)S(1)}, bf16[128,128]{1,0:T(8,128)(2,1)S(1)}, u32[]{:S(2)}, u32[]{:S(2)}) collective-permute-start(bf16[128,128]{1,0:T(8,128)(2,1)S(1)} %get-tuple-element.123), channel_id=1, source_target_pairs={{0,3},{1,17},{2,18},{3,0},{4,13},{5,6},{6,5},{7,23},{8,24},{9,25},... | collective-permute-start | bytes 98312 | tf_op jit(solution)/shard_map/ppermute | solution.py:367
  33.2 0.5 collective-permute-start.19
  33.7 1.0 %shard_map.82 = (f32[128,1024]{1,0:T(8,128)S(1)}, f32[128,1024]{1,0:T(8,128)S(1)}, f32[128,384]{1,0:T(8,128)S(1)}) custom-call(bf16[128,128]{1,0:T(8,128)(2,1)S(1)} %collective-permute-done.12.refs_0_, bf16[128,128]{1,0:T(8,128)(2,1)S(1)} %collective-permute-done.13.refs_1_, bf16[128,128]{1,0:T(8,128)(2,1)S(1)} %collective-permute-done.14.refs_2_, ...), custom_call_target="tpu_custom_call" | custom-call | flops 469762048 | bytes 5902336 | tf_op jit(solution)/shard_map/pallas_call | solution.py:332
  34.7 0.6 %collective-permute-done.16.refs_0_ = bf16[128,128]{1,0:T(8,128)(2,1)S(1)} collective-permute-done((bf16[128,128]{1,0:T(8,128)(2,1)S(1)}, bf16[128,128]{1,0:T(8,128)(2,1)S(1)}, u32[]{:S(2)}, u32[]{:S(2)}) %collective-permute-start.16) | collective-permute-done | bytes 32800 | tf_op jit(solution)/shard_map/ppermute | solution.py:367
  35.3 0.9 %collective-permute-done.17.refs_1_ = bf16[128,128]{1,0:T(8,128)(2,1)S(1)} collective-permute-done((bf16[128,128]{1,0:T(8,128)(2,1)S(1)}, bf16[128,128]{1,0:T(8,128)(2,1)S(1)}, u32[]{:S(2)}, u32[]{:S(2)}) %collective-permute-start.17) | collective-permute-done | bytes 32800 | tf_op jit(solution)/shard_map/ppermute | solution.py:367
  36.2 0.4 shard_map.83
  36.6 1.2 %collective-permute-start.20 = (bf16[128,128]{1,0:T(8,128)(2,1)S(1)}, bf16[128,128]{1,0:T(8,128)(2,1)S(1)}, u32[]{:S(2)}, u32[]{:S(2)}) collective-permute-start(bf16[128,128]{1,0:T(8,128)(2,1)S(1)} %get-tuple-element.130), channel_id=1, source_target_pairs={{0,16},{1,2},{2,1},{3,19},{4,20},{5,21},{6,22},{7,8},{8,7},{9,10},... | collective-permute-start | bytes 98312 | tf_op jit(solution)/shard_map/ppermute | solution.py:367
  37.8 1.7 %collective-permute-start.21 = (bf16[128,128]{1,0:T(8,128)(2,1)S(1)}, bf16[128,128]{1,0:T(8,128)(2,1)S(1)}, u32[]{:S(2)}, u32[]{:S(2)}) collective-permute-start(bf16[128,128]{1,0:T(8,128)(2,1)S(1)} %get-tuple-element.131), channel_id=1, source_target_pairs={{0,3},{1,17},{2,18},{3,0},{4,13},{5,6},{6,5},{7,23},{8,24},{9,25},... | collective-permute-start | bytes 98312 | tf_op jit(solution)/shard_map/ppermute | solution.py:367
  39.5 0.5 collective-permute-start.23
  40.0 1.3 %shard_map.84 = (f32[128,1024]{1,0:T(8,128)S(1)}, f32[128,384]{1,0:T(8,128)S(1)}) custom-call(bf16[128,128]{1,0:T(8,128)(2,1)S(1)} %collective-permute-done.16.refs_0_, bf16[128,128]{1,0:T(8,128)(2,1)S(1)} %collective-permute-done.17.refs_1_, bf16[128,128]{1,0:T(8,128)(2,1)S(1)} %collective-permute-done.18.refs_2_, ...), custom_call_target="tpu_custom_call" | custom-call | flops 469762048 | bytes 5738496 | tf_op jit(solution)/shard_map/pallas_call | solution.py:332
  41.3 0.5 collective-permute-done.20.refs_0_
  41.8 0.8 %collective-permute-done.21.refs_1_ = bf16[128,128]{1,0:T(8,128)(2,1)S(1)} collective-permute-done((bf16[128,128]{1,0:T(8,128)(2,1)S(1)}, bf16[128,128]{1,0:T(8,128)(2,1)S(1)}, u32[]{:S(2)}, u32[]{:S(2)}) %collective-permute-start.21) | collective-permute-done | bytes 32800 | tf_op jit(solution)/shard_map/ppermute | solution.py:367
  43.0 1.4 %collective-permute-start.24 = (bf16[128,128]{1,0:T(8,128)(2,1)S(1)}, bf16[128,128]{1,0:T(8,128)(2,1)S(1)}, u32[]{:S(2)}, u32[]{:S(2)}) collective-permute-start(bf16[128,128]{1,0:T(8,128)(2,1)S(1)} %get-tuple-element.138), channel_id=1, source_target_pairs={{0,16},{1,2},{2,1},{3,19},{4,20},{5,21},{6,22},{7,8},{8,7},{9,10},... | collective-permute-start | bytes 98312 | tf_op jit(solution)/shard_map/ppermute | solution.py:367
  44.4 1.8 %collective-permute-start.25 = (bf16[128,128]{1,0:T(8,128)(2,1)S(1)}, bf16[128,128]{1,0:T(8,128)(2,1)S(1)}, u32[]{:S(2)}, u32[]{:S(2)}) collective-permute-start(bf16[128,128]{1,0:T(8,128)(2,1)S(1)} %get-tuple-element.139), channel_id=1, source_target_pairs={{0,3},{1,17},{2,18},{3,0},{4,13},{5,6},{6,5},{7,23},{8,24},{9,25},... | collective-permute-start | bytes 98312 | tf_op jit(solution)/shard_map/ppermute | solution.py:367
  46.1 0.5 collective-permute-start.27
  46.7 1.0 %shard_map.86 = (f32[128,1024]{1,0:T(8,128)S(1)}, f32[128,1024]{1,0:T(8,128)S(1)}, f32[128,384]{1,0:T(8,128)S(1)}) custom-call(bf16[128,128]{1,0:T(8,128)(2,1)S(1)} %collective-permute-done.20.refs_0_, bf16[128,128]{1,0:T(8,128)(2,1)S(1)} %collective-permute-done.21.refs_1_, bf16[128,128]{1,0:T(8,128)(2,1)S(1)} %collective-permute-done.22.refs_2_, ...), custom_call_target="tpu_custom_call" | custom-call | flops 469762048 | bytes 5902336 | tf_op jit(solution)/shard_map/pallas_call | solution.py:332
  47.7 0.5 collective-permute-done.24.refs_0_
  48.2 1.0 %collective-permute-done.25.refs_1_ = bf16[128,128]{1,0:T(8,128)(2,1)S(1)} collective-permute-done((bf16[128,128]{1,0:T(8,128)(2,1)S(1)}, bf16[128,128]{1,0:T(8,128)(2,1)S(1)}, u32[]{:S(2)}, u32[]{:S(2)}) %collective-permute-start.25) | collective-permute-done | bytes 32800 | tf_op jit(solution)/shard_map/ppermute | solution.py:367
  49.6 1.2 %collective-permute-start.28 = (bf16[128,128]{1,0:T(8,128)(2,1)S(1)}, bf16[128,128]{1,0:T(8,128)(2,1)S(1)}, u32[]{:S(2)}, u32[]{:S(2)}) collective-permute-start(bf16[128,128]{1,0:T(8,128)(2,1)S(1)} %get-tuple-element.145), channel_id=1, source_target_pairs={{0,16},{1,2},{2,1},{3,19},{4,20},{5,21},{6,22},{7,8},{8,7},{9,10},... | collective-permute-start | bytes 98312 | tf_op jit(solution)/shard_map/ppermute | solution.py:367
  50.7 1.7 %collective-permute-start.29 = (bf16[128,128]{1,0:T(8,128)(2,1)S(1)}, bf16[128,128]{1,0:T(8,128)(2,1)S(1)}, u32[]{:S(2)}, u32[]{:S(2)}) collective-permute-start(bf16[128,128]{1,0:T(8,128)(2,1)S(1)} %get-tuple-element.146), channel_id=1, source_target_pairs={{0,3},{1,17},{2,18},{3,0},{4,13},{5,6},{6,5},{7,23},{8,24},{9,25},... | collective-permute-start | bytes 98312 | tf_op jit(solution)/shard_map/ppermute | solution.py:367
  52.5 0.5 collective-permute-start.31
  53.0 1.2 %shard_map.88.refs_5_ = f32[1024,128]{1,0:T(8,128)S(1)} custom-call(bf16[128,128]{1,0:T(8,128)(2,1)S(1)} %collective-permute-done.24.refs_0_, bf16[128,128]{1,0:T(8,128)(2,1)S(1)} %collective-permute-done.25.refs_1_, bf16[128,128]{1,0:T(8,128)(2,1)S(1)} %collective-permute-done.26.refs_2_, bf16[128,128]{1,0:T(8,128)(2,1)S(1)} %collective-permute-done.27.refs_3_, ...), custom_call_target="tpu_custom_call" | custom-call | flops 369098752 | bytes 4624384 | tf_op jit(solution)/shard_map/pallas_call | solution.py:332
  54.2 0.6 %collective-permute-done.28.refs_0_ = bf16[128,128]{1,0:T(8,128)(2,1)S(1)} collective-permute-done((bf16[128,128]{1,0:T(8,128)(2,1)S(1)}, bf16[128,128]{1,0:T(8,128)(2,1)S(1)}, u32[]{:S(2)}, u32[]{:S(2)}) %collective-permute-start.28) | collective-permute-done | bytes 32800 | tf_op jit(solution)/shard_map/ppermute | solution.py:367
  54.8 0.8 %collective-permute-done.29.refs_1_ = bf16[128,128]{1,0:T(8,128)(2,1)S(1)} collective-permute-done((bf16[128,128]{1,0:T(8,128)(2,1)S(1)}, bf16[128,128]{1,0:T(8,128)(2,1)S(1)}, u32[]{:S(2)}, u32[]{:S(2)}) %collective-permute-start.29) | collective-permute-done | bytes 32800 | tf_op jit(solution)/shard_map/ppermute | solution.py:367
  55.6 1.1 %shard_map.89 = f32[1,1024,128]{2,1,0:T(8,128)} custom-call(bf16[128,128]{1,0:T(8,128)(2,1)S(1)} %collective-permute-done.28.refs_0_, bf16[128,128]{1,0:T(8,128)(2,1)S(1)} %collective-permute-done.29.refs_1_, bf16[128,128]{1,0:T(8,128)(2,1)S(1)} %collective-permute-done.30.refs_2_, bf16[128,128]{1,0:T(8,128)(2,1)S(1)} %collective-permute-done.31.refs_3_, ...), custom_call_target="tpu_custom_call" | custom-call | flops 100663296 | bytes 1966080 | tf_op jit(solution)/shard_map/pallas_call | solution.py:332
  (33 shorter events, 2.6 us)
Async XLA Ops:
  1.8 7.5 %collective-permute-start = (bf16[128,128]{1,0:T(8,128)(2,1)S(1)}, bf16[128,128]{1,0:T(8,128)(2,1)S(1)}, u32[]{:S(2)}, u32[]{:S(2)}) collective-permute-start(bf16[128,128]{1,0:T(8,128)(2,1)S(1)} %get-tuple-element.78), channel_id=1, source_target_pairs={{0,16},{1,2},{2,1},{3,19},{4,5},{5,4},{6,15},{7,23},{8,24},{9,25},... | collective-permute-start | bytes 98312 | tf_op jit(solution)/shard_map/ppermute | solution.py:367
  4.4 5.4 %collective-permute-start.1 = (bf16[128,128]{1,0:T(8,128)(2,1)S(1)}, bf16[128,128]{1,0:T(8,128)(2,1)S(1)}, u32[]{:S(2)}, u32[]{:S(2)}) collective-permute-start(bf16[128,128]{1,0:T(8,128)(2,1)S(1)} %get-tuple-element.79), channel_id=1, source_target_pairs={{0,2},{1,17},{2,0},{3,4},{4,3},{5,6},{6,5},{7,8},{8,7},{9,10},{10,... | collective-permute-start | bytes 98312 | tf_op jit(solution)/shard_map/ppermute | solution.py:367
  5.9 3.9 %collective-permute-start.2 = (bf16[128,128]{1,0:T(8,128)(2,1)S(1)}, bf16[128,128]{1,0:T(8,128)(2,1)S(1)}, u32[]{:S(2)}, u32[]{:S(2)}) collective-permute-start(bf16[128,128]{1,0:T(8,128)(2,1)S(1)} %get-tuple-element.80), channel_id=1, source_target_pairs={{0,1},{1,0},{2,18},{3,7},{4,20},{5,21},{6,22},{7,3},{8,9},{9,8},{1... | collective-permute-start | bytes 98312 | tf_op jit(solution)/shard_map/ppermute | solution.py:367
  6.0 3.8 %collective-permute-start.3 = (bf16[128,128]{1,0:T(8,128)(2,1)S(1)}, bf16[128,128]{1,0:T(8,128)(2,1)S(1)}, u32[]{:S(2)}, u32[]{:S(2)}) collective-permute-start(bf16[128,128]{1,0:T(8,128)(2,1)S(1)} %get-tuple-element.81), channel_id=1, source_target_pairs={{0,1},{1,0},{2,3},{3,2},{4,5},{5,4},{6,7},{7,6},{8,9},{9,8},{10,11... | collective-permute-start | bytes 98312 | tf_op jit(solution)/shard_map/ppermute | solution.py:367
  10.3 5.0 %collective-permute-start.4 = (bf16[128,128]{1,0:T(8,128)(2,1)S(1)}, bf16[128,128]{1,0:T(8,128)(2,1)S(1)}, u32[]{:S(2)}, u32[]{:S(2)}) collective-permute-start(bf16[128,128]{1,0:T(8,128)(2,1)S(1)} %get-tuple-element.92), channel_id=1, source_target_pairs={{0,16},{1,2},{2,1},{3,19},{4,5},{5,4},{6,15},{7,23},{8,24},{9,25},... | collective-permute-start | bytes 98312 | tf_op jit(solution)/shard_map/ppermute | solution.py:367
  10.6 5.1 %collective-permute-start.5 = (bf16[128,128]{1,0:T(8,128)(2,1)S(1)}, bf16[128,128]{1,0:T(8,128)(2,1)S(1)}, u32[]{:S(2)}, u32[]{:S(2)}) collective-permute-start(bf16[128,128]{1,0:T(8,128)(2,1)S(1)} %get-tuple-element.93), channel_id=1, source_target_pairs={{0,2},{1,17},{2,0},{3,4},{4,3},{5,6},{6,5},{7,8},{8,7},{9,10},{10,... | collective-permute-start | bytes 98312 | tf_op jit(solution)/shard_map/ppermute | solution.py:367
  11.7 4.1 %collective-permute-start.6 = (bf16[128,128]{1,0:T(8,128)(2,1)S(1)}, bf16[128,128]{1,0:T(8,128)(2,1)S(1)}, u32[]{:S(2)}, u32[]{:S(2)}) collective-permute-start(bf16[128,128]{1,0:T(8,128)(2,1)S(1)} %get-tuple-element.94), channel_id=1, source_target_pairs={{0,1},{1,0},{2,18},{3,7},{4,20},{5,21},{6,22},{7,3},{8,9},{9,8},{1... | collective-permute-start | bytes 98312 | tf_op jit(solution)/shard_map/ppermute | solution.py:367
  11.9 3.9 %collective-permute-start.7 = (bf16[128,128]{1,0:T(8,128)(2,1)S(1)}, bf16[128,128]{1,0:T(8,128)(2,1)S(1)}, u32[]{:S(2)}, u32[]{:S(2)}) collective-permute-start(bf16[128,128]{1,0:T(8,128)(2,1)S(1)} %get-tuple-element.95), channel_id=1, source_target_pairs={{0,1},{1,0},{2,3},{3,2},{4,5},{5,4},{6,7},{7,6},{8,9},{9,8},{10,11... | collective-permute-start | bytes 98312 | tf_op jit(solution)/shard_map/ppermute | solution.py:367
  16.1 5.6 %collective-permute-start.8 = (bf16[128,128]{1,0:T(8,128)(2,1)S(1)}, bf16[128,128]{1,0:T(8,128)(2,1)S(1)}, u32[]{:S(2)}, u32[]{:S(2)}) collective-permute-start(bf16[128,128]{1,0:T(8,128)(2,1)S(1)} %get-tuple-element.104), channel_id=1, source_target_pairs={{0,16},{1,2},{2,1},{3,19},{4,20},{5,21},{6,22},{7,8},{8,7},{9,10},... | collective-permute-start | bytes 98312 | tf_op jit(solution)/shard_map/ppermute | solution.py:367
  17.7 4.9 %collective-permute-start.9 = (bf16[128,128]{1,0:T(8,128)(2,1)S(1)}, bf16[128,128]{1,0:T(8,128)(2,1)S(1)}, u32[]{:S(2)}, u32[]{:S(2)}) collective-permute-start(bf16[128,128]{1,0:T(8,128)(2,1)S(1)} %get-tuple-element.105), channel_id=1, source_target_pairs={{0,3},{1,17},{2,18},{3,0},{4,13},{5,6},{6,5},{7,23},{8,24},{9,25},... | collective-permute-start | bytes 98312 | tf_op jit(solution)/shard_map/ppermute | solution.py:367
  20.2 2.4 %collective-permute-start.10 = (bf16[128,128]{1,0:T(8,128)(2,1)S(1)}, bf16[128,128]{1,0:T(8,128)(2,1)S(1)}, u32[]{:S(2)}, u32[]{:S(2)}) collective-permute-start(bf16[128,128]{1,0:T(8,128)(2,1)S(1)} %get-tuple-element.106), channel_id=1, source_target_pairs={{0,1},{1,0},{2,5},{3,4},{4,3},{5,2},{6,7},{7,6},{8,9},{9,8},{10,11... | collective-permute-start | bytes 98312 | tf_op jit(solution)/shard_map/ppermute | solution.py:367
  20.2 2.4 %collective-permute-start.11 = (bf16[128,128]{1,0:T(8,128)(2,1)S(1)}, bf16[128,128]{1,0:T(8,128)(2,1)S(1)}, u32[]{:S(2)}, u32[]{:S(2)}) collective-permute-start(bf16[128,128]{1,0:T(8,128)(2,1)S(1)} %get-tuple-element.107), channel_id=1, source_target_pairs={{0,1},{1,0},{2,3},{3,2},{4,5},{5,4},{6,7},{7,6},{8,9},{9,8},{10,11... | collective-permute-start | bytes 98312 | tf_op jit(solution)/shard_map/ppermute | solution.py:367
  23.0 5.4 %collective-permute-start.12 = (bf16[128,128]{1,0:T(8,128)(2,1)S(1)}, bf16[128,128]{1,0:T(8,128)(2,1)S(1)}, u32[]{:S(2)}, u32[]{:S(2)}) collective-permute-start(bf16[128,128]{1,0:T(8,128)(2,1)S(1)} %get-tuple-element.113), channel_id=1, source_target_pairs={{0,16},{1,2},{2,1},{3,19},{4,20},{5,21},{6,22},{7,8},{8,7},{9,10},... | collective-permute-start | bytes 98312 | tf_op jit(solution)/shard_map/ppermute | solution.py:367
  24.8 4.8 %collective-permute-start.13 = (bf16[128,128]{1,0:T(8,128)(2,1)S(1)}, bf16[128,128]{1,0:T(8,128)(2,1)S(1)}, u32[]{:S(2)}, u32[]{:S(2)}) collective-permute-start(bf16[128,128]{1,0:T(8,128)(2,1)S(1)} %get-tuple-element.114), channel_id=1, source_target_pairs={{0,3},{1,17},{2,18},{3,0},{4,13},{5,6},{6,5},{7,23},{8,24},{9,25},... | collective-permute-start | bytes 98312 | tf_op jit(solution)/shard_map/ppermute | solution.py:367
  26.6 3.1 %collective-permute-start.14 = (bf16[128,128]{1,0:T(8,128)(2,1)S(1)}, bf16[128,128]{1,0:T(8,128)(2,1)S(1)}, u32[]{:S(2)}, u32[]{:S(2)}) collective-permute-start(bf16[128,128]{1,0:T(8,128)(2,1)S(1)} %get-tuple-element.115), channel_id=1, source_target_pairs={{0,1},{1,0},{2,5},{3,4},{4,3},{5,2},{6,7},{7,6},{8,9},{9,8},{10,11... | collective-permute-start | bytes 98312 | tf_op jit(solution)/shard_map/ppermute | solution.py:367
  26.6 3.1 %collective-permute-start.15 = (bf16[128,128]{1,0:T(8,128)(2,1)S(1)}, bf16[128,128]{1,0:T(8,128)(2,1)S(1)}, u32[]{:S(2)}, u32[]{:S(2)}) collective-permute-start(bf16[128,128]{1,0:T(8,128)(2,1)S(1)} %get-tuple-element.116), channel_id=1, source_target_pairs={{0,1},{1,0},{2,3},{3,2},{4,5},{5,4},{6,7},{7,6},{8,9},{9,8},{10,11... | collective-permute-start | bytes 98312 | tf_op jit(solution)/shard_map/ppermute | solution.py:367
  30.0 5.3 %collective-permute-start.16 = (bf16[128,128]{1,0:T(8,128)(2,1)S(1)}, bf16[128,128]{1,0:T(8,128)(2,1)S(1)}, u32[]{:S(2)}, u32[]{:S(2)}) collective-permute-start(bf16[128,128]{1,0:T(8,128)(2,1)S(1)} %get-tuple-element.122), channel_id=1, source_target_pairs={{0,16},{1,2},{2,1},{3,19},{4,20},{5,21},{6,22},{7,8},{8,7},{9,10},... | collective-permute-start | bytes 98312 | tf_op jit(solution)/shard_map/ppermute | solution.py:367
  31.4 4.8 %collective-permute-start.17 = (bf16[128,128]{1,0:T(8,128)(2,1)S(1)}, bf16[128,128]{1,0:T(8,128)(2,1)S(1)}, u32[]{:S(2)}, u32[]{:S(2)}) collective-permute-start(bf16[128,128]{1,0:T(8,128)(2,1)S(1)} %get-tuple-element.123), channel_id=1, source_target_pairs={{0,3},{1,17},{2,18},{3,0},{4,13},{5,6},{6,5},{7,23},{8,24},{9,25},... | collective-permute-start | bytes 98312 | tf_op jit(solution)/shard_map/ppermute | solution.py:367
  33.2 3.0 %collective-permute-start.18 = (bf16[128,128]{1,0:T(8,128)(2,1)S(1)}, bf16[128,128]{1,0:T(8,128)(2,1)S(1)}, u32[]{:S(2)}, u32[]{:S(2)}) collective-permute-start(bf16[128,128]{1,0:T(8,128)(2,1)S(1)} %get-tuple-element.124), channel_id=1, source_target_pairs={{0,1},{1,0},{2,5},{3,4},{4,3},{5,2},{6,7},{7,6},{8,9},{9,8},{10,11... | collective-permute-start | bytes 98312 | tf_op jit(solution)/shard_map/ppermute | solution.py:367
  33.2 3.0 %collective-permute-start.19 = (bf16[128,128]{1,0:T(8,128)(2,1)S(1)}, bf16[128,128]{1,0:T(8,128)(2,1)S(1)}, u32[]{:S(2)}, u32[]{:S(2)}) collective-permute-start(bf16[128,128]{1,0:T(8,128)(2,1)S(1)} %get-tuple-element.125), channel_id=1, source_target_pairs={{0,1},{1,0},{2,3},{3,2},{4,5},{5,4},{6,7},{7,6},{8,9},{9,8},{10,11... | collective-permute-start | bytes 98312 | tf_op jit(solution)/shard_map/ppermute | solution.py:367
  36.6 5.2 %collective-permute-start.20 = (bf16[128,128]{1,0:T(8,128)(2,1)S(1)}, bf16[128,128]{1,0:T(8,128)(2,1)S(1)}, u32[]{:S(2)}, u32[]{:S(2)}) collective-permute-start(bf16[128,128]{1,0:T(8,128)(2,1)S(1)} %get-tuple-element.130), channel_id=1, source_target_pairs={{0,16},{1,2},{2,1},{3,19},{4,20},{5,21},{6,22},{7,8},{8,7},{9,10},... | collective-permute-start | bytes 98312 | tf_op jit(solution)/shard_map/ppermute | solution.py:367
  37.8 4.8 %collective-permute-start.21 = (bf16[128,128]{1,0:T(8,128)(2,1)S(1)}, bf16[128,128]{1,0:T(8,128)(2,1)S(1)}, u32[]{:S(2)}, u32[]{:S(2)}) collective-permute-start(bf16[128,128]{1,0:T(8,128)(2,1)S(1)} %get-tuple-element.131), channel_id=1, source_target_pairs={{0,3},{1,17},{2,18},{3,0},{4,13},{5,6},{6,5},{7,23},{8,24},{9,25},... | collective-permute-start | bytes 98312 | tf_op jit(solution)/shard_map/ppermute | solution.py:367
  39.5 3.1 %collective-permute-start.22 = (bf16[128,128]{1,0:T(8,128)(2,1)S(1)}, bf16[128,128]{1,0:T(8,128)(2,1)S(1)}, u32[]{:S(2)}, u32[]{:S(2)}) collective-permute-start(bf16[128,128]{1,0:T(8,128)(2,1)S(1)} %get-tuple-element.132), channel_id=1, source_target_pairs={{0,1},{1,0},{2,5},{3,4},{4,3},{5,2},{6,7},{7,6},{8,9},{9,8},{10,11... | collective-permute-start | bytes 98312 | tf_op jit(solution)/shard_map/ppermute | solution.py:367
  39.5 3.1 %collective-permute-start.23 = (bf16[128,128]{1,0:T(8,128)(2,1)S(1)}, bf16[128,128]{1,0:T(8,128)(2,1)S(1)}, u32[]{:S(2)}, u32[]{:S(2)}) collective-permute-start(bf16[128,128]{1,0:T(8,128)(2,1)S(1)} %get-tuple-element.133), channel_id=1, source_target_pairs={{0,1},{1,0},{2,3},{3,2},{4,5},{5,4},{6,7},{7,6},{8,9},{9,8},{10,11... | collective-permute-start | bytes 98312 | tf_op jit(solution)/shard_map/ppermute | solution.py:367
  43.0 5.2 %collective-permute-start.24 = (bf16[128,128]{1,0:T(8,128)(2,1)S(1)}, bf16[128,128]{1,0:T(8,128)(2,1)S(1)}, u32[]{:S(2)}, u32[]{:S(2)}) collective-permute-start(bf16[128,128]{1,0:T(8,128)(2,1)S(1)} %get-tuple-element.138), channel_id=1, source_target_pairs={{0,16},{1,2},{2,1},{3,19},{4,20},{5,21},{6,22},{7,8},{8,7},{9,10},... | collective-permute-start | bytes 98312 | tf_op jit(solution)/shard_map/ppermute | solution.py:367
  44.4 4.8 %collective-permute-start.25 = (bf16[128,128]{1,0:T(8,128)(2,1)S(1)}, bf16[128,128]{1,0:T(8,128)(2,1)S(1)}, u32[]{:S(2)}, u32[]{:S(2)}) collective-permute-start(bf16[128,128]{1,0:T(8,128)(2,1)S(1)} %get-tuple-element.139), channel_id=1, source_target_pairs={{0,3},{1,17},{2,18},{3,0},{4,13},{5,6},{6,5},{7,23},{8,24},{9,25},... | collective-permute-start | bytes 98312 | tf_op jit(solution)/shard_map/ppermute | solution.py:367
  46.1 3.0 %collective-permute-start.26 = (bf16[128,128]{1,0:T(8,128)(2,1)S(1)}, bf16[128,128]{1,0:T(8,128)(2,1)S(1)}, u32[]{:S(2)}, u32[]{:S(2)}) collective-permute-start(bf16[128,128]{1,0:T(8,128)(2,1)S(1)} %get-tuple-element.140), channel_id=1, source_target_pairs={{0,1},{1,0},{2,5},{3,4},{4,3},{5,2},{6,7},{7,6},{8,9},{9,8},{10,11... | collective-permute-start | bytes 98312 | tf_op jit(solution)/shard_map/ppermute | solution.py:367
  46.1 3.0 %collective-permute-start.27 = (bf16[128,128]{1,0:T(8,128)(2,1)S(1)}, bf16[128,128]{1,0:T(8,128)(2,1)S(1)}, u32[]{:S(2)}, u32[]{:S(2)}) collective-permute-start(bf16[128,128]{1,0:T(8,128)(2,1)S(1)} %get-tuple-element.141), channel_id=1, source_target_pairs={{0,1},{1,0},{2,3},{3,2},{4,5},{5,4},{6,7},{7,6},{8,9},{9,8},{10,11... | collective-permute-start | bytes 98312 | tf_op jit(solution)/shard_map/ppermute | solution.py:367
  49.6 5.2 %collective-permute-start.28 = (bf16[128,128]{1,0:T(8,128)(2,1)S(1)}, bf16[128,128]{1,0:T(8,128)(2,1)S(1)}, u32[]{:S(2)}, u32[]{:S(2)}) collective-permute-start(bf16[128,128]{1,0:T(8,128)(2,1)S(1)} %get-tuple-element.145), channel_id=1, source_target_pairs={{0,16},{1,2},{2,1},{3,19},{4,20},{5,21},{6,22},{7,8},{8,7},{9,10},... | collective-permute-start | bytes 98312 | tf_op jit(solution)/shard_map/ppermute | solution.py:367
  50.7 4.8 %collective-permute-start.29 = (bf16[128,128]{1,0:T(8,128)(2,1)S(1)}, bf16[128,128]{1,0:T(8,128)(2,1)S(1)}, u32[]{:S(2)}, u32[]{:S(2)}) collective-permute-start(bf16[128,128]{1,0:T(8,128)(2,1)S(1)} %get-tuple-element.146), channel_id=1, source_target_pairs={{0,3},{1,17},{2,18},{3,0},{4,13},{5,6},{6,5},{7,23},{8,24},{9,25},... | collective-permute-start | bytes 98312 | tf_op jit(solution)/shard_map/ppermute | solution.py:367
  52.5 3.1 %collective-permute-start.30 = (bf16[128,128]{1,0:T(8,128)(2,1)S(1)}, bf16[128,128]{1,0:T(8,128)(2,1)S(1)}, u32[]{:S(2)}, u32[]{:S(2)}) collective-permute-start(bf16[128,128]{1,0:T(8,128)(2,1)S(1)} %get-tuple-element.147), channel_id=1, source_target_pairs={{0,1},{1,0},{2,5},{3,4},{4,3},{5,2},{6,7},{7,6},{8,9},{9,8},{10,11... | collective-permute-start | bytes 98312 | tf_op jit(solution)/shard_map/ppermute | solution.py:367
  52.5 3.1 %collective-permute-start.31 = (bf16[128,128]{1,0:T(8,128)(2,1)S(1)}, bf16[128,128]{1,0:T(8,128)(2,1)S(1)}, u32[]{:S(2)}, u32[]{:S(2)}) collective-permute-start(bf16[128,128]{1,0:T(8,128)(2,1)S(1)} %get-tuple-element.148), channel_id=1, source_target_pairs={{0,1},{1,0},{2,3},{3,2},{4,5},{5,4},{6,7},{7,6},{8,9},{9,8},{10,11... | collective-permute-start | bytes 98312 | tf_op jit(solution)/shard_map/ppermute | solution.py:367

commit v16 on v12

--- a/solution.py
+++ b/solution.py
@@ -127,7 +127,7 @@
         (near_in, near_ref),
         (rhs_in, rhs_ref),
         (weight_in, weight_ref),
-        (n_in, n_ref),
+        (n_in.at[0, :, pl.ds(0, n_ref.shape[1])], n_ref),
     ]
     copies = [pltpu.make_async_copy(source, target, sems.at[k]) for k, (source, target) in enumerate(pairs)]
     for copy in copies:
@@ -161,6 +161,7 @@
     n_ref,
     weight_ref,
     count_ref,
+    n_in,
     s_in,
     hot_t_ref,
     n_pick_ref,
@@ -171,11 +172,15 @@
     local_ref,
     base_ref,
     row_ref,
+    n_rest_ref,
     s_ref,
-    sem,
+    sems,
 ):
-    copy = pltpu.make_async_copy(s_in, s_ref, sem)
-    copy.start()
+    half = n_rest_ref.shape[1]
+    rest_copy = pltpu.make_async_copy(n_in.at[0, :, pl.ds(half, half)], n_rest_ref, sems.at[0])
+    s_copy = pltpu.make_async_copy(s_in, s_ref, sems.at[1])
+    rest_copy.start()
+    s_copy.start()
     hot = hot_ref[...]
     width, total = hot.shape
     weight = weight_ref[...]
@@ -196,9 +201,7 @@
     same_ref[...] = same.astype(BF16)
     inner = jnp.where(jnp.concatenate(hits, 1) > 0.0, 0.0, 1.0)
     inner_ref[...] = jnp.broadcast_to(inner, inner_ref.shape)
-    n_pick = times(hot_t_ref[...], n_ref[0]).astype(BF16)
-    n_pick_ref[...] = n_pick
-    n_small_ref[...] = times(n_pick, hot).astype(BF16)
+    n_pick_ref[:, :half] = times(hot_t_ref[...], n_ref[...]).astype(BF16)
     earlier = lax.broadcasted_iota(jnp.int32, same.shape, 0) < lax.broadcasted_iota(jnp.int32, same.shape, 1)
     repeats = jnp.sum(jnp.where(earlier, same, 0.0), 0, keepdims=True)
     first = jnp.where(repeats > 0.0, 0.0, 1.0)
@@ -213,12 +216,16 @@
     row_ref[1:2] = chosen * first
     row_ref[2:3] = first
     row_ref[3:8] = jnp.zeros((5, total), F32)
+    rest_copy.wait()
+    n_pick_ref[:, half:] = times(hot_t_ref[...], n_rest_ref[...]).astype(BF16)
+    n_pick = n_pick_ref[...]
+    n_small_ref[...] = times(n_pick, hot).astype(BF16)
     mask = jnp.where(lax.broadcasted_iota(jnp.int32, mask_ref.shape, 1) < count_ref[0], 1.0, 0.0)
     mask_ref[...] = mask
     local = mask[:1] * turned_ref[...].astype(F32)
     local_ref[...] = local
     base_ref[...] = times_t((weight * local * inner).astype(BF16), n_pick)
-    copy.wait()
+    s_copy.wait()
 
 
 def update_path_kernel(trips, links, step, last, *refs):
@@ -252,18 +259,20 @@
     scatter(links, refs, local)
 
 
-def corrected(links, arrived_refs, hot_ref, n_ref, weight_ref, mask_ref, local_ref):
+def corrected(links, arrived_refs, hot_ref, n_ref, n_rest_ref, weight_ref, mask_ref, local_ref):
     weight = weight_ref[...]
     residual = local_ref[...] + times_t(gather(links, arrived_refs), hot_ref[...])
     scaled = (weight * residual).astype(BF16)
-    return mask_ref[:1] * weight * times_t(scaled, n_ref[0])
+    half = n_ref.shape[1]
+    product = times_t(scaled[:, :half], n_ref[...]) + times_t(scaled[:, half:], n_rest_ref[...])
+    return mask_ref[:1] * weight * product
 
 
 def first_update_kernel(trips, links, *refs):
     arrived_refs, refs = refs[:trips], refs[trips:]
-    hot_ref, hot_t_ref, n_ref, s_ref, weight_ref, mask_ref, inner_ref, local_ref, picked_ref = refs[:9]
-    state_out_ref, base_ref, s_pick_ref, s_small_ref = refs[9:]
-    state = DAMPING * corrected(links, arrived_refs, hot_ref, n_ref, weight_ref, mask_ref, local_ref)
+    hot_ref, hot_t_ref, n_ref, n_rest_ref, s_ref, weight_ref, mask_ref, inner_ref, local_ref, picked_ref = refs[:10]
+    state_out_ref, base_ref, s_pick_ref, s_small_ref = refs[10:]
+    state = DAMPING * corrected(links, arrived_refs, hot_ref, n_ref, n_rest_ref, weight_ref, mask_ref, local_ref)
     state_out_ref[...] = state
     s_pick = times(s_ref[0], hot_ref[...]).astype(BF16)
     s_pick_ref[...] = s_pick
@@ -273,17 +282,17 @@
 
 def update_kernel(trips, links, *refs):
     arrived_refs, refs = refs[:trips], refs[trips:]
-    hot_ref, n_ref, weight_ref, mask_ref, inner_ref, local_ref, picked_ref, s_pick_ref, state_ref = refs[:9]
-    state_out_ref, base_ref = refs[9:]
-    state = state_ref[...] + DAMPING * corrected(links, arrived_refs, hot_ref, n_ref, weight_ref, mask_ref, local_ref)
+    hot_ref, n_ref, n_rest_ref, weight_ref, mask_ref, inner_ref, local_ref, picked_ref, s_pick_ref, state_ref = refs[:10]
+    state_out_ref, base_ref = refs[10:]
+    state = state_ref[...] + DAMPING * corrected(links, arrived_refs, hot_ref, n_ref, n_rest_ref, weight_ref, mask_ref, local_ref)
     state_out_ref[...] = state
     base_ref[...] = picked_ref[...].astype(F32) - times((state * inner_ref[:1]).astype(BF16), s_pick_ref[...])
 
 
 def last_update_kernel(trips, links, *refs):
     arrived_refs, refs = refs[:trips], refs[trips:]
-    hot_ref, n_ref, weight_ref, mask_ref, local_ref, state_ref, state_out_ref = refs
-    update = corrected(links, arrived_refs, hot_ref, n_ref, weight_ref, mask_ref, local_ref)
+    hot_ref, n_ref, n_rest_ref, weight_ref, mask_ref, local_ref, state_ref, state_out_ref = refs
+    update = corrected(links, arrived_refs, hot_ref, n_ref, n_rest_ref, weight_ref, mask_ref, local_ref)
     state_out_ref[...] = (state_ref[...] + DAMPING * update).T
 
 
@@ -348,6 +357,7 @@
     full, some = array(leads, width), array(leads, total)
     small = array(total, total, BF16)
     row = array(8, width)
+    half = array(width, width // 2, BF16)
     picks = 2 * leads * total * width
     whole = 2 * leads * width * width
     path = 4 * leads * total * total
@@ -367,7 +377,7 @@
             array(leads, total, BF16),
             array(8, total),
             same_as(weights),
-            same_as(neumann),
+            half,
             *messages,
         ],
         picks,
@@ -380,9 +390,9 @@
         ],
     )
     arrived = exchange(sent)
-    hot_t, n_pick, n_small, same, inner, mask, local, base, rows, s_mat = run(
+    hot_t, n_pick, n_small, same, inner, mask, local, base, rows, n_rest, s_mat = run(
         pick_n_kernel,
-        [hot, turned, listed, n_mat, weight, counts, schur],
+        [hot, turned, listed, n_mat, weight, counts, neumann, schur],
         [
             array(total, width, BF16),
             array(total, width, BF16),
@@ -393,11 +403,12 @@
             full,
             some,
             array(8, total),
+            half,
             same_as(schur),
         ],
         2 * total * width * width + 2 * total * total * width + picks,
-        spaces={5: pltpu.SMEM, 6: pltpu.HBM},
-        scratch=[pltpu.SemaphoreType.DMA],
+        spaces={5: pltpu.SMEM, 6: pltpu.HBM, 7: pltpu.HBM},
+        scratch=[pltpu.SemaphoreType.DMA((2,))],
     )
     near = picked
     near_state = None
@@ -412,7 +423,7 @@
             arrived = exchange(sent)
             (state,) = run(
                 bound(last_update_kernel),
-                [*came, hot, n_mat, weight, mask, local, state],
+                [*came, hot, n_mat, n_rest, weight, mask, local, state],
                 [array(width, leads)],
                 whole + picks,
             )
@@ -422,14 +433,14 @@
         if step == 0:
             state, base, s_pick, s_small = run(
                 bound(first_update_kernel),
-                [*came, hot, hot_t, n_mat, s_mat, weight, mask, inner, local, picked],
+                [*came, hot, hot_t, n_mat, n_rest, s_mat, weight, mask, inner, local, picked],
                 [full, some, array(width, total, BF16), small],
                 whole + 2 * picks + 2 * total * width * (width + total),
             )
         else:
             state, base = run(
                 bound(update_kernel),
-                [*came, hot, n_mat, weight, mask, inner, local, picked, s_pick, state],
+                [*came, hot, n_mat, n_rest, weight, mask, inner, local, picked, s_pick, state],
                 [full, some],
                 whole + 2 * picks,
             )

time: 57 us -> 57 us (level)
  waiting for transfers between devices: 11.7 us -> 10.5 us
  starting transfers between devices: 27.2 us -> 28.2 us
    ppermute x32, waiting for transfers between devices: 11.7 us -> 10.5 us  [exchange(): lax.ppermute(part, 'sub', route)]
    ppermute x32, starting transfers between devices: 27.2 us -> 28.2 us  [exchange(): lax.ppermute(part, 'sub', route)]
  transfers between devices with their start and end apart: 32 -> 32, of which waited for: 13 -> 14; matrix products, arithmetic and copies ran while one was open for 0% -> 0% of each run, Pallas kernels for 20% -> 21%
where the time goes in v16:
time: 57 us; the launch traced here: 56.8 us
  starting transfers between devices  28.2 us (49%)
  Pallas kernels  17.3 us (30%)
  waiting for transfers between devices  10.5 us (18%)
  between operations  0.83 us (1%)
    ppermute x32, starting transfers between devices, exchange(): lax.ppermute(part, 'sub', route)  28.2 us
    pallas_call x17, Pallas kernels, run(): pl.pallas_call(kernel, out_shape=results, in_specs=[pl.BlockSpec(memory_s...  17.3 us
    ppermute x32, waiting for transfers between devices, exchange(): lax.ppermute(part, 'sub', route)  10.5 us
  transfers between devices with their start and end apart: 32, of which 14 were waited for; matrix products, arithmetic and copies ran while one was open for 0% of the time, Pallas kernels for 21%

profile of v16, /device:TPU:8, one launch (start us, length us, event | category | flops | bytes accessed | tf_op | source)
XLA Modules:
  0.0 56.8 jit_solution(11523919922428499531)
XLA Ops:
  0.0 1.5 %shard_map.73 = (bf16[1024,384]{1,0:T(8,128)(2,1)S(1)}, bf16[128,1024]{1,0:T(8,128)(2,1)S(1)}, bf16[128,384]{1,0:T(8,128)(2,1)S(1)}, f32[8,384]{1,0:T(8,128)S(1)...) custom-call(s32[1,4,128]{2,1,0:T(4,128)} %rows_in.1, ...), custom_call_target="tpu_custom_call" | custom-call | flops 100663296 | bytes 4708368 | tf_op jit(solution)/shard_map/pallas_call | solution.py:330
  1.5 1.8 %collective-permute-start = (bf16[128,128]{1,0:T(8,128)(2,1)S(1)}, bf16[128,128]{1,0:T(8,128)(2,1)S(1)}, u32[]{:S(2)}, u32[]{:S(2)}) collective-permute-start(bf16[128,128]{1,0:T(8,128)(2,1)S(1)} %get-tuple-element.79), channel_id=1, source_target_pairs={{0,16},{1,17},{2,18},{3,19},{4,20},{5,6},{6,5},{7,8},{8,7},{9,25},... | collective-permute-start | bytes 98312 | tf_op jit(solution)/shard_map/ppermute | solution.py:366
  3.3 2.6 %collective-permute-start.1 = (bf16[128,128]{1,0:T(8,128)(2,1)S(1)}, bf16[128,128]{1,0:T(8,128)(2,1)S(1)}, u32[]{:S(2)}, u32[]{:S(2)}) collective-permute-start(bf16[128,128]{1,0:T(8,128)(2,1)S(1)} %get-tuple-element.80), channel_id=1, source_target_pairs={{0,5},{1,2},{2,1},{3,4},{4,3},{5,0},{6,22},{7,23},{8,24},{9,10},{1... | collective-permute-start | bytes 98312 | tf_op jit(solution)/shard_map/ppermute | solution.py:366
  5.9 0.5 collective-permute-start.3
  7.1 2.5 %shard_map.74 = (bf16[384,1024]{1,0:T(8,128)(2,1)S(1)}, bf16[384,1024]{1,0:T(8,128)(2,1)S(1)}, bf16[384,384]{1,0:T(8,128)(2,1)S(1)}, bf16[384,384]{1,0:T(8,128)(...) custom-call(bf16[1024,384]{1,0:T(8,128)(2,1)S(1)} %get-tuple-element, ...), custom_call_target="tpu_custom_call" | custom-call | flops 1207959552 | bytes 12414980 | tf_op jit(solution)/shard_map/pallas_call | solution.py:330
  10.0 1.5 %collective-permute-start.4 = (bf16[128,128]{1,0:T(8,128)(2,1)S(1)}, bf16[128,128]{1,0:T(8,128)(2,1)S(1)}, u32[]{:S(2)}, u32[]{:S(2)}) collective-permute-start(bf16[128,128]{1,0:T(8,128)(2,1)S(1)} %get-tuple-element.93), channel_id=1, source_target_pairs={{0,16},{1,17},{2,18},{3,19},{4,20},{5,6},{6,5},{7,8},{8,7},{9,25},... | collective-permute-start | bytes 98312 | tf_op jit(solution)/shard_map/ppermute | solution.py:366
  11.9 0.5 collective-permute-start.7
  12.4 2.7 %shard_map.76 = (f32[128,1024]{1,0:T(8,128)S(1)}, f32[128,384]{1,0:T(8,128)S(1)}, bf16[1024,384]{1,0:T(8,128)(2,1)S(1)}, bf16[384,384]{1,0:T(8,128)(2,1)S(1)}) custom-call(bf16[128,128]{1,0:T(8,128)(2,1)S(1)} %collective-permute-done.refs_0_, bf16[128,128]{1,0:T(8,128)(2,1)S(1)} %collective-permute-done.1.refs_1_, ...), custom_call_target="tpu_custom_call" | custom-call | flops 1577058304 | bytes 8392704 | tf_op jit(solution)/shard_map/pallas_call | solution.py:330
  15.4 1.0 %collective-permute-done.5.refs_1_ = bf16[128,128]{1,0:T(8,128)(2,1)S(1)} collective-permute-done((bf16[128,128]{1,0:T(8,128)(2,1)S(1)}, bf16[128,128]{1,0:T(8,128)(2,1)S(1)}, u32[]{:S(2)}, u32[]{:S(2)}) %collective-permute-start.5) | collective-permute-done | bytes 32800 | tf_op jit(solution)/shard_map/ppermute | solution.py:366
  16.8 1.5 %collective-permute-start.8 = (bf16[128,128]{1,0:T(8,128)(2,1)S(1)}, bf16[128,128]{1,0:T(8,128)(2,1)S(1)}, u32[]{:S(2)}, u32[]{:S(2)}) collective-permute-start(bf16[128,128]{1,0:T(8,128)(2,1)S(1)} %get-tuple-element.106), channel_id=1, source_target_pairs={{0,16},{1,17},{2,18},{3,19},{4,20},{5,6},{6,5},{7,8},{8,7},{9,25},... | collective-permute-start | bytes 98312 | tf_op jit(solution)/shard_map/ppermute | solution.py:366
  18.3 1.8 %collective-permute-start.9 = (bf16[128,128]{1,0:T(8,128)(2,1)S(1)}, bf16[128,128]{1,0:T(8,128)(2,1)S(1)}, u32[]{:S(2)}, u32[]{:S(2)}) collective-permute-start(bf16[128,128]{1,0:T(8,128)(2,1)S(1)} %get-tuple-element.107), channel_id=1, source_target_pairs={{0,5},{1,2},{2,1},{3,4},{4,3},{5,0},{6,22},{7,23},{8,24},{9,10},{1... | collective-permute-start | bytes 98312 | tf_op jit(solution)/shard_map/ppermute | solution.py:366
  20.1 0.5 collective-permute-start.11
  20.6 1.0 %shard_map.78 = (f32[128,1024]{1,0:T(8,128)S(1)}, f32[128,1024]{1,0:T(8,128)S(1)}, f32[128,384]{1,0:T(8,128)S(1)}) custom-call(bf16[128,128]{1,0:T(8,128)(2,1)S(1)} %collective-permute-done.4.refs_0_, bf16[128,128]{1,0:T(8,128)(2,1)S(1)} %collective-permute-done.5.refs_1_, bf16[128,128]{1,0:T(8,128)(2,1)S(1)} %collective-permute-done.6.refs_2_, ...), custom_call_target="tpu_custom_call" | custom-call | flops 469762048 | bytes 5902336 | tf_op jit(solution)/shard_map/pallas_call | solution.py:330
  21.6 0.4 collective-permute-done.8.refs_0_
  22.0 1.1 %collective-permute-done.9.refs_1_ = bf16[128,128]{1,0:T(8,128)(2,1)S(1)} collective-permute-done((bf16[128,128]{1,0:T(8,128)(2,1)S(1)}, bf16[128,128]{1,0:T(8,128)(2,1)S(1)}, u32[]{:S(2)}, u32[]{:S(2)}) %collective-permute-start.9) | collective-permute-done | bytes 32800 | tf_op jit(solution)/shard_map/ppermute | solution.py:366
  23.1 0.4 shard_map.79
  23.5 1.4 %collective-permute-start.12 = (bf16[128,128]{1,0:T(8,128)(2,1)S(1)}, bf16[128,128]{1,0:T(8,128)(2,1)S(1)}, u32[]{:S(2)}, u32[]{:S(2)}) collective-permute-start(bf16[128,128]{1,0:T(8,128)(2,1)S(1)} %get-tuple-element.115), channel_id=1, source_target_pairs={{0,16},{1,17},{2,18},{3,19},{4,20},{5,6},{6,5},{7,8},{8,7},{9,25},... | collective-permute-start | bytes 98312 | tf_op jit(solution)/shard_map/ppermute | solution.py:366
  24.9 1.5 %collective-permute-start.13 = (bf16[128,128]{1,0:T(8,128)(2,1)S(1)}, bf16[128,128]{1,0:T(8,128)(2,1)S(1)}, u32[]{:S(2)}, u32[]{:S(2)}) collective-permute-start(bf16[128,128]{1,0:T(8,128)(2,1)S(1)} %get-tuple-element.116), channel_id=1, source_target_pairs={{0,5},{1,2},{2,1},{3,4},{4,3},{5,0},{6,22},{7,23},{8,24},{9,10},{1... | collective-permute-start | bytes 98312 | tf_op jit(solution)/shard_map/ppermute | solution.py:366
  26.4 0.5 collective-permute-start.15
  26.9 1.3 %shard_map.80 = (f32[128,1024]{1,0:T(8,128)S(1)}, f32[128,384]{1,0:T(8,128)S(1)}) custom-call(bf16[128,128]{1,0:T(8,128)(2,1)S(1)} %collective-permute-done.8.refs_0_, bf16[128,128]{1,0:T(8,128)(2,1)S(1)} %collective-permute-done.9.refs_1_, bf16[128,128]{1,0:T(8,128)(2,1)S(1)} %collective-permute-done.10.refs_2_, ...), custom_call_target="tpu_custom_call" | custom-call | flops 469762048 | bytes 5738496 | tf_op jit(solution)/shard_map/pallas_call | solution.py:330
  28.2 0.6 %collective-permute-done.12.refs_0_ = bf16[128,128]{1,0:T(8,128)(2,1)S(1)} collective-permute-done((bf16[128,128]{1,0:T(8,128)(2,1)S(1)}, bf16[128,128]{1,0:T(8,128)(2,1)S(1)}, u32[]{:S(2)}, u32[]{:S(2)}) %collective-permute-start.12) | collective-permute-done | bytes 32800 | tf_op jit(solution)/shard_map/ppermute | solution.py:366
  28.9 0.9 %collective-permute-done.13.refs_1_ = bf16[128,128]{1,0:T(8,128)(2,1)S(1)} collective-permute-done((bf16[128,128]{1,0:T(8,128)(2,1)S(1)}, bf16[128,128]{1,0:T(8,128)(2,1)S(1)}, u32[]{:S(2)}, u32[]{:S(2)}) %collective-permute-start.13) | collective-permute-done | bytes 32800 | tf_op jit(solution)/shard_map/ppermute | solution.py:366
  30.1 1.1 %collective-permute-start.16 = (bf16[128,128]{1,0:T(8,128)(2,1)S(1)}, bf16[128,128]{1,0:T(8,128)(2,1)S(1)}, u32[]{:S(2)}, u32[]{:S(2)}) collective-permute-start(bf16[128,128]{1,0:T(8,128)(2,1)S(1)} %get-tuple-element.124), channel_id=1, source_target_pairs={{0,16},{1,17},{2,18},{3,19},{4,20},{5,6},{6,5},{7,8},{8,7},{9,25},... | collective-permute-start | bytes 98312 | tf_op jit(solution)/shard_map/ppermute | solution.py:366
  31.2 1.8 %collective-permute-start.17 = (bf16[128,128]{1,0:T(8,128)(2,1)S(1)}, bf16[128,128]{1,0:T(8,128)(2,1)S(1)}, u32[]{:S(2)}, u32[]{:S(2)}) collective-permute-start(bf16[128,128]{1,0:T(8,128)(2,1)S(1)} %get-tuple-element.125), channel_id=1, source_target_pairs={{0,5},{1,2},{2,1},{3,4},{4,3},{5,0},{6,22},{7,23},{8,24},{9,10},{1... | collective-permute-start | bytes 98312 | tf_op jit(solution)/shard_map/ppermute | solution.py:366
  33.0 0.5 collective-permute-start.19
  33.5 1.0 %shard_map.82 = (f32[128,1024]{1,0:T(8,128)S(1)}, f32[128,1024]{1,0:T(8,128)S(1)}, f32[128,384]{1,0:T(8,128)S(1)}) custom-call(bf16[128,128]{1,0:T(8,128)(2,1)S(1)} %collective-permute-done.12.refs_0_, bf16[128,128]{1,0:T(8,128)(2,1)S(1)} %collective-permute-done.13.refs_1_, bf16[128,128]{1,0:T(8,128)(2,1)S(1)} %collective-permute-done.14.refs_2_, ...), custom_call_target="tpu_custom_call" | custom-call | flops 469762048 | bytes 5902336 | tf_op jit(solution)/shard_map/pallas_call | solution.py:330
  34.6 1.1 %collective-permute-done.16.refs_0_ = bf16[128,128]{1,0:T(8,128)(2,1)S(1)} collective-permute-done((bf16[128,128]{1,0:T(8,128)(2,1)S(1)}, bf16[128,128]{1,0:T(8,128)(2,1)S(1)}, u32[]{:S(2)}, u32[]{:S(2)}) %collective-permute-start.16) | collective-permute-done | bytes 32800 | tf_op jit(solution)/shard_map/ppermute | solution.py:366
  35.6 0.4 collective-permute-done.17.refs_1_
  36.1 0.4 shard_map.83
  36.5 1.4 %collective-permute-start.20 = (bf16[128,128]{1,0:T(8,128)(2,1)S(1)}, bf16[128,128]{1,0:T(8,128)(2,1)S(1)}, u32[]{:S(2)}, u32[]{:S(2)}) collective-permute-start(bf16[128,128]{1,0:T(8,128)(2,1)S(1)} %get-tuple-element.132), channel_id=1, source_target_pairs={{0,16},{1,17},{2,18},{3,19},{4,20},{5,6},{6,5},{7,8},{8,7},{9,25},... | collective-permute-start | bytes 98312 | tf_op jit(solution)/shard_map/ppermute | solution.py:366
  37.9 1.5 %collective-permute-start.21 = (bf16[128,128]{1,0:T(8,128)(2,1)S(1)}, bf16[128,128]{1,0:T(8,128)(2,1)S(1)}, u32[]{:S(2)}, u32[]{:S(2)}) collective-permute-start(bf16[128,128]{1,0:T(8,128)(2,1)S(1)} %get-tuple-element.133), channel_id=1, source_target_pairs={{0,5},{1,2},{2,1},{3,4},{4,3},{5,0},{6,22},{7,23},{8,24},{9,10},{1... | collective-permute-start | bytes 98312 | tf_op jit(solution)/shard_map/ppermute | solution.py:366
  39.4 0.5 collective-permute-start.23
  39.9 1.3 %shard_map.84 = (f32[128,1024]{1,0:T(8,128)S(1)}, f32[128,384]{1,0:T(8,128)S(1)}) custom-call(bf16[128,128]{1,0:T(8,128)(2,1)S(1)} %collective-permute-done.16.refs_0_, bf16[128,128]{1,0:T(8,128)(2,1)S(1)} %collective-permute-done.17.refs_1_, bf16[128,128]{1,0:T(8,128)(2,1)S(1)} %collective-permute-done.18.refs_2_, ...), custom_call_target="tpu_custom_call" | custom-call | flops 469762048 | bytes 5738496 | tf_op jit(solution)/shard_map/pallas_call | solution.py:330
  41.2 0.6 %collective-permute-done.20.refs_0_ = bf16[128,128]{1,0:T(8,128)(2,1)S(1)} collective-permute-done((bf16[128,128]{1,0:T(8,128)(2,1)S(1)}, bf16[128,128]{1,0:T(8,128)(2,1)S(1)}, u32[]{:S(2)}, u32[]{:S(2)}) %collective-permute-start.20) | collective-permute-done | bytes 32800 | tf_op jit(solution)/shard_map/ppermute | solution.py:366
  41.8 1.0 %collective-permute-done.21.refs_1_ = bf16[128,128]{1,0:T(8,128)(2,1)S(1)} collective-permute-done((bf16[128,128]{1,0:T(8,128)(2,1)S(1)}, bf16[128,128]{1,0:T(8,128)(2,1)S(1)}, u32[]{:S(2)}, u32[]{:S(2)}) %collective-permute-start.21) | collective-permute-done | bytes 32800 | tf_op jit(solution)/shard_map/ppermute | solution.py:366
  43.2 1.0 %collective-permute-start.24 = (bf16[128,128]{1,0:T(8,128)(2,1)S(1)}, bf16[128,128]{1,0:T(8,128)(2,1)S(1)}, u32[]{:S(2)}, u32[]{:S(2)}) collective-permute-start(bf16[128,128]{1,0:T(8,128)(2,1)S(1)} %get-tuple-element.140), channel_id=1, source_target_pairs={{0,16},{1,17},{2,18},{3,19},{4,20},{5,6},{6,5},{7,8},{8,7},{9,25},... | collective-permute-start | bytes 98312 | tf_op jit(solution)/shard_map/ppermute | solution.py:366
  44.2 1.8 %collective-permute-start.25 = (bf16[128,128]{1,0:T(8,128)(2,1)S(1)}, bf16[128,128]{1,0:T(8,128)(2,1)S(1)}, u32[]{:S(2)}, u32[]{:S(2)}) collective-permute-start(bf16[128,128]{1,0:T(8,128)(2,1)S(1)} %get-tuple-element.141), channel_id=1, source_target_pairs={{0,5},{1,2},{2,1},{3,4},{4,3},{5,0},{6,22},{7,23},{8,24},{9,10},{1... | collective-permute-start | bytes 98312 | tf_op jit(solution)/shard_map/ppermute | solution.py:366
  46.0 0.5 collective-permute-start.27
  46.5 1.0 %shard_map.86 = (f32[128,1024]{1,0:T(8,128)S(1)}, f32[128,1024]{1,0:T(8,128)S(1)}, f32[128,384]{1,0:T(8,128)S(1)}) custom-call(bf16[128,128]{1,0:T(8,128)(2,1)S(1)} %collective-permute-done.20.refs_0_, bf16[128,128]{1,0:T(8,128)(2,1)S(1)} %collective-permute-done.21.refs_1_, bf16[128,128]{1,0:T(8,128)(2,1)S(1)} %collective-permute-done.22.refs_2_, ...), custom_call_target="tpu_custom_call" | custom-call | flops 469762048 | bytes 5902336 | tf_op jit(solution)/shard_map/pallas_call | solution.py:330
  47.5 0.9 %collective-permute-done.24.refs_0_ = bf16[128,128]{1,0:T(8,128)(2,1)S(1)} collective-permute-done((bf16[128,128]{1,0:T(8,128)(2,1)S(1)}, bf16[128,128]{1,0:T(8,128)(2,1)S(1)}, u32[]{:S(2)}, u32[]{:S(2)}) %collective-permute-start.24) | collective-permute-done | bytes 32800 | tf_op jit(solution)/shard_map/ppermute | solution.py:366
  48.4 0.6 %collective-permute-done.25.refs_1_ = bf16[128,128]{1,0:T(8,128)(2,1)S(1)} collective-permute-done((bf16[128,128]{1,0:T(8,128)(2,1)S(1)}, bf16[128,128]{1,0:T(8,128)(2,1)S(1)}, u32[]{:S(2)}, u32[]{:S(2)}) %collective-permute-start.25) | collective-permute-done | bytes 32800 | tf_op jit(solution)/shard_map/ppermute | solution.py:366
  49.5 1.5 %collective-permute-start.28 = (bf16[128,128]{1,0:T(8,128)(2,1)S(1)}, bf16[128,128]{1,0:T(8,128)(2,1)S(1)}, u32[]{:S(2)}, u32[]{:S(2)}) collective-permute-start(bf16[128,128]{1,0:T(8,128)(2,1)S(1)} %get-tuple-element.147), channel_id=1, source_target_pairs={{0,16},{1,17},{2,18},{3,19},{4,20},{5,6},{6,5},{7,8},{8,7},{9,25},... | collective-permute-start | bytes 98312 | tf_op jit(solution)/shard_map/ppermute | solution.py:366
  50.9 1.4 %collective-permute-start.29 = (bf16[128,128]{1,0:T(8,128)(2,1)S(1)}, bf16[128,128]{1,0:T(8,128)(2,1)S(1)}, u32[]{:S(2)}, u32[]{:S(2)}) collective-permute-start(bf16[128,128]{1,0:T(8,128)(2,1)S(1)} %get-tuple-element.148), channel_id=1, source_target_pairs={{0,5},{1,2},{2,1},{3,4},{4,3},{5,0},{6,22},{7,23},{8,24},{9,10},{1... | collective-permute-start | bytes 98312 | tf_op jit(solution)/shard_map/ppermute | solution.py:366
  52.4 0.5 collective-permute-start.31
  52.9 1.2 %shard_map.88.refs_5_ = f32[1024,128]{1,0:T(8,128)S(1)} custom-call(bf16[128,128]{1,0:T(8,128)(2,1)S(1)} %collective-permute-done.24.refs_0_, bf16[128,128]{1,0:T(8,128)(2,1)S(1)} %collective-permute-done.25.refs_1_, bf16[128,128]{1,0:T(8,128)(2,1)S(1)} %collective-permute-done.26.refs_2_, bf16[128,128]{1,0:T(8,128)(2,1)S(1)} %collective-permute-done.27.refs_3_, ...), custom_call_target="tpu_custom_call" | custom-call | flops 369098752 | bytes 4624384 | tf_op jit(solution)/shard_map/pallas_call | solution.py:330
  54.1 0.6 collective-permute-done.28.refs_0_
  54.7 1.1 %collective-permute-done.29.refs_1_ = bf16[128,128]{1,0:T(8,128)(2,1)S(1)} collective-permute-done((bf16[128,128]{1,0:T(8,128)(2,1)S(1)}, bf16[128,128]{1,0:T(8,128)(2,1)S(1)}, u32[]{:S(2)}, u32[]{:S(2)}) %collective-permute-start.29) | collective-permute-done | bytes 32800 | tf_op jit(solution)/shard_map/ppermute | solution.py:366
  55.8 1.1 %shard_map.89 = f32[1,1024,128]{2,1,0:T(8,128)} custom-call(bf16[128,128]{1,0:T(8,128)(2,1)S(1)} %collective-permute-done.28.refs_0_, bf16[128,128]{1,0:T(8,128)(2,1)S(1)} %collective-permute-done.29.refs_1_, bf16[128,128]{1,0:T(8,128)(2,1)S(1)} %collective-permute-done.30.refs_2_, bf16[128,128]{1,0:T(8,128)(2,1)S(1)} %collective-permute-done.31.refs_3_, ...), custom_call_target="tpu_custom_call" | custom-call | flops 100663296 | bytes 1966080 | tf_op jit(solution)/shard_map/pallas_call | solution.py:330
  (33 shorter events, 2.6 us)
Async XLA Ops:
  1.5 8.1 %collective-permute-start = (bf16[128,128]{1,0:T(8,128)(2,1)S(1)}, bf16[128,128]{1,0:T(8,128)(2,1)S(1)}, u32[]{:S(2)}, u32[]{:S(2)}) collective-permute-start(bf16[128,128]{1,0:T(8,128)(2,1)S(1)} %get-tuple-element.79), channel_id=1, source_target_pairs={{0,16},{1,17},{2,18},{3,19},{4,20},{5,6},{6,5},{7,8},{8,7},{9,25},... | collective-permute-start | bytes 98312 | tf_op jit(solution)/shard_map/ppermute | solution.py:366
  3.3 6.3 %collective-permute-start.1 = (bf16[128,128]{1,0:T(8,128)(2,1)S(1)}, bf16[128,128]{1,0:T(8,128)(2,1)S(1)}, u32[]{:S(2)}, u32[]{:S(2)}) collective-permute-start(bf16[128,128]{1,0:T(8,128)(2,1)S(1)} %get-tuple-element.80), channel_id=1, source_target_pairs={{0,5},{1,2},{2,1},{3,4},{4,3},{5,0},{6,22},{7,23},{8,24},{9,10},{1... | collective-permute-start | bytes 98312 | tf_op jit(solution)/shard_map/ppermute | solution.py:366
  5.9 3.7 %collective-permute-start.2 = (bf16[128,128]{1,0:T(8,128)(2,1)S(1)}, bf16[128,128]{1,0:T(8,128)(2,1)S(1)}, u32[]{:S(2)}, u32[]{:S(2)}) collective-permute-start(bf16[128,128]{1,0:T(8,128)(2,1)S(1)} %get-tuple-element.81), channel_id=1, source_target_pairs={{0,1},{1,0},{2,3},{3,2},{4,12},{5,21},{6,7},{7,6},{8,9},{9,8},{10,... | collective-permute-start | bytes 98312 | tf_op jit(solution)/shard_map/ppermute | solution.py:366
  5.9 3.7 %collective-permute-start.3 = (bf16[128,128]{1,0:T(8,128)(2,1)S(1)}, bf16[128,128]{1,0:T(8,128)(2,1)S(1)}, u32[]{:S(2)}, u32[]{:S(2)}) collective-permute-start(bf16[128,128]{1,0:T(8,128)(2,1)S(1)} %get-tuple-element.82), channel_id=1, source_target_pairs={{0,1},{1,0},{2,3},{3,2},{4,5},{5,4},{6,7},{7,6},{8,9},{9,8},{10,11... | collective-permute-start | bytes 98312 | tf_op jit(solution)/shard_map/ppermute | solution.py:366
  10.0 5.3 %collective-permute-start.4 = (bf16[128,128]{1,0:T(8,128)(2,1)S(1)}, bf16[128,128]{1,0:T(8,128)(2,1)S(1)}, u32[]{:S(2)}, u32[]{:S(2)}) collective-permute-start(bf16[128,128]{1,0:T(8,128)(2,1)S(1)} %get-tuple-element.93), channel_id=1, source_target_pairs={{0,16},{1,17},{2,18},{3,19},{4,20},{5,6},{6,5},{7,8},{8,7},{9,25},... | collective-permute-start | bytes 98312 | tf_op jit(solution)/shard_map/ppermute | solution.py:366
  11.6 4.8 %collective-permute-start.5 = (bf16[128,128]{1,0:T(8,128)(2,1)S(1)}, bf16[128,128]{1,0:T(8,128)(2,1)S(1)}, u32[]{:S(2)}, u32[]{:S(2)}) collective-permute-start(bf16[128,128]{1,0:T(8,128)(2,1)S(1)} %get-tuple-element.94), channel_id=1, source_target_pairs={{0,5},{1,2},{2,1},{3,4},{4,3},{5,0},{6,22},{7,23},{8,24},{9,10},{1... | collective-permute-start | bytes 98312 | tf_op jit(solution)/shard_map/ppermute | solution.py:366
  11.9 4.5 %collective-permute-start.6 = (bf16[128,128]{1,0:T(8,128)(2,1)S(1)}, bf16[128,128]{1,0:T(8,128)(2,1)S(1)}, u32[]{:S(2)}, u32[]{:S(2)}) collective-permute-start(bf16[128,128]{1,0:T(8,128)(2,1)S(1)} %get-tuple-element.95), channel_id=1, source_target_pairs={{0,1},{1,0},{2,3},{3,2},{4,12},{5,21},{6,7},{7,6},{8,9},{9,8},{10,... | collective-permute-start | bytes 98312 | tf_op jit(solution)/shard_map/ppermute | solution.py:366
  11.9 4.5 %collective-permute-start.7 = (bf16[128,128]{1,0:T(8,128)(2,1)S(1)}, bf16[128,128]{1,0:T(8,128)(2,1)S(1)}, u32[]{:S(2)}, u32[]{:S(2)}) collective-permute-start(bf16[128,128]{1,0:T(8,128)(2,1)S(1)} %get-tuple-element.96), channel_id=1, source_target_pairs={{0,1},{1,0},{2,3},{3,2},{4,5},{5,4},{6,7},{7,6},{8,9},{9,8},{10,11... | collective-permute-start | bytes 98312 | tf_op jit(solution)/shard_map/ppermute | solution.py:366
  16.8 5.2 %collective-permute-start.8 = (bf16[128,128]{1,0:T(8,128)(2,1)S(1)}, bf16[128,128]{1,0:T(8,128)(2,1)S(1)}, u32[]{:S(2)}, u32[]{:S(2)}) collective-permute-start(bf16[128,128]{1,0:T(8,128)(2,1)S(1)} %get-tuple-element.106), channel_id=1, source_target_pairs={{0,16},{1,17},{2,18},{3,19},{4,20},{5,6},{6,5},{7,8},{8,7},{9,25},... | collective-permute-start | bytes 98312 | tf_op jit(solution)/shard_map/ppermute | solution.py:366
  18.3 4.8 %collective-permute-start.9 = (bf16[128,128]{1,0:T(8,128)(2,1)S(1)}, bf16[128,128]{1,0:T(8,128)(2,1)S(1)}, u32[]{:S(2)}, u32[]{:S(2)}) collective-permute-start(bf16[128,128]{1,0:T(8,128)(2,1)S(1)} %get-tuple-element.107), channel_id=1, source_target_pairs={{0,5},{1,2},{2,1},{3,4},{4,3},{5,0},{6,22},{7,23},{8,24},{9,10},{1... | collective-permute-start | bytes 98312 | tf_op jit(solution)/shard_map/ppermute | solution.py:366
  20.1 3.0 %collective-permute-start.10 = (bf16[128,128]{1,0:T(8,128)(2,1)S(1)}, bf16[128,128]{1,0:T(8,128)(2,1)S(1)}, u32[]{:S(2)}, u32[]{:S(2)}) collective-permute-start(bf16[128,128]{1,0:T(8,128)(2,1)S(1)} %get-tuple-element.108), channel_id=1, source_target_pairs={{0,1},{1,0},{2,3},{3,2},{4,12},{5,21},{6,7},{7,6},{8,9},{9,8},{10,... | collective-permute-start | bytes 98312 | tf_op jit(solution)/shard_map/ppermute | solution.py:366
  20.1 3.0 %collective-permute-start.11 = (bf16[128,128]{1,0:T(8,128)(2,1)S(1)}, bf16[128,128]{1,0:T(8,128)(2,1)S(1)}, u32[]{:S(2)}, u32[]{:S(2)}) collective-permute-start(bf16[128,128]{1,0:T(8,128)(2,1)S(1)} %get-tuple-element.109), channel_id=1, source_target_pairs={{0,1},{1,0},{2,3},{3,2},{4,5},{5,4},{6,7},{7,6},{8,9},{9,8},{10,11... | collective-permute-start | bytes 98312 | tf_op jit(solution)/shard_map/ppermute | solution.py:366
  23.5 5.4 %collective-permute-start.12 = (bf16[128,128]{1,0:T(8,128)(2,1)S(1)}, bf16[128,128]{1,0:T(8,128)(2,1)S(1)}, u32[]{:S(2)}, u32[]{:S(2)}) collective-permute-start(bf16[128,128]{1,0:T(8,128)(2,1)S(1)} %get-tuple-element.115), channel_id=1, source_target_pairs={{0,16},{1,17},{2,18},{3,19},{4,20},{5,6},{6,5},{7,8},{8,7},{9,25},... | collective-permute-start | bytes 98312 | tf_op jit(solution)/shard_map/ppermute | solution.py:366
  24.9 4.8 %collective-permute-start.13 = (bf16[128,128]{1,0:T(8,128)(2,1)S(1)}, bf16[128,128]{1,0:T(8,128)(2,1)S(1)}, u32[]{:S(2)}, u32[]{:S(2)}) collective-permute-start(bf16[128,128]{1,0:T(8,128)(2,1)S(1)} %get-tuple-element.116), channel_id=1, source_target_pairs={{0,5},{1,2},{2,1},{3,4},{4,3},{5,0},{6,22},{7,23},{8,24},{9,10},{1... | collective-permute-start | bytes 98312 | tf_op jit(solution)/shard_map/ppermute | solution.py:366
  26.4 3.3 %collective-permute-start.14 = (bf16[128,128]{1,0:T(8,128)(2,1)S(1)}, bf16[128,128]{1,0:T(8,128)(2,1)S(1)}, u32[]{:S(2)}, u32[]{:S(2)}) collective-permute-start(bf16[128,128]{1,0:T(8,128)(2,1)S(1)} %get-tuple-element.117), channel_id=1, source_target_pairs={{0,1},{1,0},{2,3},{3,2},{4,12},{5,21},{6,7},{7,6},{8,9},{9,8},{10,... | collective-permute-start | bytes 98312 | tf_op jit(solution)/shard_map/ppermute | solution.py:366
  26.4 3.3 %collective-permute-start.15 = (bf16[128,128]{1,0:T(8,128)(2,1)S(1)}, bf16[128,128]{1,0:T(8,128)(2,1)S(1)}, u32[]{:S(2)}, u32[]{:S(2)}) collective-permute-start(bf16[128,128]{1,0:T(8,128)(2,1)S(1)} %get-tuple-element.118), channel_id=1, source_target_pairs={{0,1},{1,0},{2,3},{3,2},{4,5},{5,4},{6,7},{7,6},{8,9},{9,8},{10,11... | collective-permute-start | bytes 98312 | tf_op jit(solution)/shard_map/ppermute | solution.py:366
  30.1 5.5 %collective-permute-start.16 = (bf16[128,128]{1,0:T(8,128)(2,1)S(1)}, bf16[128,128]{1,0:T(8,128)(2,1)S(1)}, u32[]{:S(2)}, u32[]{:S(2)}) collective-permute-start(bf16[128,128]{1,0:T(8,128)(2,1)S(1)} %get-tuple-element.124), channel_id=1, source_target_pairs={{0,16},{1,17},{2,18},{3,19},{4,20},{5,6},{6,5},{7,8},{8,7},{9,25},... | collective-permute-start | bytes 98312 | tf_op jit(solution)/shard_map/ppermute | solution.py:366
  31.2 4.8 %collective-permute-start.17 = (bf16[128,128]{1,0:T(8,128)(2,1)S(1)}, bf16[128,128]{1,0:T(8,128)(2,1)S(1)}, u32[]{:S(2)}, u32[]{:S(2)}) collective-permute-start(bf16[128,128]{1,0:T(8,128)(2,1)S(1)} %get-tuple-element.125), channel_id=1, source_target_pairs={{0,5},{1,2},{2,1},{3,4},{4,3},{5,0},{6,22},{7,23},{8,24},{9,10},{1... | collective-permute-start | bytes 98312 | tf_op jit(solution)/shard_map/ppermute | solution.py:366
  33.0 3.0 %collective-permute-start.18 = (bf16[128,128]{1,0:T(8,128)(2,1)S(1)}, bf16[128,128]{1,0:T(8,128)(2,1)S(1)}, u32[]{:S(2)}, u32[]{:S(2)}) collective-permute-start(bf16[128,128]{1,0:T(8,128)(2,1)S(1)} %get-tuple-element.126), channel_id=1, source_target_pairs={{0,1},{1,0},{2,3},{3,2},{4,12},{5,21},{6,7},{7,6},{8,9},{9,8},{10,... | collective-permute-start | bytes 98312 | tf_op jit(solution)/shard_map/ppermute | solution.py:366
  33.0 3.0 %collective-permute-start.19 = (bf16[128,128]{1,0:T(8,128)(2,1)S(1)}, bf16[128,128]{1,0:T(8,128)(2,1)S(1)}, u32[]{:S(2)}, u32[]{:S(2)}) collective-permute-start(bf16[128,128]{1,0:T(8,128)(2,1)S(1)} %get-tuple-element.127), channel_id=1, source_target_pairs={{0,1},{1,0},{2,3},{3,2},{4,5},{5,4},{6,7},{7,6},{8,9},{9,8},{10,11... | collective-permute-start | bytes 98312 | tf_op jit(solution)/shard_map/ppermute | solution.py:366
  36.5 5.3 %collective-permute-start.20 = (bf16[128,128]{1,0:T(8,128)(2,1)S(1)}, bf16[128,128]{1,0:T(8,128)(2,1)S(1)}, u32[]{:S(2)}, u32[]{:S(2)}) collective-permute-start(bf16[128,128]{1,0:T(8,128)(2,1)S(1)} %get-tuple-element.132), channel_id=1, source_target_pairs={{0,16},{1,17},{2,18},{3,19},{4,20},{5,6},{6,5},{7,8},{8,7},{9,25},... | collective-permute-start | bytes 98312 | tf_op jit(solution)/shard_map/ppermute | solution.py:366
  37.9 4.9 %collective-permute-start.21 = (bf16[128,128]{1,0:T(8,128)(2,1)S(1)}, bf16[128,128]{1,0:T(8,128)(2,1)S(1)}, u32[]{:S(2)}, u32[]{:S(2)}) collective-permute-start(bf16[128,128]{1,0:T(8,128)(2,1)S(1)} %get-tuple-element.133), channel_id=1, source_target_pairs={{0,5},{1,2},{2,1},{3,4},{4,3},{5,0},{6,22},{7,23},{8,24},{9,10},{1... | collective-permute-start | bytes 98312 | tf_op jit(solution)/shard_map/ppermute | solution.py:366
  39.4 3.4 %collective-permute-start.22 = (bf16[128,128]{1,0:T(8,128)(2,1)S(1)}, bf16[128,128]{1,0:T(8,128)(2,1)S(1)}, u32[]{:S(2)}, u32[]{:S(2)}) collective-permute-start(bf16[128,128]{1,0:T(8,128)(2,1)S(1)} %get-tuple-element.134), channel_id=1, source_target_pairs={{0,1},{1,0},{2,3},{3,2},{4,12},{5,21},{6,7},{7,6},{8,9},{9,8},{10,... | collective-permute-start | bytes 98312 | tf_op jit(solution)/shard_map/ppermute | solution.py:366
  39.4 3.4 %collective-permute-start.23 = (bf16[128,128]{1,0:T(8,128)(2,1)S(1)}, bf16[128,128]{1,0:T(8,128)(2,1)S(1)}, u32[]{:S(2)}, u32[]{:S(2)}) collective-permute-start(bf16[128,128]{1,0:T(8,128)(2,1)S(1)} %get-tuple-element.135), channel_id=1, source_target_pairs={{0,1},{1,0},{2,3},{3,2},{4,5},{5,4},{6,7},{7,6},{8,9},{9,8},{10,11... | collective-permute-start | bytes 98312 | tf_op jit(solution)/shard_map/ppermute | solution.py:366
  43.2 5.2 %collective-permute-start.24 = (bf16[128,128]{1,0:T(8,128)(2,1)S(1)}, bf16[128,128]{1,0:T(8,128)(2,1)S(1)}, u32[]{:S(2)}, u32[]{:S(2)}) collective-permute-start(bf16[128,128]{1,0:T(8,128)(2,1)S(1)} %get-tuple-element.140), channel_id=1, source_target_pairs={{0,16},{1,17},{2,18},{3,19},{4,20},{5,6},{6,5},{7,8},{8,7},{9,25},... | collective-permute-start | bytes 98312 | tf_op jit(solution)/shard_map/ppermute | solution.py:366
  44.2 4.8 %collective-permute-start.25 = (bf16[128,128]{1,0:T(8,128)(2,1)S(1)}, bf16[128,128]{1,0:T(8,128)(2,1)S(1)}, u32[]{:S(2)}, u32[]{:S(2)}) collective-permute-start(bf16[128,128]{1,0:T(8,128)(2,1)S(1)} %get-tuple-element.141), channel_id=1, source_target_pairs={{0,5},{1,2},{2,1},{3,4},{4,3},{5,0},{6,22},{7,23},{8,24},{9,10},{1... | collective-permute-start | bytes 98312 | tf_op jit(solution)/shard_map/ppermute | solution.py:366
  46.0 3.0 %collective-permute-start.26 = (bf16[128,128]{1,0:T(8,128)(2,1)S(1)}, bf16[128,128]{1,0:T(8,128)(2,1)S(1)}, u32[]{:S(2)}, u32[]{:S(2)}) collective-permute-start(bf16[128,128]{1,0:T(8,128)(2,1)S(1)} %get-tuple-element.142), channel_id=1, source_target_pairs={{0,1},{1,0},{2,3},{3,2},{4,12},{5,21},{6,7},{7,6},{8,9},{9,8},{10,... | collective-permute-start | bytes 98312 | tf_op jit(solution)/shard_map/ppermute | solution.py:366
  46.0 3.0 %collective-permute-start.27 = (bf16[128,128]{1,0:T(8,128)(2,1)S(1)}, bf16[128,128]{1,0:T(8,128)(2,1)S(1)}, u32[]{:S(2)}, u32[]{:S(2)}) collective-permute-start(bf16[128,128]{1,0:T(8,128)(2,1)S(1)} %get-tuple-element.143), channel_id=1, source_target_pairs={{0,1},{1,0},{2,3},{3,2},{4,5},{5,4},{6,7},{7,6},{8,9},{9,8},{10,11... | collective-permute-start | bytes 98312 | tf_op jit(solution)/shard_map/ppermute | solution.py:366
  49.5 5.2 %collective-permute-start.28 = (bf16[128,128]{1,0:T(8,128)(2,1)S(1)}, bf16[128,128]{1,0:T(8,128)(2,1)S(1)}, u32[]{:S(2)}, u32[]{:S(2)}) collective-permute-start(bf16[128,128]{1,0:T(8,128)(2,1)S(1)} %get-tuple-element.147), channel_id=1, source_target_pairs={{0,16},{1,17},{2,18},{3,19},{4,20},{5,6},{6,5},{7,8},{8,7},{9,25},... | collective-permute-start | bytes 98312 | tf_op jit(solution)/shard_map/ppermute | solution.py:366
  50.9 4.8 %collective-permute-start.29 = (bf16[128,128]{1,0:T(8,128)(2,1)S(1)}, bf16[128,128]{1,0:T(8,128)(2,1)S(1)}, u32[]{:S(2)}, u32[]{:S(2)}) collective-permute-start(bf16[128,128]{1,0:T(8,128)(2,1)S(1)} %get-tuple-element.148), channel_id=1, source_target_pairs={{0,5},{1,2},{2,1},{3,4},{4,3},{5,0},{6,22},{7,23},{8,24},{9,10},{1... | collective-permute-start | bytes 98312 | tf_op jit(solution)/shard_map/ppermute | solution.py:366
  52.4 3.4 %collective-permute-start.30 = (bf16[128,128]{1,0:T(8,128)(2,1)S(1)}, bf16[128,128]{1,0:T(8,128)(2,1)S(1)}, u32[]{:S(2)}, u32[]{:S(2)}) collective-permute-start(bf16[128,128]{1,0:T(8,128)(2,1)S(1)} %get-tuple-element.149), channel_id=1, source_target_pairs={{0,1},{1,0},{2,3},{3,2},{4,12},{5,21},{6,7},{7,6},{8,9},{9,8},{10,... | collective-permute-start | bytes 98312 | tf_op jit(solution)/shard_map/ppermute | solution.py:366
  52.4 3.4 %collective-permute-start.31 = (bf16[128,128]{1,0:T(8,128)(2,1)S(1)}, bf16[128,128]{1,0:T(8,128)(2,1)S(1)}, u32[]{:S(2)}, u32[]{:S(2)}) collective-permute-start(bf16[128,128]{1,0:T(8,128)(2,1)S(1)} %get-tuple-element.150), channel_id=1, source_target_pairs={{0,1},{1,0},{2,3},{3,2},{4,5},{5,4},{6,7},{7,6},{8,9},{9,8},{10,11... | collective-permute-start | bytes 98312 | tf_op jit(solution)/shard_map/ppermute | solution.py:366

commit v17 on v15

--- a/solution.py
+++ b/solution.py
@@ -128,6 +128,7 @@
     turned_ref,
     picked_ref,
     list_ref,
+    chosen_ref,
     weight_ref,
     n_ref,
     *refs,
@@ -158,17 +159,29 @@
     copies[2].wait()
     turned = rhs_ref[0].T
     turned_ref[...] = turned
-    picked = times(turned, hot_ref[...]).astype(BF16)
+    copies[3].wait()
+    weight = weight_ref[...]
+    high = weight.astype(BF16).astype(F32)
+    middle = (weight - high).astype(BF16).astype(F32)
+    low = weight - high - middle
+    level = lax.broadcasted_iota(jnp.int32, (16, width), 0)
+    pieces = jnp.where(level == 0, high, jnp.where(level == 1, middle, jnp.where(level == 2, low, 0.0)))
+    rest = jnp.zeros((turned.shape[0] - 16, width), BF16)
+    product = times(jnp.concatenate([turned, pieces.astype(BF16), rest], 0), hot_ref[...])
+    leads = turned.shape[0]
+    picked = product[:leads].astype(BF16)
+    pieces = product[leads : leads + 8]
+    chosen_ref[...] = jnp.broadcast_to((pieces[0:1] + pieces[1:2]) + pieces[2:3], chosen_ref.shape)
     picked_ref[...] = picked
     scatter(links, plan_out, out_refs, picked)
-    for copy in copies[3:]:
-        copy.wait()
+    copies[4].wait()
 
 
 def pick_n_kernel(
     hot_ref,
     turned_ref,
     list_ref,
+    chosen_ref,
     n_ref,
     weight_ref,
     count_ref,
@@ -213,13 +226,7 @@
     earlier = lax.broadcasted_iota(jnp.int32, same.shape, 0) < lax.broadcasted_iota(jnp.int32, same.shape, 1)
     repeats = jnp.sum(jnp.where(earlier, same, 0.0), 0, keepdims=True)
     first = jnp.where(repeats > 0.0, 0.0, 1.0)
-    high = weight.astype(BF16).astype(F32)
-    middle = (weight - high).astype(BF16).astype(F32)
-    low = weight - high - middle
-    level = lax.broadcasted_iota(jnp.int32, (8, width), 0)
-    pieces = jnp.where(level == 0, high, jnp.where(level == 1, middle, jnp.where(level == 2, low, 0.0)))
-    pieces = times(pieces.astype(BF16), hot)
-    chosen = (pieces[0:1] + pieces[1:2]) + pieces[2:3]
+    chosen = chosen_ref[:1]
     row_ref[0:1] = chosen
     row_ref[1:2] = chosen * first
     row_ref[2:3] = first
@@ -369,13 +376,14 @@
     def bound(kernel, *settings):
         return functools.partial(kernel, trips, links, *settings)
 
-    hot, turned, picked, listed, weight, n_mat, *sent = run(
+    hot, turned, picked, listed, chosen, weight, n_mat, *sent = run(
         bound(open_kernel, plans[0], subs),
         [shared_rows, neighbours, right_side, weights, neumann],
         [
             array(width, total, BF16),
             array(leads, width, BF16),
             array(leads, total, BF16),
+            array(8, total),
             array(8, total),
             same_as(weights),
             same_as(neumann),
@@ -393,7 +401,7 @@
     arrived = exchange(sent, plans[0])
     hot_t, n_pick, n_small, same, inner, mask, local, base, rows, s_mat = run(
         pick_n_kernel,
-        [hot, turned, listed, n_mat, weight, counts, schur],
+        [hot, turned, listed, chosen, n_mat, weight, counts, schur],
         [
             array(total, width, BF16),
             array(total, width, BF16),
@@ -407,7 +415,7 @@
             same_as(schur),
         ],
         2 * total * width * width + 2 * total * total * width + picks,
-        spaces={5: pltpu.SMEM, 6: pltpu.HBM},
+        spaces={6: pltpu.SMEM, 7: pltpu.HBM},
         scratch=[pltpu.SemaphoreType.DMA],
     )
     near = picked

time: 56.8 us -> 58.5 us (1.030)
  Pallas kernels: 17.1 us -> 18.4 us
    pallas_call x17, Pallas kernels: 17.1 us -> 18.4 us  [run(): pl.pallas_call(kernel, out_shape=results, in_specs=[pl.BlockSpec(memory_s...]
  transfers between devices with their start and end apart: 32 -> 32, of which waited for: 13 -> 12; matrix products, arithmetic and copies ran while one was open for 0% -> 0% of each run, Pallas kernels for 20% -> 22%
where the time goes in v17:
time: 58.5 us; the launch traced here: 58.3 us
  starting transfers between devices  29.1 us (50%)
  Pallas kernels  18.4 us (31%)
  waiting for transfers between devices  9.93 us (17%)
  between operations  0.84 us (1%)
    ppermute x32, starting transfers between devices, exchange(): lax.ppermute(part, 'sub', route)  29.1 us
    pallas_call x17, Pallas kernels, run(): pl.pallas_call(kernel, out_shape=results, in_specs=[pl.BlockSpec(memory_s...  18.4 us
    ppermute x32, waiting for transfers between devices, exchange(): lax.ppermute(part, 'sub', route)  9.93 us
  transfers between devices with their start and end apart: 32, of which 12 were waited for; matrix products, arithmetic and copies ran while one was open for 0% of the time, Pallas kernels for 22%

profile of v17, /device:TPU:8, one launch (start us, length us, event | category | flops | bytes accessed | tf_op | source)
XLA Modules:
  0.0 58.3 jit_solution(16375757230994747092)
XLA Ops:
  0.0 1.8 %shard_map.73 = (bf16[1024,384]{1,0:T(8,128)(2,1)S(1)}, bf16[128,1024]{1,0:T(8,128)(2,1)S(1)}, bf16[128,384]{1,0:T(8,128)(2,1)S(1)}, f32[8,384]{1,0:T(8,128)S(1)...) custom-call(s32[1,4,128]{2,1,0:T(4,128)} %rows_in.1, ...), custom_call_target="tpu_custom_call" | custom-call | flops 100663296 | bytes 5769232 | tf_op jit(solution)/shard_map/pallas_call | solution.py:339
  1.8 2.7 %collective-permute-start = (bf16[128,128]{1,0:T(8,128)(2,1)S(1)}, bf16[128,128]{1,0:T(8,128)(2,1)S(1)}, u32[]{:S(2)}, u32[]{:S(2)}) collective-permute-start(bf16[128,128]{1,0:T(8,128)(2,1)S(1)} %get-tuple-element.79), channel_id=1, source_target_pairs={{0,16},{1,2},{2,1},{3,19},{4,5},{5,4},{6,15},{7,23},{8,24},{9,25},... | collective-permute-start | bytes 98312 | tf_op jit(solution)/shard_map/ppermute | solution.py:374
  4.4 1.5 %collective-permute-start.1 = (bf16[128,128]{1,0:T(8,128)(2,1)S(1)}, bf16[128,128]{1,0:T(8,128)(2,1)S(1)}, u32[]{:S(2)}, u32[]{:S(2)}) collective-permute-start(bf16[128,128]{1,0:T(8,128)(2,1)S(1)} %get-tuple-element.80), channel_id=1, source_target_pairs={{0,2},{1,17},{2,0},{3,4},{4,3},{5,6},{6,5},{7,8},{8,7},{9,10},{10,... | collective-permute-start | bytes 98312 | tf_op jit(solution)/shard_map/ppermute | solution.py:374
  6.0 0.4 collective-permute-start.3
  7.1 3.4 %shard_map.74 = (bf16[384,1024]{1,0:T(8,128)(2,1)S(1)}, bf16[384,1024]{1,0:T(8,128)(2,1)S(1)}, bf16[384,384]{1,0:T(8,128)(2,1)S(1)}, bf16[384,384]{1,0:T(8,128)(...) custom-call(bf16[1024,384]{1,0:T(8,128)(2,1)S(1)} %get-tuple-element, ...), custom_call_target="tpu_custom_call" | custom-call | flops 1207959552 | bytes 10330116 | tf_op jit(solution)/shard_map/pallas_call | solution.py:339
  10.6 0.4 shard_map.75
  11.0 0.8 %collective-permute-start.4 = (bf16[128,128]{1,0:T(8,128)(2,1)S(1)}, bf16[128,128]{1,0:T(8,128)(2,1)S(1)}, u32[]{:S(2)}, u32[]{:S(2)}) collective-permute-start(bf16[128,128]{1,0:T(8,128)(2,1)S(1)} %get-tuple-element.94), channel_id=1, source_target_pairs={{0,16},{1,2},{2,1},{3,19},{4,5},{5,4},{6,15},{7,23},{8,24},{9,25},... | collective-permute-start | bytes 98312 | tf_op jit(solution)/shard_map/ppermute | solution.py:374
  11.8 0.9 %collective-permute-start.5 = (bf16[128,128]{1,0:T(8,128)(2,1)S(1)}, bf16[128,128]{1,0:T(8,128)(2,1)S(1)}, u32[]{:S(2)}, u32[]{:S(2)}) collective-permute-start(bf16[128,128]{1,0:T(8,128)(2,1)S(1)} %get-tuple-element.95), channel_id=1, source_target_pairs={{0,2},{1,17},{2,0},{3,4},{4,3},{5,6},{6,5},{7,8},{8,7},{9,10},{10,... | collective-permute-start | bytes 98312 | tf_op jit(solution)/shard_map/ppermute | solution.py:374
  12.7 0.5 collective-permute-start.6
  13.2 2.7 %shard_map.76 = (f32[128,1024]{1,0:T(8,128)S(1)}, f32[128,384]{1,0:T(8,128)S(1)}, bf16[1024,384]{1,0:T(8,128)(2,1)S(1)}, bf16[384,384]{1,0:T(8,128)(2,1)S(1)}) custom-call(bf16[128,128]{1,0:T(8,128)(2,1)S(1)} %collective-permute-done.refs_0_, bf16[128,128]{1,0:T(8,128)(2,1)S(1)} %collective-permute-done.1.refs_1_, ...), custom_call_target="tpu_custom_call" | custom-call | flops 1577058304 | bytes 8392704 | tf_op jit(solution)/shard_map/pallas_call | solution.py:339
  15.9 1.0 %collective-permute-done.5.refs_1_ = bf16[128,128]{1,0:T(8,128)(2,1)S(1)} collective-permute-done((bf16[128,128]{1,0:T(8,128)(2,1)S(1)}, bf16[128,128]{1,0:T(8,128)(2,1)S(1)}, u32[]{:S(2)}, u32[]{:S(2)}) %collective-permute-start.5) | collective-permute-done | bytes 32800 | tf_op jit(solution)/shard_map/ppermute | solution.py:374
  17.4 1.6 %collective-permute-start.8 = (bf16[128,128]{1,0:T(8,128)(2,1)S(1)}, bf16[128,128]{1,0:T(8,128)(2,1)S(1)}, u32[]{:S(2)}, u32[]{:S(2)}) collective-permute-start(bf16[128,128]{1,0:T(8,128)(2,1)S(1)} %get-tuple-element.106), channel_id=1, source_target_pairs={{0,16},{1,2},{2,1},{3,19},{4,20},{5,21},{6,22},{7,8},{8,7},{9,10},... | collective-permute-start | bytes 98312 | tf_op jit(solution)/shard_map/ppermute | solution.py:374
  19.0 2.1 %collective-permute-start.9 = (bf16[128,128]{1,0:T(8,128)(2,1)S(1)}, bf16[128,128]{1,0:T(8,128)(2,1)S(1)}, u32[]{:S(2)}, u32[]{:S(2)}) collective-permute-start(bf16[128,128]{1,0:T(8,128)(2,1)S(1)} %get-tuple-element.107), channel_id=1, source_target_pairs={{0,3},{1,17},{2,18},{3,0},{4,13},{5,6},{6,5},{7,23},{8,24},{9,25},... | collective-permute-start | bytes 98312 | tf_op jit(solution)/shard_map/ppermute | solution.py:374
  21.1 0.5 collective-permute-start.11
  21.6 1.0 %shard_map.78 = (f32[128,1024]{1,0:T(8,128)S(1)}, f32[128,1024]{1,0:T(8,128)S(1)}, f32[128,384]{1,0:T(8,128)S(1)}) custom-call(bf16[128,128]{1,0:T(8,128)(2,1)S(1)} %collective-permute-done.4.refs_0_, bf16[128,128]{1,0:T(8,128)(2,1)S(1)} %collective-permute-done.5.refs_1_, bf16[128,128]{1,0:T(8,128)(2,1)S(1)} %collective-permute-done.6.refs_2_, ...), custom_call_target="tpu_custom_call" | custom-call | flops 469762048 | bytes 5902336 | tf_op jit(solution)/shard_map/pallas_call | solution.py:339
  22.6 1.1 %collective-permute-done.9.refs_1_ = bf16[128,128]{1,0:T(8,128)(2,1)S(1)} collective-permute-done((bf16[128,128]{1,0:T(8,128)(2,1)S(1)}, bf16[128,128]{1,0:T(8,128)(2,1)S(1)}, u32[]{:S(2)}, u32[]{:S(2)}) %collective-permute-start.9) | collective-permute-done | bytes 32800 | tf_op jit(solution)/shard_map/ppermute | solution.py:374
  23.8 0.4 shard_map.79
  24.2 2.3 %collective-permute-start.12 = (bf16[128,128]{1,0:T(8,128)(2,1)S(1)}, bf16[128,128]{1,0:T(8,128)(2,1)S(1)}, u32[]{:S(2)}, u32[]{:S(2)}) collective-permute-start(bf16[128,128]{1,0:T(8,128)(2,1)S(1)} %get-tuple-element.115), channel_id=1, source_target_pairs={{0,16},{1,2},{2,1},{3,19},{4,20},{5,21},{6,22},{7,8},{8,7},{9,10},... | collective-permute-start | bytes 98312 | tf_op jit(solution)/shard_map/ppermute | solution.py:374
  26.5 1.5 %collective-permute-start.13 = (bf16[128,128]{1,0:T(8,128)(2,1)S(1)}, bf16[128,128]{1,0:T(8,128)(2,1)S(1)}, u32[]{:S(2)}, u32[]{:S(2)}) collective-permute-start(bf16[128,128]{1,0:T(8,128)(2,1)S(1)} %get-tuple-element.116), channel_id=1, source_target_pairs={{0,3},{1,17},{2,18},{3,0},{4,13},{5,6},{6,5},{7,23},{8,24},{9,25},... | collective-permute-start | bytes 98312 | tf_op jit(solution)/shard_map/ppermute | solution.py:374
  27.9 0.5 collective-permute-start.15
  28.4 1.2 %shard_map.80 = (f32[128,1024]{1,0:T(8,128)S(1)}, f32[128,384]{1,0:T(8,128)S(1)}) custom-call(bf16[128,128]{1,0:T(8,128)(2,1)S(1)} %collective-permute-done.8.refs_0_, bf16[128,128]{1,0:T(8,128)(2,1)S(1)} %collective-permute-done.9.refs_1_, bf16[128,128]{1,0:T(8,128)(2,1)S(1)} %collective-permute-done.10.refs_2_, ...), custom_call_target="tpu_custom_call" | custom-call | flops 469762048 | bytes 5738496 | tf_op jit(solution)/shard_map/pallas_call | solution.py:339
  29.8 1.5 %collective-permute-done.13.refs_1_ = bf16[128,128]{1,0:T(8,128)(2,1)S(1)} collective-permute-done((bf16[128,128]{1,0:T(8,128)(2,1)S(1)}, bf16[128,128]{1,0:T(8,128)(2,1)S(1)}, u32[]{:S(2)}, u32[]{:S(2)}) %collective-permute-start.13) | collective-permute-done | bytes 32800 | tf_op jit(solution)/shard_map/ppermute | solution.py:374
  31.3 0.4 shard_map.81
  31.7 0.9 %collective-permute-start.16 = (bf16[128,128]{1,0:T(8,128)(2,1)S(1)}, bf16[128,128]{1,0:T(8,128)(2,1)S(1)}, u32[]{:S(2)}, u32[]{:S(2)}) collective-permute-start(bf16[128,128]{1,0:T(8,128)(2,1)S(1)} %get-tuple-element.124), channel_id=1, source_target_pairs={{0,16},{1,2},{2,1},{3,19},{4,20},{5,21},{6,22},{7,8},{8,7},{9,10},... | collective-permute-start | bytes 98312 | tf_op jit(solution)/shard_map/ppermute | solution.py:374
  32.6 1.9 %collective-permute-start.17 = (bf16[128,128]{1,0:T(8,128)(2,1)S(1)}, bf16[128,128]{1,0:T(8,128)(2,1)S(1)}, u32[]{:S(2)}, u32[]{:S(2)}) collective-permute-start(bf16[128,128]{1,0:T(8,128)(2,1)S(1)} %get-tuple-element.125), channel_id=1, source_target_pairs={{0,3},{1,17},{2,18},{3,0},{4,13},{5,6},{6,5},{7,23},{8,24},{9,25},... | collective-permute-start | bytes 98312 | tf_op jit(solution)/shard_map/ppermute | solution.py:374
  34.4 0.5 collective-permute-start.19
  34.9 1.0 %shard_map.82 = (f32[128,1024]{1,0:T(8,128)S(1)}, f32[128,1024]{1,0:T(8,128)S(1)}, f32[128,384]{1,0:T(8,128)S(1)}) custom-call(bf16[128,128]{1,0:T(8,128)(2,1)S(1)} %collective-permute-done.12.refs_0_, bf16[128,128]{1,0:T(8,128)(2,1)S(1)} %collective-permute-done.13.refs_1_, bf16[128,128]{1,0:T(8,128)(2,1)S(1)} %collective-permute-done.14.refs_2_, ...), custom_call_target="tpu_custom_call" | custom-call | flops 469762048 | bytes 5902336 | tf_op jit(solution)/shard_map/pallas_call | solution.py:339
  35.9 0.9 %collective-permute-done.16.refs_0_ = bf16[128,128]{1,0:T(8,128)(2,1)S(1)} collective-permute-done((bf16[128,128]{1,0:T(8,128)(2,1)S(1)}, bf16[128,128]{1,0:T(8,128)(2,1)S(1)}, u32[]{:S(2)}, u32[]{:S(2)}) %collective-permute-start.16) | collective-permute-done | bytes 32800 | tf_op jit(solution)/shard_map/ppermute | solution.py:374
  36.9 0.5 collective-permute-done.17.refs_1_
  37.4 0.4 shard_map.83
  37.8 1.7 %collective-permute-start.20 = (bf16[128,128]{1,0:T(8,128)(2,1)S(1)}, bf16[128,128]{1,0:T(8,128)(2,1)S(1)}, u32[]{:S(2)}, u32[]{:S(2)}) collective-permute-start(bf16[128,128]{1,0:T(8,128)(2,1)S(1)} %get-tuple-element.132), channel_id=1, source_target_pairs={{0,16},{1,2},{2,1},{3,19},{4,20},{5,21},{6,22},{7,8},{8,7},{9,10},... | collective-permute-start | bytes 98312 | tf_op jit(solution)/shard_map/ppermute | solution.py:374
  39.4 1.5 %collective-permute-start.21 = (bf16[128,128]{1,0:T(8,128)(2,1)S(1)}, bf16[128,128]{1,0:T(8,128)(2,1)S(1)}, u32[]{:S(2)}, u32[]{:S(2)}) collective-permute-start(bf16[128,128]{1,0:T(8,128)(2,1)S(1)} %get-tuple-element.133), channel_id=1, source_target_pairs={{0,3},{1,17},{2,18},{3,0},{4,13},{5,6},{6,5},{7,23},{8,24},{9,25},... | collective-permute-start | bytes 98312 | tf_op jit(solution)/shard_map/ppermute | solution.py:374
  40.9 0.5 collective-permute-start.23
  41.4 1.3 %shard_map.84 = (f32[128,1024]{1,0:T(8,128)S(1)}, f32[128,384]{1,0:T(8,128)S(1)}) custom-call(bf16[128,128]{1,0:T(8,128)(2,1)S(1)} %collective-permute-done.16.refs_0_, bf16[128,128]{1,0:T(8,128)(2,1)S(1)} %collective-permute-done.17.refs_1_, bf16[128,128]{1,0:T(8,128)(2,1)S(1)} %collective-permute-done.18.refs_2_, ...), custom_call_target="tpu_custom_call" | custom-call | flops 469762048 | bytes 5738496 | tf_op jit(solution)/shard_map/pallas_call | solution.py:339
  43.0 1.3 %collective-permute-done.21.refs_1_ = bf16[128,128]{1,0:T(8,128)(2,1)S(1)} collective-permute-done((bf16[128,128]{1,0:T(8,128)(2,1)S(1)}, bf16[128,128]{1,0:T(8,128)(2,1)S(1)}, u32[]{:S(2)}, u32[]{:S(2)}) %collective-permute-start.21) | collective-permute-done | bytes 32800 | tf_op jit(solution)/shard_map/ppermute | solution.py:374
  44.7 0.9 %collective-permute-start.24 = (bf16[128,128]{1,0:T(8,128)(2,1)S(1)}, bf16[128,128]{1,0:T(8,128)(2,1)S(1)}, u32[]{:S(2)}, u32[]{:S(2)}) collective-permute-start(bf16[128,128]{1,0:T(8,128)(2,1)S(1)} %get-tuple-element.140), channel_id=1, source_target_pairs={{0,16},{1,2},{2,1},{3,19},{4,20},{5,21},{6,22},{7,8},{8,7},{9,10},... | collective-permute-start | bytes 98312 | tf_op jit(solution)/shard_map/ppermute | solution.py:374
  45.5 1.9 %collective-permute-start.25 = (bf16[128,128]{1,0:T(8,128)(2,1)S(1)}, bf16[128,128]{1,0:T(8,128)(2,1)S(1)}, u32[]{:S(2)}, u32[]{:S(2)}) collective-permute-start(bf16[128,128]{1,0:T(8,128)(2,1)S(1)} %get-tuple-element.141), channel_id=1, source_target_pairs={{0,3},{1,17},{2,18},{3,0},{4,13},{5,6},{6,5},{7,23},{8,24},{9,25},... | collective-permute-start | bytes 98312 | tf_op jit(solution)/shard_map/ppermute | solution.py:374
  47.4 0.5 collective-permute-start.27
  47.9 1.0 %shard_map.86 = (f32[128,1024]{1,0:T(8,128)S(1)}, f32[128,1024]{1,0:T(8,128)S(1)}, f32[128,384]{1,0:T(8,128)S(1)}) custom-call(bf16[128,128]{1,0:T(8,128)(2,1)S(1)} %collective-permute-done.20.refs_0_, bf16[128,128]{1,0:T(8,128)(2,1)S(1)} %collective-permute-done.21.refs_1_, bf16[128,128]{1,0:T(8,128)(2,1)S(1)} %collective-permute-done.22.refs_2_, ...), custom_call_target="tpu_custom_call" | custom-call | flops 469762048 | bytes 5902336 | tf_op jit(solution)/shard_map/pallas_call | solution.py:339
  48.9 0.9 %collective-permute-done.24.refs_0_ = bf16[128,128]{1,0:T(8,128)(2,1)S(1)} collective-permute-done((bf16[128,128]{1,0:T(8,128)(2,1)S(1)}, bf16[128,128]{1,0:T(8,128)(2,1)S(1)}, u32[]{:S(2)}, u32[]{:S(2)}) %collective-permute-start.24) | collective-permute-done | bytes 32800 | tf_op jit(solution)/shard_map/ppermute | solution.py:374
  49.9 0.5 collective-permute-done.25.refs_1_
  50.8 1.6 %collective-permute-start.28 = (bf16[128,128]{1,0:T(8,128)(2,1)S(1)}, bf16[128,128]{1,0:T(8,128)(2,1)S(1)}, u32[]{:S(2)}, u32[]{:S(2)}) collective-permute-start(bf16[128,128]{1,0:T(8,128)(2,1)S(1)} %get-tuple-element.147), channel_id=1, source_target_pairs={{0,16},{1,2},{2,1},{3,19},{4,20},{5,21},{6,22},{7,8},{8,7},{9,10},... | collective-permute-start | bytes 98312 | tf_op jit(solution)/shard_map/ppermute | solution.py:374
  52.4 1.5 %collective-permute-start.29 = (bf16[128,128]{1,0:T(8,128)(2,1)S(1)}, bf16[128,128]{1,0:T(8,128)(2,1)S(1)}, u32[]{:S(2)}, u32[]{:S(2)}) collective-permute-start(bf16[128,128]{1,0:T(8,128)(2,1)S(1)} %get-tuple-element.148), channel_id=1, source_target_pairs={{0,3},{1,17},{2,18},{3,0},{4,13},{5,6},{6,5},{7,23},{8,24},{9,25},... | collective-permute-start | bytes 98312 | tf_op jit(solution)/shard_map/ppermute | solution.py:374
  53.9 0.5 collective-permute-start.31
  54.4 1.2 %shard_map.88.refs_5_ = f32[1024,128]{1,0:T(8,128)S(1)} custom-call(bf16[128,128]{1,0:T(8,128)(2,1)S(1)} %collective-permute-done.24.refs_0_, bf16[128,128]{1,0:T(8,128)(2,1)S(1)} %collective-permute-done.25.refs_1_, bf16[128,128]{1,0:T(8,128)(2,1)S(1)} %collective-permute-done.26.refs_2_, bf16[128,128]{1,0:T(8,128)(2,1)S(1)} %collective-permute-done.27.refs_3_, ...), custom_call_target="tpu_custom_call" | custom-call | flops 369098752 | bytes 4624384 | tf_op jit(solution)/shard_map/pallas_call | solution.py:339
  55.5 0.4 collective-permute-done.28.refs_0_
  56.0 1.3 %collective-permute-done.29.refs_1_ = bf16[128,128]{1,0:T(8,128)(2,1)S(1)} collective-permute-done((bf16[128,128]{1,0:T(8,128)(2,1)S(1)}, bf16[128,128]{1,0:T(8,128)(2,1)S(1)}, u32[]{:S(2)}, u32[]{:S(2)}) %collective-permute-start.29) | collective-permute-done | bytes 32800 | tf_op jit(solution)/shard_map/ppermute | solution.py:374
  57.2 1.1 %shard_map.89 = f32[1,1024,128]{2,1,0:T(8,128)} custom-call(bf16[128,128]{1,0:T(8,128)(2,1)S(1)} %collective-permute-done.28.refs_0_, bf16[128,128]{1,0:T(8,128)(2,1)S(1)} %collective-permute-done.29.refs_1_, bf16[128,128]{1,0:T(8,128)(2,1)S(1)} %collective-permute-done.30.refs_2_, bf16[128,128]{1,0:T(8,128)(2,1)S(1)} %collective-permute-done.31.refs_3_, ...), custom_call_target="tpu_custom_call" | custom-call | flops 100663296 | bytes 1966080 | tf_op jit(solution)/shard_map/pallas_call | solution.py:339
  (33 shorter events, 1.8 us)
Async XLA Ops:
  1.8 8.8 %collective-permute-start = (bf16[128,128]{1,0:T(8,128)(2,1)S(1)}, bf16[128,128]{1,0:T(8,128)(2,1)S(1)}, u32[]{:S(2)}, u32[]{:S(2)}) collective-permute-start(bf16[128,128]{1,0:T(8,128)(2,1)S(1)} %get-tuple-element.79), channel_id=1, source_target_pairs={{0,16},{1,2},{2,1},{3,19},{4,5},{5,4},{6,15},{7,23},{8,24},{9,25},... | collective-permute-start | bytes 98312 | tf_op jit(solution)/shard_map/ppermute | solution.py:374
  4.4 6.1 %collective-permute-start.1 = (bf16[128,128]{1,0:T(8,128)(2,1)S(1)}, bf16[128,128]{1,0:T(8,128)(2,1)S(1)}, u32[]{:S(2)}, u32[]{:S(2)}) collective-permute-start(bf16[128,128]{1,0:T(8,128)(2,1)S(1)} %get-tuple-element.80), channel_id=1, source_target_pairs={{0,2},{1,17},{2,0},{3,4},{4,3},{5,6},{6,5},{7,8},{8,7},{9,10},{10,... | collective-permute-start | bytes 98312 | tf_op jit(solution)/shard_map/ppermute | solution.py:374
  5.9 4.6 %collective-permute-start.2 = (bf16[128,128]{1,0:T(8,128)(2,1)S(1)}, bf16[128,128]{1,0:T(8,128)(2,1)S(1)}, u32[]{:S(2)}, u32[]{:S(2)}) collective-permute-start(bf16[128,128]{1,0:T(8,128)(2,1)S(1)} %get-tuple-element.81), channel_id=1, source_target_pairs={{0,1},{1,0},{2,18},{3,7},{4,20},{5,21},{6,22},{7,3},{8,9},{9,8},{1... | collective-permute-start | bytes 98312 | tf_op jit(solution)/shard_map/ppermute | solution.py:374
  6.0 4.5 %collective-permute-start.3 = (bf16[128,128]{1,0:T(8,128)(2,1)S(1)}, bf16[128,128]{1,0:T(8,128)(2,1)S(1)}, u32[]{:S(2)}, u32[]{:S(2)}) collective-permute-start(bf16[128,128]{1,0:T(8,128)(2,1)S(1)} %get-tuple-element.82), channel_id=1, source_target_pairs={{0,1},{1,0},{2,3},{3,2},{4,5},{5,4},{6,7},{7,6},{8,9},{9,8},{10,11... | collective-permute-start | bytes 98312 | tf_op jit(solution)/shard_map/ppermute | solution.py:374
  11.0 4.9 %collective-permute-start.4 = (bf16[128,128]{1,0:T(8,128)(2,1)S(1)}, bf16[128,128]{1,0:T(8,128)(2,1)S(1)}, u32[]{:S(2)}, u32[]{:S(2)}) collective-permute-start(bf16[128,128]{1,0:T(8,128)(2,1)S(1)} %get-tuple-element.94), channel_id=1, source_target_pairs={{0,16},{1,2},{2,1},{3,19},{4,5},{5,4},{6,15},{7,23},{8,24},{9,25},... | collective-permute-start | bytes 98312 | tf_op jit(solution)/shard_map/ppermute | solution.py:374
  11.8 5.1 %collective-permute-start.5 = (bf16[128,128]{1,0:T(8,128)(2,1)S(1)}, bf16[128,128]{1,0:T(8,128)(2,1)S(1)}, u32[]{:S(2)}, u32[]{:S(2)}) collective-permute-start(bf16[128,128]{1,0:T(8,128)(2,1)S(1)} %get-tuple-element.95), channel_id=1, source_target_pairs={{0,2},{1,17},{2,0},{3,4},{4,3},{5,6},{6,5},{7,8},{8,7},{9,10},{10,... | collective-permute-start | bytes 98312 | tf_op jit(solution)/shard_map/ppermute | solution.py:374
  12.7 4.3 %collective-permute-start.6 = (bf16[128,128]{1,0:T(8,128)(2,1)S(1)}, bf16[128,128]{1,0:T(8,128)(2,1)S(1)}, u32[]{:S(2)}, u32[]{:S(2)}) collective-permute-start(bf16[128,128]{1,0:T(8,128)(2,1)S(1)} %get-tuple-element.96), channel_id=1, source_target_pairs={{0,1},{1,0},{2,18},{3,7},{4,20},{5,21},{6,22},{7,3},{8,9},{9,8},{1... | collective-permute-start | bytes 98312 | tf_op jit(solution)/shard_map/ppermute | solution.py:374
  13.2 3.8 %collective-permute-start.7 = (bf16[128,128]{1,0:T(8,128)(2,1)S(1)}, bf16[128,128]{1,0:T(8,128)(2,1)S(1)}, u32[]{:S(2)}, u32[]{:S(2)}) collective-permute-start(bf16[128,128]{1,0:T(8,128)(2,1)S(1)} %get-tuple-element.97), channel_id=1, source_target_pairs={{0,1},{1,0},{2,3},{3,2},{4,5},{5,4},{6,7},{7,6},{8,9},{9,8},{10,11... | collective-permute-start | bytes 98312 | tf_op jit(solution)/shard_map/ppermute | solution.py:374
  17.4 5.3 %collective-permute-start.8 = (bf16[128,128]{1,0:T(8,128)(2,1)S(1)}, bf16[128,128]{1,0:T(8,128)(2,1)S(1)}, u32[]{:S(2)}, u32[]{:S(2)}) collective-permute-start(bf16[128,128]{1,0:T(8,128)(2,1)S(1)} %get-tuple-element.106), channel_id=1, source_target_pairs={{0,16},{1,2},{2,1},{3,19},{4,20},{5,21},{6,22},{7,8},{8,7},{9,10},... | collective-permute-start | bytes 98312 | tf_op jit(solution)/shard_map/ppermute | solution.py:374
  19.0 4.8 %collective-permute-start.9 = (bf16[128,128]{1,0:T(8,128)(2,1)S(1)}, bf16[128,128]{1,0:T(8,128)(2,1)S(1)}, u32[]{:S(2)}, u32[]{:S(2)}) collective-permute-start(bf16[128,128]{1,0:T(8,128)(2,1)S(1)} %get-tuple-element.107), channel_id=1, source_target_pairs={{0,3},{1,17},{2,18},{3,0},{4,13},{5,6},{6,5},{7,23},{8,24},{9,25},... | collective-permute-start | bytes 98312 | tf_op jit(solution)/shard_map/ppermute | solution.py:374
  21.1 2.7 %collective-permute-start.10 = (bf16[128,128]{1,0:T(8,128)(2,1)S(1)}, bf16[128,128]{1,0:T(8,128)(2,1)S(1)}, u32[]{:S(2)}, u32[]{:S(2)}) collective-permute-start(bf16[128,128]{1,0:T(8,128)(2,1)S(1)} %get-tuple-element.108), channel_id=1, source_target_pairs={{0,1},{1,0},{2,5},{3,4},{4,3},{5,2},{6,7},{7,6},{8,9},{9,8},{10,11... | collective-permute-start | bytes 98312 | tf_op jit(solution)/shard_map/ppermute | solution.py:374
  21.1 2.7 %collective-permute-start.11 = (bf16[128,128]{1,0:T(8,128)(2,1)S(1)}, bf16[128,128]{1,0:T(8,128)(2,1)S(1)}, u32[]{:S(2)}, u32[]{:S(2)}) collective-permute-start(bf16[128,128]{1,0:T(8,128)(2,1)S(1)} %get-tuple-element.109), channel_id=1, source_target_pairs={{0,1},{1,0},{2,3},{3,2},{4,5},{5,4},{6,7},{7,6},{8,9},{9,8},{10,11... | collective-permute-start | bytes 98312 | tf_op jit(solution)/shard_map/ppermute | solution.py:374
  24.2 5.6 %collective-permute-start.12 = (bf16[128,128]{1,0:T(8,128)(2,1)S(1)}, bf16[128,128]{1,0:T(8,128)(2,1)S(1)}, u32[]{:S(2)}, u32[]{:S(2)}) collective-permute-start(bf16[128,128]{1,0:T(8,128)(2,1)S(1)} %get-tuple-element.115), channel_id=1, source_target_pairs={{0,16},{1,2},{2,1},{3,19},{4,20},{5,21},{6,22},{7,8},{8,7},{9,10},... | collective-permute-start | bytes 98312 | tf_op jit(solution)/shard_map/ppermute | solution.py:374
  26.5 4.8 %collective-permute-start.13 = (bf16[128,128]{1,0:T(8,128)(2,1)S(1)}, bf16[128,128]{1,0:T(8,128)(2,1)S(1)}, u32[]{:S(2)}, u32[]{:S(2)}) collective-permute-start(bf16[128,128]{1,0:T(8,128)(2,1)S(1)} %get-tuple-element.116), channel_id=1, source_target_pairs={{0,3},{1,17},{2,18},{3,0},{4,13},{5,6},{6,5},{7,23},{8,24},{9,25},... | collective-permute-start | bytes 98312 | tf_op jit(solution)/shard_map/ppermute | solution.py:374
  27.9 3.4 %collective-permute-start.14 = (bf16[128,128]{1,0:T(8,128)(2,1)S(1)}, bf16[128,128]{1,0:T(8,128)(2,1)S(1)}, u32[]{:S(2)}, u32[]{:S(2)}) collective-permute-start(bf16[128,128]{1,0:T(8,128)(2,1)S(1)} %get-tuple-element.117), channel_id=1, source_target_pairs={{0,1},{1,0},{2,5},{3,4},{4,3},{5,2},{6,7},{7,6},{8,9},{9,8},{10,11... | collective-permute-start | bytes 98312 | tf_op jit(solution)/shard_map/ppermute | solution.py:374
  27.9 3.4 %collective-permute-start.15 = (bf16[128,128]{1,0:T(8,128)(2,1)S(1)}, bf16[128,128]{1,0:T(8,128)(2,1)S(1)}, u32[]{:S(2)}, u32[]{:S(2)}) collective-permute-start(bf16[128,128]{1,0:T(8,128)(2,1)S(1)} %get-tuple-element.118), channel_id=1, source_target_pairs={{0,1},{1,0},{2,3},{3,2},{4,5},{5,4},{6,7},{7,6},{8,9},{9,8},{10,11... | collective-permute-start | bytes 98312 | tf_op jit(solution)/shard_map/ppermute | solution.py:374
  31.7 5.2 %collective-permute-start.16 = (bf16[128,128]{1,0:T(8,128)(2,1)S(1)}, bf16[128,128]{1,0:T(8,128)(2,1)S(1)}, u32[]{:S(2)}, u32[]{:S(2)}) collective-permute-start(bf16[128,128]{1,0:T(8,128)(2,1)S(1)} %get-tuple-element.124), channel_id=1, source_target_pairs={{0,16},{1,2},{2,1},{3,19},{4,20},{5,21},{6,22},{7,8},{8,7},{9,10},... | collective-permute-start | bytes 98312 | tf_op jit(solution)/shard_map/ppermute | solution.py:374
  32.6 4.8 %collective-permute-start.17 = (bf16[128,128]{1,0:T(8,128)(2,1)S(1)}, bf16[128,128]{1,0:T(8,128)(2,1)S(1)}, u32[]{:S(2)}, u32[]{:S(2)}) collective-permute-start(bf16[128,128]{1,0:T(8,128)(2,1)S(1)} %get-tuple-element.125), channel_id=1, source_target_pairs={{0,3},{1,17},{2,18},{3,0},{4,13},{5,6},{6,5},{7,23},{8,24},{9,25},... | collective-permute-start | bytes 98312 | tf_op jit(solution)/shard_map/ppermute | solution.py:374
  34.4 2.9 %collective-permute-start.18 = (bf16[128,128]{1,0:T(8,128)(2,1)S(1)}, bf16[128,128]{1,0:T(8,128)(2,1)S(1)}, u32[]{:S(2)}, u32[]{:S(2)}) collective-permute-start(bf16[128,128]{1,0:T(8,128)(2,1)S(1)} %get-tuple-element.126), channel_id=1, source_target_pairs={{0,1},{1,0},{2,5},{3,4},{4,3},{5,2},{6,7},{7,6},{8,9},{9,8},{10,11... | collective-permute-start | bytes 98312 | tf_op jit(solution)/shard_map/ppermute | solution.py:374
  34.4 2.9 %collective-permute-start.19 = (bf16[128,128]{1,0:T(8,128)(2,1)S(1)}, bf16[128,128]{1,0:T(8,128)(2,1)S(1)}, u32[]{:S(2)}, u32[]{:S(2)}) collective-permute-start(bf16[128,128]{1,0:T(8,128)(2,1)S(1)} %get-tuple-element.127), channel_id=1, source_target_pairs={{0,1},{1,0},{2,3},{3,2},{4,5},{5,4},{6,7},{7,6},{8,9},{9,8},{10,11... | collective-permute-start | bytes 98312 | tf_op jit(solution)/shard_map/ppermute | solution.py:374
  37.8 5.2 %collective-permute-start.20 = (bf16[128,128]{1,0:T(8,128)(2,1)S(1)}, bf16[128,128]{1,0:T(8,128)(2,1)S(1)}, u32[]{:S(2)}, u32[]{:S(2)}) collective-permute-start(bf16[128,128]{1,0:T(8,128)(2,1)S(1)} %get-tuple-element.132), channel_id=1, source_target_pairs={{0,16},{1,2},{2,1},{3,19},{4,20},{5,21},{6,22},{7,8},{8,7},{9,10},... | collective-permute-start | bytes 98312 | tf_op jit(solution)/shard_map/ppermute | solution.py:374
  39.4 4.8 %collective-permute-start.21 = (bf16[128,128]{1,0:T(8,128)(2,1)S(1)}, bf16[128,128]{1,0:T(8,128)(2,1)S(1)}, u32[]{:S(2)}, u32[]{:S(2)}) collective-permute-start(bf16[128,128]{1,0:T(8,128)(2,1)S(1)} %get-tuple-element.133), channel_id=1, source_target_pairs={{0,3},{1,17},{2,18},{3,0},{4,13},{5,6},{6,5},{7,23},{8,24},{9,25},... | collective-permute-start | bytes 98312 | tf_op jit(solution)/shard_map/ppermute | solution.py:374
  40.9 3.4 %collective-permute-start.22 = (bf16[128,128]{1,0:T(8,128)(2,1)S(1)}, bf16[128,128]{1,0:T(8,128)(2,1)S(1)}, u32[]{:S(2)}, u32[]{:S(2)}) collective-permute-start(bf16[128,128]{1,0:T(8,128)(2,1)S(1)} %get-tuple-element.134), channel_id=1, source_target_pairs={{0,1},{1,0},{2,5},{3,4},{4,3},{5,2},{6,7},{7,6},{8,9},{9,8},{10,11... | collective-permute-start | bytes 98312 | tf_op jit(solution)/shard_map/ppermute | solution.py:374
  40.9 3.4 %collective-permute-start.23 = (bf16[128,128]{1,0:T(8,128)(2,1)S(1)}, bf16[128,128]{1,0:T(8,128)(2,1)S(1)}, u32[]{:S(2)}, u32[]{:S(2)}) collective-permute-start(bf16[128,128]{1,0:T(8,128)(2,1)S(1)} %get-tuple-element.135), channel_id=1, source_target_pairs={{0,1},{1,0},{2,3},{3,2},{4,5},{5,4},{6,7},{7,6},{8,9},{9,8},{10,11... | collective-permute-start | bytes 98312 | tf_op jit(solution)/shard_map/ppermute | solution.py:374
  44.7 5.2 %collective-permute-start.24 = (bf16[128,128]{1,0:T(8,128)(2,1)S(1)}, bf16[128,128]{1,0:T(8,128)(2,1)S(1)}, u32[]{:S(2)}, u32[]{:S(2)}) collective-permute-start(bf16[128,128]{1,0:T(8,128)(2,1)S(1)} %get-tuple-element.140), channel_id=1, source_target_pairs={{0,16},{1,2},{2,1},{3,19},{4,20},{5,21},{6,22},{7,8},{8,7},{9,10},... | collective-permute-start | bytes 98312 | tf_op jit(solution)/shard_map/ppermute | solution.py:374
  45.5 4.8 %collective-permute-start.25 = (bf16[128,128]{1,0:T(8,128)(2,1)S(1)}, bf16[128,128]{1,0:T(8,128)(2,1)S(1)}, u32[]{:S(2)}, u32[]{:S(2)}) collective-permute-start(bf16[128,128]{1,0:T(8,128)(2,1)S(1)} %get-tuple-element.141), channel_id=1, source_target_pairs={{0,3},{1,17},{2,18},{3,0},{4,13},{5,6},{6,5},{7,23},{8,24},{9,25},... | collective-permute-start | bytes 98312 | tf_op jit(solution)/shard_map/ppermute | solution.py:374
  47.4 2.9 %collective-permute-start.26 = (bf16[128,128]{1,0:T(8,128)(2,1)S(1)}, bf16[128,128]{1,0:T(8,128)(2,1)S(1)}, u32[]{:S(2)}, u32[]{:S(2)}) collective-permute-start(bf16[128,128]{1,0:T(8,128)(2,1)S(1)} %get-tuple-element.142), channel_id=1, source_target_pairs={{0,1},{1,0},{2,5},{3,4},{4,3},{5,2},{6,7},{7,6},{8,9},{9,8},{10,11... | collective-permute-start | bytes 98312 | tf_op jit(solution)/shard_map/ppermute | solution.py:374
  47.4 2.9 %collective-permute-start.27 = (bf16[128,128]{1,0:T(8,128)(2,1)S(1)}, bf16[128,128]{1,0:T(8,128)(2,1)S(1)}, u32[]{:S(2)}, u32[]{:S(2)}) collective-permute-start(bf16[128,128]{1,0:T(8,128)(2,1)S(1)} %get-tuple-element.143), channel_id=1, source_target_pairs={{0,1},{1,0},{2,3},{3,2},{4,5},{5,4},{6,7},{7,6},{8,9},{9,8},{10,11... | collective-permute-start | bytes 98312 | tf_op jit(solution)/shard_map/ppermute | solution.py:374
  50.8 5.2 %collective-permute-start.28 = (bf16[128,128]{1,0:T(8,128)(2,1)S(1)}, bf16[128,128]{1,0:T(8,128)(2,1)S(1)}, u32[]{:S(2)}, u32[]{:S(2)}) collective-permute-start(bf16[128,128]{1,0:T(8,128)(2,1)S(1)} %get-tuple-element.147), channel_id=1, source_target_pairs={{0,16},{1,2},{2,1},{3,19},{4,20},{5,21},{6,22},{7,8},{8,7},{9,10},... | collective-permute-start | bytes 98312 | tf_op jit(solution)/shard_map/ppermute | solution.py:374
  52.4 4.8 %collective-permute-start.29 = (bf16[128,128]{1,0:T(8,128)(2,1)S(1)}, bf16[128,128]{1,0:T(8,128)(2,1)S(1)}, u32[]{:S(2)}, u32[]{:S(2)}) collective-permute-start(bf16[128,128]{1,0:T(8,128)(2,1)S(1)} %get-tuple-element.148), channel_id=1, source_target_pairs={{0,3},{1,17},{2,18},{3,0},{4,13},{5,6},{6,5},{7,23},{8,24},{9,25},... | collective-permute-start | bytes 98312 | tf_op jit(solution)/shard_map/ppermute | solution.py:374
  53.9 3.4 %collective-permute-start.30 = (bf16[128,128]{1,0:T(8,128)(2,1)S(1)}, bf16[128,128]{1,0:T(8,128)(2,1)S(1)}, u32[]{:S(2)}, u32[]{:S(2)}) collective-permute-start(bf16[128,128]{1,0:T(8,128)(2,1)S(1)} %get-tuple-element.149), channel_id=1, source_target_pairs={{0,1},{1,0},{2,5},{3,4},{4,3},{5,2},{6,7},{7,6},{8,9},{9,8},{10,11... | collective-permute-start | bytes 98312 | tf_op jit(solution)/shard_map/ppermute | solution.py:374
  53.9 3.4 %collective-permute-start.31 = (bf16[128,128]{1,0:T(8,128)(2,1)S(1)}, bf16[128,128]{1,0:T(8,128)(2,1)S(1)}, u32[]{:S(2)}, u32[]{:S(2)}) collective-permute-start(bf16[128,128]{1,0:T(8,128)(2,1)S(1)} %get-tuple-element.150), channel_id=1, source_target_pairs={{0,1},{1,0},{2,3},{3,2},{4,5},{5,4},{6,7},{7,6},{8,9},{9,8},{10,11... | collective-permute-start | bytes 98312 | tf_op jit(solution)/shard_map/ppermute | solution.py:374

commit v18 on v17

--- a/solution.py
+++ b/solution.py
@@ -200,8 +200,7 @@
 ):
     copy = pltpu.make_async_copy(s_in, s_ref, sem)
     copy.start()
-    hot = hot_ref[...]
-    width, total = hot.shape
+    width, total = hot_ref.shape
     weight = weight_ref[...]
     side = 128
     listed = list_ref[:1]
@@ -220,9 +219,7 @@
     same_ref[...] = same.astype(BF16)
     inner = jnp.where(jnp.concatenate(hits, 1) > 0.0, 0.0, 1.0)
     inner_ref[...] = jnp.broadcast_to(inner, inner_ref.shape)
-    n_pick = times(hot_t_ref[...], n_ref[0]).astype(BF16)
-    n_pick_ref[...] = n_pick
-    n_small_ref[...] = times(n_pick, hot).astype(BF16)
+    n_pick_ref[...] = times(hot_t_ref[...], n_ref[0]).astype(BF16)
     earlier = lax.broadcasted_iota(jnp.int32, same.shape, 0) < lax.broadcasted_iota(jnp.int32, same.shape, 1)
     repeats = jnp.sum(jnp.where(earlier, same, 0.0), 0, keepdims=True)
     first = jnp.where(repeats > 0.0, 0.0, 1.0)
@@ -235,7 +232,8 @@
     mask_ref[...] = mask
     local = mask[:1] * turned_ref[...].astype(F32)
     local_ref[...] = local
-    base_ref[...] = times_t((weight * local * inner).astype(BF16), n_pick)
+    base_ref[...] = times_t((weight * local * inner).astype(BF16), n_pick_ref[...])
+    n_small_ref[...] = times(n_pick_ref[...], hot_ref[...]).astype(BF16)
     copy.wait()
 
 

time: 58.5 us -> 56.8 us (0.971)
  Pallas kernels: 18.4 us -> 17 us
  waiting for transfers between devices: 9.93 us -> 9.26 us
    pallas_call x17, Pallas kernels: 18.4 us -> 17 us  [run(): pl.pallas_call(kernel, out_shape=results, in_specs=[pl.BlockSpec(memory_s...]
    ppermute x32, waiting for transfers between devices: 9.93 us -> 9.26 us  [exchange(): lax.ppermute(part, 'sub', route)]
  transfers between devices with their start and end apart: 32 -> 32, of which waited for: 12 -> 13; matrix products, arithmetic and copies ran while one was open for 0% -> 0% of each run, Pallas kernels for 22% -> 20%
where the time goes in v18:
time: 56.8 us; the launch traced here: 56.7 us
  starting transfers between devices  29.6 us (52%)
  Pallas kernels  17 us (30%)
  waiting for transfers between devices  9.26 us (16%)
  between operations  0.82 us (1%)
    ppermute x32, starting transfers between devices, exchange(): lax.ppermute(part, 'sub', route)  29.6 us
    pallas_call x17, Pallas kernels, run(): pl.pallas_call(kernel, out_shape=results, in_specs=[pl.BlockSpec(memory_s...  17 us
    ppermute x32, waiting for transfers between devices, exchange(): lax.ppermute(part, 'sub', route)  9.26 us
  transfers between devices with their start and end apart: 32, of which 13 were waited for; matrix products, arithmetic and copies ran while one was open for 0% of the time, Pallas kernels for 20%

profile of v18, /device:TPU:8, one launch (start us, length us, event | category | flops | bytes accessed | tf_op | source)
XLA Modules:
  0.0 56.7 jit_solution(11955435223255989962)
XLA Ops:
  0.0 1.8 %shard_map.73 = (bf16[1024,384]{1,0:T(8,128)(2,1)S(1)}, bf16[128,1024]{1,0:T(8,128)(2,1)S(1)}, bf16[128,384]{1,0:T(8,128)(2,1)S(1)}, f32[8,384]{1,0:T(8,128)S(1)...) custom-call(s32[1,4,128]{2,1,0:T(4,128)} %rows_in.1, ...), custom_call_target="tpu_custom_call" | custom-call | flops 100663296 | bytes 5769232 | tf_op jit(solution)/shard_map/pallas_call | solution.py:337
  1.8 2.7 %collective-permute-start = (bf16[128,128]{1,0:T(8,128)(2,1)S(1)}, bf16[128,128]{1,0:T(8,128)(2,1)S(1)}, u32[]{:S(2)}, u32[]{:S(2)}) collective-permute-start(bf16[128,128]{1,0:T(8,128)(2,1)S(1)} %get-tuple-element.79), channel_id=1, source_target_pairs={{0,16},{1,2},{2,1},{3,19},{4,5},{5,4},{6,15},{7,23},{8,24},{9,25},... | collective-permute-start | bytes 98312 | tf_op jit(solution)/shard_map/ppermute | solution.py:372
  4.4 1.5 %collective-permute-start.1 = (bf16[128,128]{1,0:T(8,128)(2,1)S(1)}, bf16[128,128]{1,0:T(8,128)(2,1)S(1)}, u32[]{:S(2)}, u32[]{:S(2)}) collective-permute-start(bf16[128,128]{1,0:T(8,128)(2,1)S(1)} %get-tuple-element.80), channel_id=1, source_target_pairs={{0,2},{1,17},{2,0},{3,4},{4,3},{5,6},{6,5},{7,8},{8,7},{9,10},{10,... | collective-permute-start | bytes 98312 | tf_op jit(solution)/shard_map/ppermute | solution.py:372
  6.0 0.4 collective-permute-start.3
  7.1 2.0 %shard_map.74 = (bf16[384,1024]{1,0:T(8,128)(2,1)S(1)}, bf16[384,1024]{1,0:T(8,128)(2,1)S(1)}, bf16[384,384]{1,0:T(8,128)(2,1)S(1)}, bf16[384,384]{1,0:T(8,128)(...) custom-call(bf16[1024,384]{1,0:T(8,128)(2,1)S(1)} %get-tuple-element, ...), custom_call_target="tpu_custom_call" | custom-call | flops 1207959552 | bytes 10330116 | tf_op jit(solution)/shard_map/pallas_call | solution.py:337
  9.1 0.7 %collective-permute-done.1.refs_1_ = bf16[128,128]{1,0:T(8,128)(2,1)S(1)} collective-permute-done((bf16[128,128]{1,0:T(8,128)(2,1)S(1)}, bf16[128,128]{1,0:T(8,128)(2,1)S(1)}, u32[]{:S(2)}, u32[]{:S(2)}) %collective-permute-start.1) | collective-permute-done | bytes 32800 | tf_op jit(solution)/shard_map/ppermute | solution.py:372
  10.6 1.1 %collective-permute-start.5 = (bf16[128,128]{1,0:T(8,128)(2,1)S(1)}, bf16[128,128]{1,0:T(8,128)(2,1)S(1)}, u32[]{:S(2)}, u32[]{:S(2)}) collective-permute-start(bf16[128,128]{1,0:T(8,128)(2,1)S(1)} %get-tuple-element.95), channel_id=1, source_target_pairs={{0,2},{1,17},{2,0},{3,4},{4,3},{5,6},{6,5},{7,8},{8,7},{9,10},{10,... | collective-permute-start | bytes 98312 | tf_op jit(solution)/shard_map/ppermute | solution.py:372
  11.8 0.4 collective-permute-start.7
  12.2 2.7 %shard_map.76 = (f32[128,1024]{1,0:T(8,128)S(1)}, f32[128,384]{1,0:T(8,128)S(1)}, bf16[1024,384]{1,0:T(8,128)(2,1)S(1)}, bf16[384,384]{1,0:T(8,128)(2,1)S(1)}) custom-call(bf16[128,128]{1,0:T(8,128)(2,1)S(1)} %collective-permute-done.refs_0_, bf16[128,128]{1,0:T(8,128)(2,1)S(1)} %collective-permute-done.1.refs_1_, ...), custom_call_target="tpu_custom_call" | custom-call | flops 1577058304 | bytes 8392704 | tf_op jit(solution)/shard_map/pallas_call | solution.py:337
  15.2 0.5 collective-permute-done.5.refs_1_
  15.7 0.4 shard_map.77
  16.1 1.5 %collective-permute-start.8 = (bf16[128,128]{1,0:T(8,128)(2,1)S(1)}, bf16[128,128]{1,0:T(8,128)(2,1)S(1)}, u32[]{:S(2)}, u32[]{:S(2)}) collective-permute-start(bf16[128,128]{1,0:T(8,128)(2,1)S(1)} %get-tuple-element.106), channel_id=1, source_target_pairs={{0,16},{1,2},{2,1},{3,19},{4,20},{5,21},{6,22},{7,8},{8,7},{9,10},... | collective-permute-start | bytes 98312 | tf_op jit(solution)/shard_map/ppermute | solution.py:372
  17.6 2.6 %collective-permute-start.9 = (bf16[128,128]{1,0:T(8,128)(2,1)S(1)}, bf16[128,128]{1,0:T(8,128)(2,1)S(1)}, u32[]{:S(2)}, u32[]{:S(2)}) collective-permute-start(bf16[128,128]{1,0:T(8,128)(2,1)S(1)} %get-tuple-element.107), channel_id=1, source_target_pairs={{0,3},{1,17},{2,18},{3,0},{4,13},{5,6},{6,5},{7,23},{8,24},{9,25},... | collective-permute-start | bytes 98312 | tf_op jit(solution)/shard_map/ppermute | solution.py:372
  20.2 0.5 collective-permute-start.11
  20.7 1.0 %shard_map.78 = (f32[128,1024]{1,0:T(8,128)S(1)}, f32[128,1024]{1,0:T(8,128)S(1)}, f32[128,384]{1,0:T(8,128)S(1)}) custom-call(bf16[128,128]{1,0:T(8,128)(2,1)S(1)} %collective-permute-done.4.refs_0_, bf16[128,128]{1,0:T(8,128)(2,1)S(1)} %collective-permute-done.5.refs_1_, bf16[128,128]{1,0:T(8,128)(2,1)S(1)} %collective-permute-done.6.refs_2_, ...), custom_call_target="tpu_custom_call" | custom-call | flops 469762048 | bytes 5902336 | tf_op jit(solution)/shard_map/pallas_call | solution.py:337
  21.7 0.7 %collective-permute-done.9.refs_1_ = bf16[128,128]{1,0:T(8,128)(2,1)S(1)} collective-permute-done((bf16[128,128]{1,0:T(8,128)(2,1)S(1)}, bf16[128,128]{1,0:T(8,128)(2,1)S(1)}, u32[]{:S(2)}, u32[]{:S(2)}) %collective-permute-start.9) | collective-permute-done | bytes 32800 | tf_op jit(solution)/shard_map/ppermute | solution.py:372
  22.4 0.4 shard_map.79
  22.8 2.0 %collective-permute-start.12 = (bf16[128,128]{1,0:T(8,128)(2,1)S(1)}, bf16[128,128]{1,0:T(8,128)(2,1)S(1)}, u32[]{:S(2)}, u32[]{:S(2)}) collective-permute-start(bf16[128,128]{1,0:T(8,128)(2,1)S(1)} %get-tuple-element.115), channel_id=1, source_target_pairs={{0,16},{1,2},{2,1},{3,19},{4,20},{5,21},{6,22},{7,8},{8,7},{9,10},... | collective-permute-start | bytes 98312 | tf_op jit(solution)/shard_map/ppermute | solution.py:372
  24.8 1.7 %collective-permute-start.13 = (bf16[128,128]{1,0:T(8,128)(2,1)S(1)}, bf16[128,128]{1,0:T(8,128)(2,1)S(1)}, u32[]{:S(2)}, u32[]{:S(2)}) collective-permute-start(bf16[128,128]{1,0:T(8,128)(2,1)S(1)} %get-tuple-element.116), channel_id=1, source_target_pairs={{0,3},{1,17},{2,18},{3,0},{4,13},{5,6},{6,5},{7,23},{8,24},{9,25},... | collective-permute-start | bytes 98312 | tf_op jit(solution)/shard_map/ppermute | solution.py:372
  26.6 0.5 collective-permute-start.15
  27.1 1.2 %shard_map.80 = (f32[128,1024]{1,0:T(8,128)S(1)}, f32[128,384]{1,0:T(8,128)S(1)}) custom-call(bf16[128,128]{1,0:T(8,128)(2,1)S(1)} %collective-permute-done.8.refs_0_, bf16[128,128]{1,0:T(8,128)(2,1)S(1)} %collective-permute-done.9.refs_1_, bf16[128,128]{1,0:T(8,128)(2,1)S(1)} %collective-permute-done.10.refs_2_, ...), custom_call_target="tpu_custom_call" | custom-call | flops 469762048 | bytes 5738496 | tf_op jit(solution)/shard_map/pallas_call | solution.py:337
  28.3 1.3 %collective-permute-done.13.refs_1_ = bf16[128,128]{1,0:T(8,128)(2,1)S(1)} collective-permute-done((bf16[128,128]{1,0:T(8,128)(2,1)S(1)}, bf16[128,128]{1,0:T(8,128)(2,1)S(1)}, u32[]{:S(2)}, u32[]{:S(2)}) %collective-permute-start.13) | collective-permute-done | bytes 32800 | tf_op jit(solution)/shard_map/ppermute | solution.py:372
  30.1 1.3 %collective-permute-start.16 = (bf16[128,128]{1,0:T(8,128)(2,1)S(1)}, bf16[128,128]{1,0:T(8,128)(2,1)S(1)}, u32[]{:S(2)}, u32[]{:S(2)}) collective-permute-start(bf16[128,128]{1,0:T(8,128)(2,1)S(1)} %get-tuple-element.124), channel_id=1, source_target_pairs={{0,16},{1,2},{2,1},{3,19},{4,20},{5,21},{6,22},{7,8},{8,7},{9,10},... | collective-permute-start | bytes 98312 | tf_op jit(solution)/shard_map/ppermute | solution.py:372
  31.3 1.9 %collective-permute-start.17 = (bf16[128,128]{1,0:T(8,128)(2,1)S(1)}, bf16[128,128]{1,0:T(8,128)(2,1)S(1)}, u32[]{:S(2)}, u32[]{:S(2)}) collective-permute-start(bf16[128,128]{1,0:T(8,128)(2,1)S(1)} %get-tuple-element.125), channel_id=1, source_target_pairs={{0,3},{1,17},{2,18},{3,0},{4,13},{5,6},{6,5},{7,23},{8,24},{9,25},... | collective-permute-start | bytes 98312 | tf_op jit(solution)/shard_map/ppermute | solution.py:372
  33.2 0.5 collective-permute-start.19
  33.7 1.0 %shard_map.82 = (f32[128,1024]{1,0:T(8,128)S(1)}, f32[128,1024]{1,0:T(8,128)S(1)}, f32[128,384]{1,0:T(8,128)S(1)}) custom-call(bf16[128,128]{1,0:T(8,128)(2,1)S(1)} %collective-permute-done.12.refs_0_, bf16[128,128]{1,0:T(8,128)(2,1)S(1)} %collective-permute-done.13.refs_1_, bf16[128,128]{1,0:T(8,128)(2,1)S(1)} %collective-permute-done.14.refs_2_, ...), custom_call_target="tpu_custom_call" | custom-call | flops 469762048 | bytes 5902336 | tf_op jit(solution)/shard_map/pallas_call | solution.py:337
  34.7 0.7 %collective-permute-done.16.refs_0_ = bf16[128,128]{1,0:T(8,128)(2,1)S(1)} collective-permute-done((bf16[128,128]{1,0:T(8,128)(2,1)S(1)}, bf16[128,128]{1,0:T(8,128)(2,1)S(1)}, u32[]{:S(2)}, u32[]{:S(2)}) %collective-permute-start.16) | collective-permute-done | bytes 32800 | tf_op jit(solution)/shard_map/ppermute | solution.py:372
  35.4 0.8 %collective-permute-done.17.refs_1_ = bf16[128,128]{1,0:T(8,128)(2,1)S(1)} collective-permute-done((bf16[128,128]{1,0:T(8,128)(2,1)S(1)}, bf16[128,128]{1,0:T(8,128)(2,1)S(1)}, u32[]{:S(2)}, u32[]{:S(2)}) %collective-permute-start.17) | collective-permute-done | bytes 32800 | tf_op jit(solution)/shard_map/ppermute | solution.py:372
  36.1 0.4 shard_map.83
  36.5 1.3 %collective-permute-start.20 = (bf16[128,128]{1,0:T(8,128)(2,1)S(1)}, bf16[128,128]{1,0:T(8,128)(2,1)S(1)}, u32[]{:S(2)}, u32[]{:S(2)}) collective-permute-start(bf16[128,128]{1,0:T(8,128)(2,1)S(1)} %get-tuple-element.132), channel_id=1, source_target_pairs={{0,16},{1,2},{2,1},{3,19},{4,20},{5,21},{6,22},{7,8},{8,7},{9,10},... | collective-permute-start | bytes 98312 | tf_op jit(solution)/shard_map/ppermute | solution.py:372
  37.8 1.7 %collective-permute-start.21 = (bf16[128,128]{1,0:T(8,128)(2,1)S(1)}, bf16[128,128]{1,0:T(8,128)(2,1)S(1)}, u32[]{:S(2)}, u32[]{:S(2)}) collective-permute-start(bf16[128,128]{1,0:T(8,128)(2,1)S(1)} %get-tuple-element.133), channel_id=1, source_target_pairs={{0,3},{1,17},{2,18},{3,0},{4,13},{5,6},{6,5},{7,23},{8,24},{9,25},... | collective-permute-start | bytes 98312 | tf_op jit(solution)/shard_map/ppermute | solution.py:372
  39.5 0.5 collective-permute-start.23
  40.0 1.3 %shard_map.84 = (f32[128,1024]{1,0:T(8,128)S(1)}, f32[128,384]{1,0:T(8,128)S(1)}) custom-call(bf16[128,128]{1,0:T(8,128)(2,1)S(1)} %collective-permute-done.16.refs_0_, bf16[128,128]{1,0:T(8,128)(2,1)S(1)} %collective-permute-done.17.refs_1_, bf16[128,128]{1,0:T(8,128)(2,1)S(1)} %collective-permute-done.18.refs_2_, ...), custom_call_target="tpu_custom_call" | custom-call | flops 469762048 | bytes 5738496 | tf_op jit(solution)/shard_map/pallas_call | solution.py:337
  41.3 0.4 collective-permute-done.20.refs_0_
  41.7 0.9 %collective-permute-done.21.refs_1_ = bf16[128,128]{1,0:T(8,128)(2,1)S(1)} collective-permute-done((bf16[128,128]{1,0:T(8,128)(2,1)S(1)}, bf16[128,128]{1,0:T(8,128)(2,1)S(1)}, u32[]{:S(2)}, u32[]{:S(2)}) %collective-permute-start.21) | collective-permute-done | bytes 32800 | tf_op jit(solution)/shard_map/ppermute | solution.py:372
  43.0 1.3 %collective-permute-start.24 = (bf16[128,128]{1,0:T(8,128)(2,1)S(1)}, bf16[128,128]{1,0:T(8,128)(2,1)S(1)}, u32[]{:S(2)}, u32[]{:S(2)}) collective-permute-start(bf16[128,128]{1,0:T(8,128)(2,1)S(1)} %get-tuple-element.140), channel_id=1, source_target_pairs={{0,16},{1,2},{2,1},{3,19},{4,20},{5,21},{6,22},{7,8},{8,7},{9,10},... | collective-permute-start | bytes 98312 | tf_op jit(solution)/shard_map/ppermute | solution.py:372
  44.3 1.9 %collective-permute-start.25 = (bf16[128,128]{1,0:T(8,128)(2,1)S(1)}, bf16[128,128]{1,0:T(8,128)(2,1)S(1)}, u32[]{:S(2)}, u32[]{:S(2)}) collective-permute-start(bf16[128,128]{1,0:T(8,128)(2,1)S(1)} %get-tuple-element.141), channel_id=1, source_target_pairs={{0,3},{1,17},{2,18},{3,0},{4,13},{5,6},{6,5},{7,23},{8,24},{9,25},... | collective-permute-start | bytes 98312 | tf_op jit(solution)/shard_map/ppermute | solution.py:372
  46.2 0.5 collective-permute-start.27
  46.7 1.0 %shard_map.86 = (f32[128,1024]{1,0:T(8,128)S(1)}, f32[128,1024]{1,0:T(8,128)S(1)}, f32[128,384]{1,0:T(8,128)S(1)}) custom-call(bf16[128,128]{1,0:T(8,128)(2,1)S(1)} %collective-permute-done.20.refs_0_, bf16[128,128]{1,0:T(8,128)(2,1)S(1)} %collective-permute-done.21.refs_1_, bf16[128,128]{1,0:T(8,128)(2,1)S(1)} %collective-permute-done.22.refs_2_, ...), custom_call_target="tpu_custom_call" | custom-call | flops 469762048 | bytes 5902336 | tf_op jit(solution)/shard_map/pallas_call | solution.py:337
  47.7 0.6 %collective-permute-done.24.refs_0_ = bf16[128,128]{1,0:T(8,128)(2,1)S(1)} collective-permute-done((bf16[128,128]{1,0:T(8,128)(2,1)S(1)}, bf16[128,128]{1,0:T(8,128)(2,1)S(1)}, u32[]{:S(2)}, u32[]{:S(2)}) %collective-permute-start.24) | collective-permute-done | bytes 32800 | tf_op jit(solution)/shard_map/ppermute | solution.py:372
  48.2 0.9 %collective-permute-done.25.refs_1_ = bf16[128,128]{1,0:T(8,128)(2,1)S(1)} collective-permute-done((bf16[128,128]{1,0:T(8,128)(2,1)S(1)}, bf16[128,128]{1,0:T(8,128)(2,1)S(1)}, u32[]{:S(2)}, u32[]{:S(2)}) %collective-permute-start.25) | collective-permute-done | bytes 32800 | tf_op jit(solution)/shard_map/ppermute | solution.py:372
  49.5 1.3 %collective-permute-start.28 = (bf16[128,128]{1,0:T(8,128)(2,1)S(1)}, bf16[128,128]{1,0:T(8,128)(2,1)S(1)}, u32[]{:S(2)}, u32[]{:S(2)}) collective-permute-start(bf16[128,128]{1,0:T(8,128)(2,1)S(1)} %get-tuple-element.147), channel_id=1, source_target_pairs={{0,16},{1,2},{2,1},{3,19},{4,20},{5,21},{6,22},{7,8},{8,7},{9,10},... | collective-permute-start | bytes 98312 | tf_op jit(solution)/shard_map/ppermute | solution.py:372
  50.8 1.7 %collective-permute-start.29 = (bf16[128,128]{1,0:T(8,128)(2,1)S(1)}, bf16[128,128]{1,0:T(8,128)(2,1)S(1)}, u32[]{:S(2)}, u32[]{:S(2)}) collective-permute-start(bf16[128,128]{1,0:T(8,128)(2,1)S(1)} %get-tuple-element.148), channel_id=1, source_target_pairs={{0,3},{1,17},{2,18},{3,0},{4,13},{5,6},{6,5},{7,23},{8,24},{9,25},... | collective-permute-start | bytes 98312 | tf_op jit(solution)/shard_map/ppermute | solution.py:372
  52.5 0.5 collective-permute-start.31
  53.0 1.2 %shard_map.88.refs_5_ = f32[1024,128]{1,0:T(8,128)S(1)} custom-call(bf16[128,128]{1,0:T(8,128)(2,1)S(1)} %collective-permute-done.24.refs_0_, bf16[128,128]{1,0:T(8,128)(2,1)S(1)} %collective-permute-done.25.refs_1_, bf16[128,128]{1,0:T(8,128)(2,1)S(1)} %collective-permute-done.26.refs_2_, bf16[128,128]{1,0:T(8,128)(2,1)S(1)} %collective-permute-done.27.refs_3_, ...), custom_call_target="tpu_custom_call" | custom-call | flops 369098752 | bytes 4624384 | tf_op jit(solution)/shard_map/pallas_call | solution.py:337
  54.2 0.5 collective-permute-done.28.refs_0_
  54.7 0.9 %collective-permute-done.29.refs_1_ = bf16[128,128]{1,0:T(8,128)(2,1)S(1)} collective-permute-done((bf16[128,128]{1,0:T(8,128)(2,1)S(1)}, bf16[128,128]{1,0:T(8,128)(2,1)S(1)}, u32[]{:S(2)}, u32[]{:S(2)}) %collective-permute-start.29) | collective-permute-done | bytes 32800 | tf_op jit(solution)/shard_map/ppermute | solution.py:372
  55.6 1.1 %shard_map.89 = f32[1,1024,128]{2,1,0:T(8,128)} custom-call(bf16[128,128]{1,0:T(8,128)(2,1)S(1)} %collective-permute-done.28.refs_0_, bf16[128,128]{1,0:T(8,128)(2,1)S(1)} %collective-permute-done.29.refs_1_, bf16[128,128]{1,0:T(8,128)(2,1)S(1)} %collective-permute-done.30.refs_2_, bf16[128,128]{1,0:T(8,128)(2,1)S(1)} %collective-permute-done.31.refs_3_, ...), custom_call_target="tpu_custom_call" | custom-call | flops 100663296 | bytes 1966080 | tf_op jit(solution)/shard_map/pallas_call | solution.py:337
  (33 shorter events, 2.5 us)
Async XLA Ops:
  1.8 7.4 %collective-permute-start = (bf16[128,128]{1,0:T(8,128)(2,1)S(1)}, bf16[128,128]{1,0:T(8,128)(2,1)S(1)}, u32[]{:S(2)}, u32[]{:S(2)}) collective-permute-start(bf16[128,128]{1,0:T(8,128)(2,1)S(1)} %get-tuple-element.79), channel_id=1, source_target_pairs={{0,16},{1,2},{2,1},{3,19},{4,5},{5,4},{6,15},{7,23},{8,24},{9,25},... | collective-permute-start | bytes 98312 | tf_op jit(solution)/shard_map/ppermute | solution.py:372
  4.4 5.4 %collective-permute-start.1 = (bf16[128,128]{1,0:T(8,128)(2,1)S(1)}, bf16[128,128]{1,0:T(8,128)(2,1)S(1)}, u32[]{:S(2)}, u32[]{:S(2)}) collective-permute-start(bf16[128,128]{1,0:T(8,128)(2,1)S(1)} %get-tuple-element.80), channel_id=1, source_target_pairs={{0,2},{1,17},{2,0},{3,4},{4,3},{5,6},{6,5},{7,8},{8,7},{9,10},{10,... | collective-permute-start | bytes 98312 | tf_op jit(solution)/shard_map/ppermute | solution.py:372
  5.9 3.9 %collective-permute-start.2 = (bf16[128,128]{1,0:T(8,128)(2,1)S(1)}, bf16[128,128]{1,0:T(8,128)(2,1)S(1)}, u32[]{:S(2)}, u32[]{:S(2)}) collective-permute-start(bf16[128,128]{1,0:T(8,128)(2,1)S(1)} %get-tuple-element.81), channel_id=1, source_target_pairs={{0,1},{1,0},{2,18},{3,7},{4,20},{5,21},{6,22},{7,3},{8,9},{9,8},{1... | collective-permute-start | bytes 98312 | tf_op jit(solution)/shard_map/ppermute | solution.py:372
  6.0 3.8 %collective-permute-start.3 = (bf16[128,128]{1,0:T(8,128)(2,1)S(1)}, bf16[128,128]{1,0:T(8,128)(2,1)S(1)}, u32[]{:S(2)}, u32[]{:S(2)}) collective-permute-start(bf16[128,128]{1,0:T(8,128)(2,1)S(1)} %get-tuple-element.82), channel_id=1, source_target_pairs={{0,1},{1,0},{2,3},{3,2},{4,5},{5,4},{6,7},{7,6},{8,9},{9,8},{10,11... | collective-permute-start | bytes 98312 | tf_op jit(solution)/shard_map/ppermute | solution.py:372
  10.3 5.0 %collective-permute-start.4 = (bf16[128,128]{1,0:T(8,128)(2,1)S(1)}, bf16[128,128]{1,0:T(8,128)(2,1)S(1)}, u32[]{:S(2)}, u32[]{:S(2)}) collective-permute-start(bf16[128,128]{1,0:T(8,128)(2,1)S(1)} %get-tuple-element.94), channel_id=1, source_target_pairs={{0,16},{1,2},{2,1},{3,19},{4,5},{5,4},{6,15},{7,23},{8,24},{9,25},... | collective-permute-start | bytes 98312 | tf_op jit(solution)/shard_map/ppermute | solution.py:372
  10.6 5.1 %collective-permute-start.5 = (bf16[128,128]{1,0:T(8,128)(2,1)S(1)}, bf16[128,128]{1,0:T(8,128)(2,1)S(1)}, u32[]{:S(2)}, u32[]{:S(2)}) collective-permute-start(bf16[128,128]{1,0:T(8,128)(2,1)S(1)} %get-tuple-element.95), channel_id=1, source_target_pairs={{0,2},{1,17},{2,0},{3,4},{4,3},{5,6},{6,5},{7,8},{8,7},{9,10},{10,... | collective-permute-start | bytes 98312 | tf_op jit(solution)/shard_map/ppermute | solution.py:372
  11.7 4.1 %collective-permute-start.6 = (bf16[128,128]{1,0:T(8,128)(2,1)S(1)}, bf16[128,128]{1,0:T(8,128)(2,1)S(1)}, u32[]{:S(2)}, u32[]{:S(2)}) collective-permute-start(bf16[128,128]{1,0:T(8,128)(2,1)S(1)} %get-tuple-element.96), channel_id=1, source_target_pairs={{0,1},{1,0},{2,18},{3,7},{4,20},{5,21},{6,22},{7,3},{8,9},{9,8},{1... | collective-permute-start | bytes 98312 | tf_op jit(solution)/shard_map/ppermute | solution.py:372
  11.8 4.0 %collective-permute-start.7 = (bf16[128,128]{1,0:T(8,128)(2,1)S(1)}, bf16[128,128]{1,0:T(8,128)(2,1)S(1)}, u32[]{:S(2)}, u32[]{:S(2)}) collective-permute-start(bf16[128,128]{1,0:T(8,128)(2,1)S(1)} %get-tuple-element.97), channel_id=1, source_target_pairs={{0,1},{1,0},{2,3},{3,2},{4,5},{5,4},{6,7},{7,6},{8,9},{9,8},{10,11... | collective-permute-start | bytes 98312 | tf_op jit(solution)/shard_map/ppermute | solution.py:372
  16.1 5.6 %collective-permute-start.8 = (bf16[128,128]{1,0:T(8,128)(2,1)S(1)}, bf16[128,128]{1,0:T(8,128)(2,1)S(1)}, u32[]{:S(2)}, u32[]{:S(2)}) collective-permute-start(bf16[128,128]{1,0:T(8,128)(2,1)S(1)} %get-tuple-element.106), channel_id=1, source_target_pairs={{0,16},{1,2},{2,1},{3,19},{4,20},{5,21},{6,22},{7,8},{8,7},{9,10},... | collective-permute-start | bytes 98312 | tf_op jit(solution)/shard_map/ppermute | solution.py:372
  17.6 4.8 %collective-permute-start.9 = (bf16[128,128]{1,0:T(8,128)(2,1)S(1)}, bf16[128,128]{1,0:T(8,128)(2,1)S(1)}, u32[]{:S(2)}, u32[]{:S(2)}) collective-permute-start(bf16[128,128]{1,0:T(8,128)(2,1)S(1)} %get-tuple-element.107), channel_id=1, source_target_pairs={{0,3},{1,17},{2,18},{3,0},{4,13},{5,6},{6,5},{7,23},{8,24},{9,25},... | collective-permute-start | bytes 98312 | tf_op jit(solution)/shard_map/ppermute | solution.py:372
  20.2 2.3 %collective-permute-start.10 = (bf16[128,128]{1,0:T(8,128)(2,1)S(1)}, bf16[128,128]{1,0:T(8,128)(2,1)S(1)}, u32[]{:S(2)}, u32[]{:S(2)}) collective-permute-start(bf16[128,128]{1,0:T(8,128)(2,1)S(1)} %get-tuple-element.108), channel_id=1, source_target_pairs={{0,1},{1,0},{2,5},{3,4},{4,3},{5,2},{6,7},{7,6},{8,9},{9,8},{10,11... | collective-permute-start | bytes 98312 | tf_op jit(solution)/shard_map/ppermute | solution.py:372
  20.2 2.3 %collective-permute-start.11 = (bf16[128,128]{1,0:T(8,128)(2,1)S(1)}, bf16[128,128]{1,0:T(8,128)(2,1)S(1)}, u32[]{:S(2)}, u32[]{:S(2)}) collective-permute-start(bf16[128,128]{1,0:T(8,128)(2,1)S(1)} %get-tuple-element.109), channel_id=1, source_target_pairs={{0,1},{1,0},{2,3},{3,2},{4,5},{5,4},{6,7},{7,6},{8,9},{9,8},{10,11... | collective-permute-start | bytes 98312 | tf_op jit(solution)/shard_map/ppermute | solution.py:372
  22.8 5.5 %collective-permute-start.12 = (bf16[128,128]{1,0:T(8,128)(2,1)S(1)}, bf16[128,128]{1,0:T(8,128)(2,1)S(1)}, u32[]{:S(2)}, u32[]{:S(2)}) collective-permute-start(bf16[128,128]{1,0:T(8,128)(2,1)S(1)} %get-tuple-element.115), channel_id=1, source_target_pairs={{0,16},{1,2},{2,1},{3,19},{4,20},{5,21},{6,22},{7,8},{8,7},{9,10},... | collective-permute-start | bytes 98312 | tf_op jit(solution)/shard_map/ppermute | solution.py:372
  24.8 4.8 %collective-permute-start.13 = (bf16[128,128]{1,0:T(8,128)(2,1)S(1)}, bf16[128,128]{1,0:T(8,128)(2,1)S(1)}, u32[]{:S(2)}, u32[]{:S(2)}) collective-permute-start(bf16[128,128]{1,0:T(8,128)(2,1)S(1)} %get-tuple-element.116), channel_id=1, source_target_pairs={{0,3},{1,17},{2,18},{3,0},{4,13},{5,6},{6,5},{7,23},{8,24},{9,25},... | collective-permute-start | bytes 98312 | tf_op jit(solution)/shard_map/ppermute | solution.py:372
  26.6 3.1 %collective-permute-start.14 = (bf16[128,128]{1,0:T(8,128)(2,1)S(1)}, bf16[128,128]{1,0:T(8,128)(2,1)S(1)}, u32[]{:S(2)}, u32[]{:S(2)}) collective-permute-start(bf16[128,128]{1,0:T(8,128)(2,1)S(1)} %get-tuple-element.117), channel_id=1, source_target_pairs={{0,1},{1,0},{2,5},{3,4},{4,3},{5,2},{6,7},{7,6},{8,9},{9,8},{10,11... | collective-permute-start | bytes 98312 | tf_op jit(solution)/shard_map/ppermute | solution.py:372
  26.6 3.1 %collective-permute-start.15 = (bf16[128,128]{1,0:T(8,128)(2,1)S(1)}, bf16[128,128]{1,0:T(8,128)(2,1)S(1)}, u32[]{:S(2)}, u32[]{:S(2)}) collective-permute-start(bf16[128,128]{1,0:T(8,128)(2,1)S(1)} %get-tuple-element.118), channel_id=1, source_target_pairs={{0,1},{1,0},{2,3},{3,2},{4,5},{5,4},{6,7},{7,6},{8,9},{9,8},{10,11... | collective-permute-start | bytes 98312 | tf_op jit(solution)/shard_map/ppermute | solution.py:372
  30.1 5.3 %collective-permute-start.16 = (bf16[128,128]{1,0:T(8,128)(2,1)S(1)}, bf16[128,128]{1,0:T(8,128)(2,1)S(1)}, u32[]{:S(2)}, u32[]{:S(2)}) collective-permute-start(bf16[128,128]{1,0:T(8,128)(2,1)S(1)} %get-tuple-element.124), channel_id=1, source_target_pairs={{0,16},{1,2},{2,1},{3,19},{4,20},{5,21},{6,22},{7,8},{8,7},{9,10},... | collective-permute-start | bytes 98312 | tf_op jit(solution)/shard_map/ppermute | solution.py:372
  31.3 4.8 %collective-permute-start.17 = (bf16[128,128]{1,0:T(8,128)(2,1)S(1)}, bf16[128,128]{1,0:T(8,128)(2,1)S(1)}, u32[]{:S(2)}, u32[]{:S(2)}) collective-permute-start(bf16[128,128]{1,0:T(8,128)(2,1)S(1)} %get-tuple-element.125), channel_id=1, source_target_pairs={{0,3},{1,17},{2,18},{3,0},{4,13},{5,6},{6,5},{7,23},{8,24},{9,25},... | collective-permute-start | bytes 98312 | tf_op jit(solution)/shard_map/ppermute | solution.py:372
  33.2 3.0 %collective-permute-start.18 = (bf16[128,128]{1,0:T(8,128)(2,1)S(1)}, bf16[128,128]{1,0:T(8,128)(2,1)S(1)}, u32[]{:S(2)}, u32[]{:S(2)}) collective-permute-start(bf16[128,128]{1,0:T(8,128)(2,1)S(1)} %get-tuple-element.126), channel_id=1, source_target_pairs={{0,1},{1,0},{2,5},{3,4},{4,3},{5,2},{6,7},{7,6},{8,9},{9,8},{10,11... | collective-permute-start | bytes 98312 | tf_op jit(solution)/shard_map/ppermute | solution.py:372
  33.2 3.0 %collective-permute-start.19 = (bf16[128,128]{1,0:T(8,128)(2,1)S(1)}, bf16[128,128]{1,0:T(8,128)(2,1)S(1)}, u32[]{:S(2)}, u32[]{:S(2)}) collective-permute-start(bf16[128,128]{1,0:T(8,128)(2,1)S(1)} %get-tuple-element.127), channel_id=1, source_target_pairs={{0,1},{1,0},{2,3},{3,2},{4,5},{5,4},{6,7},{7,6},{8,9},{9,8},{10,11... | collective-permute-start | bytes 98312 | tf_op jit(solution)/shard_map/ppermute | solution.py:372
  36.5 5.2 %collective-permute-start.20 = (bf16[128,128]{1,0:T(8,128)(2,1)S(1)}, bf16[128,128]{1,0:T(8,128)(2,1)S(1)}, u32[]{:S(2)}, u32[]{:S(2)}) collective-permute-start(bf16[128,128]{1,0:T(8,128)(2,1)S(1)} %get-tuple-element.132), channel_id=1, source_target_pairs={{0,16},{1,2},{2,1},{3,19},{4,20},{5,21},{6,22},{7,8},{8,7},{9,10},... | collective-permute-start | bytes 98312 | tf_op jit(solution)/shard_map/ppermute | solution.py:372
  37.8 4.8 %collective-permute-start.21 = (bf16[128,128]{1,0:T(8,128)(2,1)S(1)}, bf16[128,128]{1,0:T(8,128)(2,1)S(1)}, u32[]{:S(2)}, u32[]{:S(2)}) collective-permute-start(bf16[128,128]{1,0:T(8,128)(2,1)S(1)} %get-tuple-element.133), channel_id=1, source_target_pairs={{0,3},{1,17},{2,18},{3,0},{4,13},{5,6},{6,5},{7,23},{8,24},{9,25},... | collective-permute-start | bytes 98312 | tf_op jit(solution)/shard_map/ppermute | solution.py:372
  39.5 3.1 %collective-permute-start.22 = (bf16[128,128]{1,0:T(8,128)(2,1)S(1)}, bf16[128,128]{1,0:T(8,128)(2,1)S(1)}, u32[]{:S(2)}, u32[]{:S(2)}) collective-permute-start(bf16[128,128]{1,0:T(8,128)(2,1)S(1)} %get-tuple-element.134), channel_id=1, source_target_pairs={{0,1},{1,0},{2,5},{3,4},{4,3},{5,2},{6,7},{7,6},{8,9},{9,8},{10,11... | collective-permute-start | bytes 98312 | tf_op jit(solution)/shard_map/ppermute | solution.py:372
  39.5 3.1 %collective-permute-start.23 = (bf16[128,128]{1,0:T(8,128)(2,1)S(1)}, bf16[128,128]{1,0:T(8,128)(2,1)S(1)}, u32[]{:S(2)}, u32[]{:S(2)}) collective-permute-start(bf16[128,128]{1,0:T(8,128)(2,1)S(1)} %get-tuple-element.135), channel_id=1, source_target_pairs={{0,1},{1,0},{2,3},{3,2},{4,5},{5,4},{6,7},{7,6},{8,9},{9,8},{10,11... | collective-permute-start | bytes 98312 | tf_op jit(solution)/shard_map/ppermute | solution.py:372
  43.0 5.2 %collective-permute-start.24 = (bf16[128,128]{1,0:T(8,128)(2,1)S(1)}, bf16[128,128]{1,0:T(8,128)(2,1)S(1)}, u32[]{:S(2)}, u32[]{:S(2)}) collective-permute-start(bf16[128,128]{1,0:T(8,128)(2,1)S(1)} %get-tuple-element.140), channel_id=1, source_target_pairs={{0,16},{1,2},{2,1},{3,19},{4,20},{5,21},{6,22},{7,8},{8,7},{9,10},... | collective-permute-start | bytes 98312 | tf_op jit(solution)/shard_map/ppermute | solution.py:372
  44.3 4.8 %collective-permute-start.25 = (bf16[128,128]{1,0:T(8,128)(2,1)S(1)}, bf16[128,128]{1,0:T(8,128)(2,1)S(1)}, u32[]{:S(2)}, u32[]{:S(2)}) collective-permute-start(bf16[128,128]{1,0:T(8,128)(2,1)S(1)} %get-tuple-element.141), channel_id=1, source_target_pairs={{0,3},{1,17},{2,18},{3,0},{4,13},{5,6},{6,5},{7,23},{8,24},{9,25},... | collective-permute-start | bytes 98312 | tf_op jit(solution)/shard_map/ppermute | solution.py:372
  46.1 3.0 %collective-permute-start.26 = (bf16[128,128]{1,0:T(8,128)(2,1)S(1)}, bf16[128,128]{1,0:T(8,128)(2,1)S(1)}, u32[]{:S(2)}, u32[]{:S(2)}) collective-permute-start(bf16[128,128]{1,0:T(8,128)(2,1)S(1)} %get-tuple-element.142), channel_id=1, source_target_pairs={{0,1},{1,0},{2,5},{3,4},{4,3},{5,2},{6,7},{7,6},{8,9},{9,8},{10,11... | collective-permute-start | bytes 98312 | tf_op jit(solution)/shard_map/ppermute | solution.py:372
  46.2 3.0 %collective-permute-start.27 = (bf16[128,128]{1,0:T(8,128)(2,1)S(1)}, bf16[128,128]{1,0:T(8,128)(2,1)S(1)}, u32[]{:S(2)}, u32[]{:S(2)}) collective-permute-start(bf16[128,128]{1,0:T(8,128)(2,1)S(1)} %get-tuple-element.143), channel_id=1, source_target_pairs={{0,1},{1,0},{2,3},{3,2},{4,5},{5,4},{6,7},{7,6},{8,9},{9,8},{10,11... | collective-permute-start | bytes 98312 | tf_op jit(solution)/shard_map/ppermute | solution.py:372
  49.5 5.2 %collective-permute-start.28 = (bf16[128,128]{1,0:T(8,128)(2,1)S(1)}, bf16[128,128]{1,0:T(8,128)(2,1)S(1)}, u32[]{:S(2)}, u32[]{:S(2)}) collective-permute-start(bf16[128,128]{1,0:T(8,128)(2,1)S(1)} %get-tuple-element.147), channel_id=1, source_target_pairs={{0,16},{1,2},{2,1},{3,19},{4,20},{5,21},{6,22},{7,8},{8,7},{9,10},... | collective-permute-start | bytes 98312 | tf_op jit(solution)/shard_map/ppermute | solution.py:372
  50.8 4.8 %collective-permute-start.29 = (bf16[128,128]{1,0:T(8,128)(2,1)S(1)}, bf16[128,128]{1,0:T(8,128)(2,1)S(1)}, u32[]{:S(2)}, u32[]{:S(2)}) collective-permute-start(bf16[128,128]{1,0:T(8,128)(2,1)S(1)} %get-tuple-element.148), channel_id=1, source_target_pairs={{0,3},{1,17},{2,18},{3,0},{4,13},{5,6},{6,5},{7,23},{8,24},{9,25},... | collective-permute-start | bytes 98312 | tf_op jit(solution)/shard_map/ppermute | solution.py:372
  52.5 3.1 %collective-permute-start.30 = (bf16[128,128]{1,0:T(8,128)(2,1)S(1)}, bf16[128,128]{1,0:T(8,128)(2,1)S(1)}, u32[]{:S(2)}, u32[]{:S(2)}) collective-permute-start(bf16[128,128]{1,0:T(8,128)(2,1)S(1)} %get-tuple-element.149), channel_id=1, source_target_pairs={{0,1},{1,0},{2,5},{3,4},{4,3},{5,2},{6,7},{7,6},{8,9},{9,8},{10,11... | collective-permute-start | bytes 98312 | tf_op jit(solution)/shard_map/ppermute | solution.py:372
  52.5 3.1 %collective-permute-start.31 = (bf16[128,128]{1,0:T(8,128)(2,1)S(1)}, bf16[128,128]{1,0:T(8,128)(2,1)S(1)}, u32[]{:S(2)}, u32[]{:S(2)}) collective-permute-start(bf16[128,128]{1,0:T(8,128)(2,1)S(1)} %get-tuple-element.150), channel_id=1, source_target_pairs={{0,1},{1,0},{2,3},{3,2},{4,5},{5,4},{6,7},{7,6},{8,9},{9,8},{10,11... | collective-permute-start | bytes 98312 | tf_op jit(solution)/shard_map/ppermute | solution.py:372

commit v19 on v18

--- a/solution.py
+++ b/solution.py
@@ -279,12 +279,11 @@
     arrived_refs, refs = refs[:trips], refs[trips:]
     hot_ref, hot_t_ref, n_ref, s_ref, weight_ref, mask_ref, inner_ref, local_ref, picked_ref = refs[:9]
     state_out_ref, base_ref, s_pick_ref, s_small_ref = refs[9:]
-    state = DAMPING * corrected(links, plan, arrived_refs, hot_ref, n_ref, weight_ref, mask_ref, local_ref)
-    state_out_ref[...] = state
-    s_pick = times(s_ref[0], hot_ref[...]).astype(BF16)
-    s_pick_ref[...] = s_pick
-    s_small_ref[...] = times(hot_t_ref[...], s_pick).astype(BF16)
-    base_ref[...] = picked_ref[...].astype(F32) - times((state * inner_ref[:1]).astype(BF16), s_pick)
+    s_pick_ref[...] = times(s_ref[0], hot_ref[...]).astype(BF16)
+    s_small_ref[...] = times(hot_t_ref[...], s_pick_ref[...]).astype(BF16)
+    state_out_ref[...] = DAMPING * corrected(links, plan, arrived_refs, hot_ref, n_ref, weight_ref, mask_ref, local_ref)
+    inside = (state_out_ref[...] * inner_ref[:1]).astype(BF16)
+    base_ref[...] = picked_ref[...].astype(F32) - times(inside, s_pick_ref[...])
 
 
 def update_kernel(trips, links, plan, *refs):

time: 56.8 us -> 56.8 us (level)
  no operation moved by 1% of the time
where the time goes in v19:
time: 56.8 us; the launch traced here: 56.7 us
  starting transfers between devices  29.6 us (52%)
  Pallas kernels  17 us (30%)
  waiting for transfers between devices  9.26 us (16%)
  between operations  0.82 us (1%)
    ppermute x32, starting transfers between devices, exchange(): lax.ppermute(part, 'sub', route)  29.6 us
    pallas_call x17, Pallas kernels, run(): pl.pallas_call(kernel, out_shape=results, in_specs=[pl.BlockSpec(memory_s...  17 us
    ppermute x32, waiting for transfers between devices, exchange(): lax.ppermute(part, 'sub', route)  9.26 us
  transfers between devices with their start and end apart: 32, of which 13 were waited for; matrix products, arithmetic and copies ran while one was open for 0% of the time, Pallas kernels for 20%

profile of v19, /device:TPU:8, one launch (start us, length us, event | category | flops | bytes accessed | tf_op | source)
XLA Modules:
  0.0 56.7 jit_solution(13817159887351278308)
XLA Ops:
  0.0 1.8 %shard_map.73 = (bf16[1024,384]{1,0:T(8,128)(2,1)S(1)}, bf16[128,1024]{1,0:T(8,128)(2,1)S(1)}, bf16[128,384]{1,0:T(8,128)(2,1)S(1)}, f32[8,384]{1,0:T(8,128)S(1)...) custom-call(s32[1,4,128]{2,1,0:T(4,128)} %rows_in.1, ...), custom_call_target="tpu_custom_call" | custom-call | flops 100663296 | bytes 5769232 | tf_op jit(solution)/shard_map/pallas_call | solution.py:336
  1.8 2.7 %collective-permute-start = (bf16[128,128]{1,0:T(8,128)(2,1)S(1)}, bf16[128,128]{1,0:T(8,128)(2,1)S(1)}, u32[]{:S(2)}, u32[]{:S(2)}) collective-permute-start(bf16[128,128]{1,0:T(8,128)(2,1)S(1)} %get-tuple-element.79), channel_id=1, source_target_pairs={{0,16},{1,2},{2,1},{3,19},{4,5},{5,4},{6,15},{7,23},{8,24},{9,25},... | collective-permute-start | bytes 98312 | tf_op jit(solution)/shard_map/ppermute | solution.py:371
  4.4 1.5 %collective-permute-start.1 = (bf16[128,128]{1,0:T(8,128)(2,1)S(1)}, bf16[128,128]{1,0:T(8,128)(2,1)S(1)}, u32[]{:S(2)}, u32[]{:S(2)}) collective-permute-start(bf16[128,128]{1,0:T(8,128)(2,1)S(1)} %get-tuple-element.80), channel_id=1, source_target_pairs={{0,2},{1,17},{2,0},{3,4},{4,3},{5,6},{6,5},{7,8},{8,7},{9,10},{10,... | collective-permute-start | bytes 98312 | tf_op jit(solution)/shard_map/ppermute | solution.py:371
  6.0 0.4 collective-permute-start.3
  7.1 2.0 %shard_map.74 = (bf16[384,1024]{1,0:T(8,128)(2,1)S(1)}, bf16[384,1024]{1,0:T(8,128)(2,1)S(1)}, bf16[384,384]{1,0:T(8,128)(2,1)S(1)}, bf16[384,384]{1,0:T(8,128)(...) custom-call(bf16[1024,384]{1,0:T(8,128)(2,1)S(1)} %get-tuple-element, ...), custom_call_target="tpu_custom_call" | custom-call | flops 1207959552 | bytes 10330116 | tf_op jit(solution)/shard_map/pallas_call | solution.py:336
  9.1 0.7 %collective-permute-done.1.refs_1_ = bf16[128,128]{1,0:T(8,128)(2,1)S(1)} collective-permute-done((bf16[128,128]{1,0:T(8,128)(2,1)S(1)}, bf16[128,128]{1,0:T(8,128)(2,1)S(1)}, u32[]{:S(2)}, u32[]{:S(2)}) %collective-permute-start.1) | collective-permute-done | bytes 32800 | tf_op jit(solution)/shard_map/ppermute | solution.py:371
  10.6 1.1 %collective-permute-start.5 = (bf16[128,128]{1,0:T(8,128)(2,1)S(1)}, bf16[128,128]{1,0:T(8,128)(2,1)S(1)}, u32[]{:S(2)}, u32[]{:S(2)}) collective-permute-start(bf16[128,128]{1,0:T(8,128)(2,1)S(1)} %get-tuple-element.95), channel_id=1, source_target_pairs={{0,2},{1,17},{2,0},{3,4},{4,3},{5,6},{6,5},{7,8},{8,7},{9,10},{10,... | collective-permute-start | bytes 98312 | tf_op jit(solution)/shard_map/ppermute | solution.py:371
  11.8 0.4 collective-permute-start.7
  12.2 2.7 %shard_map.76 = (f32[128,1024]{1,0:T(8,128)S(1)}, f32[128,384]{1,0:T(8,128)S(1)}, bf16[1024,384]{1,0:T(8,128)(2,1)S(1)}, bf16[384,384]{1,0:T(8,128)(2,1)S(1)}) custom-call(bf16[128,128]{1,0:T(8,128)(2,1)S(1)} %collective-permute-done.refs_0_, bf16[128,128]{1,0:T(8,128)(2,1)S(1)} %collective-permute-done.1.refs_1_, ...), custom_call_target="tpu_custom_call" | custom-call | flops 1577058304 | bytes 8392704 | tf_op jit(solution)/shard_map/pallas_call | solution.py:336
  15.2 0.5 collective-permute-done.5.refs_1_
  15.7 0.4 shard_map.77
  16.1 1.5 %collective-permute-start.8 = (bf16[128,128]{1,0:T(8,128)(2,1)S(1)}, bf16[128,128]{1,0:T(8,128)(2,1)S(1)}, u32[]{:S(2)}, u32[]{:S(2)}) collective-permute-start(bf16[128,128]{1,0:T(8,128)(2,1)S(1)} %get-tuple-element.106), channel_id=1, source_target_pairs={{0,16},{1,2},{2,1},{3,19},{4,20},{5,21},{6,22},{7,8},{8,7},{9,10},... | collective-permute-start | bytes 98312 | tf_op jit(solution)/shard_map/ppermute | solution.py:371
  17.6 2.6 %collective-permute-start.9 = (bf16[128,128]{1,0:T(8,128)(2,1)S(1)}, bf16[128,128]{1,0:T(8,128)(2,1)S(1)}, u32[]{:S(2)}, u32[]{:S(2)}) collective-permute-start(bf16[128,128]{1,0:T(8,128)(2,1)S(1)} %get-tuple-element.107), channel_id=1, source_target_pairs={{0,3},{1,17},{2,18},{3,0},{4,13},{5,6},{6,5},{7,23},{8,24},{9,25},... | collective-permute-start | bytes 98312 | tf_op jit(solution)/shard_map/ppermute | solution.py:371
  20.2 0.5 collective-permute-start.11
  20.7 1.0 %shard_map.78 = (f32[128,1024]{1,0:T(8,128)S(1)}, f32[128,1024]{1,0:T(8,128)S(1)}, f32[128,384]{1,0:T(8,128)S(1)}) custom-call(bf16[128,128]{1,0:T(8,128)(2,1)S(1)} %collective-permute-done.4.refs_0_, bf16[128,128]{1,0:T(8,128)(2,1)S(1)} %collective-permute-done.5.refs_1_, bf16[128,128]{1,0:T(8,128)(2,1)S(1)} %collective-permute-done.6.refs_2_, ...), custom_call_target="tpu_custom_call" | custom-call | flops 469762048 | bytes 5902336 | tf_op jit(solution)/shard_map/pallas_call | solution.py:336
  21.7 0.7 %collective-permute-done.9.refs_1_ = bf16[128,128]{1,0:T(8,128)(2,1)S(1)} collective-permute-done((bf16[128,128]{1,0:T(8,128)(2,1)S(1)}, bf16[128,128]{1,0:T(8,128)(2,1)S(1)}, u32[]{:S(2)}, u32[]{:S(2)}) %collective-permute-start.9) | collective-permute-done | bytes 32800 | tf_op jit(solution)/shard_map/ppermute | solution.py:371
  22.4 0.4 shard_map.79
  22.8 2.0 %collective-permute-start.12 = (bf16[128,128]{1,0:T(8,128)(2,1)S(1)}, bf16[128,128]{1,0:T(8,128)(2,1)S(1)}, u32[]{:S(2)}, u32[]{:S(2)}) collective-permute-start(bf16[128,128]{1,0:T(8,128)(2,1)S(1)} %get-tuple-element.115), channel_id=1, source_target_pairs={{0,16},{1,2},{2,1},{3,19},{4,20},{5,21},{6,22},{7,8},{8,7},{9,10},... | collective-permute-start | bytes 98312 | tf_op jit(solution)/shard_map/ppermute | solution.py:371
  24.8 1.7 %collective-permute-start.13 = (bf16[128,128]{1,0:T(8,128)(2,1)S(1)}, bf16[128,128]{1,0:T(8,128)(2,1)S(1)}, u32[]{:S(2)}, u32[]{:S(2)}) collective-permute-start(bf16[128,128]{1,0:T(8,128)(2,1)S(1)} %get-tuple-element.116), channel_id=1, source_target_pairs={{0,3},{1,17},{2,18},{3,0},{4,13},{5,6},{6,5},{7,23},{8,24},{9,25},... | collective-permute-start | bytes 98312 | tf_op jit(solution)/shard_map/ppermute | solution.py:371
  26.6 0.5 collective-permute-start.15
  27.1 1.2 %shard_map.80 = (f32[128,1024]{1,0:T(8,128)S(1)}, f32[128,384]{1,0:T(8,128)S(1)}) custom-call(bf16[128,128]{1,0:T(8,128)(2,1)S(1)} %collective-permute-done.8.refs_0_, bf16[128,128]{1,0:T(8,128)(2,1)S(1)} %collective-permute-done.9.refs_1_, bf16[128,128]{1,0:T(8,128)(2,1)S(1)} %collective-permute-done.10.refs_2_, ...), custom_call_target="tpu_custom_call" | custom-call | flops 469762048 | bytes 5738496 | tf_op jit(solution)/shard_map/pallas_call | solution.py:336
  28.3 1.3 %collective-permute-done.13.refs_1_ = bf16[128,128]{1,0:T(8,128)(2,1)S(1)} collective-permute-done((bf16[128,128]{1,0:T(8,128)(2,1)S(1)}, bf16[128,128]{1,0:T(8,128)(2,1)S(1)}, u32[]{:S(2)}, u32[]{:S(2)}) %collective-permute-start.13) | collective-permute-done | bytes 32800 | tf_op jit(solution)/shard_map/ppermute | solution.py:371
  30.1 1.3 %collective-permute-start.16 = (bf16[128,128]{1,0:T(8,128)(2,1)S(1)}, bf16[128,128]{1,0:T(8,128)(2,1)S(1)}, u32[]{:S(2)}, u32[]{:S(2)}) collective-permute-start(bf16[128,128]{1,0:T(8,128)(2,1)S(1)} %get-tuple-element.124), channel_id=1, source_target_pairs={{0,16},{1,2},{2,1},{3,19},{4,20},{5,21},{6,22},{7,8},{8,7},{9,10},... | collective-permute-start | bytes 98312 | tf_op jit(solution)/shard_map/ppermute | solution.py:371
  31.3 1.9 %collective-permute-start.17 = (bf16[128,128]{1,0:T(8,128)(2,1)S(1)}, bf16[128,128]{1,0:T(8,128)(2,1)S(1)}, u32[]{:S(2)}, u32[]{:S(2)}) collective-permute-start(bf16[128,128]{1,0:T(8,128)(2,1)S(1)} %get-tuple-element.125), channel_id=1, source_target_pairs={{0,3},{1,17},{2,18},{3,0},{4,13},{5,6},{6,5},{7,23},{8,24},{9,25},... | collective-permute-start | bytes 98312 | tf_op jit(solution)/shard_map/ppermute | solution.py:371
  33.2 0.5 collective-permute-start.19
  33.7 1.0 %shard_map.82 = (f32[128,1024]{1,0:T(8,128)S(1)}, f32[128,1024]{1,0:T(8,128)S(1)}, f32[128,384]{1,0:T(8,128)S(1)}) custom-call(bf16[128,128]{1,0:T(8,128)(2,1)S(1)} %collective-permute-done.12.refs_0_, bf16[128,128]{1,0:T(8,128)(2,1)S(1)} %collective-permute-done.13.refs_1_, bf16[128,128]{1,0:T(8,128)(2,1)S(1)} %collective-permute-done.14.refs_2_, ...), custom_call_target="tpu_custom_call" | custom-call | flops 469762048 | bytes 5902336 | tf_op jit(solution)/shard_map/pallas_call | solution.py:336
  34.7 0.7 %collective-permute-done.16.refs_0_ = bf16[128,128]{1,0:T(8,128)(2,1)S(1)} collective-permute-done((bf16[128,128]{1,0:T(8,128)(2,1)S(1)}, bf16[128,128]{1,0:T(8,128)(2,1)S(1)}, u32[]{:S(2)}, u32[]{:S(2)}) %collective-permute-start.16) | collective-permute-done | bytes 32800 | tf_op jit(solution)/shard_map/ppermute | solution.py:371
  35.4 0.8 %collective-permute-done.17.refs_1_ = bf16[128,128]{1,0:T(8,128)(2,1)S(1)} collective-permute-done((bf16[128,128]{1,0:T(8,128)(2,1)S(1)}, bf16[128,128]{1,0:T(8,128)(2,1)S(1)}, u32[]{:S(2)}, u32[]{:S(2)}) %collective-permute-start.17) | collective-permute-done | bytes 32800 | tf_op jit(solution)/shard_map/ppermute | solution.py:371
  36.1 0.4 shard_map.83
  36.5 1.3 %collective-permute-start.20 = (bf16[128,128]{1,0:T(8,128)(2,1)S(1)}, bf16[128,128]{1,0:T(8,128)(2,1)S(1)}, u32[]{:S(2)}, u32[]{:S(2)}) collective-permute-start(bf16[128,128]{1,0:T(8,128)(2,1)S(1)} %get-tuple-element.132), channel_id=1, source_target_pairs={{0,16},{1,2},{2,1},{3,19},{4,20},{5,21},{6,22},{7,8},{8,7},{9,10},... | collective-permute-start | bytes 98312 | tf_op jit(solution)/shard_map/ppermute | solution.py:371
  37.8 1.7 %collective-permute-start.21 = (bf16[128,128]{1,0:T(8,128)(2,1)S(1)}, bf16[128,128]{1,0:T(8,128)(2,1)S(1)}, u32[]{:S(2)}, u32[]{:S(2)}) collective-permute-start(bf16[128,128]{1,0:T(8,128)(2,1)S(1)} %get-tuple-element.133), channel_id=1, source_target_pairs={{0,3},{1,17},{2,18},{3,0},{4,13},{5,6},{6,5},{7,23},{8,24},{9,25},... | collective-permute-start | bytes 98312 | tf_op jit(solution)/shard_map/ppermute | solution.py:371
  39.5 0.5 collective-permute-start.23
  40.0 1.3 %shard_map.84 = (f32[128,1024]{1,0:T(8,128)S(1)}, f32[128,384]{1,0:T(8,128)S(1)}) custom-call(bf16[128,128]{1,0:T(8,128)(2,1)S(1)} %collective-permute-done.16.refs_0_, bf16[128,128]{1,0:T(8,128)(2,1)S(1)} %collective-permute-done.17.refs_1_, bf16[128,128]{1,0:T(8,128)(2,1)S(1)} %collective-permute-done.18.refs_2_, ...), custom_call_target="tpu_custom_call" | custom-call | flops 469762048 | bytes 5738496 | tf_op jit(solution)/shard_map/pallas_call | solution.py:336
  41.3 0.4 collective-permute-done.20.refs_0_
  41.7 0.9 %collective-permute-done.21.refs_1_ = bf16[128,128]{1,0:T(8,128)(2,1)S(1)} collective-permute-done((bf16[128,128]{1,0:T(8,128)(2,1)S(1)}, bf16[128,128]{1,0:T(8,128)(2,1)S(1)}, u32[]{:S(2)}, u32[]{:S(2)}) %collective-permute-start.21) | collective-permute-done | bytes 32800 | tf_op jit(solution)/shard_map/ppermute | solution.py:371
  43.0 1.3 %collective-permute-start.24 = (bf16[128,128]{1,0:T(8,128)(2,1)S(1)}, bf16[128,128]{1,0:T(8,128)(2,1)S(1)}, u32[]{:S(2)}, u32[]{:S(2)}) collective-permute-start(bf16[128,128]{1,0:T(8,128)(2,1)S(1)} %get-tuple-element.140), channel_id=1, source_target_pairs={{0,16},{1,2},{2,1},{3,19},{4,20},{5,21},{6,22},{7,8},{8,7},{9,10},... | collective-permute-start | bytes 98312 | tf_op jit(solution)/shard_map/ppermute | solution.py:371
  44.3 1.9 %collective-permute-start.25 = (bf16[128,128]{1,0:T(8,128)(2,1)S(1)}, bf16[128,128]{1,0:T(8,128)(2,1)S(1)}, u32[]{:S(2)}, u32[]{:S(2)}) collective-permute-start(bf16[128,128]{1,0:T(8,128)(2,1)S(1)} %get-tuple-element.141), channel_id=1, source_target_pairs={{0,3},{1,17},{2,18},{3,0},{4,13},{5,6},{6,5},{7,23},{8,24},{9,25},... | collective-permute-start | bytes 98312 | tf_op jit(solution)/shard_map/ppermute | solution.py:371
  46.2 0.5 collective-permute-start.27
  46.7 1.0 %shard_map.86 = (f32[128,1024]{1,0:T(8,128)S(1)}, f32[128,1024]{1,0:T(8,128)S(1)}, f32[128,384]{1,0:T(8,128)S(1)}) custom-call(bf16[128,128]{1,0:T(8,128)(2,1)S(1)} %collective-permute-done.20.refs_0_, bf16[128,128]{1,0:T(8,128)(2,1)S(1)} %collective-permute-done.21.refs_1_, bf16[128,128]{1,0:T(8,128)(2,1)S(1)} %collective-permute-done.22.refs_2_, ...), custom_call_target="tpu_custom_call" | custom-call | flops 469762048 | bytes 5902336 | tf_op jit(solution)/shard_map/pallas_call | solution.py:336
  47.7 0.6 %collective-permute-done.24.refs_0_ = bf16[128,128]{1,0:T(8,128)(2,1)S(1)} collective-permute-done((bf16[128,128]{1,0:T(8,128)(2,1)S(1)}, bf16[128,128]{1,0:T(8,128)(2,1)S(1)}, u32[]{:S(2)}, u32[]{:S(2)}) %collective-permute-start.24) | collective-permute-done | bytes 32800 | tf_op jit(solution)/shard_map/ppermute | solution.py:371
  48.2 0.9 %collective-permute-done.25.refs_1_ = bf16[128,128]{1,0:T(8,128)(2,1)S(1)} collective-permute-done((bf16[128,128]{1,0:T(8,128)(2,1)S(1)}, bf16[128,128]{1,0:T(8,128)(2,1)S(1)}, u32[]{:S(2)}, u32[]{:S(2)}) %collective-permute-start.25) | collective-permute-done | bytes 32800 | tf_op jit(solution)/shard_map/ppermute | solution.py:371
  49.5 1.3 %collective-permute-start.28 = (bf16[128,128]{1,0:T(8,128)(2,1)S(1)}, bf16[128,128]{1,0:T(8,128)(2,1)S(1)}, u32[]{:S(2)}, u32[]{:S(2)}) collective-permute-start(bf16[128,128]{1,0:T(8,128)(2,1)S(1)} %get-tuple-element.147), channel_id=1, source_target_pairs={{0,16},{1,2},{2,1},{3,19},{4,20},{5,21},{6,22},{7,8},{8,7},{9,10},... | collective-permute-start | bytes 98312 | tf_op jit(solution)/shard_map/ppermute | solution.py:371
  50.8 1.7 %collective-permute-start.29 = (bf16[128,128]{1,0:T(8,128)(2,1)S(1)}, bf16[128,128]{1,0:T(8,128)(2,1)S(1)}, u32[]{:S(2)}, u32[]{:S(2)}) collective-permute-start(bf16[128,128]{1,0:T(8,128)(2,1)S(1)} %get-tuple-element.148), channel_id=1, source_target_pairs={{0,3},{1,17},{2,18},{3,0},{4,13},{5,6},{6,5},{7,23},{8,24},{9,25},... | collective-permute-start | bytes 98312 | tf_op jit(solution)/shard_map/ppermute | solution.py:371
  52.5 0.5 collective-permute-start.31
  53.0 1.2 %shard_map.88.refs_5_ = f32[1024,128]{1,0:T(8,128)S(1)} custom-call(bf16[128,128]{1,0:T(8,128)(2,1)S(1)} %collective-permute-done.24.refs_0_, bf16[128,128]{1,0:T(8,128)(2,1)S(1)} %collective-permute-done.25.refs_1_, bf16[128,128]{1,0:T(8,128)(2,1)S(1)} %collective-permute-done.26.refs_2_, bf16[128,128]{1,0:T(8,128)(2,1)S(1)} %collective-permute-done.27.refs_3_, ...), custom_call_target="tpu_custom_call" | custom-call | flops 369098752 | bytes 4624384 | tf_op jit(solution)/shard_map/pallas_call | solution.py:336
  54.2 0.5 collective-permute-done.28.refs_0_
  54.7 0.9 %collective-permute-done.29.refs_1_ = bf16[128,128]{1,0:T(8,128)(2,1)S(1)} collective-permute-done((bf16[128,128]{1,0:T(8,128)(2,1)S(1)}, bf16[128,128]{1,0:T(8,128)(2,1)S(1)}, u32[]{:S(2)}, u32[]{:S(2)}) %collective-permute-start.29) | collective-permute-done | bytes 32800 | tf_op jit(solution)/shard_map/ppermute | solution.py:371
  55.6 1.1 %shard_map.89 = f32[1,1024,128]{2,1,0:T(8,128)} custom-call(bf16[128,128]{1,0:T(8,128)(2,1)S(1)} %collective-permute-done.28.refs_0_, bf16[128,128]{1,0:T(8,128)(2,1)S(1)} %collective-permute-done.29.refs_1_, bf16[128,128]{1,0:T(8,128)(2,1)S(1)} %collective-permute-done.30.refs_2_, bf16[128,128]{1,0:T(8,128)(2,1)S(1)} %collective-permute-done.31.refs_3_, ...), custom_call_target="tpu_custom_call" | custom-call | flops 100663296 | bytes 1966080 | tf_op jit(solution)/shard_map/pallas_call | solution.py:336
  (33 shorter events, 2.5 us)
Async XLA Ops:
  1.8 7.4 %collective-permute-start = (bf16[128,128]{1,0:T(8,128)(2,1)S(1)}, bf16[128,128]{1,0:T(8,128)(2,1)S(1)}, u32[]{:S(2)}, u32[]{:S(2)}) collective-permute-start(bf16[128,128]{1,0:T(8,128)(2,1)S(1)} %get-tuple-element.79), channel_id=1, source_target_pairs={{0,16},{1,2},{2,1},{3,19},{4,5},{5,4},{6,15},{7,23},{8,24},{9,25},... | collective-permute-start | bytes 98312 | tf_op jit(solution)/shard_map/ppermute | solution.py:371
  4.4 5.4 %collective-permute-start.1 = (bf16[128,128]{1,0:T(8,128)(2,1)S(1)}, bf16[128,128]{1,0:T(8,128)(2,1)S(1)}, u32[]{:S(2)}, u32[]{:S(2)}) collective-permute-start(bf16[128,128]{1,0:T(8,128)(2,1)S(1)} %get-tuple-element.80), channel_id=1, source_target_pairs={{0,2},{1,17},{2,0},{3,4},{4,3},{5,6},{6,5},{7,8},{8,7},{9,10},{10,... | collective-permute-start | bytes 98312 | tf_op jit(solution)/shard_map/ppermute | solution.py:371
  5.9 3.9 %collective-permute-start.2 = (bf16[128,128]{1,0:T(8,128)(2,1)S(1)}, bf16[128,128]{1,0:T(8,128)(2,1)S(1)}, u32[]{:S(2)}, u32[]{:S(2)}) collective-permute-start(bf16[128,128]{1,0:T(8,128)(2,1)S(1)} %get-tuple-element.81), channel_id=1, source_target_pairs={{0,1},{1,0},{2,18},{3,7},{4,20},{5,21},{6,22},{7,3},{8,9},{9,8},{1... | collective-permute-start | bytes 98312 | tf_op jit(solution)/shard_map/ppermute | solution.py:371
  6.0 3.8 %collective-permute-start.3 = (bf16[128,128]{1,0:T(8,128)(2,1)S(1)}, bf16[128,128]{1,0:T(8,128)(2,1)S(1)}, u32[]{:S(2)}, u32[]{:S(2)}) collective-permute-start(bf16[128,128]{1,0:T(8,128)(2,1)S(1)} %get-tuple-element.82), channel_id=1, source_target_pairs={{0,1},{1,0},{2,3},{3,2},{4,5},{5,4},{6,7},{7,6},{8,9},{9,8},{10,11... | collective-permute-start | bytes 98312 | tf_op jit(solution)/shard_map/ppermute | solution.py:371
  10.3 5.0 %collective-permute-start.4 = (bf16[128,128]{1,0:T(8,128)(2,1)S(1)}, bf16[128,128]{1,0:T(8,128)(2,1)S(1)}, u32[]{:S(2)}, u32[]{:S(2)}) collective-permute-start(bf16[128,128]{1,0:T(8,128)(2,1)S(1)} %get-tuple-element.94), channel_id=1, source_target_pairs={{0,16},{1,2},{2,1},{3,19},{4,5},{5,4},{6,15},{7,23},{8,24},{9,25},... | collective-permute-start | bytes 98312 | tf_op jit(solution)/shard_map/ppermute | solution.py:371
  10.6 5.1 %collective-permute-start.5 = (bf16[128,128]{1,0:T(8,128)(2,1)S(1)}, bf16[128,128]{1,0:T(8,128)(2,1)S(1)}, u32[]{:S(2)}, u32[]{:S(2)}) collective-permute-start(bf16[128,128]{1,0:T(8,128)(2,1)S(1)} %get-tuple-element.95), channel_id=1, source_target_pairs={{0,2},{1,17},{2,0},{3,4},{4,3},{5,6},{6,5},{7,8},{8,7},{9,10},{10,... | collective-permute-start | bytes 98312 | tf_op jit(solution)/shard_map/ppermute | solution.py:371
  11.7 4.1 %collective-permute-start.6 = (bf16[128,128]{1,0:T(8,128)(2,1)S(1)}, bf16[128,128]{1,0:T(8,128)(2,1)S(1)}, u32[]{:S(2)}, u32[]{:S(2)}) collective-permute-start(bf16[128,128]{1,0:T(8,128)(2,1)S(1)} %get-tuple-element.96), channel_id=1, source_target_pairs={{0,1},{1,0},{2,18},{3,7},{4,20},{5,21},{6,22},{7,3},{8,9},{9,8},{1... | collective-permute-start | bytes 98312 | tf_op jit(solution)/shard_map/ppermute | solution.py:371
  11.8 4.0 %collective-permute-start.7 = (bf16[128,128]{1,0:T(8,128)(2,1)S(1)}, bf16[128,128]{1,0:T(8,128)(2,1)S(1)}, u32[]{:S(2)}, u32[]{:S(2)}) collective-permute-start(bf16[128,128]{1,0:T(8,128)(2,1)S(1)} %get-tuple-element.97), channel_id=1, source_target_pairs={{0,1},{1,0},{2,3},{3,2},{4,5},{5,4},{6,7},{7,6},{8,9},{9,8},{10,11... | collective-permute-start | bytes 98312 | tf_op jit(solution)/shard_map/ppermute | solution.py:371
  16.1 5.6 %collective-permute-start.8 = (bf16[128,128]{1,0:T(8,128)(2,1)S(1)}, bf16[128,128]{1,0:T(8,128)(2,1)S(1)}, u32[]{:S(2)}, u32[]{:S(2)}) collective-permute-start(bf16[128,128]{1,0:T(8,128)(2,1)S(1)} %get-tuple-element.106), channel_id=1, source_target_pairs={{0,16},{1,2},{2,1},{3,19},{4,20},{5,21},{6,22},{7,8},{8,7},{9,10},... | collective-permute-start | bytes 98312 | tf_op jit(solution)/shard_map/ppermute | solution.py:371
  17.6 4.8 %collective-permute-start.9 = (bf16[128,128]{1,0:T(8,128)(2,1)S(1)}, bf16[128,128]{1,0:T(8,128)(2,1)S(1)}, u32[]{:S(2)}, u32[]{:S(2)}) collective-permute-start(bf16[128,128]{1,0:T(8,128)(2,1)S(1)} %get-tuple-element.107), channel_id=1, source_target_pairs={{0,3},{1,17},{2,18},{3,0},{4,13},{5,6},{6,5},{7,23},{8,24},{9,25},... | collective-permute-start | bytes 98312 | tf_op jit(solution)/shard_map/ppermute | solution.py:371
  20.2 2.3 %collective-permute-start.10 = (bf16[128,128]{1,0:T(8,128)(2,1)S(1)}, bf16[128,128]{1,0:T(8,128)(2,1)S(1)}, u32[]{:S(2)}, u32[]{:S(2)}) collective-permute-start(bf16[128,128]{1,0:T(8,128)(2,1)S(1)} %get-tuple-element.108), channel_id=1, source_target_pairs={{0,1},{1,0},{2,5},{3,4},{4,3},{5,2},{6,7},{7,6},{8,9},{9,8},{10,11... | collective-permute-start | bytes 98312 | tf_op jit(solution)/shard_map/ppermute | solution.py:371
  20.2 2.3 %collective-permute-start.11 = (bf16[128,128]{1,0:T(8,128)(2,1)S(1)}, bf16[128,128]{1,0:T(8,128)(2,1)S(1)}, u32[]{:S(2)}, u32[]{:S(2)}) collective-permute-start(bf16[128,128]{1,0:T(8,128)(2,1)S(1)} %get-tuple-element.109), channel_id=1, source_target_pairs={{0,1},{1,0},{2,3},{3,2},{4,5},{5,4},{6,7},{7,6},{8,9},{9,8},{10,11... | collective-permute-start | bytes 98312 | tf_op jit(solution)/shard_map/ppermute | solution.py:371
  22.8 5.5 %collective-permute-start.12 = (bf16[128,128]{1,0:T(8,128)(2,1)S(1)}, bf16[128,128]{1,0:T(8,128)(2,1)S(1)}, u32[]{:S(2)}, u32[]{:S(2)}) collective-permute-start(bf16[128,128]{1,0:T(8,128)(2,1)S(1)} %get-tuple-element.115), channel_id=1, source_target_pairs={{0,16},{1,2},{2,1},{3,19},{4,20},{5,21},{6,22},{7,8},{8,7},{9,10},... | collective-permute-start | bytes 98312 | tf_op jit(solution)/shard_map/ppermute | solution.py:371
  24.8 4.8 %collective-permute-start.13 = (bf16[128,128]{1,0:T(8,128)(2,1)S(1)}, bf16[128,128]{1,0:T(8,128)(2,1)S(1)}, u32[]{:S(2)}, u32[]{:S(2)}) collective-permute-start(bf16[128,128]{1,0:T(8,128)(2,1)S(1)} %get-tuple-element.116), channel_id=1, source_target_pairs={{0,3},{1,17},{2,18},{3,0},{4,13},{5,6},{6,5},{7,23},{8,24},{9,25},... | collective-permute-start | bytes 98312 | tf_op jit(solution)/shard_map/ppermute | solution.py:371
  26.6 3.1 %collective-permute-start.14 = (bf16[128,128]{1,0:T(8,128)(2,1)S(1)}, bf16[128,128]{1,0:T(8,128)(2,1)S(1)}, u32[]{:S(2)}, u32[]{:S(2)}) collective-permute-start(bf16[128,128]{1,0:T(8,128)(2,1)S(1)} %get-tuple-element.117), channel_id=1, source_target_pairs={{0,1},{1,0},{2,5},{3,4},{4,3},{5,2},{6,7},{7,6},{8,9},{9,8},{10,11... | collective-permute-start | bytes 98312 | tf_op jit(solution)/shard_map/ppermute | solution.py:371
  26.6 3.1 %collective-permute-start.15 = (bf16[128,128]{1,0:T(8,128)(2,1)S(1)}, bf16[128,128]{1,0:T(8,128)(2,1)S(1)}, u32[]{:S(2)}, u32[]{:S(2)}) collective-permute-start(bf16[128,128]{1,0:T(8,128)(2,1)S(1)} %get-tuple-element.118), channel_id=1, source_target_pairs={{0,1},{1,0},{2,3},{3,2},{4,5},{5,4},{6,7},{7,6},{8,9},{9,8},{10,11... | collective-permute-start | bytes 98312 | tf_op jit(solution)/shard_map/ppermute | solution.py:371
  30.1 5.3 %collective-permute-start.16 = (bf16[128,128]{1,0:T(8,128)(2,1)S(1)}, bf16[128,128]{1,0:T(8,128)(2,1)S(1)}, u32[]{:S(2)}, u32[]{:S(2)}) collective-permute-start(bf16[128,128]{1,0:T(8,128)(2,1)S(1)} %get-tuple-element.124), channel_id=1, source_target_pairs={{0,16},{1,2},{2,1},{3,19},{4,20},{5,21},{6,22},{7,8},{8,7},{9,10},... | collective-permute-start | bytes 98312 | tf_op jit(solution)/shard_map/ppermute | solution.py:371
  31.3 4.8 %collective-permute-start.17 = (bf16[128,128]{1,0:T(8,128)(2,1)S(1)}, bf16[128,128]{1,0:T(8,128)(2,1)S(1)}, u32[]{:S(2)}, u32[]{:S(2)}) collective-permute-start(bf16[128,128]{1,0:T(8,128)(2,1)S(1)} %get-tuple-element.125), channel_id=1, source_target_pairs={{0,3},{1,17},{2,18},{3,0},{4,13},{5,6},{6,5},{7,23},{8,24},{9,25},... | collective-permute-start | bytes 98312 | tf_op jit(solution)/shard_map/ppermute | solution.py:371
  33.2 3.0 %collective-permute-start.18 = (bf16[128,128]{1,0:T(8,128)(2,1)S(1)}, bf16[128,128]{1,0:T(8,128)(2,1)S(1)}, u32[]{:S(2)}, u32[]{:S(2)}) collective-permute-start(bf16[128,128]{1,0:T(8,128)(2,1)S(1)} %get-tuple-element.126), channel_id=1, source_target_pairs={{0,1},{1,0},{2,5},{3,4},{4,3},{5,2},{6,7},{7,6},{8,9},{9,8},{10,11... | collective-permute-start | bytes 98312 | tf_op jit(solution)/shard_map/ppermute | solution.py:371
  33.2 3.0 %collective-permute-start.19 = (bf16[128,128]{1,0:T(8,128)(2,1)S(1)}, bf16[128,128]{1,0:T(8,128)(2,1)S(1)}, u32[]{:S(2)}, u32[]{:S(2)}) collective-permute-start(bf16[128,128]{1,0:T(8,128)(2,1)S(1)} %get-tuple-element.127), channel_id=1, source_target_pairs={{0,1},{1,0},{2,3},{3,2},{4,5},{5,4},{6,7},{7,6},{8,9},{9,8},{10,11... | collective-permute-start | bytes 98312 | tf_op jit(solution)/shard_map/ppermute | solution.py:371
  36.5 5.2 %collective-permute-start.20 = (bf16[128,128]{1,0:T(8,128)(2,1)S(1)}, bf16[128,128]{1,0:T(8,128)(2,1)S(1)}, u32[]{:S(2)}, u32[]{:S(2)}) collective-permute-start(bf16[128,128]{1,0:T(8,128)(2,1)S(1)} %get-tuple-element.132), channel_id=1, source_target_pairs={{0,16},{1,2},{2,1},{3,19},{4,20},{5,21},{6,22},{7,8},{8,7},{9,10},... | collective-permute-start | bytes 98312 | tf_op jit(solution)/shard_map/ppermute | solution.py:371
  37.8 4.8 %collective-permute-start.21 = (bf16[128,128]{1,0:T(8,128)(2,1)S(1)}, bf16[128,128]{1,0:T(8,128)(2,1)S(1)}, u32[]{:S(2)}, u32[]{:S(2)}) collective-permute-start(bf16[128,128]{1,0:T(8,128)(2,1)S(1)} %get-tuple-element.133), channel_id=1, source_target_pairs={{0,3},{1,17},{2,18},{3,0},{4,13},{5,6},{6,5},{7,23},{8,24},{9,25},... | collective-permute-start | bytes 98312 | tf_op jit(solution)/shard_map/ppermute | solution.py:371
  39.5 3.1 %collective-permute-start.22 = (bf16[128,128]{1,0:T(8,128)(2,1)S(1)}, bf16[128,128]{1,0:T(8,128)(2,1)S(1)}, u32[]{:S(2)}, u32[]{:S(2)}) collective-permute-start(bf16[128,128]{1,0:T(8,128)(2,1)S(1)} %get-tuple-element.134), channel_id=1, source_target_pairs={{0,1},{1,0},{2,5},{3,4},{4,3},{5,2},{6,7},{7,6},{8,9},{9,8},{10,11... | collective-permute-start | bytes 98312 | tf_op jit(solution)/shard_map/ppermute | solution.py:371
  39.5 3.1 %collective-permute-start.23 = (bf16[128,128]{1,0:T(8,128)(2,1)S(1)}, bf16[128,128]{1,0:T(8,128)(2,1)S(1)}, u32[]{:S(2)}, u32[]{:S(2)}) collective-permute-start(bf16[128,128]{1,0:T(8,128)(2,1)S(1)} %get-tuple-element.135), channel_id=1, source_target_pairs={{0,1},{1,0},{2,3},{3,2},{4,5},{5,4},{6,7},{7,6},{8,9},{9,8},{10,11... | collective-permute-start | bytes 98312 | tf_op jit(solution)/shard_map/ppermute | solution.py:371
  43.0 5.2 %collective-permute-start.24 = (bf16[128,128]{1,0:T(8,128)(2,1)S(1)}, bf16[128,128]{1,0:T(8,128)(2,1)S(1)}, u32[]{:S(2)}, u32[]{:S(2)}) collective-permute-start(bf16[128,128]{1,0:T(8,128)(2,1)S(1)} %get-tuple-element.140), channel_id=1, source_target_pairs={{0,16},{1,2},{2,1},{3,19},{4,20},{5,21},{6,22},{7,8},{8,7},{9,10},... | collective-permute-start | bytes 98312 | tf_op jit(solution)/shard_map/ppermute | solution.py:371
  44.3 4.8 %collective-permute-start.25 = (bf16[128,128]{1,0:T(8,128)(2,1)S(1)}, bf16[128,128]{1,0:T(8,128)(2,1)S(1)}, u32[]{:S(2)}, u32[]{:S(2)}) collective-permute-start(bf16[128,128]{1,0:T(8,128)(2,1)S(1)} %get-tuple-element.141), channel_id=1, source_target_pairs={{0,3},{1,17},{2,18},{3,0},{4,13},{5,6},{6,5},{7,23},{8,24},{9,25},... | collective-permute-start | bytes 98312 | tf_op jit(solution)/shard_map/ppermute | solution.py:371
  46.1 3.0 %collective-permute-start.26 = (bf16[128,128]{1,0:T(8,128)(2,1)S(1)}, bf16[128,128]{1,0:T(8,128)(2,1)S(1)}, u32[]{:S(2)}, u32[]{:S(2)}) collective-permute-start(bf16[128,128]{1,0:T(8,128)(2,1)S(1)} %get-tuple-element.142), channel_id=1, source_target_pairs={{0,1},{1,0},{2,5},{3,4},{4,3},{5,2},{6,7},{7,6},{8,9},{9,8},{10,11... | collective-permute-start | bytes 98312 | tf_op jit(solution)/shard_map/ppermute | solution.py:371
  46.2 3.0 %collective-permute-start.27 = (bf16[128,128]{1,0:T(8,128)(2,1)S(1)}, bf16[128,128]{1,0:T(8,128)(2,1)S(1)}, u32[]{:S(2)}, u32[]{:S(2)}) collective-permute-start(bf16[128,128]{1,0:T(8,128)(2,1)S(1)} %get-tuple-element.143), channel_id=1, source_target_pairs={{0,1},{1,0},{2,3},{3,2},{4,5},{5,4},{6,7},{7,6},{8,9},{9,8},{10,11... | collective-permute-start | bytes 98312 | tf_op jit(solution)/shard_map/ppermute | solution.py:371
  49.5 5.2 %collective-permute-start.28 = (bf16[128,128]{1,0:T(8,128)(2,1)S(1)}, bf16[128,128]{1,0:T(8,128)(2,1)S(1)}, u32[]{:S(2)}, u32[]{:S(2)}) collective-permute-start(bf16[128,128]{1,0:T(8,128)(2,1)S(1)} %get-tuple-element.147), channel_id=1, source_target_pairs={{0,16},{1,2},{2,1},{3,19},{4,20},{5,21},{6,22},{7,8},{8,7},{9,10},... | collective-permute-start | bytes 98312 | tf_op jit(solution)/shard_map/ppermute | solution.py:371
  50.8 4.8 %collective-permute-start.29 = (bf16[128,128]{1,0:T(8,128)(2,1)S(1)}, bf16[128,128]{1,0:T(8,128)(2,1)S(1)}, u32[]{:S(2)}, u32[]{:S(2)}) collective-permute-start(bf16[128,128]{1,0:T(8,128)(2,1)S(1)} %get-tuple-element.148), channel_id=1, source_target_pairs={{0,3},{1,17},{2,18},{3,0},{4,13},{5,6},{6,5},{7,23},{8,24},{9,25},... | collective-permute-start | bytes 98312 | tf_op jit(solution)/shard_map/ppermute | solution.py:371
  52.5 3.1 %collective-permute-start.30 = (bf16[128,128]{1,0:T(8,128)(2,1)S(1)}, bf16[128,128]{1,0:T(8,128)(2,1)S(1)}, u32[]{:S(2)}, u32[]{:S(2)}) collective-permute-start(bf16[128,128]{1,0:T(8,128)(2,1)S(1)} %get-tuple-element.149), channel_id=1, source_target_pairs={{0,1},{1,0},{2,5},{3,4},{4,3},{5,2},{6,7},{7,6},{8,9},{9,8},{10,11... | collective-permute-start | bytes 98312 | tf_op jit(solution)/shard_map/ppermute | solution.py:371
  52.5 3.1 %collective-permute-start.31 = (bf16[128,128]{1,0:T(8,128)(2,1)S(1)}, bf16[128,128]{1,0:T(8,128)(2,1)S(1)}, u32[]{:S(2)}, u32[]{:S(2)}) collective-permute-start(bf16[128,128]{1,0:T(8,128)(2,1)S(1)} %get-tuple-element.150), channel_id=1, source_target_pairs={{0,1},{1,0},{2,3},{3,2},{4,5},{5,4},{6,7},{7,6},{8,9},{9,8},{10,11... | collective-permute-start | bytes 98312 | tf_op jit(solution)/shard_map/ppermute | solution.py:371

commit v20 on v18

--- a/solution.py
+++ b/solution.py
@@ -139,7 +139,7 @@
         (near_in, near_ref),
         (rhs_in, rhs_ref),
         (weight_in, weight_ref),
-        (n_in, n_ref),
+        (n_in.at[0, :, pl.ds(0, n_ref.shape[1])], n_ref),
     ]
     copies = [pltpu.make_async_copy(source, target, sems.at[k]) for k, (source, target) in enumerate(pairs)]
     for copy in copies:
@@ -185,6 +185,7 @@
     n_ref,
     weight_ref,
     count_ref,
+    n_in,
     s_in,
     hot_t_ref,
     n_pick_ref,
@@ -195,11 +196,15 @@
     local_ref,
     base_ref,
     row_ref,
+    n_rest_ref,
     s_ref,
-    sem,
+    sems,
 ):
-    copy = pltpu.make_async_copy(s_in, s_ref, sem)
-    copy.start()
+    half = n_rest_ref.shape[1]
+    rest_copy = pltpu.make_async_copy(n_in.at[0, :, pl.ds(half, half)], n_rest_ref, sems.at[0])
+    s_copy = pltpu.make_async_copy(s_in, s_ref, sems.at[1])
+    rest_copy.start()
+    s_copy.start()
     width, total = hot_ref.shape
     weight = weight_ref[...]
     side = 128
@@ -219,7 +224,7 @@
     same_ref[...] = same.astype(BF16)
     inner = jnp.where(jnp.concatenate(hits, 1) > 0.0, 0.0, 1.0)
     inner_ref[...] = jnp.broadcast_to(inner, inner_ref.shape)
-    n_pick_ref[...] = times(hot_t_ref[...], n_ref[0]).astype(BF16)
+    n_pick_ref[:, :half] = times(hot_t_ref[...], n_ref[...]).astype(BF16)
     earlier = lax.broadcasted_iota(jnp.int32, same.shape, 0) < lax.broadcasted_iota(jnp.int32, same.shape, 1)
     repeats = jnp.sum(jnp.where(earlier, same, 0.0), 0, keepdims=True)
     first = jnp.where(repeats > 0.0, 0.0, 1.0)
@@ -232,9 +237,11 @@
     mask_ref[...] = mask
     local = mask[:1] * turned_ref[...].astype(F32)
     local_ref[...] = local
+    rest_copy.wait()
+    n_pick_ref[:, half:] = times(hot_t_ref[...], n_rest_ref[...]).astype(BF16)
     base_ref[...] = times_t((weight * local * inner).astype(BF16), n_pick_ref[...])
     n_small_ref[...] = times(n_pick_ref[...], hot_ref[...]).astype(BF16)
-    copy.wait()
+    s_copy.wait()
 
 
 def update_path_kernel(trips, links, plan, plan_out, step, last, *refs):
@@ -268,18 +275,20 @@
     scatter(links, plan_out, refs, local)
 
 
-def corrected(links, plan, arrived_refs, hot_ref, n_ref, weight_ref, mask_ref, local_ref):
+def corrected(links, plan, arrived_refs, hot_ref, n_ref, n_rest_ref, weight_ref, mask_ref, local_ref):
     weight = weight_ref[...]
     residual = local_ref[...] + times_t(gather(links, plan, arrived_refs), hot_ref[...])
     scaled = (weight * residual).astype(BF16)
-    return mask_ref[:1] * weight * times_t(scaled, n_ref[0])
+    half = n_ref.shape[1]
+    product = times_t(scaled[:, :half], n_ref[...]) + times_t(scaled[:, half:], n_rest_ref[...])
+    return mask_ref[:1] * weight * product
 
 
 def first_update_kernel(trips, links, plan, *refs):
     arrived_refs, refs = refs[:trips], refs[trips:]
-    hot_ref, hot_t_ref, n_ref, s_ref, weight_ref, mask_ref, inner_ref, local_ref, picked_ref = refs[:9]
-    state_out_ref, base_ref, s_pick_ref, s_small_ref = refs[9:]
-    state = DAMPING * corrected(links, plan, arrived_refs, hot_ref, n_ref, weight_ref, mask_ref, local_ref)
+    hot_ref, hot_t_ref, n_ref, n_rest_ref, s_ref, weight_ref, mask_ref, inner_ref, local_ref, picked_ref = refs[:10]
+    state_out_ref, base_ref, s_pick_ref, s_small_ref = refs[10:]
+    state = DAMPING * corrected(links, plan, arrived_refs, hot_ref, n_ref, n_rest_ref, weight_ref, mask_ref, local_ref)
     state_out_ref[...] = state
     s_pick = times(s_ref[0], hot_ref[...]).astype(BF16)
     s_pick_ref[...] = s_pick
@@ -289,17 +298,17 @@
 
 def update_kernel(trips, links, plan, *refs):
     arrived_refs, refs = refs[:trips], refs[trips:]
-    hot_ref, n_ref, weight_ref, mask_ref, inner_ref, local_ref, picked_ref, s_pick_ref, state_ref = refs[:9]
-    state_out_ref, base_ref = refs[9:]
-    state = state_ref[...] + DAMPING * corrected(links, plan, arrived_refs, hot_ref, n_ref, weight_ref, mask_ref, local_ref)
+    hot_ref, n_ref, n_rest_ref, weight_ref, mask_ref, inner_ref, local_ref, picked_ref, s_pick_ref, state_ref = refs[:10]
+    state_out_ref, base_ref = refs[10:]
+    state = state_ref[...] + DAMPING * corrected(links, plan, arrived_refs, hot_ref, n_ref, n_rest_ref, weight_ref, mask_ref, local_ref)
     state_out_ref[...] = state
     base_ref[...] = picked_ref[...].astype(F32) - times((state * inner_ref[:1]).astype(BF16), s_pick_ref[...])
 
 
 def last_update_kernel(trips, links, plan, *refs):
     arrived_refs, refs = refs[:trips], refs[trips:]
-    hot_ref, n_ref, weight_ref, mask_ref, local_ref, state_ref, state_out_ref = refs
-    update = corrected(links, plan, arrived_refs, hot_ref, n_ref, weight_ref, mask_ref, local_ref)
+    hot_ref, n_ref, n_rest_ref, weight_ref, mask_ref, local_ref, state_ref, state_out_ref = refs
+    update = corrected(links, plan, arrived_refs, hot_ref, n_ref, n_rest_ref, weight_ref, mask_ref, local_ref)
     state_out_ref[...] = (state_ref[...] + DAMPING * update).T
 
 
@@ -364,6 +373,7 @@
     full, some = array(leads, width), array(leads, total)
     small = array(total, total, BF16)
     row = array(8, width)
+    half = array(width, width // 2, BF16)
     picks = 2 * leads * total * width
     whole = 2 * leads * width * width
     path = 4 * leads * total * total
@@ -384,7 +394,7 @@
             array(8, total),
             array(8, total),
             same_as(weights),
-            same_as(neumann),
+            half,
             *messages,
         ],
         picks,
@@ -397,9 +407,9 @@
         ],
     )
     arrived = exchange(sent, plans[0])
-    hot_t, n_pick, n_small, same, inner, mask, local, base, rows, s_mat = run(
+    hot_t, n_pick, n_small, same, inner, mask, local, base, rows, n_rest, s_mat = run(
         pick_n_kernel,
-        [hot, turned, listed, chosen, n_mat, weight, counts, schur],
+        [hot, turned, listed, chosen, n_mat, weight, counts, neumann, schur],
         [
             array(total, width, BF16),
             array(total, width, BF16),
@@ -410,11 +420,12 @@
             full,
             some,
             array(8, total),
+            half,
             same_as(schur),
         ],
         2 * total * width * width + 2 * total * total * width + picks,
-        spaces={6: pltpu.SMEM, 7: pltpu.HBM},
-        scratch=[pltpu.SemaphoreType.DMA],
+        spaces={6: pltpu.SMEM, 7: pltpu.HBM, 8: pltpu.HBM},
+        scratch=[pltpu.SemaphoreType.DMA((2,))],
     )
     near = picked
     near_state = None
@@ -430,7 +441,7 @@
             arrived = exchange(sent, next_plan)
             (state,) = run(
                 bound(last_update_kernel, plan),
-                [*came, hot, n_mat, weight, mask, local, state],
+                [*came, hot, n_mat, n_rest, weight, mask, local, state],
                 [array(width, leads)],
                 whole + picks,
             )
@@ -440,14 +451,14 @@
         if step == 0:
             state, base, s_pick, s_small = run(
                 bound(first_update_kernel, plan),
-                [*came, hot, hot_t, n_mat, s_mat, weight, mask, inner, local, picked],
+                [*came, hot, hot_t, n_mat, n_rest, s_mat, weight, mask, inner, local, picked],
                 [full, some, array(width, total, BF16), small],
                 whole + 2 * picks + 2 * total * width * (width + total),
             )
         else:
             state, base = run(
                 bound(update_kernel, plan),
-                [*came, hot, n_mat, weight, mask, inner, local, picked, s_pick, state],
+                [*came, hot, n_mat, n_rest, weight, mask, inner, local, picked, s_pick, state],
                 [full, some],
                 whole + 2 * picks,
             )

time: 56.8 us -> 57.3 us (level)
  Pallas kernels: 17 us -> 17.9 us
    pallas_call x17, Pallas kernels: 17 us -> 17.9 us  [run(): pl.pallas_call(kernel, out_shape=results, in_specs=[pl.BlockSpec(memory_s...]
  transfers between devices with their start and end apart: 32 -> 32, of which waited for: 13 -> 12; matrix products, arithmetic and copies ran while one was open for 0% -> 0% of each run, Pallas kernels for 20% -> 22%
where the time goes in v20:
time: 57.3 us; the launch traced here: 57.2 us
  starting transfers between devices  29.3 us (51%)
  Pallas kernels  17.9 us (31%)
  waiting for transfers between devices  9.13 us (16%)
  between operations  0.84 us (1%)
    ppermute x32, starting transfers between devices, exchange(): lax.ppermute(part, 'sub', route)  29.3 us
    pallas_call x17, Pallas kernels, run(): pl.pallas_call(kernel, out_shape=results, in_specs=[pl.BlockSpec(memory_s...  17.9 us
    ppermute x32, waiting for transfers between devices, exchange(): lax.ppermute(part, 'sub', route)  9.13 us
  transfers between devices with their start and end apart: 32, of which 12 were waited for; matrix products, arithmetic and copies ran while one was open for 0% of the time, Pallas kernels for 22%

profile of v20, /device:TPU:8, one launch (start us, length us, event | category | flops | bytes accessed | tf_op | source)
XLA Modules:
  0.0 57.2 jit_solution(5029524861571698533)
XLA Ops:
  0.0 1.7 %shard_map.73 = (bf16[1024,384]{1,0:T(8,128)(2,1)S(1)}, bf16[128,1024]{1,0:T(8,128)(2,1)S(1)}, bf16[128,384]{1,0:T(8,128)(2,1)S(1)}, f32[8,384]{1,0:T(8,128)S(1)...) custom-call(s32[1,4,128]{2,1,0:T(4,128)} %rows_in.1, ...), custom_call_target="tpu_custom_call" | custom-call | flops 100663296 | bytes 4720656 | tf_op jit(solution)/shard_map/pallas_call | solution.py:346
  1.7 2.7 %collective-permute-start = (bf16[128,128]{1,0:T(8,128)(2,1)S(1)}, bf16[128,128]{1,0:T(8,128)(2,1)S(1)}, u32[]{:S(2)}, u32[]{:S(2)}) collective-permute-start(bf16[128,128]{1,0:T(8,128)(2,1)S(1)} %get-tuple-element.80), channel_id=1, source_target_pairs={{0,16},{1,2},{2,1},{3,19},{4,5},{5,4},{6,15},{7,23},{8,24},{9,25},... | collective-permute-start | bytes 98312 | tf_op jit(solution)/shard_map/ppermute | solution.py:382
  4.4 1.5 %collective-permute-start.1 = (bf16[128,128]{1,0:T(8,128)(2,1)S(1)}, bf16[128,128]{1,0:T(8,128)(2,1)S(1)}, u32[]{:S(2)}, u32[]{:S(2)}) collective-permute-start(bf16[128,128]{1,0:T(8,128)(2,1)S(1)} %get-tuple-element.81), channel_id=1, source_target_pairs={{0,2},{1,17},{2,0},{3,4},{4,3},{5,6},{6,5},{7,8},{8,7},{9,10},{10,... | collective-permute-start | bytes 98312 | tf_op jit(solution)/shard_map/ppermute | solution.py:382
  6.0 0.4 collective-permute-start.3
  7.0 2.8 %shard_map.74 = (bf16[384,1024]{1,0:T(8,128)(2,1)S(1)}, bf16[384,1024]{1,0:T(8,128)(2,1)S(1)}, bf16[384,384]{1,0:T(8,128)(2,1)S(1)}, bf16[384,384]{1,0:T(8,128)(...) custom-call(bf16[1024,384]{1,0:T(8,128)(2,1)S(1)} %get-tuple-element, ...), custom_call_target="tpu_custom_call" | custom-call | flops 1207959552 | bytes 12427268 | tf_op jit(solution)/shard_map/pallas_call | solution.py:346
  10.3 0.8 %collective-permute-start.4 = (bf16[128,128]{1,0:T(8,128)(2,1)S(1)}, bf16[128,128]{1,0:T(8,128)(2,1)S(1)}, u32[]{:S(2)}, u32[]{:S(2)}) collective-permute-start(bf16[128,128]{1,0:T(8,128)(2,1)S(1)} %get-tuple-element.95), channel_id=1, source_target_pairs={{0,16},{1,2},{2,1},{3,19},{4,5},{5,4},{6,15},{7,23},{8,24},{9,25},... | collective-permute-start | bytes 98312 | tf_op jit(solution)/shard_map/ppermute | solution.py:382
  11.1 0.9 %collective-permute-start.5 = (bf16[128,128]{1,0:T(8,128)(2,1)S(1)}, bf16[128,128]{1,0:T(8,128)(2,1)S(1)}, u32[]{:S(2)}, u32[]{:S(2)}) collective-permute-start(bf16[128,128]{1,0:T(8,128)(2,1)S(1)} %get-tuple-element.96), channel_id=1, source_target_pairs={{0,2},{1,17},{2,0},{3,4},{4,3},{5,6},{6,5},{7,8},{8,7},{9,10},{10,... | collective-permute-start | bytes 98312 | tf_op jit(solution)/shard_map/ppermute | solution.py:382
  12.0 0.5 collective-permute-start.6
  12.5 2.8 %shard_map.76 = (f32[128,1024]{1,0:T(8,128)S(1)}, f32[128,384]{1,0:T(8,128)S(1)}, bf16[1024,384]{1,0:T(8,128)(2,1)S(1)}, bf16[384,384]{1,0:T(8,128)(2,1)S(1)}) custom-call(bf16[128,128]{1,0:T(8,128)(2,1)S(1)} %collective-permute-done.refs_0_, bf16[128,128]{1,0:T(8,128)(2,1)S(1)} %collective-permute-done.1.refs_1_, ...), custom_call_target="tpu_custom_call" | custom-call | flops 1577058304 | bytes 8392704 | tf_op jit(solution)/shard_map/pallas_call | solution.py:346
  15.3 1.0 %collective-permute-done.5.refs_1_ = bf16[128,128]{1,0:T(8,128)(2,1)S(1)} collective-permute-done((bf16[128,128]{1,0:T(8,128)(2,1)S(1)}, bf16[128,128]{1,0:T(8,128)(2,1)S(1)}, u32[]{:S(2)}, u32[]{:S(2)}) %collective-permute-start.5) | collective-permute-done | bytes 32800 | tf_op jit(solution)/shard_map/ppermute | solution.py:382
  16.7 1.7 %collective-permute-start.8 = (bf16[128,128]{1,0:T(8,128)(2,1)S(1)}, bf16[128,128]{1,0:T(8,128)(2,1)S(1)}, u32[]{:S(2)}, u32[]{:S(2)}) collective-permute-start(bf16[128,128]{1,0:T(8,128)(2,1)S(1)} %get-tuple-element.108), channel_id=1, source_target_pairs={{0,16},{1,2},{2,1},{3,19},{4,20},{5,21},{6,22},{7,8},{8,7},{9,10},... | collective-permute-start | bytes 98312 | tf_op jit(solution)/shard_map/ppermute | solution.py:382
  18.3 2.1 %collective-permute-start.9 = (bf16[128,128]{1,0:T(8,128)(2,1)S(1)}, bf16[128,128]{1,0:T(8,128)(2,1)S(1)}, u32[]{:S(2)}, u32[]{:S(2)}) collective-permute-start(bf16[128,128]{1,0:T(8,128)(2,1)S(1)} %get-tuple-element.109), channel_id=1, source_target_pairs={{0,3},{1,17},{2,18},{3,0},{4,13},{5,6},{6,5},{7,23},{8,24},{9,25},... | collective-permute-start | bytes 98312 | tf_op jit(solution)/shard_map/ppermute | solution.py:382
  20.4 0.5 collective-permute-start.11
  21.0 1.0 %shard_map.78 = (f32[128,1024]{1,0:T(8,128)S(1)}, f32[128,1024]{1,0:T(8,128)S(1)}, f32[128,384]{1,0:T(8,128)S(1)}) custom-call(bf16[128,128]{1,0:T(8,128)(2,1)S(1)} %collective-permute-done.4.refs_0_, bf16[128,128]{1,0:T(8,128)(2,1)S(1)} %collective-permute-done.5.refs_1_, bf16[128,128]{1,0:T(8,128)(2,1)S(1)} %collective-permute-done.6.refs_2_, ...), custom_call_target="tpu_custom_call" | custom-call | flops 469762048 | bytes 5902336 | tf_op jit(solution)/shard_map/pallas_call | solution.py:346
  22.0 1.2 %collective-permute-done.9.refs_1_ = bf16[128,128]{1,0:T(8,128)(2,1)S(1)} collective-permute-done((bf16[128,128]{1,0:T(8,128)(2,1)S(1)}, bf16[128,128]{1,0:T(8,128)(2,1)S(1)}, u32[]{:S(2)}, u32[]{:S(2)}) %collective-permute-start.9) | collective-permute-done | bytes 32800 | tf_op jit(solution)/shard_map/ppermute | solution.py:382
  23.2 0.4 shard_map.79
  23.6 1.8 %collective-permute-start.12 = (bf16[128,128]{1,0:T(8,128)(2,1)S(1)}, bf16[128,128]{1,0:T(8,128)(2,1)S(1)}, u32[]{:S(2)}, u32[]{:S(2)}) collective-permute-start(bf16[128,128]{1,0:T(8,128)(2,1)S(1)} %get-tuple-element.117), channel_id=1, source_target_pairs={{0,16},{1,2},{2,1},{3,19},{4,20},{5,21},{6,22},{7,8},{8,7},{9,10},... | collective-permute-start | bytes 98312 | tf_op jit(solution)/shard_map/ppermute | solution.py:382
  25.3 1.6 %collective-permute-start.13 = (bf16[128,128]{1,0:T(8,128)(2,1)S(1)}, bf16[128,128]{1,0:T(8,128)(2,1)S(1)}, u32[]{:S(2)}, u32[]{:S(2)}) collective-permute-start(bf16[128,128]{1,0:T(8,128)(2,1)S(1)} %get-tuple-element.118), channel_id=1, source_target_pairs={{0,3},{1,17},{2,18},{3,0},{4,13},{5,6},{6,5},{7,23},{8,24},{9,25},... | collective-permute-start | bytes 98312 | tf_op jit(solution)/shard_map/ppermute | solution.py:382
  26.9 0.5 collective-permute-start.15
  27.4 1.3 %shard_map.80 = (f32[128,1024]{1,0:T(8,128)S(1)}, f32[128,384]{1,0:T(8,128)S(1)}) custom-call(bf16[128,128]{1,0:T(8,128)(2,1)S(1)} %collective-permute-done.8.refs_0_, bf16[128,128]{1,0:T(8,128)(2,1)S(1)} %collective-permute-done.9.refs_1_, bf16[128,128]{1,0:T(8,128)(2,1)S(1)} %collective-permute-done.10.refs_2_, ...), custom_call_target="tpu_custom_call" | custom-call | flops 469762048 | bytes 5738496 | tf_op jit(solution)/shard_map/pallas_call | solution.py:346
  29.0 1.1 %collective-permute-done.13.refs_1_ = bf16[128,128]{1,0:T(8,128)(2,1)S(1)} collective-permute-done((bf16[128,128]{1,0:T(8,128)(2,1)S(1)}, bf16[128,128]{1,0:T(8,128)(2,1)S(1)}, u32[]{:S(2)}, u32[]{:S(2)}) %collective-permute-start.13) | collective-permute-done | bytes 32800 | tf_op jit(solution)/shard_map/ppermute | solution.py:382
  30.1 0.4 shard_map.81
  30.5 1.2 %collective-permute-start.16 = (bf16[128,128]{1,0:T(8,128)(2,1)S(1)}, bf16[128,128]{1,0:T(8,128)(2,1)S(1)}, u32[]{:S(2)}, u32[]{:S(2)}) collective-permute-start(bf16[128,128]{1,0:T(8,128)(2,1)S(1)} %get-tuple-element.126), channel_id=1, source_target_pairs={{0,16},{1,2},{2,1},{3,19},{4,20},{5,21},{6,22},{7,8},{8,7},{9,10},... | collective-permute-start | bytes 98312 | tf_op jit(solution)/shard_map/ppermute | solution.py:382
  31.7 2.0 %collective-permute-start.17 = (bf16[128,128]{1,0:T(8,128)(2,1)S(1)}, bf16[128,128]{1,0:T(8,128)(2,1)S(1)}, u32[]{:S(2)}, u32[]{:S(2)}) collective-permute-start(bf16[128,128]{1,0:T(8,128)(2,1)S(1)} %get-tuple-element.127), channel_id=1, source_target_pairs={{0,3},{1,17},{2,18},{3,0},{4,13},{5,6},{6,5},{7,23},{8,24},{9,25},... | collective-permute-start | bytes 98312 | tf_op jit(solution)/shard_map/ppermute | solution.py:382
  33.8 0.5 collective-permute-start.19
  34.3 1.0 %shard_map.82 = (f32[128,1024]{1,0:T(8,128)S(1)}, f32[128,1024]{1,0:T(8,128)S(1)}, f32[128,384]{1,0:T(8,128)S(1)}) custom-call(bf16[128,128]{1,0:T(8,128)(2,1)S(1)} %collective-permute-done.12.refs_0_, bf16[128,128]{1,0:T(8,128)(2,1)S(1)} %collective-permute-done.13.refs_1_, bf16[128,128]{1,0:T(8,128)(2,1)S(1)} %collective-permute-done.14.refs_2_, ...), custom_call_target="tpu_custom_call" | custom-call | flops 469762048 | bytes 5902336 | tf_op jit(solution)/shard_map/pallas_call | solution.py:346
  35.3 0.6 collective-permute-done.16.refs_0_
  35.9 0.7 %collective-permute-done.17.refs_1_ = bf16[128,128]{1,0:T(8,128)(2,1)S(1)} collective-permute-done((bf16[128,128]{1,0:T(8,128)(2,1)S(1)}, bf16[128,128]{1,0:T(8,128)(2,1)S(1)}, u32[]{:S(2)}, u32[]{:S(2)}) %collective-permute-start.17) | collective-permute-done | bytes 32800 | tf_op jit(solution)/shard_map/ppermute | solution.py:382
  36.6 0.4 shard_map.83
  37.0 1.3 %collective-permute-start.20 = (bf16[128,128]{1,0:T(8,128)(2,1)S(1)}, bf16[128,128]{1,0:T(8,128)(2,1)S(1)}, u32[]{:S(2)}, u32[]{:S(2)}) collective-permute-start(bf16[128,128]{1,0:T(8,128)(2,1)S(1)} %get-tuple-element.134), channel_id=1, source_target_pairs={{0,16},{1,2},{2,1},{3,19},{4,20},{5,21},{6,22},{7,8},{8,7},{9,10},... | collective-permute-start | bytes 98312 | tf_op jit(solution)/shard_map/ppermute | solution.py:382
  38.3 1.6 %collective-permute-start.21 = (bf16[128,128]{1,0:T(8,128)(2,1)S(1)}, bf16[128,128]{1,0:T(8,128)(2,1)S(1)}, u32[]{:S(2)}, u32[]{:S(2)}) collective-permute-start(bf16[128,128]{1,0:T(8,128)(2,1)S(1)} %get-tuple-element.135), channel_id=1, source_target_pairs={{0,3},{1,17},{2,18},{3,0},{4,13},{5,6},{6,5},{7,23},{8,24},{9,25},... | collective-permute-start | bytes 98312 | tf_op jit(solution)/shard_map/ppermute | solution.py:382
  39.9 0.5 collective-permute-start.23
  40.4 1.3 %shard_map.84 = (f32[128,1024]{1,0:T(8,128)S(1)}, f32[128,384]{1,0:T(8,128)S(1)}) custom-call(bf16[128,128]{1,0:T(8,128)(2,1)S(1)} %collective-permute-done.16.refs_0_, bf16[128,128]{1,0:T(8,128)(2,1)S(1)} %collective-permute-done.17.refs_1_, bf16[128,128]{1,0:T(8,128)(2,1)S(1)} %collective-permute-done.18.refs_2_, ...), custom_call_target="tpu_custom_call" | custom-call | flops 469762048 | bytes 5738496 | tf_op jit(solution)/shard_map/pallas_call | solution.py:346
  41.7 0.5 collective-permute-done.20.refs_0_
  42.2 0.9 %collective-permute-done.21.refs_1_ = bf16[128,128]{1,0:T(8,128)(2,1)S(1)} collective-permute-done((bf16[128,128]{1,0:T(8,128)(2,1)S(1)}, bf16[128,128]{1,0:T(8,128)(2,1)S(1)}, u32[]{:S(2)}, u32[]{:S(2)}) %collective-permute-start.21) | collective-permute-done | bytes 32800 | tf_op jit(solution)/shard_map/ppermute | solution.py:382
  43.5 1.2 %collective-permute-start.24 = (bf16[128,128]{1,0:T(8,128)(2,1)S(1)}, bf16[128,128]{1,0:T(8,128)(2,1)S(1)}, u32[]{:S(2)}, u32[]{:S(2)}) collective-permute-start(bf16[128,128]{1,0:T(8,128)(2,1)S(1)} %get-tuple-element.142), channel_id=1, source_target_pairs={{0,16},{1,2},{2,1},{3,19},{4,20},{5,21},{6,22},{7,8},{8,7},{9,10},... | collective-permute-start | bytes 98312 | tf_op jit(solution)/shard_map/ppermute | solution.py:382
  44.7 2.0 %collective-permute-start.25 = (bf16[128,128]{1,0:T(8,128)(2,1)S(1)}, bf16[128,128]{1,0:T(8,128)(2,1)S(1)}, u32[]{:S(2)}, u32[]{:S(2)}) collective-permute-start(bf16[128,128]{1,0:T(8,128)(2,1)S(1)} %get-tuple-element.143), channel_id=1, source_target_pairs={{0,3},{1,17},{2,18},{3,0},{4,13},{5,6},{6,5},{7,23},{8,24},{9,25},... | collective-permute-start | bytes 98312 | tf_op jit(solution)/shard_map/ppermute | solution.py:382
  46.8 0.5 collective-permute-start.27
  47.3 1.0 %shard_map.86 = (f32[128,1024]{1,0:T(8,128)S(1)}, f32[128,1024]{1,0:T(8,128)S(1)}, f32[128,384]{1,0:T(8,128)S(1)}) custom-call(bf16[128,128]{1,0:T(8,128)(2,1)S(1)} %collective-permute-done.20.refs_0_, bf16[128,128]{1,0:T(8,128)(2,1)S(1)} %collective-permute-done.21.refs_1_, bf16[128,128]{1,0:T(8,128)(2,1)S(1)} %collective-permute-done.22.refs_2_, ...), custom_call_target="tpu_custom_call" | custom-call | flops 469762048 | bytes 5902336 | tf_op jit(solution)/shard_map/pallas_call | solution.py:346
  48.3 0.5 collective-permute-done.24.refs_0_
  48.7 0.8 %collective-permute-done.25.refs_1_ = bf16[128,128]{1,0:T(8,128)(2,1)S(1)} collective-permute-done((bf16[128,128]{1,0:T(8,128)(2,1)S(1)}, bf16[128,128]{1,0:T(8,128)(2,1)S(1)}, u32[]{:S(2)}, u32[]{:S(2)}) %collective-permute-start.25) | collective-permute-done | bytes 32800 | tf_op jit(solution)/shard_map/ppermute | solution.py:382
  49.9 1.3 %collective-permute-start.28 = (bf16[128,128]{1,0:T(8,128)(2,1)S(1)}, bf16[128,128]{1,0:T(8,128)(2,1)S(1)}, u32[]{:S(2)}, u32[]{:S(2)}) collective-permute-start(bf16[128,128]{1,0:T(8,128)(2,1)S(1)} %get-tuple-element.149), channel_id=1, source_target_pairs={{0,16},{1,2},{2,1},{3,19},{4,20},{5,21},{6,22},{7,8},{8,7},{9,10},... | collective-permute-start | bytes 98312 | tf_op jit(solution)/shard_map/ppermute | solution.py:382
  51.3 1.6 %collective-permute-start.29 = (bf16[128,128]{1,0:T(8,128)(2,1)S(1)}, bf16[128,128]{1,0:T(8,128)(2,1)S(1)}, u32[]{:S(2)}, u32[]{:S(2)}) collective-permute-start(bf16[128,128]{1,0:T(8,128)(2,1)S(1)} %get-tuple-element.150), channel_id=1, source_target_pairs={{0,3},{1,17},{2,18},{3,0},{4,13},{5,6},{6,5},{7,23},{8,24},{9,25},... | collective-permute-start | bytes 98312 | tf_op jit(solution)/shard_map/ppermute | solution.py:382
  52.8 0.5 collective-permute-start.31
  53.4 1.2 %shard_map.88.refs_5_ = f32[1024,128]{1,0:T(8,128)S(1)} custom-call(bf16[128,128]{1,0:T(8,128)(2,1)S(1)} %collective-permute-done.24.refs_0_, bf16[128,128]{1,0:T(8,128)(2,1)S(1)} %collective-permute-done.25.refs_1_, bf16[128,128]{1,0:T(8,128)(2,1)S(1)} %collective-permute-done.26.refs_2_, bf16[128,128]{1,0:T(8,128)(2,1)S(1)} %collective-permute-done.27.refs_3_, ...), custom_call_target="tpu_custom_call" | custom-call | flops 369098752 | bytes 4624384 | tf_op jit(solution)/shard_map/pallas_call | solution.py:346
  54.6 0.6 collective-permute-done.28.refs_0_
  55.1 0.9 %collective-permute-done.29.refs_1_ = bf16[128,128]{1,0:T(8,128)(2,1)S(1)} collective-permute-done((bf16[128,128]{1,0:T(8,128)(2,1)S(1)}, bf16[128,128]{1,0:T(8,128)(2,1)S(1)}, u32[]{:S(2)}, u32[]{:S(2)}) %collective-permute-start.29) | collective-permute-done | bytes 32800 | tf_op jit(solution)/shard_map/ppermute | solution.py:382
  56.1 1.1 %shard_map.89 = f32[1,1024,128]{2,1,0:T(8,128)} custom-call(bf16[128,128]{1,0:T(8,128)(2,1)S(1)} %collective-permute-done.28.refs_0_, bf16[128,128]{1,0:T(8,128)(2,1)S(1)} %collective-permute-done.29.refs_1_, bf16[128,128]{1,0:T(8,128)(2,1)S(1)} %collective-permute-done.30.refs_2_, bf16[128,128]{1,0:T(8,128)(2,1)S(1)} %collective-permute-done.31.refs_3_, ...), custom_call_target="tpu_custom_call" | custom-call | flops 100663296 | bytes 1966080 | tf_op jit(solution)/shard_map/pallas_call | solution.py:346
  (33 shorter events, 2.1 us)
Async XLA Ops:
  1.7 8.2 %collective-permute-start = (bf16[128,128]{1,0:T(8,128)(2,1)S(1)}, bf16[128,128]{1,0:T(8,128)(2,1)S(1)}, u32[]{:S(2)}, u32[]{:S(2)}) collective-permute-start(bf16[128,128]{1,0:T(8,128)(2,1)S(1)} %get-tuple-element.80), channel_id=1, source_target_pairs={{0,16},{1,2},{2,1},{3,19},{4,5},{5,4},{6,15},{7,23},{8,24},{9,25},... | collective-permute-start | bytes 98312 | tf_op jit(solution)/shard_map/ppermute | solution.py:382
  4.4 5.5 %collective-permute-start.1 = (bf16[128,128]{1,0:T(8,128)(2,1)S(1)}, bf16[128,128]{1,0:T(8,128)(2,1)S(1)}, u32[]{:S(2)}, u32[]{:S(2)}) collective-permute-start(bf16[128,128]{1,0:T(8,128)(2,1)S(1)} %get-tuple-element.81), channel_id=1, source_target_pairs={{0,2},{1,17},{2,0},{3,4},{4,3},{5,6},{6,5},{7,8},{8,7},{9,10},{10,... | collective-permute-start | bytes 98312 | tf_op jit(solution)/shard_map/ppermute | solution.py:382
  5.9 4.0 %collective-permute-start.2 = (bf16[128,128]{1,0:T(8,128)(2,1)S(1)}, bf16[128,128]{1,0:T(8,128)(2,1)S(1)}, u32[]{:S(2)}, u32[]{:S(2)}) collective-permute-start(bf16[128,128]{1,0:T(8,128)(2,1)S(1)} %get-tuple-element.82), channel_id=1, source_target_pairs={{0,1},{1,0},{2,18},{3,7},{4,20},{5,21},{6,22},{7,3},{8,9},{9,8},{1... | collective-permute-start | bytes 98312 | tf_op jit(solution)/shard_map/ppermute | solution.py:382
  6.0 3.9 %collective-permute-start.3 = (bf16[128,128]{1,0:T(8,128)(2,1)S(1)}, bf16[128,128]{1,0:T(8,128)(2,1)S(1)}, u32[]{:S(2)}, u32[]{:S(2)}) collective-permute-start(bf16[128,128]{1,0:T(8,128)(2,1)S(1)} %get-tuple-element.83), channel_id=1, source_target_pairs={{0,1},{1,0},{2,3},{3,2},{4,5},{5,4},{6,7},{7,6},{8,9},{9,8},{10,11... | collective-permute-start | bytes 98312 | tf_op jit(solution)/shard_map/ppermute | solution.py:382
  10.3 5.0 %collective-permute-start.4 = (bf16[128,128]{1,0:T(8,128)(2,1)S(1)}, bf16[128,128]{1,0:T(8,128)(2,1)S(1)}, u32[]{:S(2)}, u32[]{:S(2)}) collective-permute-start(bf16[128,128]{1,0:T(8,128)(2,1)S(1)} %get-tuple-element.95), channel_id=1, source_target_pairs={{0,16},{1,2},{2,1},{3,19},{4,5},{5,4},{6,15},{7,23},{8,24},{9,25},... | collective-permute-start | bytes 98312 | tf_op jit(solution)/shard_map/ppermute | solution.py:382
  11.1 5.1 %collective-permute-start.5 = (bf16[128,128]{1,0:T(8,128)(2,1)S(1)}, bf16[128,128]{1,0:T(8,128)(2,1)S(1)}, u32[]{:S(2)}, u32[]{:S(2)}) collective-permute-start(bf16[128,128]{1,0:T(8,128)(2,1)S(1)} %get-tuple-element.96), channel_id=1, source_target_pairs={{0,2},{1,17},{2,0},{3,4},{4,3},{5,6},{6,5},{7,8},{8,7},{9,10},{10,... | collective-permute-start | bytes 98312 | tf_op jit(solution)/shard_map/ppermute | solution.py:382
  12.0 4.3 %collective-permute-start.6 = (bf16[128,128]{1,0:T(8,128)(2,1)S(1)}, bf16[128,128]{1,0:T(8,128)(2,1)S(1)}, u32[]{:S(2)}, u32[]{:S(2)}) collective-permute-start(bf16[128,128]{1,0:T(8,128)(2,1)S(1)} %get-tuple-element.97), channel_id=1, source_target_pairs={{0,1},{1,0},{2,18},{3,7},{4,20},{5,21},{6,22},{7,3},{8,9},{9,8},{1... | collective-permute-start | bytes 98312 | tf_op jit(solution)/shard_map/ppermute | solution.py:382
  12.5 3.8 %collective-permute-start.7 = (bf16[128,128]{1,0:T(8,128)(2,1)S(1)}, bf16[128,128]{1,0:T(8,128)(2,1)S(1)}, u32[]{:S(2)}, u32[]{:S(2)}) collective-permute-start(bf16[128,128]{1,0:T(8,128)(2,1)S(1)} %get-tuple-element.98), channel_id=1, source_target_pairs={{0,1},{1,0},{2,3},{3,2},{4,5},{5,4},{6,7},{7,6},{8,9},{9,8},{10,11... | collective-permute-start | bytes 98312 | tf_op jit(solution)/shard_map/ppermute | solution.py:382
  16.7 5.3 %collective-permute-start.8 = (bf16[128,128]{1,0:T(8,128)(2,1)S(1)}, bf16[128,128]{1,0:T(8,128)(2,1)S(1)}, u32[]{:S(2)}, u32[]{:S(2)}) collective-permute-start(bf16[128,128]{1,0:T(8,128)(2,1)S(1)} %get-tuple-element.108), channel_id=1, source_target_pairs={{0,16},{1,2},{2,1},{3,19},{4,20},{5,21},{6,22},{7,8},{8,7},{9,10},... | collective-permute-start | bytes 98312 | tf_op jit(solution)/shard_map/ppermute | solution.py:382
  18.3 4.8 %collective-permute-start.9 = (bf16[128,128]{1,0:T(8,128)(2,1)S(1)}, bf16[128,128]{1,0:T(8,128)(2,1)S(1)}, u32[]{:S(2)}, u32[]{:S(2)}) collective-permute-start(bf16[128,128]{1,0:T(8,128)(2,1)S(1)} %get-tuple-element.109), channel_id=1, source_target_pairs={{0,3},{1,17},{2,18},{3,0},{4,13},{5,6},{6,5},{7,23},{8,24},{9,25},... | collective-permute-start | bytes 98312 | tf_op jit(solution)/shard_map/ppermute | solution.py:382
  20.4 2.7 %collective-permute-start.10 = (bf16[128,128]{1,0:T(8,128)(2,1)S(1)}, bf16[128,128]{1,0:T(8,128)(2,1)S(1)}, u32[]{:S(2)}, u32[]{:S(2)}) collective-permute-start(bf16[128,128]{1,0:T(8,128)(2,1)S(1)} %get-tuple-element.110), channel_id=1, source_target_pairs={{0,1},{1,0},{2,5},{3,4},{4,3},{5,2},{6,7},{7,6},{8,9},{9,8},{10,11... | collective-permute-start | bytes 98312 | tf_op jit(solution)/shard_map/ppermute | solution.py:382
  20.4 2.7 %collective-permute-start.11 = (bf16[128,128]{1,0:T(8,128)(2,1)S(1)}, bf16[128,128]{1,0:T(8,128)(2,1)S(1)}, u32[]{:S(2)}, u32[]{:S(2)}) collective-permute-start(bf16[128,128]{1,0:T(8,128)(2,1)S(1)} %get-tuple-element.111), channel_id=1, source_target_pairs={{0,1},{1,0},{2,3},{3,2},{4,5},{5,4},{6,7},{7,6},{8,9},{9,8},{10,11... | collective-permute-start | bytes 98312 | tf_op jit(solution)/shard_map/ppermute | solution.py:382
  23.6 5.4 %collective-permute-start.12 = (bf16[128,128]{1,0:T(8,128)(2,1)S(1)}, bf16[128,128]{1,0:T(8,128)(2,1)S(1)}, u32[]{:S(2)}, u32[]{:S(2)}) collective-permute-start(bf16[128,128]{1,0:T(8,128)(2,1)S(1)} %get-tuple-element.117), channel_id=1, source_target_pairs={{0,16},{1,2},{2,1},{3,19},{4,20},{5,21},{6,22},{7,8},{8,7},{9,10},... | collective-permute-start | bytes 98312 | tf_op jit(solution)/shard_map/ppermute | solution.py:382
  25.3 4.8 %collective-permute-start.13 = (bf16[128,128]{1,0:T(8,128)(2,1)S(1)}, bf16[128,128]{1,0:T(8,128)(2,1)S(1)}, u32[]{:S(2)}, u32[]{:S(2)}) collective-permute-start(bf16[128,128]{1,0:T(8,128)(2,1)S(1)} %get-tuple-element.118), channel_id=1, source_target_pairs={{0,3},{1,17},{2,18},{3,0},{4,13},{5,6},{6,5},{7,23},{8,24},{9,25},... | collective-permute-start | bytes 98312 | tf_op jit(solution)/shard_map/ppermute | solution.py:382
  26.9 3.2 %collective-permute-start.14 = (bf16[128,128]{1,0:T(8,128)(2,1)S(1)}, bf16[128,128]{1,0:T(8,128)(2,1)S(1)}, u32[]{:S(2)}, u32[]{:S(2)}) collective-permute-start(bf16[128,128]{1,0:T(8,128)(2,1)S(1)} %get-tuple-element.119), channel_id=1, source_target_pairs={{0,1},{1,0},{2,5},{3,4},{4,3},{5,2},{6,7},{7,6},{8,9},{9,8},{10,11... | collective-permute-start | bytes 98312 | tf_op jit(solution)/shard_map/ppermute | solution.py:382
  26.9 3.2 %collective-permute-start.15 = (bf16[128,128]{1,0:T(8,128)(2,1)S(1)}, bf16[128,128]{1,0:T(8,128)(2,1)S(1)}, u32[]{:S(2)}, u32[]{:S(2)}) collective-permute-start(bf16[128,128]{1,0:T(8,128)(2,1)S(1)} %get-tuple-element.120), channel_id=1, source_target_pairs={{0,1},{1,0},{2,3},{3,2},{4,5},{5,4},{6,7},{7,6},{8,9},{9,8},{10,11... | collective-permute-start | bytes 98312 | tf_op jit(solution)/shard_map/ppermute | solution.py:382
  30.5 5.3 %collective-permute-start.16 = (bf16[128,128]{1,0:T(8,128)(2,1)S(1)}, bf16[128,128]{1,0:T(8,128)(2,1)S(1)}, u32[]{:S(2)}, u32[]{:S(2)}) collective-permute-start(bf16[128,128]{1,0:T(8,128)(2,1)S(1)} %get-tuple-element.126), channel_id=1, source_target_pairs={{0,16},{1,2},{2,1},{3,19},{4,20},{5,21},{6,22},{7,8},{8,7},{9,10},... | collective-permute-start | bytes 98312 | tf_op jit(solution)/shard_map/ppermute | solution.py:382
  31.7 4.8 %collective-permute-start.17 = (bf16[128,128]{1,0:T(8,128)(2,1)S(1)}, bf16[128,128]{1,0:T(8,128)(2,1)S(1)}, u32[]{:S(2)}, u32[]{:S(2)}) collective-permute-start(bf16[128,128]{1,0:T(8,128)(2,1)S(1)} %get-tuple-element.127), channel_id=1, source_target_pairs={{0,3},{1,17},{2,18},{3,0},{4,13},{5,6},{6,5},{7,23},{8,24},{9,25},... | collective-permute-start | bytes 98312 | tf_op jit(solution)/shard_map/ppermute | solution.py:382
  33.8 2.8 %collective-permute-start.18 = (bf16[128,128]{1,0:T(8,128)(2,1)S(1)}, bf16[128,128]{1,0:T(8,128)(2,1)S(1)}, u32[]{:S(2)}, u32[]{:S(2)}) collective-permute-start(bf16[128,128]{1,0:T(8,128)(2,1)S(1)} %get-tuple-element.128), channel_id=1, source_target_pairs={{0,1},{1,0},{2,5},{3,4},{4,3},{5,2},{6,7},{7,6},{8,9},{9,8},{10,11... | collective-permute-start | bytes 98312 | tf_op jit(solution)/shard_map/ppermute | solution.py:382
  33.8 2.8 %collective-permute-start.19 = (bf16[128,128]{1,0:T(8,128)(2,1)S(1)}, bf16[128,128]{1,0:T(8,128)(2,1)S(1)}, u32[]{:S(2)}, u32[]{:S(2)}) collective-permute-start(bf16[128,128]{1,0:T(8,128)(2,1)S(1)} %get-tuple-element.129), channel_id=1, source_target_pairs={{0,1},{1,0},{2,3},{3,2},{4,5},{5,4},{6,7},{7,6},{8,9},{9,8},{10,11... | collective-permute-start | bytes 98312 | tf_op jit(solution)/shard_map/ppermute | solution.py:382
  37.0 5.2 %collective-permute-start.20 = (bf16[128,128]{1,0:T(8,128)(2,1)S(1)}, bf16[128,128]{1,0:T(8,128)(2,1)S(1)}, u32[]{:S(2)}, u32[]{:S(2)}) collective-permute-start(bf16[128,128]{1,0:T(8,128)(2,1)S(1)} %get-tuple-element.134), channel_id=1, source_target_pairs={{0,16},{1,2},{2,1},{3,19},{4,20},{5,21},{6,22},{7,8},{8,7},{9,10},... | collective-permute-start | bytes 98312 | tf_op jit(solution)/shard_map/ppermute | solution.py:382
  38.3 4.8 %collective-permute-start.21 = (bf16[128,128]{1,0:T(8,128)(2,1)S(1)}, bf16[128,128]{1,0:T(8,128)(2,1)S(1)}, u32[]{:S(2)}, u32[]{:S(2)}) collective-permute-start(bf16[128,128]{1,0:T(8,128)(2,1)S(1)} %get-tuple-element.135), channel_id=1, source_target_pairs={{0,3},{1,17},{2,18},{3,0},{4,13},{5,6},{6,5},{7,23},{8,24},{9,25},... | collective-permute-start | bytes 98312 | tf_op jit(solution)/shard_map/ppermute | solution.py:382
  39.9 3.2 %collective-permute-start.22 = (bf16[128,128]{1,0:T(8,128)(2,1)S(1)}, bf16[128,128]{1,0:T(8,128)(2,1)S(1)}, u32[]{:S(2)}, u32[]{:S(2)}) collective-permute-start(bf16[128,128]{1,0:T(8,128)(2,1)S(1)} %get-tuple-element.136), channel_id=1, source_target_pairs={{0,1},{1,0},{2,5},{3,4},{4,3},{5,2},{6,7},{7,6},{8,9},{9,8},{10,11... | collective-permute-start | bytes 98312 | tf_op jit(solution)/shard_map/ppermute | solution.py:382
  39.9 3.2 %collective-permute-start.23 = (bf16[128,128]{1,0:T(8,128)(2,1)S(1)}, bf16[128,128]{1,0:T(8,128)(2,1)S(1)}, u32[]{:S(2)}, u32[]{:S(2)}) collective-permute-start(bf16[128,128]{1,0:T(8,128)(2,1)S(1)} %get-tuple-element.137), channel_id=1, source_target_pairs={{0,1},{1,0},{2,3},{3,2},{4,5},{5,4},{6,7},{7,6},{8,9},{9,8},{10,11... | collective-permute-start | bytes 98312 | tf_op jit(solution)/shard_map/ppermute | solution.py:382
  43.5 5.2 %collective-permute-start.24 = (bf16[128,128]{1,0:T(8,128)(2,1)S(1)}, bf16[128,128]{1,0:T(8,128)(2,1)S(1)}, u32[]{:S(2)}, u32[]{:S(2)}) collective-permute-start(bf16[128,128]{1,0:T(8,128)(2,1)S(1)} %get-tuple-element.142), channel_id=1, source_target_pairs={{0,16},{1,2},{2,1},{3,19},{4,20},{5,21},{6,22},{7,8},{8,7},{9,10},... | collective-permute-start | bytes 98312 | tf_op jit(solution)/shard_map/ppermute | solution.py:382
  44.7 4.8 %collective-permute-start.25 = (bf16[128,128]{1,0:T(8,128)(2,1)S(1)}, bf16[128,128]{1,0:T(8,128)(2,1)S(1)}, u32[]{:S(2)}, u32[]{:S(2)}) collective-permute-start(bf16[128,128]{1,0:T(8,128)(2,1)S(1)} %get-tuple-element.143), channel_id=1, source_target_pairs={{0,3},{1,17},{2,18},{3,0},{4,13},{5,6},{6,5},{7,23},{8,24},{9,25},... | collective-permute-start | bytes 98312 | tf_op jit(solution)/shard_map/ppermute | solution.py:382
  46.7 2.8 %collective-permute-start.26 = (bf16[128,128]{1,0:T(8,128)(2,1)S(1)}, bf16[128,128]{1,0:T(8,128)(2,1)S(1)}, u32[]{:S(2)}, u32[]{:S(2)}) collective-permute-start(bf16[128,128]{1,0:T(8,128)(2,1)S(1)} %get-tuple-element.144), channel_id=1, source_target_pairs={{0,1},{1,0},{2,5},{3,4},{4,3},{5,2},{6,7},{7,6},{8,9},{9,8},{10,11... | collective-permute-start | bytes 98312 | tf_op jit(solution)/shard_map/ppermute | solution.py:382
  46.8 2.8 %collective-permute-start.27 = (bf16[128,128]{1,0:T(8,128)(2,1)S(1)}, bf16[128,128]{1,0:T(8,128)(2,1)S(1)}, u32[]{:S(2)}, u32[]{:S(2)}) collective-permute-start(bf16[128,128]{1,0:T(8,128)(2,1)S(1)} %get-tuple-element.145), channel_id=1, source_target_pairs={{0,1},{1,0},{2,3},{3,2},{4,5},{5,4},{6,7},{7,6},{8,9},{9,8},{10,11... | collective-permute-start | bytes 98312 | tf_op jit(solution)/shard_map/ppermute | solution.py:382
  49.9 5.2 %collective-permute-start.28 = (bf16[128,128]{1,0:T(8,128)(2,1)S(1)}, bf16[128,128]{1,0:T(8,128)(2,1)S(1)}, u32[]{:S(2)}, u32[]{:S(2)}) collective-permute-start(bf16[128,128]{1,0:T(8,128)(2,1)S(1)} %get-tuple-element.149), channel_id=1, source_target_pairs={{0,16},{1,2},{2,1},{3,19},{4,20},{5,21},{6,22},{7,8},{8,7},{9,10},... | collective-permute-start | bytes 98312 | tf_op jit(solution)/shard_map/ppermute | solution.py:382
  51.3 4.8 %collective-permute-start.29 = (bf16[128,128]{1,0:T(8,128)(2,1)S(1)}, bf16[128,128]{1,0:T(8,128)(2,1)S(1)}, u32[]{:S(2)}, u32[]{:S(2)}) collective-permute-start(bf16[128,128]{1,0:T(8,128)(2,1)S(1)} %get-tuple-element.150), channel_id=1, source_target_pairs={{0,3},{1,17},{2,18},{3,0},{4,13},{5,6},{6,5},{7,23},{8,24},{9,25},... | collective-permute-start | bytes 98312 | tf_op jit(solution)/shard_map/ppermute | solution.py:382
  52.8 3.2 %collective-permute-start.30 = (bf16[128,128]{1,0:T(8,128)(2,1)S(1)}, bf16[128,128]{1,0:T(8,128)(2,1)S(1)}, u32[]{:S(2)}, u32[]{:S(2)}) collective-permute-start(bf16[128,128]{1,0:T(8,128)(2,1)S(1)} %get-tuple-element.151), channel_id=1, source_target_pairs={{0,1},{1,0},{2,5},{3,4},{4,3},{5,2},{6,7},{7,6},{8,9},{9,8},{10,11... | collective-permute-start | bytes 98312 | tf_op jit(solution)/shard_map/ppermute | solution.py:382
  52.8 3.2 %collective-permute-start.31 = (bf16[128,128]{1,0:T(8,128)(2,1)S(1)}, bf16[128,128]{1,0:T(8,128)(2,1)S(1)}, u32[]{:S(2)}, u32[]{:S(2)}) collective-permute-start(bf16[128,128]{1,0:T(8,128)(2,1)S(1)} %get-tuple-element.152), channel_id=1, source_target_pairs={{0,1},{1,0},{2,3},{3,2},{4,5},{5,4},{6,7},{7,6},{8,9},{9,8},{10,11... | collective-permute-start | bytes 98312 | tf_op jit(solution)/shard_map/ppermute | solution.py:382

commit v21 on v15

--- a/solution.py
+++ b/solution.py
@@ -101,6 +101,31 @@
             picked.append(jnp.where(is_turn(own, 0), values[0], later).astype(BF16))
         parts = [*picked, parts[3]]
     return jnp.concatenate(parts, 1)
+
+
+def early_part(links, plan, third, near):
+    if links > 3:
+        return jnp.concatenate([*[jnp.zeros_like(third)] * (links - 2), third, near], 1)
+    value, none = third.astype(F32), jnp.zeros(third.shape, F32)
+    parts = [jnp.where(is_turn(own, 2), value, none).astype(BF16) for own in turns(2 * FAR, plan)]
+    return jnp.concatenate([*parts, near], 1)
+
+
+def late_product(links, plan, first, second, same_ref):
+    parts = [first, second]
+    if links == 3:
+        values = [first.astype(F32), second.astype(F32)]
+        none = jnp.zeros(first.shape, F32)
+        parts = []
+        for own in turns(2 * FAR, plan):
+            other = jnp.where(is_turn(own, 1), values[1], none)
+            parts.append(jnp.where(is_turn(own, 0), values[0], other).astype(BF16))
+    return times(jnp.concatenate(parts, 1), same_ref[: 2 * first.shape[1], :])
+
+
+def early_kernel(links, plan, scale, third_ref, near_ref, same_ref, state_ref, out_ref):
+    arrived = early_part(links, plan, third_ref[...], near_ref[...])
+    out_ref[...] = state_ref[...].astype(F32) + scale * times(arrived, same_ref[...])
 
 
 def scatter(links, plan, refs, block):
@@ -233,10 +258,10 @@
 
 
 def update_path_kernel(trips, links, plan, plan_out, step, last, *refs):
-    arrived_refs, refs = refs[:trips], refs[trips:]
+    first_ref, second_ref, *refs = refs
     same_ref, n_small_ref, row_ref, local_ref, base_ref = refs[:5]
     refs = refs[5:]
-    residual = local_ref[...].astype(F32) + times(gather(links, plan, arrived_refs), same_ref[...])
+    residual = local_ref[...] + late_product(links, plan, first_ref[...], second_ref[...], same_ref)
     scaled = (row_ref[1:2] * residual).astype(BF16)
     sent = row_ref[0:1] * (base_ref[...] + times_t(scaled, n_small_ref[...]))
     if last:
@@ -250,9 +275,9 @@
 
 
 def residual_path_kernel(trips, links, plan, plan_out, last, *refs):
-    arrived_refs, refs = refs[:trips], refs[trips:]
+    first_ref, second_ref, *refs = refs
     same_ref, s_small_ref, row_ref, base_ref, state_ref, local_ref = refs[:6]
-    state = state_ref[...] + DAMPING * times(gather(links, plan, arrived_refs), same_ref[...])
+    state = state_ref[...] + DAMPING * late_product(links, plan, first_ref[...], second_ref[...], same_ref)
     if last:
         refs = refs[6:]
     else:
@@ -410,12 +435,18 @@
         spaces={5: pltpu.SMEM, 6: pltpu.HBM},
         scratch=[pltpu.SemaphoreType.DMA],
     )
+    def early(came, plan, scale, at):
+        kernel = functools.partial(early_kernel, links, plan, scale)
+        (out,) = run(kernel, [came[2], came[3], same, at], [some], path // 2)
+        return out
+
     near = picked
     near_state = None
     for step in range(ITERS):
         came, last = arrived, step == ITERS - 1
         plan, next_plan, after = (*plans[2 * step :], None)[:3]
-        operands = [*came, same, n_small, rows, near, base]
+        near = early(came, plan, 1.0, near)
+        operands = [*came[:2], same, n_small, rows, near, base]
         if step and not last:
             operands.append(near_state)
         kernel = bound(update_path_kernel, plan, next_plan, step, last)
@@ -449,7 +480,7 @@
         ends = step == ITERS - 2
         near, *sent = run(
             bound(residual_path_kernel, next_plan, after, ends),
-            [*came, same, s_small, rows, base, near_state],
+            [*came[:2], same, s_small, rows, base, early(came, next_plan, DAMPING, near_state)],
             [some, *([] if ends else [some]), *messages],
             path,
         )

time: 56.8 us -> 57.2 us (level)
  Pallas kernels: 17.1 us -> 18.4 us
  waiting for transfers between devices: 9.35 us -> 8.21 us
    pallas_call x17 -> x24, Pallas kernels: 17.1 us -> 18.4 us  [run(): pl.pallas_call(kernel, out_shape=results, in_specs=[pl.BlockSpec(memory_s...]
    ppermute x32, waiting for transfers between devices: 9.35 us -> 8.21 us  [exchange(): lax.ppermute(part, 'sub', route)]
  transfers between devices with their start and end apart: 32 -> 32, of which waited for: 13 -> 12; matrix products, arithmetic and copies ran while one was open for 0% -> 0% of each run, Pallas kernels for 20% -> 23%
where the time goes in v21:
time: 57.2 us; the launch traced here: 56.8 us
  starting transfers between devices  29.2 us (51%)
  Pallas kernels  18.4 us (32%)
  waiting for transfers between devices  8.21 us (14%)
  between operations  0.97 us (2%)
    ppermute x32, starting transfers between devices, exchange(): lax.ppermute(part, 'sub', route)  29.2 us
    pallas_call x24, Pallas kernels, run(): pl.pallas_call(kernel, out_shape=results, in_specs=[pl.BlockSpec(memory_s...  18.4 us
    ppermute x32, waiting for transfers between devices, exchange(): lax.ppermute(part, 'sub', route)  8.21 us
  transfers between devices with their start and end apart: 32, of which 12 were waited for; matrix products, arithmetic and copies ran while one was open for 0% of the time, Pallas kernels for 23%

profile of v21, /device:TPU:8, one launch (start us, length us, event | category | flops | bytes accessed | tf_op | source)
XLA Modules:
  0.0 56.8 jit_solution(15053057686202675717)
XLA Ops:
  0.0 1.8 %shard_map.73 = (bf16[1024,384]{1,0:T(8,128)(2,1)S(1)}, bf16[128,1024]{1,0:T(8,128)(2,1)S(1)}, bf16[128,384]{1,0:T(8,128)(2,1)S(1)}, f32[8,384]{1,0:T(8,128)S(1)...) custom-call(s32[1,4,128]{2,1,0:T(4,128)} %rows_in.1, ...), custom_call_target="tpu_custom_call" | custom-call | flops 100663296 | bytes 5756944 | tf_op jit(solution)/shard_map/pallas_call | solution.py:357
  1.8 2.7 %collective-permute-start = (bf16[128,128]{1,0:T(8,128)(2,1)S(1)}, bf16[128,128]{1,0:T(8,128)(2,1)S(1)}, u32[]{:S(2)}, u32[]{:S(2)}) collective-permute-start(bf16[128,128]{1,0:T(8,128)(2,1)S(1)} %get-tuple-element.78), channel_id=1, source_target_pairs={{0,16},{1,2},{2,1},{3,19},{4,5},{5,4},{6,15},{7,23},{8,24},{9,25},... | collective-permute-start | bytes 98312 | tf_op jit(solution)/shard_map/ppermute | solution.py:392
  4.4 1.5 %collective-permute-start.1 = (bf16[128,128]{1,0:T(8,128)(2,1)S(1)}, bf16[128,128]{1,0:T(8,128)(2,1)S(1)}, u32[]{:S(2)}, u32[]{:S(2)}) collective-permute-start(bf16[128,128]{1,0:T(8,128)(2,1)S(1)} %get-tuple-element.79), channel_id=1, source_target_pairs={{0,2},{1,17},{2,0},{3,4},{4,3},{5,6},{6,5},{7,8},{8,7},{9,10},{10,... | collective-permute-start | bytes 98312 | tf_op jit(solution)/shard_map/ppermute | solution.py:392
  6.0 0.4 collective-permute-start.3
  7.1 2.1 %shard_map.74 = (bf16[384,1024]{1,0:T(8,128)(2,1)S(1)}, bf16[384,1024]{1,0:T(8,128)(2,1)S(1)}, bf16[384,384]{1,0:T(8,128)(2,1)S(1)}, bf16[384,384]{1,0:T(8,128)(...) custom-call(bf16[1024,384]{1,0:T(8,128)(2,1)S(1)} %get-tuple-element, ...), custom_call_target="tpu_custom_call" | custom-call | flops 1207959552 | bytes 10317828 | tf_op jit(solution)/shard_map/pallas_call | solution.py:357
  9.5 0.4 collective-permute-done.1.refs_1_
  10.2 0.5 collective-permute-start.4
  10.7 0.9 %collective-permute-start.5 = (bf16[128,128]{1,0:T(8,128)(2,1)S(1)}, bf16[128,128]{1,0:T(8,128)(2,1)S(1)}, u32[]{:S(2)}, u32[]{:S(2)}) collective-permute-start(bf16[128,128]{1,0:T(8,128)(2,1)S(1)} %get-tuple-element.93), channel_id=1, source_target_pairs={{0,2},{1,17},{2,0},{3,4},{4,3},{5,6},{6,5},{7,8},{8,7},{9,10},{10,... | collective-permute-start | bytes 98312 | tf_op jit(solution)/shard_map/ppermute | solution.py:392
  11.6 0.4 collective-permute-start.6
  12.1 2.7 %shard_map.77 = (f32[128,1024]{1,0:T(8,128)S(1)}, f32[128,384]{1,0:T(8,128)S(1)}, bf16[1024,384]{1,0:T(8,128)(2,1)S(1)}, bf16[384,384]{1,0:T(8,128)(2,1)S(1)}) custom-call(bf16[128,128]{1,0:T(8,128)(2,1)S(1)} %collective-permute-done.refs_0_, bf16[128,128]{1,0:T(8,128)(2,1)S(1)} %collective-permute-done.1.refs_1_, ...), custom_call_target="tpu_custom_call" | custom-call | flops 1577058304 | bytes 8392704 | tf_op jit(solution)/shard_map/pallas_call | solution.py:357
  15.1 0.7 %collective-permute-done.5.refs_1_ = bf16[128,128]{1,0:T(8,128)(2,1)S(1)} collective-permute-done((bf16[128,128]{1,0:T(8,128)(2,1)S(1)}, bf16[128,128]{1,0:T(8,128)(2,1)S(1)}, u32[]{:S(2)}, u32[]{:S(2)}) %collective-permute-start.5) | collective-permute-done | bytes 32800 | tf_op jit(solution)/shard_map/ppermute | solution.py:392
  16.2 1.8 %collective-permute-start.8 = (bf16[128,128]{1,0:T(8,128)(2,1)S(1)}, bf16[128,128]{1,0:T(8,128)(2,1)S(1)}, u32[]{:S(2)}, u32[]{:S(2)}) collective-permute-start(bf16[128,128]{1,0:T(8,128)(2,1)S(1)} %get-tuple-element.104), channel_id=1, source_target_pairs={{0,16},{1,2},{2,1},{3,19},{4,20},{5,21},{6,22},{7,8},{8,7},{9,10},... | collective-permute-start | bytes 98312 | tf_op jit(solution)/shard_map/ppermute | solution.py:392
  18.0 2.3 %collective-permute-start.9 = (bf16[128,128]{1,0:T(8,128)(2,1)S(1)}, bf16[128,128]{1,0:T(8,128)(2,1)S(1)}, u32[]{:S(2)}, u32[]{:S(2)}) collective-permute-start(bf16[128,128]{1,0:T(8,128)(2,1)S(1)} %get-tuple-element.105), channel_id=1, source_target_pairs={{0,3},{1,17},{2,18},{3,0},{4,13},{5,6},{6,5},{7,23},{8,24},{9,25},... | collective-permute-start | bytes 98312 | tf_op jit(solution)/shard_map/ppermute | solution.py:392
  20.3 0.5 collective-permute-start.11
  20.8 1.0 %shard_map.81 = (f32[128,1024]{1,0:T(8,128)S(1)}, f32[128,1024]{1,0:T(8,128)S(1)}, f32[128,384]{1,0:T(8,128)S(1)}) custom-call(bf16[128,128]{1,0:T(8,128)(2,1)S(1)} %collective-permute-done.4.refs_0_, bf16[128,128]{1,0:T(8,128)(2,1)S(1)} %collective-permute-done.5.refs_1_, bf16[128,128]{1,0:T(8,128)(2,1)S(1)} %collective-permute-done.6.third_ref.refs_2_, ...), custom_call_target="tpu_custom_call" | custom-call | flops 469762048 | bytes 5902336 | tf_op jit(solution)/shard_map/pallas_call | solution.py:357
  22.1 0.7 %collective-permute-done.9.refs_1_ = bf16[128,128]{1,0:T(8,128)(2,1)S(1)} collective-permute-done((bf16[128,128]{1,0:T(8,128)(2,1)S(1)}, bf16[128,128]{1,0:T(8,128)(2,1)S(1)}, u32[]{:S(2)}, u32[]{:S(2)}) %collective-permute-start.9) | collective-permute-done | bytes 32800 | tf_op jit(solution)/shard_map/ppermute | solution.py:392
  22.8 0.4 shard_map.82
  23.2 1.8 %collective-permute-start.12 = (bf16[128,128]{1,0:T(8,128)(2,1)S(1)}, bf16[128,128]{1,0:T(8,128)(2,1)S(1)}, u32[]{:S(2)}, u32[]{:S(2)}) collective-permute-start(bf16[128,128]{1,0:T(8,128)(2,1)S(1)} %get-tuple-element.113), channel_id=1, source_target_pairs={{0,16},{1,2},{2,1},{3,19},{4,20},{5,21},{6,22},{7,8},{8,7},{9,10},... | collective-permute-start | bytes 98312 | tf_op jit(solution)/shard_map/ppermute | solution.py:392
  25.0 1.7 %collective-permute-start.13 = (bf16[128,128]{1,0:T(8,128)(2,1)S(1)}, bf16[128,128]{1,0:T(8,128)(2,1)S(1)}, u32[]{:S(2)}, u32[]{:S(2)}) collective-permute-start(bf16[128,128]{1,0:T(8,128)(2,1)S(1)} %get-tuple-element.114), channel_id=1, source_target_pairs={{0,3},{1,17},{2,18},{3,0},{4,13},{5,6},{6,5},{7,23},{8,24},{9,25},... | collective-permute-start | bytes 98312 | tf_op jit(solution)/shard_map/ppermute | solution.py:392
  26.7 0.5 collective-permute-start.15
  27.2 1.2 %shard_map.83 = (f32[128,1024]{1,0:T(8,128)S(1)}, f32[128,384]{1,0:T(8,128)S(1)}) custom-call(bf16[128,128]{1,0:T(8,128)(2,1)S(1)} %collective-permute-done.8.refs_0_, bf16[128,128]{1,0:T(8,128)(2,1)S(1)} %collective-permute-done.9.refs_1_, bf16[128,128]{1,0:T(8,128)(2,1)S(1)} %collective-permute-done.10.third_ref.refs_2_, ...), custom_call_target="tpu_custom_call" | custom-call | flops 469762048 | bytes 5738496 | tf_op jit(solution)/shard_map/pallas_call | solution.py:357
  28.7 1.1 %collective-permute-done.13.refs_1_ = bf16[128,128]{1,0:T(8,128)(2,1)S(1)} collective-permute-done((bf16[128,128]{1,0:T(8,128)(2,1)S(1)}, bf16[128,128]{1,0:T(8,128)(2,1)S(1)}, u32[]{:S(2)}, u32[]{:S(2)}) %collective-permute-start.13) | collective-permute-done | bytes 32800 | tf_op jit(solution)/shard_map/ppermute | solution.py:392
  30.2 1.4 %collective-permute-start.16 = (bf16[128,128]{1,0:T(8,128)(2,1)S(1)}, bf16[128,128]{1,0:T(8,128)(2,1)S(1)}, u32[]{:S(2)}, u32[]{:S(2)}) collective-permute-start(bf16[128,128]{1,0:T(8,128)(2,1)S(1)} %get-tuple-element.122), channel_id=1, source_target_pairs={{0,16},{1,2},{2,1},{3,19},{4,20},{5,21},{6,22},{7,8},{8,7},{9,10},... | collective-permute-start | bytes 98312 | tf_op jit(solution)/shard_map/ppermute | solution.py:392
  31.6 1.8 %collective-permute-start.17 = (bf16[128,128]{1,0:T(8,128)(2,1)S(1)}, bf16[128,128]{1,0:T(8,128)(2,1)S(1)}, u32[]{:S(2)}, u32[]{:S(2)}) collective-permute-start(bf16[128,128]{1,0:T(8,128)(2,1)S(1)} %get-tuple-element.123), channel_id=1, source_target_pairs={{0,3},{1,17},{2,18},{3,0},{4,13},{5,6},{6,5},{7,23},{8,24},{9,25},... | collective-permute-start | bytes 98312 | tf_op jit(solution)/shard_map/ppermute | solution.py:392
  33.5 0.5 collective-permute-start.19
  34.0 1.0 %shard_map.87 = (f32[128,1024]{1,0:T(8,128)S(1)}, f32[128,1024]{1,0:T(8,128)S(1)}, f32[128,384]{1,0:T(8,128)S(1)}) custom-call(bf16[128,128]{1,0:T(8,128)(2,1)S(1)} %collective-permute-done.12.refs_0_, bf16[128,128]{1,0:T(8,128)(2,1)S(1)} %collective-permute-done.13.refs_1_, bf16[128,128]{1,0:T(8,128)(2,1)S(1)} %collective-permute-done.14.third_ref.refs_2_, ...), custom_call_target="tpu_custom_call" | custom-call | flops 469762048 | bytes 5902336 | tf_op jit(solution)/shard_map/pallas_call | solution.py:357
  35.5 0.9 %collective-permute-done.17.refs_1_ = bf16[128,128]{1,0:T(8,128)(2,1)S(1)} collective-permute-done((bf16[128,128]{1,0:T(8,128)(2,1)S(1)}, bf16[128,128]{1,0:T(8,128)(2,1)S(1)}, u32[]{:S(2)}, u32[]{:S(2)}) %collective-permute-start.17) | collective-permute-done | bytes 32800 | tf_op jit(solution)/shard_map/ppermute | solution.py:392
  36.5 0.4 shard_map.88
  36.8 1.1 %collective-permute-start.20 = (bf16[128,128]{1,0:T(8,128)(2,1)S(1)}, bf16[128,128]{1,0:T(8,128)(2,1)S(1)}, u32[]{:S(2)}, u32[]{:S(2)}) collective-permute-start(bf16[128,128]{1,0:T(8,128)(2,1)S(1)} %get-tuple-element.130), channel_id=1, source_target_pairs={{0,16},{1,2},{2,1},{3,19},{4,20},{5,21},{6,22},{7,8},{8,7},{9,10},... | collective-permute-start | bytes 98312 | tf_op jit(solution)/shard_map/ppermute | solution.py:392
  38.0 1.6 %collective-permute-start.21 = (bf16[128,128]{1,0:T(8,128)(2,1)S(1)}, bf16[128,128]{1,0:T(8,128)(2,1)S(1)}, u32[]{:S(2)}, u32[]{:S(2)}) collective-permute-start(bf16[128,128]{1,0:T(8,128)(2,1)S(1)} %get-tuple-element.131), channel_id=1, source_target_pairs={{0,3},{1,17},{2,18},{3,0},{4,13},{5,6},{6,5},{7,23},{8,24},{9,25},... | collective-permute-start | bytes 98312 | tf_op jit(solution)/shard_map/ppermute | solution.py:392
  39.6 0.5 collective-permute-start.23
  40.1 1.3 %shard_map.89 = (f32[128,1024]{1,0:T(8,128)S(1)}, f32[128,384]{1,0:T(8,128)S(1)}) custom-call(bf16[128,128]{1,0:T(8,128)(2,1)S(1)} %collective-permute-done.16.refs_0_, bf16[128,128]{1,0:T(8,128)(2,1)S(1)} %collective-permute-done.17.refs_1_, bf16[128,128]{1,0:T(8,128)(2,1)S(1)} %collective-permute-done.18.third_ref.refs_2_, ...), custom_call_target="tpu_custom_call" | custom-call | flops 469762048 | bytes 5738496 | tf_op jit(solution)/shard_map/pallas_call | solution.py:357
  41.6 0.4 collective-permute-done.20.refs_0_
  42.0 0.7 %collective-permute-done.21.refs_1_ = bf16[128,128]{1,0:T(8,128)(2,1)S(1)} collective-permute-done((bf16[128,128]{1,0:T(8,128)(2,1)S(1)}, bf16[128,128]{1,0:T(8,128)(2,1)S(1)}, u32[]{:S(2)}, u32[]{:S(2)}) %collective-permute-start.21) | collective-permute-done | bytes 32800 | tf_op jit(solution)/shard_map/ppermute | solution.py:392
  42.8 0.4 shard_map.91
  43.1 1.4 %collective-permute-start.24 = (bf16[128,128]{1,0:T(8,128)(2,1)S(1)}, bf16[128,128]{1,0:T(8,128)(2,1)S(1)}, u32[]{:S(2)}, u32[]{:S(2)}) collective-permute-start(bf16[128,128]{1,0:T(8,128)(2,1)S(1)} %get-tuple-element.138), channel_id=1, source_target_pairs={{0,16},{1,2},{2,1},{3,19},{4,20},{5,21},{6,22},{7,8},{8,7},{9,10},... | collective-permute-start | bytes 98312 | tf_op jit(solution)/shard_map/ppermute | solution.py:392
  44.5 1.8 %collective-permute-start.25 = (bf16[128,128]{1,0:T(8,128)(2,1)S(1)}, bf16[128,128]{1,0:T(8,128)(2,1)S(1)}, u32[]{:S(2)}, u32[]{:S(2)}) collective-permute-start(bf16[128,128]{1,0:T(8,128)(2,1)S(1)} %get-tuple-element.139), channel_id=1, source_target_pairs={{0,3},{1,17},{2,18},{3,0},{4,13},{5,6},{6,5},{7,23},{8,24},{9,25},... | collective-permute-start | bytes 98312 | tf_op jit(solution)/shard_map/ppermute | solution.py:392
  46.4 0.5 collective-permute-start.27
  46.9 1.0 %shard_map.93 = (f32[128,1024]{1,0:T(8,128)S(1)}, f32[128,1024]{1,0:T(8,128)S(1)}, f32[128,384]{1,0:T(8,128)S(1)}) custom-call(bf16[128,128]{1,0:T(8,128)(2,1)S(1)} %collective-permute-done.20.refs_0_, bf16[128,128]{1,0:T(8,128)(2,1)S(1)} %collective-permute-done.21.refs_1_, bf16[128,128]{1,0:T(8,128)(2,1)S(1)} %collective-permute-done.22.third_ref.refs_2_, ...), custom_call_target="tpu_custom_call" | custom-call | flops 469762048 | bytes 5902336 | tf_op jit(solution)/shard_map/pallas_call | solution.py:357
  48.3 1.0 %collective-permute-done.25.refs_1_ = bf16[128,128]{1,0:T(8,128)(2,1)S(1)} collective-permute-done((bf16[128,128]{1,0:T(8,128)(2,1)S(1)}, bf16[128,128]{1,0:T(8,128)(2,1)S(1)}, u32[]{:S(2)}, u32[]{:S(2)}) %collective-permute-start.25) | collective-permute-done | bytes 32800 | tf_op jit(solution)/shard_map/ppermute | solution.py:392
  49.4 0.4 shard_map.94
  49.7 1.1 %collective-permute-start.28 = (bf16[128,128]{1,0:T(8,128)(2,1)S(1)}, bf16[128,128]{1,0:T(8,128)(2,1)S(1)}, u32[]{:S(2)}, u32[]{:S(2)}) collective-permute-start(bf16[128,128]{1,0:T(8,128)(2,1)S(1)} %get-tuple-element.145), channel_id=1, source_target_pairs={{0,16},{1,2},{2,1},{3,19},{4,20},{5,21},{6,22},{7,8},{8,7},{9,10},... | collective-permute-start | bytes 98312 | tf_op jit(solution)/shard_map/ppermute | solution.py:392
  50.9 1.6 %collective-permute-start.29 = (bf16[128,128]{1,0:T(8,128)(2,1)S(1)}, bf16[128,128]{1,0:T(8,128)(2,1)S(1)}, u32[]{:S(2)}, u32[]{:S(2)}) collective-permute-start(bf16[128,128]{1,0:T(8,128)(2,1)S(1)} %get-tuple-element.146), channel_id=1, source_target_pairs={{0,3},{1,17},{2,18},{3,0},{4,13},{5,6},{6,5},{7,23},{8,24},{9,25},... | collective-permute-start | bytes 98312 | tf_op jit(solution)/shard_map/ppermute | solution.py:392
  52.5 0.5 collective-permute-start.31
  53.0 1.2 %shard_map.95.refs_5_ = f32[1024,128]{1,0:T(8,128)S(1)} custom-call(bf16[128,128]{1,0:T(8,128)(2,1)S(1)} %collective-permute-done.24.refs_0_, bf16[128,128]{1,0:T(8,128)(2,1)S(1)} %collective-permute-done.25.refs_1_, bf16[128,128]{1,0:T(8,128)(2,1)S(1)} %collective-permute-done.26.third_ref.refs_2_, ...), custom_call_target="tpu_custom_call" | custom-call | flops 369098752 | bytes 4624384 | tf_op jit(solution)/shard_map/pallas_call | solution.py:357
  54.2 0.8 %collective-permute-done.28.refs_0_ = bf16[128,128]{1,0:T(8,128)(2,1)S(1)} collective-permute-done((bf16[128,128]{1,0:T(8,128)(2,1)S(1)}, bf16[128,128]{1,0:T(8,128)(2,1)S(1)}, u32[]{:S(2)}, u32[]{:S(2)}) %collective-permute-start.28) | collective-permute-done | bytes 32800 | tf_op jit(solution)/shard_map/ppermute | solution.py:392
  54.9 0.7 %collective-permute-done.29.refs_1_ = bf16[128,128]{1,0:T(8,128)(2,1)S(1)} collective-permute-done((bf16[128,128]{1,0:T(8,128)(2,1)S(1)}, bf16[128,128]{1,0:T(8,128)(2,1)S(1)}, u32[]{:S(2)}, u32[]{:S(2)}) %collective-permute-start.29) | collective-permute-done | bytes 32800 | tf_op jit(solution)/shard_map/ppermute | solution.py:392
  55.7 1.1 %shard_map.96 = f32[1,1024,128]{2,1,0:T(8,128)} custom-call(bf16[128,128]{1,0:T(8,128)(2,1)S(1)} %collective-permute-done.28.refs_0_, bf16[128,128]{1,0:T(8,128)(2,1)S(1)} %collective-permute-done.29.refs_1_, bf16[128,128]{1,0:T(8,128)(2,1)S(1)} %collective-permute-done.30.refs_2_, bf16[128,128]{1,0:T(8,128)(2,1)S(1)} %collective-permute-done.31.refs_3_, ...), custom_call_target="tpu_custom_call" | custom-call | flops 100663296 | bytes 1966080 | tf_op jit(solution)/shard_map/pallas_call | solution.py:357
  (40 shorter events, 3.4 us)
Async XLA Ops:
  1.8 7.7 %collective-permute-start = (bf16[128,128]{1,0:T(8,128)(2,1)S(1)}, bf16[128,128]{1,0:T(8,128)(2,1)S(1)}, u32[]{:S(2)}, u32[]{:S(2)}) collective-permute-start(bf16[128,128]{1,0:T(8,128)(2,1)S(1)} %get-tuple-element.78), channel_id=1, source_target_pairs={{0,16},{1,2},{2,1},{3,19},{4,5},{5,4},{6,15},{7,23},{8,24},{9,25},... | collective-permute-start | bytes 98312 | tf_op jit(solution)/shard_map/ppermute | solution.py:392
  4.4 5.4 %collective-permute-start.1 = (bf16[128,128]{1,0:T(8,128)(2,1)S(1)}, bf16[128,128]{1,0:T(8,128)(2,1)S(1)}, u32[]{:S(2)}, u32[]{:S(2)}) collective-permute-start(bf16[128,128]{1,0:T(8,128)(2,1)S(1)} %get-tuple-element.79), channel_id=1, source_target_pairs={{0,2},{1,17},{2,0},{3,4},{4,3},{5,6},{6,5},{7,8},{8,7},{9,10},{10,... | collective-permute-start | bytes 98312 | tf_op jit(solution)/shard_map/ppermute | solution.py:392
  5.9 3.3 %collective-permute-start.2 = (bf16[128,128]{1,0:T(8,128)(2,1)S(1)}, bf16[128,128]{1,0:T(8,128)(2,1)S(1)}, u32[]{:S(2)}, u32[]{:S(2)}) collective-permute-start(bf16[128,128]{1,0:T(8,128)(2,1)S(1)} %get-tuple-element.88), channel_id=1, source_target_pairs={{0,1},{1,0},{2,18},{3,7},{4,20},{5,21},{6,22},{7,3},{8,9},{9,8},{1... | collective-permute-start | bytes 98312 | tf_op jit(solution)/shard_map/ppermute | solution.py:392
  6.0 3.2 %collective-permute-start.3 = (bf16[128,128]{1,0:T(8,128)(2,1)S(1)}, bf16[128,128]{1,0:T(8,128)(2,1)S(1)}, u32[]{:S(2)}, u32[]{:S(2)}) collective-permute-start(bf16[128,128]{1,0:T(8,128)(2,1)S(1)} %get-tuple-element.89), channel_id=1, source_target_pairs={{0,1},{1,0},{2,3},{3,2},{4,5},{5,4},{6,7},{7,6},{8,9},{9,8},{10,11... | collective-permute-start | bytes 98312 | tf_op jit(solution)/shard_map/ppermute | solution.py:392
  10.2 4.9 %collective-permute-start.4 = (bf16[128,128]{1,0:T(8,128)(2,1)S(1)}, bf16[128,128]{1,0:T(8,128)(2,1)S(1)}, u32[]{:S(2)}, u32[]{:S(2)}) collective-permute-start(bf16[128,128]{1,0:T(8,128)(2,1)S(1)} %get-tuple-element.92), channel_id=1, source_target_pairs={{0,16},{1,2},{2,1},{3,19},{4,5},{5,4},{6,15},{7,23},{8,24},{9,25},... | collective-permute-start | bytes 98312 | tf_op jit(solution)/shard_map/ppermute | solution.py:392
  10.7 5.1 %collective-permute-start.5 = (bf16[128,128]{1,0:T(8,128)(2,1)S(1)}, bf16[128,128]{1,0:T(8,128)(2,1)S(1)}, u32[]{:S(2)}, u32[]{:S(2)}) collective-permute-start(bf16[128,128]{1,0:T(8,128)(2,1)S(1)} %get-tuple-element.93), channel_id=1, source_target_pairs={{0,2},{1,17},{2,0},{3,4},{4,3},{5,6},{6,5},{7,8},{8,7},{9,10},{10,... | collective-permute-start | bytes 98312 | tf_op jit(solution)/shard_map/ppermute | solution.py:392
  11.6 3.2 %collective-permute-start.6 = (bf16[128,128]{1,0:T(8,128)(2,1)S(1)}, bf16[128,128]{1,0:T(8,128)(2,1)S(1)}, u32[]{:S(2)}, u32[]{:S(2)}) collective-permute-start(bf16[128,128]{1,0:T(8,128)(2,1)S(1)} %get-tuple-element.101), channel_id=1, source_target_pairs={{0,1},{1,0},{2,18},{3,7},{4,20},{5,21},{6,22},{7,3},{8,9},{9,8},{1... | collective-permute-start | bytes 98312 | tf_op jit(solution)/shard_map/ppermute | solution.py:392
  12.0 2.8 %collective-permute-start.7 = (bf16[128,128]{1,0:T(8,128)(2,1)S(1)}, bf16[128,128]{1,0:T(8,128)(2,1)S(1)}, u32[]{:S(2)}, u32[]{:S(2)}) collective-permute-start(bf16[128,128]{1,0:T(8,128)(2,1)S(1)} %get-tuple-element.102), channel_id=1, source_target_pairs={{0,1},{1,0},{2,3},{3,2},{4,5},{5,4},{6,7},{7,6},{8,9},{9,8},{10,11... | collective-permute-start | bytes 98312 | tf_op jit(solution)/shard_map/ppermute | solution.py:392
  16.2 5.9 %collective-permute-start.8 = (bf16[128,128]{1,0:T(8,128)(2,1)S(1)}, bf16[128,128]{1,0:T(8,128)(2,1)S(1)}, u32[]{:S(2)}, u32[]{:S(2)}) collective-permute-start(bf16[128,128]{1,0:T(8,128)(2,1)S(1)} %get-tuple-element.104), channel_id=1, source_target_pairs={{0,16},{1,2},{2,1},{3,19},{4,20},{5,21},{6,22},{7,8},{8,7},{9,10},... | collective-permute-start | bytes 98312 | tf_op jit(solution)/shard_map/ppermute | solution.py:392
  18.0 4.8 %collective-permute-start.9 = (bf16[128,128]{1,0:T(8,128)(2,1)S(1)}, bf16[128,128]{1,0:T(8,128)(2,1)S(1)}, u32[]{:S(2)}, u32[]{:S(2)}) collective-permute-start(bf16[128,128]{1,0:T(8,128)(2,1)S(1)} %get-tuple-element.105), channel_id=1, source_target_pairs={{0,3},{1,17},{2,18},{3,0},{4,13},{5,6},{6,5},{7,23},{8,24},{9,25},... | collective-permute-start | bytes 98312 | tf_op jit(solution)/shard_map/ppermute | solution.py:392
  20.3 1.5 %collective-permute-start.10 = (bf16[128,128]{1,0:T(8,128)(2,1)S(1)}, bf16[128,128]{1,0:T(8,128)(2,1)S(1)}, u32[]{:S(2)}, u32[]{:S(2)}) collective-permute-start(bf16[128,128]{1,0:T(8,128)(2,1)S(1)} %get-tuple-element.106), channel_id=1, source_target_pairs={{0,1},{1,0},{2,5},{3,4},{4,3},{5,2},{6,7},{7,6},{8,9},{9,8},{10,11... | collective-permute-start | bytes 98312 | tf_op jit(solution)/shard_map/ppermute | solution.py:392
  20.3 1.5 %collective-permute-start.11 = (bf16[128,128]{1,0:T(8,128)(2,1)S(1)}, bf16[128,128]{1,0:T(8,128)(2,1)S(1)}, u32[]{:S(2)}, u32[]{:S(2)}) collective-permute-start(bf16[128,128]{1,0:T(8,128)(2,1)S(1)} %get-tuple-element.107), channel_id=1, source_target_pairs={{0,1},{1,0},{2,3},{3,2},{4,5},{5,4},{6,7},{7,6},{8,9},{9,8},{10,11... | collective-permute-start | bytes 98312 | tf_op jit(solution)/shard_map/ppermute | solution.py:392
  23.2 5.5 %collective-permute-start.12 = (bf16[128,128]{1,0:T(8,128)(2,1)S(1)}, bf16[128,128]{1,0:T(8,128)(2,1)S(1)}, u32[]{:S(2)}, u32[]{:S(2)}) collective-permute-start(bf16[128,128]{1,0:T(8,128)(2,1)S(1)} %get-tuple-element.113), channel_id=1, source_target_pairs={{0,16},{1,2},{2,1},{3,19},{4,20},{5,21},{6,22},{7,8},{8,7},{9,10},... | collective-permute-start | bytes 98312 | tf_op jit(solution)/shard_map/ppermute | solution.py:392
  25.0 4.8 %collective-permute-start.13 = (bf16[128,128]{1,0:T(8,128)(2,1)S(1)}, bf16[128,128]{1,0:T(8,128)(2,1)S(1)}, u32[]{:S(2)}, u32[]{:S(2)}) collective-permute-start(bf16[128,128]{1,0:T(8,128)(2,1)S(1)} %get-tuple-element.114), channel_id=1, source_target_pairs={{0,3},{1,17},{2,18},{3,0},{4,13},{5,6},{6,5},{7,23},{8,24},{9,25},... | collective-permute-start | bytes 98312 | tf_op jit(solution)/shard_map/ppermute | solution.py:392
  26.7 1.8 %collective-permute-start.14 = (bf16[128,128]{1,0:T(8,128)(2,1)S(1)}, bf16[128,128]{1,0:T(8,128)(2,1)S(1)}, u32[]{:S(2)}, u32[]{:S(2)}) collective-permute-start(bf16[128,128]{1,0:T(8,128)(2,1)S(1)} %get-tuple-element.119), channel_id=1, source_target_pairs={{0,1},{1,0},{2,5},{3,4},{4,3},{5,2},{6,7},{7,6},{8,9},{9,8},{10,11... | collective-permute-start | bytes 98312 | tf_op jit(solution)/shard_map/ppermute | solution.py:392
  26.7 1.8 %collective-permute-start.15 = (bf16[128,128]{1,0:T(8,128)(2,1)S(1)}, bf16[128,128]{1,0:T(8,128)(2,1)S(1)}, u32[]{:S(2)}, u32[]{:S(2)}) collective-permute-start(bf16[128,128]{1,0:T(8,128)(2,1)S(1)} %get-tuple-element.120), channel_id=1, source_target_pairs={{0,1},{1,0},{2,3},{3,2},{4,5},{5,4},{6,7},{7,6},{8,9},{9,8},{10,11... | collective-permute-start | bytes 98312 | tf_op jit(solution)/shard_map/ppermute | solution.py:392
  30.2 5.3 %collective-permute-start.16 = (bf16[128,128]{1,0:T(8,128)(2,1)S(1)}, bf16[128,128]{1,0:T(8,128)(2,1)S(1)}, u32[]{:S(2)}, u32[]{:S(2)}) collective-permute-start(bf16[128,128]{1,0:T(8,128)(2,1)S(1)} %get-tuple-element.122), channel_id=1, source_target_pairs={{0,16},{1,2},{2,1},{3,19},{4,20},{5,21},{6,22},{7,8},{8,7},{9,10},... | collective-permute-start | bytes 98312 | tf_op jit(solution)/shard_map/ppermute | solution.py:392
  31.6 4.8 %collective-permute-start.17 = (bf16[128,128]{1,0:T(8,128)(2,1)S(1)}, bf16[128,128]{1,0:T(8,128)(2,1)S(1)}, u32[]{:S(2)}, u32[]{:S(2)}) collective-permute-start(bf16[128,128]{1,0:T(8,128)(2,1)S(1)} %get-tuple-element.123), channel_id=1, source_target_pairs={{0,3},{1,17},{2,18},{3,0},{4,13},{5,6},{6,5},{7,23},{8,24},{9,25},... | collective-permute-start | bytes 98312 | tf_op jit(solution)/shard_map/ppermute | solution.py:392
  33.5 1.5 %collective-permute-start.18 = (bf16[128,128]{1,0:T(8,128)(2,1)S(1)}, bf16[128,128]{1,0:T(8,128)(2,1)S(1)}, u32[]{:S(2)}, u32[]{:S(2)}) collective-permute-start(bf16[128,128]{1,0:T(8,128)(2,1)S(1)} %get-tuple-element.124), channel_id=1, source_target_pairs={{0,1},{1,0},{2,5},{3,4},{4,3},{5,2},{6,7},{7,6},{8,9},{9,8},{10,11... | collective-permute-start | bytes 98312 | tf_op jit(solution)/shard_map/ppermute | solution.py:392
  33.5 1.5 %collective-permute-start.19 = (bf16[128,128]{1,0:T(8,128)(2,1)S(1)}, bf16[128,128]{1,0:T(8,128)(2,1)S(1)}, u32[]{:S(2)}, u32[]{:S(2)}) collective-permute-start(bf16[128,128]{1,0:T(8,128)(2,1)S(1)} %get-tuple-element.125), channel_id=1, source_target_pairs={{0,1},{1,0},{2,3},{3,2},{4,5},{5,4},{6,7},{7,6},{8,9},{9,8},{10,11... | collective-permute-start | bytes 98312 | tf_op jit(solution)/shard_map/ppermute | solution.py:392
  36.8 5.2 %collective-permute-start.20 = (bf16[128,128]{1,0:T(8,128)(2,1)S(1)}, bf16[128,128]{1,0:T(8,128)(2,1)S(1)}, u32[]{:S(2)}, u32[]{:S(2)}) collective-permute-start(bf16[128,128]{1,0:T(8,128)(2,1)S(1)} %get-tuple-element.130), channel_id=1, source_target_pairs={{0,16},{1,2},{2,1},{3,19},{4,20},{5,21},{6,22},{7,8},{8,7},{9,10},... | collective-permute-start | bytes 98312 | tf_op jit(solution)/shard_map/ppermute | solution.py:392
  38.0 4.8 %collective-permute-start.21 = (bf16[128,128]{1,0:T(8,128)(2,1)S(1)}, bf16[128,128]{1,0:T(8,128)(2,1)S(1)}, u32[]{:S(2)}, u32[]{:S(2)}) collective-permute-start(bf16[128,128]{1,0:T(8,128)(2,1)S(1)} %get-tuple-element.131), channel_id=1, source_target_pairs={{0,3},{1,17},{2,18},{3,0},{4,13},{5,6},{6,5},{7,23},{8,24},{9,25},... | collective-permute-start | bytes 98312 | tf_op jit(solution)/shard_map/ppermute | solution.py:392
  39.6 1.8 %collective-permute-start.22 = (bf16[128,128]{1,0:T(8,128)(2,1)S(1)}, bf16[128,128]{1,0:T(8,128)(2,1)S(1)}, u32[]{:S(2)}, u32[]{:S(2)}) collective-permute-start(bf16[128,128]{1,0:T(8,128)(2,1)S(1)} %get-tuple-element.135), channel_id=1, source_target_pairs={{0,1},{1,0},{2,5},{3,4},{4,3},{5,2},{6,7},{7,6},{8,9},{9,8},{10,11... | collective-permute-start | bytes 98312 | tf_op jit(solution)/shard_map/ppermute | solution.py:392
  39.6 1.8 %collective-permute-start.23 = (bf16[128,128]{1,0:T(8,128)(2,1)S(1)}, bf16[128,128]{1,0:T(8,128)(2,1)S(1)}, u32[]{:S(2)}, u32[]{:S(2)}) collective-permute-start(bf16[128,128]{1,0:T(8,128)(2,1)S(1)} %get-tuple-element.136), channel_id=1, source_target_pairs={{0,1},{1,0},{2,3},{3,2},{4,5},{5,4},{6,7},{7,6},{8,9},{9,8},{10,11... | collective-permute-start | bytes 98312 | tf_op jit(solution)/shard_map/ppermute | solution.py:392
  43.1 5.2 %collective-permute-start.24 = (bf16[128,128]{1,0:T(8,128)(2,1)S(1)}, bf16[128,128]{1,0:T(8,128)(2,1)S(1)}, u32[]{:S(2)}, u32[]{:S(2)}) collective-permute-start(bf16[128,128]{1,0:T(8,128)(2,1)S(1)} %get-tuple-element.138), channel_id=1, source_target_pairs={{0,16},{1,2},{2,1},{3,19},{4,20},{5,21},{6,22},{7,8},{8,7},{9,10},... | collective-permute-start | bytes 98312 | tf_op jit(solution)/shard_map/ppermute | solution.py:392
  44.5 4.8 %collective-permute-start.25 = (bf16[128,128]{1,0:T(8,128)(2,1)S(1)}, bf16[128,128]{1,0:T(8,128)(2,1)S(1)}, u32[]{:S(2)}, u32[]{:S(2)}) collective-permute-start(bf16[128,128]{1,0:T(8,128)(2,1)S(1)} %get-tuple-element.139), channel_id=1, source_target_pairs={{0,3},{1,17},{2,18},{3,0},{4,13},{5,6},{6,5},{7,23},{8,24},{9,25},... | collective-permute-start | bytes 98312 | tf_op jit(solution)/shard_map/ppermute | solution.py:392
  46.4 1.5 %collective-permute-start.26 = (bf16[128,128]{1,0:T(8,128)(2,1)S(1)}, bf16[128,128]{1,0:T(8,128)(2,1)S(1)}, u32[]{:S(2)}, u32[]{:S(2)}) collective-permute-start(bf16[128,128]{1,0:T(8,128)(2,1)S(1)} %get-tuple-element.140), channel_id=1, source_target_pairs={{0,1},{1,0},{2,5},{3,4},{4,3},{5,2},{6,7},{7,6},{8,9},{9,8},{10,11... | collective-permute-start | bytes 98312 | tf_op jit(solution)/shard_map/ppermute | solution.py:392
  46.4 1.5 %collective-permute-start.27 = (bf16[128,128]{1,0:T(8,128)(2,1)S(1)}, bf16[128,128]{1,0:T(8,128)(2,1)S(1)}, u32[]{:S(2)}, u32[]{:S(2)}) collective-permute-start(bf16[128,128]{1,0:T(8,128)(2,1)S(1)} %get-tuple-element.141), channel_id=1, source_target_pairs={{0,1},{1,0},{2,3},{3,2},{4,5},{5,4},{6,7},{7,6},{8,9},{9,8},{10,11... | collective-permute-start | bytes 98312 | tf_op jit(solution)/shard_map/ppermute | solution.py:392
  49.7 5.2 %collective-permute-start.28 = (bf16[128,128]{1,0:T(8,128)(2,1)S(1)}, bf16[128,128]{1,0:T(8,128)(2,1)S(1)}, u32[]{:S(2)}, u32[]{:S(2)}) collective-permute-start(bf16[128,128]{1,0:T(8,128)(2,1)S(1)} %get-tuple-element.145), channel_id=1, source_target_pairs={{0,16},{1,2},{2,1},{3,19},{4,20},{5,21},{6,22},{7,8},{8,7},{9,10},... | collective-permute-start | bytes 98312 | tf_op jit(solution)/shard_map/ppermute | solution.py:392
  50.9 4.8 %collective-permute-start.29 = (bf16[128,128]{1,0:T(8,128)(2,1)S(1)}, bf16[128,128]{1,0:T(8,128)(2,1)S(1)}, u32[]{:S(2)}, u32[]{:S(2)}) collective-permute-start(bf16[128,128]{1,0:T(8,128)(2,1)S(1)} %get-tuple-element.146), channel_id=1, source_target_pairs={{0,3},{1,17},{2,18},{3,0},{4,13},{5,6},{6,5},{7,23},{8,24},{9,25},... | collective-permute-start | bytes 98312 | tf_op jit(solution)/shard_map/ppermute | solution.py:392
  52.5 3.2 %collective-permute-start.30 = (bf16[128,128]{1,0:T(8,128)(2,1)S(1)}, bf16[128,128]{1,0:T(8,128)(2,1)S(1)}, u32[]{:S(2)}, u32[]{:S(2)}) collective-permute-start(bf16[128,128]{1,0:T(8,128)(2,1)S(1)} %get-tuple-element.147), channel_id=1, source_target_pairs={{0,1},{1,0},{2,5},{3,4},{4,3},{5,2},{6,7},{7,6},{8,9},{9,8},{10,11... | collective-permute-start | bytes 98312 | tf_op jit(solution)/shard_map/ppermute | solution.py:392
  52.5 3.2 %collective-permute-start.31 = (bf16[128,128]{1,0:T(8,128)(2,1)S(1)}, bf16[128,128]{1,0:T(8,128)(2,1)S(1)}, u32[]{:S(2)}, u32[]{:S(2)}) collective-permute-start(bf16[128,128]{1,0:T(8,128)(2,1)S(1)} %get-tuple-element.148), channel_id=1, source_target_pairs={{0,1},{1,0},{2,3},{3,2},{4,5},{5,4},{6,7},{7,6},{8,9},{9,8},{10,11... | collective-permute-start | bytes 98312 | tf_op jit(solution)/shard_map/ppermute | solution.py:392

commit v22 on v20

--- a/solution.py
+++ b/solution.py
@@ -128,7 +128,6 @@
     turned_ref,
     picked_ref,
     list_ref,
-    chosen_ref,
     weight_ref,
     n_ref,
     *refs,
@@ -159,29 +158,17 @@
     copies[2].wait()
     turned = rhs_ref[0].T
     turned_ref[...] = turned
-    copies[3].wait()
-    weight = weight_ref[...]
-    high = weight.astype(BF16).astype(F32)
-    middle = (weight - high).astype(BF16).astype(F32)
-    low = weight - high - middle
-    level = lax.broadcasted_iota(jnp.int32, (16, width), 0)
-    pieces = jnp.where(level == 0, high, jnp.where(level == 1, middle, jnp.where(level == 2, low, 0.0)))
-    rest = jnp.zeros((turned.shape[0] - 16, width), BF16)
-    product = times(jnp.concatenate([turned, pieces.astype(BF16), rest], 0), hot_ref[...])
-    leads = turned.shape[0]
-    picked = product[:leads].astype(BF16)
-    pieces = product[leads : leads + 8]
-    chosen_ref[...] = jnp.broadcast_to((pieces[0:1] + pieces[1:2]) + pieces[2:3], chosen_ref.shape)
+    picked = times(turned, hot_ref[...]).astype(BF16)
     picked_ref[...] = picked
     scatter(links, plan_out, out_refs, picked)
-    copies[4].wait()
+    for copy in copies[3:]:
+        copy.wait()
 
 
 def pick_n_kernel(
     hot_ref,
     turned_ref,
     list_ref,
-    chosen_ref,
     n_ref,
     weight_ref,
     count_ref,
@@ -200,12 +187,13 @@
     s_ref,
     sems,
 ):
-    half = n_rest_ref.shape[1]
-    rest_copy = pltpu.make_async_copy(n_in.at[0, :, pl.ds(half, half)], n_rest_ref, sems.at[0])
+    cut = n_ref.shape[1]
+    rest_copy = pltpu.make_async_copy(n_in.at[0, :, pl.ds(cut, n_rest_ref.shape[1])], n_rest_ref, sems.at[0])
     s_copy = pltpu.make_async_copy(s_in, s_ref, sems.at[1])
     rest_copy.start()
     s_copy.start()
-    width, total = hot_ref.shape
+    hot = hot_ref[...]
+    width, total = hot.shape
     weight = weight_ref[...]
     side = 128
     listed = list_ref[:1]
@@ -224,23 +212,30 @@
     same_ref[...] = same.astype(BF16)
     inner = jnp.where(jnp.concatenate(hits, 1) > 0.0, 0.0, 1.0)
     inner_ref[...] = jnp.broadcast_to(inner, inner_ref.shape)
-    n_pick_ref[:, :half] = times(hot_t_ref[...], n_ref[...]).astype(BF16)
+    n_pick_ref[:, :cut] = times(hot_t_ref[...], n_ref[...]).astype(BF16)
     earlier = lax.broadcasted_iota(jnp.int32, same.shape, 0) < lax.broadcasted_iota(jnp.int32, same.shape, 1)
     repeats = jnp.sum(jnp.where(earlier, same, 0.0), 0, keepdims=True)
     first = jnp.where(repeats > 0.0, 0.0, 1.0)
-    chosen = chosen_ref[:1]
+    high = weight.astype(BF16).astype(F32)
+    middle = (weight - high).astype(BF16).astype(F32)
+    low = weight - high - middle
+    level = lax.broadcasted_iota(jnp.int32, (8, width), 0)
+    pieces = jnp.where(level == 0, high, jnp.where(level == 1, middle, jnp.where(level == 2, low, 0.0)))
+    pieces = times(pieces.astype(BF16), hot)
+    chosen = (pieces[0:1] + pieces[1:2]) + pieces[2:3]
     row_ref[0:1] = chosen
     row_ref[1:2] = chosen * first
     row_ref[2:3] = first
     row_ref[3:8] = jnp.zeros((5, total), F32)
+    rest_copy.wait()
+    n_pick_ref[:, cut:] = times(hot_t_ref[...], n_rest_ref[...]).astype(BF16)
+    n_pick = n_pick_ref[...]
+    n_small_ref[...] = times(n_pick, hot).astype(BF16)
     mask = jnp.where(lax.broadcasted_iota(jnp.int32, mask_ref.shape, 1) < count_ref[0], 1.0, 0.0)
     mask_ref[...] = mask
     local = mask[:1] * turned_ref[...].astype(F32)
     local_ref[...] = local
-    rest_copy.wait()
-    n_pick_ref[:, half:] = times(hot_t_ref[...], n_rest_ref[...]).astype(BF16)
-    base_ref[...] = times_t((weight * local * inner).astype(BF16), n_pick_ref[...])
-    n_small_ref[...] = times(n_pick_ref[...], hot_ref[...]).astype(BF16)
+    base_ref[...] = times_t((weight * local * inner).astype(BF16), n_pick)
     s_copy.wait()
 
 
@@ -279,8 +274,8 @@
     weight = weight_ref[...]
     residual = local_ref[...] + times_t(gather(links, plan, arrived_refs), hot_ref[...])
     scaled = (weight * residual).astype(BF16)
-    half = n_ref.shape[1]
-    product = times_t(scaled[:, :half], n_ref[...]) + times_t(scaled[:, half:], n_rest_ref[...])
+    cut = n_ref.shape[1]
+    product = times_t(scaled[:, :cut], n_ref[...]) + times_t(scaled[:, cut:], n_rest_ref[...])
     return mask_ref[:1] * weight * product
 
 
@@ -373,7 +368,6 @@
     full, some = array(leads, width), array(leads, total)
     small = array(total, total, BF16)
     row = array(8, width)
-    half = array(width, width // 2, BF16)
     picks = 2 * leads * total * width
     whole = 2 * leads * width * width
     path = 4 * leads * total * total
@@ -384,7 +378,7 @@
     def bound(kernel, *settings):
         return functools.partial(kernel, trips, links, *settings)
 
-    hot, turned, picked, listed, chosen, weight, n_mat, *sent = run(
+    hot, turned, picked, listed, weight, n_mat, *sent = run(
         bound(open_kernel, plans[0], subs),
         [shared_rows, neighbours, right_side, weights, neumann],
         [
@@ -392,9 +386,8 @@
             array(leads, width, BF16),
             array(leads, total, BF16),
             array(8, total),
-            array(8, total),
             same_as(weights),
-            half,
+            array(width, width - width // 4, BF16),
             *messages,
         ],
         picks,
@@ -409,7 +402,7 @@
     arrived = exchange(sent, plans[0])
     hot_t, n_pick, n_small, same, inner, mask, local, base, rows, n_rest, s_mat = run(
         pick_n_kernel,
-        [hot, turned, listed, chosen, n_mat, weight, counts, neumann, schur],
+        [hot, turned, listed, n_mat, weight, counts, neumann, schur],
         [
             array(total, width, BF16),
             array(total, width, BF16),
@@ -420,11 +413,11 @@
             full,
             some,
             array(8, total),
-            half,
+            array(width, width // 4, BF16),
             same_as(schur),
         ],
         2 * total * width * width + 2 * total * total * width + picks,
-        spaces={6: pltpu.SMEM, 7: pltpu.HBM, 8: pltpu.HBM},
+        spaces={5: pltpu.SMEM, 6: pltpu.HBM, 7: pltpu.HBM},
         scratch=[pltpu.SemaphoreType.DMA((2,))],
     )
     near = picked

time: 57.3 us -> 58 us (1.012)
  waiting for transfers between devices: 9.13 us -> 10 us
    ppermute x32, waiting for transfers between devices: 9.13 us -> 10 us  [exchange(): lax.ppermute(part, 'sub', route)]
  transfers between devices with their start and end apart: 32 -> 32, of which waited for: 12 -> 11; matrix products, arithmetic and copies ran while one was open for 0% -> 0% of each run, Pallas kernels for 22% -> 22%
where the time goes in v22:
time: 58 us; the launch traced here: 57.8 us
  starting transfers between devices  28.8 us (50%)
  Pallas kernels  18.1 us (31%)
  waiting for transfers between devices  10 us (17%)
  between operations  0.85 us (1%)
    ppermute x32, starting transfers between devices, exchange(): lax.ppermute(part, 'sub', route)  28.8 us
    pallas_call x17, Pallas kernels, run(): pl.pallas_call(kernel, out_shape=results, in_specs=[pl.BlockSpec(memory_s...  18.1 us
    ppermute x32, waiting for transfers between devices, exchange(): lax.ppermute(part, 'sub', route)  10 us
  transfers between devices with their start and end apart: 32, of which 11 were waited for; matrix products, arithmetic and copies ran while one was open for 0% of the time, Pallas kernels for 22%

profile of v22, /device:TPU:8, one launch (start us, length us, event | category | flops | bytes accessed | tf_op | source)
XLA Modules:
  0.0 57.8 jit_solution(5144564187344622177)
XLA Ops:
  0.0 1.6 %shard_map.73 = (bf16[1024,384]{1,0:T(8,128)(2,1)S(1)}, bf16[128,1024]{1,0:T(8,128)(2,1)S(1)}, bf16[128,384]{1,0:T(8,128)(2,1)S(1)}, f32[8,384]{1,0:T(8,128)S(1)...) custom-call(s32[1,4,128]{2,1,0:T(4,128)} %rows_in.1, ...), custom_call_target="tpu_custom_call" | custom-call | flops 100663296 | bytes 5232656 | tf_op jit(solution)/shard_map/pallas_call | solution.py:341
  1.6 2.7 %collective-permute-start = (bf16[128,128]{1,0:T(8,128)(2,1)S(1)}, bf16[128,128]{1,0:T(8,128)(2,1)S(1)}, u32[]{:S(2)}, u32[]{:S(2)}) collective-permute-start(bf16[128,128]{1,0:T(8,128)(2,1)S(1)} %get-tuple-element.79), channel_id=1, source_target_pairs={{0,16},{1,2},{2,1},{3,19},{4,5},{5,4},{6,15},{7,23},{8,24},{9,25},... | collective-permute-start | bytes 98312 | tf_op jit(solution)/shard_map/ppermute | solution.py:376
  4.3 1.5 %collective-permute-start.1 = (bf16[128,128]{1,0:T(8,128)(2,1)S(1)}, bf16[128,128]{1,0:T(8,128)(2,1)S(1)}, u32[]{:S(2)}, u32[]{:S(2)}) collective-permute-start(bf16[128,128]{1,0:T(8,128)(2,1)S(1)} %get-tuple-element.80), channel_id=1, source_target_pairs={{0,2},{1,17},{2,0},{3,4},{4,3},{5,6},{6,5},{7,8},{8,7},{9,10},{10,... | collective-permute-start | bytes 98312 | tf_op jit(solution)/shard_map/ppermute | solution.py:376
  5.9 0.4 collective-permute-start.3
  6.9 3.1 %shard_map.74 = (bf16[384,1024]{1,0:T(8,128)(2,1)S(1)}, bf16[384,1024]{1,0:T(8,128)(2,1)S(1)}, bf16[384,384]{1,0:T(8,128)(2,1)S(1)}, bf16[384,384]{1,0:T(8,128)(...) custom-call(bf16[1024,384]{1,0:T(8,128)(2,1)S(1)} %get-tuple-element, ...), custom_call_target="tpu_custom_call" | custom-call | flops 1207959552 | bytes 12414980 | tf_op jit(solution)/shard_map/pallas_call | solution.py:341
  10.1 0.4 shard_map.75
  10.5 0.8 %collective-permute-start.4 = (bf16[128,128]{1,0:T(8,128)(2,1)S(1)}, bf16[128,128]{1,0:T(8,128)(2,1)S(1)}, u32[]{:S(2)}, u32[]{:S(2)}) collective-permute-start(bf16[128,128]{1,0:T(8,128)(2,1)S(1)} %get-tuple-element.93), channel_id=1, source_target_pairs={{0,16},{1,2},{2,1},{3,19},{4,5},{5,4},{6,15},{7,23},{8,24},{9,25},... | collective-permute-start | bytes 98312 | tf_op jit(solution)/shard_map/ppermute | solution.py:376
  11.3 0.9 %collective-permute-start.5 = (bf16[128,128]{1,0:T(8,128)(2,1)S(1)}, bf16[128,128]{1,0:T(8,128)(2,1)S(1)}, u32[]{:S(2)}, u32[]{:S(2)}) collective-permute-start(bf16[128,128]{1,0:T(8,128)(2,1)S(1)} %get-tuple-element.94), channel_id=1, source_target_pairs={{0,2},{1,17},{2,0},{3,4},{4,3},{5,6},{6,5},{7,8},{8,7},{9,10},{10,... | collective-permute-start | bytes 98312 | tf_op jit(solution)/shard_map/ppermute | solution.py:376
  12.2 0.5 collective-permute-start.6
  12.7 2.8 %shard_map.76 = (f32[128,1024]{1,0:T(8,128)S(1)}, f32[128,384]{1,0:T(8,128)S(1)}, bf16[1024,384]{1,0:T(8,128)(2,1)S(1)}, bf16[384,384]{1,0:T(8,128)(2,1)S(1)}) custom-call(bf16[128,128]{1,0:T(8,128)(2,1)S(1)} %collective-permute-done.refs_0_, bf16[128,128]{1,0:T(8,128)(2,1)S(1)} %collective-permute-done.1.refs_1_, ...), custom_call_target="tpu_custom_call" | custom-call | flops 1577058304 | bytes 8392704 | tf_op jit(solution)/shard_map/pallas_call | solution.py:341
  15.5 1.0 %collective-permute-done.5.refs_1_ = bf16[128,128]{1,0:T(8,128)(2,1)S(1)} collective-permute-done((bf16[128,128]{1,0:T(8,128)(2,1)S(1)}, bf16[128,128]{1,0:T(8,128)(2,1)S(1)}, u32[]{:S(2)}, u32[]{:S(2)}) %collective-permute-start.5) | collective-permute-done | bytes 32800 | tf_op jit(solution)/shard_map/ppermute | solution.py:376
  16.9 1.7 %collective-permute-start.8 = (bf16[128,128]{1,0:T(8,128)(2,1)S(1)}, bf16[128,128]{1,0:T(8,128)(2,1)S(1)}, u32[]{:S(2)}, u32[]{:S(2)}) collective-permute-start(bf16[128,128]{1,0:T(8,128)(2,1)S(1)} %get-tuple-element.106), channel_id=1, source_target_pairs={{0,16},{1,2},{2,1},{3,19},{4,20},{5,21},{6,22},{7,8},{8,7},{9,10},... | collective-permute-start | bytes 98312 | tf_op jit(solution)/shard_map/ppermute | solution.py:376
  18.5 2.1 %collective-permute-start.9 = (bf16[128,128]{1,0:T(8,128)(2,1)S(1)}, bf16[128,128]{1,0:T(8,128)(2,1)S(1)}, u32[]{:S(2)}, u32[]{:S(2)}) collective-permute-start(bf16[128,128]{1,0:T(8,128)(2,1)S(1)} %get-tuple-element.107), channel_id=1, source_target_pairs={{0,3},{1,17},{2,18},{3,0},{4,13},{5,6},{6,5},{7,23},{8,24},{9,25},... | collective-permute-start | bytes 98312 | tf_op jit(solution)/shard_map/ppermute | solution.py:376
  20.6 0.5 collective-permute-start.11
  21.1 1.0 %shard_map.78 = (f32[128,1024]{1,0:T(8,128)S(1)}, f32[128,1024]{1,0:T(8,128)S(1)}, f32[128,384]{1,0:T(8,128)S(1)}) custom-call(bf16[128,128]{1,0:T(8,128)(2,1)S(1)} %collective-permute-done.4.refs_0_, bf16[128,128]{1,0:T(8,128)(2,1)S(1)} %collective-permute-done.5.refs_1_, bf16[128,128]{1,0:T(8,128)(2,1)S(1)} %collective-permute-done.6.refs_2_, ...), custom_call_target="tpu_custom_call" | custom-call | flops 469762048 | bytes 5902336 | tf_op jit(solution)/shard_map/pallas_call | solution.py:341
  22.2 1.2 %collective-permute-done.9.refs_1_ = bf16[128,128]{1,0:T(8,128)(2,1)S(1)} collective-permute-done((bf16[128,128]{1,0:T(8,128)(2,1)S(1)}, bf16[128,128]{1,0:T(8,128)(2,1)S(1)}, u32[]{:S(2)}, u32[]{:S(2)}) %collective-permute-start.9) | collective-permute-done | bytes 32800 | tf_op jit(solution)/shard_map/ppermute | solution.py:376
  23.4 0.4 shard_map.79
  23.8 2.2 %collective-permute-start.12 = (bf16[128,128]{1,0:T(8,128)(2,1)S(1)}, bf16[128,128]{1,0:T(8,128)(2,1)S(1)}, u32[]{:S(2)}, u32[]{:S(2)}) collective-permute-start(bf16[128,128]{1,0:T(8,128)(2,1)S(1)} %get-tuple-element.115), channel_id=1, source_target_pairs={{0,16},{1,2},{2,1},{3,19},{4,20},{5,21},{6,22},{7,8},{8,7},{9,10},... | collective-permute-start | bytes 98312 | tf_op jit(solution)/shard_map/ppermute | solution.py:376
  26.0 1.5 %collective-permute-start.13 = (bf16[128,128]{1,0:T(8,128)(2,1)S(1)}, bf16[128,128]{1,0:T(8,128)(2,1)S(1)}, u32[]{:S(2)}, u32[]{:S(2)}) collective-permute-start(bf16[128,128]{1,0:T(8,128)(2,1)S(1)} %get-tuple-element.116), channel_id=1, source_target_pairs={{0,3},{1,17},{2,18},{3,0},{4,13},{5,6},{6,5},{7,23},{8,24},{9,25},... | collective-permute-start | bytes 98312 | tf_op jit(solution)/shard_map/ppermute | solution.py:376
  27.5 0.5 collective-permute-start.15
  28.0 1.3 %shard_map.80 = (f32[128,1024]{1,0:T(8,128)S(1)}, f32[128,384]{1,0:T(8,128)S(1)}) custom-call(bf16[128,128]{1,0:T(8,128)(2,1)S(1)} %collective-permute-done.8.refs_0_, bf16[128,128]{1,0:T(8,128)(2,1)S(1)} %collective-permute-done.9.refs_1_, bf16[128,128]{1,0:T(8,128)(2,1)S(1)} %collective-permute-done.10.refs_2_, ...), custom_call_target="tpu_custom_call" | custom-call | flops 469762048 | bytes 5738496 | tf_op jit(solution)/shard_map/pallas_call | solution.py:341
  29.3 1.5 %collective-permute-done.13.refs_1_ = bf16[128,128]{1,0:T(8,128)(2,1)S(1)} collective-permute-done((bf16[128,128]{1,0:T(8,128)(2,1)S(1)}, bf16[128,128]{1,0:T(8,128)(2,1)S(1)}, u32[]{:S(2)}, u32[]{:S(2)}) %collective-permute-start.13) | collective-permute-done | bytes 32800 | tf_op jit(solution)/shard_map/ppermute | solution.py:376
  31.2 1.0 %collective-permute-start.16 = (bf16[128,128]{1,0:T(8,128)(2,1)S(1)}, bf16[128,128]{1,0:T(8,128)(2,1)S(1)}, u32[]{:S(2)}, u32[]{:S(2)}) collective-permute-start(bf16[128,128]{1,0:T(8,128)(2,1)S(1)} %get-tuple-element.124), channel_id=1, source_target_pairs={{0,16},{1,2},{2,1},{3,19},{4,20},{5,21},{6,22},{7,8},{8,7},{9,10},... | collective-permute-start | bytes 98312 | tf_op jit(solution)/shard_map/ppermute | solution.py:376
  32.2 1.7 %collective-permute-start.17 = (bf16[128,128]{1,0:T(8,128)(2,1)S(1)}, bf16[128,128]{1,0:T(8,128)(2,1)S(1)}, u32[]{:S(2)}, u32[]{:S(2)}) collective-permute-start(bf16[128,128]{1,0:T(8,128)(2,1)S(1)} %get-tuple-element.125), channel_id=1, source_target_pairs={{0,3},{1,17},{2,18},{3,0},{4,13},{5,6},{6,5},{7,23},{8,24},{9,25},... | collective-permute-start | bytes 98312 | tf_op jit(solution)/shard_map/ppermute | solution.py:376
  34.0 0.5 collective-permute-start.19
  34.5 1.0 %shard_map.82 = (f32[128,1024]{1,0:T(8,128)S(1)}, f32[128,1024]{1,0:T(8,128)S(1)}, f32[128,384]{1,0:T(8,128)S(1)}) custom-call(bf16[128,128]{1,0:T(8,128)(2,1)S(1)} %collective-permute-done.12.refs_0_, bf16[128,128]{1,0:T(8,128)(2,1)S(1)} %collective-permute-done.13.refs_1_, bf16[128,128]{1,0:T(8,128)(2,1)S(1)} %collective-permute-done.14.refs_2_, ...), custom_call_target="tpu_custom_call" | custom-call | flops 469762048 | bytes 5902336 | tf_op jit(solution)/shard_map/pallas_call | solution.py:341
  35.5 0.9 %collective-permute-done.16.refs_0_ = bf16[128,128]{1,0:T(8,128)(2,1)S(1)} collective-permute-done((bf16[128,128]{1,0:T(8,128)(2,1)S(1)}, bf16[128,128]{1,0:T(8,128)(2,1)S(1)}, u32[]{:S(2)}, u32[]{:S(2)}) %collective-permute-start.16) | collective-permute-done | bytes 32800 | tf_op jit(solution)/shard_map/ppermute | solution.py:376
  36.4 0.6 %collective-permute-done.17.refs_1_ = bf16[128,128]{1,0:T(8,128)(2,1)S(1)} collective-permute-done((bf16[128,128]{1,0:T(8,128)(2,1)S(1)}, bf16[128,128]{1,0:T(8,128)(2,1)S(1)}, u32[]{:S(2)}, u32[]{:S(2)}) %collective-permute-start.17) | collective-permute-done | bytes 32800 | tf_op jit(solution)/shard_map/ppermute | solution.py:376
  37.0 0.4 shard_map.83
  37.4 1.5 %collective-permute-start.20 = (bf16[128,128]{1,0:T(8,128)(2,1)S(1)}, bf16[128,128]{1,0:T(8,128)(2,1)S(1)}, u32[]{:S(2)}, u32[]{:S(2)}) collective-permute-start(bf16[128,128]{1,0:T(8,128)(2,1)S(1)} %get-tuple-element.132), channel_id=1, source_target_pairs={{0,16},{1,2},{2,1},{3,19},{4,20},{5,21},{6,22},{7,8},{8,7},{9,10},... | collective-permute-start | bytes 98312 | tf_op jit(solution)/shard_map/ppermute | solution.py:376
  39.0 1.5 %collective-permute-start.21 = (bf16[128,128]{1,0:T(8,128)(2,1)S(1)}, bf16[128,128]{1,0:T(8,128)(2,1)S(1)}, u32[]{:S(2)}, u32[]{:S(2)}) collective-permute-start(bf16[128,128]{1,0:T(8,128)(2,1)S(1)} %get-tuple-element.133), channel_id=1, source_target_pairs={{0,3},{1,17},{2,18},{3,0},{4,13},{5,6},{6,5},{7,23},{8,24},{9,25},... | collective-permute-start | bytes 98312 | tf_op jit(solution)/shard_map/ppermute | solution.py:376
  40.4 0.5 collective-permute-start.23
  40.9 1.3 %shard_map.84 = (f32[128,1024]{1,0:T(8,128)S(1)}, f32[128,384]{1,0:T(8,128)S(1)}) custom-call(bf16[128,128]{1,0:T(8,128)(2,1)S(1)} %collective-permute-done.16.refs_0_, bf16[128,128]{1,0:T(8,128)(2,1)S(1)} %collective-permute-done.17.refs_1_, bf16[128,128]{1,0:T(8,128)(2,1)S(1)} %collective-permute-done.18.refs_2_, ...), custom_call_target="tpu_custom_call" | custom-call | flops 469762048 | bytes 5738496 | tf_op jit(solution)/shard_map/pallas_call | solution.py:341
  42.2 0.4 collective-permute-done.20.refs_0_
  42.6 1.1 %collective-permute-done.21.refs_1_ = bf16[128,128]{1,0:T(8,128)(2,1)S(1)} collective-permute-done((bf16[128,128]{1,0:T(8,128)(2,1)S(1)}, bf16[128,128]{1,0:T(8,128)(2,1)S(1)}, u32[]{:S(2)}, u32[]{:S(2)}) %collective-permute-start.21) | collective-permute-done | bytes 32800 | tf_op jit(solution)/shard_map/ppermute | solution.py:376
  44.2 1.0 %collective-permute-start.24 = (bf16[128,128]{1,0:T(8,128)(2,1)S(1)}, bf16[128,128]{1,0:T(8,128)(2,1)S(1)}, u32[]{:S(2)}, u32[]{:S(2)}) collective-permute-start(bf16[128,128]{1,0:T(8,128)(2,1)S(1)} %get-tuple-element.140), channel_id=1, source_target_pairs={{0,16},{1,2},{2,1},{3,19},{4,20},{5,21},{6,22},{7,8},{8,7},{9,10},... | collective-permute-start | bytes 98312 | tf_op jit(solution)/shard_map/ppermute | solution.py:376
  45.2 1.7 %collective-permute-start.25 = (bf16[128,128]{1,0:T(8,128)(2,1)S(1)}, bf16[128,128]{1,0:T(8,128)(2,1)S(1)}, u32[]{:S(2)}, u32[]{:S(2)}) collective-permute-start(bf16[128,128]{1,0:T(8,128)(2,1)S(1)} %get-tuple-element.141), channel_id=1, source_target_pairs={{0,3},{1,17},{2,18},{3,0},{4,13},{5,6},{6,5},{7,23},{8,24},{9,25},... | collective-permute-start | bytes 98312 | tf_op jit(solution)/shard_map/ppermute | solution.py:376
  46.9 0.5 collective-permute-start.27
  47.5 1.0 %shard_map.86 = (f32[128,1024]{1,0:T(8,128)S(1)}, f32[128,1024]{1,0:T(8,128)S(1)}, f32[128,384]{1,0:T(8,128)S(1)}) custom-call(bf16[128,128]{1,0:T(8,128)(2,1)S(1)} %collective-permute-done.20.refs_0_, bf16[128,128]{1,0:T(8,128)(2,1)S(1)} %collective-permute-done.21.refs_1_, bf16[128,128]{1,0:T(8,128)(2,1)S(1)} %collective-permute-done.22.refs_2_, ...), custom_call_target="tpu_custom_call" | custom-call | flops 469762048 | bytes 5902336 | tf_op jit(solution)/shard_map/pallas_call | solution.py:341
  48.5 0.9 %collective-permute-done.24.refs_0_ = bf16[128,128]{1,0:T(8,128)(2,1)S(1)} collective-permute-done((bf16[128,128]{1,0:T(8,128)(2,1)S(1)}, bf16[128,128]{1,0:T(8,128)(2,1)S(1)}, u32[]{:S(2)}, u32[]{:S(2)}) %collective-permute-start.24) | collective-permute-done | bytes 32800 | tf_op jit(solution)/shard_map/ppermute | solution.py:376
  49.4 0.6 %collective-permute-done.25.refs_1_ = bf16[128,128]{1,0:T(8,128)(2,1)S(1)} collective-permute-done((bf16[128,128]{1,0:T(8,128)(2,1)S(1)}, bf16[128,128]{1,0:T(8,128)(2,1)S(1)}, u32[]{:S(2)}, u32[]{:S(2)}) %collective-permute-start.25) | collective-permute-done | bytes 32800 | tf_op jit(solution)/shard_map/ppermute | solution.py:376
  50.4 1.5 %collective-permute-start.28 = (bf16[128,128]{1,0:T(8,128)(2,1)S(1)}, bf16[128,128]{1,0:T(8,128)(2,1)S(1)}, u32[]{:S(2)}, u32[]{:S(2)}) collective-permute-start(bf16[128,128]{1,0:T(8,128)(2,1)S(1)} %get-tuple-element.147), channel_id=1, source_target_pairs={{0,16},{1,2},{2,1},{3,19},{4,20},{5,21},{6,22},{7,8},{8,7},{9,10},... | collective-permute-start | bytes 98312 | tf_op jit(solution)/shard_map/ppermute | solution.py:376
  51.9 1.5 %collective-permute-start.29 = (bf16[128,128]{1,0:T(8,128)(2,1)S(1)}, bf16[128,128]{1,0:T(8,128)(2,1)S(1)}, u32[]{:S(2)}, u32[]{:S(2)}) collective-permute-start(bf16[128,128]{1,0:T(8,128)(2,1)S(1)} %get-tuple-element.148), channel_id=1, source_target_pairs={{0,3},{1,17},{2,18},{3,0},{4,13},{5,6},{6,5},{7,23},{8,24},{9,25},... | collective-permute-start | bytes 98312 | tf_op jit(solution)/shard_map/ppermute | solution.py:376
  53.4 0.5 collective-permute-start.31
  53.9 1.2 %shard_map.88.refs_5_ = f32[1024,128]{1,0:T(8,128)S(1)} custom-call(bf16[128,128]{1,0:T(8,128)(2,1)S(1)} %collective-permute-done.24.refs_0_, bf16[128,128]{1,0:T(8,128)(2,1)S(1)} %collective-permute-done.25.refs_1_, bf16[128,128]{1,0:T(8,128)(2,1)S(1)} %collective-permute-done.26.refs_2_, bf16[128,128]{1,0:T(8,128)(2,1)S(1)} %collective-permute-done.27.refs_3_, ...), custom_call_target="tpu_custom_call" | custom-call | flops 369098752 | bytes 4624384 | tf_op jit(solution)/shard_map/pallas_call | solution.py:341
  55.1 0.5 collective-permute-done.28.refs_0_
  55.6 1.1 %collective-permute-done.29.refs_1_ = bf16[128,128]{1,0:T(8,128)(2,1)S(1)} collective-permute-done((bf16[128,128]{1,0:T(8,128)(2,1)S(1)}, bf16[128,128]{1,0:T(8,128)(2,1)S(1)}, u32[]{:S(2)}, u32[]{:S(2)}) %collective-permute-start.29) | collective-permute-done | bytes 32800 | tf_op jit(solution)/shard_map/ppermute | solution.py:376
  56.8 1.1 %shard_map.89 = f32[1,1024,128]{2,1,0:T(8,128)} custom-call(bf16[128,128]{1,0:T(8,128)(2,1)S(1)} %collective-permute-done.28.refs_0_, bf16[128,128]{1,0:T(8,128)(2,1)S(1)} %collective-permute-done.29.refs_1_, bf16[128,128]{1,0:T(8,128)(2,1)S(1)} %collective-permute-done.30.refs_2_, bf16[128,128]{1,0:T(8,128)(2,1)S(1)} %collective-permute-done.31.refs_3_, ...), custom_call_target="tpu_custom_call" | custom-call | flops 100663296 | bytes 1966080 | tf_op jit(solution)/shard_map/pallas_call | solution.py:341
  (33 shorter events, 1.8 us)
Async XLA Ops:
  1.6 8.5 %collective-permute-start = (bf16[128,128]{1,0:T(8,128)(2,1)S(1)}, bf16[128,128]{1,0:T(8,128)(2,1)S(1)}, u32[]{:S(2)}, u32[]{:S(2)}) collective-permute-start(bf16[128,128]{1,0:T(8,128)(2,1)S(1)} %get-tuple-element.79), channel_id=1, source_target_pairs={{0,16},{1,2},{2,1},{3,19},{4,5},{5,4},{6,15},{7,23},{8,24},{9,25},... | collective-permute-start | bytes 98312 | tf_op jit(solution)/shard_map/ppermute | solution.py:376
  4.3 5.8 %collective-permute-start.1 = (bf16[128,128]{1,0:T(8,128)(2,1)S(1)}, bf16[128,128]{1,0:T(8,128)(2,1)S(1)}, u32[]{:S(2)}, u32[]{:S(2)}) collective-permute-start(bf16[128,128]{1,0:T(8,128)(2,1)S(1)} %get-tuple-element.80), channel_id=1, source_target_pairs={{0,2},{1,17},{2,0},{3,4},{4,3},{5,6},{6,5},{7,8},{8,7},{9,10},{10,... | collective-permute-start | bytes 98312 | tf_op jit(solution)/shard_map/ppermute | solution.py:376
  5.7 4.3 %collective-permute-start.2 = (bf16[128,128]{1,0:T(8,128)(2,1)S(1)}, bf16[128,128]{1,0:T(8,128)(2,1)S(1)}, u32[]{:S(2)}, u32[]{:S(2)}) collective-permute-start(bf16[128,128]{1,0:T(8,128)(2,1)S(1)} %get-tuple-element.81), channel_id=1, source_target_pairs={{0,1},{1,0},{2,18},{3,7},{4,20},{5,21},{6,22},{7,3},{8,9},{9,8},{1... | collective-permute-start | bytes 98312 | tf_op jit(solution)/shard_map/ppermute | solution.py:376
  5.9 4.2 %collective-permute-start.3 = (bf16[128,128]{1,0:T(8,128)(2,1)S(1)}, bf16[128,128]{1,0:T(8,128)(2,1)S(1)}, u32[]{:S(2)}, u32[]{:S(2)}) collective-permute-start(bf16[128,128]{1,0:T(8,128)(2,1)S(1)} %get-tuple-element.82), channel_id=1, source_target_pairs={{0,1},{1,0},{2,3},{3,2},{4,5},{5,4},{6,7},{7,6},{8,9},{9,8},{10,11... | collective-permute-start | bytes 98312 | tf_op jit(solution)/shard_map/ppermute | solution.py:376
  10.5 5.0 %collective-permute-start.4 = (bf16[128,128]{1,0:T(8,128)(2,1)S(1)}, bf16[128,128]{1,0:T(8,128)(2,1)S(1)}, u32[]{:S(2)}, u32[]{:S(2)}) collective-permute-start(bf16[128,128]{1,0:T(8,128)(2,1)S(1)} %get-tuple-element.93), channel_id=1, source_target_pairs={{0,16},{1,2},{2,1},{3,19},{4,5},{5,4},{6,15},{7,23},{8,24},{9,25},... | collective-permute-start | bytes 98312 | tf_op jit(solution)/shard_map/ppermute | solution.py:376
  11.3 5.1 %collective-permute-start.5 = (bf16[128,128]{1,0:T(8,128)(2,1)S(1)}, bf16[128,128]{1,0:T(8,128)(2,1)S(1)}, u32[]{:S(2)}, u32[]{:S(2)}) collective-permute-start(bf16[128,128]{1,0:T(8,128)(2,1)S(1)} %get-tuple-element.94), channel_id=1, source_target_pairs={{0,2},{1,17},{2,0},{3,4},{4,3},{5,6},{6,5},{7,8},{8,7},{9,10},{10,... | collective-permute-start | bytes 98312 | tf_op jit(solution)/shard_map/ppermute | solution.py:376
  12.2 4.3 %collective-permute-start.6 = (bf16[128,128]{1,0:T(8,128)(2,1)S(1)}, bf16[128,128]{1,0:T(8,128)(2,1)S(1)}, u32[]{:S(2)}, u32[]{:S(2)}) collective-permute-start(bf16[128,128]{1,0:T(8,128)(2,1)S(1)} %get-tuple-element.95), channel_id=1, source_target_pairs={{0,1},{1,0},{2,18},{3,7},{4,20},{5,21},{6,22},{7,3},{8,9},{9,8},{1... | collective-permute-start | bytes 98312 | tf_op jit(solution)/shard_map/ppermute | solution.py:376
  12.7 3.8 %collective-permute-start.7 = (bf16[128,128]{1,0:T(8,128)(2,1)S(1)}, bf16[128,128]{1,0:T(8,128)(2,1)S(1)}, u32[]{:S(2)}, u32[]{:S(2)}) collective-permute-start(bf16[128,128]{1,0:T(8,128)(2,1)S(1)} %get-tuple-element.96), channel_id=1, source_target_pairs={{0,1},{1,0},{2,3},{3,2},{4,5},{5,4},{6,7},{7,6},{8,9},{9,8},{10,11... | collective-permute-start | bytes 98312 | tf_op jit(solution)/shard_map/ppermute | solution.py:376
  16.9 5.3 %collective-permute-start.8 = (bf16[128,128]{1,0:T(8,128)(2,1)S(1)}, bf16[128,128]{1,0:T(8,128)(2,1)S(1)}, u32[]{:S(2)}, u32[]{:S(2)}) collective-permute-start(bf16[128,128]{1,0:T(8,128)(2,1)S(1)} %get-tuple-element.106), channel_id=1, source_target_pairs={{0,16},{1,2},{2,1},{3,19},{4,20},{5,21},{6,22},{7,8},{8,7},{9,10},... | collective-permute-start | bytes 98312 | tf_op jit(solution)/shard_map/ppermute | solution.py:376
  18.5 4.8 %collective-permute-start.9 = (bf16[128,128]{1,0:T(8,128)(2,1)S(1)}, bf16[128,128]{1,0:T(8,128)(2,1)S(1)}, u32[]{:S(2)}, u32[]{:S(2)}) collective-permute-start(bf16[128,128]{1,0:T(8,128)(2,1)S(1)} %get-tuple-element.107), channel_id=1, source_target_pairs={{0,3},{1,17},{2,18},{3,0},{4,13},{5,6},{6,5},{7,23},{8,24},{9,25},... | collective-permute-start | bytes 98312 | tf_op jit(solution)/shard_map/ppermute | solution.py:376
  20.6 2.7 %collective-permute-start.10 = (bf16[128,128]{1,0:T(8,128)(2,1)S(1)}, bf16[128,128]{1,0:T(8,128)(2,1)S(1)}, u32[]{:S(2)}, u32[]{:S(2)}) collective-permute-start(bf16[128,128]{1,0:T(8,128)(2,1)S(1)} %get-tuple-element.108), channel_id=1, source_target_pairs={{0,1},{1,0},{2,5},{3,4},{4,3},{5,2},{6,7},{7,6},{8,9},{9,8},{10,11... | collective-permute-start | bytes 98312 | tf_op jit(solution)/shard_map/ppermute | solution.py:376
  20.6 2.7 %collective-permute-start.11 = (bf16[128,128]{1,0:T(8,128)(2,1)S(1)}, bf16[128,128]{1,0:T(8,128)(2,1)S(1)}, u32[]{:S(2)}, u32[]{:S(2)}) collective-permute-start(bf16[128,128]{1,0:T(8,128)(2,1)S(1)} %get-tuple-element.109), channel_id=1, source_target_pairs={{0,1},{1,0},{2,3},{3,2},{4,5},{5,4},{6,7},{7,6},{8,9},{9,8},{10,11... | collective-permute-start | bytes 98312 | tf_op jit(solution)/shard_map/ppermute | solution.py:376
  23.8 5.5 %collective-permute-start.12 = (bf16[128,128]{1,0:T(8,128)(2,1)S(1)}, bf16[128,128]{1,0:T(8,128)(2,1)S(1)}, u32[]{:S(2)}, u32[]{:S(2)}) collective-permute-start(bf16[128,128]{1,0:T(8,128)(2,1)S(1)} %get-tuple-element.115), channel_id=1, source_target_pairs={{0,16},{1,2},{2,1},{3,19},{4,20},{5,21},{6,22},{7,8},{8,7},{9,10},... | collective-permute-start | bytes 98312 | tf_op jit(solution)/shard_map/ppermute | solution.py:376
  26.0 4.8 %collective-permute-start.13 = (bf16[128,128]{1,0:T(8,128)(2,1)S(1)}, bf16[128,128]{1,0:T(8,128)(2,1)S(1)}, u32[]{:S(2)}, u32[]{:S(2)}) collective-permute-start(bf16[128,128]{1,0:T(8,128)(2,1)S(1)} %get-tuple-element.116), channel_id=1, source_target_pairs={{0,3},{1,17},{2,18},{3,0},{4,13},{5,6},{6,5},{7,23},{8,24},{9,25},... | collective-permute-start | bytes 98312 | tf_op jit(solution)/shard_map/ppermute | solution.py:376
  27.5 3.3 %collective-permute-start.14 = (bf16[128,128]{1,0:T(8,128)(2,1)S(1)}, bf16[128,128]{1,0:T(8,128)(2,1)S(1)}, u32[]{:S(2)}, u32[]{:S(2)}) collective-permute-start(bf16[128,128]{1,0:T(8,128)(2,1)S(1)} %get-tuple-element.117), channel_id=1, source_target_pairs={{0,1},{1,0},{2,5},{3,4},{4,3},{5,2},{6,7},{7,6},{8,9},{9,8},{10,11... | collective-permute-start | bytes 98312 | tf_op jit(solution)/shard_map/ppermute | solution.py:376
  27.5 3.3 %collective-permute-start.15 = (bf16[128,128]{1,0:T(8,128)(2,1)S(1)}, bf16[128,128]{1,0:T(8,128)(2,1)S(1)}, u32[]{:S(2)}, u32[]{:S(2)}) collective-permute-start(bf16[128,128]{1,0:T(8,128)(2,1)S(1)} %get-tuple-element.118), channel_id=1, source_target_pairs={{0,1},{1,0},{2,3},{3,2},{4,5},{5,4},{6,7},{7,6},{8,9},{9,8},{10,11... | collective-permute-start | bytes 98312 | tf_op jit(solution)/shard_map/ppermute | solution.py:376
  31.2 5.2 %collective-permute-start.16 = (bf16[128,128]{1,0:T(8,128)(2,1)S(1)}, bf16[128,128]{1,0:T(8,128)(2,1)S(1)}, u32[]{:S(2)}, u32[]{:S(2)}) collective-permute-start(bf16[128,128]{1,0:T(8,128)(2,1)S(1)} %get-tuple-element.124), channel_id=1, source_target_pairs={{0,16},{1,2},{2,1},{3,19},{4,20},{5,21},{6,22},{7,8},{8,7},{9,10},... | collective-permute-start | bytes 98312 | tf_op jit(solution)/shard_map/ppermute | solution.py:376
  32.2 4.8 %collective-permute-start.17 = (bf16[128,128]{1,0:T(8,128)(2,1)S(1)}, bf16[128,128]{1,0:T(8,128)(2,1)S(1)}, u32[]{:S(2)}, u32[]{:S(2)}) collective-permute-start(bf16[128,128]{1,0:T(8,128)(2,1)S(1)} %get-tuple-element.125), channel_id=1, source_target_pairs={{0,3},{1,17},{2,18},{3,0},{4,13},{5,6},{6,5},{7,23},{8,24},{9,25},... | collective-permute-start | bytes 98312 | tf_op jit(solution)/shard_map/ppermute | solution.py:376
  34.0 3.1 %collective-permute-start.18 = (bf16[128,128]{1,0:T(8,128)(2,1)S(1)}, bf16[128,128]{1,0:T(8,128)(2,1)S(1)}, u32[]{:S(2)}, u32[]{:S(2)}) collective-permute-start(bf16[128,128]{1,0:T(8,128)(2,1)S(1)} %get-tuple-element.126), channel_id=1, source_target_pairs={{0,1},{1,0},{2,5},{3,4},{4,3},{5,2},{6,7},{7,6},{8,9},{9,8},{10,11... | collective-permute-start | bytes 98312 | tf_op jit(solution)/shard_map/ppermute | solution.py:376
  34.0 3.1 %collective-permute-start.19 = (bf16[128,128]{1,0:T(8,128)(2,1)S(1)}, bf16[128,128]{1,0:T(8,128)(2,1)S(1)}, u32[]{:S(2)}, u32[]{:S(2)}) collective-permute-start(bf16[128,128]{1,0:T(8,128)(2,1)S(1)} %get-tuple-element.127), channel_id=1, source_target_pairs={{0,1},{1,0},{2,3},{3,2},{4,5},{5,4},{6,7},{7,6},{8,9},{9,8},{10,11... | collective-permute-start | bytes 98312 | tf_op jit(solution)/shard_map/ppermute | solution.py:376
  37.4 5.2 %collective-permute-start.20 = (bf16[128,128]{1,0:T(8,128)(2,1)S(1)}, bf16[128,128]{1,0:T(8,128)(2,1)S(1)}, u32[]{:S(2)}, u32[]{:S(2)}) collective-permute-start(bf16[128,128]{1,0:T(8,128)(2,1)S(1)} %get-tuple-element.132), channel_id=1, source_target_pairs={{0,16},{1,2},{2,1},{3,19},{4,20},{5,21},{6,22},{7,8},{8,7},{9,10},... | collective-permute-start | bytes 98312 | tf_op jit(solution)/shard_map/ppermute | solution.py:376
  39.0 4.8 %collective-permute-start.21 = (bf16[128,128]{1,0:T(8,128)(2,1)S(1)}, bf16[128,128]{1,0:T(8,128)(2,1)S(1)}, u32[]{:S(2)}, u32[]{:S(2)}) collective-permute-start(bf16[128,128]{1,0:T(8,128)(2,1)S(1)} %get-tuple-element.133), channel_id=1, source_target_pairs={{0,3},{1,17},{2,18},{3,0},{4,13},{5,6},{6,5},{7,23},{8,24},{9,25},... | collective-permute-start | bytes 98312 | tf_op jit(solution)/shard_map/ppermute | solution.py:376
  40.4 3.3 %collective-permute-start.22 = (bf16[128,128]{1,0:T(8,128)(2,1)S(1)}, bf16[128,128]{1,0:T(8,128)(2,1)S(1)}, u32[]{:S(2)}, u32[]{:S(2)}) collective-permute-start(bf16[128,128]{1,0:T(8,128)(2,1)S(1)} %get-tuple-element.134), channel_id=1, source_target_pairs={{0,1},{1,0},{2,5},{3,4},{4,3},{5,2},{6,7},{7,6},{8,9},{9,8},{10,11... | collective-permute-start | bytes 98312 | tf_op jit(solution)/shard_map/ppermute | solution.py:376
  40.4 3.3 %collective-permute-start.23 = (bf16[128,128]{1,0:T(8,128)(2,1)S(1)}, bf16[128,128]{1,0:T(8,128)(2,1)S(1)}, u32[]{:S(2)}, u32[]{:S(2)}) collective-permute-start(bf16[128,128]{1,0:T(8,128)(2,1)S(1)} %get-tuple-element.135), channel_id=1, source_target_pairs={{0,1},{1,0},{2,3},{3,2},{4,5},{5,4},{6,7},{7,6},{8,9},{9,8},{10,11... | collective-permute-start | bytes 98312 | tf_op jit(solution)/shard_map/ppermute | solution.py:376
  44.2 5.2 %collective-permute-start.24 = (bf16[128,128]{1,0:T(8,128)(2,1)S(1)}, bf16[128,128]{1,0:T(8,128)(2,1)S(1)}, u32[]{:S(2)}, u32[]{:S(2)}) collective-permute-start(bf16[128,128]{1,0:T(8,128)(2,1)S(1)} %get-tuple-element.140), channel_id=1, source_target_pairs={{0,16},{1,2},{2,1},{3,19},{4,20},{5,21},{6,22},{7,8},{8,7},{9,10},... | collective-permute-start | bytes 98312 | tf_op jit(solution)/shard_map/ppermute | solution.py:376
  45.2 4.8 %collective-permute-start.25 = (bf16[128,128]{1,0:T(8,128)(2,1)S(1)}, bf16[128,128]{1,0:T(8,128)(2,1)S(1)}, u32[]{:S(2)}, u32[]{:S(2)}) collective-permute-start(bf16[128,128]{1,0:T(8,128)(2,1)S(1)} %get-tuple-element.141), channel_id=1, source_target_pairs={{0,3},{1,17},{2,18},{3,0},{4,13},{5,6},{6,5},{7,23},{8,24},{9,25},... | collective-permute-start | bytes 98312 | tf_op jit(solution)/shard_map/ppermute | solution.py:376
  46.9 3.1 %collective-permute-start.26 = (bf16[128,128]{1,0:T(8,128)(2,1)S(1)}, bf16[128,128]{1,0:T(8,128)(2,1)S(1)}, u32[]{:S(2)}, u32[]{:S(2)}) collective-permute-start(bf16[128,128]{1,0:T(8,128)(2,1)S(1)} %get-tuple-element.142), channel_id=1, source_target_pairs={{0,1},{1,0},{2,5},{3,4},{4,3},{5,2},{6,7},{7,6},{8,9},{9,8},{10,11... | collective-permute-start | bytes 98312 | tf_op jit(solution)/shard_map/ppermute | solution.py:376
  46.9 3.1 %collective-permute-start.27 = (bf16[128,128]{1,0:T(8,128)(2,1)S(1)}, bf16[128,128]{1,0:T(8,128)(2,1)S(1)}, u32[]{:S(2)}, u32[]{:S(2)}) collective-permute-start(bf16[128,128]{1,0:T(8,128)(2,1)S(1)} %get-tuple-element.143), channel_id=1, source_target_pairs={{0,1},{1,0},{2,3},{3,2},{4,5},{5,4},{6,7},{7,6},{8,9},{9,8},{10,11... | collective-permute-start | bytes 98312 | tf_op jit(solution)/shard_map/ppermute | solution.py:376
  50.4 5.2 %collective-permute-start.28 = (bf16[128,128]{1,0:T(8,128)(2,1)S(1)}, bf16[128,128]{1,0:T(8,128)(2,1)S(1)}, u32[]{:S(2)}, u32[]{:S(2)}) collective-permute-start(bf16[128,128]{1,0:T(8,128)(2,1)S(1)} %get-tuple-element.147), channel_id=1, source_target_pairs={{0,16},{1,2},{2,1},{3,19},{4,20},{5,21},{6,22},{7,8},{8,7},{9,10},... | collective-permute-start | bytes 98312 | tf_op jit(solution)/shard_map/ppermute | solution.py:376
  51.9 4.8 %collective-permute-start.29 = (bf16[128,128]{1,0:T(8,128)(2,1)S(1)}, bf16[128,128]{1,0:T(8,128)(2,1)S(1)}, u32[]{:S(2)}, u32[]{:S(2)}) collective-permute-start(bf16[128,128]{1,0:T(8,128)(2,1)S(1)} %get-tuple-element.148), channel_id=1, source_target_pairs={{0,3},{1,17},{2,18},{3,0},{4,13},{5,6},{6,5},{7,23},{8,24},{9,25},... | collective-permute-start | bytes 98312 | tf_op jit(solution)/shard_map/ppermute | solution.py:376
  53.4 3.3 %collective-permute-start.30 = (bf16[128,128]{1,0:T(8,128)(2,1)S(1)}, bf16[128,128]{1,0:T(8,128)(2,1)S(1)}, u32[]{:S(2)}, u32[]{:S(2)}) collective-permute-start(bf16[128,128]{1,0:T(8,128)(2,1)S(1)} %get-tuple-element.149), channel_id=1, source_target_pairs={{0,1},{1,0},{2,5},{3,4},{4,3},{5,2},{6,7},{7,6},{8,9},{9,8},{10,11... | collective-permute-start | bytes 98312 | tf_op jit(solution)/shard_map/ppermute | solution.py:376
  53.4 3.3 %collective-permute-start.31 = (bf16[128,128]{1,0:T(8,128)(2,1)S(1)}, bf16[128,128]{1,0:T(8,128)(2,1)S(1)}, u32[]{:S(2)}, u32[]{:S(2)}) collective-permute-start(bf16[128,128]{1,0:T(8,128)(2,1)S(1)} %get-tuple-element.150), channel_id=1, source_target_pairs={{0,1},{1,0},{2,3},{3,2},{4,5},{5,4},{6,7},{7,6},{8,9},{9,8},{10,11... | collective-permute-start | bytes 98312 | tf_op jit(solution)/shard_map/ppermute | solution.py:376

commit v23 on v22

--- a/solution.py
+++ b/solution.py
@@ -387,7 +387,7 @@
             array(leads, total, BF16),
             array(8, total),
             same_as(weights),
-            array(width, width - width // 4, BF16),
+            array(width, width // 2, BF16),
             *messages,
         ],
         picks,
@@ -413,7 +413,7 @@
             full,
             some,
             array(8, total),
-            array(width, width // 4, BF16),
+            array(width, width // 2, BF16),
             same_as(schur),
         ],
         2 * total * width * width + 2 * total * total * width + picks,

time: 58 us -> 56.8 us (0.979)
  Pallas kernels: 18.1 us -> 17.3 us
  waiting for transfers between devices: 10 us -> 9.33 us
    pallas_call x17, Pallas kernels: 18.1 us -> 17.3 us  [run(): pl.pallas_call(kernel, out_shape=results, in_specs=[pl.BlockSpec(memory_s...]
    ppermute x32, waiting for transfers between devices: 10 us -> 9.33 us  [exchange(): lax.ppermute(part, 'sub', route)]
  transfers between devices with their start and end apart: 32 -> 32, of which waited for: 11 -> 14; matrix products, arithmetic and copies ran while one was open for 0% -> 0% of each run, Pallas kernels for 22% -> 21%
where the time goes in v23:
time: 56.8 us; the launch traced here: 56.6 us
  starting transfers between devices  29.1 us (51%)
  Pallas kernels  17.3 us (30%)
  waiting for transfers between devices  9.33 us (16%)
  between operations  0.81 us (1%)
    ppermute x32, starting transfers between devices, exchange(): lax.ppermute(part, 'sub', route)  29.1 us
    pallas_call x17, Pallas kernels, run(): pl.pallas_call(kernel, out_shape=results, in_specs=[pl.BlockSpec(memory_s...  17.3 us
    ppermute x32, waiting for transfers between devices, exchange(): lax.ppermute(part, 'sub', route)  9.33 us
  transfers between devices with their start and end apart: 32, of which 14 were waited for; matrix products, arithmetic and copies ran while one was open for 0% of the time, Pallas kernels for 21%

profile of v23, /device:TPU:8, one launch (start us, length us, event | category | flops | bytes accessed | tf_op | source)
XLA Modules:
  0.0 56.6 jit_solution(5262236267604181479)
XLA Ops:
  0.0 1.5 %shard_map.73 = (bf16[1024,384]{1,0:T(8,128)(2,1)S(1)}, bf16[128,1024]{1,0:T(8,128)(2,1)S(1)}, bf16[128,384]{1,0:T(8,128)(2,1)S(1)}, f32[8,384]{1,0:T(8,128)S(1)...) custom-call(s32[1,4,128]{2,1,0:T(4,128)} %rows_in.1, ...), custom_call_target="tpu_custom_call" | custom-call | flops 100663296 | bytes 4708368 | tf_op jit(solution)/shard_map/pallas_call | solution.py:341
  1.5 2.7 %collective-permute-start = (bf16[128,128]{1,0:T(8,128)(2,1)S(1)}, bf16[128,128]{1,0:T(8,128)(2,1)S(1)}, u32[]{:S(2)}, u32[]{:S(2)}) collective-permute-start(bf16[128,128]{1,0:T(8,128)(2,1)S(1)} %get-tuple-element.79), channel_id=1, source_target_pairs={{0,16},{1,2},{2,1},{3,19},{4,5},{5,4},{6,15},{7,23},{8,24},{9,25},... | collective-permute-start | bytes 98312 | tf_op jit(solution)/shard_map/ppermute | solution.py:376
  4.2 1.5 %collective-permute-start.1 = (bf16[128,128]{1,0:T(8,128)(2,1)S(1)}, bf16[128,128]{1,0:T(8,128)(2,1)S(1)}, u32[]{:S(2)}, u32[]{:S(2)}) collective-permute-start(bf16[128,128]{1,0:T(8,128)(2,1)S(1)} %get-tuple-element.80), channel_id=1, source_target_pairs={{0,2},{1,17},{2,0},{3,4},{4,3},{5,6},{6,5},{7,8},{8,7},{9,10},{10,... | collective-permute-start | bytes 98312 | tf_op jit(solution)/shard_map/ppermute | solution.py:376
  5.8 0.4 collective-permute-start.3
  6.8 2.5 %shard_map.74 = (bf16[384,1024]{1,0:T(8,128)(2,1)S(1)}, bf16[384,1024]{1,0:T(8,128)(2,1)S(1)}, bf16[384,384]{1,0:T(8,128)(2,1)S(1)}, bf16[384,384]{1,0:T(8,128)(...) custom-call(bf16[1024,384]{1,0:T(8,128)(2,1)S(1)} %get-tuple-element, ...), custom_call_target="tpu_custom_call" | custom-call | flops 1207959552 | bytes 12414980 | tf_op jit(solution)/shard_map/pallas_call | solution.py:341
  9.6 0.4 shard_map.75
  10.0 0.6 %collective-permute-start.4 = (bf16[128,128]{1,0:T(8,128)(2,1)S(1)}, bf16[128,128]{1,0:T(8,128)(2,1)S(1)}, u32[]{:S(2)}, u32[]{:S(2)}) collective-permute-start(bf16[128,128]{1,0:T(8,128)(2,1)S(1)} %get-tuple-element.93), channel_id=1, source_target_pairs={{0,16},{1,2},{2,1},{3,19},{4,5},{5,4},{6,15},{7,23},{8,24},{9,25},... | collective-permute-start | bytes 98312 | tf_op jit(solution)/shard_map/ppermute | solution.py:376
  10.6 0.9 %collective-permute-start.5 = (bf16[128,128]{1,0:T(8,128)(2,1)S(1)}, bf16[128,128]{1,0:T(8,128)(2,1)S(1)}, u32[]{:S(2)}, u32[]{:S(2)}) collective-permute-start(bf16[128,128]{1,0:T(8,128)(2,1)S(1)} %get-tuple-element.94), channel_id=1, source_target_pairs={{0,2},{1,17},{2,0},{3,4},{4,3},{5,6},{6,5},{7,8},{8,7},{9,10},{10,... | collective-permute-start | bytes 98312 | tf_op jit(solution)/shard_map/ppermute | solution.py:376
  11.4 0.5 collective-permute-start.6
  11.9 2.7 %shard_map.76 = (f32[128,1024]{1,0:T(8,128)S(1)}, f32[128,384]{1,0:T(8,128)S(1)}, bf16[1024,384]{1,0:T(8,128)(2,1)S(1)}, bf16[384,384]{1,0:T(8,128)(2,1)S(1)}) custom-call(bf16[128,128]{1,0:T(8,128)(2,1)S(1)} %collective-permute-done.refs_0_, bf16[128,128]{1,0:T(8,128)(2,1)S(1)} %collective-permute-done.1.refs_1_, ...), custom_call_target="tpu_custom_call" | custom-call | flops 1577058304 | bytes 8392704 | tf_op jit(solution)/shard_map/pallas_call | solution.py:341
  14.9 0.9 %collective-permute-done.5.refs_1_ = bf16[128,128]{1,0:T(8,128)(2,1)S(1)} collective-permute-done((bf16[128,128]{1,0:T(8,128)(2,1)S(1)}, bf16[128,128]{1,0:T(8,128)(2,1)S(1)}, u32[]{:S(2)}, u32[]{:S(2)}) %collective-permute-start.5) | collective-permute-done | bytes 32800 | tf_op jit(solution)/shard_map/ppermute | solution.py:376
  16.1 1.6 %collective-permute-start.8 = (bf16[128,128]{1,0:T(8,128)(2,1)S(1)}, bf16[128,128]{1,0:T(8,128)(2,1)S(1)}, u32[]{:S(2)}, u32[]{:S(2)}) collective-permute-start(bf16[128,128]{1,0:T(8,128)(2,1)S(1)} %get-tuple-element.106), channel_id=1, source_target_pairs={{0,16},{1,2},{2,1},{3,19},{4,20},{5,21},{6,22},{7,8},{8,7},{9,10},... | collective-permute-start | bytes 98312 | tf_op jit(solution)/shard_map/ppermute | solution.py:376
  17.8 2.2 %collective-permute-start.9 = (bf16[128,128]{1,0:T(8,128)(2,1)S(1)}, bf16[128,128]{1,0:T(8,128)(2,1)S(1)}, u32[]{:S(2)}, u32[]{:S(2)}) collective-permute-start(bf16[128,128]{1,0:T(8,128)(2,1)S(1)} %get-tuple-element.107), channel_id=1, source_target_pairs={{0,3},{1,17},{2,18},{3,0},{4,13},{5,6},{6,5},{7,23},{8,24},{9,25},... | collective-permute-start | bytes 98312 | tf_op jit(solution)/shard_map/ppermute | solution.py:376
  20.0 0.5 collective-permute-start.11
  20.5 1.0 %shard_map.78 = (f32[128,1024]{1,0:T(8,128)S(1)}, f32[128,1024]{1,0:T(8,128)S(1)}, f32[128,384]{1,0:T(8,128)S(1)}) custom-call(bf16[128,128]{1,0:T(8,128)(2,1)S(1)} %collective-permute-done.4.refs_0_, bf16[128,128]{1,0:T(8,128)(2,1)S(1)} %collective-permute-done.5.refs_1_, bf16[128,128]{1,0:T(8,128)(2,1)S(1)} %collective-permute-done.6.refs_2_, ...), custom_call_target="tpu_custom_call" | custom-call | flops 469762048 | bytes 5902336 | tf_op jit(solution)/shard_map/pallas_call | solution.py:341
  21.5 1.1 %collective-permute-done.9.refs_1_ = bf16[128,128]{1,0:T(8,128)(2,1)S(1)} collective-permute-done((bf16[128,128]{1,0:T(8,128)(2,1)S(1)}, bf16[128,128]{1,0:T(8,128)(2,1)S(1)}, u32[]{:S(2)}, u32[]{:S(2)}) %collective-permute-start.9) | collective-permute-done | bytes 32800 | tf_op jit(solution)/shard_map/ppermute | solution.py:376
  22.6 0.4 shard_map.79
  23.0 1.8 %collective-permute-start.12 = (bf16[128,128]{1,0:T(8,128)(2,1)S(1)}, bf16[128,128]{1,0:T(8,128)(2,1)S(1)}, u32[]{:S(2)}, u32[]{:S(2)}) collective-permute-start(bf16[128,128]{1,0:T(8,128)(2,1)S(1)} %get-tuple-element.115), channel_id=1, source_target_pairs={{0,16},{1,2},{2,1},{3,19},{4,20},{5,21},{6,22},{7,8},{8,7},{9,10},... | collective-permute-start | bytes 98312 | tf_op jit(solution)/shard_map/ppermute | solution.py:376
  24.8 1.6 %collective-permute-start.13 = (bf16[128,128]{1,0:T(8,128)(2,1)S(1)}, bf16[128,128]{1,0:T(8,128)(2,1)S(1)}, u32[]{:S(2)}, u32[]{:S(2)}) collective-permute-start(bf16[128,128]{1,0:T(8,128)(2,1)S(1)} %get-tuple-element.116), channel_id=1, source_target_pairs={{0,3},{1,17},{2,18},{3,0},{4,13},{5,6},{6,5},{7,23},{8,24},{9,25},... | collective-permute-start | bytes 98312 | tf_op jit(solution)/shard_map/ppermute | solution.py:376
  26.3 0.5 collective-permute-start.15
  26.8 1.3 %shard_map.80 = (f32[128,1024]{1,0:T(8,128)S(1)}, f32[128,384]{1,0:T(8,128)S(1)}) custom-call(bf16[128,128]{1,0:T(8,128)(2,1)S(1)} %collective-permute-done.8.refs_0_, bf16[128,128]{1,0:T(8,128)(2,1)S(1)} %collective-permute-done.9.refs_1_, bf16[128,128]{1,0:T(8,128)(2,1)S(1)} %collective-permute-done.10.refs_2_, ...), custom_call_target="tpu_custom_call" | custom-call | flops 469762048 | bytes 5738496 | tf_op jit(solution)/shard_map/pallas_call | solution.py:341
  28.4 1.1 %collective-permute-done.13.refs_1_ = bf16[128,128]{1,0:T(8,128)(2,1)S(1)} collective-permute-done((bf16[128,128]{1,0:T(8,128)(2,1)S(1)}, bf16[128,128]{1,0:T(8,128)(2,1)S(1)}, u32[]{:S(2)}, u32[]{:S(2)}) %collective-permute-start.13) | collective-permute-done | bytes 32800 | tf_op jit(solution)/shard_map/ppermute | solution.py:376
  30.0 1.2 %collective-permute-start.16 = (bf16[128,128]{1,0:T(8,128)(2,1)S(1)}, bf16[128,128]{1,0:T(8,128)(2,1)S(1)}, u32[]{:S(2)}, u32[]{:S(2)}) collective-permute-start(bf16[128,128]{1,0:T(8,128)(2,1)S(1)} %get-tuple-element.124), channel_id=1, source_target_pairs={{0,16},{1,2},{2,1},{3,19},{4,20},{5,21},{6,22},{7,8},{8,7},{9,10},... | collective-permute-start | bytes 98312 | tf_op jit(solution)/shard_map/ppermute | solution.py:376
  31.2 2.0 %collective-permute-start.17 = (bf16[128,128]{1,0:T(8,128)(2,1)S(1)}, bf16[128,128]{1,0:T(8,128)(2,1)S(1)}, u32[]{:S(2)}, u32[]{:S(2)}) collective-permute-start(bf16[128,128]{1,0:T(8,128)(2,1)S(1)} %get-tuple-element.125), channel_id=1, source_target_pairs={{0,3},{1,17},{2,18},{3,0},{4,13},{5,6},{6,5},{7,23},{8,24},{9,25},... | collective-permute-start | bytes 98312 | tf_op jit(solution)/shard_map/ppermute | solution.py:376
  33.2 0.5 collective-permute-start.19
  33.7 1.0 %shard_map.82 = (f32[128,1024]{1,0:T(8,128)S(1)}, f32[128,1024]{1,0:T(8,128)S(1)}, f32[128,384]{1,0:T(8,128)S(1)}) custom-call(bf16[128,128]{1,0:T(8,128)(2,1)S(1)} %collective-permute-done.12.refs_0_, bf16[128,128]{1,0:T(8,128)(2,1)S(1)} %collective-permute-done.13.refs_1_, bf16[128,128]{1,0:T(8,128)(2,1)S(1)} %collective-permute-done.14.refs_2_, ...), custom_call_target="tpu_custom_call" | custom-call | flops 469762048 | bytes 5902336 | tf_op jit(solution)/shard_map/pallas_call | solution.py:341
  34.7 0.6 collective-permute-done.16.refs_0_
  35.3 0.7 %collective-permute-done.17.refs_1_ = bf16[128,128]{1,0:T(8,128)(2,1)S(1)} collective-permute-done((bf16[128,128]{1,0:T(8,128)(2,1)S(1)}, bf16[128,128]{1,0:T(8,128)(2,1)S(1)}, u32[]{:S(2)}, u32[]{:S(2)}) %collective-permute-start.17) | collective-permute-done | bytes 32800 | tf_op jit(solution)/shard_map/ppermute | solution.py:376
  36.0 0.4 shard_map.83
  36.4 1.3 %collective-permute-start.20 = (bf16[128,128]{1,0:T(8,128)(2,1)S(1)}, bf16[128,128]{1,0:T(8,128)(2,1)S(1)}, u32[]{:S(2)}, u32[]{:S(2)}) collective-permute-start(bf16[128,128]{1,0:T(8,128)(2,1)S(1)} %get-tuple-element.132), channel_id=1, source_target_pairs={{0,16},{1,2},{2,1},{3,19},{4,20},{5,21},{6,22},{7,8},{8,7},{9,10},... | collective-permute-start | bytes 98312 | tf_op jit(solution)/shard_map/ppermute | solution.py:376
  37.7 1.6 %collective-permute-start.21 = (bf16[128,128]{1,0:T(8,128)(2,1)S(1)}, bf16[128,128]{1,0:T(8,128)(2,1)S(1)}, u32[]{:S(2)}, u32[]{:S(2)}) collective-permute-start(bf16[128,128]{1,0:T(8,128)(2,1)S(1)} %get-tuple-element.133), channel_id=1, source_target_pairs={{0,3},{1,17},{2,18},{3,0},{4,13},{5,6},{6,5},{7,23},{8,24},{9,25},... | collective-permute-start | bytes 98312 | tf_op jit(solution)/shard_map/ppermute | solution.py:376
  39.3 0.5 collective-permute-start.23
  39.8 1.3 %shard_map.84 = (f32[128,1024]{1,0:T(8,128)S(1)}, f32[128,384]{1,0:T(8,128)S(1)}) custom-call(bf16[128,128]{1,0:T(8,128)(2,1)S(1)} %collective-permute-done.16.refs_0_, bf16[128,128]{1,0:T(8,128)(2,1)S(1)} %collective-permute-done.17.refs_1_, bf16[128,128]{1,0:T(8,128)(2,1)S(1)} %collective-permute-done.18.refs_2_, ...), custom_call_target="tpu_custom_call" | custom-call | flops 469762048 | bytes 5738496 | tf_op jit(solution)/shard_map/pallas_call | solution.py:341
  41.1 0.5 collective-permute-done.20.refs_0_
  41.6 0.9 %collective-permute-done.21.refs_1_ = bf16[128,128]{1,0:T(8,128)(2,1)S(1)} collective-permute-done((bf16[128,128]{1,0:T(8,128)(2,1)S(1)}, bf16[128,128]{1,0:T(8,128)(2,1)S(1)}, u32[]{:S(2)}, u32[]{:S(2)}) %collective-permute-start.21) | collective-permute-done | bytes 32800 | tf_op jit(solution)/shard_map/ppermute | solution.py:376
  43.0 1.2 %collective-permute-start.24 = (bf16[128,128]{1,0:T(8,128)(2,1)S(1)}, bf16[128,128]{1,0:T(8,128)(2,1)S(1)}, u32[]{:S(2)}, u32[]{:S(2)}) collective-permute-start(bf16[128,128]{1,0:T(8,128)(2,1)S(1)} %get-tuple-element.140), channel_id=1, source_target_pairs={{0,16},{1,2},{2,1},{3,19},{4,20},{5,21},{6,22},{7,8},{8,7},{9,10},... | collective-permute-start | bytes 98312 | tf_op jit(solution)/shard_map/ppermute | solution.py:376
  44.1 2.0 %collective-permute-start.25 = (bf16[128,128]{1,0:T(8,128)(2,1)S(1)}, bf16[128,128]{1,0:T(8,128)(2,1)S(1)}, u32[]{:S(2)}, u32[]{:S(2)}) collective-permute-start(bf16[128,128]{1,0:T(8,128)(2,1)S(1)} %get-tuple-element.141), channel_id=1, source_target_pairs={{0,3},{1,17},{2,18},{3,0},{4,13},{5,6},{6,5},{7,23},{8,24},{9,25},... | collective-permute-start | bytes 98312 | tf_op jit(solution)/shard_map/ppermute | solution.py:376
  46.2 0.5 collective-permute-start.27
  46.7 1.0 %shard_map.86 = (f32[128,1024]{1,0:T(8,128)S(1)}, f32[128,1024]{1,0:T(8,128)S(1)}, f32[128,384]{1,0:T(8,128)S(1)}) custom-call(bf16[128,128]{1,0:T(8,128)(2,1)S(1)} %collective-permute-done.20.refs_0_, bf16[128,128]{1,0:T(8,128)(2,1)S(1)} %collective-permute-done.21.refs_1_, bf16[128,128]{1,0:T(8,128)(2,1)S(1)} %collective-permute-done.22.refs_2_, ...), custom_call_target="tpu_custom_call" | custom-call | flops 469762048 | bytes 5902336 | tf_op jit(solution)/shard_map/pallas_call | solution.py:341
  47.7 0.5 collective-permute-done.24.refs_0_
  48.2 0.8 %collective-permute-done.25.refs_1_ = bf16[128,128]{1,0:T(8,128)(2,1)S(1)} collective-permute-done((bf16[128,128]{1,0:T(8,128)(2,1)S(1)}, bf16[128,128]{1,0:T(8,128)(2,1)S(1)}, u32[]{:S(2)}, u32[]{:S(2)}) %collective-permute-start.25) | collective-permute-done | bytes 32800 | tf_op jit(solution)/shard_map/ppermute | solution.py:376
  49.4 1.3 %collective-permute-start.28 = (bf16[128,128]{1,0:T(8,128)(2,1)S(1)}, bf16[128,128]{1,0:T(8,128)(2,1)S(1)}, u32[]{:S(2)}, u32[]{:S(2)}) collective-permute-start(bf16[128,128]{1,0:T(8,128)(2,1)S(1)} %get-tuple-element.147), channel_id=1, source_target_pairs={{0,16},{1,2},{2,1},{3,19},{4,20},{5,21},{6,22},{7,8},{8,7},{9,10},... | collective-permute-start | bytes 98312 | tf_op jit(solution)/shard_map/ppermute | solution.py:376
  50.7 1.6 %collective-permute-start.29 = (bf16[128,128]{1,0:T(8,128)(2,1)S(1)}, bf16[128,128]{1,0:T(8,128)(2,1)S(1)}, u32[]{:S(2)}, u32[]{:S(2)}) collective-permute-start(bf16[128,128]{1,0:T(8,128)(2,1)S(1)} %get-tuple-element.148), channel_id=1, source_target_pairs={{0,3},{1,17},{2,18},{3,0},{4,13},{5,6},{6,5},{7,23},{8,24},{9,25},... | collective-permute-start | bytes 98312 | tf_op jit(solution)/shard_map/ppermute | solution.py:376
  52.3 0.5 collective-permute-start.31
  52.8 1.2 %shard_map.88.refs_5_ = f32[1024,128]{1,0:T(8,128)S(1)} custom-call(bf16[128,128]{1,0:T(8,128)(2,1)S(1)} %collective-permute-done.24.refs_0_, bf16[128,128]{1,0:T(8,128)(2,1)S(1)} %collective-permute-done.25.refs_1_, bf16[128,128]{1,0:T(8,128)(2,1)S(1)} %collective-permute-done.26.refs_2_, bf16[128,128]{1,0:T(8,128)(2,1)S(1)} %collective-permute-done.27.refs_3_, ...), custom_call_target="tpu_custom_call" | custom-call | flops 369098752 | bytes 4624384 | tf_op jit(solution)/shard_map/pallas_call | solution.py:341
  54.0 0.6 collective-permute-done.28.refs_0_
  54.6 0.9 %collective-permute-done.29.refs_1_ = bf16[128,128]{1,0:T(8,128)(2,1)S(1)} collective-permute-done((bf16[128,128]{1,0:T(8,128)(2,1)S(1)}, bf16[128,128]{1,0:T(8,128)(2,1)S(1)}, u32[]{:S(2)}, u32[]{:S(2)}) %collective-permute-start.29) | collective-permute-done | bytes 32800 | tf_op jit(solution)/shard_map/ppermute | solution.py:376
  55.5 1.1 %shard_map.89 = f32[1,1024,128]{2,1,0:T(8,128)} custom-call(bf16[128,128]{1,0:T(8,128)(2,1)S(1)} %collective-permute-done.28.refs_0_, bf16[128,128]{1,0:T(8,128)(2,1)S(1)} %collective-permute-done.29.refs_1_, bf16[128,128]{1,0:T(8,128)(2,1)S(1)} %collective-permute-done.30.refs_2_, bf16[128,128]{1,0:T(8,128)(2,1)S(1)} %collective-permute-done.31.refs_3_, ...), custom_call_target="tpu_custom_call" | custom-call | flops 100663296 | bytes 1966080 | tf_op jit(solution)/shard_map/pallas_call | solution.py:341
  (33 shorter events, 2.5 us)
Async XLA Ops:
  1.5 7.8 %collective-permute-start = (bf16[128,128]{1,0:T(8,128)(2,1)S(1)}, bf16[128,128]{1,0:T(8,128)(2,1)S(1)}, u32[]{:S(2)}, u32[]{:S(2)}) collective-permute-start(bf16[128,128]{1,0:T(8,128)(2,1)S(1)} %get-tuple-element.79), channel_id=1, source_target_pairs={{0,16},{1,2},{2,1},{3,19},{4,5},{5,4},{6,15},{7,23},{8,24},{9,25},... | collective-permute-start | bytes 98312 | tf_op jit(solution)/shard_map/ppermute | solution.py:376
  4.2 5.4 %collective-permute-start.1 = (bf16[128,128]{1,0:T(8,128)(2,1)S(1)}, bf16[128,128]{1,0:T(8,128)(2,1)S(1)}, u32[]{:S(2)}, u32[]{:S(2)}) collective-permute-start(bf16[128,128]{1,0:T(8,128)(2,1)S(1)} %get-tuple-element.80), channel_id=1, source_target_pairs={{0,2},{1,17},{2,0},{3,4},{4,3},{5,6},{6,5},{7,8},{8,7},{9,10},{10,... | collective-permute-start | bytes 98312 | tf_op jit(solution)/shard_map/ppermute | solution.py:376
  5.6 3.9 %collective-permute-start.2 = (bf16[128,128]{1,0:T(8,128)(2,1)S(1)}, bf16[128,128]{1,0:T(8,128)(2,1)S(1)}, u32[]{:S(2)}, u32[]{:S(2)}) collective-permute-start(bf16[128,128]{1,0:T(8,128)(2,1)S(1)} %get-tuple-element.81), channel_id=1, source_target_pairs={{0,1},{1,0},{2,18},{3,7},{4,20},{5,21},{6,22},{7,3},{8,9},{9,8},{1... | collective-permute-start | bytes 98312 | tf_op jit(solution)/shard_map/ppermute | solution.py:376
  5.8 3.8 %collective-permute-start.3 = (bf16[128,128]{1,0:T(8,128)(2,1)S(1)}, bf16[128,128]{1,0:T(8,128)(2,1)S(1)}, u32[]{:S(2)}, u32[]{:S(2)}) collective-permute-start(bf16[128,128]{1,0:T(8,128)(2,1)S(1)} %get-tuple-element.82), channel_id=1, source_target_pairs={{0,1},{1,0},{2,3},{3,2},{4,5},{5,4},{6,7},{7,6},{8,9},{9,8},{10,11... | collective-permute-start | bytes 98312 | tf_op jit(solution)/shard_map/ppermute | solution.py:376
  10.0 4.9 %collective-permute-start.4 = (bf16[128,128]{1,0:T(8,128)(2,1)S(1)}, bf16[128,128]{1,0:T(8,128)(2,1)S(1)}, u32[]{:S(2)}, u32[]{:S(2)}) collective-permute-start(bf16[128,128]{1,0:T(8,128)(2,1)S(1)} %get-tuple-element.93), channel_id=1, source_target_pairs={{0,16},{1,2},{2,1},{3,19},{4,5},{5,4},{6,15},{7,23},{8,24},{9,25},... | collective-permute-start | bytes 98312 | tf_op jit(solution)/shard_map/ppermute | solution.py:376
  10.6 5.1 %collective-permute-start.5 = (bf16[128,128]{1,0:T(8,128)(2,1)S(1)}, bf16[128,128]{1,0:T(8,128)(2,1)S(1)}, u32[]{:S(2)}, u32[]{:S(2)}) collective-permute-start(bf16[128,128]{1,0:T(8,128)(2,1)S(1)} %get-tuple-element.94), channel_id=1, source_target_pairs={{0,2},{1,17},{2,0},{3,4},{4,3},{5,6},{6,5},{7,8},{8,7},{9,10},{10,... | collective-permute-start | bytes 98312 | tf_op jit(solution)/shard_map/ppermute | solution.py:376
  11.4 4.3 %collective-permute-start.6 = (bf16[128,128]{1,0:T(8,128)(2,1)S(1)}, bf16[128,128]{1,0:T(8,128)(2,1)S(1)}, u32[]{:S(2)}, u32[]{:S(2)}) collective-permute-start(bf16[128,128]{1,0:T(8,128)(2,1)S(1)} %get-tuple-element.95), channel_id=1, source_target_pairs={{0,1},{1,0},{2,18},{3,7},{4,20},{5,21},{6,22},{7,3},{8,9},{9,8},{1... | collective-permute-start | bytes 98312 | tf_op jit(solution)/shard_map/ppermute | solution.py:376
  11.9 3.8 %collective-permute-start.7 = (bf16[128,128]{1,0:T(8,128)(2,1)S(1)}, bf16[128,128]{1,0:T(8,128)(2,1)S(1)}, u32[]{:S(2)}, u32[]{:S(2)}) collective-permute-start(bf16[128,128]{1,0:T(8,128)(2,1)S(1)} %get-tuple-element.96), channel_id=1, source_target_pairs={{0,1},{1,0},{2,3},{3,2},{4,5},{5,4},{6,7},{7,6},{8,9},{9,8},{10,11... | collective-permute-start | bytes 98312 | tf_op jit(solution)/shard_map/ppermute | solution.py:376
  16.1 5.4 %collective-permute-start.8 = (bf16[128,128]{1,0:T(8,128)(2,1)S(1)}, bf16[128,128]{1,0:T(8,128)(2,1)S(1)}, u32[]{:S(2)}, u32[]{:S(2)}) collective-permute-start(bf16[128,128]{1,0:T(8,128)(2,1)S(1)} %get-tuple-element.106), channel_id=1, source_target_pairs={{0,16},{1,2},{2,1},{3,19},{4,20},{5,21},{6,22},{7,8},{8,7},{9,10},... | collective-permute-start | bytes 98312 | tf_op jit(solution)/shard_map/ppermute | solution.py:376
  17.8 4.8 %collective-permute-start.9 = (bf16[128,128]{1,0:T(8,128)(2,1)S(1)}, bf16[128,128]{1,0:T(8,128)(2,1)S(1)}, u32[]{:S(2)}, u32[]{:S(2)}) collective-permute-start(bf16[128,128]{1,0:T(8,128)(2,1)S(1)} %get-tuple-element.107), channel_id=1, source_target_pairs={{0,3},{1,17},{2,18},{3,0},{4,13},{5,6},{6,5},{7,23},{8,24},{9,25},... | collective-permute-start | bytes 98312 | tf_op jit(solution)/shard_map/ppermute | solution.py:376
  20.0 2.6 %collective-permute-start.10 = (bf16[128,128]{1,0:T(8,128)(2,1)S(1)}, bf16[128,128]{1,0:T(8,128)(2,1)S(1)}, u32[]{:S(2)}, u32[]{:S(2)}) collective-permute-start(bf16[128,128]{1,0:T(8,128)(2,1)S(1)} %get-tuple-element.108), channel_id=1, source_target_pairs={{0,1},{1,0},{2,5},{3,4},{4,3},{5,2},{6,7},{7,6},{8,9},{9,8},{10,11... | collective-permute-start | bytes 98312 | tf_op jit(solution)/shard_map/ppermute | solution.py:376
  20.0 2.6 %collective-permute-start.11 = (bf16[128,128]{1,0:T(8,128)(2,1)S(1)}, bf16[128,128]{1,0:T(8,128)(2,1)S(1)}, u32[]{:S(2)}, u32[]{:S(2)}) collective-permute-start(bf16[128,128]{1,0:T(8,128)(2,1)S(1)} %get-tuple-element.109), channel_id=1, source_target_pairs={{0,1},{1,0},{2,3},{3,2},{4,5},{5,4},{6,7},{7,6},{8,9},{9,8},{10,11... | collective-permute-start | bytes 98312 | tf_op jit(solution)/shard_map/ppermute | solution.py:376
  23.0 5.4 %collective-permute-start.12 = (bf16[128,128]{1,0:T(8,128)(2,1)S(1)}, bf16[128,128]{1,0:T(8,128)(2,1)S(1)}, u32[]{:S(2)}, u32[]{:S(2)}) collective-permute-start(bf16[128,128]{1,0:T(8,128)(2,1)S(1)} %get-tuple-element.115), channel_id=1, source_target_pairs={{0,16},{1,2},{2,1},{3,19},{4,20},{5,21},{6,22},{7,8},{8,7},{9,10},... | collective-permute-start | bytes 98312 | tf_op jit(solution)/shard_map/ppermute | solution.py:376
  24.8 4.8 %collective-permute-start.13 = (bf16[128,128]{1,0:T(8,128)(2,1)S(1)}, bf16[128,128]{1,0:T(8,128)(2,1)S(1)}, u32[]{:S(2)}, u32[]{:S(2)}) collective-permute-start(bf16[128,128]{1,0:T(8,128)(2,1)S(1)} %get-tuple-element.116), channel_id=1, source_target_pairs={{0,3},{1,17},{2,18},{3,0},{4,13},{5,6},{6,5},{7,23},{8,24},{9,25},... | collective-permute-start | bytes 98312 | tf_op jit(solution)/shard_map/ppermute | solution.py:376
  26.3 3.2 %collective-permute-start.14 = (bf16[128,128]{1,0:T(8,128)(2,1)S(1)}, bf16[128,128]{1,0:T(8,128)(2,1)S(1)}, u32[]{:S(2)}, u32[]{:S(2)}) collective-permute-start(bf16[128,128]{1,0:T(8,128)(2,1)S(1)} %get-tuple-element.117), channel_id=1, source_target_pairs={{0,1},{1,0},{2,5},{3,4},{4,3},{5,2},{6,7},{7,6},{8,9},{9,8},{10,11... | collective-permute-start | bytes 98312 | tf_op jit(solution)/shard_map/ppermute | solution.py:376
  26.3 3.2 %collective-permute-start.15 = (bf16[128,128]{1,0:T(8,128)(2,1)S(1)}, bf16[128,128]{1,0:T(8,128)(2,1)S(1)}, u32[]{:S(2)}, u32[]{:S(2)}) collective-permute-start(bf16[128,128]{1,0:T(8,128)(2,1)S(1)} %get-tuple-element.118), channel_id=1, source_target_pairs={{0,1},{1,0},{2,3},{3,2},{4,5},{5,4},{6,7},{7,6},{8,9},{9,8},{10,11... | collective-permute-start | bytes 98312 | tf_op jit(solution)/shard_map/ppermute | solution.py:376
  30.0 5.3 %collective-permute-start.16 = (bf16[128,128]{1,0:T(8,128)(2,1)S(1)}, bf16[128,128]{1,0:T(8,128)(2,1)S(1)}, u32[]{:S(2)}, u32[]{:S(2)}) collective-permute-start(bf16[128,128]{1,0:T(8,128)(2,1)S(1)} %get-tuple-element.124), channel_id=1, source_target_pairs={{0,16},{1,2},{2,1},{3,19},{4,20},{5,21},{6,22},{7,8},{8,7},{9,10},... | collective-permute-start | bytes 98312 | tf_op jit(solution)/shard_map/ppermute | solution.py:376
  31.2 4.8 %collective-permute-start.17 = (bf16[128,128]{1,0:T(8,128)(2,1)S(1)}, bf16[128,128]{1,0:T(8,128)(2,1)S(1)}, u32[]{:S(2)}, u32[]{:S(2)}) collective-permute-start(bf16[128,128]{1,0:T(8,128)(2,1)S(1)} %get-tuple-element.125), channel_id=1, source_target_pairs={{0,3},{1,17},{2,18},{3,0},{4,13},{5,6},{6,5},{7,23},{8,24},{9,25},... | collective-permute-start | bytes 98312 | tf_op jit(solution)/shard_map/ppermute | solution.py:376
  33.2 2.8 %collective-permute-start.18 = (bf16[128,128]{1,0:T(8,128)(2,1)S(1)}, bf16[128,128]{1,0:T(8,128)(2,1)S(1)}, u32[]{:S(2)}, u32[]{:S(2)}) collective-permute-start(bf16[128,128]{1,0:T(8,128)(2,1)S(1)} %get-tuple-element.126), channel_id=1, source_target_pairs={{0,1},{1,0},{2,5},{3,4},{4,3},{5,2},{6,7},{7,6},{8,9},{9,8},{10,11... | collective-permute-start | bytes 98312 | tf_op jit(solution)/shard_map/ppermute | solution.py:376
  33.2 2.8 %collective-permute-start.19 = (bf16[128,128]{1,0:T(8,128)(2,1)S(1)}, bf16[128,128]{1,0:T(8,128)(2,1)S(1)}, u32[]{:S(2)}, u32[]{:S(2)}) collective-permute-start(bf16[128,128]{1,0:T(8,128)(2,1)S(1)} %get-tuple-element.127), channel_id=1, source_target_pairs={{0,1},{1,0},{2,3},{3,2},{4,5},{5,4},{6,7},{7,6},{8,9},{9,8},{10,11... | collective-permute-start | bytes 98312 | tf_op jit(solution)/shard_map/ppermute | solution.py:376
  36.4 5.2 %collective-permute-start.20 = (bf16[128,128]{1,0:T(8,128)(2,1)S(1)}, bf16[128,128]{1,0:T(8,128)(2,1)S(1)}, u32[]{:S(2)}, u32[]{:S(2)}) collective-permute-start(bf16[128,128]{1,0:T(8,128)(2,1)S(1)} %get-tuple-element.132), channel_id=1, source_target_pairs={{0,16},{1,2},{2,1},{3,19},{4,20},{5,21},{6,22},{7,8},{8,7},{9,10},... | collective-permute-start | bytes 98312 | tf_op jit(solution)/shard_map/ppermute | solution.py:376
  37.7 4.8 %collective-permute-start.21 = (bf16[128,128]{1,0:T(8,128)(2,1)S(1)}, bf16[128,128]{1,0:T(8,128)(2,1)S(1)}, u32[]{:S(2)}, u32[]{:S(2)}) collective-permute-start(bf16[128,128]{1,0:T(8,128)(2,1)S(1)} %get-tuple-element.133), channel_id=1, source_target_pairs={{0,3},{1,17},{2,18},{3,0},{4,13},{5,6},{6,5},{7,23},{8,24},{9,25},... | collective-permute-start | bytes 98312 | tf_op jit(solution)/shard_map/ppermute | solution.py:376
  39.3 3.2 %collective-permute-start.22 = (bf16[128,128]{1,0:T(8,128)(2,1)S(1)}, bf16[128,128]{1,0:T(8,128)(2,1)S(1)}, u32[]{:S(2)}, u32[]{:S(2)}) collective-permute-start(bf16[128,128]{1,0:T(8,128)(2,1)S(1)} %get-tuple-element.134), channel_id=1, source_target_pairs={{0,1},{1,0},{2,5},{3,4},{4,3},{5,2},{6,7},{7,6},{8,9},{9,8},{10,11... | collective-permute-start | bytes 98312 | tf_op jit(solution)/shard_map/ppermute | solution.py:376
  39.3 3.2 %collective-permute-start.23 = (bf16[128,128]{1,0:T(8,128)(2,1)S(1)}, bf16[128,128]{1,0:T(8,128)(2,1)S(1)}, u32[]{:S(2)}, u32[]{:S(2)}) collective-permute-start(bf16[128,128]{1,0:T(8,128)(2,1)S(1)} %get-tuple-element.135), channel_id=1, source_target_pairs={{0,1},{1,0},{2,3},{3,2},{4,5},{5,4},{6,7},{7,6},{8,9},{9,8},{10,11... | collective-permute-start | bytes 98312 | tf_op jit(solution)/shard_map/ppermute | solution.py:376
  43.0 5.2 %collective-permute-start.24 = (bf16[128,128]{1,0:T(8,128)(2,1)S(1)}, bf16[128,128]{1,0:T(8,128)(2,1)S(1)}, u32[]{:S(2)}, u32[]{:S(2)}) collective-permute-start(bf16[128,128]{1,0:T(8,128)(2,1)S(1)} %get-tuple-element.140), channel_id=1, source_target_pairs={{0,16},{1,2},{2,1},{3,19},{4,20},{5,21},{6,22},{7,8},{8,7},{9,10},... | collective-permute-start | bytes 98312 | tf_op jit(solution)/shard_map/ppermute | solution.py:376
  44.1 4.8 %collective-permute-start.25 = (bf16[128,128]{1,0:T(8,128)(2,1)S(1)}, bf16[128,128]{1,0:T(8,128)(2,1)S(1)}, u32[]{:S(2)}, u32[]{:S(2)}) collective-permute-start(bf16[128,128]{1,0:T(8,128)(2,1)S(1)} %get-tuple-element.141), channel_id=1, source_target_pairs={{0,3},{1,17},{2,18},{3,0},{4,13},{5,6},{6,5},{7,23},{8,24},{9,25},... | collective-permute-start | bytes 98312 | tf_op jit(solution)/shard_map/ppermute | solution.py:376
  46.2 2.8 %collective-permute-start.26 = (bf16[128,128]{1,0:T(8,128)(2,1)S(1)}, bf16[128,128]{1,0:T(8,128)(2,1)S(1)}, u32[]{:S(2)}, u32[]{:S(2)}) collective-permute-start(bf16[128,128]{1,0:T(8,128)(2,1)S(1)} %get-tuple-element.142), channel_id=1, source_target_pairs={{0,1},{1,0},{2,5},{3,4},{4,3},{5,2},{6,7},{7,6},{8,9},{9,8},{10,11... | collective-permute-start | bytes 98312 | tf_op jit(solution)/shard_map/ppermute | solution.py:376
  46.2 2.8 %collective-permute-start.27 = (bf16[128,128]{1,0:T(8,128)(2,1)S(1)}, bf16[128,128]{1,0:T(8,128)(2,1)S(1)}, u32[]{:S(2)}, u32[]{:S(2)}) collective-permute-start(bf16[128,128]{1,0:T(8,128)(2,1)S(1)} %get-tuple-element.143), channel_id=1, source_target_pairs={{0,1},{1,0},{2,3},{3,2},{4,5},{5,4},{6,7},{7,6},{8,9},{9,8},{10,11... | collective-permute-start | bytes 98312 | tf_op jit(solution)/shard_map/ppermute | solution.py:376
  49.4 5.2 %collective-permute-start.28 = (bf16[128,128]{1,0:T(8,128)(2,1)S(1)}, bf16[128,128]{1,0:T(8,128)(2,1)S(1)}, u32[]{:S(2)}, u32[]{:S(2)}) collective-permute-start(bf16[128,128]{1,0:T(8,128)(2,1)S(1)} %get-tuple-element.147), channel_id=1, source_target_pairs={{0,16},{1,2},{2,1},{3,19},{4,20},{5,21},{6,22},{7,8},{8,7},{9,10},... | collective-permute-start | bytes 98312 | tf_op jit(solution)/shard_map/ppermute | solution.py:376
  50.7 4.8 %collective-permute-start.29 = (bf16[128,128]{1,0:T(8,128)(2,1)S(1)}, bf16[128,128]{1,0:T(8,128)(2,1)S(1)}, u32[]{:S(2)}, u32[]{:S(2)}) collective-permute-start(bf16[128,128]{1,0:T(8,128)(2,1)S(1)} %get-tuple-element.148), channel_id=1, source_target_pairs={{0,3},{1,17},{2,18},{3,0},{4,13},{5,6},{6,5},{7,23},{8,24},{9,25},... | collective-permute-start | bytes 98312 | tf_op jit(solution)/shard_map/ppermute | solution.py:376
  52.3 3.2 %collective-permute-start.30 = (bf16[128,128]{1,0:T(8,128)(2,1)S(1)}, bf16[128,128]{1,0:T(8,128)(2,1)S(1)}, u32[]{:S(2)}, u32[]{:S(2)}) collective-permute-start(bf16[128,128]{1,0:T(8,128)(2,1)S(1)} %get-tuple-element.149), channel_id=1, source_target_pairs={{0,1},{1,0},{2,5},{3,4},{4,3},{5,2},{6,7},{7,6},{8,9},{9,8},{10,11... | collective-permute-start | bytes 98312 | tf_op jit(solution)/shard_map/ppermute | solution.py:376
  52.3 3.2 %collective-permute-start.31 = (bf16[128,128]{1,0:T(8,128)(2,1)S(1)}, bf16[128,128]{1,0:T(8,128)(2,1)S(1)}, u32[]{:S(2)}, u32[]{:S(2)}) collective-permute-start(bf16[128,128]{1,0:T(8,128)(2,1)S(1)} %get-tuple-element.150), channel_id=1, source_target_pairs={{0,1},{1,0},{2,3},{3,2},{4,5},{5,4},{6,7},{7,6},{8,9},{9,8},{10,11... | collective-permute-start | bytes 98312 | tf_op jit(solution)/shard_map/ppermute | solution.py:376

commit v24 on v23

--- a/solution.py
+++ b/solution.py
@@ -11,7 +11,7 @@
 FAR = 16
 DAMPING = 0.7
 LIMIT = 16 * 2**20
-PIECES = 4
+PIECES = 8
 F32 = jnp.float32
 BF16 = jnp.bfloat16
 

time: 56.8 us -> 56.9 us (level)
  no operation moved by 1% of the time
where the time goes in v24:
time: 56.9 us; the launch traced here: 56.7 us
  starting transfers between devices  29.1 us (51%)
  Pallas kernels  17.4 us (31%)
  waiting for transfers between devices  9.33 us (16%)
  between operations  0.81 us (1%)
    ppermute x32, starting transfers between devices, exchange(): lax.ppermute(part, 'sub', route)  29.1 us
    pallas_call x17, Pallas kernels, run(): pl.pallas_call(kernel, out_shape=results, in_specs=[pl.BlockSpec(memory_s...  17.4 us
    ppermute x32, waiting for transfers between devices, exchange(): lax.ppermute(part, 'sub', route)  9.33 us
  transfers between devices with their start and end apart: 32, of which 14 were waited for; matrix products, arithmetic and copies ran while one was open for 0% of the time, Pallas kernels for 21%

profile of v24, /device:TPU:8, one launch (start us, length us, event | category | flops | bytes accessed | tf_op | source)
XLA Modules:
  0.0 56.7 jit_solution(9633532169770100820)
XLA Ops:
  0.0 1.5 %shard_map.73 = (bf16[1024,384]{1,0:T(8,128)(2,1)S(1)}, bf16[128,1024]{1,0:T(8,128)(2,1)S(1)}, bf16[128,384]{1,0:T(8,128)(2,1)S(1)}, f32[8,384]{1,0:T(8,128)S(1)...) custom-call(s32[1,4,128]{2,1,0:T(4,128)} %rows_in.1, ...), custom_call_target="tpu_custom_call" | custom-call | flops 100663296 | bytes 4708368 | tf_op jit(solution)/shard_map/pallas_call | solution.py:341
  1.5 2.7 %collective-permute-start = (bf16[128,128]{1,0:T(8,128)(2,1)S(1)}, bf16[128,128]{1,0:T(8,128)(2,1)S(1)}, u32[]{:S(2)}, u32[]{:S(2)}) collective-permute-start(bf16[128,128]{1,0:T(8,128)(2,1)S(1)} %get-tuple-element.79), channel_id=1, source_target_pairs={{0,16},{1,2},{2,1},{3,19},{4,5},{5,4},{6,15},{7,23},{8,24},{9,25},... | collective-permute-start | bytes 98312 | tf_op jit(solution)/shard_map/ppermute | solution.py:376
  4.2 1.5 %collective-permute-start.1 = (bf16[128,128]{1,0:T(8,128)(2,1)S(1)}, bf16[128,128]{1,0:T(8,128)(2,1)S(1)}, u32[]{:S(2)}, u32[]{:S(2)}) collective-permute-start(bf16[128,128]{1,0:T(8,128)(2,1)S(1)} %get-tuple-element.80), channel_id=1, source_target_pairs={{0,2},{1,17},{2,0},{3,4},{4,3},{5,6},{6,5},{7,8},{8,7},{9,10},{10,... | collective-permute-start | bytes 98312 | tf_op jit(solution)/shard_map/ppermute | solution.py:376
  5.8 0.4 collective-permute-start.3
  6.8 2.5 %shard_map.74 = (bf16[384,1024]{1,0:T(8,128)(2,1)S(1)}, bf16[384,1024]{1,0:T(8,128)(2,1)S(1)}, bf16[384,384]{1,0:T(8,128)(2,1)S(1)}, bf16[384,384]{1,0:T(8,128)(...) custom-call(bf16[1024,384]{1,0:T(8,128)(2,1)S(1)} %get-tuple-element, ...), custom_call_target="tpu_custom_call" | custom-call | flops 1207959552 | bytes 12414980 | tf_op jit(solution)/shard_map/pallas_call | solution.py:341
  9.6 0.4 shard_map.75
  10.0 0.6 %collective-permute-start.4 = (bf16[128,128]{1,0:T(8,128)(2,1)S(1)}, bf16[128,128]{1,0:T(8,128)(2,1)S(1)}, u32[]{:S(2)}, u32[]{:S(2)}) collective-permute-start(bf16[128,128]{1,0:T(8,128)(2,1)S(1)} %get-tuple-element.93), channel_id=1, source_target_pairs={{0,16},{1,2},{2,1},{3,19},{4,5},{5,4},{6,15},{7,23},{8,24},{9,25},... | collective-permute-start | bytes 98312 | tf_op jit(solution)/shard_map/ppermute | solution.py:376
  10.6 0.9 %collective-permute-start.5 = (bf16[128,128]{1,0:T(8,128)(2,1)S(1)}, bf16[128,128]{1,0:T(8,128)(2,1)S(1)}, u32[]{:S(2)}, u32[]{:S(2)}) collective-permute-start(bf16[128,128]{1,0:T(8,128)(2,1)S(1)} %get-tuple-element.94), channel_id=1, source_target_pairs={{0,2},{1,17},{2,0},{3,4},{4,3},{5,6},{6,5},{7,8},{8,7},{9,10},{10,... | collective-permute-start | bytes 98312 | tf_op jit(solution)/shard_map/ppermute | solution.py:376
  11.4 0.5 collective-permute-start.6
  11.9 2.7 %shard_map.76 = (f32[128,1024]{1,0:T(8,128)S(1)}, f32[128,384]{1,0:T(8,128)S(1)}, bf16[1024,384]{1,0:T(8,128)(2,1)S(1)}, bf16[384,384]{1,0:T(8,128)(2,1)S(1)}) custom-call(bf16[128,128]{1,0:T(8,128)(2,1)S(1)} %collective-permute-done.refs_0_, bf16[128,128]{1,0:T(8,128)(2,1)S(1)} %collective-permute-done.1.refs_1_, ...), custom_call_target="tpu_custom_call" | custom-call | flops 1577058304 | bytes 8392704 | tf_op jit(solution)/shard_map/pallas_call | solution.py:341
  14.9 0.9 %collective-permute-done.5.refs_1_ = bf16[128,128]{1,0:T(8,128)(2,1)S(1)} collective-permute-done((bf16[128,128]{1,0:T(8,128)(2,1)S(1)}, bf16[128,128]{1,0:T(8,128)(2,1)S(1)}, u32[]{:S(2)}, u32[]{:S(2)}) %collective-permute-start.5) | collective-permute-done | bytes 32800 | tf_op jit(solution)/shard_map/ppermute | solution.py:376
  16.1 1.6 %collective-permute-start.8 = (bf16[128,128]{1,0:T(8,128)(2,1)S(1)}, bf16[128,128]{1,0:T(8,128)(2,1)S(1)}, u32[]{:S(2)}, u32[]{:S(2)}) collective-permute-start(bf16[128,128]{1,0:T(8,128)(2,1)S(1)} %get-tuple-element.106), channel_id=1, source_target_pairs={{0,16},{1,2},{2,1},{3,19},{4,20},{5,21},{6,22},{7,8},{8,7},{9,10},... | collective-permute-start | bytes 98312 | tf_op jit(solution)/shard_map/ppermute | solution.py:376
  17.8 2.2 %collective-permute-start.9 = (bf16[128,128]{1,0:T(8,128)(2,1)S(1)}, bf16[128,128]{1,0:T(8,128)(2,1)S(1)}, u32[]{:S(2)}, u32[]{:S(2)}) collective-permute-start(bf16[128,128]{1,0:T(8,128)(2,1)S(1)} %get-tuple-element.107), channel_id=1, source_target_pairs={{0,3},{1,17},{2,18},{3,0},{4,13},{5,6},{6,5},{7,23},{8,24},{9,25},... | collective-permute-start | bytes 98312 | tf_op jit(solution)/shard_map/ppermute | solution.py:376
  20.0 0.5 collective-permute-start.11
  20.5 1.0 %shard_map.78 = (f32[128,1024]{1,0:T(8,128)S(1)}, f32[128,1024]{1,0:T(8,128)S(1)}, f32[128,384]{1,0:T(8,128)S(1)}) custom-call(bf16[128,128]{1,0:T(8,128)(2,1)S(1)} %collective-permute-done.4.refs_0_, bf16[128,128]{1,0:T(8,128)(2,1)S(1)} %collective-permute-done.5.refs_1_, bf16[128,128]{1,0:T(8,128)(2,1)S(1)} %collective-permute-done.6.refs_2_, ...), custom_call_target="tpu_custom_call" | custom-call | flops 469762048 | bytes 5902336 | tf_op jit(solution)/shard_map/pallas_call | solution.py:341
  21.5 1.1 %collective-permute-done.9.refs_1_ = bf16[128,128]{1,0:T(8,128)(2,1)S(1)} collective-permute-done((bf16[128,128]{1,0:T(8,128)(2,1)S(1)}, bf16[128,128]{1,0:T(8,128)(2,1)S(1)}, u32[]{:S(2)}, u32[]{:S(2)}) %collective-permute-start.9) | collective-permute-done | bytes 32800 | tf_op jit(solution)/shard_map/ppermute | solution.py:376
  22.6 0.4 shard_map.79
  23.0 1.8 %collective-permute-start.12 = (bf16[128,128]{1,0:T(8,128)(2,1)S(1)}, bf16[128,128]{1,0:T(8,128)(2,1)S(1)}, u32[]{:S(2)}, u32[]{:S(2)}) collective-permute-start(bf16[128,128]{1,0:T(8,128)(2,1)S(1)} %get-tuple-element.115), channel_id=1, source_target_pairs={{0,16},{1,2},{2,1},{3,19},{4,20},{5,21},{6,22},{7,8},{8,7},{9,10},... | collective-permute-start | bytes 98312 | tf_op jit(solution)/shard_map/ppermute | solution.py:376
  24.8 1.6 %collective-permute-start.13 = (bf16[128,128]{1,0:T(8,128)(2,1)S(1)}, bf16[128,128]{1,0:T(8,128)(2,1)S(1)}, u32[]{:S(2)}, u32[]{:S(2)}) collective-permute-start(bf16[128,128]{1,0:T(8,128)(2,1)S(1)} %get-tuple-element.116), channel_id=1, source_target_pairs={{0,3},{1,17},{2,18},{3,0},{4,13},{5,6},{6,5},{7,23},{8,24},{9,25},... | collective-permute-start | bytes 98312 | tf_op jit(solution)/shard_map/ppermute | solution.py:376
  26.3 0.5 collective-permute-start.15
  26.8 1.3 %shard_map.80 = (f32[128,1024]{1,0:T(8,128)S(1)}, f32[128,384]{1,0:T(8,128)S(1)}) custom-call(bf16[128,128]{1,0:T(8,128)(2,1)S(1)} %collective-permute-done.8.refs_0_, bf16[128,128]{1,0:T(8,128)(2,1)S(1)} %collective-permute-done.9.refs_1_, bf16[128,128]{1,0:T(8,128)(2,1)S(1)} %collective-permute-done.10.refs_2_, ...), custom_call_target="tpu_custom_call" | custom-call | flops 469762048 | bytes 5738496 | tf_op jit(solution)/shard_map/pallas_call | solution.py:341
  28.4 1.1 %collective-permute-done.13.refs_1_ = bf16[128,128]{1,0:T(8,128)(2,1)S(1)} collective-permute-done((bf16[128,128]{1,0:T(8,128)(2,1)S(1)}, bf16[128,128]{1,0:T(8,128)(2,1)S(1)}, u32[]{:S(2)}, u32[]{:S(2)}) %collective-permute-start.13) | collective-permute-done | bytes 32800 | tf_op jit(solution)/shard_map/ppermute | solution.py:376
  30.0 1.2 %collective-permute-start.16 = (bf16[128,128]{1,0:T(8,128)(2,1)S(1)}, bf16[128,128]{1,0:T(8,128)(2,1)S(1)}, u32[]{:S(2)}, u32[]{:S(2)}) collective-permute-start(bf16[128,128]{1,0:T(8,128)(2,1)S(1)} %get-tuple-element.124), channel_id=1, source_target_pairs={{0,16},{1,2},{2,1},{3,19},{4,20},{5,21},{6,22},{7,8},{8,7},{9,10},... | collective-permute-start | bytes 98312 | tf_op jit(solution)/shard_map/ppermute | solution.py:376
  31.2 2.0 %collective-permute-start.17 = (bf16[128,128]{1,0:T(8,128)(2,1)S(1)}, bf16[128,128]{1,0:T(8,128)(2,1)S(1)}, u32[]{:S(2)}, u32[]{:S(2)}) collective-permute-start(bf16[128,128]{1,0:T(8,128)(2,1)S(1)} %get-tuple-element.125), channel_id=1, source_target_pairs={{0,3},{1,17},{2,18},{3,0},{4,13},{5,6},{6,5},{7,23},{8,24},{9,25},... | collective-permute-start | bytes 98312 | tf_op jit(solution)/shard_map/ppermute | solution.py:376
  33.2 0.5 collective-permute-start.19
  33.7 1.0 %shard_map.82 = (f32[128,1024]{1,0:T(8,128)S(1)}, f32[128,1024]{1,0:T(8,128)S(1)}, f32[128,384]{1,0:T(8,128)S(1)}) custom-call(bf16[128,128]{1,0:T(8,128)(2,1)S(1)} %collective-permute-done.12.refs_0_, bf16[128,128]{1,0:T(8,128)(2,1)S(1)} %collective-permute-done.13.refs_1_, bf16[128,128]{1,0:T(8,128)(2,1)S(1)} %collective-permute-done.14.refs_2_, ...), custom_call_target="tpu_custom_call" | custom-call | flops 469762048 | bytes 5902336 | tf_op jit(solution)/shard_map/pallas_call | solution.py:341
  34.7 0.6 collective-permute-done.16.refs_0_
  35.3 0.7 %collective-permute-done.17.refs_1_ = bf16[128,128]{1,0:T(8,128)(2,1)S(1)} collective-permute-done((bf16[128,128]{1,0:T(8,128)(2,1)S(1)}, bf16[128,128]{1,0:T(8,128)(2,1)S(1)}, u32[]{:S(2)}, u32[]{:S(2)}) %collective-permute-start.17) | collective-permute-done | bytes 32800 | tf_op jit(solution)/shard_map/ppermute | solution.py:376
  36.0 0.4 shard_map.83
  36.4 1.3 %collective-permute-start.20 = (bf16[128,128]{1,0:T(8,128)(2,1)S(1)}, bf16[128,128]{1,0:T(8,128)(2,1)S(1)}, u32[]{:S(2)}, u32[]{:S(2)}) collective-permute-start(bf16[128,128]{1,0:T(8,128)(2,1)S(1)} %get-tuple-element.132), channel_id=1, source_target_pairs={{0,16},{1,2},{2,1},{3,19},{4,20},{5,21},{6,22},{7,8},{8,7},{9,10},... | collective-permute-start | bytes 98312 | tf_op jit(solution)/shard_map/ppermute | solution.py:376
  37.7 1.6 %collective-permute-start.21 = (bf16[128,128]{1,0:T(8,128)(2,1)S(1)}, bf16[128,128]{1,0:T(8,128)(2,1)S(1)}, u32[]{:S(2)}, u32[]{:S(2)}) collective-permute-start(bf16[128,128]{1,0:T(8,128)(2,1)S(1)} %get-tuple-element.133), channel_id=1, source_target_pairs={{0,3},{1,17},{2,18},{3,0},{4,13},{5,6},{6,5},{7,23},{8,24},{9,25},... | collective-permute-start | bytes 98312 | tf_op jit(solution)/shard_map/ppermute | solution.py:376
  39.3 0.5 collective-permute-start.23
  39.8 1.3 %shard_map.84 = (f32[128,1024]{1,0:T(8,128)S(1)}, f32[128,384]{1,0:T(8,128)S(1)}) custom-call(bf16[128,128]{1,0:T(8,128)(2,1)S(1)} %collective-permute-done.16.refs_0_, bf16[128,128]{1,0:T(8,128)(2,1)S(1)} %collective-permute-done.17.refs_1_, bf16[128,128]{1,0:T(8,128)(2,1)S(1)} %collective-permute-done.18.refs_2_, ...), custom_call_target="tpu_custom_call" | custom-call | flops 469762048 | bytes 5738496 | tf_op jit(solution)/shard_map/pallas_call | solution.py:341
  41.1 0.5 collective-permute-done.20.refs_0_
  41.6 0.9 %collective-permute-done.21.refs_1_ = bf16[128,128]{1,0:T(8,128)(2,1)S(1)} collective-permute-done((bf16[128,128]{1,0:T(8,128)(2,1)S(1)}, bf16[128,128]{1,0:T(8,128)(2,1)S(1)}, u32[]{:S(2)}, u32[]{:S(2)}) %collective-permute-start.21) | collective-permute-done | bytes 32800 | tf_op jit(solution)/shard_map/ppermute | solution.py:376
  43.0 1.2 %collective-permute-start.24 = (bf16[128,128]{1,0:T(8,128)(2,1)S(1)}, bf16[128,128]{1,0:T(8,128)(2,1)S(1)}, u32[]{:S(2)}, u32[]{:S(2)}) collective-permute-start(bf16[128,128]{1,0:T(8,128)(2,1)S(1)} %get-tuple-element.140), channel_id=1, source_target_pairs={{0,16},{1,2},{2,1},{3,19},{4,20},{5,21},{6,22},{7,8},{8,7},{9,10},... | collective-permute-start | bytes 98312 | tf_op jit(solution)/shard_map/ppermute | solution.py:376
  44.1 2.0 %collective-permute-start.25 = (bf16[128,128]{1,0:T(8,128)(2,1)S(1)}, bf16[128,128]{1,0:T(8,128)(2,1)S(1)}, u32[]{:S(2)}, u32[]{:S(2)}) collective-permute-start(bf16[128,128]{1,0:T(8,128)(2,1)S(1)} %get-tuple-element.141), channel_id=1, source_target_pairs={{0,3},{1,17},{2,18},{3,0},{4,13},{5,6},{6,5},{7,23},{8,24},{9,25},... | collective-permute-start | bytes 98312 | tf_op jit(solution)/shard_map/ppermute | solution.py:376
  46.2 0.5 collective-permute-start.27
  46.7 1.0 %shard_map.86 = (f32[128,1024]{1,0:T(8,128)S(1)}, f32[128,1024]{1,0:T(8,128)S(1)}, f32[128,384]{1,0:T(8,128)S(1)}) custom-call(bf16[128,128]{1,0:T(8,128)(2,1)S(1)} %collective-permute-done.20.refs_0_, bf16[128,128]{1,0:T(8,128)(2,1)S(1)} %collective-permute-done.21.refs_1_, bf16[128,128]{1,0:T(8,128)(2,1)S(1)} %collective-permute-done.22.refs_2_, ...), custom_call_target="tpu_custom_call" | custom-call | flops 469762048 | bytes 5902336 | tf_op jit(solution)/shard_map/pallas_call | solution.py:341
  47.7 0.5 collective-permute-done.24.refs_0_
  48.2 0.8 %collective-permute-done.25.refs_1_ = bf16[128,128]{1,0:T(8,128)(2,1)S(1)} collective-permute-done((bf16[128,128]{1,0:T(8,128)(2,1)S(1)}, bf16[128,128]{1,0:T(8,128)(2,1)S(1)}, u32[]{:S(2)}, u32[]{:S(2)}) %collective-permute-start.25) | collective-permute-done | bytes 32800 | tf_op jit(solution)/shard_map/ppermute | solution.py:376
  49.4 1.3 %collective-permute-start.28 = (bf16[128,128]{1,0:T(8,128)(2,1)S(1)}, bf16[128,128]{1,0:T(8,128)(2,1)S(1)}, u32[]{:S(2)}, u32[]{:S(2)}) collective-permute-start(bf16[128,128]{1,0:T(8,128)(2,1)S(1)} %get-tuple-element.147), channel_id=1, source_target_pairs={{0,16},{1,2},{2,1},{3,19},{4,20},{5,21},{6,22},{7,8},{8,7},{9,10},... | collective-permute-start | bytes 98312 | tf_op jit(solution)/shard_map/ppermute | solution.py:376
  50.7 1.6 %collective-permute-start.29 = (bf16[128,128]{1,0:T(8,128)(2,1)S(1)}, bf16[128,128]{1,0:T(8,128)(2,1)S(1)}, u32[]{:S(2)}, u32[]{:S(2)}) collective-permute-start(bf16[128,128]{1,0:T(8,128)(2,1)S(1)} %get-tuple-element.148), channel_id=1, source_target_pairs={{0,3},{1,17},{2,18},{3,0},{4,13},{5,6},{6,5},{7,23},{8,24},{9,25},... | collective-permute-start | bytes 98312 | tf_op jit(solution)/shard_map/ppermute | solution.py:376
  52.3 0.5 collective-permute-start.31
  52.8 1.2 %shard_map.88.refs_5_ = f32[1024,128]{1,0:T(8,128)S(1)} custom-call(bf16[128,128]{1,0:T(8,128)(2,1)S(1)} %collective-permute-done.24.refs_0_, bf16[128,128]{1,0:T(8,128)(2,1)S(1)} %collective-permute-done.25.refs_1_, bf16[128,128]{1,0:T(8,128)(2,1)S(1)} %collective-permute-done.26.refs_2_, bf16[128,128]{1,0:T(8,128)(2,1)S(1)} %collective-permute-done.27.refs_3_, ...), custom_call_target="tpu_custom_call" | custom-call | flops 369098752 | bytes 4624384 | tf_op jit(solution)/shard_map/pallas_call | solution.py:341
  54.0 0.6 collective-permute-done.28.refs_0_
  54.6 0.9 %collective-permute-done.29.refs_1_ = bf16[128,128]{1,0:T(8,128)(2,1)S(1)} collective-permute-done((bf16[128,128]{1,0:T(8,128)(2,1)S(1)}, bf16[128,128]{1,0:T(8,128)(2,1)S(1)}, u32[]{:S(2)}, u32[]{:S(2)}) %collective-permute-start.29) | collective-permute-done | bytes 32800 | tf_op jit(solution)/shard_map/ppermute | solution.py:376
  55.5 1.2 %shard_map.89 = f32[1,1024,128]{2,1,0:T(8,128)} custom-call(bf16[128,128]{1,0:T(8,128)(2,1)S(1)} %collective-permute-done.28.refs_0_, bf16[128,128]{1,0:T(8,128)(2,1)S(1)} %collective-permute-done.29.refs_1_, bf16[128,128]{1,0:T(8,128)(2,1)S(1)} %collective-permute-done.30.refs_2_, bf16[128,128]{1,0:T(8,128)(2,1)S(1)} %collective-permute-done.31.refs_3_, ...), custom_call_target="tpu_custom_call" | custom-call | flops 100663296 | bytes 1966080 | tf_op jit(solution)/shard_map/pallas_call | solution.py:341
  (33 shorter events, 2.5 us)
Async XLA Ops:
  1.5 7.8 %collective-permute-start = (bf16[128,128]{1,0:T(8,128)(2,1)S(1)}, bf16[128,128]{1,0:T(8,128)(2,1)S(1)}, u32[]{:S(2)}, u32[]{:S(2)}) collective-permute-start(bf16[128,128]{1,0:T(8,128)(2,1)S(1)} %get-tuple-element.79), channel_id=1, source_target_pairs={{0,16},{1,2},{2,1},{3,19},{4,5},{5,4},{6,15},{7,23},{8,24},{9,25},... | collective-permute-start | bytes 98312 | tf_op jit(solution)/shard_map/ppermute | solution.py:376
  4.2 5.4 %collective-permute-start.1 = (bf16[128,128]{1,0:T(8,128)(2,1)S(1)}, bf16[128,128]{1,0:T(8,128)(2,1)S(1)}, u32[]{:S(2)}, u32[]{:S(2)}) collective-permute-start(bf16[128,128]{1,0:T(8,128)(2,1)S(1)} %get-tuple-element.80), channel_id=1, source_target_pairs={{0,2},{1,17},{2,0},{3,4},{4,3},{5,6},{6,5},{7,8},{8,7},{9,10},{10,... | collective-permute-start | bytes 98312 | tf_op jit(solution)/shard_map/ppermute | solution.py:376
  5.6 3.9 %collective-permute-start.2 = (bf16[128,128]{1,0:T(8,128)(2,1)S(1)}, bf16[128,128]{1,0:T(8,128)(2,1)S(1)}, u32[]{:S(2)}, u32[]{:S(2)}) collective-permute-start(bf16[128,128]{1,0:T(8,128)(2,1)S(1)} %get-tuple-element.81), channel_id=1, source_target_pairs={{0,1},{1,0},{2,18},{3,7},{4,20},{5,21},{6,22},{7,3},{8,9},{9,8},{1... | collective-permute-start | bytes 98312 | tf_op jit(solution)/shard_map/ppermute | solution.py:376
  5.8 3.8 %collective-permute-start.3 = (bf16[128,128]{1,0:T(8,128)(2,1)S(1)}, bf16[128,128]{1,0:T(8,128)(2,1)S(1)}, u32[]{:S(2)}, u32[]{:S(2)}) collective-permute-start(bf16[128,128]{1,0:T(8,128)(2,1)S(1)} %get-tuple-element.82), channel_id=1, source_target_pairs={{0,1},{1,0},{2,3},{3,2},{4,5},{5,4},{6,7},{7,6},{8,9},{9,8},{10,11... | collective-permute-start | bytes 98312 | tf_op jit(solution)/shard_map/ppermute | solution.py:376
  10.0 4.9 %collective-permute-start.4 = (bf16[128,128]{1,0:T(8,128)(2,1)S(1)}, bf16[128,128]{1,0:T(8,128)(2,1)S(1)}, u32[]{:S(2)}, u32[]{:S(2)}) collective-permute-start(bf16[128,128]{1,0:T(8,128)(2,1)S(1)} %get-tuple-element.93), channel_id=1, source_target_pairs={{0,16},{1,2},{2,1},{3,19},{4,5},{5,4},{6,15},{7,23},{8,24},{9,25},... | collective-permute-start | bytes 98312 | tf_op jit(solution)/shard_map/ppermute | solution.py:376
  10.6 5.1 %collective-permute-start.5 = (bf16[128,128]{1,0:T(8,128)(2,1)S(1)}, bf16[128,128]{1,0:T(8,128)(2,1)S(1)}, u32[]{:S(2)}, u32[]{:S(2)}) collective-permute-start(bf16[128,128]{1,0:T(8,128)(2,1)S(1)} %get-tuple-element.94), channel_id=1, source_target_pairs={{0,2},{1,17},{2,0},{3,4},{4,3},{5,6},{6,5},{7,8},{8,7},{9,10},{10,... | collective-permute-start | bytes 98312 | tf_op jit(solution)/shard_map/ppermute | solution.py:376
  11.4 4.3 %collective-permute-start.6 = (bf16[128,128]{1,0:T(8,128)(2,1)S(1)}, bf16[128,128]{1,0:T(8,128)(2,1)S(1)}, u32[]{:S(2)}, u32[]{:S(2)}) collective-permute-start(bf16[128,128]{1,0:T(8,128)(2,1)S(1)} %get-tuple-element.95), channel_id=1, source_target_pairs={{0,1},{1,0},{2,18},{3,7},{4,20},{5,21},{6,22},{7,3},{8,9},{9,8},{1... | collective-permute-start | bytes 98312 | tf_op jit(solution)/shard_map/ppermute | solution.py:376
  11.9 3.8 %collective-permute-start.7 = (bf16[128,128]{1,0:T(8,128)(2,1)S(1)}, bf16[128,128]{1,0:T(8,128)(2,1)S(1)}, u32[]{:S(2)}, u32[]{:S(2)}) collective-permute-start(bf16[128,128]{1,0:T(8,128)(2,1)S(1)} %get-tuple-element.96), channel_id=1, source_target_pairs={{0,1},{1,0},{2,3},{3,2},{4,5},{5,4},{6,7},{7,6},{8,9},{9,8},{10,11... | collective-permute-start | bytes 98312 | tf_op jit(solution)/shard_map/ppermute | solution.py:376
  16.1 5.4 %collective-permute-start.8 = (bf16[128,128]{1,0:T(8,128)(2,1)S(1)}, bf16[128,128]{1,0:T(8,128)(2,1)S(1)}, u32[]{:S(2)}, u32[]{:S(2)}) collective-permute-start(bf16[128,128]{1,0:T(8,128)(2,1)S(1)} %get-tuple-element.106), channel_id=1, source_target_pairs={{0,16},{1,2},{2,1},{3,19},{4,20},{5,21},{6,22},{7,8},{8,7},{9,10},... | collective-permute-start | bytes 98312 | tf_op jit(solution)/shard_map/ppermute | solution.py:376
  17.8 4.8 %collective-permute-start.9 = (bf16[128,128]{1,0:T(8,128)(2,1)S(1)}, bf16[128,128]{1,0:T(8,128)(2,1)S(1)}, u32[]{:S(2)}, u32[]{:S(2)}) collective-permute-start(bf16[128,128]{1,0:T(8,128)(2,1)S(1)} %get-tuple-element.107), channel_id=1, source_target_pairs={{0,3},{1,17},{2,18},{3,0},{4,13},{5,6},{6,5},{7,23},{8,24},{9,25},... | collective-permute-start | bytes 98312 | tf_op jit(solution)/shard_map/ppermute | solution.py:376
  20.0 2.6 %collective-permute-start.10 = (bf16[128,128]{1,0:T(8,128)(2,1)S(1)}, bf16[128,128]{1,0:T(8,128)(2,1)S(1)}, u32[]{:S(2)}, u32[]{:S(2)}) collective-permute-start(bf16[128,128]{1,0:T(8,128)(2,1)S(1)} %get-tuple-element.108), channel_id=1, source_target_pairs={{0,1},{1,0},{2,5},{3,4},{4,3},{5,2},{6,7},{7,6},{8,9},{9,8},{10,11... | collective-permute-start | bytes 98312 | tf_op jit(solution)/shard_map/ppermute | solution.py:376
  20.0 2.6 %collective-permute-start.11 = (bf16[128,128]{1,0:T(8,128)(2,1)S(1)}, bf16[128,128]{1,0:T(8,128)(2,1)S(1)}, u32[]{:S(2)}, u32[]{:S(2)}) collective-permute-start(bf16[128,128]{1,0:T(8,128)(2,1)S(1)} %get-tuple-element.109), channel_id=1, source_target_pairs={{0,1},{1,0},{2,3},{3,2},{4,5},{5,4},{6,7},{7,6},{8,9},{9,8},{10,11... | collective-permute-start | bytes 98312 | tf_op jit(solution)/shard_map/ppermute | solution.py:376
  23.0 5.4 %collective-permute-start.12 = (bf16[128,128]{1,0:T(8,128)(2,1)S(1)}, bf16[128,128]{1,0:T(8,128)(2,1)S(1)}, u32[]{:S(2)}, u32[]{:S(2)}) collective-permute-start(bf16[128,128]{1,0:T(8,128)(2,1)S(1)} %get-tuple-element.115), channel_id=1, source_target_pairs={{0,16},{1,2},{2,1},{3,19},{4,20},{5,21},{6,22},{7,8},{8,7},{9,10},... | collective-permute-start | bytes 98312 | tf_op jit(solution)/shard_map/ppermute | solution.py:376
  24.8 4.8 %collective-permute-start.13 = (bf16[128,128]{1,0:T(8,128)(2,1)S(1)}, bf16[128,128]{1,0:T(8,128)(2,1)S(1)}, u32[]{:S(2)}, u32[]{:S(2)}) collective-permute-start(bf16[128,128]{1,0:T(8,128)(2,1)S(1)} %get-tuple-element.116), channel_id=1, source_target_pairs={{0,3},{1,17},{2,18},{3,0},{4,13},{5,6},{6,5},{7,23},{8,24},{9,25},... | collective-permute-start | bytes 98312 | tf_op jit(solution)/shard_map/ppermute | solution.py:376
  26.3 3.2 %collective-permute-start.14 = (bf16[128,128]{1,0:T(8,128)(2,1)S(1)}, bf16[128,128]{1,0:T(8,128)(2,1)S(1)}, u32[]{:S(2)}, u32[]{:S(2)}) collective-permute-start(bf16[128,128]{1,0:T(8,128)(2,1)S(1)} %get-tuple-element.117), channel_id=1, source_target_pairs={{0,1},{1,0},{2,5},{3,4},{4,3},{5,2},{6,7},{7,6},{8,9},{9,8},{10,11... | collective-permute-start | bytes 98312 | tf_op jit(solution)/shard_map/ppermute | solution.py:376
  26.3 3.2 %collective-permute-start.15 = (bf16[128,128]{1,0:T(8,128)(2,1)S(1)}, bf16[128,128]{1,0:T(8,128)(2,1)S(1)}, u32[]{:S(2)}, u32[]{:S(2)}) collective-permute-start(bf16[128,128]{1,0:T(8,128)(2,1)S(1)} %get-tuple-element.118), channel_id=1, source_target_pairs={{0,1},{1,0},{2,3},{3,2},{4,5},{5,4},{6,7},{7,6},{8,9},{9,8},{10,11... | collective-permute-start | bytes 98312 | tf_op jit(solution)/shard_map/ppermute | solution.py:376
  30.0 5.3 %collective-permute-start.16 = (bf16[128,128]{1,0:T(8,128)(2,1)S(1)}, bf16[128,128]{1,0:T(8,128)(2,1)S(1)}, u32[]{:S(2)}, u32[]{:S(2)}) collective-permute-start(bf16[128,128]{1,0:T(8,128)(2,1)S(1)} %get-tuple-element.124), channel_id=1, source_target_pairs={{0,16},{1,2},{2,1},{3,19},{4,20},{5,21},{6,22},{7,8},{8,7},{9,10},... | collective-permute-start | bytes 98312 | tf_op jit(solution)/shard_map/ppermute | solution.py:376
  31.2 4.8 %collective-permute-start.17 = (bf16[128,128]{1,0:T(8,128)(2,1)S(1)}, bf16[128,128]{1,0:T(8,128)(2,1)S(1)}, u32[]{:S(2)}, u32[]{:S(2)}) collective-permute-start(bf16[128,128]{1,0:T(8,128)(2,1)S(1)} %get-tuple-element.125), channel_id=1, source_target_pairs={{0,3},{1,17},{2,18},{3,0},{4,13},{5,6},{6,5},{7,23},{8,24},{9,25},... | collective-permute-start | bytes 98312 | tf_op jit(solution)/shard_map/ppermute | solution.py:376
  33.2 2.8 %collective-permute-start.18 = (bf16[128,128]{1,0:T(8,128)(2,1)S(1)}, bf16[128,128]{1,0:T(8,128)(2,1)S(1)}, u32[]{:S(2)}, u32[]{:S(2)}) collective-permute-start(bf16[128,128]{1,0:T(8,128)(2,1)S(1)} %get-tuple-element.126), channel_id=1, source_target_pairs={{0,1},{1,0},{2,5},{3,4},{4,3},{5,2},{6,7},{7,6},{8,9},{9,8},{10,11... | collective-permute-start | bytes 98312 | tf_op jit(solution)/shard_map/ppermute | solution.py:376
  33.2 2.8 %collective-permute-start.19 = (bf16[128,128]{1,0:T(8,128)(2,1)S(1)}, bf16[128,128]{1,0:T(8,128)(2,1)S(1)}, u32[]{:S(2)}, u32[]{:S(2)}) collective-permute-start(bf16[128,128]{1,0:T(8,128)(2,1)S(1)} %get-tuple-element.127), channel_id=1, source_target_pairs={{0,1},{1,0},{2,3},{3,2},{4,5},{5,4},{6,7},{7,6},{8,9},{9,8},{10,11... | collective-permute-start | bytes 98312 | tf_op jit(solution)/shard_map/ppermute | solution.py:376
  36.4 5.2 %collective-permute-start.20 = (bf16[128,128]{1,0:T(8,128)(2,1)S(1)}, bf16[128,128]{1,0:T(8,128)(2,1)S(1)}, u32[]{:S(2)}, u32[]{:S(2)}) collective-permute-start(bf16[128,128]{1,0:T(8,128)(2,1)S(1)} %get-tuple-element.132), channel_id=1, source_target_pairs={{0,16},{1,2},{2,1},{3,19},{4,20},{5,21},{6,22},{7,8},{8,7},{9,10},... | collective-permute-start | bytes 98312 | tf_op jit(solution)/shard_map/ppermute | solution.py:376
  37.7 4.8 %collective-permute-start.21 = (bf16[128,128]{1,0:T(8,128)(2,1)S(1)}, bf16[128,128]{1,0:T(8,128)(2,1)S(1)}, u32[]{:S(2)}, u32[]{:S(2)}) collective-permute-start(bf16[128,128]{1,0:T(8,128)(2,1)S(1)} %get-tuple-element.133), channel_id=1, source_target_pairs={{0,3},{1,17},{2,18},{3,0},{4,13},{5,6},{6,5},{7,23},{8,24},{9,25},... | collective-permute-start | bytes 98312 | tf_op jit(solution)/shard_map/ppermute | solution.py:376
  39.3 3.2 %collective-permute-start.22 = (bf16[128,128]{1,0:T(8,128)(2,1)S(1)}, bf16[128,128]{1,0:T(8,128)(2,1)S(1)}, u32[]{:S(2)}, u32[]{:S(2)}) collective-permute-start(bf16[128,128]{1,0:T(8,128)(2,1)S(1)} %get-tuple-element.134), channel_id=1, source_target_pairs={{0,1},{1,0},{2,5},{3,4},{4,3},{5,2},{6,7},{7,6},{8,9},{9,8},{10,11... | collective-permute-start | bytes 98312 | tf_op jit(solution)/shard_map/ppermute | solution.py:376
  39.3 3.2 %collective-permute-start.23 = (bf16[128,128]{1,0:T(8,128)(2,1)S(1)}, bf16[128,128]{1,0:T(8,128)(2,1)S(1)}, u32[]{:S(2)}, u32[]{:S(2)}) collective-permute-start(bf16[128,128]{1,0:T(8,128)(2,1)S(1)} %get-tuple-element.135), channel_id=1, source_target_pairs={{0,1},{1,0},{2,3},{3,2},{4,5},{5,4},{6,7},{7,6},{8,9},{9,8},{10,11... | collective-permute-start | bytes 98312 | tf_op jit(solution)/shard_map/ppermute | solution.py:376
  43.0 5.2 %collective-permute-start.24 = (bf16[128,128]{1,0:T(8,128)(2,1)S(1)}, bf16[128,128]{1,0:T(8,128)(2,1)S(1)}, u32[]{:S(2)}, u32[]{:S(2)}) collective-permute-start(bf16[128,128]{1,0:T(8,128)(2,1)S(1)} %get-tuple-element.140), channel_id=1, source_target_pairs={{0,16},{1,2},{2,1},{3,19},{4,20},{5,21},{6,22},{7,8},{8,7},{9,10},... | collective-permute-start | bytes 98312 | tf_op jit(solution)/shard_map/ppermute | solution.py:376
  44.1 4.8 %collective-permute-start.25 = (bf16[128,128]{1,0:T(8,128)(2,1)S(1)}, bf16[128,128]{1,0:T(8,128)(2,1)S(1)}, u32[]{:S(2)}, u32[]{:S(2)}) collective-permute-start(bf16[128,128]{1,0:T(8,128)(2,1)S(1)} %get-tuple-element.141), channel_id=1, source_target_pairs={{0,3},{1,17},{2,18},{3,0},{4,13},{5,6},{6,5},{7,23},{8,24},{9,25},... | collective-permute-start | bytes 98312 | tf_op jit(solution)/shard_map/ppermute | solution.py:376
  46.2 2.8 %collective-permute-start.26 = (bf16[128,128]{1,0:T(8,128)(2,1)S(1)}, bf16[128,128]{1,0:T(8,128)(2,1)S(1)}, u32[]{:S(2)}, u32[]{:S(2)}) collective-permute-start(bf16[128,128]{1,0:T(8,128)(2,1)S(1)} %get-tuple-element.142), channel_id=1, source_target_pairs={{0,1},{1,0},{2,5},{3,4},{4,3},{5,2},{6,7},{7,6},{8,9},{9,8},{10,11... | collective-permute-start | bytes 98312 | tf_op jit(solution)/shard_map/ppermute | solution.py:376
  46.2 2.8 %collective-permute-start.27 = (bf16[128,128]{1,0:T(8,128)(2,1)S(1)}, bf16[128,128]{1,0:T(8,128)(2,1)S(1)}, u32[]{:S(2)}, u32[]{:S(2)}) collective-permute-start(bf16[128,128]{1,0:T(8,128)(2,1)S(1)} %get-tuple-element.143), channel_id=1, source_target_pairs={{0,1},{1,0},{2,3},{3,2},{4,5},{5,4},{6,7},{7,6},{8,9},{9,8},{10,11... | collective-permute-start | bytes 98312 | tf_op jit(solution)/shard_map/ppermute | solution.py:376
  49.4 5.2 %collective-permute-start.28 = (bf16[128,128]{1,0:T(8,128)(2,1)S(1)}, bf16[128,128]{1,0:T(8,128)(2,1)S(1)}, u32[]{:S(2)}, u32[]{:S(2)}) collective-permute-start(bf16[128,128]{1,0:T(8,128)(2,1)S(1)} %get-tuple-element.147), channel_id=1, source_target_pairs={{0,16},{1,2},{2,1},{3,19},{4,20},{5,21},{6,22},{7,8},{8,7},{9,10},... | collective-permute-start | bytes 98312 | tf_op jit(solution)/shard_map/ppermute | solution.py:376
  50.7 4.8 %collective-permute-start.29 = (bf16[128,128]{1,0:T(8,128)(2,1)S(1)}, bf16[128,128]{1,0:T(8,128)(2,1)S(1)}, u32[]{:S(2)}, u32[]{:S(2)}) collective-permute-start(bf16[128,128]{1,0:T(8,128)(2,1)S(1)} %get-tuple-element.148), channel_id=1, source_target_pairs={{0,3},{1,17},{2,18},{3,0},{4,13},{5,6},{6,5},{7,23},{8,24},{9,25},... | collective-permute-start | bytes 98312 | tf_op jit(solution)/shard_map/ppermute | solution.py:376
  52.3 3.2 %collective-permute-start.30 = (bf16[128,128]{1,0:T(8,128)(2,1)S(1)}, bf16[128,128]{1,0:T(8,128)(2,1)S(1)}, u32[]{:S(2)}, u32[]{:S(2)}) collective-permute-start(bf16[128,128]{1,0:T(8,128)(2,1)S(1)} %get-tuple-element.149), channel_id=1, source_target_pairs={{0,1},{1,0},{2,5},{3,4},{4,3},{5,2},{6,7},{7,6},{8,9},{9,8},{10,11... | collective-permute-start | bytes 98312 | tf_op jit(solution)/shard_map/ppermute | solution.py:376
  52.3 3.2 %collective-permute-start.31 = (bf16[128,128]{1,0:T(8,128)(2,1)S(1)}, bf16[128,128]{1,0:T(8,128)(2,1)S(1)}, u32[]{:S(2)}, u32[]{:S(2)}) collective-permute-start(bf16[128,128]{1,0:T(8,128)(2,1)S(1)} %get-tuple-element.150), channel_id=1, source_target_pairs={{0,1},{1,0},{2,3},{3,2},{4,5},{5,4},{6,7},{7,6},{8,9},{9,8},{10,11... | collective-permute-start | bytes 98312 | tf_op jit(solution)/shard_map/ppermute | solution.py:376
